TPU v7x, 32 devices: a whole 2x2x4 slice. The times are simulated.
32 devices in a mesh: row: 4 (over y, x), col: 8 (over z, core).
Axes of the slice: x: 2, y: 2, z: 4, core: 2. Of those that a mesh axis runs over, the one named last changes fastest.
Arguments:
- features: bfloat16 [4, 8, 512, 512], P(None, 'col'), may hold values from -6 to 6
- degree: int32 [4, 8, 512], P(None, 'col'), may hold values from 1 to 16
- tile_vals: bfloat16 [4, 8, 48, 256, 256], P('row', 'col'), may hold values from -0.38085938 to 0.38085938
- tile_slot: int32 [4, 8, 48], P('row', 'col'), may hold values from 0 to 127, as said below
- tile_count: int32 [4, 8], P('row', 'col'), may hold values from 24 to 48, as said below
- w_first: bfloat16 [512, 512], replicated, may hold values from -0.25 to 0.25
- w_second: bfloat16 [512, 512], replicated, may hold values from -0.25 to 0.25
- cotangent: bfloat16 [16384, 512], P(('row', 'col')), may hold values from -6 to 6
Outputs:
- logits: bfloat16 [16384, 512], P(('row', 'col'))
- grad_first: float32 [512, 512], replicated
- grad_second: float32 [512, 512], replicated
Inputs may be any that keep to these rules, and one draw needn't show every extreme that they name: `tile_slot`: on each device, the used slots hold distinct positions. `tile_count`: some device uses all 48 slots.
All inputs are finite; a program needn't handle non-finite values.
Results may differ from a plain program's by a relative error of at most 0.025.
Values may be sent and summed in bfloat16 or wider, within the bound.
No kernel may reach another device: no remote copies, remote signals or barrier semaphores. Data moves between devices by JAX's collectives and lax.ppermute only.
A program may use at most 128 MiB of HBM per device.

v0:
```python
import jax
import jax.numpy as jnp
from jax import lax
from jax.sharding import PartitionSpec as P


def forward_term(tiles_here, slots_here, number, source, row_total):
    tile_edge = tiles_here.shape[-1]
    local_cols = source.shape[0] // tile_edge

    def forward_advance(position, running):
        slot_id = slots_here[position]
        row_start = slot_id // local_cols * tile_edge
        col_start = slot_id % local_cols * tile_edge

        def forward_accumulate(current):
            segment = lax.dynamic_slice_in_dim(source, col_start, tile_edge, 0)
            product = jnp.dot(tiles_here[position], segment, preferred_element_type=jnp.float32)
            previous = lax.dynamic_slice_in_dim(current, row_start, tile_edge, 0)
            return lax.dynamic_update_slice_in_dim(current, previous + product, row_start, 0)

        inside = jnp.logical_and(row_start >= 0, row_start < row_total)
        return lax.cond(inside, forward_accumulate, lambda current: current, running)

    zeroed = jnp.zeros((row_total, source.shape[1]), jnp.float32)
    return lax.fori_loop(0, number, forward_advance, zeroed)


def backward_term(tiles_here, slots_here, number, source, local_cols, row_total):
    tile_edge = tiles_here.shape[-1]

    def backward_advance(position, running):
        slot_id = slots_here[position]
        row_start = slot_id % local_cols * tile_edge
        col_start = slot_id // local_cols * tile_edge

        def backward_accumulate(current):
            segment = lax.dynamic_slice_in_dim(source, col_start, tile_edge, 0)
            product = lax.dot_general(
                tiles_here[position],
                segment,
                (((0,), (0,)), ((), ())),
                preferred_element_type=jnp.float32,
            )
            previous = lax.dynamic_slice_in_dim(current, row_start, tile_edge, 0)
            return lax.dynamic_update_slice_in_dim(current, previous + product, row_start, 0)

        inside = jnp.logical_and(row_start >= 0, row_start < row_total)
        return lax.cond(inside, backward_accumulate, lambda current: current, running)

    zeroed = jnp.zeros((row_total, source.shape[1]), jnp.float32)
    return lax.fori_loop(0, number, backward_advance, zeroed)


def per_device(features, degree, tile_vals, tile_slot, tile_count, w_first, w_second, cotangent):
    tiles_here = tile_vals[0, 0]
    slots_here = tile_slot[0, 0]
    number = tile_count[0, 0]
    row_size = lax.axis_size("row")
    row_id = lax.axis_index("row")
    piece_rows = cotangent.shape[0]
    width = cotangent.shape[1]
    tile_edge = tiles_here.shape[-1]
    col_scale = (1.0 / jnp.sqrt(degree.astype(jnp.float32))).reshape(row_size * piece_rows, 1)
    own_scale = lax.dynamic_slice_in_dim(col_scale, row_id * piece_rows, piece_rows, 0)

    def aggregate(source):

        def term(start_row, row_total):
            return forward_term(tiles_here, slots_here, number, source, row_total)

        return lax.psum_scatter(
            term(jnp.int32(0), piece_rows * lax.axis_size("col")).astype(jnp.bfloat16),
            "col",
            scatter_dimension=0,
            tiled=True,
        ).astype(jnp.float32)

    first_in = (
        features[:, 0].reshape(row_size * piece_rows, width).astype(jnp.float32) * col_scale
    ).astype(jnp.bfloat16)
    first_agg = (aggregate(first_in) * own_scale).astype(jnp.bfloat16)
    first_pre = jnp.dot(first_agg, w_first, preferred_element_type=jnp.float32)
    first_out = (jax.nn.gelu(first_pre) * own_scale).astype(jnp.bfloat16)
    gathered = lax.all_gather(first_out, "row", axis=0, tiled=True)
    second_agg = (aggregate(gathered) * own_scale).astype(jnp.bfloat16)
    logits = jnp.dot(second_agg, w_second, preferred_element_type=jnp.float32).astype(jnp.bfloat16)
    second_local = lax.dot_general(
        second_agg, cotangent, (((0,), (0,)), ((), ())), preferred_element_type=jnp.float32
    )
    logits, first_agg, first_pre, second_local = (logits, first_agg, first_pre, second_local)
    grad_agg = lax.dot_general(
        cotangent, w_second, (((1,), (1,)), ((), ())), preferred_element_type=jnp.float32
    )
    grad_agg = (grad_agg * own_scale).astype(jnp.bfloat16)
    ranged = lax.all_gather(grad_agg, "col", axis=0, tiled=True)
    local_cols = row_size * piece_rows // tile_edge

    def term(start_row, row_total):
        return backward_term(tiles_here, slots_here, number, ranged, local_cols, row_total)

    grad_hidden = lax.psum_scatter(
        term(jnp.int32(0), piece_rows * lax.axis_size("row")).astype(jnp.bfloat16),
        "row",
        scatter_dimension=0,
        tiled=True,
    ).astype(jnp.float32)
    grad_second = lax.psum(second_local, ("row", "col"))
    _, pullback = jax.vjp(jax.nn.gelu, first_pre)
    grad_pre = pullback(grad_hidden * own_scale)[0].astype(jnp.bfloat16)
    first_local = lax.dot_general(
        first_agg, grad_pre, (((0,), (0,)), ((), ())), preferred_element_type=jnp.float32
    )
    grad_first = lax.psum(first_local, ("row", "col"))
    return (logits, grad_first, grad_second)


def solution(mesh):
    return jax.shard_map(
        per_device,
        mesh=mesh,
        in_specs=(
            P(None, "col", None, None),
            P(None, "col", None),
            P("row", "col", None, None, None),
            P("row", "col", None),
            P("row", "col"),
            P(),
            P(),
            P(("row", "col"), None),
        ),
        out_specs=(P(("row", "col"), None), P(), P()),
        check_vma=False,
    )
```

profile of v0, /device:TPU:0, one launch (start us, length us, event | category | flops | bytes accessed | tf_op | source)
XLA Modules:
  0.0 1706.3 jit_solution(8312105422171705031)
XLA Ops:
  14.4 437.1 %while.45 = (s32[]{:T(128)}, f32[4096,512]{1,0:T(8,128)}, s32[]{:T(128)}, s32[48]{0:T(128)S(1)}, bf16[48,256,256]{2,1,0:T(8,128)(2,1)}, /*index=5*/bf16[2048,512...) while((s32[]{:T(128)}, f32[4096,512]{1,0:T(8,128)}, ...), condition=%wide.region_3.4_spmd, body=%wide.region_0.3_spmd.sunk | while | flops 67239984 | bytes 2491030 | solution.py:26
  18.2 6.3 conditional.6
  38.6 6.3 conditional.6
  89.6 6.3 conditional.6
  99.8 6.3 conditional.6
  140.6 6.3 conditional.6
  150.8 6.3 conditional.6
  201.8 6.3 conditional.6
  232.3 6.4 conditional.6
  252.7 6.4 conditional.6
  282.3 6.4 conditional.6
  292.6 6.4 conditional.6
  313.0 6.3 conditional.6
  374.1 6.3 conditional.6
  394.5 6.3 conditional.6
  404.7 6.4 conditional.6
  435.3 6.3 conditional.6
  459.9 97.0 %reduce-scatter.4.cloned.1.call-done = bf16[512,512]{1,0:T(8,128)(2,1)} async-done(((bf16[4096,512]{1,0:T(8,128)(2,1)}), bf16[512,512]{1,0:T(8,128)(2,1)}) %reduce-scatter.4.cloned.1.call-update) | async-done | bytes 524304 | tf_op jit(solution)/shard_map/reduce_scatter | solution.py:72
  559.5 44.9 %all-gather.5.cloned.1.call-done = bf16[4096,512]{1,0:T(8,128)(2,1)} async-done(((bf16[512,512]{1,0:T(8,128)(2,1)}), bf16[4096,512]{1,0:T(8,128)(2,1)}) %all-gather.5.cloned.1.call-update) | async-done | bytes 4194320 | tf_op jit(solution)/shard_map/all_gather | solution.py:96
  606.9 349.9 %while.47 = (s32[]{:T(128)}, f32[2048,512]{1,0:T(8,128)}, s32[]{:T(128)}, s32[48]{0:T(128)S(1)}, bf16[48,256,256]{2,1,0:T(8,128)(2,1)}, /*index=5*/bf16[4096,512...) while((s32[]{:T(128)}, f32[2048,512]{1,0:T(8,128)}, ...), condition=%wide.region_13.14_spmd, body=%wide.region_10.13_spmd.sunk | while | flops 67239984 | bytes 2491008 | solution.py:52
  965.0 440.5 %while.46 = (s32[]{:T(128)}, f32[4096,512]{1,0:T(8,128)}, s32[]{:T(128)}, s32[48]{0:T(128)S(1)}, bf16[48,256,256]{2,1,0:T(8,128)(2,1)}, /*index=5*/bf16[2048,512...) while((s32[]{:T(128)}, f32[4096,512]{1,0:T(8,128)}, ...), condition=%wide.region_8.9_spmd, body=%wide.region_5.8_spmd.sunk | while | flops 67239984 | bytes 2491030 | solution.py:26
  968.9 6.4 conditional.7
  979.2 6.4 conditional.7
  989.4 6.4 conditional.7
  999.7 6.4 conditional.7
  1010.0 6.4 conditional.7
  1020.3 6.4 conditional.7
  1030.6 6.4 conditional.7
  1040.9 6.4 conditional.7
  1051.2 6.4 conditional.7
  1061.4 6.4 conditional.7
  1071.7 6.4 conditional.7
  1082.0 6.4 conditional.7
  1092.2 6.4 conditional.7
  1102.5 6.4 conditional.7
  1112.8 6.4 conditional.7
  1123.1 6.4 conditional.7
  1133.4 6.4 conditional.7
  1143.6 6.4 conditional.7
  1153.9 6.4 conditional.7
  1164.2 6.4 conditional.7
  1174.5 6.4 conditional.7
  1184.7 6.4 conditional.7
  1195.0 6.4 conditional.7
  1205.3 6.5 conditional.7
  1224.8 6.4 conditional.7
  1235.1 6.4 conditional.7
  1245.4 6.4 conditional.7
  1255.7 6.4 conditional.7
  1266.0 6.4 conditional.7
  1276.2 6.4 conditional.7
  1286.5 6.4 conditional.7
  1296.8 6.4 conditional.7
  1307.1 6.4 conditional.7
  1317.3 6.4 conditional.7
  1327.6 6.4 conditional.7
  1337.9 6.4 conditional.7
  1348.1 6.4 conditional.7
  1358.4 6.4 conditional.7
  1368.7 6.4 conditional.7
  1379.0 6.4 conditional.7
  1389.3 6.4 conditional.7
  1415.7 140.1 %reduce-scatter.6.cloned.1.call-done = bf16[512,512]{1,0:T(8,128)(2,1)} async-done(((bf16[4096,512]{1,0:T(8,128)(2,1)}), bf16[512,512]{1,0:T(8,128)(2,1)}) %reduce-scatter.6.cloned.1.call-update) | async-done | bytes 524304 | tf_op jit(solution)/shard_map/reduce_scatter | solution.py:72
  1559.8 135.1 %all-reduce.3.cloned.1.call-done = (f32[512,512]{1,0:T(8,128)}, f32[512,512]{1,0:T(8,128)}) async-done(((f32[512,512]{1,0:T(8,128)}, f32[512,512]{1,0:T(8,128)}), (f32[512,512]{1,0:T(8,128)}, f32[512,512]{1,0:T(8,128)})) %all-reduce.3.cloned.1.call-update) | async-done | bytes 2097168 | tf_op jit(solution)/shard_map/psum | solution.py:114
  (501 shorter events, 1066.8 us)
Async XLA Ops:
  7.2 549.7 %copy-start = (bf16[512,512]{1,0:T(8,128)(2,1)S(1)}, bf16[512,512]{1,0:T(8,128)(2,1)}, u32[]{:S(2)}) copy-start(bf16[512,512]{1,0:T(8,128)(2,1)} %param.25) | copy-start | bytes 1572868
  7.2 549.7 %reduce-scatter.4.cloned.1.call-start = ((), (), s32[]{:S(2)}) async-start(), calls=%async_computation.3 | async-start | bytes 4718592 | tf_op jit(solution)/shard_map/reduce_scatter | solution.py:72
  10.0 4.3 copy-start.5
  457.4 1.0 copy-start.1
  457.4 1.2 copy-start.3
  457.4 147.0 %all-gather.5.cloned.1.call-start = ((), (), s32[]{:S(2)}) async-start(), calls=%async_computation.6 | async-start | bytes 4718592 | tf_op jit(solution)/shard_map/all_gather | solution.py:96
  459.9 500.8 %all-gather.3.cloned.1.call-start = ((), (), s32[]{:S(2)}) async-start(), calls=%async_computation.4 | async-start | bytes 2621440 | tf_op jit(solution)/shard_map/all_gather | solution.py:85
  559.5 852.1 %reduce-scatter.8.cloned.1.call-start = ((), (), s32[]{:S(2)}) async-start(), calls=%async_computation.7 | async-start | bytes 2621440 | tf_op jit(solution)/shard_map/reduce_scatter | solution.py:102
  960.6 595.2 %reduce-scatter.6.cloned.1.call-start = ((), (), s32[]{:S(2)}) async-start(), calls=%async_computation.5 | async-start | bytes 4718592 | tf_op jit(solution)/shard_map/reduce_scatter | solution.py:72
  1411.4 1.0 copy-start.4
  1411.5 283.5 %all-reduce.3.cloned.1.call-start = ((), (), s32[]{:S(2)}) async-start(), calls=%async_computation.8 | async-start | bytes 4194304 | tf_op jit(solution)/shard_map/psum | solution.py:114
  1555.8 2.7 copy-start.2
Sparse Core Ops, SparseCore 0:
  457.5 99.3 reduce-scatter.3
  559.1 45.2 all-gather.4
  606.8 34.0 all-gather.2
  960.8 78.8 reduce-scatter.7
  1411.6 144.1 reduce-scatter.5
  1562.7 132.1 all-reduce.2
where the time goes:
time: 1720 us; the launch traced here: 1710 us
  loops' own time  598 us (35%)
  local copies, waits for them, and re-layouts  464 us (27%)
  waiting for transfers between devices  417 us (24%)
  matrix products  194 us (11%)
  other arithmetic  18.4 us (1%)
    another operation x2, loops' own time, forward_term(): return lax.fori_loop(0, number, forward_advance, zeroed)  283 us
    dynamic_update_slice x86, local copies, waits for them, and re-layouts, forward_accumulate(): lax.dynamic_update_slice_in_dim(current, previous + product, row_start, 0)  253 us
    reduce_scatter x2, waiting for transfers between devices, aggregate(): lax.psum_scatter(term(jnp.int32(0), piece_rows * lax.axis_size('col')).as...  237 us
    another operation x86, loops' own time, forward_advance(): lax.cond(inside, forward_accumulate, lambda current: current, running)  171 us
    psum x1, waiting for transfers between devices, per_device(): grad_first = lax.psum(first_local, ('row', 'col'))  135 us
    dot_general x86, matrix products, forward_accumulate(): jnp.dot(tiles_here[position], segment, preferred_element_type=jnp.float32)  120 us
    dynamic_update_slice x43, local copies, waits for them, and re-layouts, backward_accumulate(): lax.dynamic_update_slice_in_dim(current, previous + product, row_start, 0)  118 us
    another operation x1, loops' own time, backward_term(): return lax.fori_loop(0, number, backward_advance, zeroed)  114 us
  transfers between devices with their start and end apart: 6, of which 4 were waited for; matrix products, arithmetic and copies ran while one was open for 26% of the time, Pallas kernels for 0%

commit v1 on v0

v1 whole, which is shorter than its diff:
```python
import functools

import jax
import jax.numpy as jnp
from jax import lax
from jax.experimental import pallas as pl
from jax.experimental.pallas import tpu as pltpu
from jax.sharding import PartitionSpec as P

F32 = jnp.float32
BF16 = jnp.bfloat16
VMEM_BYTES = 44 * 1024 * 1024
VMEM = pl.BlockSpec(memory_space=pltpu.VMEM)
SMEM = pl.BlockSpec(memory_space=pltpu.SMEM)
ANY = pl.BlockSpec(memory_space=pl.ANY)


def nbytes(items):
    return sum(x.size * x.dtype.itemsize for x in items)


def run(body, args, specs, outs, scratch=(), flops=0, trans=0):
    return pl.pallas_call(
        body,
        out_shape=outs,
        in_specs=specs,
        out_specs=[VMEM] * len(outs),
        scratch_shapes=list(scratch),
        compiler_params=pltpu.CompilerParams(vmem_limit_bytes=VMEM_BYTES),
        cost_estimate=pl.CostEstimate(
            flops=flops, bytes_accessed=nbytes(args) + nbytes(outs), transcendentals=trans
        ),
    )(*args)


def shape(dims, dtype=BF16):
    return jax.ShapeDtypeStruct(dims, dtype)


def sort_tiles(count_ref, slot_ref, number_ref, list_ref, local_cols, groups, cap, by_row):
    def clear(g, _):
        number_ref[g] = 0
        return 0

    lax.fori_loop(0, groups, clear, 0)

    def place(s, _):
        p = slot_ref[s]
        u, v = lax.div(p, local_cols), lax.rem(p, local_cols)
        g, other = (u, v) if by_row else (v, u)
        n = number_ref[g]
        list_ref[g * cap + n] = s * 1024 + other
        number_ref[g] = n + 1
        return 0

    lax.fori_loop(0, count_ref[0], place, 0)


def tile_copy(tiles_ref, held, sems, s):
    return pltpu.make_async_copy(tiles_ref.at[s], held.at[s], sems.at[s])


def start_group(g, tiles_ref, held, sems, number_ref, list_ref, cap):
    def one(j, _):
        tile_copy(tiles_ref, held, sems, list_ref[g * cap + j] // 1024).start()
        return 0

    lax.fori_loop(0, number_ref[g], one, 0)


def sum_group(g, tiles_ref, held, sems, number_ref, list_ref, cap, total, product):
    n = number_ref[g]
    odd = lax.rem(n, 2)

    def fetch(j):
        entry = list_ref[g * cap + j]
        s = entry // 1024
        tile_copy(tiles_ref, held, sems, s).wait()
        return s, lax.rem(entry, 1024)

    @pl.when(odd == 1)
    def _():
        total[...] = product([fetch(0)])

    @pl.when(odd == 0)
    def _():
        total[...] = jnp.zeros_like(total)

    def pair(m, _):
        first = fetch(odd + 2 * m)
        second = fetch(odd + 2 * m + 1)
        total[...] += product([first, second])
        return 0

    lax.fori_loop(0, lax.div(n, 2), pair, 0)


def forward_body(scaled, half, local_cols, cap, *refs):
    count_ref, slot_ref, tiles_ref = refs[:3]
    give, keep, held, source, total, sems, source_sems, number_ref, list_ref = refs[-9:]
    inputs = refs[3:-9]
    col = lax.axis_index("col")
    parts = give.shape[0]
    sort_tiles(count_ref, slot_ref, number_ref, list_ref, local_cols, 4 * parts, cap, True)

    def block_row(i, flip):
        return (col ^ (2 * i + flip)) * 2 + half

    if scaled:
        mask = 0
    else:
        mask = lax.axis_index("row") * 2
        copies = [
            pltpu.make_async_copy(x, source.at[i], source_sems.at[i]) for i, x in enumerate(inputs)
        ]
        for copy in copies:
            copy.start()
    for flip in (1, 0):

        def start(i, _):
            start_group(block_row(i, flip), tiles_ref, held, sems, number_ref, list_ref, cap)
            return 0

        lax.fori_loop(0, parts, start, 0)
    if scaled:
        values, scale = inputs

        def fill(i, _):
            source[i] = (values[i].astype(F32) * scale[i]).astype(BF16)
            return 0

        lax.fori_loop(0, local_cols, fill, 0)
    else:
        for copy in copies:
            copy.wait()

    def product(pieces):
        lhs = [held[s] for s, _ in pieces]
        rhs = [source[v ^ mask] for _, v in pieces]
        return jnp.dot(
            jnp.concatenate(lhs, 1), jnp.concatenate(rhs, 0), preferred_element_type=F32
        )

    for flip, out in ((1, give), (0, keep)):

        def block(i, _):
            sum_group(
                block_row(i, flip), tiles_ref, held, sems, number_ref, list_ref, cap, total, product
            )
            out[i] = total[...].astype(BF16)
            return 0

        lax.fori_loop(0, parts, block, 0)


def forward(count, slots, tiles, sources, scaled, half, local_cols, n_col):
    slots_n, edge, _ = tiles.shape
    width = sources[0].shape[-1]
    outs = [shape((n_col // 2, edge, width))] * 2
    return run(
        functools.partial(forward_body, scaled, half, local_cols, local_cols),
        (count, slots, tiles, *sources),
        [SMEM, SMEM, ANY] + ([VMEM] if scaled else [ANY]) * len(sources),
        outs,
        [
            pltpu.VMEM(tiles.shape, BF16),
            pltpu.VMEM((local_cols, edge, width), BF16),
            pltpu.VMEM((edge, width), F32),
            pltpu.SemaphoreType.DMA((slots_n,)),
            pltpu.SemaphoreType.DMA((local_cols,)),
            pltpu.SMEM((2 * n_col,), jnp.int32),
            pltpu.SMEM((2 * n_col * local_cols,), jnp.int32),
        ],
        flops=slots_n * edge * edge * width,
    )


def backward_body(local_cols, cap, n_in, *refs):
    count_ref, slot_ref, tiles_ref = refs[:3]
    inputs = refs[3 : 3 + n_in]
    outs = refs[3 + n_in : -7]
    held, source, total, sems, source_sems, number_ref, list_ref = refs[-7:]
    sort_tiles(count_ref, slot_ref, number_ref, list_ref, local_cols, local_cols, cap, False)
    mask = lax.axis_index("col") * 2
    row = lax.axis_index("row")
    copies = [
        pltpu.make_async_copy(x, source.at[pl.ds(2 * i, 2)], source_sems.at[i])
        for i, x in enumerate(inputs)
    ]
    for copy in copies:
        copy.start()
    order = list(range(1, len(outs))) + [0]
    for j in order:
        for e in range(2):
            start_group(
                (row ^ j) * 2 + e, tiles_ref, held, sems, number_ref, list_ref, cap
            )
    for copy in copies:
        copy.wait()

    def product(pieces):
        lhs = [source[u ^ mask] for _, u in pieces]
        rhs = [held[s] for s, _ in pieces]
        return jnp.dot(
            jnp.concatenate(lhs, 1), jnp.concatenate(rhs, 0), preferred_element_type=F32
        )

    for j in order:

        def block(e, _):
            sum_group(
                (row ^ j) * 2 + e, tiles_ref, held, sems, number_ref, list_ref, cap, total, product
            )
            outs[j][e] = total[...].astype(BF16)
            return 0

        lax.fori_loop(0, 2, block, 0)


def backward(count, slots, tiles, sources, n_row, n_col):
    slots_n, edge, _ = tiles.shape
    _, width, _ = sources[0].shape
    local_cols, block_rows = 2 * n_row, 2 * n_col
    return run(
        functools.partial(backward_body, local_cols, block_rows, len(sources)),
        (count, slots, tiles, *sources),
        [SMEM, SMEM, ANY] + [ANY] * len(sources),
        [shape((2, width, edge))] * n_row,
        [
            pltpu.VMEM(tiles.shape, BF16),
            pltpu.VMEM((block_rows, width, edge), BF16),
            pltpu.VMEM((width, edge), F32),
            pltpu.SemaphoreType.DMA((slots_n,)),
            pltpu.SemaphoreType.DMA((len(sources),)),
            pltpu.SMEM((local_cols,), jnp.int32),
            pltpu.SMEM((block_rows * local_cols,), jnp.int32),
        ],
        flops=2 * slots_n * edge * edge * width,
    )


def pair_sum_body(n, keep, come, *outs):
    for j in range(n):
        outs[j][...] = (keep[j].astype(F32) + come[j].astype(F32)).astype(BF16)


def pair_sum(keep, come):
    n = keep.shape[0]
    return run(
        functools.partial(pair_sum_body, n),
        (keep, come),
        [VMEM] * 2,
        [shape(keep.shape[1:])] * n,
        flops=keep.size,
    )


def tree(items):
    while len(items) > 1:
        items = [a + b for a, b in zip(items[::2], items[1::2])]
    return items[0]


def first_body(n, *refs):
    scale, weight = refs[n], refs[n + 1]
    agg, pre, out = refs[n + 2 :]
    summed = tree([x[...].astype(F32) for x in refs[:n]])
    agg[...] = (summed * scale[...]).astype(BF16)
    value = jnp.dot(agg[...], weight[...], preferred_element_type=F32)
    pre[...] = value
    out[...] = (jax.nn.gelu(value) * scale[...]).astype(BF16)


def first_layer(parts, scale, weight):
    dims = parts[0].shape
    return run(
        functools.partial(first_body, len(parts)),
        (*parts, scale, weight),
        [VMEM] * (len(parts) + 2),
        [shape(dims), shape(dims, F32), shape(dims)],
        flops=2 * dims[0] * weight.size,
        trans=dims[0] * dims[1],
    )


def second_body(n, *refs):
    scale, weight, out = refs[n], refs[n + 1], refs[n + 2]
    summed = tree([x[...].astype(F32) for x in refs[:n]])
    agg = (summed * scale[...]).astype(BF16)
    out[...] = jnp.dot(agg, weight[...], preferred_element_type=F32).astype(BF16)


def second_layer(parts, scale, weight):
    dims = parts[0].shape
    return run(
        functools.partial(second_body, len(parts)),
        (*parts, scale, weight),
        [VMEM] * (len(parts) + 2),
        [shape(dims)],
        flops=2 * dims[0] * weight.size,
    )[0]


def grad_body(n, *refs):
    parts = refs[:n]
    (agg0, agg1, pre0, pre1, out0, out1, scale, weight, give, keep) = refs[n:]
    core = lax.rem(lax.axis_index("col"), 2)
    first, second = 0.0, 0.0
    for e, (agg, pre, out) in enumerate(((agg0, pre0, out0), (agg1, pre1, out1))):
        hidden = tree([x[e].astype(F32) for x in parts]).astype(BF16)
        grad_hidden = lax.dot_general(
            hidden, weight[...], (((0,), (1,)), ((), ())), preferred_element_type=F32
        )
        _, pullback = jax.vjp(jax.nn.gelu, pre[...])
        grad_pre = pullback(grad_hidden * scale[e])[0].astype(BF16)
        first += lax.dot_general(
            agg[...], grad_pre, (((0,), (0,)), ((), ())), preferred_element_type=F32
        )
        second += lax.dot_general(
            out[...], hidden, (((0,), (1,)), ((), ())), preferred_element_type=F32
        )
    keep[...] = jnp.where(core == 0, first, second).astype(BF16)
    give[...] = jnp.where(core == 0, second, first).astype(BF16)


def weight_grads(parts, aggs, pres, outs, scale, weight):
    return run(
        functools.partial(grad_body, len(parts)),
        (*parts, *aggs, *pres, *outs, scale, weight),
        [VMEM] * (len(parts) + 8),
        [shape(weight.shape)] * 2,
        flops=6 * parts[0].size * weight.shape[0],
        trans=parts[0].size,
    )


def split_body(n, keep, come, *outs):
    row = lax.axis_index("row")
    rows = keep.shape[0] // n
    for j in range(n):
        part = pl.ds(pl.multiple_of((row ^ j) * rows, rows), rows)
        outs[j][...] = (keep[part, :].astype(F32) + come[part, :].astype(F32)).astype(BF16)


def split_sum(keep, come, n):
    rows, width = keep.shape
    return run(
        functools.partial(split_body, n),
        (keep, come),
        [VMEM] * 2,
        [shape((rows // n, width))] * n,
        flops=keep.size,
    )


def sum_body(n, *refs):
    refs[n][...] = tree([x[...].astype(F32) for x in refs[:n]]).astype(BF16)


def sum_parts(parts):
    return run(
        functools.partial(sum_body, len(parts)),
        tuple(parts),
        [VMEM] * len(parts),
        [shape(parts[0].shape)],
        flops=parts[0].size * len(parts),
    )[0]


def join_body(n, *refs):
    row = lax.axis_index("row")
    rows = refs[0].shape[0]
    for j in range(n):
        refs[n][pl.ds(pl.multiple_of((row ^ j) * rows, rows), rows), :] = refs[j][...]


def join(parts):
    rows, width = parts[0].shape
    return run(
        functools.partial(join_body, len(parts)),
        tuple(parts),
        [VMEM] * len(parts),
        [shape((rows * len(parts), width))],
    )[0]


def per_device(features, degree, tile_vals, tile_slot, tile_count, w_first, w_second, cotangent):
    n_row, n_col = lax.axis_size("row"), lax.axis_size("col")
    line = n_col // 2
    piece, width = cotangent.shape
    tiles = tile_vals[0, 0]
    edge = tiles.shape[-1]
    local_cols = n_row * 2
    slots, count = tile_slot[0, 0], tile_count[0]

    def col_send(value, pairs):
        return lax.ppermute(
            value, "col", [(2 * a + k, 2 * b + k) for a, b in pairs for k in range(2)]
        )

    def line_flip(value, j):
        return col_send(value, [(a, a ^ j) for a in range(line)])

    def core_flip(value):
        return lax.ppermute(value, "col", [(a, a ^ 1) for a in range(n_col)])

    def row_flip(value, j):
        return lax.ppermute(value, "row", [(a, a ^ j) for a in range(n_row)])

    def scatter_col(give, keep):
        own = pair_sum(keep, core_flip(give))
        if line != 4:
            return [own[0]] + [line_flip(own[j], j) for j in range(1, line)]
        inward = col_send(own[3], [(0, 1), (3, 2)])
        middle = col_send(own[3], [(1, 2), (2, 1)])
        near = line_flip(own[1], 1)
        far = line_flip((own[2].astype(F32) + inward.astype(F32)).astype(BF16), 2)
        return [own[0], near, middle, far]

    def gather_line(own):
        if line != 4:
            return [own] + [line_flip(own, j) for j in range(1, line)]
        position = lax.axis_index("col") // 2
        at_end = jnp.logical_or(position == 0, position == line - 1)
        near = line_flip(own, 1)
        middle = col_send(own, [(1, 2), (2, 1)])
        across = col_send(near, [(1, 2), (2, 1)])
        out_two = col_send(middle, [(1, 0), (2, 3)])
        out_three = col_send(across, [(1, 0), (2, 3)])
        return [
            own,
            near,
            jnp.where(at_end, out_two, across),
            jnp.where(at_end, out_three, middle),
        ]

    col_scale = (1.0 / jnp.sqrt(degree.astype(F32))).reshape(local_cols, edge, 1)
    own_scale = lax.dynamic_slice_in_dim(col_scale, lax.axis_index("row") * 2, 2, 0)
    halves = piece // edge

    scaled = (
        (cotangent.astype(F32) * own_scale.reshape(piece, 1))
        .astype(BF16)
        .reshape(halves, edge, width)
        .transpose(0, 2, 1)
    )
    gathered = gather_line(scaled)
    ranged = [x for g in gathered for x in (g, core_flip(g))]

    values = features[:, 0].reshape(local_cols, edge, width)
    aggs, pres, outs, spread = [], [], [], []
    for half in range(halves):
        give, keep = forward(
            count, slots, tiles, (values, col_scale), True, half, local_cols, n_col
        )
        agg, pre, out = first_layer(scatter_col(give, keep), own_scale[half], w_first)
        aggs.append(agg)
        pres.append(pre)
        outs.append(out)
        spread.append([out] + [row_flip(out, j) for j in range(1, n_row)])
    sources = [spread[e][j] for j in range(n_row) for e in range(halves)]

    partials = backward(count, slots, tiles, ranged, n_row, n_col)
    hidden = [partials[0]] + [row_flip(partials[j], j) for j in range(1, n_row)]
    give, keep = weight_grads(hidden, aggs, pres, outs, own_scale, w_second)
    parts = split_sum(keep, core_flip(give), n_row)
    part = sum_parts([parts[0]] + [row_flip(parts[j], j) for j in range(1, n_row)])
    part = sum_parts([part] + [line_flip(part, j) for j in range(1, line)])
    mine = join([part] + [row_flip(part, j) for j in range(1, n_row)])
    other = core_flip(mine)
    core = lax.rem(lax.axis_index("col"), 2)
    grad_first = jnp.where(core == 0, mine, other).astype(F32)
    grad_second = jnp.where(core == 0, other, mine).astype(F32)

    logits = []
    for half in range(halves):
        give, keep = forward(count, slots, tiles, sources, False, half, local_cols, n_col)
        logits.append(second_layer(scatter_col(give, keep), own_scale[half], w_second))
    return jnp.concatenate(logits, 0), grad_first, grad_second


def solution(mesh):
    return jax.shard_map(
        per_device,
        mesh=mesh,
        in_specs=(
            P(None, "col", None, None),
            P(None, "col", None),
            P("row", "col", None, None, None),
            P("row", "col", None),
            P("row", "col"),
            P(),
            P(),
            P(("row", "col"), None),
        ),
        out_specs=(P(("row", "col"), None), P(), P()),
        check_vma=False,
    )
```

time: 1720 us -> 240 us (0.14)
  loops' own time: 598 us -> 0 us
  local copies, waits for them, and re-layouts: 464 us -> 14.4 us
  waiting for transfers between devices: 417 us -> 99.9 us
  matrix products: 194 us -> 0 us
  starting transfers between devices: 0.25 us -> 66.7 us
  Pallas kernels: 0 us -> 47.7 us
    another operation x132 -> x0, loops' own time: 598 us -> none  [the longest x2 283 us: forward_term(): return lax.fori_loop(0, number, forward_advance, zeroed)]
    dynamic_update_slice x129 -> x0, local copies, waits for them, and re-layouts: 370 us -> none  [the longest x86 253 us: forward_accumulate(): lax.dynamic_update_slice_in_dim(current, previous + product, row_start, 0)]
    reduce_scatter x3 -> x0, waiting for transfers between devices: 237 us -> none  [the longest x2 237 us: aggregate(): lax.psum_scatter(term(jnp.int32(0), piece_rows * lax.axis_size('col')).as...]
    dot_general x134 -> x0, matrix products: 194 us -> none  [the longest x86 120 us: forward_accumulate(): jnp.dot(tiles_here[position], segment, preferred_element_type=jnp.float32)]
    psum x1 -> x0, waiting for transfers between devices: 135 us -> none  [per_device(): grad_first = lax.psum(first_local, ('row', 'col'))]
    ppermute x0 -> x49, waiting for transfers between devices: none -> 99.9 us  [the longest x24 75.7 us: col_send(): lax.ppermute(value, 'col', [(2 * a + k, 2 * b + k) for a, b in pairs for...]
    dynamic_slice x130 -> x1, local copies, waits for them, and re-layouts: 75.7 us -> 0.15 us  [per_device(): lax.dynamic_slice_in_dim(col_scale, lax.axis_index('row') * 2, 2, 0)]
    ppermute x0 -> x49, starting transfers between devices: none -> 66.7 us  [the longest x24 48 us: col_send(): lax.ppermute(value, 'col', [(2 * a + k, 2 * b + k) for a, b in pairs for...]
  transfers between devices with their start and end apart: 6 -> 49, of which waited for: 4 -> 17; matrix products, arithmetic and copies ran while one was open for 26% -> 3% of each run, Pallas kernels for 0% -> 17%
where the time goes in v1:
time: 240 us; the launch traced here: 239 us
  waiting for transfers between devices  99.9 us (42%)
  starting transfers between devices  66.7 us (28%)
  Pallas kernels  47.7 us (20%)
  local copies, waits for them, and re-layouts  14.4 us (6%)
  other arithmetic  8.89 us (4%)
    ppermute x24, waiting for transfers between devices, col_send(): lax.ppermute(value, 'col', [(2 * a + k, 2 * b + k) for a, b in pairs for...  75.7 us
    ppermute x24, starting transfers between devices, col_send(): lax.ppermute(value, 'col', [(2 * a + k, 2 * b + k) for a, b in pairs for...  48 us
    pallas_call x18, Pallas kernels, run(): pl.pallas_call(body, out_shape=outs, in_specs=specs, out_specs=[VMEM] * l...  47.7 us
    ppermute x15, waiting for transfers between devices, row_flip(): return lax.ppermute(value, 'row', [(a, a ^ j) for a in range(n_row)])  22.2 us
    ppermute x15, starting transfers between devices, row_flip(): return lax.ppermute(value, 'row', [(a, a ^ j) for a in range(n_row)])  17.7 us
    unnamed x39, local copies, waits for them, and re-layouts  11.3 us
  transfers between devices with their start and end apart: 49, of which 17 were waited for; matrix products, arithmetic and copies ran while one was open for 3% of the time, Pallas kernels for 17%

profile of v1, /device:TPU:0, one launch (start us, length us, event | category | flops | bytes accessed | tf_op | source)
XLA Modules:
  0.0 239.4 jit_solution(4146100958697692561)
XLA Ops:
  2.9 1.6 copy-done
  5.2 7.9 %shard_map.106 = (bf16[4,256,512]{2,1,0:T(8,128)(2,1)}, bf16[4,256,512]{2,1,0:T(8,128)(2,1)S(1)}) custom-call(s32[1]{0:T(128)} %bitcast.13.refs_0_, s32[48]{0:T(128)S(1)} %bitcast.19, bf16[48,256,256]{2,1,0:T(8,128)(2,1)} %bitcast.24, bf16[8,256,512]{2,1,0:T(8,128)(2,1)S(1)} %bitcast.17, f32[8,256,1]{2,1,0:T(8,128)S(1)} %reshape.16.refs_4_), custom_call_target="tpu_custom_call" | custom-call | flops 1610612736 | bytes 10494148 | tf_op jit(solution)/shard_map/pallas_call | solution.py:23
  13.1 7.1 %shard_map.103 = (bf16[4,256,512]{2,1,0:T(8,128)(2,1)}, bf16[4,256,512]{2,1,0:T(8,128)(2,1)S(1)}) custom-call(s32[1]{0:T(128)} %bitcast.12.refs_0_, s32[48]{0:T(128)S(1)} %bitcast.20, bf16[48,256,256]{2,1,0:T(8,128)(2,1)} %bitcast.25, bf16[8,256,512]{2,1,0:T(8,128)(2,1)S(1)} %bitcast.18, f32[8,256,1]{2,1,0:T(8,128)S(1)} %reshape.16.refs_4_), custom_call_target="tpu_custom_call" | custom-call | flops 1610612736 | bytes 10494148 | tf_op jit(solution)/shard_map/pallas_call | solution.py:23
  20.5 2.0 multiply_convert_fusion
  22.5 2.0 copy.14
  24.5 4.7 %collective-permute-start.27 = (bf16[2,512,256]{2,1,0:T(8,128)(2,1)}, bf16[2,512,256]{2,1,0:T(8,128)(2,1)}, u32[]{:S(2)}, u32[]{:S(2)}) collective-permute-start(bf16[2,512,256]{2,1,0:T(8,128)(2,1)} %bitcast.7.refs_3_), channel_id=1, source_target_pairs={{0,2},{1,3},{2,0},{3,1},{4,6},{5,7},{6,4},{7,5},{8,10},{9,11},{10,... | collective-permute-start | bytes 1572872 | tf_op jit(solution)/shard_map/ppermute | solution.py:397
  29.2 1.5 collective-permute-start.29
  30.7 10.9 %collective-permute-done.27.refs_5_ = bf16[2,512,256]{2,1,0:T(8,128)(2,1)} collective-permute-done((bf16[2,512,256]{2,1,0:T(8,128)(2,1)}, bf16[2,512,256]{2,1,0:T(8,128)(2,1)}, u32[]{:S(2)}, u32[]{:S(2)}) %collective-permute-start.27) | collective-permute-done | bytes 524320 | tf_op jit(solution)/shard_map/ppermute | solution.py:397
  41.7 1.5 collective-permute-start.31
  43.1 1.3 collective-permute-start.30
  44.5 1.2 copy-done.4
  45.7 1.5 shard_map.107
  47.2 7.4 %collective-permute-start.8 = (bf16[256,512]{1,0:T(8,128)(2,1)S(1)}, bf16[256,512]{1,0:T(8,128)(2,1)S(1)}, u32[]{:S(2)}, u32[]{:S(2)}) collective-permute-start(bf16[256,512]{1,0:T(8,128)(2,1)S(1)} %get-tuple-element.54), channel_id=1, source_target_pairs={{0,2},{1,3},{6,4},{7,5},{8,10},{9,11},{14,12},{15,13},{16,18},{17,... | collective-permute-start | bytes 786440 | tf_op jit(solution)/shard_map/ppermute | solution.py:397
  55.2 1.5 shard_map.104
  56.7 4.4 %collective-permute-start.3 = (bf16[256,512]{1,0:T(8,128)(2,1)S(1)}, bf16[256,512]{1,0:T(8,128)(2,1)S(1)}, u32[]{:S(2)}, u32[]{:S(2)}) collective-permute-start(bf16[256,512]{1,0:T(8,128)(2,1)S(1)} %get-tuple-element.47), channel_id=1, source_target_pairs={{0,2},{1,3},{6,4},{7,5},{8,10},{9,11},{14,12},{15,13},{16,18},{17,... | collective-permute-start | bytes 786440 | tf_op jit(solution)/shard_map/ppermute | solution.py:397
  61.9 1.3 collective-permute-start.33
  63.2 1.1 broadcast_select_fusion.1.refs_7_
  64.3 3.1 %collective-permute-start.6 = (bf16[256,512]{1,0:T(8,128)(2,1)S(1)}, bf16[256,512]{1,0:T(8,128)(2,1)S(1)}, u32[]{:S(2)}, u32[]{:S(2)}) collective-permute-start(bf16[256,512]{1,0:T(8,128)(2,1)S(1)} %get-tuple-element.53), channel_id=1, source_target_pairs={{0,2},{1,3},{2,0},{3,1},{4,6},{5,7},{6,4},{7,5},{8,10},{9,11},{10,... | collective-permute-start | bytes 786440 | tf_op jit(solution)/shard_map/ppermute | solution.py:397
  69.0 15.6 %collective-permute-done.6.refs_1_ = bf16[256,512]{1,0:T(8,128)(2,1)S(1)} collective-permute-done((bf16[256,512]{1,0:T(8,128)(2,1)S(1)}, bf16[256,512]{1,0:T(8,128)(2,1)S(1)}, u32[]{:S(2)}, u32[]{:S(2)}) %collective-permute-start.6) | collective-permute-done | bytes 262176 | tf_op jit(solution)/shard_map/ppermute | solution.py:397
  85.8 1.6 collective-permute-done.1.refs_1_
  88.1 2.9 %collective-permute-start.4 = (bf16[256,512]{1,0:T(8,128)(2,1)}, bf16[256,512]{1,0:T(8,128)(2,1)}, u32[]{:S(2)}, u32[]{:S(2)}) collective-permute-start(bf16[256,512]{1,0:T(8,128)(2,1)} %add_convert_fusion.3), channel_id=1, source_target_pairs={{0,4},{1,5},{2,6},{3,7},{4,0},{5,1},{6,2},{7,3},{8,12},{9,13},{10,... | collective-permute-start | bytes 786440 | tf_op jit(solution)/shard_map/ppermute | solution.py:397
  91.1 14.9 %collective-permute-done.9.refs_3_ = bf16[256,512]{1,0:T(8,128)(2,1)S(1)} collective-permute-done((bf16[256,512]{1,0:T(8,128)(2,1)S(1)}, bf16[256,512]{1,0:T(8,128)(2,1)S(1)}, u32[]{:S(2)}, u32[]{:S(2)}) %collective-permute-start.9) | collective-permute-done | bytes 262176 | tf_op jit(solution)/shard_map/ppermute | solution.py:397
  107.7 0.9 copy-done.14
  108.7 0.9 copy-done.16
  110.2 1.5 collective-permute-done.4.refs_3_
  111.6 1.2 collective-permute-start.11
  112.8 0.9 copy-done.6
  113.8 0.9 copy-done.10
  114.7 0.9 copy-done.12
  115.7 1.5 shard_map.105
  117.2 1.2 collective-permute-start.13
  118.4 1.1 collective-permute-start.15
  119.5 1.2 collective-permute-start.10
  120.7 1.2 collective-permute-start.12
  121.9 1.1 collective-permute-start.14
  123.0 10.0 %shard_map.115 = (bf16[2,512,256]{2,1,0:T(8,128)(2,1)S(1)}, bf16[2,512,256]{2,1,0:T(8,128)(2,1)S(1)}, bf16[2,512,256]{2,1,0:T(8,128)(2,1)S(1)}, bf16[2,512,256]{2,1,0:T(8,128)(2,1)S(1)}) custom-call(s32[1]{0:T(128)} %bitcast.16.refs_0_, s32[48]{0:T(128)S(1)} %bitcast.21, bf16[48,256,256]{2,1,0:T(8,128)(2,1)} %bitcast.26, ...), custom_call_target="tpu_custom_call" | custom-call | flops 3221225472 | bytes 12583108 | tf_op jit(solution)/shard_map/pallas_call | solution.py:23
  133.8 2.2 collective-permute-start.36
  136.6 6.7 %collective-permute-done.12.refs_7_ = bf16[256,512]{1,0:T(8,128)(2,1)S(1)} collective-permute-done((bf16[256,512]{1,0:T(8,128)(2,1)S(1)}, bf16[256,512]{1,0:T(8,128)(2,1)S(1)}, u32[]{:S(2)}, u32[]{:S(2)}) %collective-permute-start.12) | collective-permute-done | bytes 262176 | tf_op jit(solution)/shard_map/ppermute | solution.py:408
  143.3 5.9 %shard_map.109 = (bf16[4,256,512]{2,1,0:T(8,128)(2,1)S(1)}, bf16[4,256,512]{2,1,0:T(8,128)(2,1)S(1)}) custom-call(s32[1]{0:T(128)} %bitcast.14.refs_0_, s32[48]{0:T(128)S(1)} %bitcast.22, bf16[48,256,256]{2,1,0:T(8,128)(2,1)} %bitcast.27, bf16[256,512]{1,0:T(8,128)(2,1)S(1)} %get-tuple-element.49.refs_3_.refs_8_, ...), custom_call_target="tpu_custom_call" | custom-call | flops 1610612736 | bytes 10485956 | tf_op jit(solution)/shard_map/pallas_call | solution.py:23
  149.3 6.9 %shard_map.112 = (bf16[4,256,512]{2,1,0:T(8,128)(2,1)S(1)}, bf16[4,256,512]{2,1,0:T(8,128)(2,1)S(1)}) custom-call(s32[1]{0:T(128)} %bitcast.15.refs_0_, s32[48]{0:T(128)S(1)} %bitcast.23, bf16[48,256,256]{2,1,0:T(8,128)(2,1)} %bitcast.28, bf16[256,512]{1,0:T(8,128)(2,1)S(1)} %get-tuple-element.49.refs_3_.refs_8_, ...), custom_call_target="tpu_custom_call" | custom-call | flops 1610612736 | bytes 10485956 | tf_op jit(solution)/shard_map/pallas_call | solution.py:23
  156.3 8.1 %collective-permute-done.36.refs_2_ = bf16[2,512,256]{2,1,0:T(8,128)(2,1)S(1)} collective-permute-done((bf16[2,512,256]{2,1,0:T(8,128)(2,1)S(1)}, bf16[2,512,256]{2,1,0:T(8,128)(2,1)S(1)}, u32[]{:S(2)}, u32[]{:S(2)}) %collective-permute-start.36) | collective-permute-done | bytes 524320 | tf_op jit(solution)/shard_map/ppermute | solution.py:408
  164.5 1.8 shard_map.116
  166.3 1.9 collective-permute-done.38.come
  169.3 1.6 collective-permute-start.40
  170.9 1.0 collective-permute-start.41
  172.2 1.3 collective-permute-start.19
  173.5 1.3 collective-permute-done.39.refs_1_
  174.8 1.7 collective-permute-done.40.refs_2_
  177.6 2.7 %collective-permute-start.43 = (bf16[128,512]{1,0:T(8,128)(2,1)S(1)}, bf16[128,512]{1,0:T(8,128)(2,1)S(1)}, u32[]{:S(2)}, u32[]{:S(2)}) collective-permute-start(bf16[128,512]{1,0:T(8,128)(2,1)S(1)} %shard_map.118.refs_0_), channel_id=1, source_target_pairs={{0,4},{1,5},{2,6},{3,7},{4,0},{5,1},{6,2},{7,3},{8,12},{9,13},{10,... | collective-permute-start | bytes 393224 | tf_op jit(solution)/shard_map/ppermute | solution.py:397
  180.3 1.6 collective-permute-start.44
  181.9 2.4 %collective-permute-done.42.refs_1_ = bf16[128,512]{1,0:T(8,128)(2,1)S(1)} collective-permute-done((bf16[128,512]{1,0:T(8,128)(2,1)S(1)}, bf16[128,512]{1,0:T(8,128)(2,1)S(1)}, u32[]{:S(2)}, u32[]{:S(2)}) %collective-permute-start.42) | collective-permute-done | bytes 131104 | tf_op jit(solution)/shard_map/ppermute | solution.py:397
  184.3 5.9 %collective-permute-done.43.refs_2_ = bf16[128,512]{1,0:T(8,128)(2,1)S(1)} collective-permute-done((bf16[128,512]{1,0:T(8,128)(2,1)S(1)}, bf16[128,512]{1,0:T(8,128)(2,1)S(1)}, u32[]{:S(2)}, u32[]{:S(2)}) %collective-permute-start.43) | collective-permute-done | bytes 131104 | tf_op jit(solution)/shard_map/ppermute | solution.py:397
  190.4 1.3 collective-permute-start.45
  191.7 1.0 shard_map.113
  192.7 3.9 %collective-permute-start.24 = (bf16[256,512]{1,0:T(8,128)(2,1)}, bf16[256,512]{1,0:T(8,128)(2,1)S(1)}, u32[]{:S(2)}, u32[]{:S(2)}) collective-permute-start(bf16[256,512]{1,0:T(8,128)(2,1)} %get-tuple-element.67), channel_id=1, source_target_pairs={{0,2},{1,3},{6,4},{7,5},{8,10},{9,11},{14,12},{15,13},{16,18},{17,... | collective-permute-start | bytes 786440 | tf_op jit(solution)/shard_map/ppermute | solution.py:397
  197.2 2.0 collective-permute-start.17
  199.7 1.7 collective-permute-start.47
  201.5 2.7 %collective-permute-done.46.refs_2_ = bf16[128,512]{1,0:T(8,128)(2,1)S(1)} collective-permute-done((bf16[128,512]{1,0:T(8,128)(2,1)S(1)}, bf16[128,512]{1,0:T(8,128)(2,1)S(1)}, u32[]{:S(2)}, u32[]{:S(2)}) %collective-permute-start.46) | collective-permute-done | bytes 131104 | tf_op jit(solution)/shard_map/ppermute | solution.py:408
  205.6 2.2 collective-permute-start.20
  208.7 2.7 %collective-permute-start.25 = (bf16[256,512]{1,0:T(8,128)(2,1)}, bf16[256,512]{1,0:T(8,128)(2,1)}, u32[]{:S(2)}, u32[]{:S(2)}) collective-permute-start(bf16[256,512]{1,0:T(8,128)(2,1)} %add_convert_fusion), channel_id=1, source_target_pairs={{0,4},{1,5},{2,6},{3,7},{4,0},{5,1},{6,2},{7,3},{8,12},{9,13},{10,... | collective-permute-start | bytes 786440 | tf_op jit(solution)/shard_map/ppermute | solution.py:397
  211.4 19.8 %collective-permute-done.20.refs_3_ = bf16[256,512]{1,0:T(8,128)(2,1)S(1)} collective-permute-done((bf16[256,512]{1,0:T(8,128)(2,1)S(1)}, bf16[256,512]{1,0:T(8,128)(2,1)S(1)}, u32[]{:S(2)}, u32[]{:S(2)}) %collective-permute-start.20) | collective-permute-done | bytes 262176 | tf_op jit(solution)/shard_map/ppermute | solution.py:397
  231.6 3.1 %collective-permute-done.25.refs_3_ = bf16[256,512]{1,0:T(8,128)(2,1)} collective-permute-done((bf16[256,512]{1,0:T(8,128)(2,1)}, bf16[256,512]{1,0:T(8,128)(2,1)}, u32[]{:S(2)}, u32[]{:S(2)}) %collective-permute-start.25) | collective-permute-done | bytes 262176 | tf_op jit(solution)/shard_map/ppermute | solution.py:397
  234.7 1.4 shard_map.114
  236.9 2.5 %select_convert_fusion = (f32[512,512]{1,0:T(8,128)}, f32[512,512]{1,0:T(8,128)}) fusion(bf16[512,512]{1,0:T(8,128)(2,1)} %collective-permute-done.48, bf16[512,512]{1,0:T(8,128)(2,1)S(1)} %shard_map.120, pred[]{:T(512)S(6)} %eq.10), kind=kLoop, calls=%fused_computation.2 | loop fusion | flops 1048576 | bytes 3145729 | tf_op jit(solution)/shard_map/convert_element_type | solution.py:473
  (105 shorter events, 18.6 us)
Async XLA Ops:
  2.9 1.6 copy-start
  13.1 7.2 %copy-start.3 = (bf16[4,256,512]{2,1,0:T(8,128)(2,1)}, bf16[4,256,512]{2,1,0:T(8,128)(2,1)S(1)}, u32[]{:S(2)}) copy-start(bf16[4,256,512]{2,1,0:T(8,128)(2,1)S(1)} %get-tuple-element.50.keep) | copy-start | bytes 3145732
  13.1 31.4 %collective-permute-start.5 = (bf16[4,256,512]{2,1,0:T(8,128)(2,1)}, bf16[4,256,512]{2,1,0:T(8,128)(2,1)}, u32[]{:S(2)}, u32[]{:S(2)}) collective-permute-start(bf16[4,256,512]{2,1,0:T(8,128)(2,1)} %get-tuple-element.51), channel_id=1, source_target_pairs={{0,1},{1,0},{2,3},{3,2},{4,5},{5,4},{6,7},{7,6},{8,9},{9,8},{10,11... | collective-permute-start | bytes 3145736 | tf_op jit(solution)/shard_map/ppermute | solution.py:405
  20.2 86.5 %copy-start.2 = (bf16[512,512]{1,0:T(8,128)(2,1)S(1)}, bf16[512,512]{1,0:T(8,128)(2,1)}, u32[]{:S(2)}) copy-start(bf16[512,512]{1,0:T(8,128)(2,1)} %refs_5_.5) | copy-start | bytes 1572868
  20.2 35.0 %collective-permute-start = (bf16[4,256,512]{2,1,0:T(8,128)(2,1)}, bf16[4,256,512]{2,1,0:T(8,128)(2,1)}, u32[]{:S(2)}, u32[]{:S(2)}) collective-permute-start(bf16[4,256,512]{2,1,0:T(8,128)(2,1)} %get-tuple-element.44), channel_id=1, source_target_pairs={{0,1},{1,0},{2,3},{3,2},{4,5},{5,4},{6,7},{7,6},{8,9},{9,8},{10,11... | collective-permute-start | bytes 3145736 | tf_op jit(solution)/shard_map/ppermute | solution.py:405
  24.5 17.1 %collective-permute-start.27 = (bf16[2,512,256]{2,1,0:T(8,128)(2,1)}, bf16[2,512,256]{2,1,0:T(8,128)(2,1)}, u32[]{:S(2)}, u32[]{:S(2)}) collective-permute-start(bf16[2,512,256]{2,1,0:T(8,128)(2,1)} %bitcast.7.refs_3_), channel_id=1, source_target_pairs={{0,2},{1,3},{2,0},{3,1},{4,6},{5,7},{6,4},{7,5},{8,10},{9,11},{10,... | collective-permute-start | bytes 1572872 | tf_op jit(solution)/shard_map/ppermute | solution.py:397
  29.2 13.9 %collective-permute-start.29 = (bf16[2,512,256]{2,1,0:T(8,128)(2,1)}, bf16[2,512,256]{2,1,0:T(8,128)(2,1)}, u32[]{:S(2)}, u32[]{:S(2)}) collective-permute-start(bf16[2,512,256]{2,1,0:T(8,128)(2,1)} %bitcast.7.refs_3_), channel_id=1, source_target_pairs={{2,4},{3,5},{4,2},{5,3},{10,12},{11,13},{12,10},{13,11},{18,20},{1... | collective-permute-start | bytes 1572872 | tf_op jit(solution)/shard_map/ppermute | solution.py:397
  41.7 19.5 %collective-permute-start.31 = (bf16[2,512,256]{2,1,0:T(8,128)(2,1)}, bf16[2,512,256]{2,1,0:T(8,128)(2,1)}, u32[]{:S(2)}, u32[]{:S(2)}) collective-permute-start(bf16[2,512,256]{2,1,0:T(8,128)(2,1)} %collective-permute-done.27.refs_5_), channel_id=1, source_target_pairs={{2,4},{3,5},{4,2},{5,3},{10,12},{11,13},{12,10},{13,11},{18,20},{1... | collective-permute-start | bytes 1572872 | tf_op jit(solution)/shard_map/ppermute | solution.py:397
  43.1 18.7 %collective-permute-start.30 = (bf16[2,512,256]{2,1,0:T(8,128)(2,1)}, bf16[2,512,256]{2,1,0:T(8,128)(2,1)}, u32[]{:S(2)}, u32[]{:S(2)}) collective-permute-start(bf16[2,512,256]{2,1,0:T(8,128)(2,1)} %collective-permute-done.29), channel_id=1, source_target_pairs={{2,0},{3,1},{4,6},{5,7},{10,8},{11,9},{12,14},{13,15},{18,16},{19,... | collective-permute-start | bytes 1572872 | tf_op jit(solution)/shard_map/ppermute | solution.py:397
  44.5 1.2 copy-start.4
  45.7 77.4 %copy-start.18 = (s32[1,1,48]{2,1,0:T(1,128)S(1)}, s32[1,1,48]{2,1,0:T(1,128)}, u32[]{:S(2)}) copy-start(s32[1,1,48]{2,1,0:T(1,128)} %param.11) | copy-start | bytes 580
  47.2 17.1 %collective-permute-start.8 = (bf16[256,512]{1,0:T(8,128)(2,1)S(1)}, bf16[256,512]{1,0:T(8,128)(2,1)S(1)}, u32[]{:S(2)}, u32[]{:S(2)}) collective-permute-start(bf16[256,512]{1,0:T(8,128)(2,1)S(1)} %get-tuple-element.54), channel_id=1, source_target_pairs={{0,2},{1,3},{6,4},{7,5},{8,10},{9,11},{14,12},{15,13},{16,18},{17,... | collective-permute-start | bytes 786440 | tf_op jit(solution)/shard_map/ppermute | solution.py:397
  54.5 14.4 %collective-permute-start.7 = (bf16[256,512]{1,0:T(8,128)(2,1)S(1)}, bf16[256,512]{1,0:T(8,128)(2,1)S(1)}, u32[]{:S(2)}, u32[]{:S(2)}) collective-permute-start(bf16[256,512]{1,0:T(8,128)(2,1)S(1)} %get-tuple-element.54), channel_id=1, source_target_pairs={{2,4},{3,5},{4,2},{5,3},{10,12},{11,13},{12,10},{13,11},{18,20},{1... | collective-permute-start | bytes 786440 | tf_op jit(solution)/shard_map/ppermute | solution.py:397
  56.7 34.4 %copy-start.5 = (bf16[256,512]{1,0:T(8,128)(2,1)}, bf16[256,512]{1,0:T(8,128)(2,1)S(1)}, u32[]{:S(2)}) copy-start(bf16[256,512]{1,0:T(8,128)(2,1)S(1)} %get-tuple-element.45.refs_0_) | copy-start | bytes 786436
  56.7 10.7 %collective-permute-start.3 = (bf16[256,512]{1,0:T(8,128)(2,1)S(1)}, bf16[256,512]{1,0:T(8,128)(2,1)S(1)}, u32[]{:S(2)}, u32[]{:S(2)}) collective-permute-start(bf16[256,512]{1,0:T(8,128)(2,1)S(1)} %get-tuple-element.47), channel_id=1, source_target_pairs={{0,2},{1,3},{6,4},{7,5},{8,10},{9,11},{14,12},{15,13},{16,18},{17,... | collective-permute-start | bytes 786440 | tf_op jit(solution)/shard_map/ppermute | solution.py:397
  61.2 24.1 %collective-permute-start.2 = (bf16[256,512]{1,0:T(8,128)(2,1)S(1)}, bf16[256,512]{1,0:T(8,128)(2,1)S(1)}, u32[]{:S(2)}, u32[]{:S(2)}) collective-permute-start(bf16[256,512]{1,0:T(8,128)(2,1)S(1)} %get-tuple-element.47), channel_id=1, source_target_pairs={{2,4},{3,5},{4,2},{5,3},{10,12},{11,13},{12,10},{13,11},{18,20},{1... | collective-permute-start | bytes 786440 | tf_op jit(solution)/shard_map/ppermute | solution.py:397
  61.9 26.2 %collective-permute-start.33 = (bf16[2,512,256]{2,1,0:T(8,128)(2,1)}, bf16[2,512,256]{2,1,0:T(8,128)(2,1)S(1)}, u32[]{:S(2)}, u32[]{:S(2)}) collective-permute-start(bf16[2,512,256]{2,1,0:T(8,128)(2,1)} %collective-permute-done.31), channel_id=1, source_target_pairs={{2,0},{3,1},{4,6},{5,7},{10,8},{11,9},{12,14},{13,15},{18,16},{19,... | collective-permute-start | bytes 1572872 | tf_op jit(solution)/shard_map/ppermute | solution.py:397
  64.3 20.3 %collective-permute-start.6 = (bf16[256,512]{1,0:T(8,128)(2,1)S(1)}, bf16[256,512]{1,0:T(8,128)(2,1)S(1)}, u32[]{:S(2)}, u32[]{:S(2)}) collective-permute-start(bf16[256,512]{1,0:T(8,128)(2,1)S(1)} %get-tuple-element.53), channel_id=1, source_target_pairs={{0,2},{1,3},{2,0},{3,1},{4,6},{5,7},{6,4},{7,5},{8,10},{9,11},{10,... | collective-permute-start | bytes 786440 | tf_op jit(solution)/shard_map/ppermute | solution.py:397
  67.4 20.0 %collective-permute-start.1 = (bf16[256,512]{1,0:T(8,128)(2,1)S(1)}, bf16[256,512]{1,0:T(8,128)(2,1)S(1)}, u32[]{:S(2)}, u32[]{:S(2)}) collective-permute-start(bf16[256,512]{1,0:T(8,128)(2,1)S(1)} %get-tuple-element.46), channel_id=1, source_target_pairs={{0,2},{1,3},{2,0},{3,1},{4,6},{5,7},{6,4},{7,5},{8,10},{9,11},{10,... | collective-permute-start | bytes 786440 | tf_op jit(solution)/shard_map/ppermute | solution.py:397
  69.0 37.0 %copy-start.7 = (bf16[256,512]{1,0:T(8,128)(2,1)}, bf16[256,512]{1,0:T(8,128)(2,1)S(1)}, u32[]{:S(2)}) copy-start(bf16[256,512]{1,0:T(8,128)(2,1)S(1)} %collective-permute-done.7.refs_2_) | copy-start | bytes 786436
  69.0 48.2 %collective-permute-start.26 = (bf16[2,512,256]{2,1,0:T(8,128)(2,1)}, bf16[2,512,256]{2,1,0:T(8,128)(2,1)}, u32[]{:S(2)}, u32[]{:S(2)}) collective-permute-start(bf16[2,512,256]{2,1,0:T(8,128)(2,1)} %bitcast.7.refs_3_), channel_id=1, source_target_pairs={{0,1},{1,0},{2,3},{3,2},{4,5},{5,4},{6,7},{7,6},{8,9},{9,8},{10,11... | collective-permute-start | bytes 1572872 | tf_op jit(solution)/shard_map/ppermute | solution.py:405
  85.3 33.1 %collective-permute-start.28 = (bf16[2,512,256]{2,1,0:T(8,128)(2,1)}, bf16[2,512,256]{2,1,0:T(8,128)(2,1)}, u32[]{:S(2)}, u32[]{:S(2)}) collective-permute-start(bf16[2,512,256]{2,1,0:T(8,128)(2,1)} %collective-permute-done.27.refs_5_), channel_id=1, source_target_pairs={{0,1},{1,0},{2,3},{3,2},{4,5},{5,4},{6,7},{7,6},{8,9},{9,8},{10,11... | collective-permute-start | bytes 1572872 | tf_op jit(solution)/shard_map/ppermute | solution.py:405
  85.3 20.7 %copy-start.9 = (bf16[256,512]{1,0:T(8,128)(2,1)}, bf16[256,512]{1,0:T(8,128)(2,1)S(1)}, u32[]{:S(2)}) copy-start(bf16[256,512]{1,0:T(8,128)(2,1)S(1)} %collective-permute-done.2.refs_2_) | copy-start | bytes 786436
  85.3 34.2 %collective-permute-start.32 = (bf16[2,512,256]{2,1,0:T(8,128)(2,1)S(1)}, bf16[2,512,256]{2,1,0:T(8,128)(2,1)}, u32[]{:S(2)}, u32[]{:S(2)}) collective-permute-start(bf16[2,512,256]{2,1,0:T(8,128)(2,1)S(1)} %broadcast_select_fusion.1.refs_7_), channel_id=1, source_target_pairs={{0,1},{1,0},{2,3},{3,2},{4,5},{5,4},{6,7},{7,6},{8,9},{9,8},{10,11... | collective-permute-start | bytes 1572872 | tf_op jit(solution)/shard_map/ppermute | solution.py:405
  88.1 17.9 %collective-permute-start.9 = (bf16[256,512]{1,0:T(8,128)(2,1)S(1)}, bf16[256,512]{1,0:T(8,128)(2,1)S(1)}, u32[]{:S(2)}, u32[]{:S(2)}) collective-permute-start(bf16[256,512]{1,0:T(8,128)(2,1)S(1)} %add_convert_fusion.2), channel_id=1, source_target_pairs={{0,4},{1,5},{2,6},{3,7},{4,0},{5,1},{6,2},{7,3},{8,12},{9,13},{10,... | collective-permute-start | bytes 786440 | tf_op jit(solution)/shard_map/ppermute | solution.py:397
  88.1 23.6 %collective-permute-start.4 = (bf16[256,512]{1,0:T(8,128)(2,1)}, bf16[256,512]{1,0:T(8,128)(2,1)}, u32[]{:S(2)}, u32[]{:S(2)}) collective-permute-start(bf16[256,512]{1,0:T(8,128)(2,1)} %add_convert_fusion.3), channel_id=1, source_target_pairs={{0,4},{1,5},{2,6},{3,7},{4,0},{5,1},{6,2},{7,3},{8,12},{9,13},{10,... | collective-permute-start | bytes 786440 | tf_op jit(solution)/shard_map/ppermute | solution.py:397
  106.7 15.2 %collective-permute-start.34 = (bf16[2,512,256]{2,1,0:T(8,128)(2,1)S(1)}, bf16[2,512,256]{2,1,0:T(8,128)(2,1)}, u32[]{:S(2)}, u32[]{:S(2)}) collective-permute-start(bf16[2,512,256]{2,1,0:T(8,128)(2,1)S(1)} %broadcast_select_fusion.refs_9_), channel_id=1, source_target_pairs={{0,1},{1,0},{2,3},{3,2},{4,5},{5,4},{6,7},{7,6},{8,9},{9,8},{10,11... | collective-permute-start | bytes 1572872 | tf_op jit(solution)/shard_map/ppermute | solution.py:405
  106.8 1.0 copy-start.8
  107.7 0.9 copy-start.14
  108.7 0.9 copy-start.16
  111.6 9.1 %collective-permute-start.11 = (bf16[256,512]{1,0:T(8,128)(2,1)S(1)}, bf16[256,512]{1,0:T(8,128)(2,1)S(1)}, u32[]{:S(2)}, u32[]{:S(2)}) collective-permute-start(bf16[256,512]{1,0:T(8,128)(2,1)S(1)} %get-tuple-element.56.refs_4_.refs_9_), channel_id=1, source_target_pairs={{0,8},{8,0},{16,24},{24,16},{1,9},{9,1},{17,25},{25,17},{2,10},{10... | collective-permute-start | bytes 786440 | tf_op jit(solution)/shard_map/ppermute | solution.py:408
  112.8 0.9 copy-start.6
  113.8 0.9 copy-start.10
  114.7 0.9 copy-start.12
  117.2 15.9 %collective-permute-start.13 = (bf16[256,512]{1,0:T(8,128)(2,1)S(1)}, bf16[256,512]{1,0:T(8,128)(2,1)S(1)}, u32[]{:S(2)}, u32[]{:S(2)}) collective-permute-start(bf16[256,512]{1,0:T(8,128)(2,1)S(1)} %get-tuple-element.56.refs_4_.refs_9_), channel_id=1, source_target_pairs={{0,16},{8,24},{16,0},{24,8},{1,17},{9,25},{17,1},{25,9},{2,18},{10... | collective-permute-start | bytes 786440 | tf_op jit(solution)/shard_map/ppermute | solution.py:408
  118.4 15.4 %collective-permute-start.15 = (bf16[256,512]{1,0:T(8,128)(2,1)S(1)}, bf16[256,512]{1,0:T(8,128)(2,1)S(1)}, u32[]{:S(2)}, u32[]{:S(2)}) collective-permute-start(bf16[256,512]{1,0:T(8,128)(2,1)S(1)} %get-tuple-element.56.refs_4_.refs_9_), channel_id=1, source_target_pairs={{0,24},{8,16},{16,8},{24,0},{1,25},{9,17},{17,9},{25,1},{2,26},{10... | collective-permute-start | bytes 786440 | tf_op jit(solution)/shard_map/ppermute | solution.py:408
  119.5 16.4 %collective-permute-start.10 = (bf16[256,512]{1,0:T(8,128)(2,1)S(1)}, bf16[256,512]{1,0:T(8,128)(2,1)S(1)}, u32[]{:S(2)}, u32[]{:S(2)}) collective-permute-start(bf16[256,512]{1,0:T(8,128)(2,1)S(1)} %get-tuple-element.49.refs_3_.refs_8_), channel_id=1, source_target_pairs={{0,8},{8,0},{16,24},{24,16},{1,9},{9,1},{17,25},{25,17},{2,10},{10... | collective-permute-start | bytes 786440 | tf_op jit(solution)/shard_map/ppermute | solution.py:408
  120.7 22.6 %collective-permute-start.12 = (bf16[256,512]{1,0:T(8,128)(2,1)S(1)}, bf16[256,512]{1,0:T(8,128)(2,1)S(1)}, u32[]{:S(2)}, u32[]{:S(2)}) collective-permute-start(bf16[256,512]{1,0:T(8,128)(2,1)S(1)} %get-tuple-element.49.refs_3_.refs_8_), channel_id=1, source_target_pairs={{0,16},{8,24},{16,0},{24,8},{1,17},{9,25},{17,1},{25,9},{2,18},{10... | collective-permute-start | bytes 786440 | tf_op jit(solution)/shard_map/ppermute | solution.py:408
  121.9 21.4 %collective-permute-start.14 = (bf16[256,512]{1,0:T(8,128)(2,1)S(1)}, bf16[256,512]{1,0:T(8,128)(2,1)S(1)}, u32[]{:S(2)}, u32[]{:S(2)}) collective-permute-start(bf16[256,512]{1,0:T(8,128)(2,1)S(1)} %get-tuple-element.49.refs_3_.refs_8_), channel_id=1, source_target_pairs={{0,24},{8,16},{16,8},{24,0},{1,25},{9,17},{17,9},{25,1},{2,26},{10... | collective-permute-start | bytes 786440 | tf_op jit(solution)/shard_map/ppermute | solution.py:408
  133.0 23.3 %collective-permute-start.35 = (bf16[2,512,256]{2,1,0:T(8,128)(2,1)S(1)}, bf16[2,512,256]{2,1,0:T(8,128)(2,1)S(1)}, u32[]{:S(2)}, u32[]{:S(2)}) collective-permute-start(bf16[2,512,256]{2,1,0:T(8,128)(2,1)S(1)} %get-tuple-element.70), channel_id=1, source_target_pairs={{0,8},{8,0},{16,24},{24,16},{1,9},{9,1},{17,25},{25,17},{2,10},{10... | collective-permute-start | bytes 1572872 | tf_op jit(solution)/shard_map/ppermute | solution.py:408
  133.8 30.7 %collective-permute-start.36 = (bf16[2,512,256]{2,1,0:T(8,128)(2,1)S(1)}, bf16[2,512,256]{2,1,0:T(8,128)(2,1)S(1)}, u32[]{:S(2)}, u32[]{:S(2)}) collective-permute-start(bf16[2,512,256]{2,1,0:T(8,128)(2,1)S(1)} %get-tuple-element.71), channel_id=1, source_target_pairs={{0,16},{8,24},{16,0},{24,8},{1,17},{9,25},{17,1},{25,9},{2,18},{10... | collective-permute-start | bytes 1572872 | tf_op jit(solution)/shard_map/ppermute | solution.py:408
  136.0 28.5 %collective-permute-start.37 = (bf16[2,512,256]{2,1,0:T(8,128)(2,1)S(1)}, bf16[2,512,256]{2,1,0:T(8,128)(2,1)S(1)}, u32[]{:S(2)}, u32[]{:S(2)}) collective-permute-start(bf16[2,512,256]{2,1,0:T(8,128)(2,1)S(1)} %get-tuple-element.72), channel_id=1, source_target_pairs={{0,24},{8,16},{16,8},{24,0},{1,25},{9,17},{17,9},{25,1},{2,26},{10... | collective-permute-start | bytes 1572872 | tf_op jit(solution)/shard_map/ppermute | solution.py:408
  149.2 15.3 %copy-start.1 = (bf16[512,512]{1,0:T(8,128)(2,1)S(1)}, bf16[512,512]{1,0:T(8,128)(2,1)}, u32[]{:S(2)}) copy-start(bf16[512,512]{1,0:T(8,128)(2,1)} %refs_11_.1) | copy-start | bytes 1572868
  149.3 22.7 %collective-permute-start.16 = (bf16[4,256,512]{2,1,0:T(8,128)(2,1)S(1)}, bf16[4,256,512]{2,1,0:T(8,128)(2,1)S(1)}, u32[]{:S(2)}, u32[]{:S(2)}) collective-permute-start(bf16[4,256,512]{2,1,0:T(8,128)(2,1)S(1)} %get-tuple-element.58), channel_id=1, source_target_pairs={{0,1},{1,0},{2,3},{3,2},{4,5},{5,4},{6,7},{7,6},{8,9},{9,8},{10,11... | collective-permute-start | bytes 3145736 | tf_op jit(solution)/shard_map/ppermute | solution.py:405
  156.3 35.5 %collective-permute-start.21 = (bf16[4,256,512]{2,1,0:T(8,128)(2,1)S(1)}, bf16[4,256,512]{2,1,0:T(8,128)(2,1)S(1)}, u32[]{:S(2)}, u32[]{:S(2)}) collective-permute-start(bf16[4,256,512]{2,1,0:T(8,128)(2,1)S(1)} %get-tuple-element.64), channel_id=1, source_target_pairs={{0,1},{1,0},{2,3},{3,2},{4,5},{5,4},{6,7},{7,6},{8,9},{9,8},{10,11... | collective-permute-start | bytes 3145736 | tf_op jit(solution)/shard_map/ppermute | solution.py:405
  166.3 2.0 collective-permute-start.38
  168.4 6.4 %collective-permute-start.39 = (bf16[128,512]{1,0:T(8,128)(2,1)S(1)}, bf16[128,512]{1,0:T(8,128)(2,1)S(1)}, u32[]{:S(2)}, u32[]{:S(2)}) collective-permute-start(bf16[128,512]{1,0:T(8,128)(2,1)S(1)} %get-tuple-element.80), channel_id=1, source_target_pairs={{0,8},{8,0},{16,24},{24,16},{1,9},{9,1},{17,25},{25,17},{2,10},{10... | collective-permute-start | bytes 393224 | tf_op jit(solution)/shard_map/ppermute | solution.py:408
  169.3 7.2 %collective-permute-start.40 = (bf16[128,512]{1,0:T(8,128)(2,1)S(1)}, bf16[128,512]{1,0:T(8,128)(2,1)S(1)}, u32[]{:S(2)}, u32[]{:S(2)}) collective-permute-start(bf16[128,512]{1,0:T(8,128)(2,1)S(1)} %get-tuple-element.81), channel_id=1, source_target_pairs={{0,16},{8,24},{16,0},{24,8},{1,17},{9,25},{17,1},{25,9},{2,18},{10... | collective-permute-start | bytes 393224 | tf_op jit(solution)/shard_map/ppermute | solution.py:408
  170.9 6.5 %collective-permute-start.41 = (bf16[128,512]{1,0:T(8,128)(2,1)S(1)}, bf16[128,512]{1,0:T(8,128)(2,1)S(1)}, u32[]{:S(2)}, u32[]{:S(2)}) collective-permute-start(bf16[128,512]{1,0:T(8,128)(2,1)S(1)} %get-tuple-element.82), channel_id=1, source_target_pairs={{0,24},{8,16},{16,8},{24,0},{1,25},{9,17},{17,9},{25,1},{2,26},{10... | collective-permute-start | bytes 393224 | tf_op jit(solution)/shard_map/ppermute | solution.py:408
  172.2 27.0 %collective-permute-start.19 = (bf16[256,512]{1,0:T(8,128)(2,1)S(1)}, bf16[256,512]{1,0:T(8,128)(2,1)S(1)}, u32[]{:S(2)}, u32[]{:S(2)}) collective-permute-start(bf16[256,512]{1,0:T(8,128)(2,1)S(1)} %get-tuple-element.61), channel_id=1, source_target_pairs={{0,2},{1,3},{6,4},{7,5},{8,10},{9,11},{14,12},{15,13},{16,18},{17,... | collective-permute-start | bytes 786440 | tf_op jit(solution)/shard_map/ppermute | solution.py:397
  177.5 6.9 %collective-permute-start.42 = (bf16[128,512]{1,0:T(8,128)(2,1)S(1)}, bf16[128,512]{1,0:T(8,128)(2,1)S(1)}, u32[]{:S(2)}, u32[]{:S(2)}) collective-permute-start(bf16[128,512]{1,0:T(8,128)(2,1)S(1)} %shard_map.118.refs_0_), channel_id=1, source_target_pairs={{0,2},{1,3},{2,0},{3,1},{4,6},{5,7},{6,4},{7,5},{8,10},{9,11},{10,... | collective-permute-start | bytes 393224 | tf_op jit(solution)/shard_map/ppermute | solution.py:397
  177.6 12.7 %collective-permute-start.43 = (bf16[128,512]{1,0:T(8,128)(2,1)S(1)}, bf16[128,512]{1,0:T(8,128)(2,1)S(1)}, u32[]{:S(2)}, u32[]{:S(2)}) collective-permute-start(bf16[128,512]{1,0:T(8,128)(2,1)S(1)} %shard_map.118.refs_0_), channel_id=1, source_target_pairs={{0,4},{1,5},{2,6},{3,7},{4,0},{5,1},{6,2},{7,3},{8,12},{9,13},{10,... | collective-permute-start | bytes 393224 | tf_op jit(solution)/shard_map/ppermute | solution.py:397
  180.3 10.0 %collective-permute-start.44 = (bf16[128,512]{1,0:T(8,128)(2,1)S(1)}, bf16[128,512]{1,0:T(8,128)(2,1)S(1)}, u32[]{:S(2)}, u32[]{:S(2)}) collective-permute-start(bf16[128,512]{1,0:T(8,128)(2,1)S(1)} %shard_map.118.refs_0_), channel_id=1, source_target_pairs={{0,6},{1,7},{2,4},{3,5},{4,2},{5,3},{6,0},{7,1},{8,14},{9,15},{10,... | collective-permute-start | bytes 393224 | tf_op jit(solution)/shard_map/ppermute | solution.py:397
  190.4 9.3 %collective-permute-start.45 = (bf16[128,512]{1,0:T(8,128)(2,1)S(1)}, bf16[128,512]{1,0:T(8,128)(2,1)S(1)}, u32[]{:S(2)}, u32[]{:S(2)}) collective-permute-start(bf16[128,512]{1,0:T(8,128)(2,1)S(1)} %shard_map.119.refs_0_), channel_id=1, source_target_pairs={{0,8},{8,0},{16,24},{24,16},{1,9},{9,1},{17,25},{25,17},{2,10},{10... | collective-permute-start | bytes 393224 | tf_op jit(solution)/shard_map/ppermute | solution.py:408
  192.7 15.1 %collective-permute-start.24 = (bf16[256,512]{1,0:T(8,128)(2,1)}, bf16[256,512]{1,0:T(8,128)(2,1)S(1)}, u32[]{:S(2)}, u32[]{:S(2)}) collective-permute-start(bf16[256,512]{1,0:T(8,128)(2,1)} %get-tuple-element.67), channel_id=1, source_target_pairs={{0,2},{1,3},{6,4},{7,5},{8,10},{9,11},{14,12},{15,13},{16,18},{17,... | collective-permute-start | bytes 786440 | tf_op jit(solution)/shard_map/ppermute | solution.py:397
  196.5 12.2 %collective-permute-start.18 = (bf16[256,512]{1,0:T(8,128)(2,1)S(1)}, bf16[256,512]{1,0:T(8,128)(2,1)S(1)}, u32[]{:S(2)}, u32[]{:S(2)}) collective-permute-start(bf16[256,512]{1,0:T(8,128)(2,1)S(1)} %get-tuple-element.61), channel_id=1, source_target_pairs={{2,4},{3,5},{4,2},{5,3},{10,12},{11,13},{12,10},{13,11},{18,20},{1... | collective-permute-start | bytes 786440 | tf_op jit(solution)/shard_map/ppermute | solution.py:397
  197.2 11.4 %collective-permute-start.17 = (bf16[256,512]{1,0:T(8,128)(2,1)S(1)}, bf16[256,512]{1,0:T(8,128)(2,1)S(1)}, u32[]{:S(2)}, u32[]{:S(2)}) collective-permute-start(bf16[256,512]{1,0:T(8,128)(2,1)S(1)} %get-tuple-element.60), channel_id=1, source_target_pairs={{0,2},{1,3},{2,0},{3,1},{4,6},{5,7},{6,4},{7,5},{8,10},{9,11},{10,... | collective-permute-start | bytes 786440 | tf_op jit(solution)/shard_map/ppermute | solution.py:397
  199.2 5.0 %collective-permute-start.46 = (bf16[128,512]{1,0:T(8,128)(2,1)S(1)}, bf16[128,512]{1,0:T(8,128)(2,1)S(1)}, u32[]{:S(2)}, u32[]{:S(2)}) collective-permute-start(bf16[128,512]{1,0:T(8,128)(2,1)S(1)} %shard_map.119.refs_0_), channel_id=1, source_target_pairs={{0,16},{8,24},{16,0},{24,8},{1,17},{9,25},{17,1},{25,9},{2,18},{10... | collective-permute-start | bytes 393224 | tf_op jit(solution)/shard_map/ppermute | solution.py:408
  199.7 5.9 %collective-permute-start.47 = (bf16[128,512]{1,0:T(8,128)(2,1)S(1)}, bf16[128,512]{1,0:T(8,128)(2,1)S(1)}, u32[]{:S(2)}, u32[]{:S(2)}) collective-permute-start(bf16[128,512]{1,0:T(8,128)(2,1)S(1)} %shard_map.119.refs_0_), channel_id=1, source_target_pairs={{0,24},{8,16},{16,8},{24,0},{1,25},{9,17},{17,9},{25,1},{2,26},{10... | collective-permute-start | bytes 393224 | tf_op jit(solution)/shard_map/ppermute | solution.py:408
  204.2 27.5 %collective-permute-start.23 = (bf16[256,512]{1,0:T(8,128)(2,1)}, bf16[256,512]{1,0:T(8,128)(2,1)S(1)}, u32[]{:S(2)}, u32[]{:S(2)}) collective-permute-start(bf16[256,512]{1,0:T(8,128)(2,1)} %get-tuple-element.67), channel_id=1, source_target_pairs={{2,4},{3,5},{4,2},{5,3},{10,12},{11,13},{12,10},{13,11},{18,20},{1... | collective-permute-start | bytes 786440 | tf_op jit(solution)/shard_map/ppermute | solution.py:397
  205.6 25.6 %collective-permute-start.20 = (bf16[256,512]{1,0:T(8,128)(2,1)S(1)}, bf16[256,512]{1,0:T(8,128)(2,1)S(1)}, u32[]{:S(2)}, u32[]{:S(2)}) collective-permute-start(bf16[256,512]{1,0:T(8,128)(2,1)S(1)} %add_convert_fusion.1), channel_id=1, source_target_pairs={{0,4},{1,5},{2,6},{3,7},{4,0},{5,1},{6,2},{7,3},{8,12},{9,13},{10,... | collective-permute-start | bytes 786440 | tf_op jit(solution)/shard_map/ppermute | solution.py:397
  207.8 29.1 %collective-permute-start.48 = (bf16[512,512]{1,0:T(8,128)(2,1)S(1)}, bf16[512,512]{1,0:T(8,128)(2,1)}, u32[]{:S(2)}, u32[]{:S(2)}) collective-permute-start(bf16[512,512]{1,0:T(8,128)(2,1)S(1)} %shard_map.120), channel_id=1, source_target_pairs={{0,1},{1,0},{2,3},{3,2},{4,5},{5,4},{6,7},{7,6},{8,9},{9,8},{10,11... | collective-permute-start | bytes 1572872 | tf_op jit(solution)/shard_map/ppermute | solution.py:405
  208.7 23.0 %collective-permute-start.22 = (bf16[256,512]{1,0:T(8,128)(2,1)}, bf16[256,512]{1,0:T(8,128)(2,1)S(1)}, u32[]{:S(2)}, u32[]{:S(2)}) collective-permute-start(bf16[256,512]{1,0:T(8,128)(2,1)} %get-tuple-element.66), channel_id=1, source_target_pairs={{0,2},{1,3},{2,0},{3,1},{4,6},{5,7},{6,4},{7,5},{8,10},{9,11},{10,... | collective-permute-start | bytes 786440 | tf_op jit(solution)/shard_map/ppermute | solution.py:397
  208.7 26.0 %collective-permute-start.25 = (bf16[256,512]{1,0:T(8,128)(2,1)}, bf16[256,512]{1,0:T(8,128)(2,1)}, u32[]{:S(2)}, u32[]{:S(2)}) collective-permute-start(bf16[256,512]{1,0:T(8,128)(2,1)} %add_convert_fusion), channel_id=1, source_target_pairs={{0,4},{1,5},{2,6},{3,7},{4,0},{5,1},{6,2},{7,3},{8,12},{9,13},{10,... | collective-permute-start | bytes 786440 | tf_op jit(solution)/shard_map/ppermute | solution.py:397
  (4 other events, 2.8 us)

commit v2 on v1

v2 whole, which is shorter than its diff:
```python
import functools

import jax
import jax.numpy as jnp
from jax import lax
from jax.experimental import pallas as pl
from jax.experimental.pallas import tpu as pltpu
from jax.sharding import PartitionSpec as P

F32 = jnp.float32
BF16 = jnp.bfloat16
MIB = 1024 * 1024
VMEM = pl.BlockSpec(memory_space=pltpu.VMEM)
SMEM = pl.BlockSpec(memory_space=pltpu.SMEM)
ANY = pl.BlockSpec(memory_space=pl.ANY)


def nbytes(items):
    return sum(x.size * x.dtype.itemsize for x in items)


def run(body, args, specs, outs, scratch=(), flops=0, trans=0, mib=8, after=()):
    n, extra = len(args), len(after)

    def whole(*refs):
        body(*refs[:n], *refs[n + extra :])

    return pl.pallas_call(
        whole,
        out_shape=outs,
        in_specs=specs + [ANY] * extra,
        out_specs=[VMEM] * len(outs),
        scratch_shapes=list(scratch),
        compiler_params=pltpu.CompilerParams(vmem_limit_bytes=mib * MIB),
        cost_estimate=pl.CostEstimate(
            flops=flops, bytes_accessed=nbytes(args) + nbytes(outs), transcendentals=trans
        ),
    )(*args, *after)


def shape(dims, dtype=BF16):
    return jax.ShapeDtypeStruct(dims, dtype)


def sort_tiles(count_ref, slot_ref, number_ref, list_ref, local_cols, groups, cap, by_row):
    def clear(g, _):
        number_ref[g] = 0
        return 0

    lax.fori_loop(0, groups, clear, 0)

    def place(s, _):
        p = slot_ref[s]
        u, v = lax.div(p, local_cols), lax.rem(p, local_cols)
        g, other = (u, v) if by_row else (v, u)
        n = number_ref[g]
        list_ref[g * cap + n] = s * 1024 + other
        number_ref[g] = n + 1
        return 0

    lax.fori_loop(0, count_ref[0], place, 0)


def tile_copy(tiles_ref, held, sems, s):
    return pltpu.make_async_copy(tiles_ref.at[s], held.at[s], sems.at[s])


def start_group(g, tiles_ref, held, sems, number_ref, list_ref, cap):
    def one(j, _):
        tile_copy(tiles_ref, held, sems, list_ref[g * cap + j] // 1024).start()
        return 0

    lax.fori_loop(0, number_ref[g], one, 0)


def sum_group(g, tiles_ref, held, sems, number_ref, list_ref, cap, total, product):
    n = number_ref[g]
    odd = lax.rem(n, 2)

    def fetch(j):
        entry = list_ref[g * cap + j]
        s = entry // 1024
        tile_copy(tiles_ref, held, sems, s).wait()
        return s, lax.rem(entry, 1024)

    @pl.when(odd == 1)
    def _():
        total[...] = product([fetch(0)])

    @pl.when(odd == 0)
    def _():
        total[...] = jnp.zeros_like(total)

    def pair(m, _):
        first = fetch(odd + 2 * m)
        second = fetch(odd + 2 * m + 1)
        total[...] += product([first, second])
        return 0

    lax.fori_loop(0, lax.div(n, 2), pair, 0)


def forward_body(scaled, half, local_cols, cap, *refs):
    count_ref, slot_ref, tiles_ref = refs[:3]
    give, keep, held, source, total, sems, source_sems, number_ref, list_ref = refs[-9:]
    inputs = refs[3:-9]
    col = lax.axis_index("col")
    parts = give.shape[0]
    sort_tiles(count_ref, slot_ref, number_ref, list_ref, local_cols, 4 * parts, cap, True)

    def block_row(i, flip):
        return (col ^ (2 * i + flip)) * 2 + half

    row = lax.axis_index("row")
    n_row = local_cols // 2
    if not scaled:
        copies = [
            pltpu.make_async_copy(x, source.at[pl.ds(i * n_row, n_row)], source_sems.at[i])
            for i, x in enumerate(inputs)
        ]
        for copy in copies:
            copy.start()

    def locate(v):
        return v if scaled else lax.rem(v, 2) * n_row + (lax.div(v, 2) ^ row)

    for flip in (1, 0):

        def start(i, _):
            start_group(block_row(i, flip), tiles_ref, held, sems, number_ref, list_ref, cap)
            return 0

        lax.fori_loop(0, parts, start, 0)
    if scaled:
        values, scale = inputs

        def fill(i, _):
            source[i] = (values[i].astype(F32) * scale[i]).astype(BF16)
            return 0

        lax.fori_loop(0, local_cols, fill, 0)
    else:
        for copy in copies:
            copy.wait()

    def product(pieces):
        lhs = [held[s] for s, _ in pieces]
        rhs = [source[locate(v)] for _, v in pieces]
        return jnp.dot(
            jnp.concatenate(lhs, 1), jnp.concatenate(rhs, 0), preferred_element_type=F32
        )

    for flip, out in ((1, give), (0, keep)):

        def block(i, _):
            sum_group(
                block_row(i, flip), tiles_ref, held, sems, number_ref, list_ref, cap, total, product
            )
            out[i] = total[...].astype(BF16)
            return 0

        lax.fori_loop(0, parts, block, 0)


def forward(count, slots, tiles, sources, scaled, half, local_cols, n_col, after):
    slots_n, edge, _ = tiles.shape
    width = sources[0].shape[-1]
    outs = [shape((n_col // 2, edge, width))] * 2
    return run(
        functools.partial(forward_body, scaled, half, local_cols, local_cols),
        (count, slots, tiles, *sources),
        [SMEM, SMEM, ANY] + ([VMEM] if scaled else [ANY]) * len(sources),
        outs,
        [
            pltpu.VMEM(tiles.shape, BF16),
            pltpu.VMEM((local_cols, edge, width), BF16),
            pltpu.VMEM((edge, width), F32),
            pltpu.SemaphoreType.DMA((slots_n,)),
            pltpu.SemaphoreType.DMA((2,)),
            pltpu.SMEM((2 * n_col,), jnp.int32),
            pltpu.SMEM((2 * n_col * local_cols,), jnp.int32),
        ],
        flops=slots_n * edge * edge * width,
        mib=20,
        after=after,
    )


def backward_body(local_cols, cap, *refs):
    count_ref, slot_ref, tiles_ref, ranged, out = refs[:5]
    held, source, total, sems, source_sem, number_ref, list_ref = refs[5:]
    sort_tiles(count_ref, slot_ref, number_ref, list_ref, local_cols, local_cols, cap, False)
    mask = lax.axis_index("row") * 2
    copy = pltpu.make_async_copy(ranged, source, source_sem)
    copy.start()

    def start(i, _):
        start_group(i ^ mask, tiles_ref, held, sems, number_ref, list_ref, cap)
        return 0

    lax.fori_loop(0, local_cols, start, 0)
    copy.wait()

    def product(pieces):
        lhs = [source[u] for _, u in pieces]
        rhs = [held[s] for s, _ in pieces]
        return jnp.dot(
            jnp.concatenate(lhs, 1), jnp.concatenate(rhs, 0), preferred_element_type=F32
        )

    def block(i, _):
        sum_group(
            i ^ mask, tiles_ref, held, sems, number_ref, list_ref, cap, total, product
        )
        out[i] = total[...].astype(BF16)
        return 0

    lax.fori_loop(0, local_cols, block, 0)


def backward(count, slots, tiles, ranged, n_row):
    slots_n, edge, _ = tiles.shape
    block_rows, width, _ = ranged.shape
    local_cols = 2 * n_row
    return run(
        functools.partial(backward_body, local_cols, block_rows),
        (count, slots, tiles, ranged),
        [SMEM, SMEM, ANY, ANY],
        [shape((local_cols, width, edge))],
        [
            pltpu.VMEM(tiles.shape, BF16),
            pltpu.VMEM(ranged.shape, BF16),
            pltpu.VMEM((width, edge), F32),
            pltpu.SemaphoreType.DMA((slots_n,)),
            pltpu.SemaphoreType.DMA,
            pltpu.SMEM((local_cols,), jnp.int32),
            pltpu.SMEM((block_rows * local_cols,), jnp.int32),
        ],
        flops=2 * slots_n * edge * edge * width,
        mib=20,
    )[0]


def pair_sum_body(n, keep, come, *outs):
    for j in range(n):
        outs[j][...] = (keep[j].astype(F32) + come[j].astype(F32)).astype(BF16)


def pair_sum(keep, come):
    n = keep.shape[0]
    return run(
        functools.partial(pair_sum_body, n),
        (keep, come),
        [VMEM] * 2,
        [shape(keep.shape[1:])] * n,
        flops=keep.size,
    )


def tree(items):
    while len(items) > 1:
        items = [a + b for a, b in zip(items[::2], items[1::2])]
    return items[0]


def scaled_body(cot, scale, out):
    row = lax.axis_index("row")
    edge = out.shape[2]
    for e in range(out.shape[0]):
        value = cot[e * edge : (e + 1) * edge, :].astype(F32) * scale[row * 2 + e]
        out[e] = value.T.astype(BF16)


def scaled_transposed(cotangent, scale):
    _, edge, _ = scale.shape
    rows, width = cotangent.shape
    return run(
        scaled_body,
        (cotangent, scale),
        [VMEM] * 2,
        [shape((rows // edge, width, edge))],
        flops=cotangent.size,
    )[0]


def agg_body(n, half, *refs):
    scale, out = refs[n], refs[n + 1]
    summed = tree([x[...].astype(F32) for x in refs[:n]])
    out[...] = (summed * scale[lax.axis_index("row") * 2 + half]).astype(BF16)


def aggregate(parts, scale, half, after):
    return run(
        functools.partial(agg_body, len(parts), half),
        (*parts, scale),
        [VMEM] * (len(parts) + 1),
        [shape(parts[0].shape)],
        flops=parts[0].size * len(parts),
        after=after,
    )[0]


def first_body(n, half, *refs):
    scale, weight, agg, out = refs[n:]
    row = lax.axis_index("row")
    for j in range(n):
        value = jnp.dot(refs[j][...], weight[...], preferred_element_type=F32)
        out[j] = (jax.nn.gelu(value) * scale[(row ^ j) * 2 + half]).astype(BF16)
        agg[j] = refs[j][...]


def first_layer(aggs, scale, weight, half, after):
    n = len(aggs)
    dims = (n, *aggs[0].shape)
    return run(
        functools.partial(first_body, n, half),
        (*aggs, scale, weight),
        [VMEM] * (n + 2),
        [shape(dims)] * 2,
        flops=2 * n * dims[1] * weight.size,
        trans=n * aggs[0].size,
        mib=12,
        after=after,
    )


def second_body(n, half, *refs):
    scale, weight, out = refs[n:]
    summed = tree([x[...].astype(F32) for x in refs[:n]])
    agg = (summed * scale[lax.axis_index("row") * 2 + half]).astype(BF16)
    out[...] = jnp.dot(agg, weight[...], preferred_element_type=F32).astype(BF16)


def second_layer(parts, scale, weight, half):
    dims = parts[0].shape
    return run(
        functools.partial(second_body, len(parts), half),
        (*parts, scale, weight),
        [VMEM] * (len(parts) + 2),
        [shape(dims)],
        flops=2 * dims[0] * weight.size,
    )[0]


def grad_body(hidden_ref, *refs):
    aggs, outs = refs[:2], refs[2:4]
    scale, w_first, w_second, give, keep, first, second = refs[4:]
    row = lax.axis_index("row")
    core = lax.rem(lax.axis_index("col"), 2)
    first[...] = jnp.zeros_like(first)
    second[...] = jnp.zeros_like(second)
    for e in range(2):

        def block(j, _):
            hidden, agg = hidden_ref[2 * j + e], aggs[e][j]
            pre = jnp.dot(agg, w_first[...], preferred_element_type=F32)
            grad_hidden = lax.dot_general(
                hidden, w_second[...], (((0,), (1,)), ((), ())), preferred_element_type=F32
            )
            _, pullback = jax.vjp(jax.nn.gelu, pre)
            grad_pre = pullback(grad_hidden * scale[(row ^ j) * 2 + e])[0].astype(BF16)
            first[...] += lax.dot_general(
                agg, grad_pre, (((0,), (0,)), ((), ())), preferred_element_type=F32
            )
            second[...] += lax.dot_general(
                outs[e][j], hidden, (((0,), (1,)), ((), ())), preferred_element_type=F32
            )
            return 0

        lax.fori_loop(0, aggs[e].shape[0], block, 0)
    keep[...] = jnp.where(core == 0, first[...], second[...]).astype(BF16)
    give[...] = jnp.where(core == 0, second[...], first[...]).astype(BF16)


def weight_grads(hidden, aggs, outs, scale, w_first, w_second, after):
    return run(
        grad_body,
        (hidden, *aggs, *outs, scale, w_first, w_second),
        [VMEM] * 8,
        [shape(w_first.shape)] * 2,
        [pltpu.VMEM(w_first.shape, F32)] * 2,
        flops=8 * hidden.size * w_first.shape[0],
        trans=hidden.size,
        mib=28,
        after=after,
    )


def split_body(n, keep, come, *outs):
    row = lax.axis_index("row")
    rows = keep.shape[0] // n
    for j in range(n):
        part = pl.ds(pl.multiple_of((row ^ j) * rows, rows), rows)
        outs[j][...] = (keep[part, :].astype(F32) + come[part, :].astype(F32)).astype(BF16)


def split_sum(keep, come, n, after):
    rows, width = keep.shape
    return run(
        functools.partial(split_body, n),
        (keep, come),
        [VMEM] * 2,
        [shape((rows // n, width))] * n,
        flops=keep.size,
        after=after,
    )


def sum_body(n, *refs):
    refs[n][...] = tree([x[...].astype(F32) for x in refs[:n]]).astype(BF16)


def sum_parts(parts, after=()):
    return run(
        functools.partial(sum_body, len(parts)),
        tuple(parts),
        [VMEM] * len(parts),
        [shape(parts[0].shape)],
        flops=parts[0].size * len(parts),
        after=after,
    )[0]


def join_body(n, *refs):
    row = lax.axis_index("row")
    rows = refs[0].shape[0]
    for j in range(n):
        refs[n][pl.ds(pl.multiple_of((row ^ j) * rows, rows), rows), :] = refs[j][...]


def join(parts):
    rows, width = parts[0].shape
    return run(
        functools.partial(join_body, len(parts)),
        tuple(parts),
        [VMEM] * len(parts),
        [shape((rows * len(parts), width))],
    )[0]


def per_device(features, degree, tile_vals, tile_slot, tile_count, w_first, w_second, cotangent):
    n_row, n_col = lax.axis_size("row"), lax.axis_size("col")
    line = n_col // 2
    piece, width = cotangent.shape
    tiles = tile_vals[0, 0]
    edge = tiles.shape[-1]
    local_cols = n_row * 2
    slots, count = tile_slot[0, 0], tile_count[0]

    def col_send(value, pairs):
        return lax.ppermute(
            value, "col", [(2 * a + k, 2 * b + k) for a, b in pairs for k in range(2)]
        )

    def line_flip(value, j):
        return col_send(value, [(a, a ^ j) for a in range(line)])

    def core_flip(value):
        return lax.ppermute(value, "col", [(a, a ^ 1) for a in range(n_col)])

    def row_flip(value, j):
        return lax.ppermute(value, "row", [(a, a ^ j) for a in range(n_row)])

    def scatter_line(own):
        if line != 4:
            return [own[0]] + [line_flip(own[j], j) for j in range(1, line)], own[0]
        inward = col_send(own[3], [(0, 1), (3, 2)])
        middle = col_send(own[3], [(1, 2), (2, 1)])
        near = line_flip(own[1], 1)
        joined = sum_parts([own[2], inward])
        return [own[0], near, middle, line_flip(joined, 2)], joined

    values = features[:, 0].reshape(local_cols, edge, width)
    scale = (1.0 / jnp.sqrt(degree.astype(F32))).reshape(local_cols, edge, 1)
    halves = piece // edge

    ranged = lax.all_gather(scaled_transposed(cotangent, scale), "col", axis=0, tiled=True)

    aggs, outs = [], []
    partials, after = [], ()
    for half in range(halves):
        give, keep = forward(
            count, slots, tiles, (values, scale), True, half, local_cols, n_col, after
        )
        own = pair_sum(keep, core_flip(give))
        after = (own[-1],)
        partials.append(own)
    hidden = backward(count, slots, tiles, ranged, n_row)
    for half in range(halves):
        after = (agg,) if half else ()
        agg = aggregate(scatter_line(partials[half])[0], scale, half, after)
        spread = [agg] + [row_flip(agg, j) for j in range(1, n_row)]
        stacked, out = first_layer(spread, scale, w_first, half, (hidden,) if half else ())
        aggs.append(stacked)
        outs.append(out)

    partials, after = [], ()
    for half in range(halves):
        give, keep = forward(count, slots, tiles, outs, False, half, local_cols, n_col, after)
        own = pair_sum(keep, core_flip(give))
        after = (own[-1],)
        partials.append(own)

    give, keep = weight_grads(hidden, aggs, outs, scale, w_first, w_second, after)
    arrived, marks = zip(*[scatter_line(own) for own in partials])
    parts = split_sum(keep, core_flip(give), n_row, marks[:1])
    part = sum_parts([parts[0]] + [row_flip(parts[j], j) for j in range(1, n_row)], marks[1:])
    part = sum_parts([part] + [line_flip(part, j) for j in range(1, line)])
    mine = join([part] + [row_flip(part, j) for j in range(1, n_row)])
    other = core_flip(mine)
    core = lax.rem(lax.axis_index("col"), 2)
    grad_first = jnp.where(core == 0, mine, other).astype(F32)
    grad_second = jnp.where(core == 0, other, mine).astype(F32)

    logits = [second_layer(arrived[half], scale, w_second, half) for half in range(halves)]
    return jnp.concatenate(logits, 0), grad_first, grad_second


def solution(mesh):
    return jax.shard_map(
        per_device,
        mesh=mesh,
        in_specs=(
            P(None, "col", None, None),
            P(None, "col", None),
            P("row", "col", None, None, None),
            P("row", "col", None),
            P("row", "col"),
            P(),
            P(),
            P(("row", "col"), None),
        ),
        out_specs=(P(("row", "col"), None), P(), P()),
        check_vma=False,
    )
```

time: 240 us -> 251 us (1.046)
  Pallas kernels: 47.7 us -> 73.5 us
  waiting for transfers between devices: 99.9 us -> 84.9 us
  between operations: 1.8 us -> 15 us
  starting transfers between devices: 66.7 us -> 53.7 us
  other arithmetic: 8.89 us -> 4.2 us
    pallas_call x18 -> x25, Pallas kernels: 47.7 us -> 73.5 us  [run(): pl.pallas_call(whole, out_shape=outs, in_specs=specs + [ANY] * extra, out...]
    ppermute x24 -> x19, starting transfers between devices: 48 us -> 33.7 us  [col_send(): lax.ppermute(value, 'col', [(2 * a + k, 2 * b + k) for a, b in pairs for...]
    ppermute x15 -> x12, waiting for transfers between devices: 22.2 us -> 10.5 us  [row_flip(): return lax.ppermute(value, 'row', [(a, a ^ j) for a in range(n_row)])]
    ppermute x24 -> x19, waiting for transfers between devices: 75.7 us -> 67.1 us  [col_send(): lax.ppermute(value, 'col', [(2 * a + k, 2 * b + k) for a, b in pairs for...]
    ppermute x10 -> x6, waiting for transfers between devices: 1.92 us -> 7.23 us  [core_flip(): return lax.ppermute(value, 'col', [(a, a ^ 1) for a in range(n_col)])]
    ppermute x10 -> x6, starting transfers between devices: 0.94 us -> 5.78 us  [core_flip(): return lax.ppermute(value, 'col', [(a, a ^ 1) for a in range(n_col)])]
    unnamed x39 -> x40, local copies, waits for them, and re-layouts: 11.3 us -> 15.9 us
    convert_element_type x5 -> x0, other arithmetic: 3.66 us -> none  [the longest x1 2 us: per_device(): scaled = (cotangent.astype(F32) * own_scale.reshape(piece, 1)).astype(BF1...]
  transfers between devices with their start and end apart: 49 -> 38, of which waited for: 17 -> 25; matrix products, arithmetic and copies ran while one was open for 3% -> 0% of each run, Pallas kernels for 17% -> 17%
where the time goes in v2:
time: 251 us; the launch traced here: 248 us
  waiting for transfers between devices  84.9 us (34%)
  Pallas kernels  73.5 us (29%)
  starting transfers between devices  53.7 us (21%)
  local copies, waits for them, and re-layouts  16.8 us (7%)
  between operations  15 us (6%)
  other arithmetic  4.2 us (2%)
    pallas_call x25, Pallas kernels, run(): pl.pallas_call(whole, out_shape=outs, in_specs=specs + [ANY] * extra, out...  73.5 us
    ppermute x19, waiting for transfers between devices, col_send(): lax.ppermute(value, 'col', [(2 * a + k, 2 * b + k) for a, b in pairs for...  67.1 us
    ppermute x19, starting transfers between devices, col_send(): lax.ppermute(value, 'col', [(2 * a + k, 2 * b + k) for a, b in pairs for...  33.7 us
    unnamed x40, local copies, waits for them, and re-layouts  15.9 us
    ppermute x12, starting transfers between devices, row_flip(): return lax.ppermute(value, 'row', [(a, a ^ j) for a in range(n_row)])  14.2 us
    ppermute x12, waiting for transfers between devices, row_flip(): return lax.ppermute(value, 'row', [(a, a ^ j) for a in range(n_row)])  10.5 us
    ppermute x6, waiting for transfers between devices, core_flip(): return lax.ppermute(value, 'col', [(a, a ^ 1) for a in range(n_col)])  7.23 us
    ppermute x6, starting transfers between devices, core_flip(): return lax.ppermute(value, 'col', [(a, a ^ 1) for a in range(n_col)])  5.78 us
  transfers between devices with their start and end apart: 38, of which 25 were waited for; matrix products, arithmetic and copies ran while one was open for 0% of the time, Pallas kernels for 17%

profile of v2, /device:TPU:0, one launch (start us, length us, event | category | flops | bytes accessed | tf_op | source)
XLA Modules:
  0.0 248.1 jit_solution(9567410236653597587)
XLA Ops:
  7.2 0.9 rsqrt_reduce_fusion
  8.1 0.9 reshape.10.refs_4_.refs_1_.refs_5_
  9.0 1.0 copy-done.7
  10.3 0.8 copy-done.5
  11.8 2.8 %copy-done = bf16[1,1,48,256,256]{4,3,2,1,0:T(8,128)(2,1)S(1)} copy-done((bf16[1,1,48,256,256]{4,3,2,1,0:T(8,128)(2,1)S(1)}, bf16[1,1,48,256,256]{4,3,2,1,0:T(8,128)(2,1)}, u32[]{:S(2)}) %copy-start) | copy-done | bytes 6291480
  15.2 10.6 %shard_map.103 = (bf16[4,256,512]{2,1,0:T(8,128)(2,1)S(1)}, bf16[4,256,512]{2,1,0:T(8,128)(2,1)S(1)}) custom-call(s32[1]{0:T(128)} %bitcast.4.refs_0_, s32[48]{0:T(128)S(1)} %bitcast.16, bf16[48,256,256]{2,1,0:T(8,128)(2,1)S(1)} %bitcast.9, bf16[8,256,512]{2,1,0:T(8,128)(2,1)S(1)} %bitcast.14, f32[8,256,1]{2,1,0:T(8,128)S(1)} %reshape.10.refs_4_.refs_1_.refs_5_), custom_call_target="tpu_custom_call" | custom-call | flops 1610612736 | bytes 10494148 | tf_op jit(solution)/shard_map/pallas_call | solution.py:28
  25.9 0.9 collective-permute-start
  26.8 2.3 collective-permute-done.refs_1_
  29.3 10.2 %shard_map.108 = (bf16[4,256,512]{2,1,0:T(8,128)(2,1)S(1)}, bf16[4,256,512]{2,1,0:T(8,128)(2,1)S(1)}) custom-call(s32[1]{0:T(128)} %bitcast.5.refs_0_, s32[48]{0:T(128)S(1)} %bitcast.17, bf16[48,256,256]{2,1,0:T(8,128)(2,1)S(1)} %bitcast.10, bf16[8,256,512]{2,1,0:T(8,128)(2,1)S(1)} %bitcast.15, f32[8,256,1]{2,1,0:T(8,128)S(1)} %reshape.10.refs_4_.refs_1_.refs_5_, ...), custom_call_target="tpu_custom_call" | custom-call | flops 1610612736 | bytes 10494148 | tf_op jit(solution)/shard_map/pallas_call | solution.py:28
  39.5 2.3 collective-permute-start.8
  41.8 2.3 collective-permute-start.3
  44.8 2.3 collective-permute-start.1
  47.0 9.3 %collective-permute-done.3.refs_1_ = bf16[256,512]{1,0:T(8,128)(2,1)S(1)} collective-permute-done((bf16[256,512]{1,0:T(8,128)(2,1)S(1)}, bf16[256,512]{1,0:T(8,128)(2,1)S(1)}, u32[]{:S(2)}, u32[]{:S(2)}) %collective-permute-start.3) | collective-permute-done | bytes 262176 | tf_op jit(solution)/shard_map/ppermute | solution.py:451
  56.4 3.6 %collective-permute-start.4 = (bf16[256,512]{1,0:T(8,128)(2,1)S(1)}, bf16[256,512]{1,0:T(8,128)(2,1)S(1)}, u32[]{:S(2)}, u32[]{:S(2)}) collective-permute-start(bf16[256,512]{1,0:T(8,128)(2,1)S(1)} %shard_map.105), channel_id=1, source_target_pairs={{0,4},{1,5},{2,6},{3,7},{4,0},{5,1},{6,2},{7,3},{8,12},{9,13},{10,... | collective-permute-start | bytes 786440 | tf_op jit(solution)/shard_map/ppermute | solution.py:451
  60.2 1.5 collective-permute-start.11
  61.7 5.9 %collective-permute-done.1.refs_1_ = bf16[256,512]{1,0:T(8,128)(2,1)S(1)} collective-permute-done((bf16[256,512]{1,0:T(8,128)(2,1)S(1)}, bf16[256,512]{1,0:T(8,128)(2,1)S(1)}, u32[]{:S(2)}, u32[]{:S(2)}) %collective-permute-start.1) | collective-permute-done | bytes 262176 | tf_op jit(solution)/shard_map/ppermute | solution.py:451
  67.6 5.7 %collective-permute-done.4.refs_3_ = bf16[256,512]{1,0:T(8,128)(2,1)S(1)} collective-permute-done((bf16[256,512]{1,0:T(8,128)(2,1)S(1)}, bf16[256,512]{1,0:T(8,128)(2,1)S(1)}, u32[]{:S(2)}, u32[]{:S(2)}) %collective-permute-start.4) | collective-permute-done | bytes 262176 | tf_op jit(solution)/shard_map/ppermute | solution.py:451
  73.5 2.3 collective-permute-start.7
  77.7 1.0 collective-permute-done.11.refs_1_
  78.7 4.6 %collective-permute-start.9 = (bf16[256,512]{1,0:T(8,128)(2,1)S(1)}, bf16[256,512]{1,0:T(8,128)(2,1)S(1)}, u32[]{:S(2)}, u32[]{:S(2)}) collective-permute-start(bf16[256,512]{1,0:T(8,128)(2,1)S(1)} %get-tuple-element.47), channel_id=1, source_target_pairs={{0,2},{1,3},{2,0},{3,1},{4,6},{5,7},{6,4},{7,5},{8,10},{9,11},{10,... | collective-permute-start | bytes 786440 | tf_op jit(solution)/shard_map/ppermute | solution.py:451
  83.7 3.4 %collective-permute-start.12 = (bf16[256,512]{1,0:T(8,128)(2,1)S(1)}, bf16[256,512]{1,0:T(8,128)(2,1)S(1)}, u32[]{:S(2)}, u32[]{:S(2)}) collective-permute-start(bf16[256,512]{1,0:T(8,128)(2,1)S(1)} %shard_map.110), channel_id=1, source_target_pairs={{0,4},{1,5},{2,6},{3,7},{4,0},{5,1},{6,2},{7,3},{8,12},{9,13},{10,... | collective-permute-start | bytes 786440 | tf_op jit(solution)/shard_map/ppermute | solution.py:451
  87.1 0.9 collective-permute-done.6.refs_2_
  88.2 1.0 shard_map.107
  89.2 0.8 collective-permute-done.9.refs_1_
  90.1 10.9 %collective-permute-done.12.refs_3_ = bf16[256,512]{1,0:T(8,128)(2,1)S(1)} collective-permute-done((bf16[256,512]{1,0:T(8,128)(2,1)S(1)}, bf16[256,512]{1,0:T(8,128)(2,1)S(1)}, u32[]{:S(2)}, u32[]{:S(2)}) %collective-permute-start.12) | collective-permute-done | bytes 262176 | tf_op jit(solution)/shard_map/ppermute | solution.py:451
  101.1 2.5 collective-permute-start.15
  104.7 2.8 %copy-done.1 = bf16[1,1,48,256,256]{4,3,2,1,0:T(8,128)(2,1)S(1)} copy-done((bf16[1,1,48,256,256]{4,3,2,1,0:T(8,128)(2,1)S(1)}, bf16[1,1,48,256,256]{4,3,2,1,0:T(8,128)(2,1)}, u32[]{:S(2)}) %copy-start.1) | copy-done | bytes 6291480
  107.5 2.2 copy-done.3
  109.7 16.6 %shard_map.113.refs_6_.refs_0_ = bf16[8,512,256]{2,1,0:T(8,128)(2,1)S(1)} custom-call(s32[1]{0:T(128)} %bitcast.6.refs_0_, s32[48]{0:T(128)S(1)} %bitcast.18, bf16[48,256,256]{2,1,0:T(8,128)(2,1)S(1)} %bitcast.11, bf16[16,512,256]{2,1,0:T(8,128)(2,1)S(1)} %copy-done.3), custom_call_target="tpu_custom_call" | custom-call | flops 3221225472 | bytes 12583108 | tf_op jit(solution)/shard_map/pallas_call | solution.py:28
  126.3 2.0 shard_map.114
  128.4 9.9 %shard_map.115 = (bf16[4,256,512]{2,1,0:T(8,128)(2,1)S(1)}, bf16[4,256,512]{2,1,0:T(8,128)(2,1)S(1)}) custom-call(s32[1]{0:T(128)} %bitcast.7.refs_0_, s32[48]{0:T(128)S(1)} %bitcast.19, bf16[48,256,256]{2,1,0:T(8,128)(2,1)S(1)} %bitcast.12, bf16[4,256,512]{2,1,0:T(8,128)(2,1)S(1)} %get-tuple-element.43.refs_3_, ...), custom_call_target="tpu_custom_call" | custom-call | flops 1610612736 | bytes 10485956 | tf_op jit(solution)/shard_map/pallas_call | solution.py:28
  138.3 2.6 %collective-permute-done.16.refs_1_ = bf16[4,256,512]{2,1,0:T(8,128)(2,1)S(1)} collective-permute-done((bf16[4,256,512]{2,1,0:T(8,128)(2,1)S(1)}, bf16[4,256,512]{2,1,0:T(8,128)(2,1)S(1)}, u32[]{:S(2)}, u32[]{:S(2)}) %collective-permute-start.16) | collective-permute-done | bytes 1048608 | tf_op jit(solution)/shard_map/ppermute | solution.py:459
  141.3 9.7 %shard_map.119 = (bf16[4,256,512]{2,1,0:T(8,128)(2,1)S(1)}, bf16[4,256,512]{2,1,0:T(8,128)(2,1)S(1)}) custom-call(s32[1]{0:T(128)} %bitcast.8.refs_0_, s32[48]{0:T(128)S(1)} %bitcast.20, bf16[48,256,256]{2,1,0:T(8,128)(2,1)S(1)} %bitcast.13, bf16[4,256,512]{2,1,0:T(8,128)(2,1)S(1)} %get-tuple-element.43.refs_3_, ...), custom_call_target="tpu_custom_call" | custom-call | flops 1610612736 | bytes 10485956 | tf_op jit(solution)/shard_map/pallas_call | solution.py:28
  150.9 2.0 collective-permute-start.21
  153.0 2.3 collective-permute-done.21.refs_1_
  155.3 1.0 shard_map.120
  156.9 8.7 %shard_map.123 = (bf16[512,512]{1,0:T(8,128)(2,1)S(1)}, bf16[512,512]{1,0:T(8,128)(2,1)S(1)}) custom-call(bf16[8,512,256]{2,1,0:T(8,128)(2,1)S(1)} %shard_map.113.refs_6_.refs_0_, bf16[4,256,512]{2,1,0:T(8,128)(2,1)S(1)} %copy-done.19, bf16[4,256,512]{2,1,0:T(8,128)(2,1)S(1)} %get-tuple-element.64.refs_2_, ...), custom_call_target="tpu_custom_call" | custom-call | flops 4294967296 | bytes 8396800 | tf_op jit(solution)/shard_map/pallas_call | solution.py:28
  166.1 1.3 collective-permute-start.19
  167.4 1.3 collective-permute-start.24
  168.7 5.3 %collective-permute-done.19.refs_1_ = bf16[256,512]{1,0:T(8,128)(2,1)S(1)} collective-permute-done((bf16[256,512]{1,0:T(8,128)(2,1)S(1)}, bf16[256,512]{1,0:T(8,128)(2,1)S(1)}, u32[]{:S(2)}, u32[]{:S(2)}) %collective-permute-start.19) | collective-permute-done | bytes 262176 | tf_op jit(solution)/shard_map/ppermute | solution.py:451
  174.3 3.0 %collective-permute-start.28 = (bf16[128,512]{1,0:T(8,128)(2,1)S(1)}, bf16[128,512]{1,0:T(8,128)(2,1)S(1)}, u32[]{:S(2)}, u32[]{:S(2)}) collective-permute-start(bf16[128,512]{1,0:T(8,128)(2,1)S(1)} %get-tuple-element.69), channel_id=1, source_target_pairs={{0,16},{8,24},{16,0},{24,8},{1,17},{9,25},{17,1},{25,9},{2,18},{10... | collective-permute-start | bytes 393224 | tf_op jit(solution)/shard_map/ppermute | solution.py:462
  177.8 1.5 collective-permute-done.24.refs_1_
  179.3 1.0 collective-permute-done.27.refs_1_
  180.3 1.6 collective-permute-done.28.refs_2_
  181.9 1.2 collective-permute-done.29.refs_3_
  183.9 3.3 %collective-permute-start.31 = (bf16[128,512]{1,0:T(8,128)(2,1)S(1)}, bf16[128,512]{1,0:T(8,128)(2,1)S(1)}, u32[]{:S(2)}, u32[]{:S(2)}) collective-permute-start(bf16[128,512]{1,0:T(8,128)(2,1)S(1)} %shard_map.125.refs_0_), channel_id=1, source_target_pairs={{0,4},{1,5},{2,6},{3,7},{4,0},{5,1},{6,2},{7,3},{8,12},{9,13},{10,... | collective-permute-start | bytes 393224 | tf_op jit(solution)/shard_map/ppermute | solution.py:451
  187.6 1.6 collective-permute-start.17
  189.9 1.6 collective-permute-done.32.refs_3_
  191.5 5.8 %collective-permute-done.31.refs_2_ = bf16[128,512]{1,0:T(8,128)(2,1)S(1)} collective-permute-done((bf16[128,512]{1,0:T(8,128)(2,1)S(1)}, bf16[128,512]{1,0:T(8,128)(2,1)S(1)}, u32[]{:S(2)}, u32[]{:S(2)}) %collective-permute-start.31) | collective-permute-done | bytes 131104 | tf_op jit(solution)/shard_map/ppermute | solution.py:451
  197.3 1.2 collective-permute-start.35
  198.5 1.2 collective-permute-start.34
  199.7 1.2 collective-permute-start.33
  200.9 3.6 %collective-permute-done.35.refs_3_ = bf16[128,512]{1,0:T(8,128)(2,1)S(1)} collective-permute-done((bf16[128,512]{1,0:T(8,128)(2,1)S(1)}, bf16[128,512]{1,0:T(8,128)(2,1)S(1)}, u32[]{:S(2)}, u32[]{:S(2)}) %collective-permute-start.35) | collective-permute-done | bytes 131104 | tf_op jit(solution)/shard_map/ppermute | solution.py:462
  204.5 0.9 collective-permute-done.34.refs_2_
  206.3 1.4 collective-permute-start.23
  208.4 4.0 %collective-permute-start.22 = (bf16[256,512]{1,0:T(8,128)(2,1)}, bf16[256,512]{1,0:T(8,128)(2,1)}, u32[]{:S(2)}, u32[]{:S(2)}) collective-permute-start(bf16[256,512]{1,0:T(8,128)(2,1)} %get-tuple-element.60), channel_id=1, source_target_pairs={{0,2},{1,3},{2,0},{3,1},{4,6},{5,7},{6,4},{7,5},{8,10},{9,11},{10,... | collective-permute-start | bytes 786440 | tf_op jit(solution)/shard_map/ppermute | solution.py:451
  213.1 6.8 %collective-permute-done.20.refs_3_ = bf16[256,512]{1,0:T(8,128)(2,1)S(1)} collective-permute-done((bf16[256,512]{1,0:T(8,128)(2,1)S(1)}, bf16[256,512]{1,0:T(8,128)(2,1)S(1)}, u32[]{:S(2)}, u32[]{:S(2)}) %collective-permute-start.20) | collective-permute-done | bytes 262176 | tf_op jit(solution)/shard_map/ppermute | solution.py:451
  220.6 0.9 copy-done.11
  221.6 0.9 copy-done.13
  222.5 0.9 copy-done.15
  224.6 11.8 %collective-permute-done.25.refs_3_ = bf16[256,512]{1,0:T(8,128)(2,1)} collective-permute-done((bf16[256,512]{1,0:T(8,128)(2,1)S(1)}, bf16[256,512]{1,0:T(8,128)(2,1)}, u32[]{:S(2)}, u32[]{:S(2)}) %collective-permute-start.25) | collective-permute-done | bytes 262176 | tf_op jit(solution)/shard_map/ppermute | solution.py:451
  236.4 1.5 shard_map.122
  238.0 0.8 pad_maximum_fusion
  238.8 2.5 %select_convert_fusion = (f32[512,512]{1,0:T(8,128)}, f32[512,512]{1,0:T(8,128)}) fusion(bf16[512,512]{1,0:T(8,128)(2,1)} %collective-permute-done.36, bf16[512,512]{1,0:T(8,128)(2,1)S(1)} %shard_map.127, pred[]{:T(512)S(6)} %eq.4), kind=kLoop, calls=%fused_computation.1 | loop fusion | flops 1048576 | bytes 3145729 | tf_op jit(solution)/shard_map/convert_element_type | solution.py:513
  (82 shorter events, 14.7 us)
Async XLA Ops:
  7.2 4.6 %copy-start.2 = (bf16[4,1,512,512]{3,2,1,0:T(8,128)(2,1)S(1)}, bf16[4,1,512,512]{3,2,1,0:T(8,128)(2,1)}, u32[]{:S(2)}) copy-start(bf16[4,1,512,512]{3,2,1,0:T(8,128)(2,1)} %param.8) | copy-start | bytes 6291460
  7.2 97.5 %all-gather.2.cloned.1.call-start = ((), (), s32[]{:S(2)}) async-start(), calls=%async_computation | async-start | bytes 4718592 | tf_op jit(solution)/shard_map/all_gather | solution.py:477
  9.0 1.0 copy-start.7
  10.3 0.8 copy-start.5
  11.8 2.8 %copy-start = (bf16[1,1,48,256,256]{4,3,2,1,0:T(8,128)(2,1)S(1)}, bf16[1,1,48,256,256]{4,3,2,1,0:T(8,128)(2,1)}, u32[]{:S(2)}) copy-start(bf16[1,1,48,256,256]{4,3,2,1,0:T(8,128)(2,1)} %param.10) | copy-start | bytes 18874372
  14.6 0.7 copy-start.16
  15.2 14.1 %copy-start.17 = (s32[1,1,48]{2,1,0:T(1,128)S(1)}, s32[1,1,48]{2,1,0:T(1,128)}, u32[]{:S(2)}) copy-start(s32[1,1,48]{2,1,0:T(1,128)} %param.11) | copy-start | bytes 580
  25.9 3.2 %collective-permute-start = (bf16[4,256,512]{2,1,0:T(8,128)(2,1)S(1)}, bf16[4,256,512]{2,1,0:T(8,128)(2,1)S(1)}, u32[]{:S(2)}, u32[]{:S(2)}) collective-permute-start(bf16[4,256,512]{2,1,0:T(8,128)(2,1)S(1)} %get-tuple-element.38), channel_id=1, source_target_pairs={{0,1},{1,0},{2,3},{3,2},{4,5},{5,4},{6,7},{7,6},{8,9},{9,8},{10,11... | collective-permute-start | bytes 3145736 | tf_op jit(solution)/shard_map/ppermute | solution.py:459
  39.5 48.7 %copy-start.4 = (bf16[512,512]{1,0:T(8,128)(2,1)S(1)}, bf16[512,512]{1,0:T(8,128)(2,1)}, u32[]{:S(2)}) copy-start(bf16[512,512]{1,0:T(8,128)(2,1)} %refs_6_.1) | copy-start | bytes 1572868
  39.5 20.4 %collective-permute-start.8 = (bf16[4,256,512]{2,1,0:T(8,128)(2,1)S(1)}, bf16[4,256,512]{2,1,0:T(8,128)(2,1)S(1)}, u32[]{:S(2)}, u32[]{:S(2)}) collective-permute-start(bf16[4,256,512]{2,1,0:T(8,128)(2,1)S(1)} %get-tuple-element.45), channel_id=1, source_target_pairs={{0,1},{1,0},{2,3},{3,2},{4,5},{5,4},{6,7},{7,6},{8,9},{9,8},{10,11... | collective-permute-start | bytes 3145736 | tf_op jit(solution)/shard_map/ppermute | solution.py:459
  41.8 14.5 %collective-permute-start.3 = (bf16[256,512]{1,0:T(8,128)(2,1)S(1)}, bf16[256,512]{1,0:T(8,128)(2,1)S(1)}, u32[]{:S(2)}, u32[]{:S(2)}) collective-permute-start(bf16[256,512]{1,0:T(8,128)(2,1)S(1)} %get-tuple-element.41.refs_5_), channel_id=1, source_target_pairs={{0,2},{1,3},{6,4},{7,5},{8,10},{9,11},{14,12},{15,13},{16,18},{17,... | collective-permute-start | bytes 786440 | tf_op jit(solution)/shard_map/ppermute | solution.py:451
  44.1 23.5 %collective-permute-start.2 = (bf16[256,512]{1,0:T(8,128)(2,1)S(1)}, bf16[256,512]{1,0:T(8,128)(2,1)S(1)}, u32[]{:S(2)}, u32[]{:S(2)}) collective-permute-start(bf16[256,512]{1,0:T(8,128)(2,1)S(1)} %get-tuple-element.41.refs_5_), channel_id=1, source_target_pairs={{2,4},{3,5},{4,2},{5,3},{10,12},{11,13},{12,10},{13,11},{18,20},{1... | collective-permute-start | bytes 786440 | tf_op jit(solution)/shard_map/ppermute | solution.py:451
  44.8 22.8 %collective-permute-start.1 = (bf16[256,512]{1,0:T(8,128)(2,1)S(1)}, bf16[256,512]{1,0:T(8,128)(2,1)S(1)}, u32[]{:S(2)}, u32[]{:S(2)}) collective-permute-start(bf16[256,512]{1,0:T(8,128)(2,1)S(1)} %get-tuple-element.40), channel_id=1, source_target_pairs={{0,2},{1,3},{2,0},{3,1},{4,6},{5,7},{6,4},{7,5},{8,10},{9,11},{10,... | collective-permute-start | bytes 786440 | tf_op jit(solution)/shard_map/ppermute | solution.py:451
  56.4 16.9 %collective-permute-start.4 = (bf16[256,512]{1,0:T(8,128)(2,1)S(1)}, bf16[256,512]{1,0:T(8,128)(2,1)S(1)}, u32[]{:S(2)}, u32[]{:S(2)}) collective-permute-start(bf16[256,512]{1,0:T(8,128)(2,1)S(1)} %shard_map.105), channel_id=1, source_target_pairs={{0,4},{1,5},{2,6},{3,7},{4,0},{5,1},{6,2},{7,3},{8,12},{9,13},{10,... | collective-permute-start | bytes 786440 | tf_op jit(solution)/shard_map/ppermute | solution.py:451
  60.2 18.5 %collective-permute-start.11 = (bf16[256,512]{1,0:T(8,128)(2,1)S(1)}, bf16[256,512]{1,0:T(8,128)(2,1)S(1)}, u32[]{:S(2)}, u32[]{:S(2)}) collective-permute-start(bf16[256,512]{1,0:T(8,128)(2,1)S(1)} %get-tuple-element.48), channel_id=1, source_target_pairs={{0,2},{1,3},{6,4},{7,5},{8,10},{9,11},{14,12},{15,13},{16,18},{17,... | collective-permute-start | bytes 786440 | tf_op jit(solution)/shard_map/ppermute | solution.py:451
  73.5 10.2 %collective-permute-start.7 = (bf16[256,512]{1,0:T(8,128)(2,1)S(1)}, bf16[256,512]{1,0:T(8,128)(2,1)S(1)}, u32[]{:S(2)}, u32[]{:S(2)}) collective-permute-start(bf16[256,512]{1,0:T(8,128)(2,1)S(1)} %shard_map.106.refs_0_.refs_5_), channel_id=1, source_target_pairs={{0,24},{8,16},{16,8},{24,0},{1,25},{9,17},{17,9},{25,1},{2,26},{10... | collective-permute-start | bytes 786440 | tf_op jit(solution)/shard_map/ppermute | solution.py:462
  75.8 12.2 %collective-permute-start.6 = (bf16[256,512]{1,0:T(8,128)(2,1)S(1)}, bf16[256,512]{1,0:T(8,128)(2,1)S(1)}, u32[]{:S(2)}, u32[]{:S(2)}) collective-permute-start(bf16[256,512]{1,0:T(8,128)(2,1)S(1)} %shard_map.106.refs_0_.refs_5_), channel_id=1, source_target_pairs={{0,16},{8,24},{16,0},{24,8},{1,17},{9,25},{17,1},{25,9},{2,18},{10... | collective-permute-start | bytes 786440 | tf_op jit(solution)/shard_map/ppermute | solution.py:462
  76.4 11.8 %collective-permute-start.5 = (bf16[256,512]{1,0:T(8,128)(2,1)S(1)}, bf16[256,512]{1,0:T(8,128)(2,1)S(1)}, u32[]{:S(2)}, u32[]{:S(2)}) collective-permute-start(bf16[256,512]{1,0:T(8,128)(2,1)S(1)} %shard_map.106.refs_0_.refs_5_), channel_id=1, source_target_pairs={{0,8},{8,0},{16,24},{24,16},{1,9},{9,1},{17,25},{25,17},{2,10},{10... | collective-permute-start | bytes 786440 | tf_op jit(solution)/shard_map/ppermute | solution.py:462
  77.0 13.1 %collective-permute-start.10 = (bf16[256,512]{1,0:T(8,128)(2,1)S(1)}, bf16[256,512]{1,0:T(8,128)(2,1)S(1)}, u32[]{:S(2)}, u32[]{:S(2)}) collective-permute-start(bf16[256,512]{1,0:T(8,128)(2,1)S(1)} %get-tuple-element.48), channel_id=1, source_target_pairs={{2,4},{3,5},{4,2},{5,3},{10,12},{11,13},{12,10},{13,11},{18,20},{1... | collective-permute-start | bytes 786440 | tf_op jit(solution)/shard_map/ppermute | solution.py:451
  78.7 11.4 %collective-permute-start.9 = (bf16[256,512]{1,0:T(8,128)(2,1)S(1)}, bf16[256,512]{1,0:T(8,128)(2,1)S(1)}, u32[]{:S(2)}, u32[]{:S(2)}) collective-permute-start(bf16[256,512]{1,0:T(8,128)(2,1)S(1)} %get-tuple-element.47), channel_id=1, source_target_pairs={{0,2},{1,3},{2,0},{3,1},{4,6},{5,7},{6,4},{7,5},{8,10},{9,11},{10,... | collective-permute-start | bytes 786440 | tf_op jit(solution)/shard_map/ppermute | solution.py:451
  83.7 17.3 %collective-permute-start.12 = (bf16[256,512]{1,0:T(8,128)(2,1)S(1)}, bf16[256,512]{1,0:T(8,128)(2,1)S(1)}, u32[]{:S(2)}, u32[]{:S(2)}) collective-permute-start(bf16[256,512]{1,0:T(8,128)(2,1)S(1)} %shard_map.110), channel_id=1, source_target_pairs={{0,4},{1,5},{2,6},{3,7},{4,0},{5,1},{6,2},{7,3},{8,12},{9,13},{10,... | collective-permute-start | bytes 786440 | tf_op jit(solution)/shard_map/ppermute | solution.py:451
  89.2 14.4 %copy-start.18 = (bf16[4,256,512]{2,1,0:T(8,128)(2,1)}, bf16[4,256,512]{2,1,0:T(8,128)(2,1)S(1)}, u32[]{:S(2)}) copy-start(bf16[4,256,512]{2,1,0:T(8,128)(2,1)S(1)} %get-tuple-element.63.refs_1_) | copy-start | bytes 3145732
  101.1 25.2 %collective-permute-start.15 = (bf16[256,512]{1,0:T(8,128)(2,1)S(1)}, bf16[256,512]{1,0:T(8,128)(2,1)S(1)}, u32[]{:S(2)}, u32[]{:S(2)}) collective-permute-start(bf16[256,512]{1,0:T(8,128)(2,1)S(1)} %shard_map.111.refs_0_), channel_id=1, source_target_pairs={{0,24},{8,16},{16,8},{24,0},{1,25},{9,17},{17,9},{25,1},{2,26},{10... | collective-permute-start | bytes 786440 | tf_op jit(solution)/shard_map/ppermute | solution.py:462
  103.6 22.7 %collective-permute-start.14 = (bf16[256,512]{1,0:T(8,128)(2,1)S(1)}, bf16[256,512]{1,0:T(8,128)(2,1)S(1)}, u32[]{:S(2)}, u32[]{:S(2)}) collective-permute-start(bf16[256,512]{1,0:T(8,128)(2,1)S(1)} %shard_map.111.refs_0_), channel_id=1, source_target_pairs={{0,16},{8,24},{16,0},{24,8},{1,17},{9,25},{17,1},{25,9},{2,18},{10... | collective-permute-start | bytes 786440 | tf_op jit(solution)/shard_map/ppermute | solution.py:462
  104.1 22.3 %collective-permute-start.13 = (bf16[256,512]{1,0:T(8,128)(2,1)S(1)}, bf16[256,512]{1,0:T(8,128)(2,1)}, u32[]{:S(2)}, u32[]{:S(2)}) collective-permute-start(bf16[256,512]{1,0:T(8,128)(2,1)S(1)} %shard_map.111.refs_0_), channel_id=1, source_target_pairs={{0,8},{8,0},{16,24},{24,16},{1,9},{9,1},{17,25},{25,17},{2,10},{10... | collective-permute-start | bytes 786440 | tf_op jit(solution)/shard_map/ppermute | solution.py:462
  104.7 2.8 %copy-start.1 = (bf16[1,1,48,256,256]{4,3,2,1,0:T(8,128)(2,1)S(1)}, bf16[1,1,48,256,256]{4,3,2,1,0:T(8,128)(2,1)}, u32[]{:S(2)}) copy-start(bf16[1,1,48,256,256]{4,3,2,1,0:T(8,128)(2,1)} %param.10) | copy-start | bytes 18874372
  107.5 2.2 copy-start.3
  138.3 2.7 %collective-permute-start.16 = (bf16[4,256,512]{2,1,0:T(8,128)(2,1)S(1)}, bf16[4,256,512]{2,1,0:T(8,128)(2,1)S(1)}, u32[]{:S(2)}, u32[]{:S(2)}) collective-permute-start(bf16[4,256,512]{2,1,0:T(8,128)(2,1)S(1)} %get-tuple-element.52), channel_id=1, source_target_pairs={{0,1},{1,0},{2,3},{3,2},{4,5},{5,4},{6,7},{7,6},{8,9},{9,8},{10,11... | collective-permute-start | bytes 3145736 | tf_op jit(solution)/shard_map/ppermute | solution.py:459
  141.2 15.7 %copy-start.6 = (bf16[512,512]{1,0:T(8,128)(2,1)S(1)}, bf16[512,512]{1,0:T(8,128)(2,1)}, u32[]{:S(2)}) copy-start(bf16[512,512]{1,0:T(8,128)(2,1)} %refs_7_.1) | copy-start | bytes 1572868
  141.3 15.7 %copy-start.19 = (bf16[4,256,512]{2,1,0:T(8,128)(2,1)S(1)}, bf16[4,256,512]{2,1,0:T(8,128)(2,1)}, u32[]{:S(2)}) copy-start(bf16[4,256,512]{2,1,0:T(8,128)(2,1)} %copy-done.18) | copy-start | bytes 3145732
  150.9 4.3 %collective-permute-start.21 = (bf16[4,256,512]{2,1,0:T(8,128)(2,1)S(1)}, bf16[4,256,512]{2,1,0:T(8,128)(2,1)S(1)}, u32[]{:S(2)}, u32[]{:S(2)}) collective-permute-start(bf16[4,256,512]{2,1,0:T(8,128)(2,1)S(1)} %get-tuple-element.58), channel_id=1, source_target_pairs={{0,1},{1,0},{2,3},{3,2},{4,5},{5,4},{6,7},{7,6},{8,9},{9,8},{10,11... | collective-permute-start | bytes 3145736 | tf_op jit(solution)/shard_map/ppermute | solution.py:459
  156.2 0.7 copy-start.8
  165.6 8.4 %collective-permute-start.26 = (bf16[512,512]{1,0:T(8,128)(2,1)S(1)}, bf16[512,512]{1,0:T(8,128)(2,1)S(1)}, u32[]{:S(2)}, u32[]{:S(2)}) collective-permute-start(bf16[512,512]{1,0:T(8,128)(2,1)S(1)} %get-tuple-element.66), channel_id=1, source_target_pairs={{0,1},{1,0},{2,3},{3,2},{4,5},{5,4},{6,7},{7,6},{8,9},{9,8},{10,11... | collective-permute-start | bytes 1572872 | tf_op jit(solution)/shard_map/ppermute | solution.py:459
  166.1 7.9 %collective-permute-start.19 = (bf16[256,512]{1,0:T(8,128)(2,1)S(1)}, bf16[256,512]{1,0:T(8,128)(2,1)S(1)}, u32[]{:S(2)}, u32[]{:S(2)}) collective-permute-start(bf16[256,512]{1,0:T(8,128)(2,1)S(1)} %get-tuple-element.55.refs_5_), channel_id=1, source_target_pairs={{0,2},{1,3},{6,4},{7,5},{8,10},{9,11},{14,12},{15,13},{16,18},{17,... | collective-permute-start | bytes 786440 | tf_op jit(solution)/shard_map/ppermute | solution.py:451
  167.4 11.8 %collective-permute-start.24 = (bf16[256,512]{1,0:T(8,128)(2,1)}, bf16[256,512]{1,0:T(8,128)(2,1)S(1)}, u32[]{:S(2)}, u32[]{:S(2)}) collective-permute-start(bf16[256,512]{1,0:T(8,128)(2,1)} %get-tuple-element.61.refs_8_), channel_id=1, source_target_pairs={{0,2},{1,3},{6,4},{7,5},{8,10},{9,11},{14,12},{15,13},{16,18},{17,... | collective-permute-start | bytes 786440 | tf_op jit(solution)/shard_map/ppermute | solution.py:451
  174.0 62.5 %copy-start.9 = (bf16[256,512]{1,0:T(8,128)(2,1)S(1)}, bf16[256,512]{1,0:T(8,128)(2,1)}, u32[]{:S(2)}) copy-start(bf16[256,512]{1,0:T(8,128)(2,1)} %copy-done.8) | copy-start | bytes 786436
  174.2 6.1 %collective-permute-start.27 = (bf16[128,512]{1,0:T(8,128)(2,1)S(1)}, bf16[128,512]{1,0:T(8,128)(2,1)S(1)}, u32[]{:S(2)}, u32[]{:S(2)}) collective-permute-start(bf16[128,512]{1,0:T(8,128)(2,1)S(1)} %get-tuple-element.68), channel_id=1, source_target_pairs={{0,8},{8,0},{16,24},{24,16},{1,9},{9,1},{17,25},{25,17},{2,10},{10... | collective-permute-start | bytes 393224 | tf_op jit(solution)/shard_map/ppermute | solution.py:462
  174.3 7.7 %collective-permute-start.28 = (bf16[128,512]{1,0:T(8,128)(2,1)S(1)}, bf16[128,512]{1,0:T(8,128)(2,1)S(1)}, u32[]{:S(2)}, u32[]{:S(2)}) collective-permute-start(bf16[128,512]{1,0:T(8,128)(2,1)S(1)} %get-tuple-element.69), channel_id=1, source_target_pairs={{0,16},{8,24},{16,0},{24,8},{1,17},{9,25},{17,1},{25,9},{2,18},{10... | collective-permute-start | bytes 393224 | tf_op jit(solution)/shard_map/ppermute | solution.py:462
  177.3 5.9 %collective-permute-start.29 = (bf16[128,512]{1,0:T(8,128)(2,1)S(1)}, bf16[128,512]{1,0:T(8,128)(2,1)S(1)}, u32[]{:S(2)}, u32[]{:S(2)}) collective-permute-start(bf16[128,512]{1,0:T(8,128)(2,1)S(1)} %get-tuple-element.70), channel_id=1, source_target_pairs={{0,24},{8,16},{16,8},{24,0},{1,25},{9,17},{17,9},{25,1},{2,26},{10... | collective-permute-start | bytes 393224 | tf_op jit(solution)/shard_map/ppermute | solution.py:462
  183.2 8.3 %collective-permute-start.32 = (bf16[128,512]{1,0:T(8,128)(2,1)S(1)}, bf16[128,512]{1,0:T(8,128)(2,1)S(1)}, u32[]{:S(2)}, u32[]{:S(2)}) collective-permute-start(bf16[128,512]{1,0:T(8,128)(2,1)S(1)} %shard_map.125.refs_0_), channel_id=1, source_target_pairs={{0,6},{1,7},{2,4},{3,5},{4,2},{5,3},{6,0},{7,1},{8,14},{9,15},{10,... | collective-permute-start | bytes 393224 | tf_op jit(solution)/shard_map/ppermute | solution.py:451
  183.9 13.3 %collective-permute-start.31 = (bf16[128,512]{1,0:T(8,128)(2,1)S(1)}, bf16[128,512]{1,0:T(8,128)(2,1)S(1)}, u32[]{:S(2)}, u32[]{:S(2)}) collective-permute-start(bf16[128,512]{1,0:T(8,128)(2,1)S(1)} %shard_map.125.refs_0_), channel_id=1, source_target_pairs={{0,4},{1,5},{2,6},{3,7},{4,0},{5,1},{6,2},{7,3},{8,12},{9,13},{10,... | collective-permute-start | bytes 393224 | tf_op jit(solution)/shard_map/ppermute | solution.py:451
  187.2 10.0 %collective-permute-start.30 = (bf16[128,512]{1,0:T(8,128)(2,1)S(1)}, bf16[128,512]{1,0:T(8,128)(2,1)S(1)}, u32[]{:S(2)}, u32[]{:S(2)}) collective-permute-start(bf16[128,512]{1,0:T(8,128)(2,1)S(1)} %shard_map.125.refs_0_), channel_id=1, source_target_pairs={{0,2},{1,3},{2,0},{3,1},{4,6},{5,7},{6,4},{7,5},{8,10},{9,11},{10,... | collective-permute-start | bytes 393224 | tf_op jit(solution)/shard_map/ppermute | solution.py:451
  187.6 20.1 %collective-permute-start.17 = (bf16[256,512]{1,0:T(8,128)(2,1)S(1)}, bf16[256,512]{1,0:T(8,128)(2,1)S(1)}, u32[]{:S(2)}, u32[]{:S(2)}) collective-permute-start(bf16[256,512]{1,0:T(8,128)(2,1)S(1)} %get-tuple-element.54), channel_id=1, source_target_pairs={{0,2},{1,3},{2,0},{3,1},{4,6},{5,7},{6,4},{7,5},{8,10},{9,11},{10,... | collective-permute-start | bytes 786440 | tf_op jit(solution)/shard_map/ppermute | solution.py:451
  189.2 23.2 %collective-permute-start.18 = (bf16[256,512]{1,0:T(8,128)(2,1)S(1)}, bf16[256,512]{1,0:T(8,128)(2,1)S(1)}, u32[]{:S(2)}, u32[]{:S(2)}) collective-permute-start(bf16[256,512]{1,0:T(8,128)(2,1)S(1)} %get-tuple-element.55.refs_5_), channel_id=1, source_target_pairs={{2,4},{3,5},{4,2},{5,3},{10,12},{11,13},{12,10},{13,11},{18,20},{1... | collective-permute-start | bytes 786440 | tf_op jit(solution)/shard_map/ppermute | solution.py:451
  197.3 7.2 %collective-permute-start.35 = (bf16[128,512]{1,0:T(8,128)(2,1)S(1)}, bf16[128,512]{1,0:T(8,128)(2,1)S(1)}, u32[]{:S(2)}, u32[]{:S(2)}) collective-permute-start(bf16[128,512]{1,0:T(8,128)(2,1)S(1)} %shard_map.126.refs_0_), channel_id=1, source_target_pairs={{0,24},{8,16},{16,8},{24,0},{1,25},{9,17},{17,9},{25,1},{2,26},{10... | collective-permute-start | bytes 393224 | tf_op jit(solution)/shard_map/ppermute | solution.py:462
  198.5 6.8 %collective-permute-start.34 = (bf16[128,512]{1,0:T(8,128)(2,1)S(1)}, bf16[128,512]{1,0:T(8,128)(2,1)S(1)}, u32[]{:S(2)}, u32[]{:S(2)}) collective-permute-start(bf16[128,512]{1,0:T(8,128)(2,1)S(1)} %shard_map.126.refs_0_), channel_id=1, source_target_pairs={{0,16},{8,24},{16,0},{24,8},{1,17},{9,25},{17,1},{25,9},{2,18},{10... | collective-permute-start | bytes 393224 | tf_op jit(solution)/shard_map/ppermute | solution.py:462
  199.7 6.4 %collective-permute-start.33 = (bf16[128,512]{1,0:T(8,128)(2,1)S(1)}, bf16[128,512]{1,0:T(8,128)(2,1)S(1)}, u32[]{:S(2)}, u32[]{:S(2)}) collective-permute-start(bf16[128,512]{1,0:T(8,128)(2,1)S(1)} %shard_map.126.refs_0_), channel_id=1, source_target_pairs={{0,8},{8,0},{16,24},{24,16},{1,9},{9,1},{17,25},{25,17},{2,10},{10... | collective-permute-start | bytes 393224 | tf_op jit(solution)/shard_map/ppermute | solution.py:462
  206.2 32.6 %collective-permute-start.36 = (bf16[512,512]{1,0:T(8,128)(2,1)S(1)}, bf16[512,512]{1,0:T(8,128)(2,1)}, u32[]{:S(2)}, u32[]{:S(2)}) collective-permute-start(bf16[512,512]{1,0:T(8,128)(2,1)S(1)} %shard_map.127), channel_id=1, source_target_pairs={{0,1},{1,0},{2,3},{3,2},{4,5},{5,4},{6,7},{7,6},{8,9},{9,8},{10,11... | collective-permute-start | bytes 1572872 | tf_op jit(solution)/shard_map/ppermute | solution.py:459
  206.3 13.6 %collective-permute-start.20 = (bf16[256,512]{1,0:T(8,128)(2,1)S(1)}, bf16[256,512]{1,0:T(8,128)(2,1)S(1)}, u32[]{:S(2)}, u32[]{:S(2)}) collective-permute-start(bf16[256,512]{1,0:T(8,128)(2,1)S(1)} %shard_map.117.refs_2_), channel_id=1, source_target_pairs={{0,4},{1,5},{2,6},{3,7},{4,0},{5,1},{6,2},{7,3},{8,12},{9,13},{10,... | collective-permute-start | bytes 786440 | tf_op jit(solution)/shard_map/ppermute | solution.py:451
  206.3 18.3 %collective-permute-start.23 = (bf16[256,512]{1,0:T(8,128)(2,1)}, bf16[256,512]{1,0:T(8,128)(2,1)}, u32[]{:S(2)}, u32[]{:S(2)}) collective-permute-start(bf16[256,512]{1,0:T(8,128)(2,1)} %get-tuple-element.61.refs_8_), channel_id=1, source_target_pairs={{2,4},{3,5},{4,2},{5,3},{10,12},{11,13},{12,10},{13,11},{18,20},{1... | collective-permute-start | bytes 786440 | tf_op jit(solution)/shard_map/ppermute | solution.py:451
  207.7 0.7 copy-start.10
  208.4 16.2 %collective-permute-start.22 = (bf16[256,512]{1,0:T(8,128)(2,1)}, bf16[256,512]{1,0:T(8,128)(2,1)}, u32[]{:S(2)}, u32[]{:S(2)}) collective-permute-start(bf16[256,512]{1,0:T(8,128)(2,1)} %get-tuple-element.60), channel_id=1, source_target_pairs={{0,2},{1,3},{2,0},{3,1},{4,6},{5,7},{6,4},{7,5},{8,10},{9,11},{10,... | collective-permute-start | bytes 786440 | tf_op jit(solution)/shard_map/ppermute | solution.py:451
  212.4 0.7 copy-start.12
  213.1 23.3 %collective-permute-start.25 = (bf16[256,512]{1,0:T(8,128)(2,1)S(1)}, bf16[256,512]{1,0:T(8,128)(2,1)}, u32[]{:S(2)}, u32[]{:S(2)}) collective-permute-start(bf16[256,512]{1,0:T(8,128)(2,1)S(1)} %shard_map.121.refs_4_), channel_id=1, source_target_pairs={{0,4},{1,5},{2,6},{3,7},{4,0},{5,1},{6,2},{7,3},{8,12},{9,13},{10,... | collective-permute-start | bytes 786440 | tf_op jit(solution)/shard_map/ppermute | solution.py:451
  219.9 0.7 copy-start.14
  220.6 0.9 copy-start.11
  221.6 0.9 copy-start.13
  222.5 0.9 copy-start.15
Sparse Core Ops, SparseCore 0:
  11.3 56.6 all-gather.1

commit v3 on v2

v3 whole, which is shorter than its diff:
```python
import functools

import jax
import jax.numpy as jnp
from jax import lax
from jax.experimental import pallas as pl
from jax.experimental.pallas import tpu as pltpu
from jax.sharding import PartitionSpec as P

F32 = jnp.float32
BF16 = jnp.bfloat16
MIB = 1024 * 1024
VMEM = pl.BlockSpec(memory_space=pltpu.VMEM)
SMEM = pl.BlockSpec(memory_space=pltpu.SMEM)
ANY = pl.BlockSpec(memory_space=pl.ANY)


def nbytes(items):
    return sum(x.size * x.dtype.itemsize for x in items)


def run(body, args, specs, outs, scratch=(), flops=0, trans=0, mib=8, after=(), out_specs=None):
    n, extra = len(args), len(after)

    def whole(*refs):
        body(*refs[:n], *refs[n + extra :])

    return pl.pallas_call(
        whole,
        out_shape=outs,
        in_specs=specs + [ANY] * extra,
        out_specs=out_specs or [VMEM] * len(outs),
        scratch_shapes=list(scratch),
        compiler_params=pltpu.CompilerParams(vmem_limit_bytes=mib * MIB),
        cost_estimate=pl.CostEstimate(
            flops=flops, bytes_accessed=nbytes(args) + nbytes(outs), transcendentals=trans
        ),
    )(*args, *after)


def shape(dims, dtype=BF16):
    return jax.ShapeDtypeStruct(dims, dtype)


def list_tiles(count, slot_ref, number_ref, list_ref, local_cols, by_row):
    groups, cap = number_ref.shape[0], list_ref.shape[0] // number_ref.shape[0]
    blank = slot_ref.shape[0] * 1024
    bits = local_cols.bit_length() - 1

    def clear(g, _):
        number_ref[g] = 0
        for j in range(cap):
            list_ref[g * cap + j] = blank
        return 0

    lax.fori_loop(0, groups, clear, 0)

    def place(s, _):
        p = slot_ref[s]
        u, v = lax.shift_right_logical(p, bits), p & (local_cols - 1)
        g, other = (u, v) if by_row else (v, u)
        n = number_ref[g]
        list_ref[g * cap + n] = s * 1024 + other
        number_ref[g] = n + 1
        return 0

    lax.fori_loop(0, count, place, 0)


def repeat_lanes(scale, width):
    return jnp.concatenate([scale] * (width // scale.shape[-1]), 1)


def scale_body(degree, cot, scale, out):
    edge, lanes = scale.shape[1:]
    width = cot.shape[1]
    for i in range(scale.shape[0]):
        part = degree[i // 2 : i // 2 + 1, i % 2 * edge : (i % 2 + 1) * edge]
        line = 1.0 / jnp.sqrt(part.astype(F32))
        scale[i] = jnp.broadcast_to(line, (lanes, edge)).T
    row = lax.axis_index("row")
    for e in range(2):
        value = cot[e * edge : (e + 1) * edge, :].astype(F32)
        out[e] = (value * repeat_lanes(scale[row * 2 + e], width)).T.astype(BF16)


def scale_kernel(degree, cotangent, edge):
    return run(
        scale_body,
        (degree, cotangent),
        [VMEM] * 2,
        [shape((2 * degree.shape[0], edge, 128), F32), shape((2, cotangent.shape[1], edge))],
        flops=cotangent.size,
    )


def prepare_body(local_cols, count_ref, slot_ref, values, scale, out, *lists):
    list_tiles(count_ref[0], slot_ref, lists[0], lists[1], local_cols, True)
    list_tiles(count_ref[0], slot_ref, lists[2], lists[3], local_cols, False)

    def fill(i, _):
        wide = repeat_lanes(scale[i], values.shape[-1])
        out[i] = (values[i].astype(F32) * wide).astype(BF16)
        return 0

    lax.fori_loop(0, local_cols, fill, 0)


def prepare(count, slots, values, scale, block_rows):
    local_cols = values.shape[0]
    sizes = (block_rows, block_rows * local_cols, local_cols, block_rows * local_cols)
    return run(
        functools.partial(prepare_body, local_cols),
        (count, slots, values, scale),
        [SMEM] * 2 + [VMEM] * 2,
        [shape(values.shape)] + [shape((n,), jnp.int32) for n in sizes],
        flops=values.size,
        out_specs=[VMEM] + [SMEM] * 4,
        mib=12,
    )


def tile_copy(tiles_ref, held, sems, s):
    return pltpu.make_async_copy(tiles_ref.at[s], held.at[s], sems.at[s])


def each_tile(g, number_ref, list_ref, action):
    cap = list_ref.shape[0] // number_ref.shape[0]

    def one(j, _):
        action(lax.shift_right_logical(list_ref[g * cap + j], 10))
        return 0

    lax.fori_loop(0, number_ref[g], one, 0)


def sum_group(g, number_ref, list_ref, total, product, store):
    cap = list_ref.shape[0] // number_ref.shape[0]
    n = number_ref[g]

    def take(start, width):
        entries = [list_ref[g * cap + start + j] for j in range(width)]
        return product([(lax.shift_right_logical(x, 10), x & 1023) for x in entries])

    @pl.when(n == 0)
    def _():
        store(jnp.zeros_like(total))

    @pl.when(jnp.logical_and(n >= 1, n <= 2))
    def _():
        store(take(0, 2))

    @pl.when(jnp.logical_and(n >= 3, n <= 4))
    def _():
        store(take(0, 4))

    @pl.when(n > 4)
    def _():
        total[...] = jnp.zeros_like(total)

        def more(m, _):
            total[...] += take(4 * m, 4)
            return 0

        lax.fori_loop(0, lax.shift_right_logical(n + 3, 2), more, 0)
        store(total[...])


def joined_dot(lhs, rhs):
    return jnp.dot(
        jnp.concatenate(lhs, 1), jnp.concatenate(rhs, 0), preferred_element_type=F32
    )


def forward_body(first, half, n_in, *refs):
    number_ref, list_ref, tiles_ref = refs[:3]
    inputs = refs[3 : 3 + n_in]
    give, keep, held, source, total, sems, source_sems = refs[3 + n_in :]
    col, row = lax.axis_index("col"), lax.axis_index("row")
    parts = give.shape[0]
    per = source.shape[0] // n_in
    copies = [
        pltpu.make_async_copy(x, source.at[pl.ds(i * per, per)], source_sems.at[i])
        for i, x in enumerate(inputs)
    ]
    for copy in copies:
        copy.start()

    def block_row(i):
        flip = jnp.where(i < parts, 1, 0)
        return (col ^ (2 * lax.rem(i, parts) + flip)) * 2 + half

    def start(i, _):
        each_tile(
            block_row(i),
            number_ref,
            list_ref,
            lambda s: tile_copy(tiles_ref, held, sems, s).start(),
        )
        return 0

    lax.fori_loop(0, 2 * parts, start, 0)
    held[held.shape[0] - 1] = jnp.zeros(held.shape[1:], BF16)
    for copy in copies:
        copy.wait()

    def product(pieces):
        def locate(v):
            return v if first else (v & 1) * per + (lax.shift_right_logical(v, 1) ^ row)

        return joined_dot([held[s] for s, _ in pieces], [source[locate(v)] for _, v in pieces])

    for base, out in ((0, give), (parts, keep)):

        def block(i, _):
            def store(value):
                out[i] = value.astype(BF16)

            g = block_row(base + i)
            each_tile(
                g, number_ref, list_ref, lambda s: tile_copy(tiles_ref, held, sems, s).wait()
            )
            sum_group(g, number_ref, list_ref, total, product, store)
            return 0

        lax.fori_loop(0, parts, block, 0)


def forward(number, entries, tiles, sources, first, half, after):
    slots_n, edge, _ = tiles.shape
    width = sources[0].shape[-1]
    blocks = sum(x.shape[0] for x in sources)
    return run(
        functools.partial(forward_body, first, half, len(sources)),
        (number, entries, tiles, *sources),
        [SMEM, SMEM, ANY] + [ANY] * len(sources),
        [shape((number.shape[0] // 4, edge, width))] * 2,
        [
            pltpu.VMEM((slots_n + 1, edge, edge), BF16),
            pltpu.VMEM((blocks, edge, width), BF16),
            pltpu.VMEM((edge, width), F32),
            pltpu.SemaphoreType.DMA((slots_n,)),
            pltpu.SemaphoreType.DMA((len(sources),)),
        ],
        flops=slots_n * edge * edge * width,
        mib=20,
        after=after,
    )


def backward_body(number_ref, list_ref, tiles_ref, ranged, out, *refs):
    held, source, total, sems, source_sem = refs
    mask = lax.axis_index("row") * 2
    copy = pltpu.make_async_copy(ranged, source, source_sem)
    copy.start()

    def start(i, _):
        each_tile(
            i ^ mask,
            number_ref,
            list_ref,
            lambda s: tile_copy(tiles_ref, held, sems, s).start(),
        )
        return 0

    lax.fori_loop(0, out.shape[0], start, 0)
    held[held.shape[0] - 1] = jnp.zeros(held.shape[1:], BF16)
    copy.wait()

    def product(pieces):
        return joined_dot([source[u] for _, u in pieces], [held[s] for s, _ in pieces])

    def block(i, _):
        def store(value):
            out[i] = value.astype(BF16)

        each_tile(
            i ^ mask, number_ref, list_ref, lambda s: tile_copy(tiles_ref, held, sems, s).wait()
        )
        sum_group(i ^ mask, number_ref, list_ref, total, product, store)
        return 0

    lax.fori_loop(0, out.shape[0], block, 0)


def backward(number, entries, tiles, ranged):
    slots_n, edge, _ = tiles.shape
    width = ranged.shape[1]
    return run(
        backward_body,
        (number, entries, tiles, ranged),
        [SMEM, SMEM, ANY, ANY],
        [shape((number.shape[0], width, edge))],
        [
            pltpu.VMEM((slots_n + 1, edge, edge), BF16),
            pltpu.VMEM(ranged.shape, BF16),
            pltpu.VMEM((width, edge), F32),
            pltpu.SemaphoreType.DMA((slots_n,)),
            pltpu.SemaphoreType.DMA,
        ],
        flops=2 * slots_n * edge * edge * width,
        mib=20,
    )[0]


def pair_sum_body(n, keep, come, *outs):
    for j in range(n):
        outs[j][...] = (keep[j].astype(F32) + come[j].astype(F32)).astype(BF16)


def pair_sum(keep, come):
    n = keep.shape[0]
    return run(
        functools.partial(pair_sum_body, n),
        (keep, come),
        [VMEM] * 2,
        [shape(keep.shape[1:])] * n,
        flops=keep.size,
    )


def tree(items):
    while len(items) > 1:
        items = [a + b for a, b in zip(items[::2], items[1::2])]
    return items[0]


def agg_body(n, half, *refs):
    scale, out = refs[n], refs[n + 1]
    summed = tree([x[...].astype(F32) for x in refs[:n]])
    out[...] = (summed * repeat_lanes(scale[lax.axis_index("row") * 2 + half], summed.shape[1])).astype(
        BF16
    )


def aggregate(parts, scale, half, after):
    return run(
        functools.partial(agg_body, len(parts), half),
        (*parts, scale),
        [VMEM] * (len(parts) + 1),
        [shape(parts[0].shape)],
        flops=parts[0].size * len(parts),
        after=after,
    )[0]


def first_body(n, half, *refs):
    scale, weight, agg, out = refs[n:]
    row = lax.axis_index("row")
    for j in range(n):
        value = jnp.dot(refs[j][...], weight[...], preferred_element_type=F32)
        wide = repeat_lanes(scale[(row ^ j) * 2 + half], value.shape[1])
        out[j] = (jax.nn.gelu(value) * wide).astype(BF16)
        agg[j] = refs[j][...]


def first_layer(aggs, scale, weight, half, after):
    n = len(aggs)
    dims = (n, *aggs[0].shape)
    return run(
        functools.partial(first_body, n, half),
        (*aggs, scale, weight),
        [VMEM] * (n + 2),
        [shape(dims)] * 2,
        flops=2 * n * dims[1] * weight.size,
        trans=n * aggs[0].size,
        mib=12,
        after=after,
    )


def second_body(n, half, *refs):
    scale, weight, out = refs[n:]
    summed = tree([x[...].astype(F32) for x in refs[:n]])
    agg = (summed * repeat_lanes(scale[lax.axis_index("row") * 2 + half], summed.shape[1])).astype(
        BF16
    )
    out[...] = jnp.dot(agg, weight[...], preferred_element_type=F32).astype(BF16)


def second_layer(parts, scale, weight, half):
    dims = parts[0].shape
    return run(
        functools.partial(second_body, len(parts), half),
        (*parts, scale, weight),
        [VMEM] * (len(parts) + 2),
        [shape(dims)],
        flops=2 * dims[0] * weight.size,
    )[0]


def grad_body(hidden_ref, *refs):
    aggs, outs = refs[:2], refs[2:4]
    scale, w_first, w_second, give, keep, first, second = refs[4:]
    row = lax.axis_index("row")
    core = lax.rem(lax.axis_index("col"), 2)
    first[...] = jnp.zeros_like(first)
    second[...] = jnp.zeros_like(second)
    for e in range(2):

        def block(j, _):
            hidden, agg = hidden_ref[2 * j + e], aggs[e][j]
            pre = jnp.dot(agg, w_first[...], preferred_element_type=F32)
            grad_hidden = lax.dot_general(
                hidden, w_second[...], (((0,), (1,)), ((), ())), preferred_element_type=F32
            )
            _, pullback = jax.vjp(jax.nn.gelu, pre)
            wide = repeat_lanes(scale[(row ^ j) * 2 + e], pre.shape[1])
            grad_pre = pullback(grad_hidden * wide)[0].astype(BF16)
            first[...] += lax.dot_general(
                agg, grad_pre, (((0,), (0,)), ((), ())), preferred_element_type=F32
            )
            second[...] += lax.dot_general(
                outs[e][j], hidden, (((0,), (1,)), ((), ())), preferred_element_type=F32
            )
            return 0

        lax.fori_loop(0, aggs[e].shape[0], block, 0)
    keep[...] = jnp.where(core == 0, first[...], second[...]).astype(BF16)
    give[...] = jnp.where(core == 0, second[...], first[...]).astype(BF16)


def weight_grads(hidden, aggs, outs, scale, w_first, w_second, after):
    return run(
        grad_body,
        (hidden, *aggs, *outs, scale, w_first, w_second),
        [VMEM] * 8,
        [shape(w_first.shape)] * 2,
        [pltpu.VMEM(w_first.shape, F32)] * 2,
        flops=8 * hidden.size * w_first.shape[0],
        trans=hidden.size,
        mib=28,
        after=after,
    )


def split_body(n, keep, come, *outs):
    row = lax.axis_index("row")
    rows = keep.shape[0] // n
    for j in range(n):
        part = pl.ds(pl.multiple_of((row ^ j) * rows, rows), rows)
        outs[j][...] = (keep[part, :].astype(F32) + come[part, :].astype(F32)).astype(BF16)


def split_sum(keep, come, n, after):
    rows, width = keep.shape
    return run(
        functools.partial(split_body, n),
        (keep, come),
        [VMEM] * 2,
        [shape((rows // n, width))] * n,
        flops=keep.size,
        after=after,
    )


def sum_body(n, *refs):
    refs[n][...] = tree([x[...].astype(F32) for x in refs[:n]]).astype(BF16)


def sum_parts(parts, after=()):
    return run(
        functools.partial(sum_body, len(parts)),
        tuple(parts),
        [VMEM] * len(parts),
        [shape(parts[0].shape)],
        flops=parts[0].size * len(parts),
        after=after,
    )[0]


def join_body(n, *refs):
    row = lax.axis_index("row")
    rows = refs[0].shape[0]
    for j in range(n):
        refs[n][pl.ds(pl.multiple_of((row ^ j) * rows, rows), rows), :] = refs[j][...]


def join(parts):
    rows, width = parts[0].shape
    return run(
        functools.partial(join_body, len(parts)),
        tuple(parts),
        [VMEM] * len(parts),
        [shape((rows * len(parts), width))],
    )[0]


def select_body(mine, other, first, second):
    core = lax.rem(lax.axis_index("col"), 2)
    first[...] = jnp.where(core == 0, mine[...].astype(F32), other[...].astype(F32))
    second[...] = jnp.where(core == 0, other[...].astype(F32), mine[...].astype(F32))


def select(mine, other):
    return run(select_body, (mine, other), [VMEM] * 2, [shape(mine.shape, F32)] * 2)


def per_device(features, degree, tile_vals, tile_slot, tile_count, w_first, w_second, cotangent):
    n_row, n_col = lax.axis_size("row"), lax.axis_size("col")
    line = n_col // 2
    piece, width = cotangent.shape
    tiles = tile_vals[0, 0]
    edge = tiles.shape[-1]
    local_cols = n_row * 2
    slots, count = tile_slot[0, 0], tile_count[0]

    def col_send(value, pairs):
        return lax.ppermute(
            value, "col", [(2 * a + k, 2 * b + k) for a, b in pairs for k in range(2)]
        )

    def line_flip(value, j):
        return col_send(value, [(a, a ^ j) for a in range(line)])

    def core_flip(value):
        return lax.ppermute(value, "col", [(a, a ^ 1) for a in range(n_col)])

    def row_flip(value, j):
        return lax.ppermute(value, "row", [(a, a ^ j) for a in range(n_row)])

    def scatter_line(own):
        if line != 4:
            return [own[0]] + [line_flip(own[j], j) for j in range(1, line)], own[0]
        inward = col_send(own[3], [(0, 1), (3, 2)])
        middle = col_send(own[3], [(1, 2), (2, 1)])
        near = line_flip(own[1], 1)
        joined = sum_parts([own[2], inward])
        return [own[0], near, middle, line_flip(joined, 2)], joined

    halves = piece // edge
    scale, scaled = scale_kernel(degree[:, 0], cotangent, edge)
    ranged = lax.all_gather(scaled, "col", axis=0, tiled=True)
    values = features[:, 0].reshape(local_cols, edge, width)
    first_in, number, entries, t_number, t_entries = prepare(
        count, slots, values, scale, 2 * n_col
    )

    aggs, outs = [], []
    partials, after = [], ()
    for half in range(halves):
        give, keep = forward(number, entries, tiles, (first_in,), True, half, after)
        own = pair_sum(keep, core_flip(give))
        after = (own[-1],)
        partials.append(own)
    hidden = backward(t_number, t_entries, tiles, ranged)
    for half in range(halves):
        after = (agg,) if half else ()
        agg = aggregate(scatter_line(partials[half])[0], scale, half, after)
        spread = [agg] + [row_flip(agg, j) for j in range(1, n_row)]
        stacked, out = first_layer(spread, scale, w_first, half, (hidden,) if half else ())
        aggs.append(stacked)
        outs.append(out)

    partials, after = [], ()
    for half in range(halves):
        give, keep = forward(number, entries, tiles, outs, False, half, after)
        own = pair_sum(keep, core_flip(give))
        after = (own[-1],)
        partials.append(own)

    give, keep = weight_grads(hidden, aggs, outs, scale, w_first, w_second, after)
    arrived, marks = zip(*[scatter_line(own) for own in partials])
    parts = split_sum(keep, core_flip(give), n_row, marks[:1])
    part = sum_parts([parts[0]] + [row_flip(parts[j], j) for j in range(1, n_row)], marks[1:])
    part = sum_parts([part] + [line_flip(part, j) for j in range(1, line)], arrived[0][1:])
    mine = join([part] + [row_flip(part, j) for j in range(1, n_row)])
    grad_first, grad_second = select(mine, core_flip(mine))

    logits = [second_layer(arrived[half], scale, w_second, half) for half in range(halves)]
    return jnp.concatenate(logits, 0), grad_first, grad_second


def solution(mesh):
    return jax.shard_map(
        per_device,
        mesh=mesh,
        in_specs=(
            P(None, "col", None, None),
            P(None, "col", None),
            P("row", "col", None, None, None),
            P("row", "col", None),
            P("row", "col"),
            P(),
            P(),
            P(("row", "col"), None),
        ),
        out_specs=(P(("row", "col"), None), P(), P()),
        check_vma=False,
    )
```

time: 251 us -> 251 us (level)
  starting transfers between devices: 53.7 us -> 60.3 us
  local copies, waits for them, and re-layouts: 16.8 us -> 11.8 us
  other arithmetic: 4.2 us -> 0.83 us
  waiting for transfers between devices: 84.9 us -> 87.6 us
    ppermute x19, starting transfers between devices: 33.7 us -> 45.3 us  [col_send(): lax.ppermute(value, 'col', [(2 * a + k, 2 * b + k) for a, b in pairs for...]
    ppermute x19, waiting for transfers between devices: 67.1 us -> 72.9 us  [col_send(): lax.ppermute(value, 'col', [(2 * a + k, 2 * b + k) for a, b in pairs for...]
    ppermute x6, starting transfers between devices: 5.78 us -> 0.57 us  [core_flip(): return lax.ppermute(value, 'col', [(a, a ^ 1) for a in range(n_col)])]
    unnamed x40 -> x21, local copies, waits for them, and re-layouts: 15.9 us -> 11.8 us
    ppermute x12, waiting for transfers between devices: 10.5 us -> 6.8 us  [row_flip(): return lax.ppermute(value, 'row', [(a, a ^ j) for a in range(n_row)])]
    pallas_call x25 -> x27, Pallas kernels: 73.5 us -> 73.7 us  [run(): pl.pallas_call(whole, out_shape=outs, in_specs=specs + [ANY] * extra, out...]
  transfers between devices with their start and end apart: 38 -> 38, of which waited for: 25 -> 18; matrix products, arithmetic and copies ran while one was open for 0% -> 0% of each run, Pallas kernels for 17% -> 17%
where the time goes in v3:
time: 251 us; the launch traced here: 249 us
  waiting for transfers between devices  87.6 us (35%)
  Pallas kernels  73.7 us (29%)
  starting transfers between devices  60.3 us (24%)
  between operations  15.1 us (6%)
  local copies, waits for them, and re-layouts  11.8 us (5%)
    pallas_call x27, Pallas kernels, run(): pl.pallas_call(whole, out_shape=outs, in_specs=specs + [ANY] * extra, out...  73.7 us
    ppermute x19, waiting for transfers between devices, col_send(): lax.ppermute(value, 'col', [(2 * a + k, 2 * b + k) for a, b in pairs for...  72.9 us
    ppermute x19, starting transfers between devices, col_send(): lax.ppermute(value, 'col', [(2 * a + k, 2 * b + k) for a, b in pairs for...  45.3 us
    ppermute x12, starting transfers between devices, row_flip(): return lax.ppermute(value, 'row', [(a, a ^ j) for a in range(n_row)])  14.4 us
    unnamed x21, local copies, waits for them, and re-layouts  11.8 us
    ppermute x6, waiting for transfers between devices, core_flip(): return lax.ppermute(value, 'col', [(a, a ^ 1) for a in range(n_col)])  7.95 us
    ppermute x12, waiting for transfers between devices, row_flip(): return lax.ppermute(value, 'row', [(a, a ^ j) for a in range(n_row)])  6.8 us
  transfers between devices with their start and end apart: 38, of which 18 were waited for; matrix products, arithmetic and copies ran while one was open for 0% of the time, Pallas kernels for 17%

profile of v3, /device:TPU:0, one launch (start us, length us, event | category | flops | bytes accessed | tf_op | source)
XLA Modules:
  0.0 249.2 jit_solution(9353261284969324136)
XLA Ops:
  7.2 0.7 copy.13
  7.9 1.0 copy-done.6
  9.0 1.3 shard_map.103
  11.0 1.6 copy-done.4
  13.2 2.6 %shard_map.104 = (bf16[8,256,512]{2,1,0:T(8,128)(2,1)S(1)}, s32[16]{0:T(128)S(1)}, s32[128]{0:T(128)S(1)}, s32[8]{0:T(128)S(1)}, s32[128]{0:T(128)S(1)}) custom-call(s32[1]{0:T(128)} %bitcast.7.refs_0_, s32[48]{0:T(128)S(1)} %bitcast.15, bf16[8,256,512]{2,1,0:T(8,128)(2,1)S(1)} %bitcast.13, f32[8,256,128]{2,1,0:T(8,128)S(1)} %get-tuple-element.46.refs_3_.refs_4_.refs_5_), custom_call_target="tpu_custom_call" | custom-call | flops 1048576 | bytes 5244196 | tf_op jit(solution)/shard_map/pallas_call | solution.py:28
  15.8 2.8 %copy-done = bf16[1,1,48,256,256]{4,3,2,1,0:T(8,128)(2,1)S(1)} copy-done((bf16[1,1,48,256,256]{4,3,2,1,0:T(8,128)(2,1)S(1)}, bf16[1,1,48,256,256]{4,3,2,1,0:T(8,128)(2,1)}, u32[]{:S(2)}) %copy-start) | copy-done | bytes 6291480
  18.6 8.1 %shard_map.105 = (bf16[4,256,512]{2,1,0:T(8,128)(2,1)S(1)}, bf16[4,256,512]{2,1,0:T(8,128)(2,1)S(1)}) custom-call(s32[16]{0:T(128)S(1)} %get-tuple-element.47.refs_0_, s32[128]{0:T(128)S(1)} %get-tuple-element.48.refs_1_, bf16[48,256,256]{2,1,0:T(8,128)(2,1)S(1)} %bitcast.8, bf16[8,256,512]{2,1,0:T(8,128)(2,1)S(1)} %get-tuple-element.49.refs_3_), custom_call_target="tpu_custom_call" | custom-call | flops 1610612736 | bytes 10486336 | tf_op jit(solution)/shard_map/pallas_call | solution.py:28
  26.8 2.6 %collective-permute-done.refs_1_ = bf16[4,256,512]{2,1,0:T(8,128)(2,1)S(1)} collective-permute-done((bf16[4,256,512]{2,1,0:T(8,128)(2,1)S(1)}, bf16[4,256,512]{2,1,0:T(8,128)(2,1)S(1)}, u32[]{:S(2)}, u32[]{:S(2)}) %collective-permute-start) | collective-permute-done | bytes 1048608 | tf_op jit(solution)/shard_map/ppermute | solution.py:517
  29.7 10.2 %shard_map.110 = (bf16[4,256,512]{2,1,0:T(8,128)(2,1)S(1)}, bf16[4,256,512]{2,1,0:T(8,128)(2,1)S(1)}) custom-call(s32[16]{0:T(128)S(1)} %get-tuple-element.47.refs_0_, s32[128]{0:T(128)S(1)} %get-tuple-element.48.refs_1_, bf16[48,256,256]{2,1,0:T(8,128)(2,1)S(1)} %bitcast.9, bf16[8,256,512]{2,1,0:T(8,128)(2,1)S(1)} %get-tuple-element.49.refs_3_, ...), custom_call_target="tpu_custom_call" | custom-call | flops 1610612736 | bytes 10486336 | tf_op jit(solution)/shard_map/pallas_call | solution.py:28
  40.0 4.5 %collective-permute-start.3 = (bf16[256,512]{1,0:T(8,128)(2,1)S(1)}, bf16[256,512]{1,0:T(8,128)(2,1)S(1)}, u32[]{:S(2)}, u32[]{:S(2)}) collective-permute-start(bf16[256,512]{1,0:T(8,128)(2,1)S(1)} %get-tuple-element.54.refs_4_), channel_id=1, source_target_pairs={{0,2},{1,3},{6,4},{7,5},{8,10},{9,11},{14,12},{15,13},{16,18},{17,... | collective-permute-start | bytes 786440 | tf_op jit(solution)/shard_map/ppermute | solution.py:509
  44.5 0.7 collective-permute-start.2
  45.2 4.1 %collective-permute-start.1 = (bf16[256,512]{1,0:T(8,128)(2,1)S(1)}, bf16[256,512]{1,0:T(8,128)(2,1)S(1)}, u32[]{:S(2)}, u32[]{:S(2)}) collective-permute-start(bf16[256,512]{1,0:T(8,128)(2,1)S(1)} %get-tuple-element.53), channel_id=1, source_target_pairs={{0,2},{1,3},{2,0},{3,1},{4,6},{5,7},{6,4},{7,5},{8,10},{9,11},{10,... | collective-permute-start | bytes 786440 | tf_op jit(solution)/shard_map/ppermute | solution.py:509
  49.3 7.5 %collective-permute-done.3.refs_1_ = bf16[256,512]{1,0:T(8,128)(2,1)S(1)} collective-permute-done((bf16[256,512]{1,0:T(8,128)(2,1)S(1)}, bf16[256,512]{1,0:T(8,128)(2,1)S(1)}, u32[]{:S(2)}, u32[]{:S(2)}) %collective-permute-start.3) | collective-permute-done | bytes 262176 | tf_op jit(solution)/shard_map/ppermute | solution.py:509
  56.8 5.4 %collective-permute-start.4 = (bf16[256,512]{1,0:T(8,128)(2,1)S(1)}, bf16[256,512]{1,0:T(8,128)(2,1)S(1)}, u32[]{:S(2)}, u32[]{:S(2)}) collective-permute-start(bf16[256,512]{1,0:T(8,128)(2,1)S(1)} %shard_map.107), channel_id=1, source_target_pairs={{0,4},{1,5},{2,6},{3,7},{4,0},{5,1},{6,2},{7,3},{8,12},{9,13},{10,... | collective-permute-start | bytes 786440 | tf_op jit(solution)/shard_map/ppermute | solution.py:509
  62.5 1.6 collective-permute-start.11
  64.1 2.9 %collective-permute-done.1.refs_1_ = bf16[256,512]{1,0:T(8,128)(2,1)S(1)} collective-permute-done((bf16[256,512]{1,0:T(8,128)(2,1)S(1)}, bf16[256,512]{1,0:T(8,128)(2,1)S(1)}, u32[]{:S(2)}, u32[]{:S(2)}) %collective-permute-start.1) | collective-permute-done | bytes 262176 | tf_op jit(solution)/shard_map/ppermute | solution.py:509
  67.0 5.6 %collective-permute-done.4.refs_3_ = bf16[256,512]{1,0:T(8,128)(2,1)S(1)} collective-permute-done((bf16[256,512]{1,0:T(8,128)(2,1)S(1)}, bf16[256,512]{1,0:T(8,128)(2,1)S(1)}, u32[]{:S(2)}, u32[]{:S(2)}) %collective-permute-start.4) | collective-permute-done | bytes 262176 | tf_op jit(solution)/shard_map/ppermute | solution.py:509
  72.7 1.3 collective-permute-start.5
  74.1 1.5 collective-permute-start.6
  75.6 0.7 collective-permute-start.7
  76.3 0.8 collective-permute-start.10
  77.1 0.7 collective-permute-done.11.refs_1_
  77.9 4.9 %collective-permute-start.9 = (bf16[256,512]{1,0:T(8,128)(2,1)S(1)}, bf16[256,512]{1,0:T(8,128)(2,1)S(1)}, u32[]{:S(2)}, u32[]{:S(2)}) collective-permute-start(bf16[256,512]{1,0:T(8,128)(2,1)S(1)} %get-tuple-element.60), channel_id=1, source_target_pairs={{0,2},{1,3},{2,0},{3,1},{4,6},{5,7},{6,4},{7,5},{8,10},{9,11},{10,... | collective-permute-start | bytes 786440 | tf_op jit(solution)/shard_map/ppermute | solution.py:509
  82.9 2.6 %collective-permute-start.12 = (bf16[256,512]{1,0:T(8,128)(2,1)S(1)}, bf16[256,512]{1,0:T(8,128)(2,1)S(1)}, u32[]{:S(2)}, u32[]{:S(2)}) collective-permute-start(bf16[256,512]{1,0:T(8,128)(2,1)S(1)} %shard_map.112), channel_id=1, source_target_pairs={{0,4},{1,5},{2,6},{3,7},{4,0},{5,1},{6,2},{7,3},{8,12},{9,13},{10,... | collective-permute-start | bytes 786440 | tf_op jit(solution)/shard_map/ppermute | solution.py:509
  85.4 2.0 collective-permute-done.6.refs_2_
  87.4 1.0 shard_map.109
  88.5 1.0 collective-permute-done.9.refs_1_
  89.5 10.5 %collective-permute-done.12.refs_3_ = bf16[256,512]{1,0:T(8,128)(2,1)S(1)} collective-permute-done((bf16[256,512]{1,0:T(8,128)(2,1)S(1)}, bf16[256,512]{1,0:T(8,128)(2,1)S(1)}, u32[]{:S(2)}, u32[]{:S(2)}) %collective-permute-start.12) | collective-permute-done | bytes 262176 | tf_op jit(solution)/shard_map/ppermute | solution.py:509
  100.2 1.5 collective-permute-start.13
  101.7 1.6 collective-permute-start.14
  103.7 2.8 %copy-done.1 = bf16[1,1,48,256,256]{4,3,2,1,0:T(8,128)(2,1)S(1)} copy-done((bf16[1,1,48,256,256]{4,3,2,1,0:T(8,128)(2,1)S(1)}, bf16[1,1,48,256,256]{4,3,2,1,0:T(8,128)(2,1)}, u32[]{:S(2)}) %copy-start.1) | copy-done | bytes 6291480
  106.5 2.2 copy-done.2
  108.7 17.4 %shard_map.114.refs_6_.refs_0_ = bf16[8,512,256]{2,1,0:T(8,128)(2,1)S(1)} custom-call(s32[8]{0:T(128)S(1)} %get-tuple-element.63.refs_0_, s32[128]{0:T(128)S(1)} %get-tuple-element.64.refs_1_, bf16[48,256,256]{2,1,0:T(8,128)(2,1)S(1)} %bitcast.10, bf16[16,512,256]{2,1,0:T(8,128)(2,1)S(1)} %copy-done.2), custom_call_target="tpu_custom_call" | custom-call | flops 3221225472 | bytes 12583456 | tf_op jit(solution)/shard_map/pallas_call | solution.py:28
  126.1 2.0 shard_map.115
  128.2 8.1 %shard_map.116 = (bf16[4,256,512]{2,1,0:T(8,128)(2,1)S(1)}, bf16[4,256,512]{2,1,0:T(8,128)(2,1)S(1)}) custom-call(s32[16]{0:T(128)S(1)} %get-tuple-element.47.refs_0_, s32[128]{0:T(128)S(1)} %get-tuple-element.48.refs_1_, bf16[48,256,256]{2,1,0:T(8,128)(2,1)S(1)} %bitcast.11, bf16[4,256,512]{2,1,0:T(8,128)(2,1)S(1)} %get-tuple-element.56.refs_3_, ...), custom_call_target="tpu_custom_call" | custom-call | flops 1610612736 | bytes 10486336 | tf_op jit(solution)/shard_map/pallas_call | solution.py:28
  136.4 2.6 %collective-permute-done.16.refs_1_ = bf16[4,256,512]{2,1,0:T(8,128)(2,1)S(1)} collective-permute-done((bf16[4,256,512]{2,1,0:T(8,128)(2,1)S(1)}, bf16[4,256,512]{2,1,0:T(8,128)(2,1)S(1)}, u32[]{:S(2)}, u32[]{:S(2)}) %collective-permute-start.16) | collective-permute-done | bytes 1048608 | tf_op jit(solution)/shard_map/ppermute | solution.py:517
  139.3 10.2 %shard_map.120 = (bf16[4,256,512]{2,1,0:T(8,128)(2,1)S(1)}, bf16[4,256,512]{2,1,0:T(8,128)(2,1)S(1)}) custom-call(s32[16]{0:T(128)S(1)} %get-tuple-element.47.refs_0_, s32[128]{0:T(128)S(1)} %get-tuple-element.48.refs_1_, bf16[48,256,256]{2,1,0:T(8,128)(2,1)S(1)} %bitcast.12, bf16[4,256,512]{2,1,0:T(8,128)(2,1)S(1)} %get-tuple-element.56.refs_3_, ...), custom_call_target="tpu_custom_call" | custom-call | flops 1610612736 | bytes 10486336 | tf_op jit(solution)/shard_map/pallas_call | solution.py:28
  149.6 2.6 %collective-permute-done.21.refs_1_ = bf16[4,256,512]{2,1,0:T(8,128)(2,1)S(1)} collective-permute-done((bf16[4,256,512]{2,1,0:T(8,128)(2,1)S(1)}, bf16[4,256,512]{2,1,0:T(8,128)(2,1)S(1)}, u32[]{:S(2)}, u32[]{:S(2)}) %collective-permute-start.21) | collective-permute-done | bytes 1048608 | tf_op jit(solution)/shard_map/ppermute | solution.py:517
  152.5 8.7 %shard_map.124 = (bf16[512,512]{1,0:T(8,128)(2,1)S(1)}, bf16[512,512]{1,0:T(8,128)(2,1)S(1)}) custom-call(bf16[8,512,256]{2,1,0:T(8,128)(2,1)S(1)} %shard_map.114.refs_6_.refs_0_, bf16[4,256,512]{2,1,0:T(8,128)(2,1)S(1)} %copy-done.9, bf16[4,256,512]{2,1,0:T(8,128)(2,1)S(1)} %get-tuple-element.80.refs_2_, ...), custom_call_target="tpu_custom_call" | custom-call | flops 4294967296 | bytes 9437184 | tf_op jit(solution)/shard_map/pallas_call | solution.py:28
  161.4 1.3 collective-permute-start.19
  162.7 1.3 collective-permute-start.24
  164.1 5.3 %collective-permute-done.19.refs_1_ = bf16[256,512]{1,0:T(8,128)(2,1)S(1)} collective-permute-done((bf16[256,512]{1,0:T(8,128)(2,1)S(1)}, bf16[256,512]{1,0:T(8,128)(2,1)S(1)}, u32[]{:S(2)}, u32[]{:S(2)}) %collective-permute-start.19) | collective-permute-done | bytes 262176 | tf_op jit(solution)/shard_map/ppermute | solution.py:509
  169.6 2.2 collective-permute-start.27
  171.8 2.5 collective-permute-start.17
  174.7 1.1 collective-permute-start.29
  175.8 0.7 collective-permute-start.18
  176.5 4.4 %collective-permute-start.20 = (bf16[256,512]{1,0:T(8,128)(2,1)S(1)}, bf16[256,512]{1,0:T(8,128)(2,1)S(1)}, u32[]{:S(2)}, u32[]{:S(2)}) collective-permute-start(bf16[256,512]{1,0:T(8,128)(2,1)S(1)} %shard_map.118.refs_2_), channel_id=1, source_target_pairs={{0,4},{1,5},{2,6},{3,7},{4,0},{5,1},{6,2},{7,3},{8,12},{9,13},{10,... | collective-permute-start | bytes 786440 | tf_op jit(solution)/shard_map/ppermute | solution.py:509
  181.4 1.4 collective-permute-start.31
  182.8 2.8 %collective-permute-start.32 = (bf16[128,512]{1,0:T(8,128)(2,1)S(1)}, bf16[128,512]{1,0:T(8,128)(2,1)S(1)}, u32[]{:S(2)}, u32[]{:S(2)}) collective-permute-start(bf16[128,512]{1,0:T(8,128)(2,1)S(1)} %shard_map.126.refs_0_), channel_id=1, source_target_pairs={{0,6},{1,7},{2,4},{3,5},{4,2},{5,3},{6,0},{7,1},{8,14},{9,15},{10,... | collective-permute-start | bytes 393224 | tf_op jit(solution)/shard_map/ppermute | solution.py:509
  185.6 19.0 %collective-permute-done.20.refs_3_.refs_6_ = bf16[256,512]{1,0:T(8,128)(2,1)S(1)} collective-permute-done((bf16[256,512]{1,0:T(8,128)(2,1)S(1)}, bf16[256,512]{1,0:T(8,128)(2,1)S(1)}, u32[]{:S(2)}, u32[]{:S(2)}) %collective-permute-start.20) | collective-permute-done | bytes 262176 | tf_op jit(solution)/shard_map/ppermute | solution.py:509
  204.5 2.8 %collective-permute-done.31.refs_2_ = bf16[128,512]{1,0:T(8,128)(2,1)S(1)} collective-permute-done((bf16[128,512]{1,0:T(8,128)(2,1)S(1)}, bf16[128,512]{1,0:T(8,128)(2,1)S(1)}, u32[]{:S(2)}, u32[]{:S(2)}) %collective-permute-start.31) | collective-permute-done | bytes 131104 | tf_op jit(solution)/shard_map/ppermute | solution.py:509
  207.4 1.7 collective-permute-start.33
  209.1 0.8 collective-permute-start.34
  209.9 1.1 collective-permute-start.35
  211.0 2.2 collective-permute-done.33.refs_1_
  213.2 0.9 collective-permute-done.34.refs_2_
  214.1 1.7 collective-permute-done.35.refs_3_
  215.9 2.7 %collective-permute-start.22 = (bf16[256,512]{1,0:T(8,128)(2,1)S(1)}, bf16[256,512]{1,0:T(8,128)(2,1)S(1)}, u32[]{:S(2)}, u32[]{:S(2)}) collective-permute-start(bf16[256,512]{1,0:T(8,128)(2,1)S(1)} %get-tuple-element.76), channel_id=1, source_target_pairs={{0,2},{1,3},{2,0},{3,1},{4,6},{5,7},{6,4},{7,5},{8,10},{9,11},{10,... | collective-permute-start | bytes 786440 | tf_op jit(solution)/shard_map/ppermute | solution.py:509
  218.6 0.7 collective-permute-start.23
  219.2 2.8 %collective-permute-start.25 = (bf16[256,512]{1,0:T(8,128)(2,1)S(1)}, bf16[256,512]{1,0:T(8,128)(2,1)S(1)}, u32[]{:S(2)}, u32[]{:S(2)}) collective-permute-start(bf16[256,512]{1,0:T(8,128)(2,1)S(1)} %shard_map.122.refs_4_), channel_id=1, source_target_pairs={{0,4},{1,5},{2,6},{3,7},{4,0},{5,1},{6,2},{7,3},{8,12},{9,13},{10,... | collective-permute-start | bytes 786440 | tf_op jit(solution)/shard_map/ppermute | solution.py:509
  222.3 3.1 %collective-permute-done.22.refs_1_ = bf16[256,512]{1,0:T(8,128)(2,1)S(1)} collective-permute-done((bf16[256,512]{1,0:T(8,128)(2,1)S(1)}, bf16[256,512]{1,0:T(8,128)(2,1)S(1)}, u32[]{:S(2)}, u32[]{:S(2)}) %collective-permute-start.22) | collective-permute-done | bytes 262176 | tf_op jit(solution)/shard_map/ppermute | solution.py:509
  225.5 14.3 %collective-permute-done.25.refs_3_ = bf16[256,512]{1,0:T(8,128)(2,1)S(1)} collective-permute-done((bf16[256,512]{1,0:T(8,128)(2,1)S(1)}, bf16[256,512]{1,0:T(8,128)(2,1)S(1)}, u32[]{:S(2)}, u32[]{:S(2)}) %collective-permute-start.25) | collective-permute-done | bytes 262176 | tf_op jit(solution)/shard_map/ppermute | solution.py:509
  240.1 0.8 pad_maximum_fusion
  240.9 1.5 shard_map.129
  (62 shorter events, 4.9 us)
Async XLA Ops:
  7.2 96.6 %all-gather.2.cloned.1.call-start = ((), (), s32[]{:S(2)}) async-start(), calls=%async_computation | async-start | bytes 4718592 | tf_op jit(solution)/shard_map/all_gather | solution.py:533
  7.9 1.0 copy-start.6
  11.0 1.6 copy-start.4
  12.6 0.7 copy-start.7
  15.8 2.8 %copy-start = (bf16[1,1,48,256,256]{4,3,2,1,0:T(8,128)(2,1)S(1)}, bf16[1,1,48,256,256]{4,3,2,1,0:T(8,128)(2,1)}, u32[]{:S(2)}) copy-start(bf16[1,1,48,256,256]{4,3,2,1,0:T(8,128)(2,1)} %param.10) | copy-start | bytes 18874372
  26.7 2.7 %collective-permute-start = (bf16[4,256,512]{2,1,0:T(8,128)(2,1)S(1)}, bf16[4,256,512]{2,1,0:T(8,128)(2,1)S(1)}, u32[]{:S(2)}, u32[]{:S(2)}) collective-permute-start(bf16[4,256,512]{2,1,0:T(8,128)(2,1)S(1)} %get-tuple-element.51), channel_id=1, source_target_pairs={{0,1},{1,0},{2,3},{3,2},{4,5},{5,4},{6,7},{7,6},{8,9},{9,8},{10,11... | collective-permute-start | bytes 3145736 | tf_op jit(solution)/shard_map/ppermute | solution.py:517
  39.9 22.3 %collective-permute-start.8 = (bf16[4,256,512]{2,1,0:T(8,128)(2,1)S(1)}, bf16[4,256,512]{2,1,0:T(8,128)(2,1)S(1)}, u32[]{:S(2)}, u32[]{:S(2)}) collective-permute-start(bf16[4,256,512]{2,1,0:T(8,128)(2,1)S(1)} %get-tuple-element.58), channel_id=1, source_target_pairs={{0,1},{1,0},{2,3},{3,2},{4,5},{5,4},{6,7},{7,6},{8,9},{9,8},{10,11... | collective-permute-start | bytes 3145736 | tf_op jit(solution)/shard_map/ppermute | solution.py:517
  40.0 16.8 %collective-permute-start.3 = (bf16[256,512]{1,0:T(8,128)(2,1)S(1)}, bf16[256,512]{1,0:T(8,128)(2,1)S(1)}, u32[]{:S(2)}, u32[]{:S(2)}) collective-permute-start(bf16[256,512]{1,0:T(8,128)(2,1)S(1)} %get-tuple-element.54.refs_4_), channel_id=1, source_target_pairs={{0,2},{1,3},{6,4},{7,5},{8,10},{9,11},{14,12},{15,13},{16,18},{17,... | collective-permute-start | bytes 786440 | tf_op jit(solution)/shard_map/ppermute | solution.py:509
  44.5 22.5 %collective-permute-start.2 = (bf16[256,512]{1,0:T(8,128)(2,1)S(1)}, bf16[256,512]{1,0:T(8,128)(2,1)S(1)}, u32[]{:S(2)}, u32[]{:S(2)}) collective-permute-start(bf16[256,512]{1,0:T(8,128)(2,1)S(1)} %get-tuple-element.54.refs_4_), channel_id=1, source_target_pairs={{2,4},{3,5},{4,2},{5,3},{10,12},{11,13},{12,10},{13,11},{18,20},{1... | collective-permute-start | bytes 786440 | tf_op jit(solution)/shard_map/ppermute | solution.py:509
  45.2 21.8 %collective-permute-start.1 = (bf16[256,512]{1,0:T(8,128)(2,1)S(1)}, bf16[256,512]{1,0:T(8,128)(2,1)S(1)}, u32[]{:S(2)}, u32[]{:S(2)}) collective-permute-start(bf16[256,512]{1,0:T(8,128)(2,1)S(1)} %get-tuple-element.53), channel_id=1, source_target_pairs={{0,2},{1,3},{2,0},{3,1},{4,6},{5,7},{6,4},{7,5},{8,10},{9,11},{10,... | collective-permute-start | bytes 786440 | tf_op jit(solution)/shard_map/ppermute | solution.py:509
  56.8 15.8 %collective-permute-start.4 = (bf16[256,512]{1,0:T(8,128)(2,1)S(1)}, bf16[256,512]{1,0:T(8,128)(2,1)S(1)}, u32[]{:S(2)}, u32[]{:S(2)}) collective-permute-start(bf16[256,512]{1,0:T(8,128)(2,1)S(1)} %shard_map.107), channel_id=1, source_target_pairs={{0,4},{1,5},{2,6},{3,7},{4,0},{5,1},{6,2},{7,3},{8,12},{9,13},{10,... | collective-permute-start | bytes 786440 | tf_op jit(solution)/shard_map/ppermute | solution.py:509
  62.4 25.0 %copy-start.3 = (bf16[512,512]{1,0:T(8,128)(2,1)S(1)}, bf16[512,512]{1,0:T(8,128)(2,1)}, u32[]{:S(2)}) copy-start(bf16[512,512]{1,0:T(8,128)(2,1)} %refs_6_.1) | copy-start | bytes 1572868
  62.5 15.4 %collective-permute-start.11 = (bf16[256,512]{1,0:T(8,128)(2,1)S(1)}, bf16[256,512]{1,0:T(8,128)(2,1)S(1)}, u32[]{:S(2)}, u32[]{:S(2)}) collective-permute-start(bf16[256,512]{1,0:T(8,128)(2,1)S(1)} %get-tuple-element.61), channel_id=1, source_target_pairs={{0,2},{1,3},{6,4},{7,5},{8,10},{9,11},{14,12},{15,13},{16,18},{17,... | collective-permute-start | bytes 786440 | tf_op jit(solution)/shard_map/ppermute | solution.py:509
  72.7 10.1 %collective-permute-start.5 = (bf16[256,512]{1,0:T(8,128)(2,1)S(1)}, bf16[256,512]{1,0:T(8,128)(2,1)S(1)}, u32[]{:S(2)}, u32[]{:S(2)}) collective-permute-start(bf16[256,512]{1,0:T(8,128)(2,1)S(1)} %shard_map.108.refs_0_.refs_5_), channel_id=1, source_target_pairs={{0,8},{8,0},{16,24},{24,16},{1,9},{9,1},{17,25},{25,17},{2,10},{10... | collective-permute-start | bytes 786440 | tf_op jit(solution)/shard_map/ppermute | solution.py:520
  74.1 13.4 %collective-permute-start.6 = (bf16[256,512]{1,0:T(8,128)(2,1)S(1)}, bf16[256,512]{1,0:T(8,128)(2,1)S(1)}, u32[]{:S(2)}, u32[]{:S(2)}) collective-permute-start(bf16[256,512]{1,0:T(8,128)(2,1)S(1)} %shard_map.108.refs_0_.refs_5_), channel_id=1, source_target_pairs={{0,16},{8,24},{16,0},{24,8},{1,17},{9,25},{17,1},{25,9},{2,18},{10... | collective-permute-start | bytes 786440 | tf_op jit(solution)/shard_map/ppermute | solution.py:520
  75.6 11.8 %collective-permute-start.7 = (bf16[256,512]{1,0:T(8,128)(2,1)S(1)}, bf16[256,512]{1,0:T(8,128)(2,1)S(1)}, u32[]{:S(2)}, u32[]{:S(2)}) collective-permute-start(bf16[256,512]{1,0:T(8,128)(2,1)S(1)} %shard_map.108.refs_0_.refs_5_), channel_id=1, source_target_pairs={{0,24},{8,16},{16,8},{24,0},{1,25},{9,17},{17,9},{25,1},{2,26},{10... | collective-permute-start | bytes 786440 | tf_op jit(solution)/shard_map/ppermute | solution.py:520
  76.3 13.3 %collective-permute-start.10 = (bf16[256,512]{1,0:T(8,128)(2,1)S(1)}, bf16[256,512]{1,0:T(8,128)(2,1)S(1)}, u32[]{:S(2)}, u32[]{:S(2)}) collective-permute-start(bf16[256,512]{1,0:T(8,128)(2,1)S(1)} %get-tuple-element.61), channel_id=1, source_target_pairs={{2,4},{3,5},{4,2},{5,3},{10,12},{11,13},{12,10},{13,11},{18,20},{1... | collective-permute-start | bytes 786440 | tf_op jit(solution)/shard_map/ppermute | solution.py:509
  77.9 11.7 %collective-permute-start.9 = (bf16[256,512]{1,0:T(8,128)(2,1)S(1)}, bf16[256,512]{1,0:T(8,128)(2,1)S(1)}, u32[]{:S(2)}, u32[]{:S(2)}) collective-permute-start(bf16[256,512]{1,0:T(8,128)(2,1)S(1)} %get-tuple-element.60), channel_id=1, source_target_pairs={{0,2},{1,3},{2,0},{3,1},{4,6},{5,7},{6,4},{7,5},{8,10},{9,11},{10,... | collective-permute-start | bytes 786440 | tf_op jit(solution)/shard_map/ppermute | solution.py:509
  82.9 17.2 %collective-permute-start.12 = (bf16[256,512]{1,0:T(8,128)(2,1)S(1)}, bf16[256,512]{1,0:T(8,128)(2,1)S(1)}, u32[]{:S(2)}, u32[]{:S(2)}) collective-permute-start(bf16[256,512]{1,0:T(8,128)(2,1)S(1)} %shard_map.112), channel_id=1, source_target_pairs={{0,4},{1,5},{2,6},{3,7},{4,0},{5,1},{6,2},{7,3},{8,12},{9,13},{10,... | collective-permute-start | bytes 786440 | tf_op jit(solution)/shard_map/ppermute | solution.py:509
  88.5 13.2 %copy-start.8 = (bf16[4,256,512]{2,1,0:T(8,128)(2,1)}, bf16[4,256,512]{2,1,0:T(8,128)(2,1)S(1)}, u32[]{:S(2)}) copy-start(bf16[4,256,512]{2,1,0:T(8,128)(2,1)S(1)} %get-tuple-element.79.refs_1_) | copy-start | bytes 3145732
  100.2 25.9 %collective-permute-start.13 = (bf16[256,512]{1,0:T(8,128)(2,1)S(1)}, bf16[256,512]{1,0:T(8,128)(2,1)S(1)}, u32[]{:S(2)}, u32[]{:S(2)}) collective-permute-start(bf16[256,512]{1,0:T(8,128)(2,1)S(1)} %shard_map.113.refs_0_), channel_id=1, source_target_pairs={{0,8},{8,0},{16,24},{24,16},{1,9},{9,1},{17,25},{25,17},{2,10},{10... | collective-permute-start | bytes 786440 | tf_op jit(solution)/shard_map/ppermute | solution.py:520
  101.7 24.4 %collective-permute-start.14 = (bf16[256,512]{1,0:T(8,128)(2,1)S(1)}, bf16[256,512]{1,0:T(8,128)(2,1)S(1)}, u32[]{:S(2)}, u32[]{:S(2)}) collective-permute-start(bf16[256,512]{1,0:T(8,128)(2,1)S(1)} %shard_map.113.refs_0_), channel_id=1, source_target_pairs={{0,16},{8,24},{16,0},{24,8},{1,17},{9,25},{17,1},{25,9},{2,18},{10... | collective-permute-start | bytes 786440 | tf_op jit(solution)/shard_map/ppermute | solution.py:520
  103.3 22.8 %collective-permute-start.15 = (bf16[256,512]{1,0:T(8,128)(2,1)S(1)}, bf16[256,512]{1,0:T(8,128)(2,1)}, u32[]{:S(2)}, u32[]{:S(2)}) collective-permute-start(bf16[256,512]{1,0:T(8,128)(2,1)S(1)} %shard_map.113.refs_0_), channel_id=1, source_target_pairs={{0,24},{8,16},{16,8},{24,0},{1,25},{9,17},{17,9},{25,1},{2,26},{10... | collective-permute-start | bytes 786440 | tf_op jit(solution)/shard_map/ppermute | solution.py:520
  103.7 2.8 %copy-start.1 = (bf16[1,1,48,256,256]{4,3,2,1,0:T(8,128)(2,1)S(1)}, bf16[1,1,48,256,256]{4,3,2,1,0:T(8,128)(2,1)}, u32[]{:S(2)}) copy-start(bf16[1,1,48,256,256]{4,3,2,1,0:T(8,128)(2,1)} %param.10) | copy-start | bytes 18874372
  106.5 2.2 copy-start.2
  136.3 2.7 %collective-permute-start.16 = (bf16[4,256,512]{2,1,0:T(8,128)(2,1)S(1)}, bf16[4,256,512]{2,1,0:T(8,128)(2,1)S(1)}, u32[]{:S(2)}, u32[]{:S(2)}) collective-permute-start(bf16[4,256,512]{2,1,0:T(8,128)(2,1)S(1)} %get-tuple-element.68), channel_id=1, source_target_pairs={{0,1},{1,0},{2,3},{3,2},{4,5},{5,4},{6,7},{7,6},{8,9},{9,8},{10,11... | collective-permute-start | bytes 3145736 | tf_op jit(solution)/shard_map/ppermute | solution.py:517
  149.5 3.0 %copy-start.5 = (bf16[512,512]{1,0:T(8,128)(2,1)S(1)}, bf16[512,512]{1,0:T(8,128)(2,1)}, u32[]{:S(2)}) copy-start(bf16[512,512]{1,0:T(8,128)(2,1)} %refs_7_.1) | copy-start | bytes 1572868
  149.5 3.0 %copy-start.9 = (bf16[4,256,512]{2,1,0:T(8,128)(2,1)S(1)}, bf16[4,256,512]{2,1,0:T(8,128)(2,1)}, u32[]{:S(2)}) copy-start(bf16[4,256,512]{2,1,0:T(8,128)(2,1)} %copy-done.8) | copy-start | bytes 3145732
  149.5 2.7 %collective-permute-start.21 = (bf16[4,256,512]{2,1,0:T(8,128)(2,1)S(1)}, bf16[4,256,512]{2,1,0:T(8,128)(2,1)S(1)}, u32[]{:S(2)}, u32[]{:S(2)}) collective-permute-start(bf16[4,256,512]{2,1,0:T(8,128)(2,1)S(1)} %get-tuple-element.74), channel_id=1, source_target_pairs={{0,1},{1,0},{2,3},{3,2},{4,5},{5,4},{6,7},{7,6},{8,9},{9,8},{10,11... | collective-permute-start | bytes 3145736 | tf_op jit(solution)/shard_map/ppermute | solution.py:517
  161.2 8.2 %collective-permute-start.26 = (bf16[512,512]{1,0:T(8,128)(2,1)S(1)}, bf16[512,512]{1,0:T(8,128)(2,1)S(1)}, u32[]{:S(2)}, u32[]{:S(2)}) collective-permute-start(bf16[512,512]{1,0:T(8,128)(2,1)S(1)} %get-tuple-element.82), channel_id=1, source_target_pairs={{0,1},{1,0},{2,3},{3,2},{4,5},{5,4},{6,7},{7,6},{8,9},{9,8},{10,11... | collective-permute-start | bytes 1572872 | tf_op jit(solution)/shard_map/ppermute | solution.py:517
  161.4 8.0 %collective-permute-start.19 = (bf16[256,512]{1,0:T(8,128)(2,1)S(1)}, bf16[256,512]{1,0:T(8,128)(2,1)S(1)}, u32[]{:S(2)}, u32[]{:S(2)}) collective-permute-start(bf16[256,512]{1,0:T(8,128)(2,1)S(1)} %get-tuple-element.71.refs_5_), channel_id=1, source_target_pairs={{0,2},{1,3},{6,4},{7,5},{8,10},{9,11},{14,12},{15,13},{16,18},{17,... | collective-permute-start | bytes 786440 | tf_op jit(solution)/shard_map/ppermute | solution.py:509
  162.7 13.1 %collective-permute-start.24 = (bf16[256,512]{1,0:T(8,128)(2,1)S(1)}, bf16[256,512]{1,0:T(8,128)(2,1)S(1)}, u32[]{:S(2)}, u32[]{:S(2)}) collective-permute-start(bf16[256,512]{1,0:T(8,128)(2,1)S(1)} %get-tuple-element.77.refs_8_), channel_id=1, source_target_pairs={{0,2},{1,3},{6,4},{7,5},{8,10},{9,11},{14,12},{15,13},{16,18},{17,... | collective-permute-start | bytes 786440 | tf_op jit(solution)/shard_map/ppermute | solution.py:509
  169.6 6.9 %collective-permute-start.27 = (bf16[128,512]{1,0:T(8,128)(2,1)S(1)}, bf16[128,512]{1,0:T(8,128)(2,1)S(1)}, u32[]{:S(2)}, u32[]{:S(2)}) collective-permute-start(bf16[128,512]{1,0:T(8,128)(2,1)S(1)} %get-tuple-element.84), channel_id=1, source_target_pairs={{0,8},{8,0},{16,24},{24,16},{1,9},{9,1},{17,25},{25,17},{2,10},{10... | collective-permute-start | bytes 393224 | tf_op jit(solution)/shard_map/ppermute | solution.py:520
  171.8 11.0 %collective-permute-start.17 = (bf16[256,512]{1,0:T(8,128)(2,1)S(1)}, bf16[256,512]{1,0:T(8,128)(2,1)S(1)}, u32[]{:S(2)}, u32[]{:S(2)}) collective-permute-start(bf16[256,512]{1,0:T(8,128)(2,1)S(1)} %get-tuple-element.70), channel_id=1, source_target_pairs={{0,2},{1,3},{2,0},{3,1},{4,6},{5,7},{6,4},{7,5},{8,10},{9,11},{10,... | collective-permute-start | bytes 786440 | tf_op jit(solution)/shard_map/ppermute | solution.py:509
  174.3 6.7 %collective-permute-start.28 = (bf16[128,512]{1,0:T(8,128)(2,1)S(1)}, bf16[128,512]{1,0:T(8,128)(2,1)S(1)}, u32[]{:S(2)}, u32[]{:S(2)}) collective-permute-start(bf16[128,512]{1,0:T(8,128)(2,1)S(1)} %get-tuple-element.85), channel_id=1, source_target_pairs={{0,16},{8,24},{16,0},{24,8},{1,17},{9,25},{17,1},{25,9},{2,18},{10... | collective-permute-start | bytes 393224 | tf_op jit(solution)/shard_map/ppermute | solution.py:520
  174.7 6.3 %collective-permute-start.29 = (bf16[128,512]{1,0:T(8,128)(2,1)S(1)}, bf16[128,512]{1,0:T(8,128)(2,1)S(1)}, u32[]{:S(2)}, u32[]{:S(2)}) collective-permute-start(bf16[128,512]{1,0:T(8,128)(2,1)S(1)} %get-tuple-element.86), channel_id=1, source_target_pairs={{0,24},{8,16},{16,8},{24,0},{1,25},{9,17},{17,9},{25,1},{2,26},{10... | collective-permute-start | bytes 393224 | tf_op jit(solution)/shard_map/ppermute | solution.py:520
  175.8 9.7 %collective-permute-start.18 = (bf16[256,512]{1,0:T(8,128)(2,1)S(1)}, bf16[256,512]{1,0:T(8,128)(2,1)S(1)}, u32[]{:S(2)}, u32[]{:S(2)}) collective-permute-start(bf16[256,512]{1,0:T(8,128)(2,1)S(1)} %get-tuple-element.71.refs_5_), channel_id=1, source_target_pairs={{2,4},{3,5},{4,2},{5,3},{10,12},{11,13},{12,10},{13,11},{18,20},{1... | collective-permute-start | bytes 786440 | tf_op jit(solution)/shard_map/ppermute | solution.py:509
  176.5 28.0 %collective-permute-start.20 = (bf16[256,512]{1,0:T(8,128)(2,1)S(1)}, bf16[256,512]{1,0:T(8,128)(2,1)S(1)}, u32[]{:S(2)}, u32[]{:S(2)}) collective-permute-start(bf16[256,512]{1,0:T(8,128)(2,1)S(1)} %shard_map.118.refs_2_), channel_id=1, source_target_pairs={{0,4},{1,5},{2,6},{3,7},{4,0},{5,1},{6,2},{7,3},{8,12},{9,13},{10,... | collective-permute-start | bytes 786440 | tf_op jit(solution)/shard_map/ppermute | solution.py:509
  181.1 23.4 %collective-permute-start.30 = (bf16[128,512]{1,0:T(8,128)(2,1)S(1)}, bf16[128,512]{1,0:T(8,128)(2,1)S(1)}, u32[]{:S(2)}, u32[]{:S(2)}) collective-permute-start(bf16[128,512]{1,0:T(8,128)(2,1)S(1)} %shard_map.126.refs_0_), channel_id=1, source_target_pairs={{0,2},{1,3},{2,0},{3,1},{4,6},{5,7},{6,4},{7,5},{8,10},{9,11},{10,... | collective-permute-start | bytes 393224 | tf_op jit(solution)/shard_map/ppermute | solution.py:509
  181.4 25.9 %collective-permute-start.31 = (bf16[128,512]{1,0:T(8,128)(2,1)S(1)}, bf16[128,512]{1,0:T(8,128)(2,1)S(1)}, u32[]{:S(2)}, u32[]{:S(2)}) collective-permute-start(bf16[128,512]{1,0:T(8,128)(2,1)S(1)} %shard_map.126.refs_0_), channel_id=1, source_target_pairs={{0,4},{1,5},{2,6},{3,7},{4,0},{5,1},{6,2},{7,3},{8,12},{9,13},{10,... | collective-permute-start | bytes 393224 | tf_op jit(solution)/shard_map/ppermute | solution.py:509
  182.8 24.5 %collective-permute-start.32 = (bf16[128,512]{1,0:T(8,128)(2,1)S(1)}, bf16[128,512]{1,0:T(8,128)(2,1)S(1)}, u32[]{:S(2)}, u32[]{:S(2)}) collective-permute-start(bf16[128,512]{1,0:T(8,128)(2,1)S(1)} %shard_map.126.refs_0_), channel_id=1, source_target_pairs={{0,6},{1,7},{2,4},{3,5},{4,2},{5,3},{6,0},{7,1},{8,14},{9,15},{10,... | collective-permute-start | bytes 393224 | tf_op jit(solution)/shard_map/ppermute | solution.py:509
  207.4 5.8 %collective-permute-start.33 = (bf16[128,512]{1,0:T(8,128)(2,1)S(1)}, bf16[128,512]{1,0:T(8,128)(2,1)S(1)}, u32[]{:S(2)}, u32[]{:S(2)}) collective-permute-start(bf16[128,512]{1,0:T(8,128)(2,1)S(1)} %shard_map.127.refs_0_), channel_id=1, source_target_pairs={{0,8},{8,0},{16,24},{24,16},{1,9},{9,1},{17,25},{25,17},{2,10},{10... | collective-permute-start | bytes 393224 | tf_op jit(solution)/shard_map/ppermute | solution.py:520
  209.1 5.0 %collective-permute-start.34 = (bf16[128,512]{1,0:T(8,128)(2,1)S(1)}, bf16[128,512]{1,0:T(8,128)(2,1)S(1)}, u32[]{:S(2)}, u32[]{:S(2)}) collective-permute-start(bf16[128,512]{1,0:T(8,128)(2,1)S(1)} %shard_map.127.refs_0_), channel_id=1, source_target_pairs={{0,16},{8,24},{16,0},{24,8},{1,17},{9,25},{17,1},{25,9},{2,18},{10... | collective-permute-start | bytes 393224 | tf_op jit(solution)/shard_map/ppermute | solution.py:520
  209.9 5.9 %collective-permute-start.35 = (bf16[128,512]{1,0:T(8,128)(2,1)S(1)}, bf16[128,512]{1,0:T(8,128)(2,1)S(1)}, u32[]{:S(2)}, u32[]{:S(2)}) collective-permute-start(bf16[128,512]{1,0:T(8,128)(2,1)S(1)} %shard_map.127.refs_0_), channel_id=1, source_target_pairs={{0,24},{8,16},{16,8},{24,0},{1,25},{9,17},{17,9},{25,1},{2,26},{10... | collective-permute-start | bytes 393224 | tf_op jit(solution)/shard_map/ppermute | solution.py:520
  215.8 25.1 %collective-permute-start.36 = (bf16[512,512]{1,0:T(8,128)(2,1)S(1)}, bf16[512,512]{1,0:T(8,128)(2,1)S(1)}, u32[]{:S(2)}, u32[]{:S(2)}) collective-permute-start(bf16[512,512]{1,0:T(8,128)(2,1)S(1)} %shard_map.128.refs_0_), channel_id=1, source_target_pairs={{0,1},{1,0},{2,3},{3,2},{4,5},{5,4},{6,7},{7,6},{8,9},{9,8},{10,11... | collective-permute-start | bytes 1572872 | tf_op jit(solution)/shard_map/ppermute | solution.py:517
  215.9 9.6 %collective-permute-start.22 = (bf16[256,512]{1,0:T(8,128)(2,1)S(1)}, bf16[256,512]{1,0:T(8,128)(2,1)S(1)}, u32[]{:S(2)}, u32[]{:S(2)}) collective-permute-start(bf16[256,512]{1,0:T(8,128)(2,1)S(1)} %get-tuple-element.76), channel_id=1, source_target_pairs={{0,2},{1,3},{2,0},{3,1},{4,6},{5,7},{6,4},{7,5},{8,10},{9,11},{10,... | collective-permute-start | bytes 786440 | tf_op jit(solution)/shard_map/ppermute | solution.py:509
  218.6 6.9 %collective-permute-start.23 = (bf16[256,512]{1,0:T(8,128)(2,1)S(1)}, bf16[256,512]{1,0:T(8,128)(2,1)S(1)}, u32[]{:S(2)}, u32[]{:S(2)}) collective-permute-start(bf16[256,512]{1,0:T(8,128)(2,1)S(1)} %get-tuple-element.77.refs_8_), channel_id=1, source_target_pairs={{2,4},{3,5},{4,2},{5,3},{10,12},{11,13},{12,10},{13,11},{18,20},{1... | collective-permute-start | bytes 786440 | tf_op jit(solution)/shard_map/ppermute | solution.py:509
  219.2 20.5 %collective-permute-start.25 = (bf16[256,512]{1,0:T(8,128)(2,1)S(1)}, bf16[256,512]{1,0:T(8,128)(2,1)S(1)}, u32[]{:S(2)}, u32[]{:S(2)}) collective-permute-start(bf16[256,512]{1,0:T(8,128)(2,1)S(1)} %shard_map.122.refs_4_), channel_id=1, source_target_pairs={{0,4},{1,5},{2,6},{3,7},{4,0},{5,1},{6,2},{7,3},{8,12},{9,13},{10,... | collective-permute-start | bytes 786440 | tf_op jit(solution)/shard_map/ppermute | solution.py:509
Sparse Core Ops, SparseCore 0:
  10.4 55.6 all-gather.1

commit v4 on v3

--- a/solution.py
+++ b/solution.py
@@ -120,20 +120,6 @@
     )
 
 
-def tile_copy(tiles_ref, held, sems, s):
-    return pltpu.make_async_copy(tiles_ref.at[s], held.at[s], sems.at[s])
-
-
-def each_tile(g, number_ref, list_ref, action):
-    cap = list_ref.shape[0] // number_ref.shape[0]
-
-    def one(j, _):
-        action(lax.shift_right_logical(list_ref[g * cap + j], 10))
-        return 0
-
-    lax.fori_loop(0, number_ref[g], one, 0)
-
-
 def sum_group(g, number_ref, list_ref, total, product, store):
     cap = list_ref.shape[0] // number_ref.shape[0]
     n = number_ref[g]
@@ -142,27 +128,33 @@
         entries = [list_ref[g * cap + start + j] for j in range(width)]
         return product([(lax.shift_right_logical(x, 10), x & 1023) for x in entries])
 
+    def exact(width):
+        @pl.when(n == width)
+        def _():
+            store(take(0, width))
+
     @pl.when(n == 0)
     def _():
         store(jnp.zeros_like(total))
 
-    @pl.when(jnp.logical_and(n >= 1, n <= 2))
-    def _():
-        store(take(0, 2))
-
-    @pl.when(jnp.logical_and(n >= 3, n <= 4))
-    def _():
-        store(take(0, 4))
+    for width in range(1, 5):
+        exact(width)
 
     @pl.when(n > 4)
     def _():
         total[...] = jnp.zeros_like(total)
-
-        def more(m, _):
+        fours = lax.shift_right_logical(n, 2)
+
+        def four(m, _):
             total[...] += take(4 * m, 4)
             return 0
 
-        lax.fori_loop(0, lax.shift_right_logical(n + 3, 2), more, 0)
+        def one(m, _):
+            total[...] += take(m, 1)
+            return 0
+
+        lax.fori_loop(0, fours, four, 0)
+        lax.fori_loop(4 * fours, n, one, 0)
         store(total[...])
 
 
@@ -172,111 +164,54 @@
     )
 
 
-def forward_body(first, half, n_in, *refs):
-    number_ref, list_ref, tiles_ref = refs[:3]
-    inputs = refs[3 : 3 + n_in]
-    give, keep, held, source, total, sems, source_sems = refs[3 + n_in :]
+def forward_body(first, half, number_ref, list_ref, tiles, source, give, keep, total):
     col, row = lax.axis_index("col"), lax.axis_index("row")
-    parts = give.shape[0]
-    per = source.shape[0] // n_in
-    copies = [
-        pltpu.make_async_copy(x, source.at[pl.ds(i * per, per)], source_sems.at[i])
-        for i, x in enumerate(inputs)
-    ]
-    for copy in copies:
-        copy.start()
-
-    def block_row(i):
-        flip = jnp.where(i < parts, 1, 0)
-        return (col ^ (2 * lax.rem(i, parts) + flip)) * 2 + half
-
-    def start(i, _):
-        each_tile(
-            block_row(i),
-            number_ref,
-            list_ref,
-            lambda s: tile_copy(tiles_ref, held, sems, s).start(),
-        )
-        return 0
-
-    lax.fori_loop(0, 2 * parts, start, 0)
-    held[held.shape[0] - 1] = jnp.zeros(held.shape[1:], BF16)
-    for copy in copies:
-        copy.wait()
+    per = source.shape[0] // 2
 
     def product(pieces):
         def locate(v):
             return v if first else (v & 1) * per + (lax.shift_right_logical(v, 1) ^ row)
 
-        return joined_dot([held[s] for s, _ in pieces], [source[locate(v)] for _, v in pieces])
-
-    for base, out in ((0, give), (parts, keep)):
+        return joined_dot([tiles[s] for s, _ in pieces], [source[locate(v)] for _, v in pieces])
+
+    for flip, out in ((1, give), (0, keep)):
 
         def block(i, _):
             def store(value):
                 out[i] = value.astype(BF16)
 
-            g = block_row(base + i)
-            each_tile(
-                g, number_ref, list_ref, lambda s: tile_copy(tiles_ref, held, sems, s).wait()
-            )
+            g = (col ^ (2 * i + flip)) * 2 + half
             sum_group(g, number_ref, list_ref, total, product, store)
             return 0
 
-        lax.fori_loop(0, parts, block, 0)
-
-
-def forward(number, entries, tiles, sources, first, half, after):
+        lax.fori_loop(0, out.shape[0], block, 0)
+
+
+def forward(number, entries, tiles, source, first, half, after):
     slots_n, edge, _ = tiles.shape
-    width = sources[0].shape[-1]
-    blocks = sum(x.shape[0] for x in sources)
-    return run(
-        functools.partial(forward_body, first, half, len(sources)),
-        (number, entries, tiles, *sources),
-        [SMEM, SMEM, ANY] + [ANY] * len(sources),
+    width = source.shape[-1]
+    return run(
+        functools.partial(forward_body, first, half),
+        (number, entries, tiles, source),
+        [SMEM, SMEM, VMEM, VMEM],
         [shape((number.shape[0] // 4, edge, width))] * 2,
-        [
-            pltpu.VMEM((slots_n + 1, edge, edge), BF16),
-            pltpu.VMEM((blocks, edge, width), BF16),
-            pltpu.VMEM((edge, width), F32),
-            pltpu.SemaphoreType.DMA((slots_n,)),
-            pltpu.SemaphoreType.DMA((len(sources),)),
-        ],
+        [pltpu.VMEM((edge, width), F32)],
         flops=slots_n * edge * edge * width,
-        mib=20,
+        mib=16,
         after=after,
     )
 
 
-def backward_body(number_ref, list_ref, tiles_ref, ranged, out, *refs):
-    held, source, total, sems, source_sem = refs
+def backward_body(number_ref, list_ref, tiles, ranged, out, total):
     mask = lax.axis_index("row") * 2
-    copy = pltpu.make_async_copy(ranged, source, source_sem)
-    copy.start()
-
-    def start(i, _):
-        each_tile(
-            i ^ mask,
-            number_ref,
-            list_ref,
-            lambda s: tile_copy(tiles_ref, held, sems, s).start(),
-        )
-        return 0
-
-    lax.fori_loop(0, out.shape[0], start, 0)
-    held[held.shape[0] - 1] = jnp.zeros(held.shape[1:], BF16)
-    copy.wait()
 
     def product(pieces):
-        return joined_dot([source[u] for _, u in pieces], [held[s] for s, _ in pieces])
+        return joined_dot([ranged[u] for _, u in pieces], [tiles[s] for s, _ in pieces])
 
     def block(i, _):
         def store(value):
             out[i] = value.astype(BF16)
 
-        each_tile(
-            i ^ mask, number_ref, list_ref, lambda s: tile_copy(tiles_ref, held, sems, s).wait()
-        )
         sum_group(i ^ mask, number_ref, list_ref, total, product, store)
         return 0
 
@@ -289,17 +224,11 @@
     return run(
         backward_body,
         (number, entries, tiles, ranged),
-        [SMEM, SMEM, ANY, ANY],
+        [SMEM, SMEM, VMEM, VMEM],
         [shape((number.shape[0], width, edge))],
-        [
-            pltpu.VMEM((slots_n + 1, edge, edge), BF16),
-            pltpu.VMEM(ranged.shape, BF16),
-            pltpu.VMEM((width, edge), F32),
-            pltpu.SemaphoreType.DMA((slots_n,)),
-            pltpu.SemaphoreType.DMA,
-        ],
+        [pltpu.VMEM((width, edge), F32)],
         flops=2 * slots_n * edge * edge * width,
-        mib=20,
+        mib=18,
     )[0]
 
 
@@ -345,26 +274,29 @@
 
 
 def first_body(n, half, *refs):
-    scale, weight, agg, out = refs[n:]
+    scale, weight, agg, out = refs[n], refs[n + 1], refs[-2], refs[-1]
     row = lax.axis_index("row")
+    if half:
+        agg[: half * n] = refs[n + 2][...]
+        out[: half * n] = refs[n + 3][...]
     for j in range(n):
         value = jnp.dot(refs[j][...], weight[...], preferred_element_type=F32)
         wide = repeat_lanes(scale[(row ^ j) * 2 + half], value.shape[1])
-        out[j] = (jax.nn.gelu(value) * wide).astype(BF16)
-        agg[j] = refs[j][...]
-
-
-def first_layer(aggs, scale, weight, half, after):
+        out[half * n + j] = (jax.nn.gelu(value) * wide).astype(BF16)
+        agg[half * n + j] = refs[j][...]
+
+
+def first_layer(aggs, scale, weight, half, before, after):
     n = len(aggs)
-    dims = (n, *aggs[0].shape)
+    dims = ((half + 1) * n, *aggs[0].shape)
     return run(
         functools.partial(first_body, n, half),
-        (*aggs, scale, weight),
-        [VMEM] * (n + 2),
+        (*aggs, scale, weight, *before),
+        [VMEM] * (n + 2 + len(before)),
         [shape(dims)] * 2,
         flops=2 * n * dims[1] * weight.size,
         trans=n * aggs[0].size,
-        mib=12,
+        mib=14,
         after=after,
     )
 
@@ -389,17 +321,16 @@
     )[0]
 
 
-def grad_body(hidden_ref, *refs):
-    aggs, outs = refs[:2], refs[2:4]
-    scale, w_first, w_second, give, keep, first, second = refs[4:]
+def grad_body(hidden_ref, aggs, outs, scale, w_first, w_second, give, keep, first, second):
     row = lax.axis_index("row")
     core = lax.rem(lax.axis_index("col"), 2)
+    n = aggs.shape[0] // 2
     first[...] = jnp.zeros_like(first)
     second[...] = jnp.zeros_like(second)
     for e in range(2):
 
         def block(j, _):
-            hidden, agg = hidden_ref[2 * j + e], aggs[e][j]
+            hidden, agg = hidden_ref[2 * j + e], aggs[e * n + j]
             pre = jnp.dot(agg, w_first[...], preferred_element_type=F32)
             grad_hidden = lax.dot_general(
                 hidden, w_second[...], (((0,), (1,)), ((), ())), preferred_element_type=F32
@@ -411,11 +342,11 @@
                 agg, grad_pre, (((0,), (0,)), ((), ())), preferred_element_type=F32
             )
             second[...] += lax.dot_general(
-                outs[e][j], hidden, (((0,), (1,)), ((), ())), preferred_element_type=F32
+                outs[e * n + j], hidden, (((0,), (1,)), ((), ())), preferred_element_type=F32
             )
             return 0
 
-        lax.fori_loop(0, aggs[e].shape[0], block, 0)
+        lax.fori_loop(0, n, block, 0)
     keep[...] = jnp.where(core == 0, first[...], second[...]).astype(BF16)
     give[...] = jnp.where(core == 0, second[...], first[...]).astype(BF16)
 
@@ -423,13 +354,13 @@
 def weight_grads(hidden, aggs, outs, scale, w_first, w_second, after):
     return run(
         grad_body,
-        (hidden, *aggs, *outs, scale, w_first, w_second),
-        [VMEM] * 8,
+        (hidden, aggs, outs, scale, w_first, w_second),
+        [VMEM] * 6,
         [shape(w_first.shape)] * 2,
         [pltpu.VMEM(w_first.shape, F32)] * 2,
         flops=8 * hidden.size * w_first.shape[0],
         trans=hidden.size,
-        mib=28,
+        mib=24,
         after=after,
     )
 
@@ -536,10 +467,9 @@
         count, slots, values, scale, 2 * n_col
     )
 
-    aggs, outs = [], []
-    partials, after = [], ()
+    partials, after, stacked = [], (), ()
     for half in range(halves):
-        give, keep = forward(number, entries, tiles, (first_in,), True, half, after)
+        give, keep = forward(number, entries, tiles, first_in, True, half, after)
         own = pair_sum(keep, core_flip(give))
         after = (own[-1],)
         partials.append(own)
@@ -548,9 +478,10 @@
         after = (agg,) if half else ()
         agg = aggregate(scatter_line(partials[half])[0], scale, half, after)
         spread = [agg] + [row_flip(agg, j) for j in range(1, n_row)]
-        stacked, out = first_layer(spread, scale, w_first, half, (hidden,) if half else ())
-        aggs.append(stacked)
-        outs.append(out)
+        stacked = first_layer(
+            spread, scale, w_first, half, stacked, (hidden,) if half else ()
+        )
+    aggs, outs = stacked
 
     partials, after = [], ()
     for half in range(halves):

time: 251 us -> 226 us (0.900)
  Pallas kernels: 73.7 us -> 38 us
  waiting for transfers between devices: 87.6 us -> 102 us
  starting transfers between devices: 60.3 us -> 57.2 us
    pallas_call x27, Pallas kernels: 73.7 us -> 38 us  [run(): pl.pallas_call(whole, out_shape=outs, in_specs=specs + [ANY] * extra, out...]
    ppermute x19, waiting for transfers between devices: 72.9 us -> 81.2 us  [col_send(): lax.ppermute(value, 'col', [(2 * a + k, 2 * b + k) for a, b in pairs for...]
    ppermute x12, waiting for transfers between devices: 6.8 us -> 13.2 us  [row_flip(): return lax.ppermute(value, 'row', [(a, a ^ j) for a in range(n_row)])]
    ppermute x19, starting transfers between devices: 45.3 us -> 39.8 us  [col_send(): lax.ppermute(value, 'col', [(2 * a + k, 2 * b + k) for a, b in pairs for...]
    unnamed x21 -> x31, local copies, waits for them, and re-layouts: 11.8 us -> 11.8 us
  transfers between devices with their start and end apart: 38 -> 38, of which waited for: 18 -> 18; matrix products, arithmetic and copies ran while one was open for 0% -> 0% of each run, Pallas kernels for 17% -> 8%
where the time goes in v4:
time: 226 us; the launch traced here: 225 us
  waiting for transfers between devices  102 us (45%)
  starting transfers between devices  57.2 us (25%)
  Pallas kernels  38 us (17%)
  between operations  15.1 us (7%)
  local copies, waits for them, and re-layouts  11.8 us (5%)
    ppermute x19, waiting for transfers between devices, col_send(): lax.ppermute(value, 'col', [(2 * a + k, 2 * b + k) for a, b in pairs for...  81.2 us
    ppermute x19, starting transfers between devices, col_send(): lax.ppermute(value, 'col', [(2 * a + k, 2 * b + k) for a, b in pairs for...  39.8 us
    pallas_call x27, Pallas kernels, run(): pl.pallas_call(whole, out_shape=outs, in_specs=specs + [ANY] * extra, out...  38 us
    ppermute x12, starting transfers between devices, row_flip(): return lax.ppermute(value, 'row', [(a, a ^ j) for a in range(n_row)])  15.5 us
    ppermute x12, waiting for transfers between devices, row_flip(): return lax.ppermute(value, 'row', [(a, a ^ j) for a in range(n_row)])  13.2 us
    unnamed x31, local copies, waits for them, and re-layouts  11.8 us
    ppermute x6, waiting for transfers between devices, core_flip(): return lax.ppermute(value, 'col', [(a, a ^ 1) for a in range(n_col)])  7.59 us
  transfers between devices with their start and end apart: 38, of which 18 were waited for; matrix products, arithmetic and copies ran while one was open for 0% of the time, Pallas kernels for 8%

profile of v4, /device:TPU:0, one launch (start us, length us, event | category | flops | bytes accessed | tf_op | source)
XLA Modules:
  0.0 224.9 jit_solution(6777270356165408281)
XLA Ops:
  7.2 0.7 copy.13
  7.9 1.0 copy-done.11
  9.0 1.3 shard_map.103
  11.0 1.6 copy-done.3
  12.6 0.7 copy-done.12
  13.2 2.4 %shard_map.104 = (bf16[8,256,512]{2,1,0:T(8,128)(2,1)S(1)}, s32[16]{0:T(128)S(1)}, s32[128]{0:T(128)S(1)}, s32[8]{0:T(128)S(1)}, s32[128]{0:T(128)S(1)}) custom-call(s32[1]{0:T(128)} %bitcast.7.refs_0_, s32[48]{0:T(128)S(1)} %bitcast.17, bf16[8,256,512]{2,1,0:T(8,128)(2,1)S(1)} %bitcast.15, f32[8,256,128]{2,1,0:T(8,128)S(1)} %get-tuple-element.46.refs_3_.refs_4_), custom_call_target="tpu_custom_call" | custom-call | flops 1048576 | bytes 5244196 | tf_op jit(solution)/shard_map/pallas_call | solution.py:28
  15.6 2.8 %copy-done = bf16[1,1,48,256,256]{4,3,2,1,0:T(8,128)(2,1)S(1)} copy-done((bf16[1,1,48,256,256]{4,3,2,1,0:T(8,128)(2,1)S(1)}, bf16[1,1,48,256,256]{4,3,2,1,0:T(8,128)(2,1)}, u32[]{:S(2)}) %copy-start) | copy-done | bytes 6291480
  18.4 2.9 %shard_map.105 = (bf16[4,256,512]{2,1,0:T(8,128)(2,1)S(1)}, bf16[4,256,512]{2,1,0:T(8,128)(2,1)S(1)}) custom-call(s32[16]{0:T(128)S(1)} %get-tuple-element.47.refs_0_, s32[128]{0:T(128)S(1)} %get-tuple-element.48.refs_1_, bf16[48,256,256]{2,1,0:T(8,128)(2,1)S(1)} %bitcast.8, bf16[8,256,512]{2,1,0:T(8,128)(2,1)S(1)} %get-tuple-element.49.refs_3_), custom_call_target="tpu_custom_call" | custom-call | flops 1610612736 | bytes 10486336 | tf_op jit(solution)/shard_map/pallas_call | solution.py:28
  21.3 1.4 collective-permute-start
  22.7 2.3 %collective-permute-done.refs_1_ = bf16[4,256,512]{2,1,0:T(8,128)(2,1)S(1)} collective-permute-done((bf16[4,256,512]{2,1,0:T(8,128)(2,1)S(1)}, bf16[4,256,512]{2,1,0:T(8,128)(2,1)S(1)}, u32[]{:S(2)}, u32[]{:S(2)}) %collective-permute-start) | collective-permute-done | bytes 1048608 | tf_op jit(solution)/shard_map/ppermute | solution.py:448
  25.2 3.5 %shard_map.107 = (bf16[4,256,512]{2,1,0:T(8,128)(2,1)S(1)}, bf16[4,256,512]{2,1,0:T(8,128)(2,1)S(1)}) custom-call(s32[16]{0:T(128)S(1)} %get-tuple-element.47.refs_0_, s32[128]{0:T(128)S(1)} %get-tuple-element.48.refs_1_, bf16[48,256,256]{2,1,0:T(8,128)(2,1)S(1)} %bitcast.9, bf16[8,256,512]{2,1,0:T(8,128)(2,1)S(1)} %get-tuple-element.49.refs_3_, ...), custom_call_target="tpu_custom_call" | custom-call | flops 1610612736 | bytes 10486336 | tf_op jit(solution)/shard_map/pallas_call | solution.py:28
  28.8 5.0 %collective-permute-start.8 = (bf16[256,512]{1,0:T(8,128)(2,1)S(1)}, bf16[256,512]{1,0:T(8,128)(2,1)S(1)}, u32[]{:S(2)}, u32[]{:S(2)}) collective-permute-start(bf16[256,512]{1,0:T(8,128)(2,1)S(1)} %get-tuple-element.52.refs_4_), channel_id=1, source_target_pairs={{0,2},{1,3},{6,4},{7,5},{8,10},{9,11},{14,12},{15,13},{16,18},{17,... | collective-permute-start | bytes 786440 | tf_op jit(solution)/shard_map/ppermute | solution.py:440
  33.8 0.7 collective-permute-start.7
  34.5 3.0 %collective-permute-start.6 = (bf16[256,512]{1,0:T(8,128)(2,1)S(1)}, bf16[256,512]{1,0:T(8,128)(2,1)S(1)}, u32[]{:S(2)}, u32[]{:S(2)}) collective-permute-start(bf16[256,512]{1,0:T(8,128)(2,1)S(1)} %get-tuple-element.60), channel_id=1, source_target_pairs={{0,2},{1,3},{2,0},{3,1},{4,6},{5,7},{6,4},{7,5},{8,10},{9,11},{10,... | collective-permute-start | bytes 786440 | tf_op jit(solution)/shard_map/ppermute | solution.py:440
  37.5 8.5 %collective-permute-done.8.refs_1_ = bf16[256,512]{1,0:T(8,128)(2,1)S(1)} collective-permute-done((bf16[256,512]{1,0:T(8,128)(2,1)S(1)}, bf16[256,512]{1,0:T(8,128)(2,1)S(1)}, u32[]{:S(2)}, u32[]{:S(2)}) %collective-permute-start.8) | collective-permute-done | bytes 262176 | tf_op jit(solution)/shard_map/ppermute | solution.py:440
  46.1 4.3 %collective-permute-start.9 = (bf16[256,512]{1,0:T(8,128)(2,1)S(1)}, bf16[256,512]{1,0:T(8,128)(2,1)S(1)}, u32[]{:S(2)}, u32[]{:S(2)}) collective-permute-start(bf16[256,512]{1,0:T(8,128)(2,1)S(1)} %shard_map.110), channel_id=1, source_target_pairs={{0,4},{1,5},{2,6},{3,7},{4,0},{5,1},{6,2},{7,3},{8,12},{9,13},{10,... | collective-permute-start | bytes 786440 | tf_op jit(solution)/shard_map/ppermute | solution.py:440
  50.7 1.6 collective-permute-start.4
  52.3 8.8 %collective-permute-done.6.refs_1_ = bf16[256,512]{1,0:T(8,128)(2,1)S(1)} collective-permute-done((bf16[256,512]{1,0:T(8,128)(2,1)S(1)}, bf16[256,512]{1,0:T(8,128)(2,1)S(1)}, u32[]{:S(2)}, u32[]{:S(2)}) %collective-permute-start.6) | collective-permute-done | bytes 262176 | tf_op jit(solution)/shard_map/ppermute | solution.py:440
  61.2 12.8 %collective-permute-done.9.refs_3_ = bf16[256,512]{1,0:T(8,128)(2,1)S(1)} collective-permute-done((bf16[256,512]{1,0:T(8,128)(2,1)S(1)}, bf16[256,512]{1,0:T(8,128)(2,1)S(1)}, u32[]{:S(2)}, u32[]{:S(2)}) %collective-permute-start.9) | collective-permute-done | bytes 262176 | tf_op jit(solution)/shard_map/ppermute | solution.py:440
  74.1 1.6 collective-permute-start.13
  75.7 1.4 collective-permute-start.14
  77.7 0.8 collective-permute-start.3
  78.5 1.7 collective-permute-start.2
  80.3 3.0 %collective-permute-done.13.refs_1_ = bf16[256,512]{1,0:T(8,128)(2,1)S(1)} collective-permute-done((bf16[256,512]{1,0:T(8,128)(2,1)S(1)}, bf16[256,512]{1,0:T(8,128)(2,1)S(1)}, u32[]{:S(2)}, u32[]{:S(2)}) %collective-permute-start.13) | collective-permute-done | bytes 262176 | tf_op jit(solution)/shard_map/ppermute | solution.py:451
  83.4 5.9 %collective-permute-done.14.refs_2_ = bf16[256,512]{1,0:T(8,128)(2,1)S(1)} collective-permute-done((bf16[256,512]{1,0:T(8,128)(2,1)S(1)}, bf16[256,512]{1,0:T(8,128)(2,1)S(1)}, u32[]{:S(2)}, u32[]{:S(2)}) %collective-permute-start.14) | collective-permute-done | bytes 262176 | tf_op jit(solution)/shard_map/ppermute | solution.py:451
  89.3 1.0 shard_map.113
  90.4 0.8 collective-permute-done.2.refs_1_
  91.2 5.3 %collective-permute-done.5.refs_3_ = bf16[256,512]{1,0:T(8,128)(2,1)S(1)} collective-permute-done((bf16[256,512]{1,0:T(8,128)(2,1)S(1)}, bf16[256,512]{1,0:T(8,128)(2,1)S(1)}, u32[]{:S(2)}, u32[]{:S(2)}) %collective-permute-start.5) | collective-permute-done | bytes 262176 | tf_op jit(solution)/shard_map/ppermute | solution.py:440
  96.6 1.5 collective-permute-start.10
  98.1 1.4 collective-permute-start.11
  100.2 2.8 %copy-done.1 = bf16[1,1,48,256,256]{4,3,2,1,0:T(8,128)(2,1)S(1)} copy-done((bf16[1,1,48,256,256]{4,3,2,1,0:T(8,128)(2,1)S(1)}, bf16[1,1,48,256,256]{4,3,2,1,0:T(8,128)(2,1)}, u32[]{:S(2)}) %copy-start.1) | copy-done | bytes 6291480
  103.0 2.2 copy-done.2
  105.2 5.4 %shard_map.114.refs_8_.refs_0_ = bf16[8,512,256]{2,1,0:T(8,128)(2,1)S(1)} custom-call(s32[8]{0:T(128)S(1)} %get-tuple-element.64.refs_0_, s32[128]{0:T(128)S(1)} %get-tuple-element.65.refs_1_, bf16[48,256,256]{2,1,0:T(8,128)(2,1)S(1)} %bitcast.10, bf16[16,512,256]{2,1,0:T(8,128)(2,1)S(1)} %copy-done.2), custom_call_target="tpu_custom_call" | custom-call | flops 3221225472 | bytes 12583456 | tf_op jit(solution)/shard_map/pallas_call | solution.py:28
  110.7 2.3 %shard_map.115 = (bf16[8,256,512]{2,1,0:T(8,128)(2,1)S(1)}, bf16[8,256,512]{2,1,0:T(8,128)(2,1)S(1)}) custom-call(bf16[256,512]{1,0:T(8,128)(2,1)S(1)} %shard_map.112.refs_0_, bf16[256,512]{1,0:T(8,128)(2,1)} %collective-permute-done.10.refs_1_, bf16[256,512]{1,0:T(8,128)(2,1)} %collective-permute-done.11.refs_2_, ...), custom_call_target="tpu_custom_call" | custom-call | flops 536870912 | bytes 8912896 | tf_op jit(solution)/shard_map/pallas_call | solution.py:28
  113.0 2.9 %shard_map.116 = (bf16[4,256,512]{2,1,0:T(8,128)(2,1)S(1)}, bf16[4,256,512]{2,1,0:T(8,128)(2,1)S(1)}) custom-call(s32[16]{0:T(128)S(1)} %get-tuple-element.47.refs_0_, s32[128]{0:T(128)S(1)} %get-tuple-element.48.refs_1_, bf16[48,256,256]{2,1,0:T(8,128)(2,1)S(1)} %bitcast.13, bf16[8,256,512]{2,1,0:T(8,128)(2,1)S(1)} %get-tuple-element.67.refs_3_.refs_2_), custom_call_target="tpu_custom_call" | custom-call | flops 1610612736 | bytes 10486336 | tf_op jit(solution)/shard_map/pallas_call | solution.py:28
  116.0 2.6 %collective-permute-done.16.refs_1_ = bf16[4,256,512]{2,1,0:T(8,128)(2,1)S(1)} collective-permute-done((bf16[4,256,512]{2,1,0:T(8,128)(2,1)S(1)}, bf16[4,256,512]{2,1,0:T(8,128)(2,1)S(1)}, u32[]{:S(2)}, u32[]{:S(2)}) %collective-permute-start.16) | collective-permute-done | bytes 1048608 | tf_op jit(solution)/shard_map/ppermute | solution.py:448
  118.9 3.5 %shard_map.120 = (bf16[4,256,512]{2,1,0:T(8,128)(2,1)S(1)}, bf16[4,256,512]{2,1,0:T(8,128)(2,1)S(1)}) custom-call(s32[16]{0:T(128)S(1)} %get-tuple-element.47.refs_0_, s32[128]{0:T(128)S(1)} %get-tuple-element.48.refs_1_, bf16[48,256,256]{2,1,0:T(8,128)(2,1)S(1)} %bitcast.14, bf16[8,256,512]{2,1,0:T(8,128)(2,1)S(1)} %get-tuple-element.67.refs_3_.refs_2_, ...), custom_call_target="tpu_custom_call" | custom-call | flops 1610612736 | bytes 10486336 | tf_op jit(solution)/shard_map/pallas_call | solution.py:28
  122.5 2.6 %collective-permute-done.21.refs_1_ = bf16[4,256,512]{2,1,0:T(8,128)(2,1)S(1)} collective-permute-done((bf16[4,256,512]{2,1,0:T(8,128)(2,1)S(1)}, bf16[4,256,512]{2,1,0:T(8,128)(2,1)S(1)}, u32[]{:S(2)}, u32[]{:S(2)}) %collective-permute-start.21) | collective-permute-done | bytes 1048608 | tf_op jit(solution)/shard_map/ppermute | solution.py:448
  125.4 8.7 %shard_map.124 = (bf16[512,512]{1,0:T(8,128)(2,1)S(1)}, bf16[512,512]{1,0:T(8,128)(2,1)S(1)}) custom-call(bf16[8,512,256]{2,1,0:T(8,128)(2,1)S(1)} %shard_map.114.refs_8_.refs_0_, bf16[8,256,512]{2,1,0:T(8,128)(2,1)S(1)} %get-tuple-element.80.refs_1_, bf16[8,256,512]{2,1,0:T(8,128)(2,1)S(1)} %get-tuple-element.67.refs_3_.refs_2_, ...), custom_call_target="tpu_custom_call" | custom-call | flops 4294967296 | bytes 9437184 | tf_op jit(solution)/shard_map/pallas_call | solution.py:28
  134.3 2.7 %collective-permute-start.19 = (bf16[256,512]{1,0:T(8,128)(2,1)S(1)}, bf16[256,512]{1,0:T(8,128)(2,1)S(1)}, u32[]{:S(2)}, u32[]{:S(2)}) collective-permute-start(bf16[256,512]{1,0:T(8,128)(2,1)S(1)} %get-tuple-element.72.refs_4_), channel_id=1, source_target_pairs={{0,2},{1,3},{6,4},{7,5},{8,10},{9,11},{14,12},{15,13},{16,18},{17,... | collective-permute-start | bytes 786440 | tf_op jit(solution)/shard_map/ppermute | solution.py:440
  137.0 1.5 collective-permute-start.24
  138.6 5.1 %collective-permute-done.19.refs_1_ = bf16[256,512]{1,0:T(8,128)(2,1)S(1)} collective-permute-done((bf16[256,512]{1,0:T(8,128)(2,1)S(1)}, bf16[256,512]{1,0:T(8,128)(2,1)S(1)}, u32[]{:S(2)}, u32[]{:S(2)}) %collective-permute-start.19) | collective-permute-done | bytes 262176 | tf_op jit(solution)/shard_map/ppermute | solution.py:440
  143.9 3.3 %collective-permute-start.27 = (bf16[128,512]{1,0:T(8,128)(2,1)S(1)}, bf16[128,512]{1,0:T(8,128)(2,1)S(1)}, u32[]{:S(2)}, u32[]{:S(2)}) collective-permute-start(bf16[128,512]{1,0:T(8,128)(2,1)S(1)} %get-tuple-element.84), channel_id=1, source_target_pairs={{0,8},{8,0},{16,24},{24,16},{1,9},{9,1},{17,25},{25,17},{2,10},{10... | collective-permute-start | bytes 393224 | tf_op jit(solution)/shard_map/ppermute | solution.py:451
  147.1 2.5 %collective-permute-start.17 = (bf16[256,512]{1,0:T(8,128)(2,1)S(1)}, bf16[256,512]{1,0:T(8,128)(2,1)S(1)}, u32[]{:S(2)}, u32[]{:S(2)}) collective-permute-start(bf16[256,512]{1,0:T(8,128)(2,1)S(1)} %get-tuple-element.71), channel_id=1, source_target_pairs={{0,2},{1,3},{2,0},{3,1},{4,6},{5,7},{6,4},{7,5},{8,10},{9,11},{10,... | collective-permute-start | bytes 786440 | tf_op jit(solution)/shard_map/ppermute | solution.py:440
  149.6 1.5 collective-permute-start.29
  151.2 0.7 collective-permute-start.18
  151.8 5.0 %collective-permute-start.20 = (bf16[256,512]{1,0:T(8,128)(2,1)S(1)}, bf16[256,512]{1,0:T(8,128)(2,1)S(1)}, u32[]{:S(2)}, u32[]{:S(2)}) collective-permute-start(bf16[256,512]{1,0:T(8,128)(2,1)S(1)} %shard_map.118.refs_2_), channel_id=1, source_target_pairs={{0,4},{1,5},{2,6},{3,7},{4,0},{5,1},{6,2},{7,3},{8,12},{9,13},{10,... | collective-permute-start | bytes 786440 | tf_op jit(solution)/shard_map/ppermute | solution.py:440
  157.7 2.9 %collective-permute-start.31 = (bf16[128,512]{1,0:T(8,128)(2,1)S(1)}, bf16[128,512]{1,0:T(8,128)(2,1)S(1)}, u32[]{:S(2)}, u32[]{:S(2)}) collective-permute-start(bf16[128,512]{1,0:T(8,128)(2,1)S(1)} %shard_map.126.refs_0_), channel_id=1, source_target_pairs={{0,4},{1,5},{2,6},{3,7},{4,0},{5,1},{6,2},{7,3},{8,12},{9,13},{10,... | collective-permute-start | bytes 393224 | tf_op jit(solution)/shard_map/ppermute | solution.py:440
  160.6 0.9 collective-permute-start.32
  161.5 19.3 %collective-permute-done.20.refs_3_.refs_6_ = bf16[256,512]{1,0:T(8,128)(2,1)S(1)} collective-permute-done((bf16[256,512]{1,0:T(8,128)(2,1)S(1)}, bf16[256,512]{1,0:T(8,128)(2,1)S(1)}, u32[]{:S(2)}, u32[]{:S(2)}) %collective-permute-start.20) | collective-permute-done | bytes 262176 | tf_op jit(solution)/shard_map/ppermute | solution.py:440
  180.8 2.8 %collective-permute-done.31.refs_2_ = bf16[128,512]{1,0:T(8,128)(2,1)S(1)} collective-permute-done((bf16[128,512]{1,0:T(8,128)(2,1)S(1)}, bf16[128,512]{1,0:T(8,128)(2,1)S(1)}, u32[]{:S(2)}, u32[]{:S(2)}) %collective-permute-start.31) | collective-permute-done | bytes 131104 | tf_op jit(solution)/shard_map/ppermute | solution.py:440
  183.7 1.0 collective-permute-start.33
  184.7 0.9 collective-permute-start.34
  185.5 1.7 collective-permute-start.35
  187.2 1.5 collective-permute-done.33.refs_1_
  188.7 0.9 collective-permute-done.34.refs_2_
  189.7 1.8 collective-permute-done.35.refs_3_
  191.5 2.0 collective-permute-start.22
  193.6 0.7 collective-permute-start.23
  194.2 3.1 %collective-permute-start.25 = (bf16[256,512]{1,0:T(8,128)(2,1)S(1)}, bf16[256,512]{1,0:T(8,128)(2,1)S(1)}, u32[]{:S(2)}, u32[]{:S(2)}) collective-permute-start(bf16[256,512]{1,0:T(8,128)(2,1)S(1)} %shard_map.122.refs_4_), channel_id=1, source_target_pairs={{0,4},{1,5},{2,6},{3,7},{4,0},{5,1},{6,2},{7,3},{8,12},{9,13},{10,... | collective-permute-start | bytes 786440 | tf_op jit(solution)/shard_map/ppermute | solution.py:440
  197.7 2.8 %collective-permute-done.22.refs_1_ = bf16[256,512]{1,0:T(8,128)(2,1)S(1)} collective-permute-done((bf16[256,512]{1,0:T(8,128)(2,1)S(1)}, bf16[256,512]{1,0:T(8,128)(2,1)S(1)}, u32[]{:S(2)}, u32[]{:S(2)}) %collective-permute-start.22) | collective-permute-done | bytes 262176 | tf_op jit(solution)/shard_map/ppermute | solution.py:440
  200.5 14.9 %collective-permute-done.25.refs_3_ = bf16[256,512]{1,0:T(8,128)(2,1)S(1)} collective-permute-done((bf16[256,512]{1,0:T(8,128)(2,1)S(1)}, bf16[256,512]{1,0:T(8,128)(2,1)S(1)}, u32[]{:S(2)}, u32[]{:S(2)}) %collective-permute-start.25) | collective-permute-done | bytes 262176 | tf_op jit(solution)/shard_map/ppermute | solution.py:440
  215.7 0.8 pad_maximum_fusion
  216.6 1.5 shard_map.129
  (73 shorter events, 4.9 us)
Async XLA Ops:
  7.2 93.0 %all-gather.2.cloned.1.call-start = ((), (), s32[]{:S(2)}) async-start(), calls=%async_computation | async-start | bytes 4718592 | tf_op jit(solution)/shard_map/all_gather | solution.py:464
  7.9 1.0 copy-start.11
  11.0 1.6 copy-start.3
  12.6 0.7 copy-start.12
  15.6 2.8 %copy-start = (bf16[1,1,48,256,256]{4,3,2,1,0:T(8,128)(2,1)S(1)}, bf16[1,1,48,256,256]{4,3,2,1,0:T(8,128)(2,1)}, u32[]{:S(2)}) copy-start(bf16[1,1,48,256,256]{4,3,2,1,0:T(8,128)(2,1)} %param.10) | copy-start | bytes 18874372
  21.3 3.7 %collective-permute-start = (bf16[4,256,512]{2,1,0:T(8,128)(2,1)S(1)}, bf16[4,256,512]{2,1,0:T(8,128)(2,1)S(1)}, u32[]{:S(2)}, u32[]{:S(2)}) collective-permute-start(bf16[4,256,512]{2,1,0:T(8,128)(2,1)S(1)} %get-tuple-element.51), channel_id=1, source_target_pairs={{0,1},{1,0},{2,3},{3,2},{4,5},{5,4},{6,7},{7,6},{8,9},{9,8},{10,11... | collective-permute-start | bytes 3145736 | tf_op jit(solution)/shard_map/ppermute | solution.py:448
  28.7 21.7 %collective-permute-start.1 = (bf16[4,256,512]{2,1,0:T(8,128)(2,1)S(1)}, bf16[4,256,512]{2,1,0:T(8,128)(2,1)S(1)}, u32[]{:S(2)}, u32[]{:S(2)}) collective-permute-start(bf16[4,256,512]{2,1,0:T(8,128)(2,1)S(1)} %get-tuple-element.54), channel_id=1, source_target_pairs={{0,1},{1,0},{2,3},{3,2},{4,5},{5,4},{6,7},{7,6},{8,9},{9,8},{10,11... | collective-permute-start | bytes 3145736 | tf_op jit(solution)/shard_map/ppermute | solution.py:448
  28.8 17.2 %collective-permute-start.8 = (bf16[256,512]{1,0:T(8,128)(2,1)S(1)}, bf16[256,512]{1,0:T(8,128)(2,1)S(1)}, u32[]{:S(2)}, u32[]{:S(2)}) collective-permute-start(bf16[256,512]{1,0:T(8,128)(2,1)S(1)} %get-tuple-element.52.refs_4_), channel_id=1, source_target_pairs={{0,2},{1,3},{6,4},{7,5},{8,10},{9,11},{14,12},{15,13},{16,18},{17,... | collective-permute-start | bytes 786440 | tf_op jit(solution)/shard_map/ppermute | solution.py:440
  33.8 27.3 %collective-permute-start.7 = (bf16[256,512]{1,0:T(8,128)(2,1)S(1)}, bf16[256,512]{1,0:T(8,128)(2,1)S(1)}, u32[]{:S(2)}, u32[]{:S(2)}) collective-permute-start(bf16[256,512]{1,0:T(8,128)(2,1)S(1)} %get-tuple-element.52.refs_4_), channel_id=1, source_target_pairs={{2,4},{3,5},{4,2},{5,3},{10,12},{11,13},{12,10},{13,11},{18,20},{1... | collective-permute-start | bytes 786440 | tf_op jit(solution)/shard_map/ppermute | solution.py:440
  34.5 26.6 %collective-permute-start.6 = (bf16[256,512]{1,0:T(8,128)(2,1)S(1)}, bf16[256,512]{1,0:T(8,128)(2,1)S(1)}, u32[]{:S(2)}, u32[]{:S(2)}) collective-permute-start(bf16[256,512]{1,0:T(8,128)(2,1)S(1)} %get-tuple-element.60), channel_id=1, source_target_pairs={{0,2},{1,3},{2,0},{3,1},{4,6},{5,7},{6,4},{7,5},{8,10},{9,11},{10,... | collective-permute-start | bytes 786440 | tf_op jit(solution)/shard_map/ppermute | solution.py:440
  46.1 27.9 %collective-permute-start.9 = (bf16[256,512]{1,0:T(8,128)(2,1)S(1)}, bf16[256,512]{1,0:T(8,128)(2,1)S(1)}, u32[]{:S(2)}, u32[]{:S(2)}) collective-permute-start(bf16[256,512]{1,0:T(8,128)(2,1)S(1)} %shard_map.110), channel_id=1, source_target_pairs={{0,4},{1,5},{2,6},{3,7},{4,0},{5,1},{6,2},{7,3},{8,12},{9,13},{10,... | collective-permute-start | bytes 786440 | tf_op jit(solution)/shard_map/ppermute | solution.py:440
  50.7 38.6 %copy-start.4 = (bf16[512,512]{1,0:T(8,128)(2,1)S(1)}, bf16[512,512]{1,0:T(8,128)(2,1)}, u32[]{:S(2)}) copy-start(bf16[512,512]{1,0:T(8,128)(2,1)} %refs_4_.1) | copy-start | bytes 1572868
  50.7 27.8 %collective-permute-start.4 = (bf16[256,512]{1,0:T(8,128)(2,1)S(1)}, bf16[256,512]{1,0:T(8,128)(2,1)S(1)}, u32[]{:S(2)}, u32[]{:S(2)}) collective-permute-start(bf16[256,512]{1,0:T(8,128)(2,1)S(1)} %get-tuple-element.57), channel_id=1, source_target_pairs={{0,2},{1,3},{6,4},{7,5},{8,10},{9,11},{14,12},{15,13},{16,18},{17,... | collective-permute-start | bytes 786440 | tf_op jit(solution)/shard_map/ppermute | solution.py:440
  74.1 9.2 %collective-permute-start.13 = (bf16[256,512]{1,0:T(8,128)(2,1)S(1)}, bf16[256,512]{1,0:T(8,128)(2,1)S(1)}, u32[]{:S(2)}, u32[]{:S(2)}) collective-permute-start(bf16[256,512]{1,0:T(8,128)(2,1)S(1)} %shard_map.111.refs_5_.refs_0_), channel_id=1, source_target_pairs={{0,8},{8,0},{16,24},{24,16},{1,9},{9,1},{17,25},{25,17},{2,10},{10... | collective-permute-start | bytes 786440 | tf_op jit(solution)/shard_map/ppermute | solution.py:451
  75.7 13.6 %collective-permute-start.14 = (bf16[256,512]{1,0:T(8,128)(2,1)S(1)}, bf16[256,512]{1,0:T(8,128)(2,1)S(1)}, u32[]{:S(2)}, u32[]{:S(2)}) collective-permute-start(bf16[256,512]{1,0:T(8,128)(2,1)S(1)} %shard_map.111.refs_5_.refs_0_), channel_id=1, source_target_pairs={{0,16},{8,24},{16,0},{24,8},{1,17},{9,25},{17,1},{25,9},{2,18},{10... | collective-permute-start | bytes 786440 | tf_op jit(solution)/shard_map/ppermute | solution.py:451
  77.2 12.1 %collective-permute-start.15 = (bf16[256,512]{1,0:T(8,128)(2,1)S(1)}, bf16[256,512]{1,0:T(8,128)(2,1)S(1)}, u32[]{:S(2)}, u32[]{:S(2)}) collective-permute-start(bf16[256,512]{1,0:T(8,128)(2,1)S(1)} %shard_map.111.refs_5_.refs_0_), channel_id=1, source_target_pairs={{0,24},{8,16},{16,8},{24,0},{1,25},{9,17},{17,9},{25,1},{2,26},{10... | collective-permute-start | bytes 786440 | tf_op jit(solution)/shard_map/ppermute | solution.py:451
  77.7 13.5 %collective-permute-start.3 = (bf16[256,512]{1,0:T(8,128)(2,1)S(1)}, bf16[256,512]{1,0:T(8,128)(2,1)S(1)}, u32[]{:S(2)}, u32[]{:S(2)}) collective-permute-start(bf16[256,512]{1,0:T(8,128)(2,1)S(1)} %get-tuple-element.57), channel_id=1, source_target_pairs={{2,4},{3,5},{4,2},{5,3},{10,12},{11,13},{12,10},{13,11},{18,20},{1... | collective-permute-start | bytes 786440 | tf_op jit(solution)/shard_map/ppermute | solution.py:440
  78.5 12.7 %collective-permute-start.2 = (bf16[256,512]{1,0:T(8,128)(2,1)S(1)}, bf16[256,512]{1,0:T(8,128)(2,1)S(1)}, u32[]{:S(2)}, u32[]{:S(2)}) collective-permute-start(bf16[256,512]{1,0:T(8,128)(2,1)S(1)} %get-tuple-element.56), channel_id=1, source_target_pairs={{0,2},{1,3},{2,0},{3,1},{4,6},{5,7},{6,4},{7,5},{8,10},{9,11},{10,... | collective-permute-start | bytes 786440 | tf_op jit(solution)/shard_map/ppermute | solution.py:440
  83.3 13.1 %collective-permute-start.5 = (bf16[256,512]{1,0:T(8,128)(2,1)S(1)}, bf16[256,512]{1,0:T(8,128)(2,1)S(1)}, u32[]{:S(2)}, u32[]{:S(2)}) collective-permute-start(bf16[256,512]{1,0:T(8,128)(2,1)S(1)} %shard_map.109), channel_id=1, source_target_pairs={{0,4},{1,5},{2,6},{3,7},{4,0},{5,1},{6,2},{7,3},{8,12},{9,13},{10,... | collective-permute-start | bytes 786440 | tf_op jit(solution)/shard_map/ppermute | solution.py:440
  89.3 23.7 %slice-start = ((s8[6291456]{0:T(1024)(128)(4,1)}), s8[2097152]{0:T(1024)(128)(4,1)S(1)}, s32[]{:S(2)}) async-start(s8[6291456]{0:T(1024)(128)(4,1)} %bitcast.11), calls=%async_computation.1 | async-start | bytes 4194304
  90.4 6.3 %copy-start.7 = (bf16[4,256,512]{2,1,0:T(8,128)(2,1)}, bf16[4,256,512]{2,1,0:T(8,128)(2,1)S(1)}, u32[]{:S(2)}) copy-start(bf16[4,256,512]{2,1,0:T(8,128)(2,1)S(1)} %get-tuple-element.62.refs_6_) | copy-start | bytes 3145732
  90.4 7.8 %copy-start.9 = (bf16[4,256,512]{2,1,0:T(8,128)(2,1)}, bf16[4,256,512]{2,1,0:T(8,128)(2,1)S(1)}, u32[]{:S(2)}) copy-start(bf16[4,256,512]{2,1,0:T(8,128)(2,1)S(1)} %get-tuple-element.63.refs_7_) | copy-start | bytes 3145732
  96.6 14.0 %collective-permute-start.10 = (bf16[256,512]{1,0:T(8,128)(2,1)S(1)}, bf16[256,512]{1,0:T(8,128)(2,1)}, u32[]{:S(2)}, u32[]{:S(2)}) collective-permute-start(bf16[256,512]{1,0:T(8,128)(2,1)S(1)} %shard_map.112.refs_0_), channel_id=1, source_target_pairs={{0,8},{8,0},{16,24},{24,16},{1,9},{9,1},{17,25},{25,17},{2,10},{10... | collective-permute-start | bytes 786440 | tf_op jit(solution)/shard_map/ppermute | solution.py:451
  98.1 12.5 %collective-permute-start.11 = (bf16[256,512]{1,0:T(8,128)(2,1)S(1)}, bf16[256,512]{1,0:T(8,128)(2,1)}, u32[]{:S(2)}, u32[]{:S(2)}) collective-permute-start(bf16[256,512]{1,0:T(8,128)(2,1)S(1)} %shard_map.112.refs_0_), channel_id=1, source_target_pairs={{0,16},{8,24},{16,0},{24,8},{1,17},{9,25},{17,1},{25,9},{2,18},{10... | collective-permute-start | bytes 786440 | tf_op jit(solution)/shard_map/ppermute | solution.py:451
  99.6 11.1 %collective-permute-start.12 = (bf16[256,512]{1,0:T(8,128)(2,1)S(1)}, bf16[256,512]{1,0:T(8,128)(2,1)}, u32[]{:S(2)}, u32[]{:S(2)}) collective-permute-start(bf16[256,512]{1,0:T(8,128)(2,1)S(1)} %shard_map.112.refs_0_), channel_id=1, source_target_pairs={{0,24},{8,16},{16,8},{24,0},{1,25},{9,17},{17,9},{25,1},{2,26},{10... | collective-permute-start | bytes 786440 | tf_op jit(solution)/shard_map/ppermute | solution.py:451
  100.2 2.8 %copy-start.1 = (bf16[1,1,48,256,256]{4,3,2,1,0:T(8,128)(2,1)S(1)}, bf16[1,1,48,256,256]{4,3,2,1,0:T(8,128)(2,1)}, u32[]{:S(2)}) copy-start(bf16[1,1,48,256,256]{4,3,2,1,0:T(8,128)(2,1)} %param.10) | copy-start | bytes 18874372
  103.0 2.2 copy-start.2
  105.2 5.5 %copy-start.5 = (bf16[512,512]{1,0:T(8,128)(2,1)S(1)}, bf16[512,512]{1,0:T(8,128)(2,1)}, u32[]{:S(2)}) copy-start(bf16[512,512]{1,0:T(8,128)(2,1)} %refs_4_.1) | copy-start | bytes 1572868
  105.2 5.5 %copy-start.8 = (bf16[4,256,512]{2,1,0:T(8,128)(2,1)S(1)}, bf16[4,256,512]{2,1,0:T(8,128)(2,1)}, u32[]{:S(2)}) copy-start(bf16[4,256,512]{2,1,0:T(8,128)(2,1)} %copy-done.7) | copy-start | bytes 3145732
  105.2 5.5 %copy-start.10 = (bf16[4,256,512]{2,1,0:T(8,128)(2,1)S(1)}, bf16[4,256,512]{2,1,0:T(8,128)(2,1)}, u32[]{:S(2)}) copy-start(bf16[4,256,512]{2,1,0:T(8,128)(2,1)} %copy-done.9) | copy-start | bytes 3145732
  105.2 7.8 %slice-start.1 = ((s8[6291456]{0:T(1024)(128)(4,1)}), s8[4194304]{0:T(1024)(128)(4,1)S(1)}, s32[]{:S(2)}) async-start(s8[6291456]{0:T(1024)(128)(4,1)} %bitcast.11), calls=%async_computation.2 | async-start | bytes 8388608
  115.9 2.7 %collective-permute-start.16 = (bf16[4,256,512]{2,1,0:T(8,128)(2,1)S(1)}, bf16[4,256,512]{2,1,0:T(8,128)(2,1)S(1)}, u32[]{:S(2)}, u32[]{:S(2)}) collective-permute-start(bf16[4,256,512]{2,1,0:T(8,128)(2,1)S(1)} %get-tuple-element.69), channel_id=1, source_target_pairs={{0,1},{1,0},{2,3},{3,2},{4,5},{5,4},{6,7},{7,6},{8,9},{9,8},{10,11... | collective-permute-start | bytes 3145736 | tf_op jit(solution)/shard_map/ppermute | solution.py:448
  122.4 3.0 %copy-start.6 = (bf16[512,512]{1,0:T(8,128)(2,1)S(1)}, bf16[512,512]{1,0:T(8,128)(2,1)}, u32[]{:S(2)}) copy-start(bf16[512,512]{1,0:T(8,128)(2,1)} %refs_5_.9) | copy-start | bytes 1572868
  122.5 2.7 %collective-permute-start.21 = (bf16[4,256,512]{2,1,0:T(8,128)(2,1)S(1)}, bf16[4,256,512]{2,1,0:T(8,128)(2,1)S(1)}, u32[]{:S(2)}, u32[]{:S(2)}) collective-permute-start(bf16[4,256,512]{2,1,0:T(8,128)(2,1)S(1)} %get-tuple-element.75), channel_id=1, source_target_pairs={{0,1},{1,0},{2,3},{3,2},{4,5},{5,4},{6,7},{7,6},{8,9},{9,8},{10,11... | collective-permute-start | bytes 3145736 | tf_op jit(solution)/shard_map/ppermute | solution.py:448
  134.1 9.6 %collective-permute-start.26 = (bf16[512,512]{1,0:T(8,128)(2,1)S(1)}, bf16[512,512]{1,0:T(8,128)(2,1)S(1)}, u32[]{:S(2)}, u32[]{:S(2)}) collective-permute-start(bf16[512,512]{1,0:T(8,128)(2,1)S(1)} %get-tuple-element.82), channel_id=1, source_target_pairs={{0,1},{1,0},{2,3},{3,2},{4,5},{5,4},{6,7},{7,6},{8,9},{9,8},{10,11... | collective-permute-start | bytes 1572872 | tf_op jit(solution)/shard_map/ppermute | solution.py:448
  134.3 9.3 %collective-permute-start.19 = (bf16[256,512]{1,0:T(8,128)(2,1)S(1)}, bf16[256,512]{1,0:T(8,128)(2,1)S(1)}, u32[]{:S(2)}, u32[]{:S(2)}) collective-permute-start(bf16[256,512]{1,0:T(8,128)(2,1)S(1)} %get-tuple-element.72.refs_4_), channel_id=1, source_target_pairs={{0,2},{1,3},{6,4},{7,5},{8,10},{9,11},{14,12},{15,13},{16,18},{17,... | collective-permute-start | bytes 786440 | tf_op jit(solution)/shard_map/ppermute | solution.py:440
  137.0 14.1 %collective-permute-start.24 = (bf16[256,512]{1,0:T(8,128)(2,1)S(1)}, bf16[256,512]{1,0:T(8,128)(2,1)S(1)}, u32[]{:S(2)}, u32[]{:S(2)}) collective-permute-start(bf16[256,512]{1,0:T(8,128)(2,1)S(1)} %get-tuple-element.78.refs_6_), channel_id=1, source_target_pairs={{0,2},{1,3},{6,4},{7,5},{8,10},{9,11},{14,12},{15,13},{16,18},{17,... | collective-permute-start | bytes 786440 | tf_op jit(solution)/shard_map/ppermute | solution.py:440
  143.9 8.0 %collective-permute-start.27 = (bf16[128,512]{1,0:T(8,128)(2,1)S(1)}, bf16[128,512]{1,0:T(8,128)(2,1)S(1)}, u32[]{:S(2)}, u32[]{:S(2)}) collective-permute-start(bf16[128,512]{1,0:T(8,128)(2,1)S(1)} %get-tuple-element.84), channel_id=1, source_target_pairs={{0,8},{8,0},{16,24},{24,16},{1,9},{9,1},{17,25},{25,17},{2,10},{10... | collective-permute-start | bytes 393224 | tf_op jit(solution)/shard_map/ppermute | solution.py:451
  147.1 13.4 %collective-permute-start.17 = (bf16[256,512]{1,0:T(8,128)(2,1)S(1)}, bf16[256,512]{1,0:T(8,128)(2,1)S(1)}, u32[]{:S(2)}, u32[]{:S(2)}) collective-permute-start(bf16[256,512]{1,0:T(8,128)(2,1)S(1)} %get-tuple-element.71), channel_id=1, source_target_pairs={{0,2},{1,3},{2,0},{3,1},{4,6},{5,7},{6,4},{7,5},{8,10},{9,11},{10,... | collective-permute-start | bytes 786440 | tf_op jit(solution)/shard_map/ppermute | solution.py:440
  149.6 7.3 %collective-permute-start.28 = (bf16[128,512]{1,0:T(8,128)(2,1)S(1)}, bf16[128,512]{1,0:T(8,128)(2,1)S(1)}, u32[]{:S(2)}, u32[]{:S(2)}) collective-permute-start(bf16[128,512]{1,0:T(8,128)(2,1)S(1)} %get-tuple-element.85), channel_id=1, source_target_pairs={{0,16},{8,24},{16,0},{24,8},{1,17},{9,25},{17,1},{25,9},{2,18},{10... | collective-permute-start | bytes 393224 | tf_op jit(solution)/shard_map/ppermute | solution.py:451
  149.6 7.3 %collective-permute-start.29 = (bf16[128,512]{1,0:T(8,128)(2,1)S(1)}, bf16[128,512]{1,0:T(8,128)(2,1)S(1)}, u32[]{:S(2)}, u32[]{:S(2)}) collective-permute-start(bf16[128,512]{1,0:T(8,128)(2,1)S(1)} %get-tuple-element.86), channel_id=1, source_target_pairs={{0,24},{8,16},{16,8},{24,0},{1,25},{9,17},{17,9},{25,1},{2,26},{10... | collective-permute-start | bytes 393224 | tf_op jit(solution)/shard_map/ppermute | solution.py:451
  151.2 10.3 %collective-permute-start.18 = (bf16[256,512]{1,0:T(8,128)(2,1)S(1)}, bf16[256,512]{1,0:T(8,128)(2,1)S(1)}, u32[]{:S(2)}, u32[]{:S(2)}) collective-permute-start(bf16[256,512]{1,0:T(8,128)(2,1)S(1)} %get-tuple-element.72.refs_4_), channel_id=1, source_target_pairs={{2,4},{3,5},{4,2},{5,3},{10,12},{11,13},{12,10},{13,11},{18,20},{1... | collective-permute-start | bytes 786440 | tf_op jit(solution)/shard_map/ppermute | solution.py:440
  151.8 29.0 %collective-permute-start.20 = (bf16[256,512]{1,0:T(8,128)(2,1)S(1)}, bf16[256,512]{1,0:T(8,128)(2,1)S(1)}, u32[]{:S(2)}, u32[]{:S(2)}) collective-permute-start(bf16[256,512]{1,0:T(8,128)(2,1)S(1)} %shard_map.118.refs_2_), channel_id=1, source_target_pairs={{0,4},{1,5},{2,6},{3,7},{4,0},{5,1},{6,2},{7,3},{8,12},{9,13},{10,... | collective-permute-start | bytes 786440 | tf_op jit(solution)/shard_map/ppermute | solution.py:440
  157.0 23.8 %collective-permute-start.30 = (bf16[128,512]{1,0:T(8,128)(2,1)S(1)}, bf16[128,512]{1,0:T(8,128)(2,1)S(1)}, u32[]{:S(2)}, u32[]{:S(2)}) collective-permute-start(bf16[128,512]{1,0:T(8,128)(2,1)S(1)} %shard_map.126.refs_0_), channel_id=1, source_target_pairs={{0,2},{1,3},{2,0},{3,1},{4,6},{5,7},{6,4},{7,5},{8,10},{9,11},{10,... | collective-permute-start | bytes 393224 | tf_op jit(solution)/shard_map/ppermute | solution.py:440
  157.7 25.9 %collective-permute-start.31 = (bf16[128,512]{1,0:T(8,128)(2,1)S(1)}, bf16[128,512]{1,0:T(8,128)(2,1)S(1)}, u32[]{:S(2)}, u32[]{:S(2)}) collective-permute-start(bf16[128,512]{1,0:T(8,128)(2,1)S(1)} %shard_map.126.refs_0_), channel_id=1, source_target_pairs={{0,4},{1,5},{2,6},{3,7},{4,0},{5,1},{6,2},{7,3},{8,12},{9,13},{10,... | collective-permute-start | bytes 393224 | tf_op jit(solution)/shard_map/ppermute | solution.py:440
  160.6 23.0 %collective-permute-start.32 = (bf16[128,512]{1,0:T(8,128)(2,1)S(1)}, bf16[128,512]{1,0:T(8,128)(2,1)S(1)}, u32[]{:S(2)}, u32[]{:S(2)}) collective-permute-start(bf16[128,512]{1,0:T(8,128)(2,1)S(1)} %shard_map.126.refs_0_), channel_id=1, source_target_pairs={{0,6},{1,7},{2,4},{3,5},{4,2},{5,3},{6,0},{7,1},{8,14},{9,15},{10,... | collective-permute-start | bytes 393224 | tf_op jit(solution)/shard_map/ppermute | solution.py:440
  183.7 5.0 %collective-permute-start.33 = (bf16[128,512]{1,0:T(8,128)(2,1)S(1)}, bf16[128,512]{1,0:T(8,128)(2,1)S(1)}, u32[]{:S(2)}, u32[]{:S(2)}) collective-permute-start(bf16[128,512]{1,0:T(8,128)(2,1)S(1)} %shard_map.127.refs_0_), channel_id=1, source_target_pairs={{0,8},{8,0},{16,24},{24,16},{1,9},{9,1},{17,25},{25,17},{2,10},{10... | collective-permute-start | bytes 393224 | tf_op jit(solution)/shard_map/ppermute | solution.py:451
  184.7 5.0 %collective-permute-start.34 = (bf16[128,512]{1,0:T(8,128)(2,1)S(1)}, bf16[128,512]{1,0:T(8,128)(2,1)S(1)}, u32[]{:S(2)}, u32[]{:S(2)}) collective-permute-start(bf16[128,512]{1,0:T(8,128)(2,1)S(1)} %shard_map.127.refs_0_), channel_id=1, source_target_pairs={{0,16},{8,24},{16,0},{24,8},{1,17},{9,25},{17,1},{25,9},{2,18},{10... | collective-permute-start | bytes 393224 | tf_op jit(solution)/shard_map/ppermute | solution.py:451
  185.5 5.9 %collective-permute-start.35 = (bf16[128,512]{1,0:T(8,128)(2,1)S(1)}, bf16[128,512]{1,0:T(8,128)(2,1)S(1)}, u32[]{:S(2)}, u32[]{:S(2)}) collective-permute-start(bf16[128,512]{1,0:T(8,128)(2,1)S(1)} %shard_map.127.refs_0_), channel_id=1, source_target_pairs={{0,24},{8,16},{16,8},{24,0},{1,25},{9,17},{17,9},{25,1},{2,26},{10... | collective-permute-start | bytes 393224 | tf_op jit(solution)/shard_map/ppermute | solution.py:451
  191.5 25.1 %collective-permute-start.36 = (bf16[512,512]{1,0:T(8,128)(2,1)S(1)}, bf16[512,512]{1,0:T(8,128)(2,1)S(1)}, u32[]{:S(2)}, u32[]{:S(2)}) collective-permute-start(bf16[512,512]{1,0:T(8,128)(2,1)S(1)} %shard_map.128.refs_0_), channel_id=1, source_target_pairs={{0,1},{1,0},{2,3},{3,2},{4,5},{5,4},{6,7},{7,6},{8,9},{9,8},{10,11... | collective-permute-start | bytes 1572872 | tf_op jit(solution)/shard_map/ppermute | solution.py:448
  191.5 8.9 %collective-permute-start.22 = (bf16[256,512]{1,0:T(8,128)(2,1)S(1)}, bf16[256,512]{1,0:T(8,128)(2,1)S(1)}, u32[]{:S(2)}, u32[]{:S(2)}) collective-permute-start(bf16[256,512]{1,0:T(8,128)(2,1)S(1)} %get-tuple-element.77), channel_id=1, source_target_pairs={{0,2},{1,3},{2,0},{3,1},{4,6},{5,7},{6,4},{7,5},{8,10},{9,11},{10,... | collective-permute-start | bytes 786440 | tf_op jit(solution)/shard_map/ppermute | solution.py:440
  193.6 6.9 %collective-permute-start.23 = (bf16[256,512]{1,0:T(8,128)(2,1)S(1)}, bf16[256,512]{1,0:T(8,128)(2,1)S(1)}, u32[]{:S(2)}, u32[]{:S(2)}) collective-permute-start(bf16[256,512]{1,0:T(8,128)(2,1)S(1)} %get-tuple-element.78.refs_6_), channel_id=1, source_target_pairs={{2,4},{3,5},{4,2},{5,3},{10,12},{11,13},{12,10},{13,11},{18,20},{1... | collective-permute-start | bytes 786440 | tf_op jit(solution)/shard_map/ppermute | solution.py:440
  194.2 21.2 %collective-permute-start.25 = (bf16[256,512]{1,0:T(8,128)(2,1)S(1)}, bf16[256,512]{1,0:T(8,128)(2,1)S(1)}, u32[]{:S(2)}, u32[]{:S(2)}) collective-permute-start(bf16[256,512]{1,0:T(8,128)(2,1)S(1)} %shard_map.122.refs_4_), channel_id=1, source_target_pairs={{0,4},{1,5},{2,6},{3,7},{4,0},{5,1},{6,2},{7,3},{8,12},{9,13},{10,... | collective-permute-start | bytes 786440 | tf_op jit(solution)/shard_map/ppermute | solution.py:440
Sparse Core Ops, SparseCore 0:
  10.4 66.0 all-gather.1

commit v5 on v4

v5 whole, which is shorter than its diff:
```python
import functools

import jax
import jax.numpy as jnp
from jax import lax
from jax.experimental import pallas as pl
from jax.experimental.pallas import tpu as pltpu
from jax.sharding import PartitionSpec as P

F32 = jnp.float32
BF16 = jnp.bfloat16
MIB = 1024 * 1024
VMEM = pl.BlockSpec(memory_space=pltpu.VMEM)
SMEM = pl.BlockSpec(memory_space=pltpu.SMEM)
ANY = pl.BlockSpec(memory_space=pl.ANY)


def run(body, args, specs, outs, scratch=(), mib=8, after=(), out_specs=None):
    n, extra = len(args), len(after)

    def whole(*refs):
        body(*refs[:n], *refs[n + extra :])

    return pl.pallas_call(
        whole,
        out_shape=outs,
        in_specs=specs + [ANY] * extra,
        out_specs=out_specs or [VMEM] * len(outs),
        scratch_shapes=list(scratch),
        compiler_params=pltpu.CompilerParams(vmem_limit_bytes=mib * MIB),
        cost_estimate=pl.CostEstimate(
            flops=int(COST.get(getattr(body, "func", body), 0) * 1e9),
            bytes_accessed=0,
            transcendentals=0,
        ),
    )(*args, *after)


def shape(dims, dtype=BF16):
    return jax.ShapeDtypeStruct(dims, dtype)


def list_tiles(count, slot_ref, number_ref, list_ref, local_cols, by_row):
    groups, cap = number_ref.shape[0], list_ref.shape[0] // number_ref.shape[0]
    blank = slot_ref.shape[0] * 1024
    bits = local_cols.bit_length() - 1

    def clear(g, _):
        number_ref[g] = 0
        for j in range(cap):
            list_ref[g * cap + j] = blank
        return 0

    lax.fori_loop(0, groups, clear, 0)

    def place(s, _):
        p = slot_ref[s]
        u, v = lax.shift_right_logical(p, bits), p & (local_cols - 1)
        g, other = (u, v) if by_row else (v, u)
        n = number_ref[g]
        list_ref[g * cap + n] = s * 1024 + other
        number_ref[g] = n + 1
        return 0

    lax.fori_loop(0, count, place, 0)


def repeat_lanes(scale, width):
    return jnp.concatenate([scale] * (width // scale.shape[-1]), 1)


def scale_body(degree, cot, scale, out):
    edge, lanes = scale.shape[1:]
    width = cot.shape[1]
    for i in range(scale.shape[0]):
        part = degree[i // 2 : i // 2 + 1, i % 2 * edge : (i % 2 + 1) * edge]
        line = 1.0 / jnp.sqrt(part.astype(F32))
        scale[i] = jnp.broadcast_to(line, (lanes, edge)).T
    row = lax.axis_index("row")
    for e in range(2):
        value = cot[e * edge : (e + 1) * edge, :].astype(F32)
        out[e] = (value * repeat_lanes(scale[row * 2 + e], width)).T.astype(BF16)


def scale_kernel(degree, cotangent, edge):
    return run(
        scale_body,
        (degree, cotangent),
        [VMEM] * 2,
        [shape((2 * degree.shape[0], edge, 128), F32), shape((2, cotangent.shape[1], edge))],
    )


def prepare_body(local_cols, count_ref, slot_ref, values, scale, out, *lists):
    list_tiles(count_ref[0], slot_ref, lists[0], lists[1], local_cols, True)
    list_tiles(count_ref[0], slot_ref, lists[2], lists[3], local_cols, False)

    def fill(i, _):
        wide = repeat_lanes(scale[i], values.shape[-1])
        out[i] = (values[i].astype(F32) * wide).astype(BF16)
        return 0

    lax.fori_loop(0, local_cols, fill, 0)


def prepare(count, slots, values, scale, block_rows):
    local_cols = values.shape[0]
    sizes = (block_rows, block_rows * local_cols, local_cols, block_rows * local_cols)
    return run(
        functools.partial(prepare_body, local_cols),
        (count, slots, values, scale),
        [SMEM] * 2 + [VMEM] * 2,
        [shape(values.shape)] + [shape((n,), jnp.int32) for n in sizes],
        out_specs=[VMEM] + [SMEM] * 4,
        mib=12,
    )


def sum_group(g, number_ref, list_ref, total, product, store):
    cap = list_ref.shape[0] // number_ref.shape[0]
    n = number_ref[g]

    def take(start, width):
        entries = [list_ref[g * cap + start + j] for j in range(width)]
        return product([(lax.shift_right_logical(x, 10), x & 1023) for x in entries])

    def exact(width):
        @pl.when(n == width)
        def _():
            store(take(0, width))

    @pl.when(n == 0)
    def _():
        store(jnp.zeros_like(total))

    for width in range(1, 5):
        exact(width)

    @pl.when(n > 4)
    def _():
        total[...] = jnp.zeros_like(total)
        fours = lax.shift_right_logical(n, 2)

        def four(m, _):
            total[...] += take(4 * m, 4)
            return 0

        def one(m, _):
            total[...] += take(m, 1)
            return 0

        lax.fori_loop(0, fours, four, 0)
        lax.fori_loop(4 * fours, n, one, 0)
        store(total[...])


def joined_dot(lhs, rhs):
    return jnp.dot(
        jnp.concatenate(lhs, 1), jnp.concatenate(rhs, 0), preferred_element_type=F32
    )


def forward_body(first, flip, number_ref, list_ref, tiles, source, out, total):
    col, row = lax.axis_index("col"), lax.axis_index("row")
    line = out.shape[0] // 2

    def product(pieces):
        def locate(v):
            return v if first else v ^ (2 * row)

        return joined_dot([tiles[s] for s, _ in pieces], [source[locate(v)] for _, v in pieces])

    for half in range(2):

        def block(i, _):
            def store(value):
                out[half * line + i] = value.astype(BF16)

            g = (col ^ (2 * i + flip)) * 2 + half
            sum_group(g, number_ref, list_ref, total, product, store)
            return 0

        lax.fori_loop(0, line, block, 0)


def forward(number, entries, tiles, source, first, flip, after=()):
    slots_n, edge, _ = tiles.shape
    width = source.shape[-1]
    return run(
        functools.partial(forward_body, first, flip),
        (number, entries, tiles, source),
        [SMEM, SMEM, VMEM, VMEM],
        [shape((number.shape[0] // 2, edge, width))],
        [pltpu.VMEM((edge, width), F32)],
        mib=16,
        after=after,
    )[0]


def backward_body(n, number_ref, list_ref, tiles, *refs):
    pieces_in, (out, ranged, total) = refs[:n], refs[n:]
    mask, flips = lax.axis_index("row") * 2, lax.axis_index("col") * 2
    for i, piece in enumerate(pieces_in):
        ranged[2 * i : 2 * i + 2] = piece[...]

    def product(pieces):
        return joined_dot([ranged[u ^ flips] for _, u in pieces], [tiles[s] for s, _ in pieces])

    def block(i, _):
        def store(value):
            out[i] = value.astype(BF16)

        sum_group(i ^ mask, number_ref, list_ref, total, product, store)
        return 0

    lax.fori_loop(0, out.shape[0], block, 0)


def backward(number, entries, tiles, pieces, after=()):
    slots_n, edge, _ = tiles.shape
    _, width, _ = pieces[0].shape
    n = len(pieces)
    return run(
        functools.partial(backward_body, n),
        (number, entries, tiles, *pieces),
        [SMEM, SMEM] + [VMEM] * (n + 1),
        [shape((number.shape[0], width, edge))],
        [pltpu.VMEM((2 * n, width, edge), BF16), pltpu.VMEM((width, edge), F32)],
        mib=20,
        after=after,
    )[0]


def pair_sum_body(n, keep, come, *outs):
    for j in range(n):
        for half in range(2):
            i = half * n + j
            outs[j][half] = (keep[i].astype(F32) + come[i].astype(F32)).astype(BF16)


def pair_sum(keep, come):
    n = keep.shape[0] // 2
    return run(
        functools.partial(pair_sum_body, n),
        (keep, come),
        [VMEM] * 2,
        [shape((2, *keep.shape[1:]))] * n,
        mib=12,
    )


def tree(items):
    while len(items) > 1:
        items = [a + b for a, b in zip(items[::2], items[1::2])]
    return items[0]


def onward_body(own, far, near, middle, inward, part, message):
    part[...] = own[...].astype(F32) + near[...].astype(F32) + middle[...].astype(F32)
    message[...] = (far[...].astype(F32) + inward[...].astype(F32)).astype(BF16)


def onward(own, far, near, middle, inward, after):
    return run(
        onward_body,
        (own, far, near, middle, inward),
        [VMEM] * 5,
        [shape(own.shape, F32), shape(own.shape)],
        mib=12,
        after=after,
    )


def relay_body(n, *refs):
    for source, out in zip(refs[:n], refs[n:]):
        out[...] = source[...]


def relay(items, after):
    return run(
        functools.partial(relay_body, len(items)),
        tuple(items),
        [VMEM] * len(items),
        [shape(x.shape) for x in items],
        after=after,
    )


def choose_body(at_ends, across, middle, out_two, out_three, two, three):
    position = lax.shift_right_logical(lax.axis_index("col"), 1)
    ends = jnp.logical_or(position == 0, position == at_ends)
    two[...] = jnp.where(ends, out_two[...], across[...])
    three[...] = jnp.where(ends, out_three[...], middle[...])


def choose(last, across, middle, out_two, out_three):
    return run(
        functools.partial(choose_body, last),
        (across, middle, out_two, out_three),
        [VMEM] * 4,
        [shape(across.shape)] * 2,
    )


def agg_body(part, *refs):
    scale, out = refs[-2:]
    for half in range(2):
        summed = part[half]
        for x in refs[:-2]:
            summed = summed + x[half].astype(F32)
        wide = repeat_lanes(scale[lax.axis_index("row") * 2 + half], summed.shape[1])
        out[half] = (summed * wide).astype(BF16)


def aggregate(part, far, scale):
    return run(
        agg_body,
        (part, *far, scale),
        [VMEM] * (2 + len(far)),
        [shape(part.shape)],
    )[0]


def first_body(start, n, *refs):
    scale, weight, agg, out = refs[n], refs[n + 1], refs[-2], refs[-1]
    row = lax.axis_index("row")
    if start:
        agg[: 2 * start] = refs[n + 2][...]
        out[: 2 * start] = refs[n + 3][...]
    for i in range(n):
        j = start + i
        for half in range(2):
            value = jnp.dot(refs[i][half], weight[...], preferred_element_type=F32)
            wide = repeat_lanes(scale[(row ^ j) * 2 + half], value.shape[1])
            out[2 * j + half] = (jax.nn.gelu(value) * wide).astype(BF16)
            agg[2 * j + half] = refs[i][half]


def first_layer(aggs, scale, weight, before=(), after=()):
    n = len(aggs)
    start = before[0].shape[0] // 2 if before else 0
    return run(
        functools.partial(first_body, start, n),
        (*aggs, scale, weight, *before),
        [VMEM] * (n + 2 + len(before)),
        [shape((2 * (start + n), *aggs[0].shape[1:]))] * 2,
        mib=14,
        after=after,
    )


def second_body(part, *refs):
    scale, weight, out = refs[-3:]
    edge = part.shape[1]
    for half in range(2):
        summed = part[half]
        for x in refs[:-3]:
            summed = summed + x[half].astype(F32)
        wide = repeat_lanes(scale[lax.axis_index("row") * 2 + half], summed.shape[1])
        agg = (summed * wide).astype(BF16)
        value = jnp.dot(agg, weight[...], preferred_element_type=F32)
        out[half * edge : (half + 1) * edge, :] = value.astype(BF16)


def second_layer(part, far, scale, weight):
    halves, edge, width = part.shape
    return run(
        second_body,
        (part, *far, scale, weight),
        [VMEM] * (3 + len(far)),
        [shape((halves * edge, width))],
    )[0]


def grad_body(start, last, hidden_ref, aggs, outs, scale, w_first, w_second, *refs):
    row = lax.axis_index("row")
    core = lax.rem(lax.axis_index("col"), 2)
    first, second = refs[-2:]
    if start:
        first[...] = refs[0][...]
        second[...] = refs[1][...]
    else:
        first[...] = jnp.zeros_like(first)
        second[...] = jnp.zeros_like(second)

    def block(i, _):
        hidden, agg = hidden_ref[i], aggs[i]
        pre = jnp.dot(agg, w_first[...], preferred_element_type=F32)
        grad_hidden = lax.dot_general(
            hidden, w_second[...], (((0,), (1,)), ((), ())), preferred_element_type=F32
        )
        _, pullback = jax.vjp(jax.nn.gelu, pre)
        wide = repeat_lanes(scale[i ^ (2 * row)], pre.shape[1])
        grad_pre = pullback(grad_hidden * wide)[0].astype(BF16)
        first[...] += lax.dot_general(
            agg, grad_pre, (((0,), (0,)), ((), ())), preferred_element_type=F32
        )
        second[...] += lax.dot_general(
            outs[i], hidden, (((0,), (1,)), ((), ())), preferred_element_type=F32
        )
        return 0

    lax.fori_loop(start, aggs.shape[0], block, 0)
    if last:
        give, keep = refs[2:4]
        keep[...] = jnp.where(core == 0, first[...], second[...]).astype(BF16)
        give[...] = jnp.where(core == 0, second[...], first[...]).astype(BF16)


def weight_grads(start, hidden, aggs, outs, scale, w_first, w_second, before=(), after=()):
    dims = w_first.shape
    last = aggs.shape[0] == hidden.shape[0]
    return run(
        functools.partial(grad_body, start, last),
        (hidden, aggs, outs, scale, w_first, w_second, *before),
        [VMEM] * (6 + len(before)),
        [shape(dims)] * 2 if last else [shape(dims, F32)] * 2,
        [pltpu.VMEM(dims, F32)] * 2 if last else [],
        mib=26,
        after=after,
    )


def split_body(n, keep, come, *outs):
    row = lax.axis_index("row")
    rows = keep.shape[0] // n
    for j in range(n):
        part = pl.ds(pl.multiple_of((row ^ j) * rows, rows), rows)
        outs[j][...] = (keep[part, :].astype(F32) + come[part, :].astype(F32)).astype(BF16)


def split_sum(keep, come, n, after):
    rows, width = keep.shape
    return run(
        functools.partial(split_body, n),
        (keep, come),
        [VMEM] * 2,
        [shape((rows // n, width))] * n,
        after=after,
    )


def sum_body(n, *refs):
    refs[n][...] = tree([x[...].astype(F32) for x in refs[:n]]).astype(BF16)


def sum_parts(parts, after=()):
    return run(
        functools.partial(sum_body, len(parts)),
        tuple(parts),
        [VMEM] * len(parts),
        [shape(parts[0].shape)],
        after=after,
    )[0]


def join_body(n, *refs):
    row = lax.axis_index("row")
    rows = refs[0].shape[0]
    for j in range(n):
        refs[n][pl.ds(pl.multiple_of((row ^ j) * rows, rows), rows), :] = refs[j][...]


def join(parts):
    rows, width = parts[0].shape
    return run(
        functools.partial(join_body, len(parts)),
        tuple(parts),
        [VMEM] * len(parts),
        [shape((rows * len(parts), width))],
    )[0]


def select_body(mine, other, first, second):
    core = lax.rem(lax.axis_index("col"), 2)
    first[...] = jnp.where(core == 0, mine[...].astype(F32), other[...].astype(F32))
    second[...] = jnp.where(core == 0, other[...].astype(F32), mine[...].astype(F32))


def select(mine, other):
    return run(select_body, (mine, other), [VMEM] * 2, [shape(mine.shape, F32)] * 2)


COST = {
    prepare_body: 36,
    forward_body: 36,
    backward_body: 36,
    grad_body: 36,
}


def per_device(features, degree, tile_vals, tile_slot, tile_count, w_first, w_second, cotangent):
    n_row, n_col = lax.axis_size("row"), lax.axis_size("col")
    line = n_col // 2
    piece, width = cotangent.shape
    tiles = tile_vals[0, 0]
    edge = tiles.shape[-1]
    local_cols = n_row * 2
    slots, count = tile_slot[0, 0], tile_count[0]

    def col_send(value, pairs):
        return lax.ppermute(
            value, "col", [(2 * a + k, 2 * b + k) for a, b in pairs for k in range(2)]
        )

    def line_flip(value, j):
        return col_send(value, [(a, a ^ j) for a in range(line)])

    def core_flip(value):
        return lax.ppermute(value, "col", [(a, a ^ 1) for a in range(n_col)])

    def row_flip(value, j):
        return lax.ppermute(value, "row", [(a, a ^ j) for a in range(n_row)])

    def scatter_line(own, after=()):
        if line != 4:
            parts = [own[0]] + [line_flip(own[j], j) for j in range(1, line)]
            return tree([x.astype(F32) for x in parts]), []
        inward = col_send(own[3], [(0, 1), (3, 2)])
        middle = col_send(own[3], [(1, 2), (2, 1)])
        near = line_flip(own[1], 1)
        part, message = onward(own[0], own[2], near, middle, inward, after)
        return part, [line_flip(message, 2)]

    def gather_near(own):
        if line != 4:
            return []
        return [line_flip(own, 1), col_send(own, [(1, 2), (2, 1)])]

    def gather_far(own, near, middle, after):
        (across,) = relay([col_send(near, [(1, 2), (2, 1)])], after)
        out_two = col_send(middle, [(1, 0), (2, 3)])
        out_three = col_send(across, [(1, 0), (2, 3)])
        return [own, near, *choose(line - 1, across, middle, out_two, out_three)]

    halves = piece // edge
    scale, scaled = scale_kernel(degree[:, 0], cotangent, edge)
    early = gather_near(scaled)
    values = features[:, 0].reshape(local_cols, edge, width)
    first_in, number, entries, t_number, t_entries = prepare(
        count, slots, values, scale, 2 * n_col
    )

    give = forward(number, entries, tiles, first_in, True, 1)
    keep = forward(number, entries, tiles, first_in, True, 0)
    if early:
        early = relay(early, (keep,))
    own = pair_sum(keep, core_flip(give))
    part, far = scatter_line(own)
    if early:
        gathered = gather_far(scaled, *early, (own[0],))
    else:
        gathered = [scaled] + [line_flip(scaled, j) for j in range(1, line)]
    ranged = [x for g in gathered for x in (g, core_flip(g))]
    hidden = backward(t_number, t_entries, tiles, ranged)
    agg = aggregate(part, far, scale)
    spread = [agg] + [row_flip(agg, j) for j in range(1, n_row)]
    stacked = first_layer(spread[:-1], scale, w_first)
    sums = weight_grads(0, hidden, *stacked, scale, w_first, w_second)
    aggs, outs = first_layer(spread[-1:], scale, w_first, stacked, sums[:1])

    give = forward(number, entries, tiles, outs, False, 1)
    keep = forward(number, entries, tiles, outs, False, 0)
    own = pair_sum(keep, core_flip(give))

    give, keep = weight_grads(
        2 * n_row - 2, hidden, aggs, outs, scale, w_first, w_second, sums, (own[0],)
    )
    part, far = scatter_line(own, (keep,))
    parts = split_sum(keep, core_flip(give), n_row, (part,))
    moment = sum_parts([parts[0]] + [row_flip(parts[j], j) for j in range(1, n_row)])
    moment = sum_parts([moment] + [line_flip(moment, j) for j in range(1, line)], far)
    mine = join([moment] + [row_flip(moment, j) for j in range(1, n_row)])
    grad_first, grad_second = select(mine, core_flip(mine))
    return second_layer(part, far, scale, w_second), grad_first, grad_second


def solution(mesh):
    return jax.shard_map(
        per_device,
        mesh=mesh,
        in_specs=(
            P(None, "col", None, None),
            P(None, "col", None),
            P("row", "col", None, None, None),
            P("row", "col", None),
            P("row", "col"),
            P(),
            P(),
            P(("row", "col"), None),
        ),
        out_specs=(P(("row", "col"), None), P(), P()),
        check_vma=False,
    )
```

time: 226 us -> 197 us (0.87)
  between operations: 15.1 us -> 1.63 us
  starting transfers between devices: 57.2 us -> 45.9 us
  local copies, waits for them, and re-layouts: 11.8 us -> 4.52 us
  waiting for transfers between devices: 102 us -> 109 us
  Pallas kernels: 38 us -> 34.4 us
    ppermute x12 -> x9, waiting for transfers between devices: 13.2 us -> 25.8 us  [row_flip(): return lax.ppermute(value, 'row', [(a, a ^ j) for a in range(n_row)])]
    unnamed x31 -> x13, local copies, waits for them, and re-layouts: 11.8 us -> 4.52 us
    ppermute x19 -> x16, starting transfers between devices: 39.8 us -> 33.8 us  [col_send(): lax.ppermute(value, 'col', [(2 * a + k, 2 * b + k) for a, b in pairs for...]
    ppermute x6 -> x8, waiting for transfers between devices: 7.59 us -> 2.25 us  [core_flip(): return lax.ppermute(value, 'col', [(a, a ^ 1) for a in range(n_col)])]
    ppermute x12 -> x9, starting transfers between devices: 15.5 us -> 10.7 us  [row_flip(): return lax.ppermute(value, 'row', [(a, a ^ j) for a in range(n_row)])]
    pallas_call x27 -> x25, Pallas kernels: 38 us -> 34.4 us  [run(): pl.pallas_call(whole, out_shape=outs, in_specs=specs + [ANY] * extra, out...]
    ppermute x19 -> x16, waiting for transfers between devices: 81.2 us -> 81 us  [col_send(): lax.ppermute(value, 'col', [(2 * a + k, 2 * b + k) for a, b in pairs for...]
  transfers between devices with their start and end apart: 38 -> 33, of which waited for: 18 -> 20; matrix products, arithmetic and copies ran while one was open for 0% -> 0% of each run, Pallas kernels for 8% -> 14%
where the time goes in v5:
time: 197 us; the launch traced here: 195 us
  waiting for transfers between devices  109 us (55%)
  starting transfers between devices  45.9 us (23%)
  Pallas kernels  34.4 us (17%)
  local copies, waits for them, and re-layouts  4.52 us (2%)
    ppermute x16, waiting for transfers between devices, col_send(): lax.ppermute(value, 'col', [(2 * a + k, 2 * b + k) for a, b in pairs for...  81 us
    pallas_call x25, Pallas kernels, run(): pl.pallas_call(whole, out_shape=outs, in_specs=specs + [ANY] * extra, out...  34.4 us
    ppermute x16, starting transfers between devices, col_send(): lax.ppermute(value, 'col', [(2 * a + k, 2 * b + k) for a, b in pairs for...  33.8 us
    ppermute x9, waiting for transfers between devices, row_flip(): return lax.ppermute(value, 'row', [(a, a ^ j) for a in range(n_row)])  25.8 us
    ppermute x9, starting transfers between devices, row_flip(): return lax.ppermute(value, 'row', [(a, a ^ j) for a in range(n_row)])  10.7 us
    unnamed x13, local copies, waits for them, and re-layouts  4.52 us
  transfers between devices with their start and end apart: 33, of which 20 were waited for; matrix products, arithmetic and copies ran while one was open for 0% of the time, Pallas kernels for 14%

profile of v5, /device:TPU:0, one launch (start us, length us, event | category | flops | bytes accessed | tf_op | source)
XLA Modules:
  0.0 195.5 jit_solution(3056780542867716166)
XLA Ops:
  0.6 0.7 copy.13
  1.3 1.0 copy-done.2
  2.4 0.6 shard_map.103
  2.9 0.7 collective-permute-start.10
  3.6 5.9 %collective-permute-start.9 = (bf16[2,512,256]{2,1,0:T(8,128)(2,1)S(1)}, bf16[2,512,256]{2,1,0:T(8,128)(2,1)S(1)}, u32[]{:S(2)}, u32[]{:S(2)}) collective-permute-start(bf16[2,512,256]{2,1,0:T(8,128)(2,1)S(1)} %get-tuple-element.54.refs_3_), channel_id=1, source_target_pairs={{0,2},{1,3},{2,0},{3,1},{4,6},{5,7},{6,4},{7,5},{8,10},{9,11},{10,... | collective-permute-start | bytes 1572872 | tf_op jit(solution)/shard_map/ppermute | solution.py:502
  10.2 1.6 copy-done.4
  11.8 0.7 copy-done.5
  12.4 2.2 %shard_map.104 = (bf16[8,256,512]{2,1,0:T(8,128)(2,1)S(1)}, s32[16]{0:T(128)S(1)}, s32[128]{0:T(128)S(1)}, s32[8]{0:T(128)S(1)}, s32[128]{0:T(128)S(1)}) custom-call(s32[1]{0:T(128)} %bitcast.7.refs_0_, s32[48]{0:T(128)S(1)} %bitcast.15, bf16[8,256,512]{2,1,0:T(8,128)(2,1)S(1)} %bitcast.14, f32[8,256,128]{2,1,0:T(8,128)S(1)} %get-tuple-element.40.refs_3_.refs_2_.refs_1_), custom_call_target="tpu_custom_call" | custom-call | flops 35999997952 | tf_op jit(solution)/shard_map/pallas_call | solution.py:24
  14.7 0.5 copy-done.3
  15.2 2.8 %shard_map.106 = bf16[8,256,512]{2,1,0:T(8,128)(2,1)S(1)} custom-call(s32[16]{0:T(128)S(1)} %get-tuple-element.41.refs_0_, s32[128]{0:T(128)S(1)} %get-tuple-element.42.refs_1_, bf16[48,256,256]{2,1,0:T(8,128)(2,1)S(1)} %bitcast.9, bf16[8,256,512]{2,1,0:T(8,128)(2,1)S(1)} %get-tuple-element.43.refs_3_), custom_call_target="tpu_custom_call" | custom-call | flops 35999997952 | tf_op jit(solution)/shard_map/pallas_call | solution.py:24
  18.1 2.9 %shard_map.105.refs_0_.refs_2_ = bf16[8,256,512]{2,1,0:T(8,128)(2,1)S(1)} custom-call(s32[16]{0:T(128)S(1)} %get-tuple-element.41.refs_0_, s32[128]{0:T(128)S(1)} %get-tuple-element.42.refs_1_, bf16[48,256,256]{2,1,0:T(8,128)(2,1)S(1)} %bitcast.10, bf16[8,256,512]{2,1,0:T(8,128)(2,1)S(1)} %get-tuple-element.43.refs_3_), custom_call_target="tpu_custom_call" | custom-call | flops 35999997952 | tf_op jit(solution)/shard_map/pallas_call | solution.py:24
  21.0 0.2 collective-permute-done.9.refs_0_
  21.2 0.7 collective-permute-start.12
  21.9 0.3 collective-permute-done.refs_1_
  22.3 0.5 shard_map.107
  22.7 0.7 collective-permute-start.2
  23.4 7.8 %collective-permute-start.3 = (bf16[2,256,512]{2,1,0:T(8,128)(2,1)S(1)}, bf16[2,256,512]{2,1,0:T(8,128)(2,1)S(1)}, u32[]{:S(2)}, u32[]{:S(2)}) collective-permute-start(bf16[2,256,512]{2,1,0:T(8,128)(2,1)S(1)} %get-tuple-element.47), channel_id=1, source_target_pairs={{0,2},{1,3},{6,4},{7,5},{8,10},{9,11},{14,12},{15,13},{16,18},{17,... | collective-permute-start | bytes 1572872 | tf_op jit(solution)/shard_map/ppermute | solution.py:502
  31.3 1.3 collective-permute-start.13
  32.7 1.5 collective-permute-start.14
  34.2 9.3 %collective-permute-done.3.refs_4_ = bf16[2,256,512]{2,1,0:T(8,128)(2,1)S(1)} collective-permute-done((bf16[2,256,512]{2,1,0:T(8,128)(2,1)S(1)}, bf16[2,256,512]{2,1,0:T(8,128)(2,1)S(1)}, u32[]{:S(2)}, u32[]{:S(2)}) %collective-permute-start.3) | collective-permute-done | bytes 524320 | tf_op jit(solution)/shard_map/ppermute | solution.py:502
  43.5 10.4 %collective-permute-done.1.refs_2_ = bf16[2,256,512]{2,1,0:T(8,128)(2,1)S(1)} collective-permute-done((bf16[2,256,512]{2,1,0:T(8,128)(2,1)S(1)}, bf16[2,256,512]{2,1,0:T(8,128)(2,1)S(1)}, u32[]{:S(2)}, u32[]{:S(2)}) %collective-permute-start.1) | collective-permute-done | bytes 524320 | tf_op jit(solution)/shard_map/ppermute | solution.py:502
  53.9 0.3 shard_map.108
  54.2 2.2 %collective-permute-start.4 = (bf16[2,256,512]{2,1,0:T(8,128)(2,1)S(1)}, bf16[2,256,512]{2,1,0:T(8,128)(2,1)S(1)}, u32[]{:S(2)}, u32[]{:S(2)}) collective-permute-start(bf16[2,256,512]{2,1,0:T(8,128)(2,1)S(1)} %get-tuple-element.49), channel_id=1, source_target_pairs={{0,4},{1,5},{2,6},{3,7},{4,0},{5,1},{6,2},{7,3},{8,12},{9,13},{10,... | collective-permute-start | bytes 1572872 | tf_op jit(solution)/shard_map/ppermute | solution.py:502
  56.5 0.5 collective-permute-start.11
  57.0 2.3 %collective-permute-done.13.refs_2_ = bf16[2,512,256]{2,1,0:T(8,128)(2,1)S(1)} collective-permute-done((bf16[2,512,256]{2,1,0:T(8,128)(2,1)S(1)}, bf16[2,512,256]{2,1,0:T(8,128)(2,1)S(1)}, u32[]{:S(2)}, u32[]{:S(2)}) %collective-permute-start.13) | collective-permute-done | bytes 524320 | tf_op jit(solution)/shard_map/ppermute | solution.py:502
  59.3 10.1 %collective-permute-done.14.refs_3_ = bf16[2,512,256]{2,1,0:T(8,128)(2,1)S(1)} collective-permute-done((bf16[2,512,256]{2,1,0:T(8,128)(2,1)S(1)}, bf16[2,512,256]{2,1,0:T(8,128)(2,1)S(1)}, u32[]{:S(2)}, u32[]{:S(2)}) %collective-permute-start.14) | collective-permute-done | bytes 524320 | tf_op jit(solution)/shard_map/ppermute | solution.py:502
  69.7 0.5 collective-permute-start.16
  70.2 9.5 %collective-permute-done.4.refs_1_ = bf16[2,256,512]{2,1,0:T(8,128)(2,1)S(1)} collective-permute-done((bf16[2,256,512]{2,1,0:T(8,128)(2,1)S(1)}, bf16[2,256,512]{2,1,0:T(8,128)(2,1)S(1)}, u32[]{:S(2)}, u32[]{:S(2)}) %collective-permute-start.4) | collective-permute-done | bytes 524320 | tf_op jit(solution)/shard_map/ppermute | solution.py:502
  79.6 0.1 shard_map.109.refs_0_
  79.8 0.8 collective-permute-start.6
  80.6 0.7 collective-permute-start.7
  81.3 2.1 %collective-permute-start.5 = (bf16[2,256,512]{2,1,0:T(8,128)(2,1)S(1)}, bf16[2,256,512]{2,1,0:T(8,128)(2,1)S(1)}, u32[]{:S(2)}, u32[]{:S(2)}) collective-permute-start(bf16[2,256,512]{2,1,0:T(8,128)(2,1)S(1)} %shard_map.109.refs_0_), channel_id=1, source_target_pairs={{0,24},{8,16},{16,8},{24,0},{1,25},{9,17},{17,9},{25,1},{2,26},{10... | collective-permute-start | bytes 1572872 | tf_op jit(solution)/shard_map/ppermute | solution.py:513
  83.3 4.2 %shard_map.114.refs_0_ = bf16[8,512,256]{2,1,0:T(8,128)(2,1)S(1)} custom-call(s32[8]{0:T(128)S(1)} %get-tuple-element.52.refs_0_, s32[128]{0:T(128)S(1)} %get-tuple-element.53.refs_1_, bf16[48,256,256]{2,1,0:T(8,128)(2,1)S(1)} %bitcast.11, bf16[2,512,256]{2,1,0:T(8,128)(2,1)S(1)} %get-tuple-element.54.refs_3_, ...), custom_call_target="tpu_custom_call" | custom-call | flops 35999997952 | tf_op jit(solution)/shard_map/pallas_call | solution.py:24
  87.5 7.2 %collective-permute-done.6.refs_1_ = bf16[2,256,512]{2,1,0:T(8,128)(2,1)S(1)} collective-permute-done((bf16[2,256,512]{2,1,0:T(8,128)(2,1)S(1)}, bf16[2,256,512]{2,1,0:T(8,128)(2,1)S(1)}, u32[]{:S(2)}, u32[]{:S(2)}) %collective-permute-start.6) | collective-permute-done | bytes 524320 | tf_op jit(solution)/shard_map/ppermute | solution.py:513
  94.7 10.0 %collective-permute-done.7.refs_2_ = bf16[2,256,512]{2,1,0:T(8,128)(2,1)S(1)} collective-permute-done((bf16[2,256,512]{2,1,0:T(8,128)(2,1)S(1)}, bf16[2,256,512]{2,1,0:T(8,128)(2,1)S(1)}, u32[]{:S(2)}, u32[]{:S(2)}) %collective-permute-start.7) | collective-permute-done | bytes 524320 | tf_op jit(solution)/shard_map/ppermute | solution.py:513
  104.7 1.5 shard_map.110
  106.2 6.4 %shard_map.115 = (f32[512,512]{1,0:T(8,128)S(1)}, f32[512,512]{1,0:T(8,128)S(1)}) custom-call(bf16[8,512,256]{2,1,0:T(8,128)(2,1)S(1)} %shard_map.114.refs_0_, bf16[6,256,512]{2,1,0:T(8,128)(2,1)S(1)} %get-tuple-element.50.refs_1_.refs_3_, bf16[6,256,512]{2,1,0:T(8,128)(2,1)S(1)} %get-tuple-element.51.refs_2_.refs_4_, ...), custom_call_target="tpu_custom_call" | custom-call | flops 35999997952 | tf_op jit(solution)/shard_map/pallas_call | solution.py:24
  112.6 0.9 shard_map.116
  113.5 2.8 %shard_map.118 = bf16[8,256,512]{2,1,0:T(8,128)(2,1)S(1)} custom-call(s32[16]{0:T(128)S(1)} %get-tuple-element.41.refs_0_, s32[128]{0:T(128)S(1)} %get-tuple-element.42.refs_1_, bf16[48,256,256]{2,1,0:T(8,128)(2,1)S(1)} %bitcast.12, bf16[8,256,512]{2,1,0:T(8,128)(2,1)S(1)} %get-tuple-element.60.refs_3_.refs_2_), custom_call_target="tpu_custom_call" | custom-call | flops 35999997952 | tf_op jit(solution)/shard_map/pallas_call | solution.py:24
  116.4 2.9 %shard_map.117.refs_0_ = bf16[8,256,512]{2,1,0:T(8,128)(2,1)S(1)} custom-call(s32[16]{0:T(128)S(1)} %get-tuple-element.41.refs_0_, s32[128]{0:T(128)S(1)} %get-tuple-element.42.refs_1_, bf16[48,256,256]{2,1,0:T(8,128)(2,1)S(1)} %bitcast.13, bf16[8,256,512]{2,1,0:T(8,128)(2,1)S(1)} %get-tuple-element.60.refs_3_.refs_2_), custom_call_target="tpu_custom_call" | custom-call | flops 35999997952 | tf_op jit(solution)/shard_map/pallas_call | solution.py:24
  119.3 1.3 collective-permute-done.17.refs_1_
  120.6 0.5 shard_map.119
  121.1 0.7 collective-permute-start.19
  121.8 4.2 %collective-permute-start.20 = (bf16[2,256,512]{2,1,0:T(8,128)(2,1)S(1)}, bf16[2,256,512]{2,1,0:T(8,128)(2,1)S(1)}, u32[]{:S(2)}, u32[]{:S(2)}) collective-permute-start(bf16[2,256,512]{2,1,0:T(8,128)(2,1)S(1)} %get-tuple-element.64), channel_id=1, source_target_pairs={{0,2},{1,3},{6,4},{7,5},{8,10},{9,11},{14,12},{15,13},{16,18},{17,... | collective-permute-start | bytes 1572872 | tf_op jit(solution)/shard_map/ppermute | solution.py:502
  126.0 2.4 %shard_map.120 = (bf16[512,512]{1,0:T(8,128)(2,1)S(1)}, bf16[512,512]{1,0:T(8,128)(2,1)S(1)}) custom-call(bf16[8,512,256]{2,1,0:T(8,128)(2,1)S(1)} %shard_map.114.refs_0_, bf16[8,256,512]{2,1,0:T(8,128)(2,1)S(1)} %get-tuple-element.65.refs_1_, bf16[8,256,512]{2,1,0:T(8,128)(2,1)S(1)} %get-tuple-element.60.refs_3_.refs_2_, ...), custom_call_target="tpu_custom_call" | custom-call | flops 35999997952 | tf_op jit(solution)/shard_map/pallas_call | solution.py:24
  128.5 19.6 %collective-permute-done.18.refs_2_ = bf16[2,256,512]{2,1,0:T(8,128)(2,1)S(1)} collective-permute-done((bf16[2,256,512]{2,1,0:T(8,128)(2,1)S(1)}, bf16[2,256,512]{2,1,0:T(8,128)(2,1)S(1)}, u32[]{:S(2)}, u32[]{:S(2)}) %collective-permute-start.18) | collective-permute-done | bytes 524320 | tf_op jit(solution)/shard_map/ppermute | solution.py:502
  148.2 0.3 shard_map.121
  148.4 3.6 %collective-permute-start.21 = (bf16[2,256,512]{2,1,0:T(8,128)(2,1)S(1)}, bf16[2,256,512]{2,1,0:T(8,128)(2,1)S(1)}, u32[]{:S(2)}, u32[]{:S(2)}) collective-permute-start(bf16[2,256,512]{2,1,0:T(8,128)(2,1)S(1)} %get-tuple-element.69), channel_id=1, source_target_pairs={{0,4},{1,5},{2,6},{3,7},{4,0},{5,1},{6,2},{7,3},{8,12},{9,13},{10,... | collective-permute-start | bytes 1572872 | tf_op jit(solution)/shard_map/ppermute | solution.py:502
  152.3 1.8 collective-permute-start.24
  154.0 1.7 collective-permute-start.25
  155.7 2.7 %collective-permute-done.23.refs_1_ = bf16[128,512]{1,0:T(8,128)(2,1)S(1)} collective-permute-done((bf16[128,512]{1,0:T(8,128)(2,1)S(1)}, bf16[128,512]{1,0:T(8,128)(2,1)S(1)}, u32[]{:S(2)}, u32[]{:S(2)}) %collective-permute-start.23) | collective-permute-done | bytes 131104 | tf_op jit(solution)/shard_map/ppermute | solution.py:513
  158.5 1.4 collective-permute-done.25.refs_3_
  160.0 2.3 %collective-permute-start.27 = (bf16[128,512]{1,0:T(8,128)(2,1)S(1)}, bf16[128,512]{1,0:T(8,128)(2,1)S(1)}, u32[]{:S(2)}, u32[]{:S(2)}) collective-permute-start(bf16[128,512]{1,0:T(8,128)(2,1)S(1)} %shard_map.124.refs_0_), channel_id=1, source_target_pairs={{0,4},{1,5},{2,6},{3,7},{4,0},{5,1},{6,2},{7,3},{8,12},{9,13},{10,... | collective-permute-start | bytes 393224 | tf_op jit(solution)/shard_map/ppermute | solution.py:502
  162.3 2.1 %collective-permute-start.28 = (bf16[128,512]{1,0:T(8,128)(2,1)S(1)}, bf16[128,512]{1,0:T(8,128)(2,1)S(1)}, u32[]{:S(2)}, u32[]{:S(2)}) collective-permute-start(bf16[128,512]{1,0:T(8,128)(2,1)S(1)} %shard_map.124.refs_0_), channel_id=1, source_target_pairs={{0,6},{1,7},{2,4},{3,5},{4,2},{5,3},{6,0},{7,1},{8,14},{9,15},{10,... | collective-permute-start | bytes 393224 | tf_op jit(solution)/shard_map/ppermute | solution.py:502
  164.4 2.8 %collective-permute-done.26.refs_1_ = bf16[128,512]{1,0:T(8,128)(2,1)S(1)} collective-permute-done((bf16[128,512]{1,0:T(8,128)(2,1)S(1)}, bf16[128,512]{1,0:T(8,128)(2,1)S(1)}, u32[]{:S(2)}, u32[]{:S(2)}) %collective-permute-start.26) | collective-permute-done | bytes 131104 | tf_op jit(solution)/shard_map/ppermute | solution.py:502
  167.2 16.7 %collective-permute-done.27.refs_2_ = bf16[128,512]{1,0:T(8,128)(2,1)S(1)} collective-permute-done((bf16[128,512]{1,0:T(8,128)(2,1)S(1)}, bf16[128,512]{1,0:T(8,128)(2,1)S(1)}, u32[]{:S(2)}, u32[]{:S(2)}) %collective-permute-start.27) | collective-permute-done | bytes 131104 | tf_op jit(solution)/shard_map/ppermute | solution.py:502
  184.0 0.2 collective-permute-start.29
  184.3 1.9 collective-permute-start.30
  186.1 1.5 collective-permute-start.31
  187.6 2.4 %collective-permute-done.29.refs_1_ = bf16[128,512]{1,0:T(8,128)(2,1)S(1)} collective-permute-done((bf16[128,512]{1,0:T(8,128)(2,1)S(1)}, bf16[128,512]{1,0:T(8,128)(2,1)S(1)}, u32[]{:S(2)}, u32[]{:S(2)}) %collective-permute-start.29) | collective-permute-done | bytes 131104 | tf_op jit(solution)/shard_map/ppermute | solution.py:513
  190.1 1.9 collective-permute-done.31.refs_3_
  192.1 1.3 shard_map.122
  193.4 0.6 collective-permute-done.32.refs_1_
  194.0 1.5 shard_map.127
  (40 shorter events, 1.4 us)
Async XLA Ops:
  1.3 1.0 copy-start.2
  2.9 18.1 %collective-permute-start.10 = (bf16[2,512,256]{2,1,0:T(8,128)(2,1)S(1)}, bf16[2,512,256]{2,1,0:T(8,128)(2,1)S(1)}, u32[]{:S(2)}, u32[]{:S(2)}) collective-permute-start(bf16[2,512,256]{2,1,0:T(8,128)(2,1)S(1)} %get-tuple-element.54.refs_3_), channel_id=1, source_target_pairs={{2,4},{3,5},{4,2},{5,3},{10,12},{11,13},{12,10},{13,11},{18,20},{1... | collective-permute-start | bytes 1572872 | tf_op jit(solution)/shard_map/ppermute | solution.py:502
  3.6 17.5 %collective-permute-start.9 = (bf16[2,512,256]{2,1,0:T(8,128)(2,1)S(1)}, bf16[2,512,256]{2,1,0:T(8,128)(2,1)S(1)}, u32[]{:S(2)}, u32[]{:S(2)}) collective-permute-start(bf16[2,512,256]{2,1,0:T(8,128)(2,1)S(1)} %get-tuple-element.54.refs_3_), channel_id=1, source_target_pairs={{0,2},{1,3},{2,0},{3,1},{4,6},{5,7},{6,4},{7,5},{8,10},{9,11},{10,... | collective-permute-start | bytes 1572872 | tf_op jit(solution)/shard_map/ppermute | solution.py:502
  10.2 1.6 copy-start.4
  11.8 0.7 copy-start.5
  12.4 2.8 %copy-start.3 = (bf16[1,1,48,256,256]{4,3,2,1,0:T(8,128)(2,1)S(1)}, bf16[1,1,48,256,256]{4,3,2,1,0:T(8,128)(2,1)}, u32[]{:S(2)}) copy-start(bf16[1,1,48,256,256]{4,3,2,1,0:T(8,128)(2,1)} %param.10) | copy-start | bytes 18874372
  18.0 4.2 %collective-permute-start = (bf16[8,256,512]{2,1,0:T(8,128)(2,1)S(1)}, bf16[8,256,512]{2,1,0:T(8,128)(2,1)S(1)}, u32[]{:S(2)}, u32[]{:S(2)}) collective-permute-start(bf16[8,256,512]{2,1,0:T(8,128)(2,1)S(1)} %shard_map.106), channel_id=1, source_target_pairs={{0,1},{1,0},{2,3},{3,2},{4,5},{5,4},{6,7},{7,6},{8,9},{9,8},{10,11... | collective-permute-start | bytes 6291464 | tf_op jit(solution)/shard_map/ppermute | solution.py:510
  21.2 11.4 %collective-permute-start.12 = (bf16[2,512,256]{2,1,0:T(8,128)(2,1)S(1)}, bf16[2,512,256]{2,1,0:T(8,128)(2,1)S(1)}, u32[]{:S(2)}, u32[]{:S(2)}) collective-permute-start(bf16[2,512,256]{2,1,0:T(8,128)(2,1)S(1)} %get-tuple-element.55.refs_5_), channel_id=1, source_target_pairs={{2,4},{3,5},{4,2},{5,3},{10,12},{11,13},{12,10},{13,11},{18,20},{1... | collective-permute-start | bytes 1572872 | tf_op jit(solution)/shard_map/ppermute | solution.py:502
  22.7 11.4 %collective-permute-start.2 = (bf16[2,256,512]{2,1,0:T(8,128)(2,1)S(1)}, bf16[2,256,512]{2,1,0:T(8,128)(2,1)S(1)}, u32[]{:S(2)}, u32[]{:S(2)}) collective-permute-start(bf16[2,256,512]{2,1,0:T(8,128)(2,1)S(1)} %get-tuple-element.47), channel_id=1, source_target_pairs={{2,4},{3,5},{4,2},{5,3},{10,12},{11,13},{12,10},{13,11},{18,20},{1... | collective-permute-start | bytes 1572872 | tf_op jit(solution)/shard_map/ppermute | solution.py:502
  23.4 20.1 %collective-permute-start.3 = (bf16[2,256,512]{2,1,0:T(8,128)(2,1)S(1)}, bf16[2,256,512]{2,1,0:T(8,128)(2,1)S(1)}, u32[]{:S(2)}, u32[]{:S(2)}) collective-permute-start(bf16[2,256,512]{2,1,0:T(8,128)(2,1)S(1)} %get-tuple-element.47), channel_id=1, source_target_pairs={{0,2},{1,3},{6,4},{7,5},{8,10},{9,11},{14,12},{15,13},{16,18},{17,... | collective-permute-start | bytes 1572872 | tf_op jit(solution)/shard_map/ppermute | solution.py:502
  31.3 22.7 %collective-permute-start.1 = (bf16[2,256,512]{2,1,0:T(8,128)(2,1)S(1)}, bf16[2,256,512]{2,1,0:T(8,128)(2,1)S(1)}, u32[]{:S(2)}, u32[]{:S(2)}) collective-permute-start(bf16[2,256,512]{2,1,0:T(8,128)(2,1)S(1)} %get-tuple-element.46), channel_id=1, source_target_pairs={{0,2},{1,3},{2,0},{3,1},{4,6},{5,7},{6,4},{7,5},{8,10},{9,11},{10,... | collective-permute-start | bytes 1572872 | tf_op jit(solution)/shard_map/ppermute | solution.py:502
  31.3 28.0 %collective-permute-start.13 = (bf16[2,512,256]{2,1,0:T(8,128)(2,1)S(1)}, bf16[2,512,256]{2,1,0:T(8,128)(2,1)S(1)}, u32[]{:S(2)}, u32[]{:S(2)}) collective-permute-start(bf16[2,512,256]{2,1,0:T(8,128)(2,1)S(1)} %get-tuple-element.56.refs_1_), channel_id=1, source_target_pairs={{2,0},{3,1},{4,6},{5,7},{10,8},{11,9},{12,14},{13,15},{18,16},{19,... | collective-permute-start | bytes 1572872 | tf_op jit(solution)/shard_map/ppermute | solution.py:502
  32.7 36.8 %collective-permute-start.14 = (bf16[2,512,256]{2,1,0:T(8,128)(2,1)S(1)}, bf16[2,512,256]{2,1,0:T(8,128)(2,1)S(1)}, u32[]{:S(2)}, u32[]{:S(2)}) collective-permute-start(bf16[2,512,256]{2,1,0:T(8,128)(2,1)S(1)} %shard_map.112.refs_0_), channel_id=1, source_target_pairs={{2,0},{3,1},{4,6},{5,7},{10,8},{11,9},{12,14},{13,15},{18,16},{19,... | collective-permute-start | bytes 1572872 | tf_op jit(solution)/shard_map/ppermute | solution.py:502
  54.2 25.4 %collective-permute-start.4 = (bf16[2,256,512]{2,1,0:T(8,128)(2,1)S(1)}, bf16[2,256,512]{2,1,0:T(8,128)(2,1)S(1)}, u32[]{:S(2)}, u32[]{:S(2)}) collective-permute-start(bf16[2,256,512]{2,1,0:T(8,128)(2,1)S(1)} %get-tuple-element.49), channel_id=1, source_target_pairs={{0,4},{1,5},{2,6},{3,7},{4,0},{5,1},{6,2},{7,3},{8,12},{9,13},{10,... | collective-permute-start | bytes 1572872 | tf_op jit(solution)/shard_map/ppermute | solution.py:502
  56.5 24.1 %collective-permute-start.8 = (bf16[2,512,256]{2,1,0:T(8,128)(2,1)S(1)}, bf16[2,512,256]{2,1,0:T(8,128)(2,1)S(1)}, u32[]{:S(2)}, u32[]{:S(2)}) collective-permute-start(bf16[2,512,256]{2,1,0:T(8,128)(2,1)S(1)} %get-tuple-element.54.refs_3_), channel_id=1, source_target_pairs={{0,1},{1,0},{2,3},{3,2},{4,5},{5,4},{6,7},{7,6},{8,9},{9,8},{10,11... | collective-permute-start | bytes 1572872 | tf_op jit(solution)/shard_map/ppermute | solution.py:510
  56.5 24.8 %collective-permute-start.11 = (bf16[2,512,256]{2,1,0:T(8,128)(2,1)S(1)}, bf16[2,512,256]{2,1,0:T(8,128)(2,1)S(1)}, u32[]{:S(2)}, u32[]{:S(2)}) collective-permute-start(bf16[2,512,256]{2,1,0:T(8,128)(2,1)S(1)} %get-tuple-element.55.refs_5_), channel_id=1, source_target_pairs={{0,1},{1,0},{2,3},{3,2},{4,5},{5,4},{6,7},{7,6},{8,9},{9,8},{10,11... | collective-permute-start | bytes 1572872 | tf_op jit(solution)/shard_map/ppermute | solution.py:510
  69.6 13.7 %collective-permute-start.15 = (bf16[2,512,256]{2,1,0:T(8,128)(2,1)S(1)}, bf16[2,512,256]{2,1,0:T(8,128)(2,1)S(1)}, u32[]{:S(2)}, u32[]{:S(2)}) collective-permute-start(bf16[2,512,256]{2,1,0:T(8,128)(2,1)S(1)} %get-tuple-element.57.refs_7_), channel_id=1, source_target_pairs={{0,1},{1,0},{2,3},{3,2},{4,5},{5,4},{6,7},{7,6},{8,9},{9,8},{10,11... | collective-permute-start | bytes 1572872 | tf_op jit(solution)/shard_map/ppermute | solution.py:510
  69.7 13.7 %collective-permute-start.16 = (bf16[2,512,256]{2,1,0:T(8,128)(2,1)S(1)}, bf16[2,512,256]{2,1,0:T(8,128)(2,1)S(1)}, u32[]{:S(2)}, u32[]{:S(2)}) collective-permute-start(bf16[2,512,256]{2,1,0:T(8,128)(2,1)S(1)} %get-tuple-element.58.refs_9_), channel_id=1, source_target_pairs={{0,1},{1,0},{2,3},{3,2},{4,5},{5,4},{6,7},{7,6},{8,9},{9,8},{10,11... | collective-permute-start | bytes 1572872 | tf_op jit(solution)/shard_map/ppermute | solution.py:510
  79.8 14.9 %collective-permute-start.6 = (bf16[2,256,512]{2,1,0:T(8,128)(2,1)S(1)}, bf16[2,256,512]{2,1,0:T(8,128)(2,1)S(1)}, u32[]{:S(2)}, u32[]{:S(2)}) collective-permute-start(bf16[2,256,512]{2,1,0:T(8,128)(2,1)S(1)} %shard_map.109.refs_0_), channel_id=1, source_target_pairs={{0,8},{8,0},{16,24},{24,16},{1,9},{9,1},{17,25},{25,17},{2,10},{10... | collective-permute-start | bytes 1572872 | tf_op jit(solution)/shard_map/ppermute | solution.py:513
  80.6 24.1 %collective-permute-start.7 = (bf16[2,256,512]{2,1,0:T(8,128)(2,1)S(1)}, bf16[2,256,512]{2,1,0:T(8,128)(2,1)S(1)}, u32[]{:S(2)}, u32[]{:S(2)}) collective-permute-start(bf16[2,256,512]{2,1,0:T(8,128)(2,1)S(1)} %shard_map.109.refs_0_), channel_id=1, source_target_pairs={{0,16},{8,24},{16,0},{24,8},{1,17},{9,25},{17,1},{25,9},{2,18},{10... | collective-permute-start | bytes 1572872 | tf_op jit(solution)/shard_map/ppermute | solution.py:513
  81.3 31.4 %collective-permute-start.5 = (bf16[2,256,512]{2,1,0:T(8,128)(2,1)S(1)}, bf16[2,256,512]{2,1,0:T(8,128)(2,1)S(1)}, u32[]{:S(2)}, u32[]{:S(2)}) collective-permute-start(bf16[2,256,512]{2,1,0:T(8,128)(2,1)S(1)} %shard_map.109.refs_0_), channel_id=1, source_target_pairs={{0,24},{8,16},{16,8},{24,0},{1,25},{9,17},{17,9},{25,1},{2,26},{10... | collective-permute-start | bytes 1572872 | tf_op jit(solution)/shard_map/ppermute | solution.py:513
  83.3 21.4 %copy-start = (bf16[512,512]{1,0:T(8,128)(2,1)S(1)}, bf16[512,512]{1,0:T(8,128)(2,1)}, u32[]{:S(2)}) copy-start(bf16[512,512]{1,0:T(8,128)(2,1)} %refs_4_.5) | copy-start | bytes 1572868
  87.5 18.7 %copy-start.1 = (bf16[512,512]{1,0:T(8,128)(2,1)S(1)}, bf16[512,512]{1,0:T(8,128)(2,1)}, u32[]{:S(2)}) copy-start(bf16[512,512]{1,0:T(8,128)(2,1)} %refs_3_.1) | copy-start | bytes 1572868
  116.4 4.2 %collective-permute-start.17 = (bf16[8,256,512]{2,1,0:T(8,128)(2,1)S(1)}, bf16[8,256,512]{2,1,0:T(8,128)(2,1)S(1)}, u32[]{:S(2)}, u32[]{:S(2)}) collective-permute-start(bf16[8,256,512]{2,1,0:T(8,128)(2,1)S(1)} %shard_map.118), channel_id=1, source_target_pairs={{0,1},{1,0},{2,3},{3,2},{4,5},{5,4},{6,7},{7,6},{8,9},{9,8},{10,11... | collective-permute-start | bytes 6291464 | tf_op jit(solution)/shard_map/ppermute | solution.py:510
  121.1 27.1 %collective-permute-start.19 = (bf16[2,256,512]{2,1,0:T(8,128)(2,1)S(1)}, bf16[2,256,512]{2,1,0:T(8,128)(2,1)S(1)}, u32[]{:S(2)}, u32[]{:S(2)}) collective-permute-start(bf16[2,256,512]{2,1,0:T(8,128)(2,1)S(1)} %get-tuple-element.64), channel_id=1, source_target_pairs={{2,4},{3,5},{4,2},{5,3},{10,12},{11,13},{12,10},{13,11},{18,20},{1... | collective-permute-start | bytes 1572872 | tf_op jit(solution)/shard_map/ppermute | solution.py:502
  121.8 26.4 %collective-permute-start.20 = (bf16[2,256,512]{2,1,0:T(8,128)(2,1)S(1)}, bf16[2,256,512]{2,1,0:T(8,128)(2,1)S(1)}, u32[]{:S(2)}, u32[]{:S(2)}) collective-permute-start(bf16[2,256,512]{2,1,0:T(8,128)(2,1)S(1)} %get-tuple-element.64), channel_id=1, source_target_pairs={{0,2},{1,3},{6,4},{7,5},{8,10},{9,11},{14,12},{15,13},{16,18},{17,... | collective-permute-start | bytes 1572872 | tf_op jit(solution)/shard_map/ppermute | solution.py:502
  125.9 22.2 %collective-permute-start.18 = (bf16[2,256,512]{2,1,0:T(8,128)(2,1)S(1)}, bf16[2,256,512]{2,1,0:T(8,128)(2,1)S(1)}, u32[]{:S(2)}, u32[]{:S(2)}) collective-permute-start(bf16[2,256,512]{2,1,0:T(8,128)(2,1)S(1)} %get-tuple-element.63), channel_id=1, source_target_pairs={{0,2},{1,3},{2,0},{3,1},{4,6},{5,7},{6,4},{7,5},{8,10},{9,11},{10,... | collective-permute-start | bytes 1572872 | tf_op jit(solution)/shard_map/ppermute | solution.py:502
  128.4 23.6 %collective-permute-start.22 = (bf16[512,512]{1,0:T(8,128)(2,1)S(1)}, bf16[512,512]{1,0:T(8,128)(2,1)S(1)}, u32[]{:S(2)}, u32[]{:S(2)}) collective-permute-start(bf16[512,512]{1,0:T(8,128)(2,1)S(1)} %get-tuple-element.70), channel_id=1, source_target_pairs={{0,1},{1,0},{2,3},{3,2},{4,5},{5,4},{6,7},{7,6},{8,9},{9,8},{10,11... | collective-permute-start | bytes 1572872 | tf_op jit(solution)/shard_map/ppermute | solution.py:510
  148.4 35.5 %collective-permute-start.21 = (bf16[2,256,512]{2,1,0:T(8,128)(2,1)S(1)}, bf16[2,256,512]{2,1,0:T(8,128)(2,1)S(1)}, u32[]{:S(2)}, u32[]{:S(2)}) collective-permute-start(bf16[2,256,512]{2,1,0:T(8,128)(2,1)S(1)} %get-tuple-element.69), channel_id=1, source_target_pairs={{0,4},{1,5},{2,6},{3,7},{4,0},{5,1},{6,2},{7,3},{8,12},{9,13},{10,... | collective-permute-start | bytes 1572872 | tf_op jit(solution)/shard_map/ppermute | solution.py:502
  152.2 6.2 %collective-permute-start.23 = (bf16[128,512]{1,0:T(8,128)(2,1)S(1)}, bf16[128,512]{1,0:T(8,128)(2,1)S(1)}, u32[]{:S(2)}, u32[]{:S(2)}) collective-permute-start(bf16[128,512]{1,0:T(8,128)(2,1)S(1)} %get-tuple-element.72), channel_id=1, source_target_pairs={{0,8},{8,0},{16,24},{24,16},{1,9},{9,1},{17,25},{25,17},{2,10},{10... | collective-permute-start | bytes 393224 | tf_op jit(solution)/shard_map/ppermute | solution.py:513
  152.3 6.2 %collective-permute-start.24 = (bf16[128,512]{1,0:T(8,128)(2,1)S(1)}, bf16[128,512]{1,0:T(8,128)(2,1)S(1)}, u32[]{:S(2)}, u32[]{:S(2)}) collective-permute-start(bf16[128,512]{1,0:T(8,128)(2,1)S(1)} %get-tuple-element.73), channel_id=1, source_target_pairs={{0,16},{8,24},{16,0},{24,8},{1,17},{9,25},{17,1},{25,9},{2,18},{10... | collective-permute-start | bytes 393224 | tf_op jit(solution)/shard_map/ppermute | solution.py:513
  154.0 5.9 %collective-permute-start.25 = (bf16[128,512]{1,0:T(8,128)(2,1)S(1)}, bf16[128,512]{1,0:T(8,128)(2,1)S(1)}, u32[]{:S(2)}, u32[]{:S(2)}) collective-permute-start(bf16[128,512]{1,0:T(8,128)(2,1)S(1)} %get-tuple-element.74), channel_id=1, source_target_pairs={{0,24},{8,16},{16,8},{24,0},{1,25},{9,17},{17,9},{25,1},{2,26},{10... | collective-permute-start | bytes 393224 | tf_op jit(solution)/shard_map/ppermute | solution.py:513
  160.0 7.2 %collective-permute-start.26 = (bf16[128,512]{1,0:T(8,128)(2,1)S(1)}, bf16[128,512]{1,0:T(8,128)(2,1)S(1)}, u32[]{:S(2)}, u32[]{:S(2)}) collective-permute-start(bf16[128,512]{1,0:T(8,128)(2,1)S(1)} %shard_map.124.refs_0_), channel_id=1, source_target_pairs={{0,2},{1,3},{2,0},{3,1},{4,6},{5,7},{6,4},{7,5},{8,10},{9,11},{10,... | collective-permute-start | bytes 393224 | tf_op jit(solution)/shard_map/ppermute | solution.py:502
  160.0 23.9 %collective-permute-start.27 = (bf16[128,512]{1,0:T(8,128)(2,1)S(1)}, bf16[128,512]{1,0:T(8,128)(2,1)S(1)}, u32[]{:S(2)}, u32[]{:S(2)}) collective-permute-start(bf16[128,512]{1,0:T(8,128)(2,1)S(1)} %shard_map.124.refs_0_), channel_id=1, source_target_pairs={{0,4},{1,5},{2,6},{3,7},{4,0},{5,1},{6,2},{7,3},{8,12},{9,13},{10,... | collective-permute-start | bytes 393224 | tf_op jit(solution)/shard_map/ppermute | solution.py:502
  162.3 21.6 %collective-permute-start.28 = (bf16[128,512]{1,0:T(8,128)(2,1)S(1)}, bf16[128,512]{1,0:T(8,128)(2,1)S(1)}, u32[]{:S(2)}, u32[]{:S(2)}) collective-permute-start(bf16[128,512]{1,0:T(8,128)(2,1)S(1)} %shard_map.124.refs_0_), channel_id=1, source_target_pairs={{0,6},{1,7},{2,4},{3,5},{4,2},{5,3},{6,0},{7,1},{8,14},{9,15},{10,... | collective-permute-start | bytes 393224 | tf_op jit(solution)/shard_map/ppermute | solution.py:502
  184.0 6.0 %collective-permute-start.29 = (bf16[128,512]{1,0:T(8,128)(2,1)S(1)}, bf16[128,512]{1,0:T(8,128)(2,1)S(1)}, u32[]{:S(2)}, u32[]{:S(2)}) collective-permute-start(bf16[128,512]{1,0:T(8,128)(2,1)S(1)} %shard_map.125.refs_0_), channel_id=1, source_target_pairs={{0,8},{8,0},{16,24},{24,16},{1,9},{9,1},{17,25},{25,17},{2,10},{10... | collective-permute-start | bytes 393224 | tf_op jit(solution)/shard_map/ppermute | solution.py:513
  184.3 5.8 %collective-permute-start.30 = (bf16[128,512]{1,0:T(8,128)(2,1)S(1)}, bf16[128,512]{1,0:T(8,128)(2,1)S(1)}, u32[]{:S(2)}, u32[]{:S(2)}) collective-permute-start(bf16[128,512]{1,0:T(8,128)(2,1)S(1)} %shard_map.125.refs_0_), channel_id=1, source_target_pairs={{0,16},{8,24},{16,0},{24,8},{1,17},{9,25},{17,1},{25,9},{2,18},{10... | collective-permute-start | bytes 393224 | tf_op jit(solution)/shard_map/ppermute | solution.py:513
  186.1 5.9 %collective-permute-start.31 = (bf16[128,512]{1,0:T(8,128)(2,1)S(1)}, bf16[128,512]{1,0:T(8,128)(2,1)S(1)}, u32[]{:S(2)}, u32[]{:S(2)}) collective-permute-start(bf16[128,512]{1,0:T(8,128)(2,1)S(1)} %shard_map.125.refs_0_), channel_id=1, source_target_pairs={{0,24},{8,16},{16,8},{24,0},{1,25},{9,17},{17,9},{25,1},{2,26},{10... | collective-permute-start | bytes 393224 | tf_op jit(solution)/shard_map/ppermute | solution.py:513
  192.0 2.0 %collective-permute-start.32 = (bf16[512,512]{1,0:T(8,128)(2,1)S(1)}, bf16[512,512]{1,0:T(8,128)(2,1)S(1)}, u32[]{:S(2)}, u32[]{:S(2)}) collective-permute-start(bf16[512,512]{1,0:T(8,128)(2,1)S(1)} %shard_map.126.refs_0_), channel_id=1, source_target_pairs={{0,1},{1,0},{2,3},{3,2},{4,5},{5,4},{6,7},{7,6},{8,9},{9,8},{10,11... | collective-permute-start | bytes 1572872 | tf_op jit(solution)/shard_map/ppermute | solution.py:510

commit v6 on v5

--- a/solution.py
+++ b/solution.py
@@ -251,24 +251,9 @@
 
 def tree(items):
     while len(items) > 1:
-        items = [a + b for a, b in zip(items[::2], items[1::2])]
+        rest = items[len(items) // 2 * 2 :]
+        items = [a + b for a, b in zip(items[::2], items[1::2])] + rest
     return items[0]
-
-
-def onward_body(own, far, near, middle, inward, part, message):
-    part[...] = own[...].astype(F32) + near[...].astype(F32) + middle[...].astype(F32)
-    message[...] = (far[...].astype(F32) + inward[...].astype(F32)).astype(BF16)
-
-
-def onward(own, far, near, middle, inward, after):
-    return run(
-        onward_body,
-        (own, far, near, middle, inward),
-        [VMEM] * 5,
-        [shape(own.shape, F32), shape(own.shape)],
-        mib=12,
-        after=after,
-    )
 
 
 def relay_body(n, *refs):
@@ -302,38 +287,35 @@
     )
 
 
-def agg_body(part, *refs):
-    scale, out = refs[-2:]
-    for half in range(2):
-        summed = part[half]
-        for x in refs[:-2]:
-            summed = summed + x[half].astype(F32)
+def agg_body(n, *refs):
+    scale, outs = refs[n], refs[n + 1 :]
+    for half, out in enumerate(outs):
+        summed = tree([x[half].astype(F32) for x in refs[:n]])
         wide = repeat_lanes(scale[lax.axis_index("row") * 2 + half], summed.shape[1])
-        out[half] = (summed * wide).astype(BF16)
-
-
-def aggregate(part, far, scale):
-    return run(
-        agg_body,
-        (part, *far, scale),
-        [VMEM] * (2 + len(far)),
-        [shape(part.shape)],
-    )[0]
+        out[...] = (summed * wide).astype(BF16)
+
+
+def aggregate(parts, scale):
+    return run(
+        functools.partial(agg_body, len(parts)),
+        (*parts, scale),
+        [VMEM] * (len(parts) + 1),
+        [shape(parts[0].shape[1:])] * 2,
+    )
 
 
 def first_body(start, n, *refs):
-    scale, weight, agg, out = refs[n], refs[n + 1], refs[-2], refs[-1]
+    scale, weight, agg, out = refs[2 * n], refs[2 * n + 1], refs[-2], refs[-1]
     row = lax.axis_index("row")
     if start:
-        agg[: 2 * start] = refs[n + 2][...]
-        out[: 2 * start] = refs[n + 3][...]
-    for i in range(n):
-        j = start + i
-        for half in range(2):
-            value = jnp.dot(refs[i][half], weight[...], preferred_element_type=F32)
-            wide = repeat_lanes(scale[(row ^ j) * 2 + half], value.shape[1])
-            out[2 * j + half] = (jax.nn.gelu(value) * wide).astype(BF16)
-            agg[2 * j + half] = refs[i][half]
+        agg[: 2 * start] = refs[2 * n + 2][...]
+        out[: 2 * start] = refs[2 * n + 3][...]
+    for i in range(2 * n):
+        block = 2 * start + i
+        value = jnp.dot(refs[i][...], weight[...], preferred_element_type=F32)
+        wide = repeat_lanes(scale[block ^ (2 * row)], value.shape[1])
+        out[block] = (jax.nn.gelu(value) * wide).astype(BF16)
+        agg[block] = refs[i][...]
 
 
 def first_layer(aggs, scale, weight, before=(), after=()):
@@ -341,33 +323,31 @@
     start = before[0].shape[0] // 2 if before else 0
     return run(
         functools.partial(first_body, start, n),
-        (*aggs, scale, weight, *before),
-        [VMEM] * (n + 2 + len(before)),
-        [shape((2 * (start + n), *aggs[0].shape[1:]))] * 2,
+        (*[x for pair in aggs for x in pair], scale, weight, *before),
+        [VMEM] * (2 * n + 2 + len(before)),
+        [shape((2 * (start + n), *aggs[0][0].shape))] * 2,
         mib=14,
         after=after,
     )
 
 
-def second_body(part, *refs):
+def second_body(*refs):
     scale, weight, out = refs[-3:]
-    edge = part.shape[1]
+    edge = refs[0].shape[1]
     for half in range(2):
-        summed = part[half]
-        for x in refs[:-3]:
-            summed = summed + x[half].astype(F32)
+        summed = tree([x[half].astype(F32) for x in refs[:-3]])
         wide = repeat_lanes(scale[lax.axis_index("row") * 2 + half], summed.shape[1])
         agg = (summed * wide).astype(BF16)
         value = jnp.dot(agg, weight[...], preferred_element_type=F32)
         out[half * edge : (half + 1) * edge, :] = value.astype(BF16)
 
 
-def second_layer(part, far, scale, weight):
-    halves, edge, width = part.shape
+def second_layer(parts, scale, weight):
+    halves, edge, width = parts[0].shape
     return run(
         second_body,
-        (part, *far, scale, weight),
-        [VMEM] * (3 + len(far)),
+        (*parts, scale, weight),
+        [VMEM] * (2 + len(parts)),
         [shape((halves * edge, width))],
     )[0]
 
@@ -421,20 +401,26 @@
     )
 
 
-def split_body(n, keep, come, *outs):
-    row = lax.axis_index("row")
-    rows = keep.shape[0] // n
+def position(axis):
+    if axis == "row":
+        return lax.axis_index("row")
+    return lax.shift_right_logical(lax.axis_index("col"), 1)
+
+
+def split_body(n, axis, *refs):
+    ins, outs = refs[:-n], refs[-n:]
+    rows = ins[0].shape[0] // n
     for j in range(n):
-        part = pl.ds(pl.multiple_of((row ^ j) * rows, rows), rows)
-        outs[j][...] = (keep[part, :].astype(F32) + come[part, :].astype(F32)).astype(BF16)
-
-
-def split_sum(keep, come, n, after):
-    rows, width = keep.shape
-    return run(
-        functools.partial(split_body, n),
-        (keep, come),
-        [VMEM] * 2,
+        part = pl.ds(pl.multiple_of((position(axis) ^ j) * rows, rows), rows)
+        outs[j][...] = tree([x[part, :].astype(F32) for x in ins]).astype(BF16)
+
+
+def split_sum(items, n, axis, after=()):
+    rows, width = items[0].shape
+    return run(
+        functools.partial(split_body, n, axis),
+        tuple(items),
+        [VMEM] * len(items),
         [shape((rows // n, width))] * n,
         after=after,
     )
@@ -454,20 +440,21 @@
     )[0]
 
 
-def join_body(n, *refs):
-    row = lax.axis_index("row")
+def join_body(n, axis, *refs):
     rows = refs[0].shape[0]
     for j in range(n):
-        refs[n][pl.ds(pl.multiple_of((row ^ j) * rows, rows), rows), :] = refs[j][...]
-
-
-def join(parts):
+        part = pl.ds(pl.multiple_of((position(axis) ^ j) * rows, rows), rows)
+        refs[n][part, :] = refs[j][...]
+
+
+def join(parts, axis, after=()):
     rows, width = parts[0].shape
     return run(
-        functools.partial(join_body, len(parts)),
+        functools.partial(join_body, len(parts), axis),
         tuple(parts),
         [VMEM] * len(parts),
         [shape((rows * len(parts), width))],
+        after=after,
     )[0]
 
 
@@ -514,13 +501,21 @@
 
     def scatter_line(own, after=()):
         if line != 4:
-            parts = [own[0]] + [line_flip(own[j], j) for j in range(1, line)]
-            return tree([x.astype(F32) for x in parts]), []
+            return [own[0]] + [line_flip(own[j], j) for j in range(1, line)]
         inward = col_send(own[3], [(0, 1), (3, 2)])
         middle = col_send(own[3], [(1, 2), (2, 1)])
+        onward = col_send(sum_parts([own[2], inward], after), [(1, 3), (2, 0)])
         near = line_flip(own[1], 1)
-        part, message = onward(own[0], own[2], near, middle, inward, after)
-        return part, [line_flip(message, 2)]
+        far = col_send(own[2], [(0, 2), (3, 1)])
+        return [own[0], near, middle, onward, far]
+
+    def gather_row(pair):
+        if n_row != 4:
+            return [pair] + [[row_flip(x, j) for x in pair] for j in range(1, n_row)]
+        x_first, y_second = row_flip(pair[0], 1), row_flip(pair[1], 2)
+        x_second, y_first = row_flip(pair[1], 1), row_flip(pair[0], 2)
+        diagonal = [row_flip(x_first, 2), row_flip(y_second, 1)]
+        return [pair, [x_first, x_second], [y_first, y_second], diagonal]
 
     def gather_near(own):
         if line != 4:
@@ -544,35 +539,41 @@
     give = forward(number, entries, tiles, first_in, True, 1)
     keep = forward(number, entries, tiles, first_in, True, 0)
     if early:
-        early = relay(early, (keep,))
+        early = relay(early, (give,))
     own = pair_sum(keep, core_flip(give))
-    part, far = scatter_line(own)
+    parts = scatter_line(own)
     if early:
         gathered = gather_far(scaled, *early, (own[0],))
     else:
         gathered = [scaled] + [line_flip(scaled, j) for j in range(1, line)]
     ranged = [x for g in gathered for x in (g, core_flip(g))]
-    hidden = backward(t_number, t_entries, tiles, ranged)
-    agg = aggregate(part, far, scale)
-    spread = [agg] + [row_flip(agg, j) for j in range(1, n_row)]
-    stacked = first_layer(spread[:-1], scale, w_first)
+    spread = gather_row(aggregate(parts, scale))
+    arrived = [spread[1][0], spread[2][1]]
+    hidden = backward(t_number, t_entries, tiles, ranged, arrived)
+    stacked = first_layer(spread[:1], scale, w_first)
     sums = weight_grads(0, hidden, *stacked, scale, w_first, w_second)
-    aggs, outs = first_layer(spread[-1:], scale, w_first, stacked, sums[:1])
+    stacked = first_layer(spread[1:-1], scale, w_first, stacked, sums[:1])
+    aggs, outs = first_layer(spread[-1:], scale, w_first, stacked)
 
     give = forward(number, entries, tiles, outs, False, 1)
     keep = forward(number, entries, tiles, outs, False, 0)
     own = pair_sum(keep, core_flip(give))
 
-    give, keep = weight_grads(
-        2 * n_row - 2, hidden, aggs, outs, scale, w_first, w_second, sums, (own[0],)
-    )
-    part, far = scatter_line(own, (keep,))
-    parts = split_sum(keep, core_flip(give), n_row, (part,))
-    moment = sum_parts([parts[0]] + [row_flip(parts[j], j) for j in range(1, n_row)])
-    moment = sum_parts([moment] + [line_flip(moment, j) for j in range(1, line)], far)
-    mine = join([moment] + [row_flip(moment, j) for j in range(1, n_row)])
+    give, keep = weight_grads(2, hidden, aggs, outs, scale, w_first, w_second, sums, (own[0],))
+    parts = scatter_line(own, (keep,))
+    split = split_sum([keep, core_flip(give)], n_row, "row")
+    moment = [split[0]] + [row_flip(split[j], j) for j in range(1, n_row)]
+    if moment[0].shape[0] % (16 * line) == 0:
+        split = split_sum(moment, line, "line", parts[1:3])
+        moment = sum_parts([split[0]] + [line_flip(split[j], j) for j in range(1, line)])
+        moment = [moment] + [line_flip(moment, j) for j in range(1, line)]
+        moment = join(moment, "line", parts[3:])
+    else:
+        moment = sum_parts(moment)
+        moment = sum_parts([moment] + [line_flip(moment, j) for j in range(1, line)])
+    mine = join([moment] + [row_flip(moment, j) for j in range(1, n_row)], "row")
     grad_first, grad_second = select(mine, core_flip(mine))
-    return second_layer(part, far, scale, w_second), grad_first, grad_second
+    return second_layer(parts, scale, w_second), grad_first, grad_second
 
 
 def solution(mesh):

time: 197 us -> 185 us (0.939)
  waiting for transfers between devices: 109 us -> 60 us
  starting transfers between devices: 45.9 us -> 75.4 us
  Pallas kernels: 34.4 us -> 42.2 us
    ppermute x16 -> x21, waiting for transfers between devices: 81 us -> 47.6 us  [col_send(): lax.ppermute(value, 'col', [(2 * a + k, 2 * b + k) for a, b in pairs for...]
    ppermute x16 -> x21, starting transfers between devices: 33.8 us -> 57.4 us  [col_send(): lax.ppermute(value, 'col', [(2 * a + k, 2 * b + k) for a, b in pairs for...]
    ppermute x9 -> x12, waiting for transfers between devices: 25.8 us -> 11.8 us  [row_flip(): return lax.ppermute(value, 'row', [(a, a ^ j) for a in range(n_row)])]
    pallas_call x25 -> x27, Pallas kernels: 34.4 us -> 42.2 us  [run(): pl.pallas_call(whole, out_shape=outs, in_specs=specs + [ANY] * extra, out...]
    ppermute x9 -> x12, starting transfers between devices: 10.7 us -> 17 us  [row_flip(): return lax.ppermute(value, 'row', [(a, a ^ j) for a in range(n_row)])]
  transfers between devices with their start and end apart: 33 -> 41, of which waited for: 20 -> 15; matrix products, arithmetic and copies ran while one was open for 0% -> 0% of each run, Pallas kernels for 14% -> 19%
where the time goes in v6:
time: 185 us; the launch traced here: 184 us
  starting transfers between devices  75.4 us (41%)
  waiting for transfers between devices  60 us (32%)
  Pallas kernels  42.2 us (23%)
  local copies, waits for them, and re-layouts  4.2 us (2%)
    ppermute x21, starting transfers between devices, col_send(): lax.ppermute(value, 'col', [(2 * a + k, 2 * b + k) for a, b in pairs for...  57.4 us
    ppermute x21, waiting for transfers between devices, col_send(): lax.ppermute(value, 'col', [(2 * a + k, 2 * b + k) for a, b in pairs for...  47.6 us
    pallas_call x27, Pallas kernels, run(): pl.pallas_call(whole, out_shape=outs, in_specs=specs + [ANY] * extra, out...  42.2 us
    ppermute x12, starting transfers between devices, row_flip(): return lax.ppermute(value, 'row', [(a, a ^ j) for a in range(n_row)])  17 us
    ppermute x12, waiting for transfers between devices, row_flip(): return lax.ppermute(value, 'row', [(a, a ^ j) for a in range(n_row)])  11.8 us
    unnamed x13, local copies, waits for them, and re-layouts  4.2 us
  transfers between devices with their start and end apart: 41, of which 15 were waited for; matrix products, arithmetic and copies ran while one was open for 0% of the time, Pallas kernels for 19%

profile of v6, /device:TPU:0, one launch (start us, length us, event | category | flops | bytes accessed | tf_op | source)
XLA Modules:
  0.0 183.6 jit_solution(6949598899267645949)
XLA Ops:
  0.6 0.7 copy.13
  1.3 1.0 copy-done.2
  2.4 0.6 shard_map.103
  2.9 3.1 %collective-permute-start.13 = (bf16[2,512,256]{2,1,0:T(8,128)(2,1)S(1)}, bf16[2,512,256]{2,1,0:T(8,128)(2,1)S(1)}, u32[]{:S(2)}, u32[]{:S(2)}) collective-permute-start(bf16[2,512,256]{2,1,0:T(8,128)(2,1)S(1)} %get-tuple-element.58.refs_3_), channel_id=1, source_target_pairs={{0,2},{1,3},{2,0},{3,1},{4,6},{5,7},{6,4},{7,5},{8,10},{9,11},{10,... | collective-permute-start | bytes 1572872 | tf_op jit(solution)/shard_map/ppermute | solution.py:489
  6.0 0.7 collective-permute-start.14
  7.4 1.6 copy-done.4
  9.0 0.7 copy-done.5
  9.6 2.6 %shard_map.104 = (bf16[8,256,512]{2,1,0:T(8,128)(2,1)S(1)}, s32[16]{0:T(128)S(1)}, s32[128]{0:T(128)S(1)}, s32[8]{0:T(128)S(1)}, s32[128]{0:T(128)S(1)}) custom-call(s32[1]{0:T(128)} %bitcast.7.refs_0_, s32[48]{0:T(128)S(1)} %bitcast.15, bf16[8,256,512]{2,1,0:T(8,128)(2,1)S(1)} %bitcast.14, f32[8,256,128]{2,1,0:T(8,128)S(1)} %get-tuple-element.44.refs_3_.refs_5_.refs_2_.refs_4_), custom_call_target="tpu_custom_call" | custom-call | flops 35999997952 | tf_op jit(solution)/shard_map/pallas_call | solution.py:24
  12.4 3.4 %shard_map.106.refs_2_ = bf16[8,256,512]{2,1,0:T(8,128)(2,1)S(1)} custom-call(s32[16]{0:T(128)S(1)} %get-tuple-element.45.refs_0_, s32[128]{0:T(128)S(1)} %get-tuple-element.46.refs_1_, bf16[48,256,256]{2,1,0:T(8,128)(2,1)S(1)} %bitcast.9, bf16[8,256,512]{2,1,0:T(8,128)(2,1)S(1)} %get-tuple-element.47.refs_3_), custom_call_target="tpu_custom_call" | custom-call | flops 35999997952 | tf_op jit(solution)/shard_map/pallas_call | solution.py:24
  15.8 2.1 %collective-permute-done.13.refs_0_ = bf16[2,512,256]{2,1,0:T(8,128)(2,1)S(1)} collective-permute-done((bf16[2,512,256]{2,1,0:T(8,128)(2,1)S(1)}, bf16[2,512,256]{2,1,0:T(8,128)(2,1)S(1)}, u32[]{:S(2)}, u32[]{:S(2)}) %collective-permute-start.13) | collective-permute-done | bytes 524320 | tf_op jit(solution)/shard_map/ppermute | solution.py:489
  18.0 0.7 collective-permute-start.16
  18.7 4.2 %shard_map.105.refs_0_ = bf16[8,256,512]{2,1,0:T(8,128)(2,1)S(1)} custom-call(s32[16]{0:T(128)S(1)} %get-tuple-element.45.refs_0_, s32[128]{0:T(128)S(1)} %get-tuple-element.46.refs_1_, bf16[48,256,256]{2,1,0:T(8,128)(2,1)S(1)} %bitcast.10, bf16[8,256,512]{2,1,0:T(8,128)(2,1)S(1)} %get-tuple-element.47.refs_3_), custom_call_target="tpu_custom_call" | custom-call | flops 35999997952 | tf_op jit(solution)/shard_map/pallas_call | solution.py:24
  22.9 0.5 shard_map.107
  23.4 9.7 %collective-permute-start.3 = (bf16[2,256,512]{2,1,0:T(8,128)(2,1)S(1)}, bf16[2,256,512]{2,1,0:T(8,128)(2,1)S(1)}, u32[]{:S(2)}, u32[]{:S(2)}) collective-permute-start(bf16[2,256,512]{2,1,0:T(8,128)(2,1)S(1)} %get-tuple-element.50), channel_id=1, source_target_pairs={{0,2},{1,3},{6,4},{7,5},{8,10},{9,11},{14,12},{15,13},{16,18},{17,... | collective-permute-start | bytes 1572872 | tf_op jit(solution)/shard_map/ppermute | solution.py:489
  33.1 1.3 collective-permute-start.17
  34.5 1.3 collective-permute-start.18
  35.8 0.7 collective-permute-start.2
  36.5 7.7 %collective-permute-start.5 = (bf16[2,256,512]{2,1,0:T(8,128)(2,1)S(1)}, bf16[2,256,512]{2,1,0:T(8,128)(2,1)S(1)}, u32[]{:S(2)}, u32[]{:S(2)}) collective-permute-start(bf16[2,256,512]{2,1,0:T(8,128)(2,1)S(1)} %get-tuple-element.51.refs_0_), channel_id=1, source_target_pairs={{0,4},{1,5},{6,2},{7,3},{8,12},{9,13},{14,10},{15,11},{16,20},{17,... | collective-permute-start | bytes 1572872 | tf_op jit(solution)/shard_map/ppermute | solution.py:489
  44.6 5.2 %collective-permute-done.17.refs_2_ = bf16[2,512,256]{2,1,0:T(8,128)(2,1)S(1)} collective-permute-done((bf16[2,512,256]{2,1,0:T(8,128)(2,1)S(1)}, bf16[2,512,256]{2,1,0:T(8,128)(2,1)S(1)}, u32[]{:S(2)}, u32[]{:S(2)}) %collective-permute-start.17) | collective-permute-done | bytes 524320 | tf_op jit(solution)/shard_map/ppermute | solution.py:489
  49.9 1.5 collective-permute-start.4
  51.4 10.6 %collective-permute-done.18.refs_3_ = bf16[2,512,256]{2,1,0:T(8,128)(2,1)S(1)} collective-permute-done((bf16[2,512,256]{2,1,0:T(8,128)(2,1)S(1)}, bf16[2,512,256]{2,1,0:T(8,128)(2,1)S(1)}, u32[]{:S(2)}, u32[]{:S(2)}) %collective-permute-start.18) | collective-permute-done | bytes 524320 | tf_op jit(solution)/shard_map/ppermute | solution.py:489
  62.1 0.6 collective-permute-start.15
  62.8 17.1 %collective-permute-done.1.refs_1_ = bf16[2,256,512]{2,1,0:T(8,128)(2,1)S(1)} collective-permute-done((bf16[2,256,512]{2,1,0:T(8,128)(2,1)S(1)}, bf16[2,256,512]{2,1,0:T(8,128)(2,1)S(1)}, u32[]{:S(2)}, u32[]{:S(2)}) %collective-permute-start.1) | collective-permute-done | bytes 524320 | tf_op jit(solution)/shard_map/ppermute | solution.py:489
  80.3 0.9 collective-permute-start.6
  81.2 1.7 collective-permute-start.8
  83.0 0.6 shard_map.110
  83.6 1.2 collective-permute-start.10
  85.1 4.3 %collective-permute-done.6.refs_11_.refs_0_ = bf16[256,512]{1,0:T(8,128)(2,1)S(1)} collective-permute-done((bf16[256,512]{1,0:T(8,128)(2,1)S(1)}, bf16[256,512]{1,0:T(8,128)(2,1)S(1)}, u32[]{:S(2)}, u32[]{:S(2)}) %collective-permute-start.6) | collective-permute-done | bytes 262176 | tf_op jit(solution)/shard_map/ppermute | solution.py:500
  89.4 1.7 collective-permute-start.7
  91.1 0.9 collective-permute-start.9
  92.1 7.8 %shard_map.114.refs_0_ = bf16[8,512,256]{2,1,0:T(8,128)(2,1)S(1)} custom-call(s32[8]{0:T(128)S(1)} %get-tuple-element.56.refs_0_, s32[128]{0:T(128)S(1)} %get-tuple-element.57.refs_1_, bf16[48,256,256]{2,1,0:T(8,128)(2,1)S(1)} %bitcast.11, bf16[2,512,256]{2,1,0:T(8,128)(2,1)S(1)} %get-tuple-element.58.refs_3_, ...), custom_call_target="tpu_custom_call" | custom-call | flops 35999997952 | tf_op jit(solution)/shard_map/pallas_call | solution.py:24
  99.9 2.2 %shard_map.115 = (f32[512,512]{1,0:T(8,128)S(1)}, f32[512,512]{1,0:T(8,128)S(1)}) custom-call(bf16[8,512,256]{2,1,0:T(8,128)(2,1)S(1)} %shard_map.114.refs_0_, bf16[2,256,512]{2,1,0:T(8,128)(2,1)S(1)} %get-tuple-element.54.refs_1_.refs_6_, bf16[2,256,512]{2,1,0:T(8,128)(2,1)S(1)} %get-tuple-element.55.refs_2_.refs_7_, ...), custom_call_target="tpu_custom_call" | custom-call | flops 35999997952 | tf_op jit(solution)/shard_map/pallas_call | solution.py:24
  102.1 1.1 shard_map.116
  103.3 0.9 shard_map.117
  104.1 3.4 %shard_map.119 = bf16[8,256,512]{2,1,0:T(8,128)(2,1)S(1)} custom-call(s32[16]{0:T(128)S(1)} %get-tuple-element.45.refs_0_, s32[128]{0:T(128)S(1)} %get-tuple-element.46.refs_1_, bf16[48,256,256]{2,1,0:T(8,128)(2,1)S(1)} %bitcast.12, bf16[8,256,512]{2,1,0:T(8,128)(2,1)S(1)} %get-tuple-element.66.refs_3_.refs_2_), custom_call_target="tpu_custom_call" | custom-call | flops 35999997952 | tf_op jit(solution)/shard_map/pallas_call | solution.py:24
  107.6 4.2 %shard_map.118.refs_0_ = bf16[8,256,512]{2,1,0:T(8,128)(2,1)S(1)} custom-call(s32[16]{0:T(128)S(1)} %get-tuple-element.45.refs_0_, s32[128]{0:T(128)S(1)} %get-tuple-element.46.refs_1_, bf16[48,256,256]{2,1,0:T(8,128)(2,1)S(1)} %bitcast.13, bf16[8,256,512]{2,1,0:T(8,128)(2,1)S(1)} %get-tuple-element.66.refs_3_.refs_2_), custom_call_target="tpu_custom_call" | custom-call | flops 35999997952 | tf_op jit(solution)/shard_map/pallas_call | solution.py:24
  111.8 0.5 shard_map.120
  112.3 1.5 collective-permute-start.24
  113.8 6.6 %shard_map.121 = (bf16[512,512]{1,0:T(8,128)(2,1)S(1)}, bf16[512,512]{1,0:T(8,128)(2,1)S(1)}) custom-call(bf16[8,512,256]{2,1,0:T(8,128)(2,1)S(1)} %shard_map.114.refs_0_, bf16[8,256,512]{2,1,0:T(8,128)(2,1)S(1)} %get-tuple-element.71.refs_1_, bf16[8,256,512]{2,1,0:T(8,128)(2,1)S(1)} %get-tuple-element.66.refs_3_.refs_2_, ...), custom_call_target="tpu_custom_call" | custom-call | flops 35999997952 | tf_op jit(solution)/shard_map/pallas_call | solution.py:24
  120.6 0.7 collective-permute-start.23
  121.3 6.8 %collective-permute-start.26 = (bf16[2,256,512]{2,1,0:T(8,128)(2,1)S(1)}, bf16[2,256,512]{2,1,0:T(8,128)(2,1)S(1)}, u32[]{:S(2)}, u32[]{:S(2)}) collective-permute-start(bf16[2,256,512]{2,1,0:T(8,128)(2,1)S(1)} %get-tuple-element.70.refs_0_), channel_id=1, source_target_pairs={{0,4},{1,5},{6,2},{7,3},{8,12},{9,13},{14,10},{15,11},{16,20},{17,... | collective-permute-start | bytes 1572872 | tf_op jit(solution)/shard_map/ppermute | solution.py:489
  128.2 1.3 collective-permute-start.25
  129.7 2.5 %collective-permute-start.28 = (bf16[128,512]{1,0:T(8,128)(2,1)S(1)}, bf16[128,512]{1,0:T(8,128)(2,1)S(1)}, u32[]{:S(2)}, u32[]{:S(2)}) collective-permute-start(bf16[128,512]{1,0:T(8,128)(2,1)S(1)} %get-tuple-element.76), channel_id=1, source_target_pairs={{0,8},{8,0},{16,24},{24,16},{1,9},{9,1},{17,25},{25,17},{2,10},{10... | collective-permute-start | bytes 393224 | tf_op jit(solution)/shard_map/ppermute | solution.py:500
  132.2 4.8 %collective-permute-done.22.refs_1_.refs_4_ = bf16[2,256,512]{2,1,0:T(8,128)(2,1)S(1)} collective-permute-done((bf16[2,256,512]{2,1,0:T(8,128)(2,1)S(1)}, bf16[2,256,512]{2,1,0:T(8,128)(2,1)S(1)}, u32[]{:S(2)}, u32[]{:S(2)}) %collective-permute-start.22) | collective-permute-done | bytes 524320 | tf_op jit(solution)/shard_map/ppermute | solution.py:489
  137.0 1.0 collective-permute-start.29
  138.0 3.2 %collective-permute-start.30 = (bf16[128,512]{1,0:T(8,128)(2,1)S(1)}, bf16[128,512]{1,0:T(8,128)(2,1)S(1)}, u32[]{:S(2)}, u32[]{:S(2)}) collective-permute-start(bf16[128,512]{1,0:T(8,128)(2,1)S(1)} %get-tuple-element.78), channel_id=1, source_target_pairs={{0,24},{8,16},{16,8},{24,0},{1,25},{9,17},{17,9},{25,1},{2,26},{10... | collective-permute-start | bytes 393224 | tf_op jit(solution)/shard_map/ppermute | solution.py:500
  141.2 3.4 %collective-permute-done.29.refs_2_ = bf16[128,512]{1,0:T(8,128)(2,1)S(1)} collective-permute-done((bf16[128,512]{1,0:T(8,128)(2,1)S(1)}, bf16[128,512]{1,0:T(8,128)(2,1)S(1)}, u32[]{:S(2)}, u32[]{:S(2)}) %collective-permute-start.29) | collective-permute-done | bytes 131104 | tf_op jit(solution)/shard_map/ppermute | solution.py:500
  144.7 12.1 %collective-permute-start.31 = (bf16[32,512]{1,0:T(8,128)(2,1)S(1)}, bf16[32,512]{1,0:T(8,128)(2,1)S(1)}, u32[]{:S(2)}, u32[]{:S(2)}) collective-permute-start(bf16[32,512]{1,0:T(8,128)(2,1)S(1)} %get-tuple-element.80), channel_id=1, source_target_pairs={{0,2},{1,3},{2,0},{3,1},{4,6},{5,7},{6,4},{7,5},{8,10},{9,11},{10,... | collective-permute-start | bytes 98312 | tf_op jit(solution)/shard_map/ppermute | solution.py:489
  156.8 2.1 %collective-permute-start.32 = (bf16[32,512]{1,0:T(8,128)(2,1)S(1)}, bf16[32,512]{1,0:T(8,128)(2,1)S(1)}, u32[]{:S(2)}, u32[]{:S(2)}) collective-permute-start(bf16[32,512]{1,0:T(8,128)(2,1)S(1)} %get-tuple-element.81), channel_id=1, source_target_pairs={{0,4},{1,5},{2,6},{3,7},{4,0},{5,1},{6,2},{7,3},{8,12},{9,13},{10,... | collective-permute-start | bytes 98312 | tf_op jit(solution)/shard_map/ppermute | solution.py:489
  158.9 1.4 collective-permute-start.33
  160.3 2.1 %collective-permute-done.31.refs_1_ = bf16[32,512]{1,0:T(8,128)(2,1)S(1)} collective-permute-done((bf16[32,512]{1,0:T(8,128)(2,1)S(1)}, bf16[32,512]{1,0:T(8,128)(2,1)S(1)}, u32[]{:S(2)}, u32[]{:S(2)}) %collective-permute-start.31) | collective-permute-done | bytes 32800 | tf_op jit(solution)/shard_map/ppermute | solution.py:489
  162.4 0.6 collective-permute-done.32.refs_2_
  163.0 1.6 collective-permute-done.33.refs_3_
  164.9 1.9 %collective-permute-start.35 = (bf16[32,512]{1,0:T(8,128)(2,1)S(1)}, bf16[32,512]{1,0:T(8,128)(2,1)S(1)}, u32[]{:S(2)}, u32[]{:S(2)}) collective-permute-start(bf16[32,512]{1,0:T(8,128)(2,1)S(1)} %shard_map.126.refs_0_), channel_id=1, source_target_pairs={{0,4},{1,5},{2,6},{3,7},{4,0},{5,1},{6,2},{7,3},{8,12},{9,13},{10,... | collective-permute-start | bytes 98312 | tf_op jit(solution)/shard_map/ppermute | solution.py:489
  166.8 2.3 %collective-permute-start.36 = (bf16[32,512]{1,0:T(8,128)(2,1)S(1)}, bf16[32,512]{1,0:T(8,128)(2,1)S(1)}, u32[]{:S(2)}, u32[]{:S(2)}) collective-permute-start(bf16[32,512]{1,0:T(8,128)(2,1)S(1)} %shard_map.126.refs_0_), channel_id=1, source_target_pairs={{0,6},{1,7},{2,4},{3,5},{4,2},{5,3},{6,0},{7,1},{8,14},{9,15},{10,... | collective-permute-start | bytes 98312 | tf_op jit(solution)/shard_map/ppermute | solution.py:489
  169.1 0.6 collective-permute-done.35.refs_2_
  169.7 2.8 %collective-permute-done.36.refs_3_ = bf16[32,512]{1,0:T(8,128)(2,1)S(1)} collective-permute-done((bf16[32,512]{1,0:T(8,128)(2,1)S(1)}, bf16[32,512]{1,0:T(8,128)(2,1)S(1)}, u32[]{:S(2)}, u32[]{:S(2)}) %collective-permute-start.36) | collective-permute-done | bytes 32800 | tf_op jit(solution)/shard_map/ppermute | solution.py:489
  172.5 1.3 collective-permute-start.37
  174.0 2.1 %collective-permute-start.39 = (bf16[128,512]{1,0:T(8,128)(2,1)S(1)}, bf16[128,512]{1,0:T(8,128)(2,1)S(1)}, u32[]{:S(2)}, u32[]{:S(2)}) collective-permute-start(bf16[128,512]{1,0:T(8,128)(2,1)S(1)} %shard_map.127.refs_0_), channel_id=1, source_target_pairs={{0,24},{8,16},{16,8},{24,0},{1,25},{9,17},{17,9},{25,1},{2,26},{10... | collective-permute-start | bytes 393224 | tf_op jit(solution)/shard_map/ppermute | solution.py:500
  176.1 1.5 collective-permute-done.37.refs_1_
  177.5 2.6 %collective-permute-done.38.refs_2_ = bf16[128,512]{1,0:T(8,128)(2,1)S(1)} collective-permute-done((bf16[128,512]{1,0:T(8,128)(2,1)S(1)}, bf16[128,512]{1,0:T(8,128)(2,1)S(1)}, u32[]{:S(2)}, u32[]{:S(2)}) %collective-permute-start.38) | collective-permute-done | bytes 131104 | tf_op jit(solution)/shard_map/ppermute | solution.py:500
  180.3 1.3 shard_map.123
  181.6 0.6 collective-permute-done.40.refs_1_
  182.2 1.5 shard_map.129
  (58 shorter events, 3.0 us)
Async XLA Ops:
  1.3 1.0 copy-start.2
  2.9 15.0 %collective-permute-start.13 = (bf16[2,512,256]{2,1,0:T(8,128)(2,1)S(1)}, bf16[2,512,256]{2,1,0:T(8,128)(2,1)S(1)}, u32[]{:S(2)}, u32[]{:S(2)}) collective-permute-start(bf16[2,512,256]{2,1,0:T(8,128)(2,1)S(1)} %get-tuple-element.58.refs_3_), channel_id=1, source_target_pairs={{0,2},{1,3},{2,0},{3,1},{4,6},{5,7},{6,4},{7,5},{8,10},{9,11},{10,... | collective-permute-start | bytes 1572872 | tf_op jit(solution)/shard_map/ppermute | solution.py:489
  6.0 11.9 %collective-permute-start.14 = (bf16[2,512,256]{2,1,0:T(8,128)(2,1)S(1)}, bf16[2,512,256]{2,1,0:T(8,128)(2,1)S(1)}, u32[]{:S(2)}, u32[]{:S(2)}) collective-permute-start(bf16[2,512,256]{2,1,0:T(8,128)(2,1)S(1)} %get-tuple-element.58.refs_3_), channel_id=1, source_target_pairs={{2,4},{3,5},{4,2},{5,3},{10,12},{11,13},{12,10},{13,11},{18,20},{1... | collective-permute-start | bytes 1572872 | tf_op jit(solution)/shard_map/ppermute | solution.py:489
  7.4 1.6 copy-start.4
  9.0 0.7 copy-start.5
  9.6 2.8 %copy-start.3 = (bf16[1,1,48,256,256]{4,3,2,1,0:T(8,128)(2,1)S(1)}, bf16[1,1,48,256,256]{4,3,2,1,0:T(8,128)(2,1)}, u32[]{:S(2)}) copy-start(bf16[1,1,48,256,256]{4,3,2,1,0:T(8,128)(2,1)} %param.10) | copy-start | bytes 18874372
  15.8 7.1 %collective-permute-start = (bf16[8,256,512]{2,1,0:T(8,128)(2,1)S(1)}, bf16[8,256,512]{2,1,0:T(8,128)(2,1)S(1)}, u32[]{:S(2)}, u32[]{:S(2)}) collective-permute-start(bf16[8,256,512]{2,1,0:T(8,128)(2,1)S(1)} %shard_map.106.refs_2_), channel_id=1, source_target_pairs={{0,1},{1,0},{2,3},{3,2},{4,5},{5,4},{6,7},{7,6},{8,9},{9,8},{10,11... | collective-permute-start | bytes 6291464 | tf_op jit(solution)/shard_map/ppermute | solution.py:497
  18.0 16.4 %collective-permute-start.16 = (bf16[2,512,256]{2,1,0:T(8,128)(2,1)S(1)}, bf16[2,512,256]{2,1,0:T(8,128)(2,1)S(1)}, u32[]{:S(2)}, u32[]{:S(2)}) collective-permute-start(bf16[2,512,256]{2,1,0:T(8,128)(2,1)S(1)} %get-tuple-element.59.refs_5_), channel_id=1, source_target_pairs={{2,4},{3,5},{4,2},{5,3},{10,12},{11,13},{12,10},{13,11},{18,20},{1... | collective-permute-start | bytes 1572872 | tf_op jit(solution)/shard_map/ppermute | solution.py:489
  23.4 20.8 %collective-permute-start.3 = (bf16[2,256,512]{2,1,0:T(8,128)(2,1)S(1)}, bf16[2,256,512]{2,1,0:T(8,128)(2,1)S(1)}, u32[]{:S(2)}, u32[]{:S(2)}) collective-permute-start(bf16[2,256,512]{2,1,0:T(8,128)(2,1)S(1)} %get-tuple-element.50), channel_id=1, source_target_pairs={{0,2},{1,3},{6,4},{7,5},{8,10},{9,11},{14,12},{15,13},{16,18},{17,... | collective-permute-start | bytes 1572872 | tf_op jit(solution)/shard_map/ppermute | solution.py:489
  33.1 16.8 %collective-permute-start.17 = (bf16[2,512,256]{2,1,0:T(8,128)(2,1)S(1)}, bf16[2,512,256]{2,1,0:T(8,128)(2,1)S(1)}, u32[]{:S(2)}, u32[]{:S(2)}) collective-permute-start(bf16[2,512,256]{2,1,0:T(8,128)(2,1)S(1)} %get-tuple-element.60.refs_1_), channel_id=1, source_target_pairs={{2,0},{3,1},{4,6},{5,7},{10,8},{11,9},{12,14},{13,15},{18,16},{19,... | collective-permute-start | bytes 1572872 | tf_op jit(solution)/shard_map/ppermute | solution.py:489
  34.5 27.5 %collective-permute-start.18 = (bf16[2,512,256]{2,1,0:T(8,128)(2,1)S(1)}, bf16[2,512,256]{2,1,0:T(8,128)(2,1)S(1)}, u32[]{:S(2)}, u32[]{:S(2)}) collective-permute-start(bf16[2,512,256]{2,1,0:T(8,128)(2,1)S(1)} %shard_map.112.refs_0_), channel_id=1, source_target_pairs={{2,0},{3,1},{4,6},{5,7},{10,8},{11,9},{12,14},{13,15},{18,16},{19,... | collective-permute-start | bytes 1572872 | tf_op jit(solution)/shard_map/ppermute | solution.py:489
  35.8 26.3 %collective-permute-start.2 = (bf16[2,256,512]{2,1,0:T(8,128)(2,1)S(1)}, bf16[2,256,512]{2,1,0:T(8,128)(2,1)S(1)}, u32[]{:S(2)}, u32[]{:S(2)}) collective-permute-start(bf16[2,256,512]{2,1,0:T(8,128)(2,1)S(1)} %get-tuple-element.50), channel_id=1, source_target_pairs={{2,4},{3,5},{4,2},{5,3},{10,12},{11,13},{12,10},{13,11},{18,20},{1... | collective-permute-start | bytes 1572872 | tf_op jit(solution)/shard_map/ppermute | solution.py:489
  36.5 26.2 %collective-permute-start.5 = (bf16[2,256,512]{2,1,0:T(8,128)(2,1)S(1)}, bf16[2,256,512]{2,1,0:T(8,128)(2,1)S(1)}, u32[]{:S(2)}, u32[]{:S(2)}) collective-permute-start(bf16[2,256,512]{2,1,0:T(8,128)(2,1)S(1)} %get-tuple-element.51.refs_0_), channel_id=1, source_target_pairs={{0,4},{1,5},{6,2},{7,3},{8,12},{9,13},{14,10},{15,11},{16,20},{17,... | collective-permute-start | bytes 1572872 | tf_op jit(solution)/shard_map/ppermute | solution.py:489
  44.2 35.7 %collective-permute-start.1 = (bf16[2,256,512]{2,1,0:T(8,128)(2,1)S(1)}, bf16[2,256,512]{2,1,0:T(8,128)(2,1)S(1)}, u32[]{:S(2)}, u32[]{:S(2)}) collective-permute-start(bf16[2,256,512]{2,1,0:T(8,128)(2,1)S(1)} %get-tuple-element.49), channel_id=1, source_target_pairs={{0,2},{1,3},{2,0},{3,1},{4,6},{5,7},{6,4},{7,5},{8,10},{9,11},{10,... | collective-permute-start | bytes 1572872 | tf_op jit(solution)/shard_map/ppermute | solution.py:489
  49.9 30.0 %collective-permute-start.4 = (bf16[2,256,512]{2,1,0:T(8,128)(2,1)S(1)}, bf16[2,256,512]{2,1,0:T(8,128)(2,1)S(1)}, u32[]{:S(2)}, u32[]{:S(2)}) collective-permute-start(bf16[2,256,512]{2,1,0:T(8,128)(2,1)S(1)} %shard_map.108), channel_id=1, source_target_pairs={{2,6},{3,7},{4,0},{5,1},{10,14},{11,15},{12,8},{13,9},{18,22},{19,... | collective-permute-start | bytes 1572872 | tf_op jit(solution)/shard_map/ppermute | solution.py:489
  62.0 19.2 %collective-permute-start.12 = (bf16[2,512,256]{2,1,0:T(8,128)(2,1)S(1)}, bf16[2,512,256]{2,1,0:T(8,128)(2,1)S(1)}, u32[]{:S(2)}, u32[]{:S(2)}) collective-permute-start(bf16[2,512,256]{2,1,0:T(8,128)(2,1)S(1)} %get-tuple-element.58.refs_3_), channel_id=1, source_target_pairs={{0,1},{1,0},{2,3},{3,2},{4,5},{5,4},{6,7},{7,6},{8,9},{9,8},{10,11... | collective-permute-start | bytes 1572872 | tf_op jit(solution)/shard_map/ppermute | solution.py:497
  62.1 20.8 %copy-start = (bf16[512,512]{1,0:T(8,128)(2,1)S(1)}, bf16[512,512]{1,0:T(8,128)(2,1)}, u32[]{:S(2)}) copy-start(bf16[512,512]{1,0:T(8,128)(2,1)} %refs_4_.3) | copy-start | bytes 1572868
  62.1 21.4 %collective-permute-start.15 = (bf16[2,512,256]{2,1,0:T(8,128)(2,1)S(1)}, bf16[2,512,256]{2,1,0:T(8,128)(2,1)S(1)}, u32[]{:S(2)}, u32[]{:S(2)}) collective-permute-start(bf16[2,512,256]{2,1,0:T(8,128)(2,1)S(1)} %get-tuple-element.59.refs_5_), channel_id=1, source_target_pairs={{0,1},{1,0},{2,3},{3,2},{4,5},{5,4},{6,7},{7,6},{8,9},{9,8},{10,11... | collective-permute-start | bytes 1572872 | tf_op jit(solution)/shard_map/ppermute | solution.py:497
  62.7 22.0 %collective-permute-start.19 = (bf16[2,512,256]{2,1,0:T(8,128)(2,1)S(1)}, bf16[2,512,256]{2,1,0:T(8,128)(2,1)S(1)}, u32[]{:S(2)}, u32[]{:S(2)}) collective-permute-start(bf16[2,512,256]{2,1,0:T(8,128)(2,1)S(1)} %get-tuple-element.61.refs_7_), channel_id=1, source_target_pairs={{0,1},{1,0},{2,3},{3,2},{4,5},{5,4},{6,7},{7,6},{8,9},{9,8},{10,11... | collective-permute-start | bytes 1572872 | tf_op jit(solution)/shard_map/ppermute | solution.py:497
  79.9 12.2 %collective-permute-start.20 = (bf16[2,512,256]{2,1,0:T(8,128)(2,1)S(1)}, bf16[2,512,256]{2,1,0:T(8,128)(2,1)S(1)}, u32[]{:S(2)}, u32[]{:S(2)}) collective-permute-start(bf16[2,512,256]{2,1,0:T(8,128)(2,1)S(1)} %get-tuple-element.62.refs_9_), channel_id=1, source_target_pairs={{0,1},{1,0},{2,3},{3,2},{4,5},{5,4},{6,7},{7,6},{8,9},{9,8},{10,11... | collective-permute-start | bytes 1572872 | tf_op jit(solution)/shard_map/ppermute | solution.py:497
  80.3 9.2 %collective-permute-start.6 = (bf16[256,512]{1,0:T(8,128)(2,1)S(1)}, bf16[256,512]{1,0:T(8,128)(2,1)S(1)}, u32[]{:S(2)}, u32[]{:S(2)}) collective-permute-start(bf16[256,512]{1,0:T(8,128)(2,1)S(1)} %get-tuple-element.52.refs_0_), channel_id=1, source_target_pairs={{0,8},{8,0},{16,24},{24,16},{1,9},{9,1},{17,25},{25,17},{2,10},{10... | collective-permute-start | bytes 786440 | tf_op jit(solution)/shard_map/ppermute | solution.py:500
  81.2 9.9 %collective-permute-start.8 = (bf16[256,512]{1,0:T(8,128)(2,1)S(1)}, bf16[256,512]{1,0:T(8,128)(2,1)S(1)}, u32[]{:S(2)}, u32[]{:S(2)}) collective-permute-start(bf16[256,512]{1,0:T(8,128)(2,1)S(1)} %get-tuple-element.53.refs_1_), channel_id=1, source_target_pairs={{0,16},{8,24},{16,0},{24,8},{1,17},{9,25},{17,1},{25,9},{2,18},{10... | collective-permute-start | bytes 786440 | tf_op jit(solution)/shard_map/ppermute | solution.py:500
  83.6 18.5 %collective-permute-start.10 = (bf16[256,512]{1,0:T(8,128)(2,1)S(1)}, bf16[256,512]{1,0:T(8,128)(2,1)S(1)}, u32[]{:S(2)}, u32[]{:S(2)}) collective-permute-start(bf16[256,512]{1,0:T(8,128)(2,1)S(1)} %get-tuple-element.53.refs_1_), channel_id=1, source_target_pairs={{0,8},{8,0},{16,24},{24,16},{1,9},{9,1},{17,25},{25,17},{2,10},{10... | collective-permute-start | bytes 786440 | tf_op jit(solution)/shard_map/ppermute | solution.py:500
  84.7 17.4 %collective-permute-start.11 = (bf16[256,512]{1,0:T(8,128)(2,1)S(1)}, bf16[256,512]{1,0:T(8,128)(2,1)S(1)}, u32[]{:S(2)}, u32[]{:S(2)}) collective-permute-start(bf16[256,512]{1,0:T(8,128)(2,1)S(1)} %get-tuple-element.52.refs_0_), channel_id=1, source_target_pairs={{0,16},{8,24},{16,0},{24,8},{1,17},{9,25},{17,1},{25,9},{2,18},{10... | collective-permute-start | bytes 786440 | tf_op jit(solution)/shard_map/ppermute | solution.py:500
  89.4 13.8 %collective-permute-start.7 = (bf16[256,512]{1,0:T(8,128)(2,1)S(1)}, bf16[256,512]{1,0:T(8,128)(2,1)S(1)}, u32[]{:S(2)}, u32[]{:S(2)}) collective-permute-start(bf16[256,512]{1,0:T(8,128)(2,1)S(1)} %collective-permute-done.6.refs_11_.refs_0_), channel_id=1, source_target_pairs={{0,16},{8,24},{16,0},{24,8},{1,17},{9,25},{17,1},{25,9},{2,18},{10... | collective-permute-start | bytes 786440 | tf_op jit(solution)/shard_map/ppermute | solution.py:500
  91.1 12.1 %collective-permute-start.9 = (bf16[256,512]{1,0:T(8,128)(2,1)S(1)}, bf16[256,512]{1,0:T(8,128)(2,1)S(1)}, u32[]{:S(2)}, u32[]{:S(2)}) collective-permute-start(bf16[256,512]{1,0:T(8,128)(2,1)S(1)} %collective-permute-done.8.refs_12_.refs_3_), channel_id=1, source_target_pairs={{0,8},{8,0},{16,24},{24,16},{1,9},{9,1},{17,25},{25,17},{2,10},{10... | collective-permute-start | bytes 786440 | tf_op jit(solution)/shard_map/ppermute | solution.py:500
  92.1 7.8 %copy-start.1 = (bf16[512,512]{1,0:T(8,128)(2,1)S(1)}, bf16[512,512]{1,0:T(8,128)(2,1)}, u32[]{:S(2)}) copy-start(bf16[512,512]{1,0:T(8,128)(2,1)} %refs_6_.1) | copy-start | bytes 1572868
  107.5 4.3 %collective-permute-start.21 = (bf16[8,256,512]{2,1,0:T(8,128)(2,1)S(1)}, bf16[8,256,512]{2,1,0:T(8,128)(2,1)S(1)}, u32[]{:S(2)}, u32[]{:S(2)}) collective-permute-start(bf16[8,256,512]{2,1,0:T(8,128)(2,1)S(1)} %shard_map.119), channel_id=1, source_target_pairs={{0,1},{1,0},{2,3},{3,2},{4,5},{5,4},{6,7},{7,6},{8,9},{9,8},{10,11... | collective-permute-start | bytes 6291464 | tf_op jit(solution)/shard_map/ppermute | solution.py:497
  112.3 15.8 %collective-permute-start.24 = (bf16[2,256,512]{2,1,0:T(8,128)(2,1)S(1)}, bf16[2,256,512]{2,1,0:T(8,128)(2,1)S(1)}, u32[]{:S(2)}, u32[]{:S(2)}) collective-permute-start(bf16[2,256,512]{2,1,0:T(8,128)(2,1)S(1)} %get-tuple-element.69), channel_id=1, source_target_pairs={{0,2},{1,3},{6,4},{7,5},{8,10},{9,11},{14,12},{15,13},{16,18},{17,... | collective-permute-start | bytes 1572872 | tf_op jit(solution)/shard_map/ppermute | solution.py:489
  120.4 9.1 %collective-permute-start.27 = (bf16[512,512]{1,0:T(8,128)(2,1)S(1)}, bf16[512,512]{1,0:T(8,128)(2,1)S(1)}, u32[]{:S(2)}, u32[]{:S(2)}) collective-permute-start(bf16[512,512]{1,0:T(8,128)(2,1)S(1)} %get-tuple-element.74), channel_id=1, source_target_pairs={{0,1},{1,0},{2,3},{3,2},{4,5},{5,4},{6,7},{7,6},{8,9},{9,8},{10,11... | collective-permute-start | bytes 1572872 | tf_op jit(solution)/shard_map/ppermute | solution.py:497
  120.6 16.4 %collective-permute-start.22 = (bf16[2,256,512]{2,1,0:T(8,128)(2,1)S(1)}, bf16[2,256,512]{2,1,0:T(8,128)(2,1)S(1)}, u32[]{:S(2)}, u32[]{:S(2)}) collective-permute-start(bf16[2,256,512]{2,1,0:T(8,128)(2,1)S(1)} %get-tuple-element.68), channel_id=1, source_target_pairs={{0,2},{1,3},{2,0},{3,1},{4,6},{5,7},{6,4},{7,5},{8,10},{9,11},{10,... | collective-permute-start | bytes 1572872 | tf_op jit(solution)/shard_map/ppermute | solution.py:489
  120.6 17.4 %collective-permute-start.23 = (bf16[2,256,512]{2,1,0:T(8,128)(2,1)S(1)}, bf16[2,256,512]{2,1,0:T(8,128)(2,1)S(1)}, u32[]{:S(2)}, u32[]{:S(2)}) collective-permute-start(bf16[2,256,512]{2,1,0:T(8,128)(2,1)S(1)} %get-tuple-element.69), channel_id=1, source_target_pairs={{2,4},{3,5},{4,2},{5,3},{10,12},{11,13},{12,10},{13,11},{18,20},{1... | collective-permute-start | bytes 1572872 | tf_op jit(solution)/shard_map/ppermute | solution.py:489
  121.3 47.8 %collective-permute-start.26 = (bf16[2,256,512]{2,1,0:T(8,128)(2,1)S(1)}, bf16[2,256,512]{2,1,0:T(8,128)(2,1)S(1)}, u32[]{:S(2)}, u32[]{:S(2)}) collective-permute-start(bf16[2,256,512]{2,1,0:T(8,128)(2,1)S(1)} %get-tuple-element.70.refs_0_), channel_id=1, source_target_pairs={{0,4},{1,5},{6,2},{7,3},{8,12},{9,13},{14,10},{15,11},{16,20},{17,... | collective-permute-start | bytes 1572872 | tf_op jit(solution)/shard_map/ppermute | solution.py:489
  128.2 44.2 %collective-permute-start.25 = (bf16[2,256,512]{2,1,0:T(8,128)(2,1)S(1)}, bf16[2,256,512]{2,1,0:T(8,128)(2,1)S(1)}, u32[]{:S(2)}, u32[]{:S(2)}) collective-permute-start(bf16[2,256,512]{2,1,0:T(8,128)(2,1)S(1)} %shard_map.122), channel_id=1, source_target_pairs={{2,6},{3,7},{4,0},{5,1},{10,14},{11,15},{12,8},{13,9},{18,22},{19,... | collective-permute-start | bytes 1572872 | tf_op jit(solution)/shard_map/ppermute | solution.py:489
  129.7 11.5 %collective-permute-start.28 = (bf16[128,512]{1,0:T(8,128)(2,1)S(1)}, bf16[128,512]{1,0:T(8,128)(2,1)S(1)}, u32[]{:S(2)}, u32[]{:S(2)}) collective-permute-start(bf16[128,512]{1,0:T(8,128)(2,1)S(1)} %get-tuple-element.76), channel_id=1, source_target_pairs={{0,8},{8,0},{16,24},{24,16},{1,9},{9,1},{17,25},{25,17},{2,10},{10... | collective-permute-start | bytes 393224 | tf_op jit(solution)/shard_map/ppermute | solution.py:500
  137.0 7.5 %collective-permute-start.29 = (bf16[128,512]{1,0:T(8,128)(2,1)S(1)}, bf16[128,512]{1,0:T(8,128)(2,1)S(1)}, u32[]{:S(2)}, u32[]{:S(2)}) collective-permute-start(bf16[128,512]{1,0:T(8,128)(2,1)S(1)} %get-tuple-element.77), channel_id=1, source_target_pairs={{0,16},{8,24},{16,0},{24,8},{1,17},{9,25},{17,1},{25,9},{2,18},{10... | collective-permute-start | bytes 393224 | tf_op jit(solution)/shard_map/ppermute | solution.py:500
  138.0 6.6 %collective-permute-start.30 = (bf16[128,512]{1,0:T(8,128)(2,1)S(1)}, bf16[128,512]{1,0:T(8,128)(2,1)S(1)}, u32[]{:S(2)}, u32[]{:S(2)}) collective-permute-start(bf16[128,512]{1,0:T(8,128)(2,1)S(1)} %get-tuple-element.78), channel_id=1, source_target_pairs={{0,24},{8,16},{16,8},{24,0},{1,25},{9,17},{17,9},{25,1},{2,26},{10... | collective-permute-start | bytes 393224 | tf_op jit(solution)/shard_map/ppermute | solution.py:500
  144.7 17.7 %collective-permute-start.31 = (bf16[32,512]{1,0:T(8,128)(2,1)S(1)}, bf16[32,512]{1,0:T(8,128)(2,1)S(1)}, u32[]{:S(2)}, u32[]{:S(2)}) collective-permute-start(bf16[32,512]{1,0:T(8,128)(2,1)S(1)} %get-tuple-element.80), channel_id=1, source_target_pairs={{0,2},{1,3},{2,0},{3,1},{4,6},{5,7},{6,4},{7,5},{8,10},{9,11},{10,... | collective-permute-start | bytes 98312 | tf_op jit(solution)/shard_map/ppermute | solution.py:489
  156.8 6.2 %collective-permute-start.32 = (bf16[32,512]{1,0:T(8,128)(2,1)S(1)}, bf16[32,512]{1,0:T(8,128)(2,1)S(1)}, u32[]{:S(2)}, u32[]{:S(2)}) collective-permute-start(bf16[32,512]{1,0:T(8,128)(2,1)S(1)} %get-tuple-element.81), channel_id=1, source_target_pairs={{0,4},{1,5},{2,6},{3,7},{4,0},{5,1},{6,2},{7,3},{8,12},{9,13},{10,... | collective-permute-start | bytes 98312 | tf_op jit(solution)/shard_map/ppermute | solution.py:489
  158.9 5.7 %collective-permute-start.33 = (bf16[32,512]{1,0:T(8,128)(2,1)S(1)}, bf16[32,512]{1,0:T(8,128)(2,1)S(1)}, u32[]{:S(2)}, u32[]{:S(2)}) collective-permute-start(bf16[32,512]{1,0:T(8,128)(2,1)S(1)} %get-tuple-element.82), channel_id=1, source_target_pairs={{0,6},{1,7},{2,4},{3,5},{4,2},{5,3},{6,0},{7,1},{8,14},{9,15},{10,... | collective-permute-start | bytes 98312 | tf_op jit(solution)/shard_map/ppermute | solution.py:489
  164.6 4.5 %collective-permute-start.34 = (bf16[32,512]{1,0:T(8,128)(2,1)S(1)}, bf16[32,512]{1,0:T(8,128)(2,1)S(1)}, u32[]{:S(2)}, u32[]{:S(2)}) collective-permute-start(bf16[32,512]{1,0:T(8,128)(2,1)S(1)} %shard_map.126.refs_0_), channel_id=1, source_target_pairs={{0,2},{1,3},{2,0},{3,1},{4,6},{5,7},{6,4},{7,5},{8,10},{9,11},{10,... | collective-permute-start | bytes 98312 | tf_op jit(solution)/shard_map/ppermute | solution.py:489
  164.9 4.8 %collective-permute-start.35 = (bf16[32,512]{1,0:T(8,128)(2,1)S(1)}, bf16[32,512]{1,0:T(8,128)(2,1)S(1)}, u32[]{:S(2)}, u32[]{:S(2)}) collective-permute-start(bf16[32,512]{1,0:T(8,128)(2,1)S(1)} %shard_map.126.refs_0_), channel_id=1, source_target_pairs={{0,4},{1,5},{2,6},{3,7},{4,0},{5,1},{6,2},{7,3},{8,12},{9,13},{10,... | collective-permute-start | bytes 98312 | tf_op jit(solution)/shard_map/ppermute | solution.py:489
  166.8 5.7 %collective-permute-start.36 = (bf16[32,512]{1,0:T(8,128)(2,1)S(1)}, bf16[32,512]{1,0:T(8,128)(2,1)S(1)}, u32[]{:S(2)}, u32[]{:S(2)}) collective-permute-start(bf16[32,512]{1,0:T(8,128)(2,1)S(1)} %shard_map.126.refs_0_), channel_id=1, source_target_pairs={{0,6},{1,7},{2,4},{3,5},{4,2},{5,3},{6,0},{7,1},{8,14},{9,15},{10,... | collective-permute-start | bytes 98312 | tf_op jit(solution)/shard_map/ppermute | solution.py:489
  172.5 5.0 %collective-permute-start.37 = (bf16[128,512]{1,0:T(8,128)(2,1)S(1)}, bf16[128,512]{1,0:T(8,128)(2,1)S(1)}, u32[]{:S(2)}, u32[]{:S(2)}) collective-permute-start(bf16[128,512]{1,0:T(8,128)(2,1)S(1)} %shard_map.127.refs_0_), channel_id=1, source_target_pairs={{0,8},{8,0},{16,24},{24,16},{1,9},{9,1},{17,25},{25,17},{2,10},{10... | collective-permute-start | bytes 393224 | tf_op jit(solution)/shard_map/ppermute | solution.py:500
  173.8 6.4 %collective-permute-start.38 = (bf16[128,512]{1,0:T(8,128)(2,1)S(1)}, bf16[128,512]{1,0:T(8,128)(2,1)S(1)}, u32[]{:S(2)}, u32[]{:S(2)}) collective-permute-start(bf16[128,512]{1,0:T(8,128)(2,1)S(1)} %shard_map.127.refs_0_), channel_id=1, source_target_pairs={{0,16},{8,24},{16,0},{24,8},{1,17},{9,25},{17,1},{25,9},{2,18},{10... | collective-permute-start | bytes 393224 | tf_op jit(solution)/shard_map/ppermute | solution.py:500
  174.0 6.1 %collective-permute-start.39 = (bf16[128,512]{1,0:T(8,128)(2,1)S(1)}, bf16[128,512]{1,0:T(8,128)(2,1)S(1)}, u32[]{:S(2)}, u32[]{:S(2)}) collective-permute-start(bf16[128,512]{1,0:T(8,128)(2,1)S(1)} %shard_map.127.refs_0_), channel_id=1, source_target_pairs={{0,24},{8,16},{16,8},{24,0},{1,25},{9,17},{17,9},{25,1},{2,26},{10... | collective-permute-start | bytes 393224 | tf_op jit(solution)/shard_map/ppermute | solution.py:500
  180.2 2.0 %collective-permute-start.40 = (bf16[512,512]{1,0:T(8,128)(2,1)S(1)}, bf16[512,512]{1,0:T(8,128)(2,1)S(1)}, u32[]{:S(2)}, u32[]{:S(2)}) collective-permute-start(bf16[512,512]{1,0:T(8,128)(2,1)S(1)} %shard_map.128.refs_0_), channel_id=1, source_target_pairs={{0,1},{1,0},{2,3},{3,2},{4,5},{5,4},{6,7},{7,6},{8,9},{9,8},{10,11... | collective-permute-start | bytes 1572872 | tf_op jit(solution)/shard_map/ppermute | solution.py:497

commit v7 on v6

--- a/solution.py
+++ b/solution.py
@@ -91,7 +91,8 @@
     )
 
 
-def prepare_body(local_cols, count_ref, slot_ref, values, scale, out, *lists):
+def prepare_body(count_ref, slot_ref, values, scale, out, *lists):
+    local_cols = values.shape[0]
     list_tiles(count_ref[0], slot_ref, lists[0], lists[1], local_cols, True)
     list_tiles(count_ref[0], slot_ref, lists[2], lists[3], local_cols, False)
 
@@ -107,7 +108,7 @@
     local_cols = values.shape[0]
     sizes = (block_rows, block_rows * local_cols, local_cols, block_rows * local_cols)
     return run(
-        functools.partial(prepare_body, local_cols),
+        prepare_body,
         (count, slots, values, scale),
         [SMEM] * 2 + [VMEM] * 2,
         [shape(values.shape)] + [shape((n,), jnp.int32) for n in sizes],
@@ -278,12 +279,13 @@
     three[...] = jnp.where(ends, out_three[...], middle[...])
 
 
-def choose(last, across, middle, out_two, out_three):
+def choose(last, across, middle, out_two, out_three, after):
     return run(
         functools.partial(choose_body, last),
         (across, middle, out_two, out_three),
         [VMEM] * 4,
         [shape(across.shape)] * 2,
+        after=after,
     )
 
 
@@ -295,12 +297,13 @@
         out[...] = (summed * wide).astype(BF16)
 
 
-def aggregate(parts, scale):
+def aggregate(parts, scale, after):
     return run(
         functools.partial(agg_body, len(parts)),
         (*parts, scale),
         [VMEM] * (len(parts) + 1),
         [shape(parts[0].shape[1:])] * 2,
+        after=after,
     )
 
 
@@ -469,9 +472,7 @@
 
 
 COST = {
-    prepare_body: 36,
     forward_body: 36,
-    backward_body: 36,
     grad_body: 36,
 }
 
@@ -499,15 +500,24 @@
     def row_flip(value, j):
         return lax.ppermute(value, "row", [(a, a ^ j) for a in range(n_row)])
 
-    def scatter_line(own, after=()):
+    def scatter_begin(own, after=()):
+        if line != 4:
+            return own[2], None
+        to_three = col_send(own[3], [(0, 1), (3, 2)])
+        to_two = col_send(own[2], [(0, 1), (3, 2)])
+        return sum_parts([own[2], to_three], after), to_two
+
+    def scatter_next(own, begun, after):
+        if line != 4:
+            return own[3], []
+        crossing = sum_parts([own[3], begun[1]], after)
+        onward = col_send(begun[0], [(1, 3), (2, 0)])
+        return crossing, [col_send(crossing, [(1, 2), (2, 1)]), onward]
+
+    def scatter_end(own, arrived, near):
         if line != 4:
             return [own[0]] + [line_flip(own[j], j) for j in range(1, line)]
-        inward = col_send(own[3], [(0, 1), (3, 2)])
-        middle = col_send(own[3], [(1, 2), (2, 1)])
-        onward = col_send(sum_parts([own[2], inward], after), [(1, 3), (2, 0)])
-        near = line_flip(own[1], 1)
-        far = col_send(own[2], [(0, 2), (3, 1)])
-        return [own[0], near, middle, onward, far]
+        return [own[0], line_flip(near, 1), *arrived]
 
     def gather_row(pair):
         if n_row != 4:
@@ -522,11 +532,11 @@
             return []
         return [line_flip(own, 1), col_send(own, [(1, 2), (2, 1)])]
 
-    def gather_far(own, near, middle, after):
+    def gather_far(own, near, middle, after, late):
         (across,) = relay([col_send(near, [(1, 2), (2, 1)])], after)
         out_two = col_send(middle, [(1, 0), (2, 3)])
         out_three = col_send(across, [(1, 0), (2, 3)])
-        return [own, near, *choose(line - 1, across, middle, out_two, out_three)]
+        return [own, near, *choose(line - 1, across, middle, out_two, out_three, late)]
 
     halves = piece // edge
     scale, scaled = scale_kernel(degree[:, 0], cotangent, edge)
@@ -541,15 +551,17 @@
     if early:
         early = relay(early, (give,))
     own = pair_sum(keep, core_flip(give))
-    parts = scatter_line(own)
+    begun = scatter_begin(own)
+    crossing, arrived = scatter_next(own, begun, begun[:1])
+    parts = scatter_end(own, arrived, own[1])
     if early:
-        gathered = gather_far(scaled, *early, (own[0],))
+        late = (crossing, arrived[1])
+        gathered = gather_far(scaled, *early, begun[:1], late)
     else:
         gathered = [scaled] + [line_flip(scaled, j) for j in range(1, line)]
     ranged = [x for g in gathered for x in (g, core_flip(g))]
-    spread = gather_row(aggregate(parts, scale))
-    arrived = [spread[1][0], spread[2][1]]
-    hidden = backward(t_number, t_entries, tiles, ranged, arrived)
+    hidden = backward(t_number, t_entries, tiles, ranged)
+    spread = gather_row(aggregate(parts, scale, (hidden,)))
     stacked = first_layer(spread[:1], scale, w_first)
     sums = weight_grads(0, hidden, *stacked, scale, w_first, w_second)
     stacked = first_layer(spread[1:-1], scale, w_first, stacked, sums[:1])
@@ -560,19 +572,24 @@
     own = pair_sum(keep, core_flip(give))
 
     give, keep = weight_grads(2, hidden, aggs, outs, scale, w_first, w_second, sums, (own[0],))
-    parts = scatter_line(own, (keep,))
-    split = split_sum([keep, core_flip(give)], n_row, "row")
+    begun = scatter_begin(own, (keep,))
+    split = split_sum([keep, core_flip(give)], n_row, "row", begun[:1])
     moment = [split[0]] + [row_flip(split[j], j) for j in range(1, n_row)]
+    crossing, arrived = scatter_next(own, begun, moment[1:])
     if moment[0].shape[0] % (16 * line) == 0:
-        split = split_sum(moment, line, "line", parts[1:3])
-        moment = sum_parts([split[0]] + [line_flip(split[j], j) for j in range(1, line)])
-        moment = [moment] + [line_flip(moment, j) for j in range(1, line)]
-        moment = join(moment, "line", parts[3:])
+        split = split_sum(moment, line, "line", (crossing,))
+        moment = sum_parts(
+            [split[0]] + [line_flip(split[j], j) for j in range(1, line)], arrived[1:]
+        )
+        moment = join([moment] + [line_flip(moment, j) for j in range(1, line)], "line")
     else:
         moment = sum_parts(moment)
         moment = sum_parts([moment] + [line_flip(moment, j) for j in range(1, line)])
-    mine = join([moment] + [row_flip(moment, j) for j in range(1, n_row)], "row")
+    (near,) = relay(own[1:2], (moment,))
+    moment = [moment] + [row_flip(moment, j) for j in range(1, n_row)]
+    mine = join(moment, "row", arrived[:1])
     grad_first, grad_second = select(mine, core_flip(mine))
+    parts = scatter_end(own, arrived, near)
     return second_layer(parts, scale, w_second), grad_first, grad_second
 
 

time: 185 us -> 186 us (level)
  waiting for transfers between devices: 60 us -> 84.8 us
  starting transfers between devices: 75.4 us -> 56.4 us
  Pallas kernels: 42.2 us -> 36.7 us
  local copies, waits for them, and re-layouts: 4.2 us -> 6.79 us
    ppermute x21, waiting for transfers between devices: 47.6 us -> 68.2 us  [col_send(): lax.ppermute(value, 'col', [(2 * a + k, 2 * b + k) for a, b in pairs for...]
    ppermute x21, starting transfers between devices: 57.4 us -> 41.5 us  [col_send(): lax.ppermute(value, 'col', [(2 * a + k, 2 * b + k) for a, b in pairs for...]
    pallas_call x27 -> x30, Pallas kernels: 42.2 us -> 36.7 us  [run(): pl.pallas_call(whole, out_shape=outs, in_specs=specs + [ANY] * extra, out...]
    ppermute x12, starting transfers between devices: 17 us -> 12.4 us  [row_flip(): return lax.ppermute(value, 'row', [(a, a ^ j) for a in range(n_row)])]
    unnamed x13 -> x17, local copies, waits for them, and re-layouts: 4.2 us -> 6.79 us
    ppermute x8, waiting for transfers between devices: 0.6 us -> 2.95 us  [core_flip(): return lax.ppermute(value, 'col', [(a, a ^ 1) for a in range(n_col)])]
  transfers between devices with their start and end apart: 41 -> 41, of which waited for: 15 -> 22; matrix products, arithmetic and copies ran while one was open for 0% -> 0% of each run, Pallas kernels for 19% -> 16%
where the time goes in v7:
time: 186 us
  waiting for transfers between devices  84.8 us (46%)
  starting transfers between devices  56.4 us (30%)
  Pallas kernels  36.7 us (20%)
  local copies, waits for them, and re-layouts  6.79 us (4%)
    ppermute x21, waiting for transfers between devices, col_send(): lax.ppermute(value, 'col', [(2 * a + k, 2 * b + k) for a, b in pairs for...  68.2 us
    ppermute x21, starting transfers between devices, col_send(): lax.ppermute(value, 'col', [(2 * a + k, 2 * b + k) for a, b in pairs for...  41.5 us
    pallas_call x30, Pallas kernels, run(): pl.pallas_call(whole, out_shape=outs, in_specs=specs + [ANY] * extra, out...  36.7 us
    ppermute x12, waiting for transfers between devices, row_flip(): return lax.ppermute(value, 'row', [(a, a ^ j) for a in range(n_row)])  13.6 us
    ppermute x12, starting transfers between devices, row_flip(): return lax.ppermute(value, 'row', [(a, a ^ j) for a in range(n_row)])  12.4 us
    unnamed x17, local copies, waits for them, and re-layouts  6.79 us
  transfers between devices with their start and end apart: 41, of which 22 were waited for; matrix products, arithmetic and copies ran while one was open for 0% of the time, Pallas kernels for 16%

profile of v7, /device:TPU:0, one launch (start us, length us, event | category | flops | bytes accessed | tf_op | source)
XLA Modules:
  0.0 186.4 jit_solution(18264429409945777303)
XLA Ops:
  0.6 0.7 copy.13
  1.3 1.0 copy-done.3
  2.9 3.1 %collective-permute-start.7 = (bf16[2,512,256]{2,1,0:T(8,128)(2,1)S(1)}, bf16[2,512,256]{2,1,0:T(8,128)(2,1)S(1)}, u32[]{:S(2)}, u32[]{:S(2)}) collective-permute-start(bf16[2,512,256]{2,1,0:T(8,128)(2,1)S(1)} %get-tuple-element.54.refs_3_), channel_id=1, source_target_pairs={{0,2},{1,3},{2,0},{3,1},{4,6},{5,7},{6,4},{7,5},{8,10},{9,11},{10,... | collective-permute-start | bytes 1572872 | tf_op jit(solution)/shard_map/ppermute | solution.py:490
  6.0 0.7 collective-permute-start.8
  7.4 1.6 copy-done.2
  9.6 2.3 %shard_map.104 = (bf16[8,256,512]{2,1,0:T(8,128)(2,1)S(1)}, s32[16]{0:T(128)S(1)}, s32[128]{0:T(128)S(1)}, s32[8]{0:T(128)S(1)}, s32[128]{0:T(128)S(1)}) custom-call(s32[1]{0:T(128)} %bitcast.7.refs_0_, s32[48]{0:T(128)S(1)} %bitcast.17, bf16[8,256,512]{2,1,0:T(8,128)(2,1)S(1)} %bitcast.15, f32[8,256,128]{2,1,0:T(8,128)S(1)} %get-tuple-element.44.refs_3_.refs_4_.refs_2_), custom_call_target="tpu_custom_call" | custom-call | tf_op jit(solution)/shard_map/pallas_call | solution.py:24
  11.9 2.8 %copy-done = bf16[1,1,48,256,256]{4,3,2,1,0:T(8,128)(2,1)S(1)} copy-done((bf16[1,1,48,256,256]{4,3,2,1,0:T(8,128)(2,1)S(1)}, bf16[1,1,48,256,256]{4,3,2,1,0:T(8,128)(2,1)}, u32[]{:S(2)}) %copy-start) | copy-done | bytes 6291480
  14.7 3.0 %shard_map.106.refs_2_ = bf16[8,256,512]{2,1,0:T(8,128)(2,1)S(1)} custom-call(s32[16]{0:T(128)S(1)} %get-tuple-element.45.refs_0_, s32[128]{0:T(128)S(1)} %get-tuple-element.46.refs_1_, bf16[48,256,256]{2,1,0:T(8,128)(2,1)S(1)} %bitcast.8, bf16[8,256,512]{2,1,0:T(8,128)(2,1)S(1)} %get-tuple-element.47.refs_3_), custom_call_target="tpu_custom_call" | custom-call | flops 35999997952 | tf_op jit(solution)/shard_map/pallas_call | solution.py:24
  17.8 3.2 %shard_map.105.refs_0_ = bf16[8,256,512]{2,1,0:T(8,128)(2,1)S(1)} custom-call(s32[16]{0:T(128)S(1)} %get-tuple-element.45.refs_0_, s32[128]{0:T(128)S(1)} %get-tuple-element.46.refs_1_, bf16[48,256,256]{2,1,0:T(8,128)(2,1)S(1)} %bitcast.9, bf16[8,256,512]{2,1,0:T(8,128)(2,1)S(1)} %get-tuple-element.47.refs_3_), custom_call_target="tpu_custom_call" | custom-call | flops 35999997952 | tf_op jit(solution)/shard_map/pallas_call | solution.py:24
  21.1 0.8 collective-permute-done.refs_1_
  22.4 6.8 %collective-permute-start.3 = (bf16[2,256,512]{2,1,0:T(8,128)(2,1)S(1)}, bf16[2,256,512]{2,1,0:T(8,128)(2,1)S(1)}, u32[]{:S(2)}, u32[]{:S(2)}) collective-permute-start(bf16[2,256,512]{2,1,0:T(8,128)(2,1)S(1)} %get-tuple-element.50.refs_0_), channel_id=1, source_target_pairs={{0,2},{1,3},{6,4},{7,5},{8,10},{9,11},{14,12},{15,13},{16,18},{17,... | collective-permute-start | bytes 1572872 | tf_op jit(solution)/shard_map/ppermute | solution.py:490
  29.1 0.7 collective-permute-start.10
  29.8 1.3 collective-permute-start.11
  31.2 4.7 %collective-permute-start.2 = (bf16[2,256,512]{2,1,0:T(8,128)(2,1)S(1)}, bf16[2,256,512]{2,1,0:T(8,128)(2,1)S(1)}, u32[]{:S(2)}, u32[]{:S(2)}) collective-permute-start(bf16[2,256,512]{2,1,0:T(8,128)(2,1)S(1)} %get-tuple-element.51.refs_0_), channel_id=1, source_target_pairs={{0,2},{1,3},{6,4},{7,5},{8,10},{9,11},{14,12},{15,13},{16,18},{17,... | collective-permute-start | bytes 1572872 | tf_op jit(solution)/shard_map/ppermute | solution.py:490
  35.9 5.3 %collective-permute-done.3.refs_1_ = bf16[2,256,512]{2,1,0:T(8,128)(2,1)S(1)} collective-permute-done((bf16[2,256,512]{2,1,0:T(8,128)(2,1)S(1)}, bf16[2,256,512]{2,1,0:T(8,128)(2,1)S(1)}, u32[]{:S(2)}, u32[]{:S(2)}) %collective-permute-start.3) | collective-permute-done | bytes 524320 | tf_op jit(solution)/shard_map/ppermute | solution.py:490
  41.4 1.3 collective-permute-start.12
  42.7 1.3 collective-permute-start.5
  44.6 7.8 %collective-permute-done.2.refs_1_ = bf16[2,256,512]{2,1,0:T(8,128)(2,1)S(1)} collective-permute-done((bf16[2,256,512]{2,1,0:T(8,128)(2,1)S(1)}, bf16[2,256,512]{2,1,0:T(8,128)(2,1)S(1)}, u32[]{:S(2)}, u32[]{:S(2)}) %collective-permute-start.2) | collective-permute-done | bytes 524320 | tf_op jit(solution)/shard_map/ppermute | solution.py:490
  52.9 17.0 %collective-permute-done.12.refs_3_ = bf16[2,512,256]{2,1,0:T(8,128)(2,1)S(1)} collective-permute-done((bf16[2,512,256]{2,1,0:T(8,128)(2,1)S(1)}, bf16[2,512,256]{2,1,0:T(8,128)(2,1)S(1)}, u32[]{:S(2)}, u32[]{:S(2)}) %collective-permute-start.12) | collective-permute-done | bytes 524320 | tf_op jit(solution)/shard_map/ppermute | solution.py:490
  70.7 0.9 collective-permute-start.4
  72.1 0.7 collective-permute-done.14.refs_10_
  72.8 5.0 %shard_map.113.refs_5_.refs_0_ = bf16[8,512,256]{2,1,0:T(8,128)(2,1)S(1)} custom-call(s32[8]{0:T(128)S(1)} %get-tuple-element.52.refs_0_, s32[128]{0:T(128)S(1)} %get-tuple-element.53.refs_1_, bf16[48,256,256]{2,1,0:T(8,128)(2,1)S(1)} %bitcast.12, bf16[2,512,256]{2,1,0:T(8,128)(2,1)S(1)} %get-tuple-element.54.refs_3_, ...), custom_call_target="tpu_custom_call" | custom-call | tf_op jit(solution)/shard_map/pallas_call | solution.py:24
  77.9 6.7 %collective-permute-done.1.refs_1_ = bf16[2,256,512]{2,1,0:T(8,128)(2,1)S(1)} collective-permute-done((bf16[2,256,512]{2,1,0:T(8,128)(2,1)S(1)}, bf16[2,256,512]{2,1,0:T(8,128)(2,1)S(1)}, u32[]{:S(2)}, u32[]{:S(2)}) %collective-permute-start.1) | collective-permute-done | bytes 524320 | tf_op jit(solution)/shard_map/ppermute | solution.py:490
  84.9 1.1 collective-permute-start.15
  86.0 0.7 collective-permute-start.17
  87.2 1.8 collective-permute-start.20
  89.6 4.6 %collective-permute-done.15.refs_0_ = bf16[256,512]{1,0:T(8,128)(2,1)S(1)} collective-permute-done((bf16[256,512]{1,0:T(8,128)(2,1)S(1)}, bf16[256,512]{1,0:T(8,128)(2,1)S(1)}, u32[]{:S(2)}, u32[]{:S(2)}) %collective-permute-start.15) | collective-permute-done | bytes 262176 | tf_op jit(solution)/shard_map/ppermute | solution.py:501
  94.4 0.9 collective-permute-done.17.refs_3_
  95.2 1.0 collective-permute-start.18
  96.2 2.2 %shard_map.116 = (f32[512,512]{1,0:T(8,128)S(1)}, f32[512,512]{1,0:T(8,128)S(1)}) custom-call(bf16[8,512,256]{2,1,0:T(8,128)(2,1)S(1)} %shard_map.113.refs_5_.refs_0_, bf16[2,256,512]{2,1,0:T(8,128)(2,1)S(1)} %get-tuple-element.61.refs_1_.refs_6_, bf16[2,256,512]{2,1,0:T(8,128)(2,1)S(1)} %get-tuple-element.62.refs_2_.refs_7_, ...), custom_call_target="tpu_custom_call" | custom-call | flops 35999997952 | tf_op jit(solution)/shard_map/pallas_call | solution.py:24
  98.5 1.4 collective-permute-done.19.refs_1_
  99.8 1.1 collective-permute-done.20.refs_2_
  100.9 1.1 shard_map.117
  102.0 2.4 %collective-permute-done.16.refs_0_ = bf16[256,512]{1,0:T(8,128)(2,1)S(1)} collective-permute-done((bf16[256,512]{1,0:T(8,128)(2,1)S(1)}, bf16[256,512]{1,0:T(8,128)(2,1)S(1)}, u32[]{:S(2)}, u32[]{:S(2)}) %collective-permute-start.16) | collective-permute-done | bytes 262176 | tf_op jit(solution)/shard_map/ppermute | solution.py:501
  104.4 0.9 shard_map.118
  105.3 3.0 %shard_map.120 = bf16[8,256,512]{2,1,0:T(8,128)(2,1)S(1)} custom-call(s32[16]{0:T(128)S(1)} %get-tuple-element.45.refs_0_, s32[128]{0:T(128)S(1)} %get-tuple-element.46.refs_1_, bf16[48,256,256]{2,1,0:T(8,128)(2,1)S(1)} %bitcast.13, bf16[8,256,512]{2,1,0:T(8,128)(2,1)S(1)} %get-tuple-element.66.refs_3_.refs_2_), custom_call_target="tpu_custom_call" | custom-call | flops 35999997952 | tf_op jit(solution)/shard_map/pallas_call | solution.py:24
  108.4 3.2 %shard_map.119.refs_0_ = bf16[8,256,512]{2,1,0:T(8,128)(2,1)S(1)} custom-call(s32[16]{0:T(128)S(1)} %get-tuple-element.45.refs_0_, s32[128]{0:T(128)S(1)} %get-tuple-element.46.refs_1_, bf16[48,256,256]{2,1,0:T(8,128)(2,1)S(1)} %bitcast.14, bf16[8,256,512]{2,1,0:T(8,128)(2,1)S(1)} %get-tuple-element.66.refs_3_.refs_2_), custom_call_target="tpu_custom_call" | custom-call | flops 35999997952 | tf_op jit(solution)/shard_map/pallas_call | solution.py:24
  111.6 0.9 collective-permute-done.21.refs_1_
  113.0 5.8 %collective-permute-start.23 = (bf16[2,256,512]{2,1,0:T(8,128)(2,1)S(1)}, bf16[2,256,512]{2,1,0:T(8,128)(2,1)S(1)}, u32[]{:S(2)}, u32[]{:S(2)}) collective-permute-start(bf16[2,256,512]{2,1,0:T(8,128)(2,1)S(1)} %get-tuple-element.74.refs_0_), channel_id=1, source_target_pairs={{0,2},{1,3},{6,4},{7,5},{8,10},{9,11},{14,12},{15,13},{16,18},{17,... | collective-permute-start | bytes 1572872 | tf_op jit(solution)/shard_map/ppermute | solution.py:490
  118.8 6.6 %shard_map.122 = (bf16[512,512]{1,0:T(8,128)(2,1)S(1)}, bf16[512,512]{1,0:T(8,128)(2,1)S(1)}) custom-call(bf16[8,512,256]{2,1,0:T(8,128)(2,1)S(1)} %shard_map.113.refs_5_.refs_0_, bf16[8,256,512]{2,1,0:T(8,128)(2,1)S(1)} %get-tuple-element.69.refs_1_, bf16[8,256,512]{2,1,0:T(8,128)(2,1)S(1)} %get-tuple-element.66.refs_3_.refs_2_, ...), custom_call_target="tpu_custom_call" | custom-call | flops 35999997952 | tf_op jit(solution)/shard_map/pallas_call | solution.py:24
  125.4 0.8 collective-permute-start.22
  126.2 1.6 collective-permute-start.27
  127.7 3.1 %collective-permute-done.23.refs_1_ = bf16[2,256,512]{2,1,0:T(8,128)(2,1)S(1)} collective-permute-done((bf16[2,256,512]{2,1,0:T(8,128)(2,1)S(1)}, bf16[2,256,512]{2,1,0:T(8,128)(2,1)S(1)}, u32[]{:S(2)}, u32[]{:S(2)}) %collective-permute-start.23) | collective-permute-done | bytes 524320 | tf_op jit(solution)/shard_map/ppermute | solution.py:490
  130.9 1.3 collective-permute-start.31
  132.4 1.9 %collective-permute-start.24 = (bf16[128,512]{1,0:T(8,128)(2,1)S(1)}, bf16[128,512]{1,0:T(8,128)(2,1)S(1)}, u32[]{:S(2)}, u32[]{:S(2)}) collective-permute-start(bf16[128,512]{1,0:T(8,128)(2,1)S(1)} %get-tuple-element.76), channel_id=1, source_target_pairs={{0,8},{8,0},{16,24},{24,16},{1,9},{9,1},{17,25},{25,17},{2,10},{10... | collective-permute-start | bytes 393224 | tf_op jit(solution)/shard_map/ppermute | solution.py:501
  134.3 1.7 collective-permute-start.26
  136.0 6.1 %collective-permute-done.27.refs_1_ = bf16[2,256,512]{2,1,0:T(8,128)(2,1)S(1)} collective-permute-done((bf16[2,256,512]{2,1,0:T(8,128)(2,1)S(1)}, bf16[2,256,512]{2,1,0:T(8,128)(2,1)S(1)}, u32[]{:S(2)}, u32[]{:S(2)}) %collective-permute-start.27) | collective-permute-done | bytes 524320 | tf_op jit(solution)/shard_map/ppermute | solution.py:490
  142.2 0.7 collective-permute-start.36
  143.0 4.4 %collective-permute-start.28 = (bf16[32,512]{1,0:T(8,128)(2,1)S(1)}, bf16[32,512]{1,0:T(8,128)(2,1)S(1)}, u32[]{:S(2)}, u32[]{:S(2)}) collective-permute-start(bf16[32,512]{1,0:T(8,128)(2,1)S(1)} %get-tuple-element.80), channel_id=1, source_target_pairs={{0,2},{1,3},{2,0},{3,1},{4,6},{5,7},{6,4},{7,5},{8,10},{9,11},{10,... | collective-permute-start | bytes 98312 | tf_op jit(solution)/shard_map/ppermute | solution.py:490
  147.4 0.9 collective-permute-start.29
  148.3 1.6 collective-permute-start.30
  149.9 12.5 %collective-permute-done.29.refs_2_ = bf16[32,512]{1,0:T(8,128)(2,1)S(1)} collective-permute-done((bf16[32,512]{1,0:T(8,128)(2,1)S(1)}, bf16[32,512]{1,0:T(8,128)(2,1)S(1)}, u32[]{:S(2)}, u32[]{:S(2)}) %collective-permute-start.29) | collective-permute-done | bytes 32800 | tf_op jit(solution)/shard_map/ppermute | solution.py:490
  162.4 1.0 collective-permute-start.32
  163.4 0.8 collective-permute-start.33
  164.3 2.6 %collective-permute-start.34 = (bf16[32,512]{1,0:T(8,128)(2,1)S(1)}, bf16[32,512]{1,0:T(8,128)(2,1)S(1)}, u32[]{:S(2)}, u32[]{:S(2)}) collective-permute-start(bf16[32,512]{1,0:T(8,128)(2,1)S(1)} %shard_map.127.refs_0_), channel_id=1, source_target_pairs={{0,6},{1,7},{2,4},{3,5},{4,2},{5,3},{6,0},{7,1},{8,14},{9,15},{10,... | collective-permute-start | bytes 98312 | tf_op jit(solution)/shard_map/ppermute | solution.py:490
  166.9 1.3 collective-permute-done.33.refs_2_
  168.2 1.7 collective-permute-done.34.refs_3_
  170.3 0.9 collective-permute-start.38
  171.1 2.4 %collective-permute-start.39 = (bf16[128,512]{1,0:T(8,128)(2,1)S(1)}, bf16[128,512]{1,0:T(8,128)(2,1)S(1)}, u32[]{:S(2)}, u32[]{:S(2)}) collective-permute-start(bf16[128,512]{1,0:T(8,128)(2,1)S(1)} %shard_map.128.refs_1_.refs_0_), channel_id=1, source_target_pairs={{0,24},{8,16},{16,8},{24,0},{1,25},{9,17},{17,9},{25,1},{2,26},{10... | collective-permute-start | bytes 393224 | tf_op jit(solution)/shard_map/ppermute | solution.py:501
  173.7 1.4 collective-permute-done.37.refs_1_
  175.2 1.8 collective-permute-done.39.refs_3_
  177.1 6.6 %collective-permute-done.35.refs_1_ = bf16[2,256,512]{2,1,0:T(8,128)(2,1)S(1)} collective-permute-done((bf16[2,256,512]{2,1,0:T(8,128)(2,1)S(1)}, bf16[2,256,512]{2,1,0:T(8,128)(2,1)S(1)}, u32[]{:S(2)}, u32[]{:S(2)}) %collective-permute-start.35) | collective-permute-done | bytes 524320 | tf_op jit(solution)/shard_map/ppermute | solution.py:490
  183.7 1.3 shard_map.130
  185.0 1.5 shard_map.132
  (66 shorter events, 7.7 us)
Async XLA Ops:
  1.3 1.0 copy-start.3
  2.9 18.1 %collective-permute-start.7 = (bf16[2,512,256]{2,1,0:T(8,128)(2,1)S(1)}, bf16[2,512,256]{2,1,0:T(8,128)(2,1)S(1)}, u32[]{:S(2)}, u32[]{:S(2)}) collective-permute-start(bf16[2,512,256]{2,1,0:T(8,128)(2,1)S(1)} %get-tuple-element.54.refs_3_), channel_id=1, source_target_pairs={{0,2},{1,3},{2,0},{3,1},{4,6},{5,7},{6,4},{7,5},{8,10},{9,11},{10,... | collective-permute-start | bytes 1572872 | tf_op jit(solution)/shard_map/ppermute | solution.py:490
  6.0 15.0 %collective-permute-start.8 = (bf16[2,512,256]{2,1,0:T(8,128)(2,1)S(1)}, bf16[2,512,256]{2,1,0:T(8,128)(2,1)S(1)}, u32[]{:S(2)}, u32[]{:S(2)}) collective-permute-start(bf16[2,512,256]{2,1,0:T(8,128)(2,1)S(1)} %get-tuple-element.54.refs_3_), channel_id=1, source_target_pairs={{2,4},{3,5},{4,2},{5,3},{10,12},{11,13},{12,10},{13,11},{18,20},{1... | collective-permute-start | bytes 1572872 | tf_op jit(solution)/shard_map/ppermute | solution.py:490
  7.4 1.6 copy-start.2
  9.0 0.7 copy-start.5
  11.9 2.8 %copy-start = (bf16[1,1,48,256,256]{4,3,2,1,0:T(8,128)(2,1)S(1)}, bf16[1,1,48,256,256]{4,3,2,1,0:T(8,128)(2,1)}, u32[]{:S(2)}) copy-start(bf16[1,1,48,256,256]{4,3,2,1,0:T(8,128)(2,1)} %param.10) | copy-start | bytes 18874372
  17.7 4.2 %collective-permute-start = (bf16[8,256,512]{2,1,0:T(8,128)(2,1)S(1)}, bf16[8,256,512]{2,1,0:T(8,128)(2,1)S(1)}, u32[]{:S(2)}, u32[]{:S(2)}) collective-permute-start(bf16[8,256,512]{2,1,0:T(8,128)(2,1)S(1)} %shard_map.106.refs_2_), channel_id=1, source_target_pairs={{0,1},{1,0},{2,3},{3,2},{4,5},{5,4},{6,7},{7,6},{8,9},{9,8},{10,11... | collective-permute-start | bytes 6291464 | tf_op jit(solution)/shard_map/ppermute | solution.py:498
  21.0 51.8 %slice-start = ((s8[6291456]{0:T(1024)(128)(4,1)}), s8[4194304]{0:T(1024)(128)(4,1)S(1)}, s32[]{:S(2)}) async-start(s8[6291456]{0:T(1024)(128)(4,1)} %bitcast.10), calls=%async_computation | async-start | bytes 8388608
  22.4 18.8 %collective-permute-start.3 = (bf16[2,256,512]{2,1,0:T(8,128)(2,1)S(1)}, bf16[2,256,512]{2,1,0:T(8,128)(2,1)S(1)}, u32[]{:S(2)}, u32[]{:S(2)}) collective-permute-start(bf16[2,256,512]{2,1,0:T(8,128)(2,1)S(1)} %get-tuple-element.50.refs_0_), channel_id=1, source_target_pairs={{0,2},{1,3},{6,4},{7,5},{8,10},{9,11},{14,12},{15,13},{16,18},{17,... | collective-permute-start | bytes 1572872 | tf_op jit(solution)/shard_map/ppermute | solution.py:490
  29.1 12.2 %collective-permute-start.10 = (bf16[2,512,256]{2,1,0:T(8,128)(2,1)S(1)}, bf16[2,512,256]{2,1,0:T(8,128)(2,1)S(1)}, u32[]{:S(2)}, u32[]{:S(2)}) collective-permute-start(bf16[2,512,256]{2,1,0:T(8,128)(2,1)S(1)} %get-tuple-element.55.refs_5_), channel_id=1, source_target_pairs={{2,4},{3,5},{4,2},{5,3},{10,12},{11,13},{12,10},{13,11},{18,20},{1... | collective-permute-start | bytes 1572872 | tf_op jit(solution)/shard_map/ppermute | solution.py:490
  29.8 23.0 %collective-permute-start.11 = (bf16[2,512,256]{2,1,0:T(8,128)(2,1)S(1)}, bf16[2,512,256]{2,1,0:T(8,128)(2,1)S(1)}, u32[]{:S(2)}, u32[]{:S(2)}) collective-permute-start(bf16[2,512,256]{2,1,0:T(8,128)(2,1)S(1)} %get-tuple-element.56.refs_1_), channel_id=1, source_target_pairs={{2,0},{3,1},{4,6},{5,7},{10,8},{11,9},{12,14},{13,15},{18,16},{19,... | collective-permute-start | bytes 1572872 | tf_op jit(solution)/shard_map/ppermute | solution.py:490
  31.1 41.7 %slice-start.1 = ((s8[6291456]{0:T(1024)(128)(4,1)}), s8[2097152]{0:T(1024)(128)(4,1)S(1)}, s32[]{:S(2)}) async-start(s8[6291456]{0:T(1024)(128)(4,1)} %bitcast.10), calls=%async_computation.1 | async-start | bytes 4194304
  31.2 21.2 %collective-permute-start.2 = (bf16[2,256,512]{2,1,0:T(8,128)(2,1)S(1)}, bf16[2,256,512]{2,1,0:T(8,128)(2,1)S(1)}, u32[]{:S(2)}, u32[]{:S(2)}) collective-permute-start(bf16[2,256,512]{2,1,0:T(8,128)(2,1)S(1)} %get-tuple-element.51.refs_0_), channel_id=1, source_target_pairs={{0,2},{1,3},{6,4},{7,5},{8,10},{9,11},{14,12},{15,13},{16,18},{17,... | collective-permute-start | bytes 1572872 | tf_op jit(solution)/shard_map/ppermute | solution.py:490
  41.4 28.6 %collective-permute-start.12 = (bf16[2,512,256]{2,1,0:T(8,128)(2,1)S(1)}, bf16[2,512,256]{2,1,0:T(8,128)(2,1)S(1)}, u32[]{:S(2)}, u32[]{:S(2)}) collective-permute-start(bf16[2,512,256]{2,1,0:T(8,128)(2,1)S(1)} %shard_map.111.refs_0_), channel_id=1, source_target_pairs={{2,0},{3,1},{4,6},{5,7},{10,8},{11,9},{12,14},{13,15},{18,16},{19,... | collective-permute-start | bytes 1572872 | tf_op jit(solution)/shard_map/ppermute | solution.py:490
  42.7 27.3 %collective-permute-start.5 = (bf16[2,256,512]{2,1,0:T(8,128)(2,1)S(1)}, bf16[2,256,512]{2,1,0:T(8,128)(2,1)S(1)}, u32[]{:S(2)}, u32[]{:S(2)}) collective-permute-start(bf16[2,256,512]{2,1,0:T(8,128)(2,1)S(1)} %shard_map.108.refs_2_.refs_1_), channel_id=1, source_target_pairs={{2,6},{3,7},{4,0},{5,1},{10,14},{11,15},{12,8},{13,9},{18,22},{19,... | collective-permute-start | bytes 1572872 | tf_op jit(solution)/shard_map/ppermute | solution.py:490
  44.0 26.7 %collective-permute-start.6 = (bf16[2,512,256]{2,1,0:T(8,128)(2,1)S(1)}, bf16[2,512,256]{2,1,0:T(8,128)(2,1)S(1)}, u32[]{:S(2)}, u32[]{:S(2)}) collective-permute-start(bf16[2,512,256]{2,1,0:T(8,128)(2,1)S(1)} %get-tuple-element.54.refs_3_), channel_id=1, source_target_pairs={{0,1},{1,0},{2,3},{3,2},{4,5},{5,4},{6,7},{7,6},{8,9},{9,8},{10,11... | collective-permute-start | bytes 1572872 | tf_op jit(solution)/shard_map/ppermute | solution.py:498
  52.4 19.1 %collective-permute-start.9 = (bf16[2,512,256]{2,1,0:T(8,128)(2,1)S(1)}, bf16[2,512,256]{2,1,0:T(8,128)(2,1)S(1)}, u32[]{:S(2)}, u32[]{:S(2)}) collective-permute-start(bf16[2,512,256]{2,1,0:T(8,128)(2,1)S(1)} %get-tuple-element.55.refs_5_), channel_id=1, source_target_pairs={{0,1},{1,0},{2,3},{3,2},{4,5},{5,4},{6,7},{7,6},{8,9},{9,8},{10,11... | collective-permute-start | bytes 1572872 | tf_op jit(solution)/shard_map/ppermute | solution.py:498
  70.1 2.0 %collective-permute-start.13 = (bf16[2,512,256]{2,1,0:T(8,128)(2,1)S(1)}, bf16[2,512,256]{2,1,0:T(8,128)(2,1)S(1)}, u32[]{:S(2)}, u32[]{:S(2)}) collective-permute-start(bf16[2,512,256]{2,1,0:T(8,128)(2,1)S(1)} %get-tuple-element.57.refs_7_), channel_id=1, source_target_pairs={{0,1},{1,0},{2,3},{3,2},{4,5},{5,4},{6,7},{7,6},{8,9},{9,8},{10,11... | collective-permute-start | bytes 1572872 | tf_op jit(solution)/shard_map/ppermute | solution.py:498
  70.2 2.6 %collective-permute-start.14 = (bf16[2,512,256]{2,1,0:T(8,128)(2,1)S(1)}, bf16[2,512,256]{2,1,0:T(8,128)(2,1)S(1)}, u32[]{:S(2)}, u32[]{:S(2)}) collective-permute-start(bf16[2,512,256]{2,1,0:T(8,128)(2,1)S(1)} %get-tuple-element.58.refs_9_), channel_id=1, source_target_pairs={{0,1},{1,0},{2,3},{3,2},{4,5},{5,4},{6,7},{7,6},{8,9},{9,8},{10,11... | collective-permute-start | bytes 1572872 | tf_op jit(solution)/shard_map/ppermute | solution.py:498
  70.7 13.9 %collective-permute-start.1 = (bf16[2,256,512]{2,1,0:T(8,128)(2,1)S(1)}, bf16[2,256,512]{2,1,0:T(8,128)(2,1)S(1)}, u32[]{:S(2)}, u32[]{:S(2)}) collective-permute-start(bf16[2,256,512]{2,1,0:T(8,128)(2,1)S(1)} %get-tuple-element.49), channel_id=1, source_target_pairs={{0,2},{1,3},{2,0},{3,1},{4,6},{5,7},{6,4},{7,5},{8,10},{9,11},{10,... | collective-permute-start | bytes 1572872 | tf_op jit(solution)/shard_map/ppermute | solution.py:490
  70.7 13.9 %collective-permute-start.4 = (bf16[2,256,512]{2,1,0:T(8,128)(2,1)S(1)}, bf16[2,256,512]{2,1,0:T(8,128)(2,1)S(1)}, u32[]{:S(2)}, u32[]{:S(2)}) collective-permute-start(bf16[2,256,512]{2,1,0:T(8,128)(2,1)S(1)} %shard_map.109.refs_4_), channel_id=1, source_target_pairs={{2,4},{3,5},{4,2},{5,3},{10,12},{11,13},{12,10},{13,11},{18,20},{1... | collective-permute-start | bytes 1572872 | tf_op jit(solution)/shard_map/ppermute | solution.py:490
  84.6 4.4 %copy-start.1 = (bf16[512,512]{1,0:T(8,128)(2,1)S(1)}, bf16[512,512]{1,0:T(8,128)(2,1)}, u32[]{:S(2)}) copy-start(bf16[512,512]{1,0:T(8,128)(2,1)} %refs_4_.3) | copy-start | bytes 1572868
  84.9 11.3 %copy-start.4 = (bf16[512,512]{1,0:T(8,128)(2,1)S(1)}, bf16[512,512]{1,0:T(8,128)(2,1)}, u32[]{:S(2)}) copy-start(bf16[512,512]{1,0:T(8,128)(2,1)} %refs_5_.7) | copy-start | bytes 1572868
  84.9 9.3 %collective-permute-start.15 = (bf16[256,512]{1,0:T(8,128)(2,1)S(1)}, bf16[256,512]{1,0:T(8,128)(2,1)S(1)}, u32[]{:S(2)}, u32[]{:S(2)}) collective-permute-start(bf16[256,512]{1,0:T(8,128)(2,1)S(1)} %get-tuple-element.59.refs_0_), channel_id=1, source_target_pairs={{0,8},{8,0},{16,24},{24,16},{1,9},{9,1},{17,25},{25,17},{2,10},{10... | collective-permute-start | bytes 786440 | tf_op jit(solution)/shard_map/ppermute | solution.py:501
  86.0 9.2 %collective-permute-start.17 = (bf16[256,512]{1,0:T(8,128)(2,1)S(1)}, bf16[256,512]{1,0:T(8,128)(2,1)S(1)}, u32[]{:S(2)}, u32[]{:S(2)}) collective-permute-start(bf16[256,512]{1,0:T(8,128)(2,1)S(1)} %get-tuple-element.60.refs_1_), channel_id=1, source_target_pairs={{0,16},{8,24},{16,0},{24,8},{1,17},{9,25},{17,1},{25,9},{2,18},{10... | collective-permute-start | bytes 786440 | tf_op jit(solution)/shard_map/ppermute | solution.py:501
  86.7 13.1 %collective-permute-start.19 = (bf16[256,512]{1,0:T(8,128)(2,1)S(1)}, bf16[256,512]{1,0:T(8,128)(2,1)S(1)}, u32[]{:S(2)}, u32[]{:S(2)}) collective-permute-start(bf16[256,512]{1,0:T(8,128)(2,1)S(1)} %get-tuple-element.60.refs_1_), channel_id=1, source_target_pairs={{0,8},{8,0},{16,24},{24,16},{1,9},{9,1},{17,25},{25,17},{2,10},{10... | collective-permute-start | bytes 786440 | tf_op jit(solution)/shard_map/ppermute | solution.py:501
  87.2 13.7 %collective-permute-start.20 = (bf16[256,512]{1,0:T(8,128)(2,1)S(1)}, bf16[256,512]{1,0:T(8,128)(2,1)S(1)}, u32[]{:S(2)}, u32[]{:S(2)}) collective-permute-start(bf16[256,512]{1,0:T(8,128)(2,1)S(1)} %get-tuple-element.59.refs_0_), channel_id=1, source_target_pairs={{0,16},{8,24},{16,0},{24,8},{1,17},{9,25},{17,1},{25,9},{2,18},{10... | collective-permute-start | bytes 786440 | tf_op jit(solution)/shard_map/ppermute | solution.py:501
  94.2 10.2 %collective-permute-start.16 = (bf16[256,512]{1,0:T(8,128)(2,1)S(1)}, bf16[256,512]{1,0:T(8,128)(2,1)S(1)}, u32[]{:S(2)}, u32[]{:S(2)}) collective-permute-start(bf16[256,512]{1,0:T(8,128)(2,1)S(1)} %collective-permute-done.15.refs_0_), channel_id=1, source_target_pairs={{0,16},{8,24},{16,0},{24,8},{1,17},{9,25},{17,1},{25,9},{2,18},{10... | collective-permute-start | bytes 786440 | tf_op jit(solution)/shard_map/ppermute | solution.py:501
  95.2 9.2 %collective-permute-start.18 = (bf16[256,512]{1,0:T(8,128)(2,1)S(1)}, bf16[256,512]{1,0:T(8,128)(2,1)S(1)}, u32[]{:S(2)}, u32[]{:S(2)}) collective-permute-start(bf16[256,512]{1,0:T(8,128)(2,1)S(1)} %collective-permute-done.17.refs_3_), channel_id=1, source_target_pairs={{0,8},{8,0},{16,24},{24,16},{1,9},{9,1},{17,25},{25,17},{2,10},{10... | collective-permute-start | bytes 786440 | tf_op jit(solution)/shard_map/ppermute | solution.py:501
  108.3 4.2 %collective-permute-start.21 = (bf16[8,256,512]{2,1,0:T(8,128)(2,1)S(1)}, bf16[8,256,512]{2,1,0:T(8,128)(2,1)S(1)}, u32[]{:S(2)}, u32[]{:S(2)}) collective-permute-start(bf16[8,256,512]{2,1,0:T(8,128)(2,1)S(1)} %shard_map.120), channel_id=1, source_target_pairs={{0,1},{1,0},{2,3},{3,2},{4,5},{5,4},{6,7},{7,6},{8,9},{9,8},{10,11... | collective-permute-start | bytes 6291464 | tf_op jit(solution)/shard_map/ppermute | solution.py:498
  113.0 17.8 %collective-permute-start.23 = (bf16[2,256,512]{2,1,0:T(8,128)(2,1)S(1)}, bf16[2,256,512]{2,1,0:T(8,128)(2,1)S(1)}, u32[]{:S(2)}, u32[]{:S(2)}) collective-permute-start(bf16[2,256,512]{2,1,0:T(8,128)(2,1)S(1)} %get-tuple-element.74.refs_0_), channel_id=1, source_target_pairs={{0,2},{1,3},{6,4},{7,5},{8,10},{9,11},{14,12},{15,13},{16,18},{17,... | collective-permute-start | bytes 1572872 | tf_op jit(solution)/shard_map/ppermute | solution.py:490
  125.4 6.9 %collective-permute-start.22 = (bf16[512,512]{1,0:T(8,128)(2,1)S(1)}, bf16[512,512]{1,0:T(8,128)(2,1)S(1)}, u32[]{:S(2)}, u32[]{:S(2)}) collective-permute-start(bf16[512,512]{1,0:T(8,128)(2,1)S(1)} %get-tuple-element.72), channel_id=1, source_target_pairs={{0,1},{1,0},{2,3},{3,2},{4,5},{5,4},{6,7},{7,6},{8,9},{9,8},{10,11... | collective-permute-start | bytes 1572872 | tf_op jit(solution)/shard_map/ppermute | solution.py:498
  126.2 15.9 %collective-permute-start.27 = (bf16[2,256,512]{2,1,0:T(8,128)(2,1)S(1)}, bf16[2,256,512]{2,1,0:T(8,128)(2,1)S(1)}, u32[]{:S(2)}, u32[]{:S(2)}) collective-permute-start(bf16[2,256,512]{2,1,0:T(8,128)(2,1)S(1)} %get-tuple-element.73.refs_0_), channel_id=1, source_target_pairs={{0,2},{1,3},{6,4},{7,5},{8,10},{9,11},{14,12},{15,13},{16,18},{17,... | collective-permute-start | bytes 1572872 | tf_op jit(solution)/shard_map/ppermute | solution.py:490
  130.9 31.5 %collective-permute-start.31 = (bf16[2,256,512]{2,1,0:T(8,128)(2,1)S(1)}, bf16[2,256,512]{2,1,0:T(8,128)(2,1)S(1)}, u32[]{:S(2)}, u32[]{:S(2)}) collective-permute-start(bf16[2,256,512]{2,1,0:T(8,128)(2,1)S(1)} %shard_map.123.refs_2_), channel_id=1, source_target_pairs={{2,6},{3,7},{4,0},{5,1},{10,14},{11,15},{12,8},{13,9},{18,22},{19,... | collective-permute-start | bytes 1572872 | tf_op jit(solution)/shard_map/ppermute | solution.py:490
  132.4 9.7 %collective-permute-start.24 = (bf16[128,512]{1,0:T(8,128)(2,1)S(1)}, bf16[128,512]{1,0:T(8,128)(2,1)S(1)}, u32[]{:S(2)}, u32[]{:S(2)}) collective-permute-start(bf16[128,512]{1,0:T(8,128)(2,1)S(1)} %get-tuple-element.76), channel_id=1, source_target_pairs={{0,8},{8,0},{16,24},{24,16},{1,9},{9,1},{17,25},{25,17},{2,10},{10... | collective-permute-start | bytes 393224 | tf_op jit(solution)/shard_map/ppermute | solution.py:501
  134.3 7.8 %collective-permute-start.25 = (bf16[128,512]{1,0:T(8,128)(2,1)S(1)}, bf16[128,512]{1,0:T(8,128)(2,1)S(1)}, u32[]{:S(2)}, u32[]{:S(2)}) collective-permute-start(bf16[128,512]{1,0:T(8,128)(2,1)S(1)} %get-tuple-element.77), channel_id=1, source_target_pairs={{0,16},{8,24},{16,0},{24,8},{1,17},{9,25},{17,1},{25,9},{2,18},{10... | collective-permute-start | bytes 393224 | tf_op jit(solution)/shard_map/ppermute | solution.py:501
  134.3 7.8 %collective-permute-start.26 = (bf16[128,512]{1,0:T(8,128)(2,1)S(1)}, bf16[128,512]{1,0:T(8,128)(2,1)S(1)}, u32[]{:S(2)}, u32[]{:S(2)}) collective-permute-start(bf16[128,512]{1,0:T(8,128)(2,1)S(1)} %get-tuple-element.78), channel_id=1, source_target_pairs={{0,24},{8,16},{16,8},{24,0},{1,25},{9,17},{17,9},{25,1},{2,26},{10... | collective-permute-start | bytes 393224 | tf_op jit(solution)/shard_map/ppermute | solution.py:501
  142.2 31.5 %collective-permute-start.36 = (bf16[2,256,512]{2,1,0:T(8,128)(2,1)S(1)}, bf16[2,256,512]{2,1,0:T(8,128)(2,1)S(1)}, u32[]{:S(2)}, u32[]{:S(2)}) collective-permute-start(bf16[2,256,512]{2,1,0:T(8,128)(2,1)S(1)} %shard_map.125.refs_4_), channel_id=1, source_target_pairs={{2,4},{3,5},{4,2},{5,3},{10,12},{11,13},{12,10},{13,11},{18,20},{1... | collective-permute-start | bytes 1572872 | tf_op jit(solution)/shard_map/ppermute | solution.py:490
  143.0 6.9 %collective-permute-start.28 = (bf16[32,512]{1,0:T(8,128)(2,1)S(1)}, bf16[32,512]{1,0:T(8,128)(2,1)S(1)}, u32[]{:S(2)}, u32[]{:S(2)}) collective-permute-start(bf16[32,512]{1,0:T(8,128)(2,1)S(1)} %get-tuple-element.80), channel_id=1, source_target_pairs={{0,2},{1,3},{2,0},{3,1},{4,6},{5,7},{6,4},{7,5},{8,10},{9,11},{10,... | collective-permute-start | bytes 98312 | tf_op jit(solution)/shard_map/ppermute | solution.py:490
  147.4 15.0 %collective-permute-start.29 = (bf16[32,512]{1,0:T(8,128)(2,1)S(1)}, bf16[32,512]{1,0:T(8,128)(2,1)S(1)}, u32[]{:S(2)}, u32[]{:S(2)}) collective-permute-start(bf16[32,512]{1,0:T(8,128)(2,1)S(1)} %get-tuple-element.81), channel_id=1, source_target_pairs={{0,4},{1,5},{2,6},{3,7},{4,0},{5,1},{6,2},{7,3},{8,12},{9,13},{10,... | collective-permute-start | bytes 98312 | tf_op jit(solution)/shard_map/ppermute | solution.py:490
  148.3 14.1 %collective-permute-start.30 = (bf16[32,512]{1,0:T(8,128)(2,1)S(1)}, bf16[32,512]{1,0:T(8,128)(2,1)S(1)}, u32[]{:S(2)}, u32[]{:S(2)}) collective-permute-start(bf16[32,512]{1,0:T(8,128)(2,1)S(1)} %get-tuple-element.82), channel_id=1, source_target_pairs={{0,6},{1,7},{2,4},{3,5},{4,2},{5,3},{6,0},{7,1},{8,14},{9,15},{10,... | collective-permute-start | bytes 98312 | tf_op jit(solution)/shard_map/ppermute | solution.py:490
  162.4 4.5 %collective-permute-start.32 = (bf16[32,512]{1,0:T(8,128)(2,1)S(1)}, bf16[32,512]{1,0:T(8,128)(2,1)S(1)}, u32[]{:S(2)}, u32[]{:S(2)}) collective-permute-start(bf16[32,512]{1,0:T(8,128)(2,1)S(1)} %shard_map.127.refs_0_), channel_id=1, source_target_pairs={{0,2},{1,3},{2,0},{3,1},{4,6},{5,7},{6,4},{7,5},{8,10},{9,11},{10,... | collective-permute-start | bytes 98312 | tf_op jit(solution)/shard_map/ppermute | solution.py:490
  163.4 4.8 %collective-permute-start.33 = (bf16[32,512]{1,0:T(8,128)(2,1)S(1)}, bf16[32,512]{1,0:T(8,128)(2,1)S(1)}, u32[]{:S(2)}, u32[]{:S(2)}) collective-permute-start(bf16[32,512]{1,0:T(8,128)(2,1)S(1)} %shard_map.127.refs_0_), channel_id=1, source_target_pairs={{0,4},{1,5},{2,6},{3,7},{4,0},{5,1},{6,2},{7,3},{8,12},{9,13},{10,... | collective-permute-start | bytes 98312 | tf_op jit(solution)/shard_map/ppermute | solution.py:490
  164.3 5.7 %collective-permute-start.34 = (bf16[32,512]{1,0:T(8,128)(2,1)S(1)}, bf16[32,512]{1,0:T(8,128)(2,1)S(1)}, u32[]{:S(2)}, u32[]{:S(2)}) collective-permute-start(bf16[32,512]{1,0:T(8,128)(2,1)S(1)} %shard_map.127.refs_0_), channel_id=1, source_target_pairs={{0,6},{1,7},{2,4},{3,5},{4,2},{5,3},{6,0},{7,1},{8,14},{9,15},{10,... | collective-permute-start | bytes 98312 | tf_op jit(solution)/shard_map/ppermute | solution.py:490
  170.0 5.0 %collective-permute-start.37 = (bf16[128,512]{1,0:T(8,128)(2,1)S(1)}, bf16[128,512]{1,0:T(8,128)(2,1)S(1)}, u32[]{:S(2)}, u32[]{:S(2)}) collective-permute-start(bf16[128,512]{1,0:T(8,128)(2,1)S(1)} %shard_map.128.refs_1_.refs_0_), channel_id=1, source_target_pairs={{0,8},{8,0},{16,24},{24,16},{1,9},{9,1},{17,25},{25,17},{2,10},{10... | collective-permute-start | bytes 393224 | tf_op jit(solution)/shard_map/ppermute | solution.py:501
  170.3 5.0 %collective-permute-start.38 = (bf16[128,512]{1,0:T(8,128)(2,1)S(1)}, bf16[128,512]{1,0:T(8,128)(2,1)S(1)}, u32[]{:S(2)}, u32[]{:S(2)}) collective-permute-start(bf16[128,512]{1,0:T(8,128)(2,1)S(1)} %shard_map.128.refs_1_.refs_0_), channel_id=1, source_target_pairs={{0,16},{8,24},{16,0},{24,8},{1,17},{9,25},{17,1},{25,9},{2,18},{10... | collective-permute-start | bytes 393224 | tf_op jit(solution)/shard_map/ppermute | solution.py:501
  171.1 5.9 %collective-permute-start.39 = (bf16[128,512]{1,0:T(8,128)(2,1)S(1)}, bf16[128,512]{1,0:T(8,128)(2,1)S(1)}, u32[]{:S(2)}, u32[]{:S(2)}) collective-permute-start(bf16[128,512]{1,0:T(8,128)(2,1)S(1)} %shard_map.128.refs_1_.refs_0_), channel_id=1, source_target_pairs={{0,24},{8,16},{16,8},{24,0},{1,25},{9,17},{17,9},{25,1},{2,26},{10... | collective-permute-start | bytes 393224 | tf_op jit(solution)/shard_map/ppermute | solution.py:501
  173.6 10.1 %collective-permute-start.35 = (bf16[2,256,512]{2,1,0:T(8,128)(2,1)S(1)}, bf16[2,256,512]{2,1,0:T(8,128)(2,1)S(1)}, u32[]{:S(2)}, u32[]{:S(2)}) collective-permute-start(bf16[2,256,512]{2,1,0:T(8,128)(2,1)S(1)} %shard_map.129), channel_id=1, source_target_pairs={{0,2},{1,3},{2,0},{3,1},{4,6},{5,7},{6,4},{7,5},{8,10},{9,11},{10,... | collective-permute-start | bytes 1572872 | tf_op jit(solution)/shard_map/ppermute | solution.py:490
  177.1 7.9 %collective-permute-start.40 = (bf16[512,512]{1,0:T(8,128)(2,1)S(1)}, bf16[512,512]{1,0:T(8,128)(2,1)S(1)}, u32[]{:S(2)}, u32[]{:S(2)}) collective-permute-start(bf16[512,512]{1,0:T(8,128)(2,1)S(1)} %shard_map.131.refs_0_), channel_id=1, source_target_pairs={{0,1},{1,0},{2,3},{3,2},{4,5},{5,4},{6,7},{7,6},{8,9},{9,8},{10,11... | collective-permute-start | bytes 1572872 | tf_op jit(solution)/shard_map/ppermute | solution.py:498

commit v8 on v7

--- a/solution.py
+++ b/solution.py
@@ -239,7 +239,7 @@
             outs[j][half] = (keep[i].astype(F32) + come[i].astype(F32)).astype(BF16)
 
 
-def pair_sum(keep, come):
+def pair_sum(keep, come, after=()):
     n = keep.shape[0] // 2
     return run(
         functools.partial(pair_sum_body, n),
@@ -247,6 +247,7 @@
         [VMEM] * 2,
         [shape((2, *keep.shape[1:]))] * n,
         mib=12,
+        after=after,
     )
 
 
@@ -450,14 +451,13 @@
         refs[n][part, :] = refs[j][...]
 
 
-def join(parts, axis, after=()):
+def join(parts, axis):
     rows, width = parts[0].shape
     return run(
         functools.partial(join_body, len(parts), axis),
         tuple(parts),
         [VMEM] * len(parts),
         [shape((rows * len(parts), width))],
-        after=after,
     )[0]
 
 
@@ -467,13 +467,18 @@
     second[...] = jnp.where(core == 0, other[...].astype(F32), mine[...].astype(F32))
 
 
-def select(mine, other):
-    return run(select_body, (mine, other), [VMEM] * 2, [shape(mine.shape, F32)] * 2)
+def select(mine, other, after):
+    return run(
+        select_body, (mine, other), [VMEM] * 2, [shape(mine.shape, F32)] * 2, after=after
+    )
 
 
 COST = {
+    scale_body: 36,
+    prepare_body: 36,
     forward_body: 36,
     grad_body: 36,
+    second_body: 36,
 }
 
 
@@ -500,24 +505,17 @@
     def row_flip(value, j):
         return lax.ppermute(value, "row", [(a, a ^ j) for a in range(n_row)])
 
-    def scatter_begin(own, after=()):
+    def scatter_line(own, after=()):
         if line != 4:
-            return own[2], None
+            return [own[0]] + [line_flip(own[j], j) for j in range(1, line)], own[:2]
         to_three = col_send(own[3], [(0, 1), (3, 2)])
         to_two = col_send(own[2], [(0, 1), (3, 2)])
-        return sum_parts([own[2], to_three], after), to_two
-
-    def scatter_next(own, begun, after):
-        if line != 4:
-            return own[3], []
-        crossing = sum_parts([own[3], begun[1]], after)
-        onward = col_send(begun[0], [(1, 3), (2, 0)])
-        return crossing, [col_send(crossing, [(1, 2), (2, 1)]), onward]
-
-    def scatter_end(own, arrived, near):
-        if line != 4:
-            return [own[0]] + [line_flip(own[j], j) for j in range(1, line)]
-        return [own[0], line_flip(near, 1), *arrived]
+        crossing = sum_parts([own[2], to_three])
+        meeting = sum_parts([own[3], to_two], (crossing, *after))
+        crossed = col_send(crossing, [(1, 2), (2, 1)])
+        met = col_send(meeting, [(1, 2), (2, 1)])
+        outward = sum_parts([own[1], crossed])
+        return [own[0], line_flip(outward, 1), met], (meeting, outward)
 
     def gather_row(pair):
         if n_row != 4:
@@ -551,46 +549,38 @@
     if early:
         early = relay(early, (give,))
     own = pair_sum(keep, core_flip(give))
-    begun = scatter_begin(own)
-    crossing, arrived = scatter_next(own, begun, begun[:1])
-    parts = scatter_end(own, arrived, own[1])
+    parts, late = scatter_line(own)
     if early:
-        late = (crossing, arrived[1])
-        gathered = gather_far(scaled, *early, begun[:1], late)
+        gathered = gather_far(scaled, *early, (own[0],), late)
     else:
         gathered = [scaled] + [line_flip(scaled, j) for j in range(1, line)]
     ranged = [x for g in gathered for x in (g, core_flip(g))]
     hidden = backward(t_number, t_entries, tiles, ranged)
     spread = gather_row(aggregate(parts, scale, (hidden,)))
-    stacked = first_layer(spread[:1], scale, w_first)
-    sums = weight_grads(0, hidden, *stacked, scale, w_first, w_second)
-    stacked = first_layer(spread[1:-1], scale, w_first, stacked, sums[:1])
-    aggs, outs = first_layer(spread[-1:], scale, w_first, stacked)
-
-    give = forward(number, entries, tiles, outs, False, 1)
-    keep = forward(number, entries, tiles, outs, False, 0)
-    own = pair_sum(keep, core_flip(give))
-
-    give, keep = weight_grads(2, hidden, aggs, outs, scale, w_first, w_second, sums, (own[0],))
-    begun = scatter_begin(own, (keep,))
-    split = split_sum([keep, core_flip(give)], n_row, "row", begun[:1])
+    sums, stacked = (), ()
+    for group in (spread[:1], spread[1:-1], spread[-1:]):
+        start = stacked[0].shape[0] if stacked else 0
+        stacked = first_layer(group, scale, w_first, stacked, sums[:1])
+        sums = weight_grads(start, hidden, *stacked, scale, w_first, w_second, sums)
+
+    give, keep = sums
+    split = split_sum([keep, core_flip(give)], n_row, "row")
     moment = [split[0]] + [row_flip(split[j], j) for j in range(1, n_row)]
-    crossing, arrived = scatter_next(own, begun, moment[1:])
-    if moment[0].shape[0] % (16 * line) == 0:
-        split = split_sum(moment, line, "line", (crossing,))
-        moment = sum_parts(
-            [split[0]] + [line_flip(split[j], j) for j in range(1, line)], arrived[1:]
-        )
+    give = forward(number, entries, tiles, stacked[1], False, 1, (keep,))
+    keep = forward(number, entries, tiles, stacked[1], False, 0, (split[0],))
+    if split[0].shape[0] % (16 * line) == 0:
+        split = split_sum(moment, line, "line")
+        moment = sum_parts([split[0]] + [line_flip(split[j], j) for j in range(1, line)])
         moment = join([moment] + [line_flip(moment, j) for j in range(1, line)], "line")
     else:
-        moment = sum_parts(moment)
-        moment = sum_parts([moment] + [line_flip(moment, j) for j in range(1, line)])
-    (near,) = relay(own[1:2], (moment,))
+        split = [sum_parts(moment)]
+        moment = sum_parts(split + [line_flip(split[0], j) for j in range(1, line)])
+    own = pair_sum(keep, core_flip(give), split[:1])
+    parts, _ = scatter_line(own, (moment,))
     moment = [moment] + [row_flip(moment, j) for j in range(1, n_row)]
-    mine = join(moment, "row", arrived[:1])
-    grad_first, grad_second = select(mine, core_flip(mine))
-    parts = scatter_end(own, arrived, near)
-    return second_layer(parts, scale, w_second), grad_first, grad_second
+    mine = join(moment, "row")
+    logits = second_layer(parts, scale, w_second)
+    return logits, *select(mine, core_flip(mine), (logits,))
 
 
 def solution(mesh):

time: 186 us -> 167 us (0.90); the launches traced: 186 us -> 165 us
  waiting for transfers between devices: 84.8 us -> 61.1 us
  Pallas kernels: 36.7 us -> 44.2 us
  local copies, waits for them, and re-layouts: 6.79 us -> 2.81 us
    ppermute x21, waiting for transfers between devices: 68.2 us -> 46.9 us  [col_send(): lax.ppermute(value, 'col', [(2 * a + k, 2 * b + k) for a, b in pairs for...]
    pallas_call x30 -> x32, Pallas kernels: 36.7 us -> 44.2 us  [run(): pl.pallas_call(whole, out_shape=outs, in_specs=specs + [ANY] * extra, out...]
    unnamed x17, local copies, waits for them, and re-layouts: 6.79 us -> 2.81 us
    ppermute x8, waiting for transfers between devices: 2.95 us -> 1.06 us  [core_flip(): return lax.ppermute(value, 'col', [(a, a ^ 1) for a in range(n_col)])]
  transfers between devices with their start and end apart: 41 -> 41, of which waited for: 22 -> 19; matrix products, arithmetic and copies ran while one was open for 0% -> 0% of each run, Pallas kernels for 16% -> 23%
where the time goes in v8:
time: 167 us; the launch traced here: 165 us
  waiting for transfers between devices  61.1 us (37%)
  starting transfers between devices  55.4 us (33%)
  Pallas kernels  44.2 us (26%)
  local copies, waits for them, and re-layouts  2.81 us (2%)
  between operations  1.82 us (1%)
    ppermute x21, waiting for transfers between devices, col_send(): lax.ppermute(value, 'col', [(2 * a + k, 2 * b + k) for a, b in pairs for...  46.9 us
    pallas_call x32, Pallas kernels, run(): pl.pallas_call(whole, out_shape=outs, in_specs=specs + [ANY] * extra, out...  44.2 us
    ppermute x21, starting transfers between devices, col_send(): lax.ppermute(value, 'col', [(2 * a + k, 2 * b + k) for a, b in pairs for...  40.9 us
    ppermute x12, starting transfers between devices, row_flip(): return lax.ppermute(value, 'row', [(a, a ^ j) for a in range(n_row)])  13.7 us
    ppermute x12, waiting for transfers between devices, row_flip(): return lax.ppermute(value, 'row', [(a, a ^ j) for a in range(n_row)])  13.1 us
  transfers between devices with their start and end apart: 41, of which 19 were waited for; matrix products, arithmetic and copies ran while one was open for 0% of the time, Pallas kernels for 23%

profile of v8, /device:TPU:0, one launch (start us, length us, event | category | flops | bytes accessed | tf_op | source)
XLA Modules:
  0.0 165.4 jit_solution(311618993566847174)
XLA Ops:
  0.6 0.7 copy.13
  1.3 1.0 copy-done.3
  2.9 0.8 collective-permute-start.8
  3.8 6.0 %collective-permute-start.7 = (bf16[2,512,256]{2,1,0:T(8,128)(2,1)S(1)}, bf16[2,512,256]{2,1,0:T(8,128)(2,1)S(1)}, u32[]{:S(2)}, u32[]{:S(2)}) collective-permute-start(bf16[2,512,256]{2,1,0:T(8,128)(2,1)S(1)} %get-tuple-element.56.refs_3_), channel_id=1, source_target_pairs={{0,2},{1,3},{2,0},{3,1},{4,6},{5,7},{6,4},{7,5},{8,10},{9,11},{10,... | collective-permute-start | bytes 1572872 | tf_op jit(solution)/shard_map/ppermute | solution.py:495
  10.5 2.6 %shard_map.104 = (bf16[8,256,512]{2,1,0:T(8,128)(2,1)S(1)}, s32[16]{0:T(128)S(1)}, s32[128]{0:T(128)S(1)}, s32[8]{0:T(128)S(1)}, s32[128]{0:T(128)S(1)}) custom-call(s32[1]{0:T(128)} %bitcast.7.refs_0_, s32[48]{0:T(128)S(1)} %bitcast.17, bf16[8,256,512]{2,1,0:T(8,128)(2,1)S(1)} %bitcast.16, f32[8,256,128]{2,1,0:T(8,128)S(1)} %get-tuple-element.46.refs_3_.refs_2_.refs_4_), custom_call_target="tpu_custom_call" | custom-call | flops 35999997952 | tf_op jit(solution)/shard_map/pallas_call | solution.py:24
  13.1 4.3 %shard_map.106.refs_2_ = bf16[8,256,512]{2,1,0:T(8,128)(2,1)S(1)} custom-call(s32[16]{0:T(128)S(1)} %get-tuple-element.47.refs_0_, s32[128]{0:T(128)S(1)} %get-tuple-element.48.refs_1_, bf16[48,256,256]{2,1,0:T(8,128)(2,1)S(1)} %bitcast.10, bf16[8,256,512]{2,1,0:T(8,128)(2,1)S(1)} %get-tuple-element.49.refs_3_), custom_call_target="tpu_custom_call" | custom-call | flops 35999997952 | tf_op jit(solution)/shard_map/pallas_call | solution.py:24
  17.5 3.7 %shard_map.105.refs_0_ = bf16[8,256,512]{2,1,0:T(8,128)(2,1)S(1)} custom-call(s32[16]{0:T(128)S(1)} %get-tuple-element.47.refs_0_, s32[128]{0:T(128)S(1)} %get-tuple-element.48.refs_1_, bf16[48,256,256]{2,1,0:T(8,128)(2,1)S(1)} %bitcast.11, bf16[8,256,512]{2,1,0:T(8,128)(2,1)S(1)} %get-tuple-element.49.refs_3_), custom_call_target="tpu_custom_call" | custom-call | flops 35999997952 | tf_op jit(solution)/shard_map/pallas_call | solution.py:24
  22.1 1.3 collective-permute-start.1
  23.5 0.7 collective-permute-start.10
  24.2 1.3 collective-permute-start.11
  25.5 4.6 %collective-permute-start.4 = (bf16[2,256,512]{2,1,0:T(8,128)(2,1)S(1)}, bf16[2,256,512]{2,1,0:T(8,128)(2,1)S(1)}, u32[]{:S(2)}, u32[]{:S(2)}) collective-permute-start(bf16[2,256,512]{2,1,0:T(8,128)(2,1)S(1)} %get-tuple-element.52.refs_0_), channel_id=1, source_target_pairs={{0,2},{1,3},{6,4},{7,5},{8,10},{9,11},{14,12},{15,13},{16,18},{17,... | collective-permute-start | bytes 1572872 | tf_op jit(solution)/shard_map/ppermute | solution.py:495
  30.2 5.5 %collective-permute-done.1.refs_1_ = bf16[2,256,512]{2,1,0:T(8,128)(2,1)S(1)} collective-permute-done((bf16[2,256,512]{2,1,0:T(8,128)(2,1)S(1)}, bf16[2,256,512]{2,1,0:T(8,128)(2,1)S(1)}, u32[]{:S(2)}, u32[]{:S(2)}) %collective-permute-start.1) | collective-permute-done | bytes 524320 | tf_op jit(solution)/shard_map/ppermute | solution.py:495
  35.8 0.7 collective-permute-start.2
  36.5 1.3 collective-permute-start.12
  37.9 8.5 %collective-permute-done.4.refs_1_ = bf16[2,256,512]{2,1,0:T(8,128)(2,1)S(1)} collective-permute-done((bf16[2,256,512]{2,1,0:T(8,128)(2,1)S(1)}, bf16[2,256,512]{2,1,0:T(8,128)(2,1)S(1)}, u32[]{:S(2)}, u32[]{:S(2)}) %collective-permute-start.4) | collective-permute-done | bytes 524320 | tf_op jit(solution)/shard_map/ppermute | solution.py:495
  46.7 6.1 %collective-permute-done.12.refs_3_ = bf16[2,512,256]{2,1,0:T(8,128)(2,1)S(1)} collective-permute-done((bf16[2,512,256]{2,1,0:T(8,128)(2,1)S(1)}, bf16[2,512,256]{2,1,0:T(8,128)(2,1)S(1)}, u32[]{:S(2)}, u32[]{:S(2)}) %collective-permute-start.12) | collective-permute-done | bytes 524320 | tf_op jit(solution)/shard_map/ppermute | solution.py:495
  53.4 0.7 collective-permute-start.5
  54.1 2.6 %collective-permute-start.3 = (bf16[2,256,512]{2,1,0:T(8,128)(2,1)S(1)}, bf16[2,256,512]{2,1,0:T(8,128)(2,1)S(1)}, u32[]{:S(2)}, u32[]{:S(2)}) collective-permute-start(bf16[2,256,512]{2,1,0:T(8,128)(2,1)S(1)} %shard_map.109.refs_5_), channel_id=1, source_target_pairs={{0,2},{1,3},{2,0},{3,1},{4,6},{5,7},{6,4},{7,5},{8,10},{9,11},{10,... | collective-permute-start | bytes 1572872 | tf_op jit(solution)/shard_map/ppermute | solution.py:495
  56.7 8.1 %shard_map.114.refs_4_.refs_0_ = bf16[8,512,256]{2,1,0:T(8,128)(2,1)S(1)} custom-call(s32[8]{0:T(128)S(1)} %get-tuple-element.54.refs_0_, s32[128]{0:T(128)S(1)} %get-tuple-element.55.refs_1_, bf16[48,256,256]{2,1,0:T(8,128)(2,1)S(1)} %bitcast.12, bf16[2,512,256]{2,1,0:T(8,128)(2,1)S(1)} %get-tuple-element.56.refs_3_, ...), custom_call_target="tpu_custom_call" | custom-call | tf_op jit(solution)/shard_map/pallas_call | solution.py:24
  64.8 3.8 %collective-permute-done.3.refs_1_ = bf16[2,256,512]{2,1,0:T(8,128)(2,1)S(1)} collective-permute-done((bf16[2,256,512]{2,1,0:T(8,128)(2,1)S(1)}, bf16[2,256,512]{2,1,0:T(8,128)(2,1)S(1)}, u32[]{:S(2)}, u32[]{:S(2)}) %collective-permute-start.3) | collective-permute-done | bytes 524320 | tf_op jit(solution)/shard_map/ppermute | solution.py:495
  68.8 0.9 collective-permute-start.20
  69.7 0.8 collective-permute-start.15
  70.5 1.2 collective-permute-start.19
  71.7 1.2 collective-permute-start.17
  72.9 0.6 shard_map.116
  73.6 2.2 %shard_map.117 = (f32[512,512]{1,0:T(8,128)S(1)}, f32[512,512]{1,0:T(8,128)S(1)}) custom-call(bf16[8,512,256]{2,1,0:T(8,128)(2,1)S(1)} %shard_map.114.refs_4_.refs_0_, bf16[2,256,512]{2,1,0:T(8,128)(2,1)S(1)} %get-tuple-element.63.refs_1_.refs_6_, bf16[2,256,512]{2,1,0:T(8,128)(2,1)S(1)} %get-tuple-element.64.refs_2_.refs_7_, ...), custom_call_target="tpu_custom_call" | custom-call | flops 35999997952 | tf_op jit(solution)/shard_map/pallas_call | solution.py:24
  75.8 3.1 %collective-permute-done.15.refs_0_ = bf16[256,512]{1,0:T(8,128)(2,1)S(1)} collective-permute-done((bf16[256,512]{1,0:T(8,128)(2,1)S(1)}, bf16[256,512]{1,0:T(8,128)(2,1)S(1)}, u32[]{:S(2)}, u32[]{:S(2)}) %collective-permute-start.15) | collective-permute-done | bytes 262176 | tf_op jit(solution)/shard_map/ppermute | solution.py:506
  78.9 1.2 collective-permute-start.16
  80.1 3.6 %collective-permute-done.17.refs_3_ = bf16[256,512]{1,0:T(8,128)(2,1)S(1)} collective-permute-done((bf16[256,512]{1,0:T(8,128)(2,1)S(1)}, bf16[256,512]{1,0:T(8,128)(2,1)S(1)}, u32[]{:S(2)}, u32[]{:S(2)}) %collective-permute-start.17) | collective-permute-done | bytes 262176 | tf_op jit(solution)/shard_map/ppermute | solution.py:506
  83.7 0.8 collective-permute-start.18
  84.6 1.1 shard_map.118
  85.7 4.3 %shard_map.119 = (f32[512,512]{1,0:T(8,128)S(1)}, f32[512,512]{1,0:T(8,128)S(1)}) custom-call(bf16[8,512,256]{2,1,0:T(8,128)(2,1)S(1)} %shard_map.114.refs_4_.refs_0_, bf16[6,256,512]{2,1,0:T(8,128)(2,1)S(1)} %get-tuple-element.66.refs_1_.refs_4_, bf16[6,256,512]{2,1,0:T(8,128)(2,1)S(1)} %get-tuple-element.67.refs_2_.refs_5_, ...), custom_call_target="tpu_custom_call" | custom-call | flops 35999997952 | tf_op jit(solution)/shard_map/pallas_call | solution.py:24
  90.1 0.9 shard_map.120
  91.0 2.4 %shard_map.121 = (bf16[512,512]{1,0:T(8,128)(2,1)S(1)}, bf16[512,512]{1,0:T(8,128)(2,1)S(1)}) custom-call(bf16[8,512,256]{2,1,0:T(8,128)(2,1)S(1)} %shard_map.114.refs_4_.refs_0_, bf16[8,256,512]{2,1,0:T(8,128)(2,1)S(1)} %get-tuple-element.71.refs_1_, bf16[8,256,512]{2,1,0:T(8,128)(2,1)S(1)} %get-tuple-element.70.refs_2_.refs_3_, ...), custom_call_target="tpu_custom_call" | custom-call | flops 35999997952 | tf_op jit(solution)/shard_map/pallas_call | solution.py:24
  93.5 4.3 %shard_map.124 = bf16[8,256,512]{2,1,0:T(8,128)(2,1)S(1)} custom-call(s32[16]{0:T(128)S(1)} %get-tuple-element.47.refs_0_, s32[128]{0:T(128)S(1)} %get-tuple-element.48.refs_1_, bf16[48,256,256]{2,1,0:T(8,128)(2,1)S(1)} %bitcast.13, bf16[8,256,512]{2,1,0:T(8,128)(2,1)S(1)} %get-tuple-element.70.refs_2_.refs_3_, ...), custom_call_target="tpu_custom_call" | custom-call | flops 35999997952 | tf_op jit(solution)/shard_map/pallas_call | solution.py:24
  98.0 1.5 collective-permute-start.23
  99.5 0.7 collective-permute-start.24
  100.2 1.3 collective-permute-start.25
  101.6 3.9 %shard_map.123.refs_0_ = bf16[8,256,512]{2,1,0:T(8,128)(2,1)S(1)} custom-call(s32[16]{0:T(128)S(1)} %get-tuple-element.47.refs_0_, s32[128]{0:T(128)S(1)} %get-tuple-element.48.refs_1_, bf16[48,256,256]{2,1,0:T(8,128)(2,1)S(1)} %bitcast.14, bf16[8,256,512]{2,1,0:T(8,128)(2,1)S(1)} %get-tuple-element.70.refs_2_.refs_3_, ...), custom_call_target="tpu_custom_call" | custom-call | flops 35999997952 | tf_op jit(solution)/shard_map/pallas_call | solution.py:24
  105.5 1.9 %collective-permute-done.24.refs_2_ = bf16[128,512]{1,0:T(8,128)(2,1)S(1)} collective-permute-done((bf16[128,512]{1,0:T(8,128)(2,1)S(1)}, bf16[128,512]{1,0:T(8,128)(2,1)S(1)}, u32[]{:S(2)}, u32[]{:S(2)}) %collective-permute-start.24) | collective-permute-done | bytes 131104 | tf_op jit(solution)/shard_map/ppermute | solution.py:506
  108.0 2.9 %collective-permute-start.26 = (bf16[2,256,512]{2,1,0:T(8,128)(2,1)S(1)}, bf16[2,256,512]{2,1,0:T(8,128)(2,1)S(1)}, u32[]{:S(2)}, u32[]{:S(2)}) collective-permute-start(bf16[2,256,512]{2,1,0:T(8,128)(2,1)S(1)} %get-tuple-element.83.refs_0_), channel_id=1, source_target_pairs={{0,2},{1,3},{6,4},{7,5},{8,10},{9,11},{14,12},{15,13},{16,18},{17,... | collective-permute-start | bytes 1572872 | tf_op jit(solution)/shard_map/ppermute | solution.py:495
  111.0 1.3 collective-permute-start.29
  112.3 11.0 %collective-permute-done.26.refs_1_ = bf16[2,256,512]{2,1,0:T(8,128)(2,1)S(1)} collective-permute-done((bf16[2,256,512]{2,1,0:T(8,128)(2,1)S(1)}, bf16[2,256,512]{2,1,0:T(8,128)(2,1)S(1)}, u32[]{:S(2)}, u32[]{:S(2)}) %collective-permute-start.26) | collective-permute-done | bytes 524320 | tf_op jit(solution)/shard_map/ppermute | solution.py:495
  123.4 0.7 collective-permute-start.27
  124.1 5.1 %collective-permute-start.30 = (bf16[32,512]{1,0:T(8,128)(2,1)S(1)}, bf16[32,512]{1,0:T(8,128)(2,1)S(1)}, u32[]{:S(2)}, u32[]{:S(2)}) collective-permute-start(bf16[32,512]{1,0:T(8,128)(2,1)S(1)} %get-tuple-element.84), channel_id=1, source_target_pairs={{0,2},{1,3},{2,0},{3,1},{4,6},{5,7},{6,4},{7,5},{8,10},{9,11},{10,... | collective-permute-start | bytes 98312 | tf_op jit(solution)/shard_map/ppermute | solution.py:495
  129.4 2.3 %collective-permute-start.32 = (bf16[32,512]{1,0:T(8,128)(2,1)S(1)}, bf16[32,512]{1,0:T(8,128)(2,1)S(1)}, u32[]{:S(2)}, u32[]{:S(2)}) collective-permute-start(bf16[32,512]{1,0:T(8,128)(2,1)S(1)} %get-tuple-element.86), channel_id=1, source_target_pairs={{0,6},{1,7},{2,4},{3,5},{4,2},{5,3},{6,0},{7,1},{8,14},{9,15},{10,... | collective-permute-start | bytes 98312 | tf_op jit(solution)/shard_map/ppermute | solution.py:495
  131.7 2.3 %collective-permute-done.30.refs_1_ = bf16[32,512]{1,0:T(8,128)(2,1)S(1)} collective-permute-done((bf16[32,512]{1,0:T(8,128)(2,1)S(1)}, bf16[32,512]{1,0:T(8,128)(2,1)S(1)}, u32[]{:S(2)}, u32[]{:S(2)}) %collective-permute-start.30) | collective-permute-done | bytes 32800 | tf_op jit(solution)/shard_map/ppermute | solution.py:495
  134.0 7.2 %collective-permute-done.31.refs_2_ = bf16[32,512]{1,0:T(8,128)(2,1)S(1)} collective-permute-done((bf16[32,512]{1,0:T(8,128)(2,1)S(1)}, bf16[32,512]{1,0:T(8,128)(2,1)S(1)}, u32[]{:S(2)}, u32[]{:S(2)}) %collective-permute-start.31) | collective-permute-done | bytes 32800 | tf_op jit(solution)/shard_map/ppermute | solution.py:495
  141.2 1.2 collective-permute-start.35
  142.4 1.2 collective-permute-start.34
  143.6 2.0 %collective-permute-start.33 = (bf16[32,512]{1,0:T(8,128)(2,1)S(1)}, bf16[32,512]{1,0:T(8,128)(2,1)S(1)}, u32[]{:S(2)}, u32[]{:S(2)}) collective-permute-start(bf16[32,512]{1,0:T(8,128)(2,1)S(1)} %shard_map.129.refs_0_), channel_id=1, source_target_pairs={{0,2},{1,3},{2,0},{3,1},{4,6},{5,7},{6,4},{7,5},{8,10},{9,11},{10,... | collective-permute-start | bytes 98312 | tf_op jit(solution)/shard_map/ppermute | solution.py:495
  145.6 1.5 collective-permute-done.35.refs_3_
  147.1 1.1 collective-permute-done.34.refs_2_
  148.5 0.7 collective-permute-start.36
  149.3 3.2 %collective-permute-start.28 = (bf16[2,256,512]{2,1,0:T(8,128)(2,1)S(1)}, bf16[2,256,512]{2,1,0:T(8,128)(2,1)S(1)}, u32[]{:S(2)}, u32[]{:S(2)}) collective-permute-start(bf16[2,256,512]{2,1,0:T(8,128)(2,1)S(1)} %shard_map.128), channel_id=1, source_target_pairs={{0,2},{1,3},{2,0},{3,1},{4,6},{5,7},{6,4},{7,5},{8,10},{9,11},{10,... | collective-permute-start | bytes 1572872 | tf_op jit(solution)/shard_map/ppermute | solution.py:495
  152.5 2.1 %collective-permute-start.39 = (bf16[128,512]{1,0:T(8,128)(2,1)S(1)}, bf16[128,512]{1,0:T(8,128)(2,1)S(1)}, u32[]{:S(2)}, u32[]{:S(2)}) collective-permute-start(bf16[128,512]{1,0:T(8,128)(2,1)S(1)} %shard_map.130.refs_3_.refs_0_), channel_id=1, source_target_pairs={{0,24},{8,16},{16,8},{24,0},{1,25},{9,17},{17,9},{25,1},{2,26},{10... | collective-permute-start | bytes 393224 | tf_op jit(solution)/shard_map/ppermute | solution.py:506
  155.0 1.4 collective-permute-start.37
  156.4 1.9 %collective-permute-done.39.refs_3_ = bf16[128,512]{1,0:T(8,128)(2,1)S(1)} collective-permute-done((bf16[128,512]{1,0:T(8,128)(2,1)S(1)}, bf16[128,512]{1,0:T(8,128)(2,1)S(1)}, u32[]{:S(2)}, u32[]{:S(2)}) %collective-permute-start.39) | collective-permute-done | bytes 131104 | tf_op jit(solution)/shard_map/ppermute | solution.py:506
  158.4 1.4 collective-permute-done.38.refs_2_
  159.8 1.1 collective-permute-done.37.refs_1_
  161.0 1.3 shard_map.132.refs_2_
  162.2 0.6 collective-permute-done.40.refs_1_
  162.9 1.0 copy-done.1
  163.9 1.5 shard_map.134
  (68 shorter events, 5.2 us)
Async XLA Ops:
  1.3 1.0 copy-start.3
  2.4 8.1 %copy-start.2 = (bf16[4,1,512,512]{3,2,1,0:T(8,128)(2,1)S(1)}, bf16[4,1,512,512]{3,2,1,0:T(8,128)(2,1)}, u32[]{:S(2)}) copy-start(bf16[4,1,512,512]{3,2,1,0:T(8,128)(2,1)} %param.8) | copy-start | bytes 6291460
  2.4 8.1 %copy-start.5 = (s32[1,1,48]{2,1,0:T(1,128)S(1)}, s32[1,1,48]{2,1,0:T(1,128)}, u32[]{:S(2)}) copy-start(s32[1,1,48]{2,1,0:T(1,128)} %param.11) | copy-start | bytes 580
  2.4 10.7 %slice-start = ((s8[6291456]{0:T(1024)(128)(4,1)}), s8[4194304]{0:T(1024)(128)(4,1)S(1)}, s32[]{:S(2)}) async-start(s8[6291456]{0:T(1024)(128)(4,1)} %bitcast.8), calls=%async_computation | async-start | bytes 8388608
  2.9 20.5 %collective-permute-start.8 = (bf16[2,512,256]{2,1,0:T(8,128)(2,1)S(1)}, bf16[2,512,256]{2,1,0:T(8,128)(2,1)S(1)}, u32[]{:S(2)}, u32[]{:S(2)}) collective-permute-start(bf16[2,512,256]{2,1,0:T(8,128)(2,1)S(1)} %get-tuple-element.56.refs_3_), channel_id=1, source_target_pairs={{2,4},{3,5},{4,2},{5,3},{10,12},{11,13},{12,10},{13,11},{18,20},{1... | collective-permute-start | bytes 1572872 | tf_op jit(solution)/shard_map/ppermute | solution.py:495
  3.8 19.7 %collective-permute-start.7 = (bf16[2,512,256]{2,1,0:T(8,128)(2,1)S(1)}, bf16[2,512,256]{2,1,0:T(8,128)(2,1)S(1)}, u32[]{:S(2)}, u32[]{:S(2)}) collective-permute-start(bf16[2,512,256]{2,1,0:T(8,128)(2,1)S(1)} %get-tuple-element.56.refs_3_), channel_id=1, source_target_pairs={{0,2},{1,3},{2,0},{3,1},{4,6},{5,7},{6,4},{7,5},{8,10},{9,11},{10,... | collective-permute-start | bytes 1572872 | tf_op jit(solution)/shard_map/ppermute | solution.py:495
  10.4 2.7 %slice-start.1 = ((s8[6291456]{0:T(1024)(128)(4,1)}), s8[2097152]{0:T(1024)(128)(4,1)S(1)}, s32[]{:S(2)}) async-start(s8[6291456]{0:T(1024)(128)(4,1)} %bitcast.8), calls=%async_computation.1 | async-start | bytes 4194304
  17.4 4.2 %collective-permute-start = (bf16[8,256,512]{2,1,0:T(8,128)(2,1)S(1)}, bf16[8,256,512]{2,1,0:T(8,128)(2,1)S(1)}, u32[]{:S(2)}, u32[]{:S(2)}) collective-permute-start(bf16[8,256,512]{2,1,0:T(8,128)(2,1)S(1)} %shard_map.106.refs_2_), channel_id=1, source_target_pairs={{0,1},{1,0},{2,3},{3,2},{4,5},{5,4},{6,7},{7,6},{8,9},{9,8},{10,11... | collective-permute-start | bytes 6291464 | tf_op jit(solution)/shard_map/ppermute | solution.py:503
  22.1 13.5 %collective-permute-start.1 = (bf16[2,256,512]{2,1,0:T(8,128)(2,1)S(1)}, bf16[2,256,512]{2,1,0:T(8,128)(2,1)S(1)}, u32[]{:S(2)}, u32[]{:S(2)}) collective-permute-start(bf16[2,256,512]{2,1,0:T(8,128)(2,1)S(1)} %get-tuple-element.53.refs_0_), channel_id=1, source_target_pairs={{0,2},{1,3},{6,4},{7,5},{8,10},{9,11},{14,12},{15,13},{16,18},{17,... | collective-permute-start | bytes 1572872 | tf_op jit(solution)/shard_map/ppermute | solution.py:495
  23.5 12.9 %collective-permute-start.10 = (bf16[2,512,256]{2,1,0:T(8,128)(2,1)S(1)}, bf16[2,512,256]{2,1,0:T(8,128)(2,1)S(1)}, u32[]{:S(2)}, u32[]{:S(2)}) collective-permute-start(bf16[2,512,256]{2,1,0:T(8,128)(2,1)S(1)} %get-tuple-element.57.refs_5_), channel_id=1, source_target_pairs={{2,4},{3,5},{4,2},{5,3},{10,12},{11,13},{12,10},{13,11},{18,20},{1... | collective-permute-start | bytes 1572872 | tf_op jit(solution)/shard_map/ppermute | solution.py:495
  24.2 22.4 %collective-permute-start.11 = (bf16[2,512,256]{2,1,0:T(8,128)(2,1)S(1)}, bf16[2,512,256]{2,1,0:T(8,128)(2,1)S(1)}, u32[]{:S(2)}, u32[]{:S(2)}) collective-permute-start(bf16[2,512,256]{2,1,0:T(8,128)(2,1)S(1)} %get-tuple-element.58.refs_1_), channel_id=1, source_target_pairs={{2,0},{3,1},{4,6},{5,7},{10,8},{11,9},{12,14},{13,15},{18,16},{19,... | collective-permute-start | bytes 1572872 | tf_op jit(solution)/shard_map/ppermute | solution.py:495
  25.5 20.8 %collective-permute-start.4 = (bf16[2,256,512]{2,1,0:T(8,128)(2,1)S(1)}, bf16[2,256,512]{2,1,0:T(8,128)(2,1)S(1)}, u32[]{:S(2)}, u32[]{:S(2)}) collective-permute-start(bf16[2,256,512]{2,1,0:T(8,128)(2,1)S(1)} %get-tuple-element.52.refs_0_), channel_id=1, source_target_pairs={{0,2},{1,3},{6,4},{7,5},{8,10},{9,11},{14,12},{15,13},{16,18},{17,... | collective-permute-start | bytes 1572872 | tf_op jit(solution)/shard_map/ppermute | solution.py:495
  35.8 10.8 %collective-permute-start.2 = (bf16[2,256,512]{2,1,0:T(8,128)(2,1)S(1)}, bf16[2,256,512]{2,1,0:T(8,128)(2,1)S(1)}, u32[]{:S(2)}, u32[]{:S(2)}) collective-permute-start(bf16[2,256,512]{2,1,0:T(8,128)(2,1)S(1)} %shard_map.108.refs_2_), channel_id=1, source_target_pairs={{2,4},{3,5},{4,2},{5,3},{10,12},{11,13},{12,10},{13,11},{18,20},{1... | collective-permute-start | bytes 1572872 | tf_op jit(solution)/shard_map/ppermute | solution.py:495
  36.5 16.2 %collective-permute-start.12 = (bf16[2,512,256]{2,1,0:T(8,128)(2,1)S(1)}, bf16[2,512,256]{2,1,0:T(8,128)(2,1)S(1)}, u32[]{:S(2)}, u32[]{:S(2)}) collective-permute-start(bf16[2,512,256]{2,1,0:T(8,128)(2,1)S(1)} %shard_map.112.refs_0_), channel_id=1, source_target_pairs={{2,0},{3,1},{4,6},{5,7},{10,8},{11,9},{12,14},{13,15},{18,16},{19,... | collective-permute-start | bytes 1572872 | tf_op jit(solution)/shard_map/ppermute | solution.py:495
  37.8 16.3 %collective-permute-start.6 = (bf16[2,512,256]{2,1,0:T(8,128)(2,1)S(1)}, bf16[2,512,256]{2,1,0:T(8,128)(2,1)S(1)}, u32[]{:S(2)}, u32[]{:S(2)}) collective-permute-start(bf16[2,512,256]{2,1,0:T(8,128)(2,1)S(1)} %get-tuple-element.56.refs_3_), channel_id=1, source_target_pairs={{0,1},{1,0},{2,3},{3,2},{4,5},{5,4},{6,7},{7,6},{8,9},{9,8},{10,11... | collective-permute-start | bytes 1572872 | tf_op jit(solution)/shard_map/ppermute | solution.py:503
  46.4 10.3 %collective-permute-start.9 = (bf16[2,512,256]{2,1,0:T(8,128)(2,1)S(1)}, bf16[2,512,256]{2,1,0:T(8,128)(2,1)S(1)}, u32[]{:S(2)}, u32[]{:S(2)}) collective-permute-start(bf16[2,512,256]{2,1,0:T(8,128)(2,1)S(1)} %get-tuple-element.57.refs_5_), channel_id=1, source_target_pairs={{0,1},{1,0},{2,3},{3,2},{4,5},{5,4},{6,7},{7,6},{8,9},{9,8},{10,11... | collective-permute-start | bytes 1572872 | tf_op jit(solution)/shard_map/ppermute | solution.py:503
  52.8 3.8 %collective-permute-start.13 = (bf16[2,512,256]{2,1,0:T(8,128)(2,1)S(1)}, bf16[2,512,256]{2,1,0:T(8,128)(2,1)S(1)}, u32[]{:S(2)}, u32[]{:S(2)}) collective-permute-start(bf16[2,512,256]{2,1,0:T(8,128)(2,1)S(1)} %get-tuple-element.59.refs_7_), channel_id=1, source_target_pairs={{0,1},{1,0},{2,3},{3,2},{4,5},{5,4},{6,7},{7,6},{8,9},{9,8},{10,11... | collective-permute-start | bytes 1572872 | tf_op jit(solution)/shard_map/ppermute | solution.py:503
  52.9 3.8 %collective-permute-start.14 = (bf16[2,512,256]{2,1,0:T(8,128)(2,1)S(1)}, bf16[2,512,256]{2,1,0:T(8,128)(2,1)S(1)}, u32[]{:S(2)}, u32[]{:S(2)}) collective-permute-start(bf16[2,512,256]{2,1,0:T(8,128)(2,1)S(1)} %get-tuple-element.60.refs_9_), channel_id=1, source_target_pairs={{0,1},{1,0},{2,3},{3,2},{4,5},{5,4},{6,7},{7,6},{8,9},{9,8},{10,11... | collective-permute-start | bytes 1572872 | tf_op jit(solution)/shard_map/ppermute | solution.py:503
  53.4 11.4 %collective-permute-start.5 = (bf16[2,256,512]{2,1,0:T(8,128)(2,1)S(1)}, bf16[2,256,512]{2,1,0:T(8,128)(2,1)S(1)}, u32[]{:S(2)}, u32[]{:S(2)}) collective-permute-start(bf16[2,256,512]{2,1,0:T(8,128)(2,1)S(1)} %shard_map.110.refs_4_), channel_id=1, source_target_pairs={{2,4},{3,5},{4,2},{5,3},{10,12},{11,13},{12,10},{13,11},{18,20},{1... | collective-permute-start | bytes 1572872 | tf_op jit(solution)/shard_map/ppermute | solution.py:495
  54.1 14.4 %collective-permute-start.3 = (bf16[2,256,512]{2,1,0:T(8,128)(2,1)S(1)}, bf16[2,256,512]{2,1,0:T(8,128)(2,1)S(1)}, u32[]{:S(2)}, u32[]{:S(2)}) collective-permute-start(bf16[2,256,512]{2,1,0:T(8,128)(2,1)S(1)} %shard_map.109.refs_5_), channel_id=1, source_target_pairs={{0,2},{1,3},{2,0},{3,1},{4,6},{5,7},{6,4},{7,5},{8,10},{9,11},{10,... | collective-permute-start | bytes 1572872 | tf_op jit(solution)/shard_map/ppermute | solution.py:495
  64.8 8.1 %copy-start = (bf16[512,512]{1,0:T(8,128)(2,1)S(1)}, bf16[512,512]{1,0:T(8,128)(2,1)}, u32[]{:S(2)}) copy-start(bf16[512,512]{1,0:T(8,128)(2,1)} %refs_4_.6) | copy-start | bytes 1572868
  68.8 4.8 %copy-start.4 = (bf16[512,512]{1,0:T(8,128)(2,1)S(1)}, bf16[512,512]{1,0:T(8,128)(2,1)}, u32[]{:S(2)}) copy-start(bf16[512,512]{1,0:T(8,128)(2,1)} %refs_4_.7) | copy-start | bytes 1572868
  68.8 15.8 %collective-permute-start.20 = (bf16[256,512]{1,0:T(8,128)(2,1)S(1)}, bf16[256,512]{1,0:T(8,128)(2,1)S(1)}, u32[]{:S(2)}, u32[]{:S(2)}) collective-permute-start(bf16[256,512]{1,0:T(8,128)(2,1)S(1)} %get-tuple-element.61.refs_0_), channel_id=1, source_target_pairs={{0,16},{8,24},{16,0},{24,8},{1,17},{9,25},{17,1},{25,9},{2,18},{10... | collective-permute-start | bytes 786440 | tf_op jit(solution)/shard_map/ppermute | solution.py:506
  69.7 9.2 %collective-permute-start.15 = (bf16[256,512]{1,0:T(8,128)(2,1)S(1)}, bf16[256,512]{1,0:T(8,128)(2,1)S(1)}, u32[]{:S(2)}, u32[]{:S(2)}) collective-permute-start(bf16[256,512]{1,0:T(8,128)(2,1)S(1)} %get-tuple-element.61.refs_0_), channel_id=1, source_target_pairs={{0,8},{8,0},{16,24},{24,16},{1,9},{9,1},{17,25},{25,17},{2,10},{10... | collective-permute-start | bytes 786440 | tf_op jit(solution)/shard_map/ppermute | solution.py:506
  70.5 14.1 %collective-permute-start.19 = (bf16[256,512]{1,0:T(8,128)(2,1)S(1)}, bf16[256,512]{1,0:T(8,128)(2,1)S(1)}, u32[]{:S(2)}, u32[]{:S(2)}) collective-permute-start(bf16[256,512]{1,0:T(8,128)(2,1)S(1)} %get-tuple-element.62.refs_1_), channel_id=1, source_target_pairs={{0,8},{8,0},{16,24},{24,16},{1,9},{9,1},{17,25},{25,17},{2,10},{10... | collective-permute-start | bytes 786440 | tf_op jit(solution)/shard_map/ppermute | solution.py:506
  71.7 12.0 %collective-permute-start.17 = (bf16[256,512]{1,0:T(8,128)(2,1)S(1)}, bf16[256,512]{1,0:T(8,128)(2,1)S(1)}, u32[]{:S(2)}, u32[]{:S(2)}) collective-permute-start(bf16[256,512]{1,0:T(8,128)(2,1)S(1)} %get-tuple-element.62.refs_1_), channel_id=1, source_target_pairs={{0,16},{8,24},{16,0},{24,8},{1,17},{9,25},{17,1},{25,9},{2,18},{10... | collective-permute-start | bytes 786440 | tf_op jit(solution)/shard_map/ppermute | solution.py:506
  78.9 11.1 %collective-permute-start.16 = (bf16[256,512]{1,0:T(8,128)(2,1)S(1)}, bf16[256,512]{1,0:T(8,128)(2,1)S(1)}, u32[]{:S(2)}, u32[]{:S(2)}) collective-permute-start(bf16[256,512]{1,0:T(8,128)(2,1)S(1)} %collective-permute-done.15.refs_0_), channel_id=1, source_target_pairs={{0,16},{8,24},{16,0},{24,8},{1,17},{9,25},{17,1},{25,9},{2,18},{10... | collective-permute-start | bytes 786440 | tf_op jit(solution)/shard_map/ppermute | solution.py:506
  83.7 6.4 %collective-permute-start.18 = (bf16[256,512]{1,0:T(8,128)(2,1)S(1)}, bf16[256,512]{1,0:T(8,128)(2,1)S(1)}, u32[]{:S(2)}, u32[]{:S(2)}) collective-permute-start(bf16[256,512]{1,0:T(8,128)(2,1)S(1)} %collective-permute-done.17.refs_3_), channel_id=1, source_target_pairs={{0,8},{8,0},{16,24},{24,16},{1,9},{9,1},{17,25},{25,17},{2,10},{10... | collective-permute-start | bytes 786440 | tf_op jit(solution)/shard_map/ppermute | solution.py:506
  93.4 4.4 %collective-permute-start.21 = (bf16[512,512]{1,0:T(8,128)(2,1)S(1)}, bf16[512,512]{1,0:T(8,128)(2,1)S(1)}, u32[]{:S(2)}, u32[]{:S(2)}) collective-permute-start(bf16[512,512]{1,0:T(8,128)(2,1)S(1)} %get-tuple-element.74), channel_id=1, source_target_pairs={{0,1},{1,0},{2,3},{3,2},{4,5},{5,4},{6,7},{7,6},{8,9},{9,8},{10,11... | collective-permute-start | bytes 1572872 | tf_op jit(solution)/shard_map/ppermute | solution.py:503
  97.8 9.8 %collective-permute-start.22 = (bf16[8,256,512]{2,1,0:T(8,128)(2,1)S(1)}, bf16[8,256,512]{2,1,0:T(8,128)(2,1)S(1)}, u32[]{:S(2)}, u32[]{:S(2)}) collective-permute-start(bf16[8,256,512]{2,1,0:T(8,128)(2,1)S(1)} %shard_map.124), channel_id=1, source_target_pairs={{0,1},{1,0},{2,3},{3,2},{4,5},{5,4},{6,7},{7,6},{8,9},{9,8},{10,11... | collective-permute-start | bytes 6291464 | tf_op jit(solution)/shard_map/ppermute | solution.py:503
  98.0 7.5 %collective-permute-start.23 = (bf16[128,512]{1,0:T(8,128)(2,1)S(1)}, bf16[128,512]{1,0:T(8,128)(2,1)S(1)}, u32[]{:S(2)}, u32[]{:S(2)}) collective-permute-start(bf16[128,512]{1,0:T(8,128)(2,1)S(1)} %get-tuple-element.76), channel_id=1, source_target_pairs={{0,8},{8,0},{16,24},{24,16},{1,9},{9,1},{17,25},{25,17},{2,10},{10... | collective-permute-start | bytes 393224 | tf_op jit(solution)/shard_map/ppermute | solution.py:506
  99.5 8.0 %collective-permute-start.24 = (bf16[128,512]{1,0:T(8,128)(2,1)S(1)}, bf16[128,512]{1,0:T(8,128)(2,1)S(1)}, u32[]{:S(2)}, u32[]{:S(2)}) collective-permute-start(bf16[128,512]{1,0:T(8,128)(2,1)S(1)} %get-tuple-element.77), channel_id=1, source_target_pairs={{0,16},{8,24},{16,0},{24,8},{1,17},{9,25},{17,1},{25,9},{2,18},{10... | collective-permute-start | bytes 393224 | tf_op jit(solution)/shard_map/ppermute | solution.py:506
  100.2 7.2 %collective-permute-start.25 = (bf16[128,512]{1,0:T(8,128)(2,1)S(1)}, bf16[128,512]{1,0:T(8,128)(2,1)S(1)}, u32[]{:S(2)}, u32[]{:S(2)}) collective-permute-start(bf16[128,512]{1,0:T(8,128)(2,1)S(1)} %get-tuple-element.78), channel_id=1, source_target_pairs={{0,24},{8,16},{16,8},{24,0},{1,25},{9,17},{17,9},{25,1},{2,26},{10... | collective-permute-start | bytes 393224 | tf_op jit(solution)/shard_map/ppermute | solution.py:506
  108.0 15.3 %collective-permute-start.26 = (bf16[2,256,512]{2,1,0:T(8,128)(2,1)S(1)}, bf16[2,256,512]{2,1,0:T(8,128)(2,1)S(1)}, u32[]{:S(2)}, u32[]{:S(2)}) collective-permute-start(bf16[2,256,512]{2,1,0:T(8,128)(2,1)S(1)} %get-tuple-element.83.refs_0_), channel_id=1, source_target_pairs={{0,2},{1,3},{6,4},{7,5},{8,10},{9,11},{14,12},{15,13},{16,18},{17,... | collective-permute-start | bytes 1572872 | tf_op jit(solution)/shard_map/ppermute | solution.py:495
  111.0 37.4 %collective-permute-start.29 = (bf16[2,256,512]{2,1,0:T(8,128)(2,1)S(1)}, bf16[2,256,512]{2,1,0:T(8,128)(2,1)S(1)}, u32[]{:S(2)}, u32[]{:S(2)}) collective-permute-start(bf16[2,256,512]{2,1,0:T(8,128)(2,1)S(1)} %get-tuple-element.82.refs_0_), channel_id=1, source_target_pairs={{0,2},{1,3},{6,4},{7,5},{8,10},{9,11},{14,12},{15,13},{16,18},{17,... | collective-permute-start | bytes 1572872 | tf_op jit(solution)/shard_map/ppermute | solution.py:495
  123.4 25.7 %collective-permute-start.27 = (bf16[2,256,512]{2,1,0:T(8,128)(2,1)S(1)}, bf16[2,256,512]{2,1,0:T(8,128)(2,1)S(1)}, u32[]{:S(2)}, u32[]{:S(2)}) collective-permute-start(bf16[2,256,512]{2,1,0:T(8,128)(2,1)S(1)} %shard_map.127.refs_2_), channel_id=1, source_target_pairs={{2,4},{3,5},{4,2},{5,3},{10,12},{11,13},{12,10},{13,11},{18,20},{1... | collective-permute-start | bytes 1572872 | tf_op jit(solution)/shard_map/ppermute | solution.py:495
  124.1 9.9 %collective-permute-start.30 = (bf16[32,512]{1,0:T(8,128)(2,1)S(1)}, bf16[32,512]{1,0:T(8,128)(2,1)S(1)}, u32[]{:S(2)}, u32[]{:S(2)}) collective-permute-start(bf16[32,512]{1,0:T(8,128)(2,1)S(1)} %get-tuple-element.84), channel_id=1, source_target_pairs={{0,2},{1,3},{2,0},{3,1},{4,6},{5,7},{6,4},{7,5},{8,10},{9,11},{10,... | collective-permute-start | bytes 98312 | tf_op jit(solution)/shard_map/ppermute | solution.py:495
  129.2 11.9 %collective-permute-start.31 = (bf16[32,512]{1,0:T(8,128)(2,1)S(1)}, bf16[32,512]{1,0:T(8,128)(2,1)S(1)}, u32[]{:S(2)}, u32[]{:S(2)}) collective-permute-start(bf16[32,512]{1,0:T(8,128)(2,1)S(1)} %get-tuple-element.85), channel_id=1, source_target_pairs={{0,4},{1,5},{2,6},{3,7},{4,0},{5,1},{6,2},{7,3},{8,12},{9,13},{10,... | collective-permute-start | bytes 98312 | tf_op jit(solution)/shard_map/ppermute | solution.py:495
  129.4 11.7 %collective-permute-start.32 = (bf16[32,512]{1,0:T(8,128)(2,1)S(1)}, bf16[32,512]{1,0:T(8,128)(2,1)S(1)}, u32[]{:S(2)}, u32[]{:S(2)}) collective-permute-start(bf16[32,512]{1,0:T(8,128)(2,1)S(1)} %get-tuple-element.86), channel_id=1, source_target_pairs={{0,6},{1,7},{2,4},{3,5},{4,2},{5,3},{6,0},{7,1},{8,14},{9,15},{10,... | collective-permute-start | bytes 98312 | tf_op jit(solution)/shard_map/ppermute | solution.py:495
  141.2 5.9 %collective-permute-start.35 = (bf16[32,512]{1,0:T(8,128)(2,1)S(1)}, bf16[32,512]{1,0:T(8,128)(2,1)S(1)}, u32[]{:S(2)}, u32[]{:S(2)}) collective-permute-start(bf16[32,512]{1,0:T(8,128)(2,1)S(1)} %shard_map.129.refs_0_), channel_id=1, source_target_pairs={{0,6},{1,7},{2,4},{3,5},{4,2},{5,3},{6,0},{7,1},{8,14},{9,15},{10,... | collective-permute-start | bytes 98312 | tf_op jit(solution)/shard_map/ppermute | solution.py:495
  142.4 5.8 %collective-permute-start.34 = (bf16[32,512]{1,0:T(8,128)(2,1)S(1)}, bf16[32,512]{1,0:T(8,128)(2,1)S(1)}, u32[]{:S(2)}, u32[]{:S(2)}) collective-permute-start(bf16[32,512]{1,0:T(8,128)(2,1)S(1)} %shard_map.129.refs_0_), channel_id=1, source_target_pairs={{0,4},{1,5},{2,6},{3,7},{4,0},{5,1},{6,2},{7,3},{8,12},{9,13},{10,... | collective-permute-start | bytes 98312 | tf_op jit(solution)/shard_map/ppermute | solution.py:495
  143.6 4.7 %collective-permute-start.33 = (bf16[32,512]{1,0:T(8,128)(2,1)S(1)}, bf16[32,512]{1,0:T(8,128)(2,1)S(1)}, u32[]{:S(2)}, u32[]{:S(2)}) collective-permute-start(bf16[32,512]{1,0:T(8,128)(2,1)S(1)} %shard_map.129.refs_0_), channel_id=1, source_target_pairs={{0,2},{1,3},{2,0},{3,1},{4,6},{5,7},{6,4},{7,5},{8,10},{9,11},{10,... | collective-permute-start | bytes 98312 | tf_op jit(solution)/shard_map/ppermute | solution.py:495
  148.5 12.5 %collective-permute-start.36 = (bf16[2,256,512]{2,1,0:T(8,128)(2,1)S(1)}, bf16[2,256,512]{2,1,0:T(8,128)(2,1)S(1)}, u32[]{:S(2)}, u32[]{:S(2)}) collective-permute-start(bf16[2,256,512]{2,1,0:T(8,128)(2,1)S(1)} %shard_map.131), channel_id=1, source_target_pairs={{2,4},{3,5},{4,2},{5,3},{10,12},{11,13},{12,10},{13,11},{18,20},{1... | collective-permute-start | bytes 1572872 | tf_op jit(solution)/shard_map/ppermute | solution.py:495
  149.3 11.7 %collective-permute-start.28 = (bf16[2,256,512]{2,1,0:T(8,128)(2,1)S(1)}, bf16[2,256,512]{2,1,0:T(8,128)(2,1)S(1)}, u32[]{:S(2)}, u32[]{:S(2)}) collective-permute-start(bf16[2,256,512]{2,1,0:T(8,128)(2,1)S(1)} %shard_map.128), channel_id=1, source_target_pairs={{0,2},{1,3},{2,0},{3,1},{4,6},{5,7},{6,4},{7,5},{8,10},{9,11},{10,... | collective-permute-start | bytes 1572872 | tf_op jit(solution)/shard_map/ppermute | solution.py:495
  152.5 5.9 %collective-permute-start.39 = (bf16[128,512]{1,0:T(8,128)(2,1)S(1)}, bf16[128,512]{1,0:T(8,128)(2,1)S(1)}, u32[]{:S(2)}, u32[]{:S(2)}) collective-permute-start(bf16[128,512]{1,0:T(8,128)(2,1)S(1)} %shard_map.130.refs_3_.refs_0_), channel_id=1, source_target_pairs={{0,24},{8,16},{16,8},{24,0},{1,25},{9,17},{17,9},{25,1},{2,26},{10... | collective-permute-start | bytes 393224 | tf_op jit(solution)/shard_map/ppermute | solution.py:506
  154.6 5.2 %collective-permute-start.38 = (bf16[128,512]{1,0:T(8,128)(2,1)S(1)}, bf16[128,512]{1,0:T(8,128)(2,1)S(1)}, u32[]{:S(2)}, u32[]{:S(2)}) collective-permute-start(bf16[128,512]{1,0:T(8,128)(2,1)S(1)} %shard_map.130.refs_3_.refs_0_), channel_id=1, source_target_pairs={{0,16},{8,24},{16,0},{24,8},{1,17},{9,25},{17,1},{25,9},{2,18},{10... | collective-permute-start | bytes 393224 | tf_op jit(solution)/shard_map/ppermute | solution.py:506
  155.0 5.8 %collective-permute-start.37 = (bf16[128,512]{1,0:T(8,128)(2,1)S(1)}, bf16[128,512]{1,0:T(8,128)(2,1)S(1)}, u32[]{:S(2)}, u32[]{:S(2)}) collective-permute-start(bf16[128,512]{1,0:T(8,128)(2,1)S(1)} %shard_map.130.refs_3_.refs_0_), channel_id=1, source_target_pairs={{0,8},{8,0},{16,24},{24,16},{1,9},{9,1},{17,25},{25,17},{2,10},{10... | collective-permute-start | bytes 393224 | tf_op jit(solution)/shard_map/ppermute | solution.py:506
  160.9 2.0 %collective-permute-start.40 = (bf16[512,512]{1,0:T(8,128)(2,1)S(1)}, bf16[512,512]{1,0:T(8,128)(2,1)S(1)}, u32[]{:S(2)}, u32[]{:S(2)}) collective-permute-start(bf16[512,512]{1,0:T(8,128)(2,1)S(1)} %shard_map.133.refs_0_), channel_id=1, source_target_pairs={{0,1},{1,0},{2,3},{3,2},{4,5},{5,4},{6,7},{7,6},{8,9},{9,8},{10,11... | collective-permute-start | bytes 1572872 | tf_op jit(solution)/shard_map/ppermute | solution.py:503
  162.9 1.0 copy-start.1

commit v9 on v8

--- a/solution.py
+++ b/solution.py
@@ -201,11 +201,17 @@
 def backward_body(n, number_ref, list_ref, tiles, *refs):
     pieces_in, (out, ranged, total) = refs[:n], refs[n:]
     mask, flips = lax.axis_index("row") * 2, lax.axis_index("col") * 2
-    for i, piece in enumerate(pieces_in):
-        ranged[2 * i : 2 * i + 2] = piece[...]
+    blocks, start = ranged.shape[0], 0
+    for piece in pieces_in:
+        ranged[start : start + piece.shape[0]] = piece[...]
+        start += piece.shape[0]
 
     def product(pieces):
-        return joined_dot([ranged[u ^ flips] for _, u in pieces], [tiles[s] for s, _ in pieces])
+        def locate(u):
+            x = u ^ flips
+            return (x & 2) * (blocks // 4) + lax.shift_right_logical(x, 2) * 2 + (x & 1)
+
+        return joined_dot([ranged[locate(u)] for _, u in pieces], [tiles[s] for s, _ in pieces])
 
     def block(i, _):
         def store(value):
@@ -220,13 +226,13 @@
 def backward(number, entries, tiles, pieces, after=()):
     slots_n, edge, _ = tiles.shape
     _, width, _ = pieces[0].shape
-    n = len(pieces)
+    n, blocks = len(pieces), sum(x.shape[0] for x in pieces)
     return run(
         functools.partial(backward_body, n),
         (number, entries, tiles, *pieces),
         [SMEM, SMEM] + [VMEM] * (n + 1),
         [shape((number.shape[0], width, edge))],
-        [pltpu.VMEM((2 * n, width, edge), BF16), pltpu.VMEM((width, edge), F32)],
+        [pltpu.VMEM((blocks, width, edge), BF16), pltpu.VMEM((width, edge), F32)],
         mib=20,
         after=after,
     )[0]
@@ -273,11 +279,11 @@
     )
 
 
-def choose_body(at_ends, across, middle, out_two, out_three, two, three):
-    position = lax.shift_right_logical(lax.axis_index("col"), 1)
-    ends = jnp.logical_or(position == 0, position == at_ends)
-    two[...] = jnp.where(ends, out_two[...], across[...])
-    three[...] = jnp.where(ends, out_three[...], middle[...])
+def choose_body(last, across, middle, out_two, out_three, *outs):
+    ends = jnp.logical_or(position("col") == 0, position("col") == last)
+    for half in range(2):
+        outs[half][0] = jnp.where(ends, out_two[half], across[half])
+        outs[2 + half][0] = jnp.where(ends, out_three[half], middle[half])
 
 
 def choose(last, across, middle, out_two, out_three, after):
@@ -285,7 +291,7 @@
         functools.partial(choose_body, last),
         (across, middle, out_two, out_three),
         [VMEM] * 4,
-        [shape(across.shape)] * 2,
+        [shape((1, *across.shape[1:]))] * 4,
         after=after,
     )
 
@@ -505,23 +511,23 @@
     def row_flip(value, j):
         return lax.ppermute(value, "row", [(a, a ^ j) for a in range(n_row)])
 
-    def scatter_line(own, after=()):
+    def scatter_line(own, behind):
         if line != 4:
             return [own[0]] + [line_flip(own[j], j) for j in range(1, line)], own[:2]
         to_three = col_send(own[3], [(0, 1), (3, 2)])
-        to_two = col_send(own[2], [(0, 1), (3, 2)])
-        crossing = sum_parts([own[2], to_three])
-        meeting = sum_parts([own[3], to_two], (crossing, *after))
+        to_two = col_send(behind, [(0, 1), (3, 2)])
+        crossing = sum_parts([behind, to_three])
+        meeting = sum_parts([own[3], to_two], (crossing,))
         crossed = col_send(crossing, [(1, 2), (2, 1)])
         met = col_send(meeting, [(1, 2), (2, 1)])
         outward = sum_parts([own[1], crossed])
         return [own[0], line_flip(outward, 1), met], (meeting, outward)
 
-    def gather_row(pair):
+    def gather_row(pair, behind):
         if n_row != 4:
             return [pair] + [[row_flip(x, j) for x in pair] for j in range(1, n_row)]
         x_first, y_second = row_flip(pair[0], 1), row_flip(pair[1], 2)
-        x_second, y_first = row_flip(pair[1], 1), row_flip(pair[0], 2)
+        x_second, y_first = row_flip(behind[1], 1), row_flip(behind[0], 2)
         diagonal = [row_flip(x_first, 2), row_flip(y_second, 1)]
         return [pair, [x_first, x_second], [y_first, y_second], diagonal]
 
@@ -549,36 +555,39 @@
     if early:
         early = relay(early, (give,))
     own = pair_sum(keep, core_flip(give))
-    parts, late = scatter_line(own)
+    parts, late = scatter_line(own, own[2])
     if early:
         gathered = gather_far(scaled, *early, (own[0],), late)
     else:
         gathered = [scaled] + [line_flip(scaled, j) for j in range(1, line)]
-    ranged = [x for g in gathered for x in (g, core_flip(g))]
+    ranged = gathered + [core_flip(g) for g in gathered]
     hidden = backward(t_number, t_entries, tiles, ranged)
-    spread = gather_row(aggregate(parts, scale, (hidden,)))
-    sums, stacked = (), ()
-    for group in (spread[:1], spread[1:-1], spread[-1:]):
-        start = stacked[0].shape[0] if stacked else 0
+    pair = aggregate(parts, scale, (hidden,))
+    stacked = first_layer([pair], scale, w_first)
+    spread = gather_row(pair, relay(pair, stacked[:1]))
+    sums = weight_grads(0, hidden, *stacked, scale, w_first, w_second)
+    for group in (spread[1:-1], spread[-1:]):
+        start = stacked[0].shape[0]
         stacked = first_layer(group, scale, w_first, stacked, sums[:1])
         sums = weight_grads(start, hidden, *stacked, scale, w_first, w_second, sums)
 
-    give, keep = sums
-    split = split_sum([keep, core_flip(give)], n_row, "row")
+    grad_give, grad_keep = sums
+    give = forward(number, entries, tiles, stacked[1], False, 1, (grad_keep,))
+    keep = forward(number, entries, tiles, stacked[1], False, 0)
+    own = pair_sum(keep, core_flip(give))
+    split = split_sum([grad_keep, core_flip(grad_give)], n_row, "row", own[:1])
     moment = [split[0]] + [row_flip(split[j], j) for j in range(1, n_row)]
-    give = forward(number, entries, tiles, stacked[1], False, 1, (keep,))
-    keep = forward(number, entries, tiles, stacked[1], False, 0, (split[0],))
     if split[0].shape[0] % (16 * line) == 0:
         split = split_sum(moment, line, "line")
         moment = sum_parts([split[0]] + [line_flip(split[j], j) for j in range(1, line)])
         moment = join([moment] + [line_flip(moment, j) for j in range(1, line)], "line")
     else:
-        split = [sum_parts(moment)]
-        moment = sum_parts(split + [line_flip(split[0], j) for j in range(1, line)])
-    own = pair_sum(keep, core_flip(give), split[:1])
-    parts, _ = scatter_line(own, (moment,))
+        moment = sum_parts(moment)
+        moment = sum_parts([moment] + [line_flip(moment, j) for j in range(1, line)])
+    (behind,) = relay(own[2:3], (moment,))
     moment = [moment] + [row_flip(moment, j) for j in range(1, n_row)]
     mine = join(moment, "row")
+    parts, _ = scatter_line(own, behind)
     logits = second_layer(parts, scale, w_second)
     return logits, *select(mine, core_flip(mine), (logits,))
 

time: 167 us -> 161 us (0.964)
  Pallas kernels: 44.2 us -> 37 us
  waiting for transfers between devices: 61.1 us -> 62.8 us
    pallas_call x32 -> x34, Pallas kernels: 44.2 us -> 37 us  [run(): pl.pallas_call(whole, out_shape=outs, in_specs=specs + [ANY] * extra, out...]
    ppermute x21, waiting for transfers between devices: 46.9 us -> 41.4 us  [col_send(): lax.ppermute(value, 'col', [(2 * a + k, 2 * b + k) for a, b in pairs for...]
    ppermute x12, waiting for transfers between devices: 13.1 us -> 17.1 us  [row_flip(): return lax.ppermute(value, 'row', [(a, a ^ j) for a in range(n_row)])]
    ppermute x8 -> x10, waiting for transfers between devices: 1.06 us -> 4.26 us  [core_flip(): return lax.ppermute(value, 'col', [(a, a ^ 1) for a in range(n_col)])]
    ppermute x21, starting transfers between devices: 40.9 us -> 42.7 us  [col_send(): lax.ppermute(value, 'col', [(2 * a + k, 2 * b + k) for a, b in pairs for...]
  transfers between devices with their start and end apart: 41 -> 43, of which waited for: 19 -> 25; matrix products, arithmetic and copies ran while one was open for 0% -> 0% of each run, Pallas kernels for 23% -> 20%
where the time goes in v9:
time: 161 us
  waiting for transfers between devices  62.8 us (39%)
  starting transfers between devices  56.4 us (35%)
  Pallas kernels  37 us (23%)
  local copies, waits for them, and re-layouts  2.81 us (2%)
  between operations  1.82 us (1%)
    ppermute x21, starting transfers between devices, col_send(): lax.ppermute(value, 'col', [(2 * a + k, 2 * b + k) for a, b in pairs for...  42.7 us
    ppermute x21, waiting for transfers between devices, col_send(): lax.ppermute(value, 'col', [(2 * a + k, 2 * b + k) for a, b in pairs for...  41.4 us
    pallas_call x34, Pallas kernels, run(): pl.pallas_call(whole, out_shape=outs, in_specs=specs + [ANY] * extra, out...  37 us
    ppermute x12, waiting for transfers between devices, row_flip(): return lax.ppermute(value, 'row', [(a, a ^ j) for a in range(n_row)])  17.1 us
    ppermute x12, starting transfers between devices, row_flip(): return lax.ppermute(value, 'row', [(a, a ^ j) for a in range(n_row)])  12.3 us
    ppermute x10, waiting for transfers between devices, core_flip(): return lax.ppermute(value, 'col', [(a, a ^ 1) for a in range(n_col)])  4.26 us
  transfers between devices with their start and end apart: 43, of which 25 were waited for; matrix products, arithmetic and copies ran while one was open for 0% of the time, Pallas kernels for 20%

profile of v9, /device:TPU:0, one launch (start us, length us, event | category | flops | bytes accessed | tf_op | source)
XLA Modules:
  0.0 160.8 jit_solution(2105263407907977431)
XLA Ops:
  0.6 0.7 copy.13
  1.3 1.0 copy-done.3
  2.9 0.8 collective-permute-start.7
  3.8 6.0 %collective-permute-start.6 = (bf16[2,512,256]{2,1,0:T(8,128)(2,1)S(1)}, bf16[2,512,256]{2,1,0:T(8,128)(2,1)S(1)}, u32[]{:S(2)}, u32[]{:S(2)}) collective-permute-start(bf16[2,512,256]{2,1,0:T(8,128)(2,1)S(1)} %get-tuple-element.60.refs_3_), channel_id=1, source_target_pairs={{0,2},{1,3},{2,0},{3,1},{4,6},{5,7},{6,4},{7,5},{8,10},{9,11},{10,... | collective-permute-start | bytes 1572872 | tf_op jit(solution)/shard_map/ppermute | solution.py:501
  10.5 2.3 %shard_map.104 = (bf16[8,256,512]{2,1,0:T(8,128)(2,1)S(1)}, s32[16]{0:T(128)S(1)}, s32[128]{0:T(128)S(1)}, s32[8]{0:T(128)S(1)}, s32[128]{0:T(128)S(1)}) custom-call(s32[1]{0:T(128)} %bitcast.7.refs_0_, s32[48]{0:T(128)S(1)} %bitcast.17, bf16[8,256,512]{2,1,0:T(8,128)(2,1)S(1)} %bitcast.16, f32[8,256,128]{2,1,0:T(8,128)S(1)} %get-tuple-element.50.refs_3_.refs_2_.refs_4_), custom_call_target="tpu_custom_call" | custom-call | flops 35999997952 | tf_op jit(solution)/shard_map/pallas_call | solution.py:24
  12.8 3.2 %shard_map.106.refs_2_ = bf16[8,256,512]{2,1,0:T(8,128)(2,1)S(1)} custom-call(s32[16]{0:T(128)S(1)} %get-tuple-element.51.refs_0_, s32[128]{0:T(128)S(1)} %get-tuple-element.52.refs_1_, bf16[48,256,256]{2,1,0:T(8,128)(2,1)S(1)} %bitcast.10, bf16[8,256,512]{2,1,0:T(8,128)(2,1)S(1)} %get-tuple-element.53.refs_3_), custom_call_target="tpu_custom_call" | custom-call | flops 35999997952 | tf_op jit(solution)/shard_map/pallas_call | solution.py:24
  16.1 2.9 %shard_map.105.refs_0_ = bf16[8,256,512]{2,1,0:T(8,128)(2,1)S(1)} custom-call(s32[16]{0:T(128)S(1)} %get-tuple-element.51.refs_0_, s32[128]{0:T(128)S(1)} %get-tuple-element.52.refs_1_, bf16[48,256,256]{2,1,0:T(8,128)(2,1)S(1)} %bitcast.11, bf16[8,256,512]{2,1,0:T(8,128)(2,1)S(1)} %get-tuple-element.53.refs_3_), custom_call_target="tpu_custom_call" | custom-call | flops 35999997952 | tf_op jit(solution)/shard_map/pallas_call | solution.py:24
  18.9 1.3 collective-permute-done.refs_1_
  20.7 3.7 %collective-permute-start.1 = (bf16[2,256,512]{2,1,0:T(8,128)(2,1)S(1)}, bf16[2,256,512]{2,1,0:T(8,128)(2,1)S(1)}, u32[]{:S(2)}, u32[]{:S(2)}) collective-permute-start(bf16[2,256,512]{2,1,0:T(8,128)(2,1)S(1)} %get-tuple-element.57.refs_0_), channel_id=1, source_target_pairs={{0,2},{1,3},{6,4},{7,5},{8,10},{9,11},{14,12},{15,13},{16,18},{17,... | collective-permute-start | bytes 1572872 | tf_op jit(solution)/shard_map/ppermute | solution.py:501
  24.5 0.7 collective-permute-start.8
  25.2 2.5 %collective-permute-start.4 = (bf16[2,256,512]{2,1,0:T(8,128)(2,1)S(1)}, bf16[2,256,512]{2,1,0:T(8,128)(2,1)S(1)}, u32[]{:S(2)}, u32[]{:S(2)}) collective-permute-start(bf16[2,256,512]{2,1,0:T(8,128)(2,1)S(1)} %get-tuple-element.56.refs_0_), channel_id=1, source_target_pairs={{0,2},{1,3},{6,4},{7,5},{8,10},{9,11},{14,12},{15,13},{16,18},{17,... | collective-permute-start | bytes 1572872 | tf_op jit(solution)/shard_map/ppermute | solution.py:501
  27.7 1.3 collective-permute-start.9
  29.0 7.6 %collective-permute-done.1.refs_1_ = bf16[2,256,512]{2,1,0:T(8,128)(2,1)S(1)} collective-permute-done((bf16[2,256,512]{2,1,0:T(8,128)(2,1)S(1)}, bf16[2,256,512]{2,1,0:T(8,128)(2,1)S(1)}, u32[]{:S(2)}, u32[]{:S(2)}) %collective-permute-start.1) | collective-permute-done | bytes 524320 | tf_op jit(solution)/shard_map/ppermute | solution.py:501
  36.7 0.7 collective-permute-start.2
  37.5 1.3 collective-permute-start.10
  38.9 8.2 %collective-permute-done.4.refs_1_ = bf16[2,256,512]{2,1,0:T(8,128)(2,1)S(1)} collective-permute-done((bf16[2,256,512]{2,1,0:T(8,128)(2,1)S(1)}, bf16[2,256,512]{2,1,0:T(8,128)(2,1)S(1)}, u32[]{:S(2)}, u32[]{:S(2)}) %collective-permute-start.4) | collective-permute-done | bytes 524320 | tf_op jit(solution)/shard_map/ppermute | solution.py:501
  47.3 7.2 %collective-permute-done.10.refs_3_ = bf16[2,512,256]{2,1,0:T(8,128)(2,1)S(1)} collective-permute-done((bf16[2,512,256]{2,1,0:T(8,128)(2,1)S(1)}, bf16[2,512,256]{2,1,0:T(8,128)(2,1)S(1)}, u32[]{:S(2)}, u32[]{:S(2)}) %collective-permute-start.10) | collective-permute-done | bytes 524320 | tf_op jit(solution)/shard_map/ppermute | solution.py:501
  54.7 0.7 collective-permute-start.5
  55.4 2.6 %collective-permute-start.3 = (bf16[2,256,512]{2,1,0:T(8,128)(2,1)S(1)}, bf16[2,256,512]{2,1,0:T(8,128)(2,1)S(1)}, u32[]{:S(2)}, u32[]{:S(2)}) collective-permute-start(bf16[2,256,512]{2,1,0:T(8,128)(2,1)S(1)} %shard_map.109.refs_5_), channel_id=1, source_target_pairs={{0,2},{1,3},{2,0},{3,1},{4,6},{5,7},{6,4},{7,5},{8,10},{9,11},{10,... | collective-permute-start | bytes 1572872 | tf_op jit(solution)/shard_map/ppermute | solution.py:501
  58.6 0.9 collective-permute-done.14.refs_12_
  60.3 5.1 %shard_map.114.refs_4_.refs_0_ = bf16[8,512,256]{2,1,0:T(8,128)(2,1)S(1)} custom-call(s32[8]{0:T(128)S(1)} %get-tuple-element.58.refs_0_, s32[128]{0:T(128)S(1)} %get-tuple-element.59.refs_1_, bf16[48,256,256]{2,1,0:T(8,128)(2,1)S(1)} %bitcast.12, bf16[2,512,256]{2,1,0:T(8,128)(2,1)S(1)} %get-tuple-element.60.refs_3_, ...), custom_call_target="tpu_custom_call" | custom-call | tf_op jit(solution)/shard_map/pallas_call | solution.py:24
  65.4 4.8 %collective-permute-done.3.refs_1_ = bf16[2,256,512]{2,1,0:T(8,128)(2,1)S(1)} collective-permute-done((bf16[2,256,512]{2,1,0:T(8,128)(2,1)S(1)}, bf16[2,256,512]{2,1,0:T(8,128)(2,1)S(1)}, u32[]{:S(2)}, u32[]{:S(2)}) %collective-permute-start.3) | collective-permute-done | bytes 524320 | tf_op jit(solution)/shard_map/ppermute | solution.py:501
  70.5 1.2 collective-permute-start.17
  72.9 0.7 collective-permute-start.21
  73.5 1.8 %collective-permute-start.22 = (bf16[256,512]{1,0:T(8,128)(2,1)S(1)}, bf16[256,512]{1,0:T(8,128)(2,1)S(1)}, u32[]{:S(2)}, u32[]{:S(2)}) collective-permute-start(bf16[256,512]{1,0:T(8,128)(2,1)S(1)} %get-tuple-element.71), channel_id=1, source_target_pairs={{0,16},{8,24},{16,0},{24,8},{1,17},{9,25},{17,1},{25,9},{2,18},{10... | collective-permute-start | bytes 786440 | tf_op jit(solution)/shard_map/ppermute | solution.py:512
  75.4 2.2 %shard_map.118 = (f32[512,512]{1,0:T(8,128)S(1)}, f32[512,512]{1,0:T(8,128)S(1)}) custom-call(bf16[8,512,256]{2,1,0:T(8,128)(2,1)S(1)} %shard_map.114.refs_4_.refs_0_, bf16[2,256,512]{2,1,0:T(8,128)(2,1)S(1)} %get-tuple-element.69.refs_2_.refs_1_.refs_6_, bf16[2,256,512]{2,1,0:T(8,128)(2,1)S(1)} %get-tuple-element.72.refs_2_.refs_7_, ...), custom_call_target="tpu_custom_call" | custom-call | flops 35999997952 | tf_op jit(solution)/shard_map/pallas_call | solution.py:24
  77.6 2.2 %collective-permute-done.17.refs_0_ = bf16[256,512]{1,0:T(8,128)(2,1)S(1)} collective-permute-done((bf16[256,512]{1,0:T(8,128)(2,1)S(1)}, bf16[256,512]{1,0:T(8,128)(2,1)S(1)}, u32[]{:S(2)}, u32[]{:S(2)}) %collective-permute-start.17) | collective-permute-done | bytes 262176 | tf_op jit(solution)/shard_map/ppermute | solution.py:512
  80.0 0.9 collective-permute-done.19.refs_3_
  80.9 0.9 collective-permute-start.20
  81.8 3.6 %collective-permute-done.21.refs_1_ = bf16[256,512]{1,0:T(8,128)(2,1)S(1)} collective-permute-done((bf16[256,512]{1,0:T(8,128)(2,1)S(1)}, bf16[256,512]{1,0:T(8,128)(2,1)S(1)}, u32[]{:S(2)}, u32[]{:S(2)}) %collective-permute-start.21) | collective-permute-done | bytes 262176 | tf_op jit(solution)/shard_map/ppermute | solution.py:512
  85.4 1.2 collective-permute-done.22.refs_2_
  86.6 1.1 shard_map.119
  87.7 4.3 %shard_map.120 = (f32[512,512]{1,0:T(8,128)S(1)}, f32[512,512]{1,0:T(8,128)S(1)}) custom-call(bf16[8,512,256]{2,1,0:T(8,128)(2,1)S(1)} %shard_map.114.refs_4_.refs_0_, bf16[6,256,512]{2,1,0:T(8,128)(2,1)S(1)} %get-tuple-element.74.refs_1_.refs_4_, bf16[6,256,512]{2,1,0:T(8,128)(2,1)S(1)} %get-tuple-element.75.refs_2_.refs_5_, ...), custom_call_target="tpu_custom_call" | custom-call | flops 35999997952 | tf_op jit(solution)/shard_map/pallas_call | solution.py:24
  92.0 0.9 shard_map.121
  92.9 2.4 %shard_map.123 = (bf16[512,512]{1,0:T(8,128)(2,1)S(1)}, bf16[512,512]{1,0:T(8,128)(2,1)S(1)}) custom-call(bf16[8,512,256]{2,1,0:T(8,128)(2,1)S(1)} %shard_map.114.refs_4_.refs_0_, bf16[8,256,512]{2,1,0:T(8,128)(2,1)S(1)} %get-tuple-element.79.refs_1_, bf16[8,256,512]{2,1,0:T(8,128)(2,1)S(1)} %get-tuple-element.78.refs_3_.refs_2_, ...), custom_call_target="tpu_custom_call" | custom-call | flops 35999997952 | tf_op jit(solution)/shard_map/pallas_call | solution.py:24
  95.4 3.1 %shard_map.124 = bf16[8,256,512]{2,1,0:T(8,128)(2,1)S(1)} custom-call(s32[16]{0:T(128)S(1)} %get-tuple-element.51.refs_0_, s32[128]{0:T(128)S(1)} %get-tuple-element.52.refs_1_, bf16[48,256,256]{2,1,0:T(8,128)(2,1)S(1)} %bitcast.13, bf16[8,256,512]{2,1,0:T(8,128)(2,1)S(1)} %get-tuple-element.78.refs_3_.refs_2_, ...), custom_call_target="tpu_custom_call" | custom-call | flops 35999997952 | tf_op jit(solution)/shard_map/pallas_call | solution.py:24
  99.0 3.1 %shard_map.122.refs_0_ = bf16[8,256,512]{2,1,0:T(8,128)(2,1)S(1)} custom-call(s32[16]{0:T(128)S(1)} %get-tuple-element.51.refs_0_, s32[128]{0:T(128)S(1)} %get-tuple-element.52.refs_1_, bf16[48,256,256]{2,1,0:T(8,128)(2,1)S(1)} %bitcast.14, bf16[8,256,512]{2,1,0:T(8,128)(2,1)S(1)} %get-tuple-element.78.refs_3_.refs_2_), custom_call_target="tpu_custom_call" | custom-call | flops 35999997952 | tf_op jit(solution)/shard_map/pallas_call | solution.py:24
  102.1 0.7 collective-permute-done.23.refs_1_
  103.3 4.1 %collective-permute-start.34 = (bf16[2,256,512]{2,1,0:T(8,128)(2,1)S(1)}, bf16[2,256,512]{2,1,0:T(8,128)(2,1)S(1)}, u32[]{:S(2)}, u32[]{:S(2)}) collective-permute-start(bf16[2,256,512]{2,1,0:T(8,128)(2,1)S(1)} %get-tuple-element.94.refs_0_), channel_id=1, source_target_pairs={{0,2},{1,3},{6,4},{7,5},{8,10},{9,11},{14,12},{15,13},{16,18},{17,... | collective-permute-start | bytes 1572872 | tf_op jit(solution)/shard_map/ppermute | solution.py:501
  107.6 0.7 collective-permute-start.25
  108.5 2.6 %collective-permute-start.27 = (bf16[128,512]{1,0:T(8,128)(2,1)S(1)}, bf16[128,512]{1,0:T(8,128)(2,1)S(1)}, u32[]{:S(2)}, u32[]{:S(2)}) collective-permute-start(bf16[128,512]{1,0:T(8,128)(2,1)S(1)} %get-tuple-element.89), channel_id=1, source_target_pairs={{0,24},{8,16},{16,8},{24,0},{1,25},{9,17},{17,9},{25,1},{2,26},{10... | collective-permute-start | bytes 393224 | tf_op jit(solution)/shard_map/ppermute | solution.py:512
  111.1 2.9 %collective-permute-done.25.refs_1_ = bf16[128,512]{1,0:T(8,128)(2,1)S(1)} collective-permute-done((bf16[128,512]{1,0:T(8,128)(2,1)S(1)}, bf16[128,512]{1,0:T(8,128)(2,1)S(1)}, u32[]{:S(2)}, u32[]{:S(2)}) %collective-permute-start.25) | collective-permute-done | bytes 131104 | tf_op jit(solution)/shard_map/ppermute | solution.py:512
  114.0 2.1 %collective-permute-done.26.refs_2_ = bf16[128,512]{1,0:T(8,128)(2,1)S(1)} collective-permute-done((bf16[128,512]{1,0:T(8,128)(2,1)S(1)}, bf16[128,512]{1,0:T(8,128)(2,1)S(1)}, u32[]{:S(2)}, u32[]{:S(2)}) %collective-permute-start.26) | collective-permute-done | bytes 131104 | tf_op jit(solution)/shard_map/ppermute | solution.py:512
  116.3 3.1 %collective-permute-start.29 = (bf16[32,512]{1,0:T(8,128)(2,1)S(1)}, bf16[32,512]{1,0:T(8,128)(2,1)S(1)}, u32[]{:S(2)}, u32[]{:S(2)}) collective-permute-start(bf16[32,512]{1,0:T(8,128)(2,1)S(1)} %get-tuple-element.92), channel_id=1, source_target_pairs={{0,4},{1,5},{2,6},{3,7},{4,0},{5,1},{6,2},{7,3},{8,12},{9,13},{10,... | collective-permute-start | bytes 98312 | tf_op jit(solution)/shard_map/ppermute | solution.py:501
  119.4 1.3 collective-permute-start.30
  121.2 3.8 %collective-permute-done.30.refs_3_ = bf16[32,512]{1,0:T(8,128)(2,1)S(1)} collective-permute-done((bf16[32,512]{1,0:T(8,128)(2,1)S(1)}, bf16[32,512]{1,0:T(8,128)(2,1)S(1)}, u32[]{:S(2)}, u32[]{:S(2)}) %collective-permute-start.30) | collective-permute-done | bytes 32800 | tf_op jit(solution)/shard_map/ppermute | solution.py:501
  125.1 1.3 collective-permute-start.33
  126.4 3.1 %collective-permute-start.31 = (bf16[32,512]{1,0:T(8,128)(2,1)S(1)}, bf16[32,512]{1,0:T(8,128)(2,1)S(1)}, u32[]{:S(2)}, u32[]{:S(2)}) collective-permute-start(bf16[32,512]{1,0:T(8,128)(2,1)S(1)} %shard_map.128.refs_0_), channel_id=1, source_target_pairs={{0,2},{1,3},{2,0},{3,1},{4,6},{5,7},{6,4},{7,5},{8,10},{9,11},{10,... | collective-permute-start | bytes 98312 | tf_op jit(solution)/shard_map/ppermute | solution.py:501
  129.5 1.3 collective-permute-done.33.refs_3_
  130.9 0.8 collective-permute-done.32.refs_2_
  131.8 3.6 %collective-permute-start.37 = (bf16[2,256,512]{2,1,0:T(8,128)(2,1)S(1)}, bf16[2,256,512]{2,1,0:T(8,128)(2,1)S(1)}, u32[]{:S(2)}, u32[]{:S(2)}) collective-permute-start(bf16[2,256,512]{2,1,0:T(8,128)(2,1)S(1)} %shard_map.130.refs_0_), channel_id=1, source_target_pairs={{0,2},{1,3},{6,4},{7,5},{8,10},{9,11},{14,12},{15,13},{16,18},{17,... | collective-permute-start | bytes 1572872 | tf_op jit(solution)/shard_map/ppermute | solution.py:501
  135.6 0.7 collective-permute-start.35
  136.3 6.9 %collective-permute-done.37.refs_1_ = bf16[2,256,512]{2,1,0:T(8,128)(2,1)S(1)} collective-permute-done((bf16[2,256,512]{2,1,0:T(8,128)(2,1)S(1)}, bf16[2,256,512]{2,1,0:T(8,128)(2,1)S(1)}, u32[]{:S(2)}, u32[]{:S(2)}) %collective-permute-start.37) | collective-permute-done | bytes 524320 | tf_op jit(solution)/shard_map/ppermute | solution.py:501
  143.4 0.7 collective-permute-start.38
  144.2 4.4 %collective-permute-start.36 = (bf16[2,256,512]{2,1,0:T(8,128)(2,1)S(1)}, bf16[2,256,512]{2,1,0:T(8,128)(2,1)S(1)}, u32[]{:S(2)}, u32[]{:S(2)}) collective-permute-start(bf16[2,256,512]{2,1,0:T(8,128)(2,1)S(1)} %shard_map.132), channel_id=1, source_target_pairs={{0,2},{1,3},{2,0},{3,1},{4,6},{5,7},{6,4},{7,5},{8,10},{9,11},{10,... | collective-permute-start | bytes 1572872 | tf_op jit(solution)/shard_map/ppermute | solution.py:501
  148.6 1.4 collective-permute-start.41
  149.9 1.4 collective-permute-start.40
  151.3 0.7 collective-permute-start.39
  152.0 2.5 %collective-permute-done.41.refs_3_ = bf16[128,512]{1,0:T(8,128)(2,1)S(1)} collective-permute-done((bf16[128,512]{1,0:T(8,128)(2,1)S(1)}, bf16[128,512]{1,0:T(8,128)(2,1)S(1)}, u32[]{:S(2)}, u32[]{:S(2)}) %collective-permute-start.41) | collective-permute-done | bytes 131104 | tf_op jit(solution)/shard_map/ppermute | solution.py:512
  154.5 1.3 collective-permute-done.40.refs_2_
  156.4 1.3 shard_map.134.refs_2_
  157.7 0.6 collective-permute-done.42.refs_1_
  158.3 1.0 copy-done.1
  159.3 1.5 shard_map.136
  (74 shorter events, 8.0 us)
Async XLA Ops:
  1.3 1.0 copy-start.3
  2.4 8.1 %copy-start.2 = (bf16[4,1,512,512]{3,2,1,0:T(8,128)(2,1)S(1)}, bf16[4,1,512,512]{3,2,1,0:T(8,128)(2,1)}, u32[]{:S(2)}) copy-start(bf16[4,1,512,512]{3,2,1,0:T(8,128)(2,1)} %param.8) | copy-start | bytes 6291460
  2.4 8.1 %copy-start.5 = (s32[1,1,48]{2,1,0:T(1,128)S(1)}, s32[1,1,48]{2,1,0:T(1,128)}, u32[]{:S(2)}) copy-start(s32[1,1,48]{2,1,0:T(1,128)} %param.11) | copy-start | bytes 580
  2.4 10.4 %slice-start = ((s8[6291456]{0:T(1024)(128)(4,1)}), s8[4194304]{0:T(1024)(128)(4,1)S(1)}, s32[]{:S(2)}) async-start(s8[6291456]{0:T(1024)(128)(4,1)} %bitcast.8), calls=%async_computation | async-start | bytes 8388608
  2.9 21.4 %collective-permute-start.7 = (bf16[2,512,256]{2,1,0:T(8,128)(2,1)S(1)}, bf16[2,512,256]{2,1,0:T(8,128)(2,1)S(1)}, u32[]{:S(2)}, u32[]{:S(2)}) collective-permute-start(bf16[2,512,256]{2,1,0:T(8,128)(2,1)S(1)} %get-tuple-element.60.refs_3_), channel_id=1, source_target_pairs={{2,4},{3,5},{4,2},{5,3},{10,12},{11,13},{12,10},{13,11},{18,20},{1... | collective-permute-start | bytes 1572872 | tf_op jit(solution)/shard_map/ppermute | solution.py:501
  3.8 20.6 %collective-permute-start.6 = (bf16[2,512,256]{2,1,0:T(8,128)(2,1)S(1)}, bf16[2,512,256]{2,1,0:T(8,128)(2,1)S(1)}, u32[]{:S(2)}, u32[]{:S(2)}) collective-permute-start(bf16[2,512,256]{2,1,0:T(8,128)(2,1)S(1)} %get-tuple-element.60.refs_3_), channel_id=1, source_target_pairs={{0,2},{1,3},{2,0},{3,1},{4,6},{5,7},{6,4},{7,5},{8,10},{9,11},{10,... | collective-permute-start | bytes 1572872 | tf_op jit(solution)/shard_map/ppermute | solution.py:501
  10.4 2.4 %slice-start.1 = ((s8[6291456]{0:T(1024)(128)(4,1)}), s8[2097152]{0:T(1024)(128)(4,1)S(1)}, s32[]{:S(2)}) async-start(s8[6291456]{0:T(1024)(128)(4,1)} %bitcast.8), calls=%async_computation.1 | async-start | bytes 4194304
  16.0 4.2 %collective-permute-start = (bf16[8,256,512]{2,1,0:T(8,128)(2,1)S(1)}, bf16[8,256,512]{2,1,0:T(8,128)(2,1)S(1)}, u32[]{:S(2)}, u32[]{:S(2)}) collective-permute-start(bf16[8,256,512]{2,1,0:T(8,128)(2,1)S(1)} %shard_map.106.refs_2_), channel_id=1, source_target_pairs={{0,1},{1,0},{2,3},{3,2},{4,5},{5,4},{6,7},{7,6},{8,9},{9,8},{10,11... | collective-permute-start | bytes 6291464 | tf_op jit(solution)/shard_map/ppermute | solution.py:509
  20.7 15.9 %collective-permute-start.1 = (bf16[2,256,512]{2,1,0:T(8,128)(2,1)S(1)}, bf16[2,256,512]{2,1,0:T(8,128)(2,1)S(1)}, u32[]{:S(2)}, u32[]{:S(2)}) collective-permute-start(bf16[2,256,512]{2,1,0:T(8,128)(2,1)S(1)} %get-tuple-element.57.refs_0_), channel_id=1, source_target_pairs={{0,2},{1,3},{6,4},{7,5},{8,10},{9,11},{14,12},{15,13},{16,18},{17,... | collective-permute-start | bytes 1572872 | tf_op jit(solution)/shard_map/ppermute | solution.py:501
  24.5 13.0 %collective-permute-start.8 = (bf16[2,512,256]{2,1,0:T(8,128)(2,1)S(1)}, bf16[2,512,256]{2,1,0:T(8,128)(2,1)S(1)}, u32[]{:S(2)}, u32[]{:S(2)}) collective-permute-start(bf16[2,512,256]{2,1,0:T(8,128)(2,1)S(1)} %get-tuple-element.61.refs_4_), channel_id=1, source_target_pairs={{2,4},{3,5},{4,2},{5,3},{10,12},{11,13},{12,10},{13,11},{18,20},{1... | collective-permute-start | bytes 1572872 | tf_op jit(solution)/shard_map/ppermute | solution.py:501
  25.2 21.9 %collective-permute-start.4 = (bf16[2,256,512]{2,1,0:T(8,128)(2,1)S(1)}, bf16[2,256,512]{2,1,0:T(8,128)(2,1)S(1)}, u32[]{:S(2)}, u32[]{:S(2)}) collective-permute-start(bf16[2,256,512]{2,1,0:T(8,128)(2,1)S(1)} %get-tuple-element.56.refs_0_), channel_id=1, source_target_pairs={{0,2},{1,3},{6,4},{7,5},{8,10},{9,11},{14,12},{15,13},{16,18},{17,... | collective-permute-start | bytes 1572872 | tf_op jit(solution)/shard_map/ppermute | solution.py:501
  27.7 19.6 %collective-permute-start.9 = (bf16[2,512,256]{2,1,0:T(8,128)(2,1)S(1)}, bf16[2,512,256]{2,1,0:T(8,128)(2,1)S(1)}, u32[]{:S(2)}, u32[]{:S(2)}) collective-permute-start(bf16[2,512,256]{2,1,0:T(8,128)(2,1)S(1)} %get-tuple-element.62.refs_1_), channel_id=1, source_target_pairs={{2,0},{3,1},{4,6},{5,7},{10,8},{11,9},{12,14},{13,15},{18,16},{19,... | collective-permute-start | bytes 1572872 | tf_op jit(solution)/shard_map/ppermute | solution.py:501
  36.7 10.4 %collective-permute-start.2 = (bf16[2,256,512]{2,1,0:T(8,128)(2,1)S(1)}, bf16[2,256,512]{2,1,0:T(8,128)(2,1)S(1)}, u32[]{:S(2)}, u32[]{:S(2)}) collective-permute-start(bf16[2,256,512]{2,1,0:T(8,128)(2,1)S(1)} %shard_map.108.refs_2_), channel_id=1, source_target_pairs={{2,4},{3,5},{4,2},{5,3},{10,12},{11,13},{12,10},{13,11},{18,20},{1... | collective-permute-start | bytes 1572872 | tf_op jit(solution)/shard_map/ppermute | solution.py:501
  37.5 17.0 %collective-permute-start.10 = (bf16[2,512,256]{2,1,0:T(8,128)(2,1)S(1)}, bf16[2,512,256]{2,1,0:T(8,128)(2,1)S(1)}, u32[]{:S(2)}, u32[]{:S(2)}) collective-permute-start(bf16[2,512,256]{2,1,0:T(8,128)(2,1)S(1)} %shard_map.112.refs_0_), channel_id=1, source_target_pairs={{2,0},{3,1},{4,6},{5,7},{10,8},{11,9},{12,14},{13,15},{18,16},{19,... | collective-permute-start | bytes 1572872 | tf_op jit(solution)/shard_map/ppermute | solution.py:501
  38.8 19.2 %collective-permute-start.11 = (bf16[2,512,256]{2,1,0:T(8,128)(2,1)S(1)}, bf16[2,512,256]{2,1,0:T(8,128)(2,1)S(1)}, u32[]{:S(2)}, u32[]{:S(2)}) collective-permute-start(bf16[2,512,256]{2,1,0:T(8,128)(2,1)S(1)} %get-tuple-element.60.refs_3_), channel_id=1, source_target_pairs={{0,1},{1,0},{2,3},{3,2},{4,5},{5,4},{6,7},{7,6},{8,9},{9,8},{10,11... | collective-permute-start | bytes 1572872 | tf_op jit(solution)/shard_map/ppermute | solution.py:509
  47.0 10.9 %collective-permute-start.12 = (bf16[2,512,256]{2,1,0:T(8,128)(2,1)S(1)}, bf16[2,512,256]{2,1,0:T(8,128)(2,1)S(1)}, u32[]{:S(2)}, u32[]{:S(2)}) collective-permute-start(bf16[2,512,256]{2,1,0:T(8,128)(2,1)S(1)} %get-tuple-element.61.refs_4_), channel_id=1, source_target_pairs={{0,1},{1,0},{2,3},{3,2},{4,5},{5,4},{6,7},{7,6},{8,9},{9,8},{10,11... | collective-permute-start | bytes 1572872 | tf_op jit(solution)/shard_map/ppermute | solution.py:509
  54.6 3.9 %collective-permute-start.13 = (bf16[1,512,256]{2,1,0:T(8,128)(2,1)S(1)}, bf16[1,512,256]{2,1,0:T(8,128)(2,1)S(1)}, u32[]{:S(2)}, u32[]{:S(2)}) collective-permute-start(bf16[1,512,256]{2,1,0:T(8,128)(2,1)S(1)} %get-tuple-element.63.refs_5_), channel_id=1, source_target_pairs={{0,1},{1,0},{2,3},{3,2},{4,5},{5,4},{6,7},{7,6},{8,9},{9,8},{10,11... | collective-permute-start | bytes 786440 | tf_op jit(solution)/shard_map/ppermute | solution.py:509
  54.7 10.7 %collective-permute-start.5 = (bf16[2,256,512]{2,1,0:T(8,128)(2,1)S(1)}, bf16[2,256,512]{2,1,0:T(8,128)(2,1)S(1)}, u32[]{:S(2)}, u32[]{:S(2)}) collective-permute-start(bf16[2,256,512]{2,1,0:T(8,128)(2,1)S(1)} %shard_map.110.refs_4_), channel_id=1, source_target_pairs={{2,4},{3,5},{4,2},{5,3},{10,12},{11,13},{12,10},{13,11},{18,20},{1... | collective-permute-start | bytes 1572872 | tf_op jit(solution)/shard_map/ppermute | solution.py:501
  55.4 14.9 %collective-permute-start.3 = (bf16[2,256,512]{2,1,0:T(8,128)(2,1)S(1)}, bf16[2,256,512]{2,1,0:T(8,128)(2,1)S(1)}, u32[]{:S(2)}, u32[]{:S(2)}) collective-permute-start(bf16[2,256,512]{2,1,0:T(8,128)(2,1)S(1)} %shard_map.109.refs_5_), channel_id=1, source_target_pairs={{0,2},{1,3},{2,0},{3,1},{4,6},{5,7},{6,4},{7,5},{8,10},{9,11},{10,... | collective-permute-start | bytes 1572872 | tf_op jit(solution)/shard_map/ppermute | solution.py:501
  58.0 1.5 collective-permute-start.14
  58.0 1.9 %collective-permute-start.15 = (bf16[1,512,256]{2,1,0:T(8,128)(2,1)S(1)}, bf16[1,512,256]{2,1,0:T(8,128)(2,1)S(1)}, u32[]{:S(2)}, u32[]{:S(2)}) collective-permute-start(bf16[1,512,256]{2,1,0:T(8,128)(2,1)S(1)} %get-tuple-element.65.refs_7_), channel_id=1, source_target_pairs={{0,1},{1,0},{2,3},{3,2},{4,5},{5,4},{6,7},{7,6},{8,9},{9,8},{10,11... | collective-permute-start | bytes 786440 | tf_op jit(solution)/shard_map/ppermute | solution.py:509
  58.5 1.8 %collective-permute-start.16 = (bf16[1,512,256]{2,1,0:T(8,128)(2,1)S(1)}, bf16[1,512,256]{2,1,0:T(8,128)(2,1)S(1)}, u32[]{:S(2)}, u32[]{:S(2)}) collective-permute-start(bf16[1,512,256]{2,1,0:T(8,128)(2,1)S(1)} %get-tuple-element.66.refs_8_), channel_id=1, source_target_pairs={{0,1},{1,0},{2,3},{3,2},{4,5},{5,4},{6,7},{7,6},{8,9},{9,8},{10,11... | collective-permute-start | bytes 786440 | tf_op jit(solution)/shard_map/ppermute | solution.py:509
  65.4 6.8 %copy-start = (bf16[512,512]{1,0:T(8,128)(2,1)S(1)}, bf16[512,512]{1,0:T(8,128)(2,1)}, u32[]{:S(2)}) copy-start(bf16[512,512]{1,0:T(8,128)(2,1)} %refs_4_.6) | copy-start | bytes 1572868
  70.5 4.9 %copy-start.4 = (bf16[512,512]{1,0:T(8,128)(2,1)S(1)}, bf16[512,512]{1,0:T(8,128)(2,1)}, u32[]{:S(2)}) copy-start(bf16[512,512]{1,0:T(8,128)(2,1)} %refs_4_.7) | copy-start | bytes 1572868
  70.5 9.3 %collective-permute-start.17 = (bf16[256,512]{1,0:T(8,128)(2,1)S(1)}, bf16[256,512]{1,0:T(8,128)(2,1)S(1)}, u32[]{:S(2)}, u32[]{:S(2)}) collective-permute-start(bf16[256,512]{1,0:T(8,128)(2,1)S(1)} %get-tuple-element.67.refs_0_), channel_id=1, source_target_pairs={{0,8},{8,0},{16,24},{24,16},{1,9},{9,1},{17,25},{25,17},{2,10},{10... | collective-permute-start | bytes 786440 | tf_op jit(solution)/shard_map/ppermute | solution.py:512
  71.7 9.2 %collective-permute-start.19 = (bf16[256,512]{1,0:T(8,128)(2,1)S(1)}, bf16[256,512]{1,0:T(8,128)(2,1)S(1)}, u32[]{:S(2)}, u32[]{:S(2)}) collective-permute-start(bf16[256,512]{1,0:T(8,128)(2,1)S(1)} %get-tuple-element.68.refs_1_), channel_id=1, source_target_pairs={{0,16},{8,24},{16,0},{24,8},{1,17},{9,25},{17,1},{25,9},{2,18},{10... | collective-permute-start | bytes 786440 | tf_op jit(solution)/shard_map/ppermute | solution.py:512
  72.9 12.5 %collective-permute-start.21 = (bf16[256,512]{1,0:T(8,128)(2,1)S(1)}, bf16[256,512]{1,0:T(8,128)(2,1)S(1)}, u32[]{:S(2)}, u32[]{:S(2)}) collective-permute-start(bf16[256,512]{1,0:T(8,128)(2,1)S(1)} %get-tuple-element.70), channel_id=1, source_target_pairs={{0,8},{8,0},{16,24},{24,16},{1,9},{9,1},{17,25},{25,17},{2,10},{10... | collective-permute-start | bytes 786440 | tf_op jit(solution)/shard_map/ppermute | solution.py:512
  73.5 13.0 %collective-permute-start.22 = (bf16[256,512]{1,0:T(8,128)(2,1)S(1)}, bf16[256,512]{1,0:T(8,128)(2,1)S(1)}, u32[]{:S(2)}, u32[]{:S(2)}) collective-permute-start(bf16[256,512]{1,0:T(8,128)(2,1)S(1)} %get-tuple-element.71), channel_id=1, source_target_pairs={{0,16},{8,24},{16,0},{24,8},{1,17},{9,25},{17,1},{25,9},{2,18},{10... | collective-permute-start | bytes 786440 | tf_op jit(solution)/shard_map/ppermute | solution.py:512
  79.8 12.2 %collective-permute-start.18 = (bf16[256,512]{1,0:T(8,128)(2,1)S(1)}, bf16[256,512]{1,0:T(8,128)(2,1)S(1)}, u32[]{:S(2)}, u32[]{:S(2)}) collective-permute-start(bf16[256,512]{1,0:T(8,128)(2,1)S(1)} %collective-permute-done.17.refs_0_), channel_id=1, source_target_pairs={{0,16},{8,24},{16,0},{24,8},{1,17},{9,25},{17,1},{25,9},{2,18},{10... | collective-permute-start | bytes 786440 | tf_op jit(solution)/shard_map/ppermute | solution.py:512
  80.9 11.1 %collective-permute-start.20 = (bf16[256,512]{1,0:T(8,128)(2,1)S(1)}, bf16[256,512]{1,0:T(8,128)(2,1)S(1)}, u32[]{:S(2)}, u32[]{:S(2)}) collective-permute-start(bf16[256,512]{1,0:T(8,128)(2,1)S(1)} %collective-permute-done.19.refs_3_), channel_id=1, source_target_pairs={{0,8},{8,0},{16,24},{24,16},{1,9},{9,1},{17,25},{25,17},{2,10},{10... | collective-permute-start | bytes 786440 | tf_op jit(solution)/shard_map/ppermute | solution.py:512
  95.3 12.1 %collective-permute-start.24 = (bf16[512,512]{1,0:T(8,128)(2,1)S(1)}, bf16[512,512]{1,0:T(8,128)(2,1)S(1)}, u32[]{:S(2)}, u32[]{:S(2)}) collective-permute-start(bf16[512,512]{1,0:T(8,128)(2,1)S(1)} %get-tuple-element.85), channel_id=1, source_target_pairs={{0,1},{1,0},{2,3},{3,2},{4,5},{5,4},{6,7},{7,6},{8,9},{9,8},{10,11... | collective-permute-start | bytes 1572872 | tf_op jit(solution)/shard_map/ppermute | solution.py:509
  98.6 4.2 %collective-permute-start.23 = (bf16[8,256,512]{2,1,0:T(8,128)(2,1)S(1)}, bf16[8,256,512]{2,1,0:T(8,128)(2,1)S(1)}, u32[]{:S(2)}, u32[]{:S(2)}) collective-permute-start(bf16[8,256,512]{2,1,0:T(8,128)(2,1)S(1)} %shard_map.124), channel_id=1, source_target_pairs={{0,1},{1,0},{2,3},{3,2},{4,5},{5,4},{6,7},{7,6},{8,9},{9,8},{10,11... | collective-permute-start | bytes 6291464 | tf_op jit(solution)/shard_map/ppermute | solution.py:509
  103.3 32.2 %collective-permute-start.34 = (bf16[2,256,512]{2,1,0:T(8,128)(2,1)S(1)}, bf16[2,256,512]{2,1,0:T(8,128)(2,1)S(1)}, u32[]{:S(2)}, u32[]{:S(2)}) collective-permute-start(bf16[2,256,512]{2,1,0:T(8,128)(2,1)S(1)} %get-tuple-element.94.refs_0_), channel_id=1, source_target_pairs={{0,2},{1,3},{6,4},{7,5},{8,10},{9,11},{14,12},{15,13},{16,18},{17,... | collective-permute-start | bytes 1572872 | tf_op jit(solution)/shard_map/ppermute | solution.py:501
  107.6 6.4 %collective-permute-start.25 = (bf16[128,512]{1,0:T(8,128)(2,1)S(1)}, bf16[128,512]{1,0:T(8,128)(2,1)S(1)}, u32[]{:S(2)}, u32[]{:S(2)}) collective-permute-start(bf16[128,512]{1,0:T(8,128)(2,1)S(1)} %get-tuple-element.87), channel_id=1, source_target_pairs={{0,8},{8,0},{16,24},{24,16},{1,9},{9,1},{17,25},{25,17},{2,10},{10... | collective-permute-start | bytes 393224 | tf_op jit(solution)/shard_map/ppermute | solution.py:512
  108.3 7.8 %collective-permute-start.26 = (bf16[128,512]{1,0:T(8,128)(2,1)S(1)}, bf16[128,512]{1,0:T(8,128)(2,1)S(1)}, u32[]{:S(2)}, u32[]{:S(2)}) collective-permute-start(bf16[128,512]{1,0:T(8,128)(2,1)S(1)} %get-tuple-element.88), channel_id=1, source_target_pairs={{0,16},{8,24},{16,0},{24,8},{1,17},{9,25},{17,1},{25,9},{2,18},{10... | collective-permute-start | bytes 393224 | tf_op jit(solution)/shard_map/ppermute | solution.py:512
  108.5 7.6 %collective-permute-start.27 = (bf16[128,512]{1,0:T(8,128)(2,1)S(1)}, bf16[128,512]{1,0:T(8,128)(2,1)S(1)}, u32[]{:S(2)}, u32[]{:S(2)}) collective-permute-start(bf16[128,512]{1,0:T(8,128)(2,1)S(1)} %get-tuple-element.89), channel_id=1, source_target_pairs={{0,24},{8,16},{16,8},{24,0},{1,25},{9,17},{17,9},{25,1},{2,26},{10... | collective-permute-start | bytes 393224 | tf_op jit(solution)/shard_map/ppermute | solution.py:512
  116.2 4.5 %collective-permute-start.28 = (bf16[32,512]{1,0:T(8,128)(2,1)S(1)}, bf16[32,512]{1,0:T(8,128)(2,1)S(1)}, u32[]{:S(2)}, u32[]{:S(2)}) collective-permute-start(bf16[32,512]{1,0:T(8,128)(2,1)S(1)} %get-tuple-element.91), channel_id=1, source_target_pairs={{0,2},{1,3},{2,0},{3,1},{4,6},{5,7},{6,4},{7,5},{8,10},{9,11},{10,... | collective-permute-start | bytes 98312 | tf_op jit(solution)/shard_map/ppermute | solution.py:501
  116.3 5.0 %collective-permute-start.29 = (bf16[32,512]{1,0:T(8,128)(2,1)S(1)}, bf16[32,512]{1,0:T(8,128)(2,1)S(1)}, u32[]{:S(2)}, u32[]{:S(2)}) collective-permute-start(bf16[32,512]{1,0:T(8,128)(2,1)S(1)} %get-tuple-element.92), channel_id=1, source_target_pairs={{0,4},{1,5},{2,6},{3,7},{4,0},{5,1},{6,2},{7,3},{8,12},{9,13},{10,... | collective-permute-start | bytes 98312 | tf_op jit(solution)/shard_map/ppermute | solution.py:501
  119.4 5.7 %collective-permute-start.30 = (bf16[32,512]{1,0:T(8,128)(2,1)S(1)}, bf16[32,512]{1,0:T(8,128)(2,1)S(1)}, u32[]{:S(2)}, u32[]{:S(2)}) collective-permute-start(bf16[32,512]{1,0:T(8,128)(2,1)S(1)} %get-tuple-element.93), channel_id=1, source_target_pairs={{0,6},{1,7},{2,4},{3,5},{4,2},{5,3},{6,0},{7,1},{8,14},{9,15},{10,... | collective-permute-start | bytes 98312 | tf_op jit(solution)/shard_map/ppermute | solution.py:501
  125.1 5.8 %collective-permute-start.33 = (bf16[32,512]{1,0:T(8,128)(2,1)S(1)}, bf16[32,512]{1,0:T(8,128)(2,1)S(1)}, u32[]{:S(2)}, u32[]{:S(2)}) collective-permute-start(bf16[32,512]{1,0:T(8,128)(2,1)S(1)} %shard_map.128.refs_0_), channel_id=1, source_target_pairs={{0,6},{1,7},{2,4},{3,5},{4,2},{5,3},{6,0},{7,1},{8,14},{9,15},{10,... | collective-permute-start | bytes 98312 | tf_op jit(solution)/shard_map/ppermute | solution.py:501
  126.4 5.2 %collective-permute-start.32 = (bf16[32,512]{1,0:T(8,128)(2,1)S(1)}, bf16[32,512]{1,0:T(8,128)(2,1)S(1)}, u32[]{:S(2)}, u32[]{:S(2)}) collective-permute-start(bf16[32,512]{1,0:T(8,128)(2,1)S(1)} %shard_map.128.refs_0_), channel_id=1, source_target_pairs={{0,4},{1,5},{2,6},{3,7},{4,0},{5,1},{6,2},{7,3},{8,12},{9,13},{10,... | collective-permute-start | bytes 98312 | tf_op jit(solution)/shard_map/ppermute | solution.py:501
  126.4 5.3 %collective-permute-start.31 = (bf16[32,512]{1,0:T(8,128)(2,1)S(1)}, bf16[32,512]{1,0:T(8,128)(2,1)S(1)}, u32[]{:S(2)}, u32[]{:S(2)}) collective-permute-start(bf16[32,512]{1,0:T(8,128)(2,1)S(1)} %shard_map.128.refs_0_), channel_id=1, source_target_pairs={{0,2},{1,3},{2,0},{3,1},{4,6},{5,7},{6,4},{7,5},{8,10},{9,11},{10,... | collective-permute-start | bytes 98312 | tf_op jit(solution)/shard_map/ppermute | solution.py:501
  131.8 11.4 %collective-permute-start.37 = (bf16[2,256,512]{2,1,0:T(8,128)(2,1)S(1)}, bf16[2,256,512]{2,1,0:T(8,128)(2,1)S(1)}, u32[]{:S(2)}, u32[]{:S(2)}) collective-permute-start(bf16[2,256,512]{2,1,0:T(8,128)(2,1)S(1)} %shard_map.130.refs_0_), channel_id=1, source_target_pairs={{0,2},{1,3},{6,4},{7,5},{8,10},{9,11},{14,12},{15,13},{16,18},{17,... | collective-permute-start | bytes 1572872 | tf_op jit(solution)/shard_map/ppermute | solution.py:501
  135.6 8.5 %collective-permute-start.35 = (bf16[2,256,512]{2,1,0:T(8,128)(2,1)S(1)}, bf16[2,256,512]{2,1,0:T(8,128)(2,1)S(1)}, u32[]{:S(2)}, u32[]{:S(2)}) collective-permute-start(bf16[2,256,512]{2,1,0:T(8,128)(2,1)S(1)} %shard_map.131.refs_2_), channel_id=1, source_target_pairs={{2,4},{3,5},{4,2},{5,3},{10,12},{11,13},{12,10},{13,11},{18,20},{1... | collective-permute-start | bytes 1572872 | tf_op jit(solution)/shard_map/ppermute | solution.py:501
  143.4 13.1 %collective-permute-start.38 = (bf16[2,256,512]{2,1,0:T(8,128)(2,1)S(1)}, bf16[2,256,512]{2,1,0:T(8,128)(2,1)S(1)}, u32[]{:S(2)}, u32[]{:S(2)}) collective-permute-start(bf16[2,256,512]{2,1,0:T(8,128)(2,1)S(1)} %shard_map.133), channel_id=1, source_target_pairs={{2,4},{3,5},{4,2},{5,3},{10,12},{11,13},{12,10},{13,11},{18,20},{1... | collective-permute-start | bytes 1572872 | tf_op jit(solution)/shard_map/ppermute | solution.py:501
  144.2 12.2 %collective-permute-start.36 = (bf16[2,256,512]{2,1,0:T(8,128)(2,1)S(1)}, bf16[2,256,512]{2,1,0:T(8,128)(2,1)S(1)}, u32[]{:S(2)}, u32[]{:S(2)}) collective-permute-start(bf16[2,256,512]{2,1,0:T(8,128)(2,1)S(1)} %shard_map.132), channel_id=1, source_target_pairs={{0,2},{1,3},{2,0},{3,1},{4,6},{5,7},{6,4},{7,5},{8,10},{9,11},{10,... | collective-permute-start | bytes 1572872 | tf_op jit(solution)/shard_map/ppermute | solution.py:501
  148.6 6.0 %collective-permute-start.41 = (bf16[128,512]{1,0:T(8,128)(2,1)S(1)}, bf16[128,512]{1,0:T(8,128)(2,1)S(1)}, u32[]{:S(2)}, u32[]{:S(2)}) collective-permute-start(bf16[128,512]{1,0:T(8,128)(2,1)S(1)} %shard_map.129.refs_1_.refs_0_), channel_id=1, source_target_pairs={{0,24},{8,16},{16,8},{24,0},{1,25},{9,17},{17,9},{25,1},{2,26},{10... | collective-permute-start | bytes 393224 | tf_op jit(solution)/shard_map/ppermute | solution.py:512
  149.9 5.9 %collective-permute-start.40 = (bf16[128,512]{1,0:T(8,128)(2,1)S(1)}, bf16[128,512]{1,0:T(8,128)(2,1)S(1)}, u32[]{:S(2)}, u32[]{:S(2)}) collective-permute-start(bf16[128,512]{1,0:T(8,128)(2,1)S(1)} %shard_map.129.refs_1_.refs_0_), channel_id=1, source_target_pairs={{0,16},{8,24},{16,0},{24,8},{1,17},{9,25},{17,1},{25,9},{2,18},{10... | collective-permute-start | bytes 393224 | tf_op jit(solution)/shard_map/ppermute | solution.py:512
  151.3 5.0 %collective-permute-start.39 = (bf16[128,512]{1,0:T(8,128)(2,1)S(1)}, bf16[128,512]{1,0:T(8,128)(2,1)S(1)}, u32[]{:S(2)}, u32[]{:S(2)}) collective-permute-start(bf16[128,512]{1,0:T(8,128)(2,1)S(1)} %shard_map.129.refs_1_.refs_0_), channel_id=1, source_target_pairs={{0,8},{8,0},{16,24},{24,16},{1,9},{9,1},{17,25},{25,17},{2,10},{10... | collective-permute-start | bytes 393224 | tf_op jit(solution)/shard_map/ppermute | solution.py:512
  156.3 2.0 %collective-permute-start.42 = (bf16[512,512]{1,0:T(8,128)(2,1)S(1)}, bf16[512,512]{1,0:T(8,128)(2,1)S(1)}, u32[]{:S(2)}, u32[]{:S(2)}) collective-permute-start(bf16[512,512]{1,0:T(8,128)(2,1)S(1)} %shard_map.135.refs_0_), channel_id=1, source_target_pairs={{0,1},{1,0},{2,3},{3,2},{4,5},{5,4},{6,7},{7,6},{8,9},{9,8},{10,11... | collective-permute-start | bytes 1572872 | tf_op jit(solution)/shard_map/ppermute | solution.py:509
  158.3 1.0 copy-start.1

commit v10 on v9

--- a/solution.py
+++ b/solution.py
@@ -15,8 +15,9 @@
 ANY = pl.BlockSpec(memory_space=pl.ANY)
 
 
-def run(body, args, specs, outs, scratch=(), mib=8, after=(), out_specs=None):
+def run(body, args, specs, outs, scratch=(), mib=8, after=(), out_specs=None, cost=None):
     n, extra = len(args), len(after)
+    cost = COST.get(getattr(body, "func", body), 0) if cost is None else cost
 
     def whole(*refs):
         body(*refs[:n], *refs[n + extra :])
@@ -29,7 +30,7 @@
         scratch_shapes=list(scratch),
         compiler_params=pltpu.CompilerParams(vmem_limit_bytes=mib * MIB),
         cost_estimate=pl.CostEstimate(
-            flops=int(COST.get(getattr(body, "func", body), 0) * 1e9),
+            flops=int(cost * 1e9),
             bytes_accessed=0,
             transcendentals=0,
         ),
@@ -161,9 +162,9 @@
     )
 
 
-def forward_body(first, flip, number_ref, list_ref, tiles, source, out, total):
+def forward_body(first, flip, parts, number_ref, list_ref, tiles, source, out, total):
     col, row = lax.axis_index("col"), lax.axis_index("row")
-    line = out.shape[0] // 2
+    n = out.shape[0] // (2 * len(parts))
 
     def product(pieces):
         def locate(v):
@@ -171,30 +172,31 @@
 
         return joined_dot([tiles[s] for s, _ in pieces], [source[locate(v)] for _, v in pieces])
 
-    for half in range(2):
-
-        def block(i, _):
-            def store(value):
-                out[half * line + i] = value.astype(BF16)
-
-            g = (col ^ (2 * i + flip)) * 2 + half
-            sum_group(g, number_ref, list_ref, total, product, store)
-            return 0
-
-        lax.fori_loop(0, line, block, 0)
-
-
-def forward(number, entries, tiles, source, first, flip, after=()):
-    slots_n, edge, _ = tiles.shape
-    width = source.shape[-1]
-    return run(
-        functools.partial(forward_body, first, flip),
+    for place, part in enumerate(parts):
+        for half in range(2):
+
+            def block(i, _):
+                def store(value):
+                    out[(2 * place + half) * n + i] = value.astype(BF16)
+
+                g = (col ^ (2 * (part * n + i) + flip)) * 2 + half
+                sum_group(g, number_ref, list_ref, total, product, store)
+                return 0
+
+            lax.fori_loop(0, n, block, 0)
+
+
+def forward(number, entries, tiles, source, first, flip, parts, after=()):
+    edge, width = tiles.shape[-1], source.shape[-1]
+    return run(
+        functools.partial(forward_body, first, flip, parts),
         (number, entries, tiles, source),
         [SMEM, SMEM, VMEM, VMEM],
-        [shape((number.shape[0] // 2, edge, width))],
+        [shape((len(parts) * number.shape[0] // 4, edge, width))],
         [pltpu.VMEM((edge, width), F32)],
         mib=16,
         after=after,
+        cost=36 if parts == (0,) else 20,
     )[0]
 
 
@@ -238,22 +240,21 @@
     )[0]
 
 
-def pair_sum_body(n, keep, come, *outs):
+def pair_sum_body(start, n, keep, come, *outs):
     for j in range(n):
         for half in range(2):
             i = half * n + j
-            outs[j][half] = (keep[i].astype(F32) + come[i].astype(F32)).astype(BF16)
-
-
-def pair_sum(keep, come, after=()):
+            outs[j][half] = (keep[i].astype(F32) + come[start + i].astype(F32)).astype(BF16)
+
+
+def pair_sum(keep, come, start):
     n = keep.shape[0] // 2
     return run(
-        functools.partial(pair_sum_body, n),
+        functools.partial(pair_sum_body, start, n),
         (keep, come),
         [VMEM] * 2,
         [shape((2, *keep.shape[1:]))] * n,
         mib=12,
-        after=after,
     )
 
 
@@ -482,7 +483,6 @@
 COST = {
     scale_body: 36,
     prepare_body: 36,
-    forward_body: 36,
     grad_body: 36,
     second_body: 36,
 }
@@ -511,13 +511,13 @@
     def row_flip(value, j):
         return lax.ppermute(value, "row", [(a, a ^ j) for a in range(n_row)])
 
-    def scatter_line(own, behind):
+    def scatter_line(own, behind, after=()):
         if line != 4:
             return [own[0]] + [line_flip(own[j], j) for j in range(1, line)], own[:2]
         to_three = col_send(own[3], [(0, 1), (3, 2)])
         to_two = col_send(behind, [(0, 1), (3, 2)])
-        crossing = sum_parts([behind, to_three])
-        meeting = sum_parts([own[3], to_two], (crossing,))
+        crossing = sum_parts([behind, to_three], own[:1])
+        meeting = sum_parts([own[3], to_two], (crossing, *after))
         crossed = col_send(crossing, [(1, 2), (2, 1)])
         met = col_send(meeting, [(1, 2), (2, 1)])
         outward = sum_parts([own[1], crossed])
@@ -550,14 +550,22 @@
         count, slots, values, scale, 2 * n_col
     )
 
-    give = forward(number, entries, tiles, first_in, True, 1)
-    keep = forward(number, entries, tiles, first_in, True, 0)
+    def run_pass(source, first, after):
+        sums = {}
+        come = core_flip(forward(number, entries, tiles, source, first, 1, (1, 0), after))
+        for place, part in enumerate((1, 0)):
+            keep = forward(number, entries, tiles, source, first, 0, (part,), after)
+            sums[part] = pair_sum(keep, come, place * line)
+            after = sums[part][:1]
+        return sums[0], sums[1]
+
+    own_near, own_far = run_pass(first_in, True, ())
+    own = (*own_near, *own_far)
     if early:
-        early = relay(early, (give,))
-    own = pair_sum(keep, core_flip(give))
-    parts, late = scatter_line(own, own[2])
+        early = relay(early, own_near[:1])
+    parts, late = scatter_line(own, relay(own[2:3], own_near[:1])[0])
     if early:
-        gathered = gather_far(scaled, *early, (own[0],), late)
+        gathered = gather_far(scaled, *early, own_far[:1], late)
     else:
         gathered = [scaled] + [line_flip(scaled, j) for j in range(1, line)]
     ranged = gathered + [core_flip(g) for g in gathered]
@@ -572,22 +580,23 @@
         sums = weight_grads(start, hidden, *stacked, scale, w_first, w_second, sums)
 
     grad_give, grad_keep = sums
-    give = forward(number, entries, tiles, stacked[1], False, 1, (grad_keep,))
-    keep = forward(number, entries, tiles, stacked[1], False, 0)
-    own = pair_sum(keep, core_flip(give))
-    split = split_sum([grad_keep, core_flip(grad_give)], n_row, "row", own[:1])
+    own_near, own_far = run_pass(stacked[1], False, (grad_keep,))
+    own = (*own_near, *own_far)
+    split = split_sum([grad_keep, core_flip(grad_give)], n_row, "row", own_near[:1])
     moment = [split[0]] + [row_flip(split[j], j) for j in range(1, n_row)]
     if split[0].shape[0] % (16 * line) == 0:
         split = split_sum(moment, line, "line")
-        moment = sum_parts([split[0]] + [line_flip(split[j], j) for j in range(1, line)])
+        moment = [split[0]] + [line_flip(split[j], j) for j in range(1, line)]
+        summed = moment = sum_parts(moment)
         moment = join([moment] + [line_flip(moment, j) for j in range(1, line)], "line")
     else:
         moment = sum_parts(moment)
-        moment = sum_parts([moment] + [line_flip(moment, j) for j in range(1, line)])
-    (behind,) = relay(own[2:3], (moment,))
+        moment = [moment] + [line_flip(moment, j) for j in range(1, line)]
+        summed = moment = sum_parts(moment)
+    (behind,) = relay(own[2:3], (summed,))
+    parts, _ = scatter_line(own, behind, (moment,))
     moment = [moment] + [row_flip(moment, j) for j in range(1, n_row)]
     mine = join(moment, "row")
-    parts, _ = scatter_line(own, behind)
     logits = second_layer(parts, scale, w_second)
     return logits, *select(mine, core_flip(mine), (logits,))
 

time: 161 us -> 174 us (1.081)
  Pallas kernels: 37 us -> 45.8 us
  waiting for transfers between devices: 62.8 us -> 69.4 us
  starting transfers between devices: 56.4 us -> 52.9 us
    pallas_call x34 -> x39, Pallas kernels: 37 us -> 45.8 us  [run(): pl.pallas_call(whole, out_shape=outs, in_specs=specs + [ANY] * extra, out...]
    ppermute x21, waiting for transfers between devices: 41.4 us -> 49 us  [col_send(): lax.ppermute(value, 'col', [(2 * a + k, 2 * b + k) for a, b in pairs for...]
    ppermute x21, starting transfers between devices: 42.7 us -> 36.6 us  [col_send(): lax.ppermute(value, 'col', [(2 * a + k, 2 * b + k) for a, b in pairs for...]
  transfers between devices with their start and end apart: 43 -> 43, of which waited for: 25 -> 24; matrix products, arithmetic and copies ran while one was open for 0% -> 0% of each run, Pallas kernels for 20% -> 18%
where the time goes in v10:
time: 174 us
  waiting for transfers between devices  69.4 us (40%)
  starting transfers between devices  52.9 us (30%)
  Pallas kernels  45.8 us (26%)
  local copies, waits for them, and re-layouts  3.83 us (2%)
  between operations  1.84 us (1%)
    ppermute x21, waiting for transfers between devices, col_send(): lax.ppermute(value, 'col', [(2 * a + k, 2 * b + k) for a, b in pairs for...  49 us
    pallas_call x39, Pallas kernels, run(): pl.pallas_call(whole, out_shape=outs, in_specs=specs + [ANY] * extra, out...  45.8 us
    ppermute x21, starting transfers between devices, col_send(): lax.ppermute(value, 'col', [(2 * a + k, 2 * b + k) for a, b in pairs for...  36.6 us
    ppermute x12, waiting for transfers between devices, row_flip(): return lax.ppermute(value, 'row', [(a, a ^ j) for a in range(n_row)])  17.3 us
    ppermute x12, starting transfers between devices, row_flip(): return lax.ppermute(value, 'row', [(a, a ^ j) for a in range(n_row)])  13.4 us
    unnamed x17, local copies, waits for them, and re-layouts  3.83 us
  transfers between devices with their start and end apart: 43, of which 24 were waited for; matrix products, arithmetic and copies ran while one was open for 0% of the time, Pallas kernels for 18%

profile of v10, /device:TPU:0, one launch (start us, length us, event | category | flops | bytes accessed | tf_op | source)
XLA Modules:
  0.0 173.8 jit_solution(7087302508461417863)
XLA Ops:
  1.3 0.7 copy.13
  2.0 1.0 copy-done.3
  3.6 1.0 copy-done.2
  4.6 2.6 %shard_map.104 = (bf16[8,256,512]{2,1,0:T(8,128)(2,1)S(1)}, s32[16]{0:T(128)S(1)}, s32[128]{0:T(128)S(1)}, s32[8]{0:T(128)S(1)}, s32[128]{0:T(128)S(1)}) custom-call(s32[1]{0:T(128)} %bitcast.7.refs_0_, s32[48]{0:T(128)S(1)} %bitcast.19, bf16[8,256,512]{2,1,0:T(8,128)(2,1)S(1)} %bitcast.18, f32[8,256,128]{2,1,0:T(8,128)S(1)} %get-tuple-element.50.refs_3_.refs_2_.refs_4_), custom_call_target="tpu_custom_call" | custom-call | flops 35999997952 | tf_op jit(solution)/shard_map/pallas_call | solution.py:25
  7.3 3.3 %shard_map.106 = bf16[8,256,512]{2,1,0:T(8,128)(2,1)S(1)} custom-call(s32[16]{0:T(128)S(1)} %get-tuple-element.51.refs_0_, s32[128]{0:T(128)S(1)} %get-tuple-element.52.refs_1_, bf16[48,256,256]{2,1,0:T(8,128)(2,1)S(1)} %bitcast.10, bf16[8,256,512]{2,1,0:T(8,128)(2,1)S(1)} %get-tuple-element.53.refs_3_), custom_call_target="tpu_custom_call" | custom-call | flops 20000000000 | tf_op jit(solution)/shard_map/pallas_call | solution.py:25
  10.6 1.6 collective-permute-start
  12.8 4.9 %collective-permute-start.6 = (bf16[2,512,256]{2,1,0:T(8,128)(2,1)S(1)}, bf16[2,512,256]{2,1,0:T(8,128)(2,1)S(1)}, u32[]{:S(2)}, u32[]{:S(2)}) collective-permute-start(bf16[2,512,256]{2,1,0:T(8,128)(2,1)S(1)} %get-tuple-element.60.refs_3_), channel_id=1, source_target_pairs={{0,2},{1,3},{2,0},{3,1},{4,6},{5,7},{6,4},{7,5},{8,10},{9,11},{10,... | collective-permute-start | bytes 1572872 | tf_op jit(solution)/shard_map/ppermute | solution.py:501
  17.7 2.8 %shard_map.105.refs_0_ = bf16[4,256,512]{2,1,0:T(8,128)(2,1)S(1)} custom-call(s32[16]{0:T(128)S(1)} %get-tuple-element.51.refs_0_, s32[128]{0:T(128)S(1)} %get-tuple-element.52.refs_1_, bf16[48,256,256]{2,1,0:T(8,128)(2,1)S(1)} %bitcast.11, bf16[8,256,512]{2,1,0:T(8,128)(2,1)S(1)} %get-tuple-element.53.refs_3_), custom_call_target="tpu_custom_call" | custom-call | flops 20000000000 | tf_op jit(solution)/shard_map/pallas_call | solution.py:25
  20.8 2.5 %shard_map.108.refs_0_ = bf16[4,256,512]{2,1,0:T(8,128)(2,1)S(1)} custom-call(s32[16]{0:T(128)S(1)} %get-tuple-element.51.refs_0_, s32[128]{0:T(128)S(1)} %get-tuple-element.52.refs_1_, bf16[48,256,256]{2,1,0:T(8,128)(2,1)S(1)} %bitcast.12, bf16[8,256,512]{2,1,0:T(8,128)(2,1)S(1)} %get-tuple-element.53.refs_3_, ...), custom_call_target="tpu_custom_call" | custom-call | flops 35999997952 | tf_op jit(solution)/shard_map/pallas_call | solution.py:25
  23.3 1.3 collective-permute-start.1
  24.9 5.1 %collective-permute-done.6.refs_0_ = bf16[2,512,256]{2,1,0:T(8,128)(2,1)S(1)} collective-permute-done((bf16[2,512,256]{2,1,0:T(8,128)(2,1)S(1)}, bf16[2,512,256]{2,1,0:T(8,128)(2,1)S(1)}, u32[]{:S(2)}, u32[]{:S(2)}) %collective-permute-start.6) | collective-permute-done | bytes 524320 | tf_op jit(solution)/shard_map/ppermute | solution.py:501
  30.1 0.7 collective-permute-start.8
  30.8 5.6 %collective-permute-start.4 = (bf16[2,256,512]{2,1,0:T(8,128)(2,1)S(1)}, bf16[2,256,512]{2,1,0:T(8,128)(2,1)S(1)}, u32[]{:S(2)}, u32[]{:S(2)}) collective-permute-start(bf16[2,256,512]{2,1,0:T(8,128)(2,1)S(1)} %shard_map.110.refs_0_), channel_id=1, source_target_pairs={{0,2},{1,3},{6,4},{7,5},{8,10},{9,11},{14,12},{15,13},{16,18},{17,... | collective-permute-start | bytes 1572872 | tf_op jit(solution)/shard_map/ppermute | solution.py:501
  36.5 4.8 %collective-permute-done.1.refs_1_ = bf16[2,256,512]{2,1,0:T(8,128)(2,1)S(1)} collective-permute-done((bf16[2,256,512]{2,1,0:T(8,128)(2,1)S(1)}, bf16[2,256,512]{2,1,0:T(8,128)(2,1)S(1)}, u32[]{:S(2)}, u32[]{:S(2)}) %collective-permute-start.1) | collective-permute-done | bytes 524320 | tf_op jit(solution)/shard_map/ppermute | solution.py:501
  42.1 1.3 collective-permute-start.9
  43.4 1.3 collective-permute-start.10
  44.8 6.9 %collective-permute-done.4.refs_1_ = bf16[2,256,512]{2,1,0:T(8,128)(2,1)S(1)} collective-permute-done((bf16[2,256,512]{2,1,0:T(8,128)(2,1)S(1)}, bf16[2,256,512]{2,1,0:T(8,128)(2,1)S(1)}, u32[]{:S(2)}, u32[]{:S(2)}) %collective-permute-start.4) | collective-permute-done | bytes 524320 | tf_op jit(solution)/shard_map/ppermute | solution.py:501
  52.0 7.9 %collective-permute-done.9.refs_2_ = bf16[2,512,256]{2,1,0:T(8,128)(2,1)S(1)} collective-permute-done((bf16[2,512,256]{2,1,0:T(8,128)(2,1)S(1)}, bf16[2,512,256]{2,1,0:T(8,128)(2,1)S(1)}, u32[]{:S(2)}, u32[]{:S(2)}) %collective-permute-start.9) | collective-permute-done | bytes 524320 | tf_op jit(solution)/shard_map/ppermute | solution.py:501
  59.9 9.5 %collective-permute-done.10.refs_3_ = bf16[2,512,256]{2,1,0:T(8,128)(2,1)S(1)} collective-permute-done((bf16[2,512,256]{2,1,0:T(8,128)(2,1)S(1)}, bf16[2,512,256]{2,1,0:T(8,128)(2,1)S(1)}, u32[]{:S(2)}, u32[]{:S(2)}) %collective-permute-start.10) | collective-permute-done | bytes 524320 | tf_op jit(solution)/shard_map/ppermute | solution.py:501
  69.5 0.9 collective-permute-start.5
  70.4 2.2 %collective-permute-start.3 = (bf16[2,256,512]{2,1,0:T(8,128)(2,1)S(1)}, bf16[2,256,512]{2,1,0:T(8,128)(2,1)S(1)}, u32[]{:S(2)}, u32[]{:S(2)}) collective-permute-start(bf16[2,256,512]{2,1,0:T(8,128)(2,1)S(1)} %shard_map.112.refs_5_), channel_id=1, source_target_pairs={{0,2},{1,3},{2,0},{3,1},{4,6},{5,7},{6,4},{7,5},{8,10},{9,11},{10,... | collective-permute-start | bytes 1572872 | tf_op jit(solution)/shard_map/ppermute | solution.py:501
  73.2 0.9 collective-permute-done.14.refs_12_
  74.9 8.4 %shard_map.117.refs_4_.refs_0_ = bf16[8,512,256]{2,1,0:T(8,128)(2,1)S(1)} custom-call(s32[8]{0:T(128)S(1)} %get-tuple-element.58.refs_0_, s32[128]{0:T(128)S(1)} %get-tuple-element.59.refs_1_, bf16[48,256,256]{2,1,0:T(8,128)(2,1)S(1)} %bitcast.13, bf16[2,512,256]{2,1,0:T(8,128)(2,1)S(1)} %get-tuple-element.60.refs_3_, ...), custom_call_target="tpu_custom_call" | custom-call | tf_op jit(solution)/shard_map/pallas_call | solution.py:25
  83.4 1.6 collective-permute-done.3.refs_1_
  85.2 1.7 collective-permute-start.17
  86.9 1.0 collective-permute-start.19
  89.0 1.0 collective-permute-start.22
  90.0 2.2 %shard_map.121 = (f32[512,512]{1,0:T(8,128)S(1)}, f32[512,512]{1,0:T(8,128)S(1)}) custom-call(bf16[8,512,256]{2,1,0:T(8,128)(2,1)S(1)} %shard_map.117.refs_4_.refs_0_, bf16[2,256,512]{2,1,0:T(8,128)(2,1)S(1)} %get-tuple-element.69.refs_2_.refs_1_.refs_6_, bf16[2,256,512]{2,1,0:T(8,128)(2,1)S(1)} %get-tuple-element.72.refs_2_.refs_7_, ...), custom_call_target="tpu_custom_call" | custom-call | flops 35999997952 | tf_op jit(solution)/shard_map/pallas_call | solution.py:25
  92.3 2.2 %collective-permute-done.17.refs_0_ = bf16[256,512]{1,0:T(8,128)(2,1)S(1)} collective-permute-done((bf16[256,512]{1,0:T(8,128)(2,1)S(1)}, bf16[256,512]{1,0:T(8,128)(2,1)S(1)}, u32[]{:S(2)}, u32[]{:S(2)}) %collective-permute-start.17) | collective-permute-done | bytes 262176 | tf_op jit(solution)/shard_map/ppermute | solution.py:512
  94.5 1.0 collective-permute-start.18
  95.4 0.7 collective-permute-done.19.refs_3_
  96.1 1.0 collective-permute-start.20
  97.1 3.0 %collective-permute-done.21.refs_1_ = bf16[256,512]{1,0:T(8,128)(2,1)S(1)} collective-permute-done((bf16[256,512]{1,0:T(8,128)(2,1)S(1)}, bf16[256,512]{1,0:T(8,128)(2,1)S(1)}, u32[]{:S(2)}, u32[]{:S(2)}) %collective-permute-start.21) | collective-permute-done | bytes 262176 | tf_op jit(solution)/shard_map/ppermute | solution.py:512
  100.1 1.7 collective-permute-done.22.refs_2_
  101.7 1.1 shard_map.122
  102.8 4.3 %shard_map.123 = (f32[512,512]{1,0:T(8,128)S(1)}, f32[512,512]{1,0:T(8,128)S(1)}) custom-call(bf16[8,512,256]{2,1,0:T(8,128)(2,1)S(1)} %shard_map.117.refs_4_.refs_0_, bf16[6,256,512]{2,1,0:T(8,128)(2,1)S(1)} %get-tuple-element.74.refs_1_.refs_4_, bf16[6,256,512]{2,1,0:T(8,128)(2,1)S(1)} %get-tuple-element.75.refs_2_.refs_5_, ...), custom_call_target="tpu_custom_call" | custom-call | flops 35999997952 | tf_op jit(solution)/shard_map/pallas_call | solution.py:25
  107.2 0.9 shard_map.124
  108.1 2.4 %shard_map.125 = (bf16[512,512]{1,0:T(8,128)(2,1)S(1)}, bf16[512,512]{1,0:T(8,128)(2,1)S(1)}) custom-call(bf16[8,512,256]{2,1,0:T(8,128)(2,1)S(1)} %shard_map.117.refs_4_.refs_0_, bf16[8,256,512]{2,1,0:T(8,128)(2,1)S(1)} %get-tuple-element.79.refs_1_, bf16[8,256,512]{2,1,0:T(8,128)(2,1)S(1)} %get-tuple-element.78.refs_2_.refs_3_, ...), custom_call_target="tpu_custom_call" | custom-call | flops 35999997952 | tf_op jit(solution)/shard_map/pallas_call | solution.py:25
  110.5 3.5 %shard_map.127 = bf16[8,256,512]{2,1,0:T(8,128)(2,1)S(1)} custom-call(s32[16]{0:T(128)S(1)} %get-tuple-element.51.refs_0_, s32[128]{0:T(128)S(1)} %get-tuple-element.52.refs_1_, bf16[48,256,256]{2,1,0:T(8,128)(2,1)S(1)} %bitcast.14, bf16[8,256,512]{2,1,0:T(8,128)(2,1)S(1)} %get-tuple-element.78.refs_2_.refs_3_, ...), custom_call_target="tpu_custom_call" | custom-call | flops 20000000000 | tf_op jit(solution)/shard_map/pallas_call | solution.py:25
  114.6 2.8 %shard_map.126.refs_0_ = bf16[4,256,512]{2,1,0:T(8,128)(2,1)S(1)} custom-call(s32[16]{0:T(128)S(1)} %get-tuple-element.51.refs_0_, s32[128]{0:T(128)S(1)} %get-tuple-element.52.refs_1_, bf16[48,256,256]{2,1,0:T(8,128)(2,1)S(1)} %bitcast.15, bf16[8,256,512]{2,1,0:T(8,128)(2,1)S(1)} %get-tuple-element.78.refs_2_.refs_3_, ...), custom_call_target="tpu_custom_call" | custom-call | flops 20000000000 | tf_op jit(solution)/shard_map/pallas_call | solution.py:25
  117.5 0.8 collective-permute-done.23.refs_1_
  118.5 3.2 %collective-permute-start.31 = (bf16[2,256,512]{2,1,0:T(8,128)(2,1)S(1)}, bf16[2,256,512]{2,1,0:T(8,128)(2,1)S(1)}, u32[]{:S(2)}, u32[]{:S(2)}) collective-permute-start(bf16[2,256,512]{2,1,0:T(8,128)(2,1)S(1)} %get-tuple-element.94.refs_0_), channel_id=1, source_target_pairs={{0,2},{1,3},{6,4},{7,5},{8,10},{9,11},{14,12},{15,13},{16,18},{17,... | collective-permute-start | bytes 1572872 | tf_op jit(solution)/shard_map/ppermute | solution.py:501
  121.7 2.5 %shard_map.129.refs_0_ = bf16[4,256,512]{2,1,0:T(8,128)(2,1)S(1)} custom-call(s32[16]{0:T(128)S(1)} %get-tuple-element.51.refs_0_, s32[128]{0:T(128)S(1)} %get-tuple-element.52.refs_1_, bf16[48,256,256]{2,1,0:T(8,128)(2,1)S(1)} %bitcast.16, bf16[8,256,512]{2,1,0:T(8,128)(2,1)S(1)} %get-tuple-element.78.refs_2_.refs_3_, ...), custom_call_target="tpu_custom_call" | custom-call | flops 35999997952 | tf_op jit(solution)/shard_map/pallas_call | solution.py:25
  125.6 2.5 %collective-permute-start.27 = (bf16[128,512]{1,0:T(8,128)(2,1)S(1)}, bf16[128,512]{1,0:T(8,128)(2,1)S(1)}, u32[]{:S(2)}, u32[]{:S(2)}) collective-permute-start(bf16[128,512]{1,0:T(8,128)(2,1)S(1)} %get-tuple-element.89), channel_id=1, source_target_pairs={{0,24},{8,16},{16,8},{24,0},{1,25},{9,17},{17,9},{25,1},{2,26},{10... | collective-permute-start | bytes 393224 | tf_op jit(solution)/shard_map/ppermute | solution.py:512
  128.1 2.9 %collective-permute-done.25.refs_1_ = bf16[128,512]{1,0:T(8,128)(2,1)S(1)} collective-permute-done((bf16[128,512]{1,0:T(8,128)(2,1)S(1)}, bf16[128,512]{1,0:T(8,128)(2,1)S(1)}, u32[]{:S(2)}, u32[]{:S(2)}) %collective-permute-start.25) | collective-permute-done | bytes 131104 | tf_op jit(solution)/shard_map/ppermute | solution.py:512
  131.0 1.9 %collective-permute-done.26.refs_2_ = bf16[128,512]{1,0:T(8,128)(2,1)S(1)} collective-permute-done((bf16[128,512]{1,0:T(8,128)(2,1)S(1)}, bf16[128,512]{1,0:T(8,128)(2,1)S(1)}, u32[]{:S(2)}, u32[]{:S(2)}) %collective-permute-start.26) | collective-permute-done | bytes 131104 | tf_op jit(solution)/shard_map/ppermute | solution.py:512
  133.1 3.1 %collective-permute-start.29 = (bf16[32,512]{1,0:T(8,128)(2,1)S(1)}, bf16[32,512]{1,0:T(8,128)(2,1)S(1)}, u32[]{:S(2)}, u32[]{:S(2)}) collective-permute-start(bf16[32,512]{1,0:T(8,128)(2,1)S(1)} %get-tuple-element.92), channel_id=1, source_target_pairs={{0,4},{1,5},{2,6},{3,7},{4,0},{5,1},{6,2},{7,3},{8,12},{9,13},{10,... | collective-permute-start | bytes 98312 | tf_op jit(solution)/shard_map/ppermute | solution.py:501
  136.2 1.3 collective-permute-start.30
  138.0 3.8 %collective-permute-done.30.refs_3_ = bf16[32,512]{1,0:T(8,128)(2,1)S(1)} collective-permute-done((bf16[32,512]{1,0:T(8,128)(2,1)S(1)}, bf16[32,512]{1,0:T(8,128)(2,1)S(1)}, u32[]{:S(2)}, u32[]{:S(2)}) %collective-permute-start.30) | collective-permute-done | bytes 32800 | tf_op jit(solution)/shard_map/ppermute | solution.py:501
  141.9 1.3 collective-permute-start.34
  144.1 1.4 collective-permute-start.37
  145.5 1.0 collective-permute-start.36
  146.5 2.1 %collective-permute-start.35 = (bf16[32,512]{1,0:T(8,128)(2,1)S(1)}, bf16[32,512]{1,0:T(8,128)(2,1)S(1)}, u32[]{:S(2)}, u32[]{:S(2)}) collective-permute-start(bf16[32,512]{1,0:T(8,128)(2,1)S(1)} %shard_map.133.refs_1_.refs_0_), channel_id=1, source_target_pairs={{0,2},{1,3},{2,0},{3,1},{4,6},{5,7},{6,4},{7,5},{8,10},{9,11},{10,... | collective-permute-start | bytes 98312 | tf_op jit(solution)/shard_map/ppermute | solution.py:501
  148.6 7.0 %collective-permute-done.37.refs_3_ = bf16[32,512]{1,0:T(8,128)(2,1)S(1)} collective-permute-done((bf16[32,512]{1,0:T(8,128)(2,1)S(1)}, bf16[32,512]{1,0:T(8,128)(2,1)S(1)}, u32[]{:S(2)}, u32[]{:S(2)}) %collective-permute-start.37) | collective-permute-done | bytes 32800 | tf_op jit(solution)/shard_map/ppermute | solution.py:501
  155.6 1.8 %collective-permute-done.36.refs_2_ = bf16[32,512]{1,0:T(8,128)(2,1)S(1)} collective-permute-done((bf16[32,512]{1,0:T(8,128)(2,1)S(1)}, bf16[32,512]{1,0:T(8,128)(2,1)S(1)}, u32[]{:S(2)}, u32[]{:S(2)}) %collective-permute-start.36) | collective-permute-done | bytes 32800 | tf_op jit(solution)/shard_map/ppermute | solution.py:501
  158.4 2.2 %collective-permute-start.33 = (bf16[2,256,512]{2,1,0:T(8,128)(2,1)S(1)}, bf16[2,256,512]{2,1,0:T(8,128)(2,1)S(1)}, u32[]{:S(2)}, u32[]{:S(2)}) collective-permute-start(bf16[2,256,512]{2,1,0:T(8,128)(2,1)S(1)} %shard_map.136), channel_id=1, source_target_pairs={{0,2},{1,3},{2,0},{3,1},{4,6},{5,7},{6,4},{7,5},{8,10},{9,11},{10,... | collective-permute-start | bytes 1572872 | tf_op jit(solution)/shard_map/ppermute | solution.py:501
  160.6 1.6 collective-permute-start.41
  162.2 2.1 %collective-permute-start.40 = (bf16[128,512]{1,0:T(8,128)(2,1)S(1)}, bf16[128,512]{1,0:T(8,128)(2,1)S(1)}, u32[]{:S(2)}, u32[]{:S(2)}) collective-permute-start(bf16[128,512]{1,0:T(8,128)(2,1)S(1)} %shard_map.137.refs_3_.refs_0_), channel_id=1, source_target_pairs={{0,16},{8,24},{16,0},{24,8},{1,17},{9,25},{17,1},{25,9},{2,18},{10... | collective-permute-start | bytes 393224 | tf_op jit(solution)/shard_map/ppermute | solution.py:512
  164.3 2.2 %collective-permute-done.41.refs_3_ = bf16[128,512]{1,0:T(8,128)(2,1)S(1)} collective-permute-done((bf16[128,512]{1,0:T(8,128)(2,1)S(1)}, bf16[128,512]{1,0:T(8,128)(2,1)S(1)}, u32[]{:S(2)}, u32[]{:S(2)}) %collective-permute-start.41) | collective-permute-done | bytes 131104 | tf_op jit(solution)/shard_map/ppermute | solution.py:512
  166.5 1.3 collective-permute-done.40.refs_2_
  167.9 1.4 collective-permute-done.39.refs_1_
  169.5 1.3 shard_map.139.refs_2_
  171.3 1.0 copy-done.1
  172.4 1.5 shard_map.141
  (79 shorter events, 11.3 us)
Async XLA Ops:
  2.0 1.0 copy-start.3
  3.0 1.6 copy-start.2
  3.0 1.6 copy-start.5
  3.0 4.2 %slice-start = ((s8[6291456]{0:T(1024)(128)(4,1)}), s8[4194304]{0:T(1024)(128)(4,1)S(1)}, s32[]{:S(2)}) async-start(s8[6291456]{0:T(1024)(128)(4,1)} %bitcast.8), calls=%async_computation | async-start | bytes 8388608
  3.6 3.7 %slice-start.1 = ((s8[6291456]{0:T(1024)(128)(4,1)}), s8[2097152]{0:T(1024)(128)(4,1)S(1)}, s32[]{:S(2)}) async-start(s8[6291456]{0:T(1024)(128)(4,1)} %bitcast.8), calls=%async_computation.1 | async-start | bytes 4194304
  10.6 9.9 %collective-permute-start = (bf16[8,256,512]{2,1,0:T(8,128)(2,1)S(1)}, bf16[8,256,512]{2,1,0:T(8,128)(2,1)S(1)}, u32[]{:S(2)}, u32[]{:S(2)}) collective-permute-start(bf16[8,256,512]{2,1,0:T(8,128)(2,1)S(1)} %shard_map.106), channel_id=1, source_target_pairs={{0,1},{1,0},{2,3},{3,2},{4,5},{5,4},{6,7},{7,6},{8,9},{9,8},{10,11... | collective-permute-start | bytes 6291464 | tf_op jit(solution)/shard_map/ppermute | solution.py:509
  12.2 12.7 %collective-permute-start.7 = (bf16[2,512,256]{2,1,0:T(8,128)(2,1)S(1)}, bf16[2,512,256]{2,1,0:T(8,128)(2,1)S(1)}, u32[]{:S(2)}, u32[]{:S(2)}) collective-permute-start(bf16[2,512,256]{2,1,0:T(8,128)(2,1)S(1)} %get-tuple-element.60.refs_3_), channel_id=1, source_target_pairs={{2,4},{3,5},{4,2},{5,3},{10,12},{11,13},{12,10},{13,11},{18,20},{1... | collective-permute-start | bytes 1572872 | tf_op jit(solution)/shard_map/ppermute | solution.py:501
  12.8 17.2 %collective-permute-start.6 = (bf16[2,512,256]{2,1,0:T(8,128)(2,1)S(1)}, bf16[2,512,256]{2,1,0:T(8,128)(2,1)S(1)}, u32[]{:S(2)}, u32[]{:S(2)}) collective-permute-start(bf16[2,512,256]{2,1,0:T(8,128)(2,1)S(1)} %get-tuple-element.60.refs_3_), channel_id=1, source_target_pairs={{0,2},{1,3},{2,0},{3,1},{4,6},{5,7},{6,4},{7,5},{8,10},{9,11},{10,... | collective-permute-start | bytes 1572872 | tf_op jit(solution)/shard_map/ppermute | solution.py:501
  23.3 17.9 %collective-permute-start.1 = (bf16[2,256,512]{2,1,0:T(8,128)(2,1)S(1)}, bf16[2,256,512]{2,1,0:T(8,128)(2,1)S(1)}, u32[]{:S(2)}, u32[]{:S(2)}) collective-permute-start(bf16[2,256,512]{2,1,0:T(8,128)(2,1)S(1)} %get-tuple-element.57.refs_0_), channel_id=1, source_target_pairs={{0,2},{1,3},{6,4},{7,5},{8,10},{9,11},{14,12},{15,13},{16,18},{17,... | collective-permute-start | bytes 1572872 | tf_op jit(solution)/shard_map/ppermute | solution.py:501
  30.1 13.3 %collective-permute-start.8 = (bf16[2,512,256]{2,1,0:T(8,128)(2,1)S(1)}, bf16[2,512,256]{2,1,0:T(8,128)(2,1)S(1)}, u32[]{:S(2)}, u32[]{:S(2)}) collective-permute-start(bf16[2,512,256]{2,1,0:T(8,128)(2,1)S(1)} %get-tuple-element.61.refs_4_), channel_id=1, source_target_pairs={{2,4},{3,5},{4,2},{5,3},{10,12},{11,13},{12,10},{13,11},{18,20},{1... | collective-permute-start | bytes 1572872 | tf_op jit(solution)/shard_map/ppermute | solution.py:501
  30.8 20.9 %collective-permute-start.4 = (bf16[2,256,512]{2,1,0:T(8,128)(2,1)S(1)}, bf16[2,256,512]{2,1,0:T(8,128)(2,1)S(1)}, u32[]{:S(2)}, u32[]{:S(2)}) collective-permute-start(bf16[2,256,512]{2,1,0:T(8,128)(2,1)S(1)} %shard_map.110.refs_0_), channel_id=1, source_target_pairs={{0,2},{1,3},{6,4},{7,5},{8,10},{9,11},{14,12},{15,13},{16,18},{17,... | collective-permute-start | bytes 1572872 | tf_op jit(solution)/shard_map/ppermute | solution.py:501
  41.4 10.5 %collective-permute-start.2 = (bf16[2,256,512]{2,1,0:T(8,128)(2,1)S(1)}, bf16[2,256,512]{2,1,0:T(8,128)(2,1)S(1)}, u32[]{:S(2)}, u32[]{:S(2)}) collective-permute-start(bf16[2,256,512]{2,1,0:T(8,128)(2,1)S(1)} %shard_map.111.refs_2_), channel_id=1, source_target_pairs={{2,4},{3,5},{4,2},{5,3},{10,12},{11,13},{12,10},{13,11},{18,20},{1... | collective-permute-start | bytes 1572872 | tf_op jit(solution)/shard_map/ppermute | solution.py:501
  42.1 17.8 %collective-permute-start.9 = (bf16[2,512,256]{2,1,0:T(8,128)(2,1)S(1)}, bf16[2,512,256]{2,1,0:T(8,128)(2,1)S(1)}, u32[]{:S(2)}, u32[]{:S(2)}) collective-permute-start(bf16[2,512,256]{2,1,0:T(8,128)(2,1)S(1)} %get-tuple-element.62.refs_1_), channel_id=1, source_target_pairs={{2,0},{3,1},{4,6},{5,7},{10,8},{11,9},{12,14},{13,15},{18,16},{19,... | collective-permute-start | bytes 1572872 | tf_op jit(solution)/shard_map/ppermute | solution.py:501
  43.4 25.9 %collective-permute-start.10 = (bf16[2,512,256]{2,1,0:T(8,128)(2,1)S(1)}, bf16[2,512,256]{2,1,0:T(8,128)(2,1)S(1)}, u32[]{:S(2)}, u32[]{:S(2)}) collective-permute-start(bf16[2,512,256]{2,1,0:T(8,128)(2,1)S(1)} %shard_map.115.refs_0_), channel_id=1, source_target_pairs={{2,0},{3,1},{4,6},{5,7},{10,8},{11,9},{12,14},{13,15},{18,16},{19,... | collective-permute-start | bytes 1572872 | tf_op jit(solution)/shard_map/ppermute | solution.py:501
  44.7 27.9 %collective-permute-start.11 = (bf16[2,512,256]{2,1,0:T(8,128)(2,1)S(1)}, bf16[2,512,256]{2,1,0:T(8,128)(2,1)S(1)}, u32[]{:S(2)}, u32[]{:S(2)}) collective-permute-start(bf16[2,512,256]{2,1,0:T(8,128)(2,1)S(1)} %get-tuple-element.60.refs_3_), channel_id=1, source_target_pairs={{0,1},{1,0},{2,3},{3,2},{4,5},{5,4},{6,7},{7,6},{8,9},{9,8},{10,11... | collective-permute-start | bytes 1572872 | tf_op jit(solution)/shard_map/ppermute | solution.py:509
  51.7 20.9 %collective-permute-start.12 = (bf16[2,512,256]{2,1,0:T(8,128)(2,1)S(1)}, bf16[2,512,256]{2,1,0:T(8,128)(2,1)S(1)}, u32[]{:S(2)}, u32[]{:S(2)}) collective-permute-start(bf16[2,512,256]{2,1,0:T(8,128)(2,1)S(1)} %get-tuple-element.61.refs_4_), channel_id=1, source_target_pairs={{0,1},{1,0},{2,3},{3,2},{4,5},{5,4},{6,7},{7,6},{8,9},{9,8},{10,11... | collective-permute-start | bytes 1572872 | tf_op jit(solution)/shard_map/ppermute | solution.py:509
  69.4 3.7 %collective-permute-start.13 = (bf16[1,512,256]{2,1,0:T(8,128)(2,1)S(1)}, bf16[1,512,256]{2,1,0:T(8,128)(2,1)S(1)}, u32[]{:S(2)}, u32[]{:S(2)}) collective-permute-start(bf16[1,512,256]{2,1,0:T(8,128)(2,1)S(1)} %get-tuple-element.63.refs_5_), channel_id=1, source_target_pairs={{0,1},{1,0},{2,3},{3,2},{4,5},{5,4},{6,7},{7,6},{8,9},{9,8},{10,11... | collective-permute-start | bytes 786440 | tf_op jit(solution)/shard_map/ppermute | solution.py:509
  69.5 13.8 %collective-permute-start.5 = (bf16[2,256,512]{2,1,0:T(8,128)(2,1)S(1)}, bf16[2,256,512]{2,1,0:T(8,128)(2,1)S(1)}, u32[]{:S(2)}, u32[]{:S(2)}) collective-permute-start(bf16[2,256,512]{2,1,0:T(8,128)(2,1)S(1)} %shard_map.113.refs_4_), channel_id=1, source_target_pairs={{2,4},{3,5},{4,2},{5,3},{10,12},{11,13},{12,10},{13,11},{18,20},{1... | collective-permute-start | bytes 1572872 | tf_op jit(solution)/shard_map/ppermute | solution.py:501
  70.4 14.5 %collective-permute-start.3 = (bf16[2,256,512]{2,1,0:T(8,128)(2,1)S(1)}, bf16[2,256,512]{2,1,0:T(8,128)(2,1)S(1)}, u32[]{:S(2)}, u32[]{:S(2)}) collective-permute-start(bf16[2,256,512]{2,1,0:T(8,128)(2,1)S(1)} %shard_map.112.refs_5_), channel_id=1, source_target_pairs={{0,2},{1,3},{2,0},{3,1},{4,6},{5,7},{6,4},{7,5},{8,10},{9,11},{10,... | collective-permute-start | bytes 1572872 | tf_op jit(solution)/shard_map/ppermute | solution.py:501
  72.6 1.5 collective-permute-start.14
  72.7 1.9 %collective-permute-start.15 = (bf16[1,512,256]{2,1,0:T(8,128)(2,1)S(1)}, bf16[1,512,256]{2,1,0:T(8,128)(2,1)S(1)}, u32[]{:S(2)}, u32[]{:S(2)}) collective-permute-start(bf16[1,512,256]{2,1,0:T(8,128)(2,1)S(1)} %get-tuple-element.65.refs_7_), channel_id=1, source_target_pairs={{0,1},{1,0},{2,3},{3,2},{4,5},{5,4},{6,7},{7,6},{8,9},{9,8},{10,11... | collective-permute-start | bytes 786440 | tf_op jit(solution)/shard_map/ppermute | solution.py:509
  73.2 1.8 %collective-permute-start.16 = (bf16[1,512,256]{2,1,0:T(8,128)(2,1)S(1)}, bf16[1,512,256]{2,1,0:T(8,128)(2,1)S(1)}, u32[]{:S(2)}, u32[]{:S(2)}) collective-permute-start(bf16[1,512,256]{2,1,0:T(8,128)(2,1)S(1)} %get-tuple-element.66.refs_8_), channel_id=1, source_target_pairs={{0,1},{1,0},{2,3},{3,2},{4,5},{5,4},{6,7},{7,6},{8,9},{9,8},{10,11... | collective-permute-start | bytes 786440 | tf_op jit(solution)/shard_map/ppermute | solution.py:509
  83.3 4.6 %copy-start = (bf16[512,512]{1,0:T(8,128)(2,1)S(1)}, bf16[512,512]{1,0:T(8,128)(2,1)}, u32[]{:S(2)}) copy-start(bf16[512,512]{1,0:T(8,128)(2,1)} %refs_4_.6) | copy-start | bytes 1572868
  85.2 4.9 %copy-start.4 = (bf16[512,512]{1,0:T(8,128)(2,1)S(1)}, bf16[512,512]{1,0:T(8,128)(2,1)}, u32[]{:S(2)}) copy-start(bf16[512,512]{1,0:T(8,128)(2,1)} %refs_4_.7) | copy-start | bytes 1572868
  85.2 9.3 %collective-permute-start.17 = (bf16[256,512]{1,0:T(8,128)(2,1)S(1)}, bf16[256,512]{1,0:T(8,128)(2,1)S(1)}, u32[]{:S(2)}, u32[]{:S(2)}) collective-permute-start(bf16[256,512]{1,0:T(8,128)(2,1)S(1)} %get-tuple-element.67.refs_0_), channel_id=1, source_target_pairs={{0,8},{8,0},{16,24},{24,16},{1,9},{9,1},{17,25},{25,17},{2,10},{10... | collective-permute-start | bytes 786440 | tf_op jit(solution)/shard_map/ppermute | solution.py:512
  86.9 9.2 %collective-permute-start.19 = (bf16[256,512]{1,0:T(8,128)(2,1)S(1)}, bf16[256,512]{1,0:T(8,128)(2,1)S(1)}, u32[]{:S(2)}, u32[]{:S(2)}) collective-permute-start(bf16[256,512]{1,0:T(8,128)(2,1)S(1)} %get-tuple-element.68.refs_1_), channel_id=1, source_target_pairs={{0,16},{8,24},{16,0},{24,8},{1,17},{9,25},{17,1},{25,9},{2,18},{10... | collective-permute-start | bytes 786440 | tf_op jit(solution)/shard_map/ppermute | solution.py:512
  88.6 11.5 %collective-permute-start.21 = (bf16[256,512]{1,0:T(8,128)(2,1)S(1)}, bf16[256,512]{1,0:T(8,128)(2,1)S(1)}, u32[]{:S(2)}, u32[]{:S(2)}) collective-permute-start(bf16[256,512]{1,0:T(8,128)(2,1)S(1)} %get-tuple-element.70), channel_id=1, source_target_pairs={{0,8},{8,0},{16,24},{24,16},{1,9},{9,1},{17,25},{25,17},{2,10},{10... | collective-permute-start | bytes 786440 | tf_op jit(solution)/shard_map/ppermute | solution.py:512
  89.0 12.8 %collective-permute-start.22 = (bf16[256,512]{1,0:T(8,128)(2,1)S(1)}, bf16[256,512]{1,0:T(8,128)(2,1)S(1)}, u32[]{:S(2)}, u32[]{:S(2)}) collective-permute-start(bf16[256,512]{1,0:T(8,128)(2,1)S(1)} %get-tuple-element.71), channel_id=1, source_target_pairs={{0,16},{8,24},{16,0},{24,8},{1,17},{9,25},{17,1},{25,9},{2,18},{10... | collective-permute-start | bytes 786440 | tf_op jit(solution)/shard_map/ppermute | solution.py:512
  94.5 12.7 %collective-permute-start.18 = (bf16[256,512]{1,0:T(8,128)(2,1)S(1)}, bf16[256,512]{1,0:T(8,128)(2,1)S(1)}, u32[]{:S(2)}, u32[]{:S(2)}) collective-permute-start(bf16[256,512]{1,0:T(8,128)(2,1)S(1)} %collective-permute-done.17.refs_0_), channel_id=1, source_target_pairs={{0,16},{8,24},{16,0},{24,8},{1,17},{9,25},{17,1},{25,9},{2,18},{10... | collective-permute-start | bytes 786440 | tf_op jit(solution)/shard_map/ppermute | solution.py:512
  96.1 11.1 %collective-permute-start.20 = (bf16[256,512]{1,0:T(8,128)(2,1)S(1)}, bf16[256,512]{1,0:T(8,128)(2,1)S(1)}, u32[]{:S(2)}, u32[]{:S(2)}) collective-permute-start(bf16[256,512]{1,0:T(8,128)(2,1)S(1)} %collective-permute-done.19.refs_3_), channel_id=1, source_target_pairs={{0,8},{8,0},{16,24},{24,16},{1,9},{9,1},{17,25},{25,17},{2,10},{10... | collective-permute-start | bytes 786440 | tf_op jit(solution)/shard_map/ppermute | solution.py:512
  114.0 4.2 %collective-permute-start.23 = (bf16[8,256,512]{2,1,0:T(8,128)(2,1)S(1)}, bf16[8,256,512]{2,1,0:T(8,128)(2,1)S(1)}, u32[]{:S(2)}, u32[]{:S(2)}) collective-permute-start(bf16[8,256,512]{2,1,0:T(8,128)(2,1)S(1)} %shard_map.127), channel_id=1, source_target_pairs={{0,1},{1,0},{2,3},{3,2},{4,5},{5,4},{6,7},{7,6},{8,9},{9,8},{10,11... | collective-permute-start | bytes 6291464 | tf_op jit(solution)/shard_map/ppermute | solution.py:509
  114.1 10.3 %collective-permute-start.24 = (bf16[512,512]{1,0:T(8,128)(2,1)S(1)}, bf16[512,512]{1,0:T(8,128)(2,1)S(1)}, u32[]{:S(2)}, u32[]{:S(2)}) collective-permute-start(bf16[512,512]{1,0:T(8,128)(2,1)S(1)} %get-tuple-element.85), channel_id=1, source_target_pairs={{0,1},{1,0},{2,3},{3,2},{4,5},{5,4},{6,7},{7,6},{8,9},{9,8},{10,11... | collective-permute-start | bytes 1572872 | tf_op jit(solution)/shard_map/ppermute | solution.py:509
  118.5 24.7 %collective-permute-start.31 = (bf16[2,256,512]{2,1,0:T(8,128)(2,1)S(1)}, bf16[2,256,512]{2,1,0:T(8,128)(2,1)S(1)}, u32[]{:S(2)}, u32[]{:S(2)}) collective-permute-start(bf16[2,256,512]{2,1,0:T(8,128)(2,1)S(1)} %get-tuple-element.94.refs_0_), channel_id=1, source_target_pairs={{0,2},{1,3},{6,4},{7,5},{8,10},{9,11},{14,12},{15,13},{16,18},{17,... | collective-permute-start | bytes 1572872 | tf_op jit(solution)/shard_map/ppermute | solution.py:501
  124.6 6.4 %collective-permute-start.25 = (bf16[128,512]{1,0:T(8,128)(2,1)S(1)}, bf16[128,512]{1,0:T(8,128)(2,1)S(1)}, u32[]{:S(2)}, u32[]{:S(2)}) collective-permute-start(bf16[128,512]{1,0:T(8,128)(2,1)S(1)} %get-tuple-element.87), channel_id=1, source_target_pairs={{0,8},{8,0},{16,24},{24,16},{1,9},{9,1},{17,25},{25,17},{2,10},{10... | collective-permute-start | bytes 393224 | tf_op jit(solution)/shard_map/ppermute | solution.py:512
  125.2 7.8 %collective-permute-start.26 = (bf16[128,512]{1,0:T(8,128)(2,1)S(1)}, bf16[128,512]{1,0:T(8,128)(2,1)S(1)}, u32[]{:S(2)}, u32[]{:S(2)}) collective-permute-start(bf16[128,512]{1,0:T(8,128)(2,1)S(1)} %get-tuple-element.88), channel_id=1, source_target_pairs={{0,16},{8,24},{16,0},{24,8},{1,17},{9,25},{17,1},{25,9},{2,18},{10... | collective-permute-start | bytes 393224 | tf_op jit(solution)/shard_map/ppermute | solution.py:512
  125.6 7.3 %collective-permute-start.27 = (bf16[128,512]{1,0:T(8,128)(2,1)S(1)}, bf16[128,512]{1,0:T(8,128)(2,1)S(1)}, u32[]{:S(2)}, u32[]{:S(2)}) collective-permute-start(bf16[128,512]{1,0:T(8,128)(2,1)S(1)} %get-tuple-element.89), channel_id=1, source_target_pairs={{0,24},{8,16},{16,8},{24,0},{1,25},{9,17},{17,9},{25,1},{2,26},{10... | collective-permute-start | bytes 393224 | tf_op jit(solution)/shard_map/ppermute | solution.py:512
  133.0 4.5 %collective-permute-start.28 = (bf16[32,512]{1,0:T(8,128)(2,1)S(1)}, bf16[32,512]{1,0:T(8,128)(2,1)S(1)}, u32[]{:S(2)}, u32[]{:S(2)}) collective-permute-start(bf16[32,512]{1,0:T(8,128)(2,1)S(1)} %get-tuple-element.91), channel_id=1, source_target_pairs={{0,2},{1,3},{2,0},{3,1},{4,6},{5,7},{6,4},{7,5},{8,10},{9,11},{10,... | collective-permute-start | bytes 98312 | tf_op jit(solution)/shard_map/ppermute | solution.py:501
  133.1 5.0 %collective-permute-start.29 = (bf16[32,512]{1,0:T(8,128)(2,1)S(1)}, bf16[32,512]{1,0:T(8,128)(2,1)S(1)}, u32[]{:S(2)}, u32[]{:S(2)}) collective-permute-start(bf16[32,512]{1,0:T(8,128)(2,1)S(1)} %get-tuple-element.92), channel_id=1, source_target_pairs={{0,4},{1,5},{2,6},{3,7},{4,0},{5,1},{6,2},{7,3},{8,12},{9,13},{10,... | collective-permute-start | bytes 98312 | tf_op jit(solution)/shard_map/ppermute | solution.py:501
  136.2 5.7 %collective-permute-start.30 = (bf16[32,512]{1,0:T(8,128)(2,1)S(1)}, bf16[32,512]{1,0:T(8,128)(2,1)S(1)}, u32[]{:S(2)}, u32[]{:S(2)}) collective-permute-start(bf16[32,512]{1,0:T(8,128)(2,1)S(1)} %get-tuple-element.93), channel_id=1, source_target_pairs={{0,6},{1,7},{2,4},{3,5},{4,2},{5,3},{6,0},{7,1},{8,14},{9,15},{10,... | collective-permute-start | bytes 98312 | tf_op jit(solution)/shard_map/ppermute | solution.py:501
  141.9 15.5 %collective-permute-start.34 = (bf16[2,256,512]{2,1,0:T(8,128)(2,1)S(1)}, bf16[2,256,512]{2,1,0:T(8,128)(2,1)S(1)}, u32[]{:S(2)}, u32[]{:S(2)}) collective-permute-start(bf16[2,256,512]{2,1,0:T(8,128)(2,1)S(1)} %shard_map.134.refs_0_), channel_id=1, source_target_pairs={{0,2},{1,3},{6,4},{7,5},{8,10},{9,11},{14,12},{15,13},{16,18},{17,... | collective-permute-start | bytes 1572872 | tf_op jit(solution)/shard_map/ppermute | solution.py:501
  143.4 14.8 %collective-permute-start.32 = (bf16[2,256,512]{2,1,0:T(8,128)(2,1)S(1)}, bf16[2,256,512]{2,1,0:T(8,128)(2,1)S(1)}, u32[]{:S(2)}, u32[]{:S(2)}) collective-permute-start(bf16[2,256,512]{2,1,0:T(8,128)(2,1)S(1)} %shard_map.135.refs_2_), channel_id=1, source_target_pairs={{2,4},{3,5},{4,2},{5,3},{10,12},{11,13},{12,10},{13,11},{18,20},{1... | collective-permute-start | bytes 1572872 | tf_op jit(solution)/shard_map/ppermute | solution.py:501
  144.1 11.5 %collective-permute-start.37 = (bf16[32,512]{1,0:T(8,128)(2,1)S(1)}, bf16[32,512]{1,0:T(8,128)(2,1)S(1)}, u32[]{:S(2)}, u32[]{:S(2)}) collective-permute-start(bf16[32,512]{1,0:T(8,128)(2,1)S(1)} %shard_map.133.refs_1_.refs_0_), channel_id=1, source_target_pairs={{0,6},{1,7},{2,4},{3,5},{4,2},{5,3},{6,0},{7,1},{8,14},{9,15},{10,... | collective-permute-start | bytes 98312 | tf_op jit(solution)/shard_map/ppermute | solution.py:501
  145.5 11.9 %collective-permute-start.36 = (bf16[32,512]{1,0:T(8,128)(2,1)S(1)}, bf16[32,512]{1,0:T(8,128)(2,1)S(1)}, u32[]{:S(2)}, u32[]{:S(2)}) collective-permute-start(bf16[32,512]{1,0:T(8,128)(2,1)S(1)} %shard_map.133.refs_1_.refs_0_), channel_id=1, source_target_pairs={{0,4},{1,5},{2,6},{3,7},{4,0},{5,1},{6,2},{7,3},{8,12},{9,13},{10,... | collective-permute-start | bytes 98312 | tf_op jit(solution)/shard_map/ppermute | solution.py:501
  146.5 10.9 %collective-permute-start.35 = (bf16[32,512]{1,0:T(8,128)(2,1)S(1)}, bf16[32,512]{1,0:T(8,128)(2,1)S(1)}, u32[]{:S(2)}, u32[]{:S(2)}) collective-permute-start(bf16[32,512]{1,0:T(8,128)(2,1)S(1)} %shard_map.133.refs_1_.refs_0_), channel_id=1, source_target_pairs={{0,2},{1,3},{2,0},{3,1},{4,6},{5,7},{6,4},{7,5},{8,10},{9,11},{10,... | collective-permute-start | bytes 98312 | tf_op jit(solution)/shard_map/ppermute | solution.py:501
  157.5 11.9 %collective-permute-start.38 = (bf16[2,256,512]{2,1,0:T(8,128)(2,1)S(1)}, bf16[2,256,512]{2,1,0:T(8,128)(2,1)S(1)}, u32[]{:S(2)}, u32[]{:S(2)}) collective-permute-start(bf16[2,256,512]{2,1,0:T(8,128)(2,1)S(1)} %shard_map.138), channel_id=1, source_target_pairs={{2,4},{3,5},{4,2},{5,3},{10,12},{11,13},{12,10},{13,11},{18,20},{1... | collective-permute-start | bytes 1572872 | tf_op jit(solution)/shard_map/ppermute | solution.py:501
  158.4 11.1 %collective-permute-start.33 = (bf16[2,256,512]{2,1,0:T(8,128)(2,1)S(1)}, bf16[2,256,512]{2,1,0:T(8,128)(2,1)S(1)}, u32[]{:S(2)}, u32[]{:S(2)}) collective-permute-start(bf16[2,256,512]{2,1,0:T(8,128)(2,1)S(1)} %shard_map.136), channel_id=1, source_target_pairs={{0,2},{1,3},{2,0},{3,1},{4,6},{5,7},{6,4},{7,5},{8,10},{9,11},{10,... | collective-permute-start | bytes 1572872 | tf_op jit(solution)/shard_map/ppermute | solution.py:501
  160.6 5.9 %collective-permute-start.41 = (bf16[128,512]{1,0:T(8,128)(2,1)S(1)}, bf16[128,512]{1,0:T(8,128)(2,1)S(1)}, u32[]{:S(2)}, u32[]{:S(2)}) collective-permute-start(bf16[128,512]{1,0:T(8,128)(2,1)S(1)} %shard_map.137.refs_3_.refs_0_), channel_id=1, source_target_pairs={{0,24},{8,16},{16,8},{24,0},{1,25},{9,17},{17,9},{25,1},{2,26},{10... | collective-permute-start | bytes 393224 | tf_op jit(solution)/shard_map/ppermute | solution.py:512
  162.2 5.7 %collective-permute-start.40 = (bf16[128,512]{1,0:T(8,128)(2,1)S(1)}, bf16[128,512]{1,0:T(8,128)(2,1)S(1)}, u32[]{:S(2)}, u32[]{:S(2)}) collective-permute-start(bf16[128,512]{1,0:T(8,128)(2,1)S(1)} %shard_map.137.refs_3_.refs_0_), channel_id=1, source_target_pairs={{0,16},{8,24},{16,0},{24,8},{1,17},{9,25},{17,1},{25,9},{2,18},{10... | collective-permute-start | bytes 393224 | tf_op jit(solution)/shard_map/ppermute | solution.py:512
  164.3 5.0 %collective-permute-start.39 = (bf16[128,512]{1,0:T(8,128)(2,1)S(1)}, bf16[128,512]{1,0:T(8,128)(2,1)S(1)}, u32[]{:S(2)}, u32[]{:S(2)}) collective-permute-start(bf16[128,512]{1,0:T(8,128)(2,1)S(1)} %shard_map.137.refs_3_.refs_0_), channel_id=1, source_target_pairs={{0,8},{8,0},{16,24},{24,16},{1,9},{9,1},{17,25},{25,17},{2,10},{10... | collective-permute-start | bytes 393224 | tf_op jit(solution)/shard_map/ppermute | solution.py:512
  169.4 2.0 %collective-permute-start.42 = (bf16[512,512]{1,0:T(8,128)(2,1)S(1)}, bf16[512,512]{1,0:T(8,128)(2,1)S(1)}, u32[]{:S(2)}, u32[]{:S(2)}) collective-permute-start(bf16[512,512]{1,0:T(8,128)(2,1)S(1)} %shard_map.140.refs_0_), channel_id=1, source_target_pairs={{0,1},{1,0},{2,3},{3,2},{4,5},{5,4},{6,7},{7,6},{8,9},{9,8},{10,11... | collective-permute-start | bytes 1572872 | tf_op jit(solution)/shard_map/ppermute | solution.py:509
  171.3 1.0 copy-start.1

commit v11 on v9

--- a/solution.py
+++ b/solution.py
@@ -117,6 +117,35 @@
     )
 
 
+def sum_large_group(g, number_ref, list_ref, total, product, store):
+    cap = list_ref.shape[0] // number_ref.shape[0]
+    n = number_ref[g]
+    rest = jnp.where(n == 0, 0, ((n - 1) & 3) + 1)
+
+    def take(start, width):
+        entries = [list_ref[g * cap + start + j] for j in range(width)]
+        return product([(lax.shift_right_logical(x, 10), x & 1023) for x in entries])
+
+    @pl.when(n == 0)
+    def _():
+        total[...] = jnp.zeros_like(total)
+
+    def exact(width):
+        @pl.when(rest == width)
+        def _():
+            total[...] = take(0, width)
+
+    for width in range(1, 5):
+        exact(width)
+
+    def four(m, _):
+        total[...] += take(rest + 4 * m, 4)
+        return 0
+
+    lax.fori_loop(0, lax.shift_right_logical(n - rest, 2), four, 0)
+    store(total[...])
+
+
 def sum_group(g, number_ref, list_ref, total, product, store):
     cap = list_ref.shape[0] // number_ref.shape[0]
     n = number_ref[g]
@@ -217,7 +246,7 @@
         def store(value):
             out[i] = value.astype(BF16)
 
-        sum_group(i ^ mask, number_ref, list_ref, total, product, store)
+        sum_large_group(i ^ mask, number_ref, list_ref, total, product, store)
         return 0
 
     lax.fori_loop(0, out.shape[0], block, 0)
@@ -352,13 +381,14 @@
         out[half * edge : (half + 1) * edge, :] = value.astype(BF16)
 
 
-def second_layer(parts, scale, weight):
+def second_layer(parts, scale, weight, after):
     halves, edge, width = parts[0].shape
     return run(
         second_body,
         (*parts, scale, weight),
         [VMEM] * (2 + len(parts)),
         [shape((halves * edge, width))],
+        after=after,
     )[0]
 
 
@@ -473,10 +503,8 @@
     second[...] = jnp.where(core == 0, other[...].astype(F32), mine[...].astype(F32))
 
 
-def select(mine, other, after):
-    return run(
-        select_body, (mine, other), [VMEM] * 2, [shape(mine.shape, F32)] * 2, after=after
-    )
+def select(mine, other):
+    return run(select_body, (mine, other), [VMEM] * 2, [shape(mine.shape, F32)] * 2)
 
 
 COST = {
@@ -511,13 +539,13 @@
     def row_flip(value, j):
         return lax.ppermute(value, "row", [(a, a ^ j) for a in range(n_row)])
 
-    def scatter_line(own, behind):
+    def scatter_line(own, behind, after=()):
         if line != 4:
             return [own[0]] + [line_flip(own[j], j) for j in range(1, line)], own[:2]
         to_three = col_send(own[3], [(0, 1), (3, 2)])
         to_two = col_send(behind, [(0, 1), (3, 2)])
         crossing = sum_parts([behind, to_three])
-        meeting = sum_parts([own[3], to_two], (crossing,))
+        meeting = sum_parts([own[3], to_two], (crossing, *after))
         crossed = col_send(crossing, [(1, 2), (2, 1)])
         met = col_send(meeting, [(1, 2), (2, 1)])
         outward = sum_parts([own[1], crossed])
@@ -587,9 +615,10 @@
     (behind,) = relay(own[2:3], (moment,))
     moment = [moment] + [row_flip(moment, j) for j in range(1, n_row)]
     mine = join(moment, "row")
-    parts, _ = scatter_line(own, behind)
-    logits = second_layer(parts, scale, w_second)
-    return logits, *select(mine, core_flip(mine), (logits,))
+    parts, _ = scatter_line(own, behind, (mine,))
+    grad_first, grad_second = select(mine, core_flip(mine))
+    logits = second_layer(parts, scale, w_second, (grad_second,))
+    return logits, grad_first, grad_second
 
 
 def solution(mesh):

time: 161 us -> 164 us (1.019)
  Pallas kernels: 37 us -> 40.6 us
  waiting for transfers between devices: 62.8 us -> 61.1 us
    pallas_call x34, Pallas kernels: 37 us -> 40.6 us  [run(): pl.pallas_call(whole, out_shape=outs, in_specs=specs + [ANY] * extra, out...]
    ppermute x12, starting transfers between devices: 12.3 us -> 15.7 us  [row_flip(): return lax.ppermute(value, 'row', [(a, a ^ j) for a in range(n_row)])]
    ppermute x21, starting transfers between devices: 42.7 us -> 39.4 us  [col_send(): lax.ppermute(value, 'col', [(2 * a + k, 2 * b + k) for a, b in pairs for...]
    ppermute x10, waiting for transfers between devices: 4.26 us -> 2.03 us  [core_flip(): return lax.ppermute(value, 'col', [(a, a ^ 1) for a in range(n_col)])]
  transfers between devices with their start and end apart: 43 -> 43, of which waited for: 25 -> 21; matrix products, arithmetic and copies ran while one was open for 0% -> 0% of each run, Pallas kernels for 20% -> 22%
where the time goes in v11:
time: 164 us; the launch traced here: 163 us
  waiting for transfers between devices  61.1 us (37%)
  starting transfers between devices  56.6 us (35%)
  Pallas kernels  40.6 us (25%)
  local copies, waits for them, and re-layouts  3 us (2%)
  between operations  1.83 us (1%)
    ppermute x21, waiting for transfers between devices, col_send(): lax.ppermute(value, 'col', [(2 * a + k, 2 * b + k) for a, b in pairs for...  43 us
    pallas_call x34, Pallas kernels, run(): pl.pallas_call(whole, out_shape=outs, in_specs=specs + [ANY] * extra, out...  40.6 us
    ppermute x21, starting transfers between devices, col_send(): lax.ppermute(value, 'col', [(2 * a + k, 2 * b + k) for a, b in pairs for...  39.4 us
    ppermute x12, waiting for transfers between devices, row_flip(): return lax.ppermute(value, 'row', [(a, a ^ j) for a in range(n_row)])  16.1 us
    ppermute x12, starting transfers between devices, row_flip(): return lax.ppermute(value, 'row', [(a, a ^ j) for a in range(n_row)])  15.7 us
  transfers between devices with their start and end apart: 43, of which 21 were waited for; matrix products, arithmetic and copies ran while one was open for 0% of the time, Pallas kernels for 22%

profile of v11, /device:TPU:0, one launch (start us, length us, event | category | flops | bytes accessed | tf_op | source)
XLA Modules:
  0.0 163.2 jit_solution(199084703600097023)
XLA Ops:
  0.6 0.7 copy.13
  1.3 1.0 copy-done.3
  2.4 0.6 shard_map.103
  2.9 0.8 collective-permute-start.7
  3.8 6.0 %collective-permute-start.6 = (bf16[2,512,256]{2,1,0:T(8,128)(2,1)S(1)}, bf16[2,512,256]{2,1,0:T(8,128)(2,1)S(1)}, u32[]{:S(2)}, u32[]{:S(2)}) collective-permute-start(bf16[2,512,256]{2,1,0:T(8,128)(2,1)S(1)} %get-tuple-element.60.refs_3_), channel_id=1, source_target_pairs={{0,2},{1,3},{2,0},{3,1},{4,6},{5,7},{6,4},{7,5},{8,10},{9,11},{10,... | collective-permute-start | bytes 1572872 | tf_op jit(solution)/shard_map/ppermute | solution.py:529
  10.5 2.5 %shard_map.104 = (bf16[8,256,512]{2,1,0:T(8,128)(2,1)S(1)}, s32[16]{0:T(128)S(1)}, s32[128]{0:T(128)S(1)}, s32[8]{0:T(128)S(1)}, s32[128]{0:T(128)S(1)}) custom-call(s32[1]{0:T(128)} %bitcast.7.refs_0_, s32[48]{0:T(128)S(1)} %bitcast.17, bf16[8,256,512]{2,1,0:T(8,128)(2,1)S(1)} %bitcast.16, f32[8,256,128]{2,1,0:T(8,128)S(1)} %get-tuple-element.50.refs_3_.refs_2_.refs_4_), custom_call_target="tpu_custom_call" | custom-call | flops 35999997952 | tf_op jit(solution)/shard_map/pallas_call | solution.py:24
  13.0 3.4 %shard_map.106.refs_2_ = bf16[8,256,512]{2,1,0:T(8,128)(2,1)S(1)} custom-call(s32[16]{0:T(128)S(1)} %get-tuple-element.51.refs_0_, s32[128]{0:T(128)S(1)} %get-tuple-element.52.refs_1_, bf16[48,256,256]{2,1,0:T(8,128)(2,1)S(1)} %bitcast.10, bf16[8,256,512]{2,1,0:T(8,128)(2,1)S(1)} %get-tuple-element.53.refs_3_), custom_call_target="tpu_custom_call" | custom-call | flops 35999997952 | tf_op jit(solution)/shard_map/pallas_call | solution.py:24
  16.5 3.8 %shard_map.105.refs_0_ = bf16[8,256,512]{2,1,0:T(8,128)(2,1)S(1)} custom-call(s32[16]{0:T(128)S(1)} %get-tuple-element.51.refs_0_, s32[128]{0:T(128)S(1)} %get-tuple-element.52.refs_1_, bf16[48,256,256]{2,1,0:T(8,128)(2,1)S(1)} %bitcast.11, bf16[8,256,512]{2,1,0:T(8,128)(2,1)S(1)} %get-tuple-element.53.refs_3_), custom_call_target="tpu_custom_call" | custom-call | flops 35999997952 | tf_op jit(solution)/shard_map/pallas_call | solution.py:24
  21.1 1.7 %collective-permute-start.1 = (bf16[2,256,512]{2,1,0:T(8,128)(2,1)S(1)}, bf16[2,256,512]{2,1,0:T(8,128)(2,1)S(1)}, u32[]{:S(2)}, u32[]{:S(2)}) collective-permute-start(bf16[2,256,512]{2,1,0:T(8,128)(2,1)S(1)} %get-tuple-element.57.refs_0_), channel_id=1, source_target_pairs={{0,2},{1,3},{6,4},{7,5},{8,10},{9,11},{14,12},{15,13},{16,18},{17,... | collective-permute-start | bytes 1572872 | tf_op jit(solution)/shard_map/ppermute | solution.py:529
  22.9 0.7 collective-permute-start.8
  23.6 3.9 %collective-permute-start.4 = (bf16[2,256,512]{2,1,0:T(8,128)(2,1)S(1)}, bf16[2,256,512]{2,1,0:T(8,128)(2,1)S(1)}, u32[]{:S(2)}, u32[]{:S(2)}) collective-permute-start(bf16[2,256,512]{2,1,0:T(8,128)(2,1)S(1)} %get-tuple-element.56.refs_0_), channel_id=1, source_target_pairs={{0,2},{1,3},{6,4},{7,5},{8,10},{9,11},{14,12},{15,13},{16,18},{17,... | collective-permute-start | bytes 1572872 | tf_op jit(solution)/shard_map/ppermute | solution.py:529
  27.6 1.3 collective-permute-start.9
  28.9 6.1 %collective-permute-done.1.refs_1_ = bf16[2,256,512]{2,1,0:T(8,128)(2,1)S(1)} collective-permute-done((bf16[2,256,512]{2,1,0:T(8,128)(2,1)S(1)}, bf16[2,256,512]{2,1,0:T(8,128)(2,1)S(1)}, u32[]{:S(2)}, u32[]{:S(2)}) %collective-permute-start.1) | collective-permute-done | bytes 524320 | tf_op jit(solution)/shard_map/ppermute | solution.py:529
  35.1 0.7 collective-permute-start.2
  35.9 1.3 collective-permute-start.10
  37.3 8.6 %collective-permute-done.4.refs_1_ = bf16[2,256,512]{2,1,0:T(8,128)(2,1)S(1)} collective-permute-done((bf16[2,256,512]{2,1,0:T(8,128)(2,1)S(1)}, bf16[2,256,512]{2,1,0:T(8,128)(2,1)S(1)}, u32[]{:S(2)}, u32[]{:S(2)}) %collective-permute-start.4) | collective-permute-done | bytes 524320 | tf_op jit(solution)/shard_map/ppermute | solution.py:529
  46.1 7.8 %collective-permute-done.10.refs_3_ = bf16[2,512,256]{2,1,0:T(8,128)(2,1)S(1)} collective-permute-done((bf16[2,512,256]{2,1,0:T(8,128)(2,1)S(1)}, bf16[2,512,256]{2,1,0:T(8,128)(2,1)S(1)}, u32[]{:S(2)}, u32[]{:S(2)}) %collective-permute-start.10) | collective-permute-done | bytes 524320 | tf_op jit(solution)/shard_map/ppermute | solution.py:529
  54.1 0.9 collective-permute-start.5
  55.0 1.6 collective-permute-start.3
  57.2 0.9 collective-permute-done.14.refs_12_
  58.9 6.1 %shard_map.114.refs_4_.refs_0_ = bf16[8,512,256]{2,1,0:T(8,128)(2,1)S(1)} custom-call(s32[8]{0:T(128)S(1)} %get-tuple-element.58.refs_0_, s32[128]{0:T(128)S(1)} %get-tuple-element.59.refs_1_, bf16[48,256,256]{2,1,0:T(8,128)(2,1)S(1)} %bitcast.12, bf16[2,512,256]{2,1,0:T(8,128)(2,1)S(1)} %get-tuple-element.60.refs_3_, ...), custom_call_target="tpu_custom_call" | custom-call | tf_op jit(solution)/shard_map/pallas_call | solution.py:24
  65.0 4.3 %collective-permute-done.3.refs_1_ = bf16[2,256,512]{2,1,0:T(8,128)(2,1)S(1)} collective-permute-done((bf16[2,256,512]{2,1,0:T(8,128)(2,1)S(1)}, bf16[2,256,512]{2,1,0:T(8,128)(2,1)S(1)}, u32[]{:S(2)}, u32[]{:S(2)}) %collective-permute-start.3) | collective-permute-done | bytes 524320 | tf_op jit(solution)/shard_map/ppermute | solution.py:529
  69.6 1.2 collective-permute-start.17
  70.8 1.6 collective-permute-start.19
  72.4 0.6 shard_map.116
  73.1 2.0 %collective-permute-start.21 = (bf16[256,512]{1,0:T(8,128)(2,1)S(1)}, bf16[256,512]{1,0:T(8,128)(2,1)S(1)}, u32[]{:S(2)}, u32[]{:S(2)}) collective-permute-start(bf16[256,512]{1,0:T(8,128)(2,1)S(1)} %get-tuple-element.70), channel_id=1, source_target_pairs={{0,8},{8,0},{16,24},{24,16},{1,9},{9,1},{17,25},{25,17},{2,10},{10... | collective-permute-start | bytes 786440 | tf_op jit(solution)/shard_map/ppermute | solution.py:540
  75.1 2.2 %shard_map.118 = (f32[512,512]{1,0:T(8,128)S(1)}, f32[512,512]{1,0:T(8,128)S(1)}) custom-call(bf16[8,512,256]{2,1,0:T(8,128)(2,1)S(1)} %shard_map.114.refs_4_.refs_0_, bf16[2,256,512]{2,1,0:T(8,128)(2,1)S(1)} %get-tuple-element.69.refs_2_.refs_1_.refs_6_, bf16[2,256,512]{2,1,0:T(8,128)(2,1)S(1)} %get-tuple-element.72.refs_2_.refs_7_, ...), custom_call_target="tpu_custom_call" | custom-call | flops 35999997952 | tf_op jit(solution)/shard_map/pallas_call | solution.py:24
  77.3 1.5 collective-permute-done.17.refs_0_
  78.9 2.7 %collective-permute-start.18 = (bf16[256,512]{1,0:T(8,128)(2,1)S(1)}, bf16[256,512]{1,0:T(8,128)(2,1)S(1)}, u32[]{:S(2)}, u32[]{:S(2)}) collective-permute-start(bf16[256,512]{1,0:T(8,128)(2,1)S(1)} %collective-permute-done.17.refs_0_), channel_id=1, source_target_pairs={{0,16},{8,24},{16,0},{24,8},{1,17},{9,25},{17,1},{25,9},{2,18},{10... | collective-permute-start | bytes 786440 | tf_op jit(solution)/shard_map/ppermute | solution.py:540
  81.6 2.9 %collective-permute-done.21.refs_1_ = bf16[256,512]{1,0:T(8,128)(2,1)S(1)} collective-permute-done((bf16[256,512]{1,0:T(8,128)(2,1)S(1)}, bf16[256,512]{1,0:T(8,128)(2,1)S(1)}, u32[]{:S(2)}, u32[]{:S(2)}) %collective-permute-start.21) | collective-permute-done | bytes 262176 | tf_op jit(solution)/shard_map/ppermute | solution.py:540
  84.5 1.2 collective-permute-done.22.refs_2_
  85.7 1.1 shard_map.119
  86.8 4.3 %shard_map.120 = (f32[512,512]{1,0:T(8,128)S(1)}, f32[512,512]{1,0:T(8,128)S(1)}) custom-call(bf16[8,512,256]{2,1,0:T(8,128)(2,1)S(1)} %shard_map.114.refs_4_.refs_0_, bf16[6,256,512]{2,1,0:T(8,128)(2,1)S(1)} %get-tuple-element.74.refs_1_.refs_4_, bf16[6,256,512]{2,1,0:T(8,128)(2,1)S(1)} %get-tuple-element.75.refs_2_.refs_5_, ...), custom_call_target="tpu_custom_call" | custom-call | flops 35999997952 | tf_op jit(solution)/shard_map/pallas_call | solution.py:24
  91.1 0.9 shard_map.121
  92.0 2.4 %shard_map.123 = (bf16[512,512]{1,0:T(8,128)(2,1)S(1)}, bf16[512,512]{1,0:T(8,128)(2,1)S(1)}) custom-call(bf16[8,512,256]{2,1,0:T(8,128)(2,1)S(1)} %shard_map.114.refs_4_.refs_0_, bf16[8,256,512]{2,1,0:T(8,128)(2,1)S(1)} %get-tuple-element.79.refs_1_, bf16[8,256,512]{2,1,0:T(8,128)(2,1)S(1)} %get-tuple-element.78.refs_3_.refs_2_, ...), custom_call_target="tpu_custom_call" | custom-call | flops 35999997952 | tf_op jit(solution)/shard_map/pallas_call | solution.py:24
  94.5 3.4 %shard_map.124 = bf16[8,256,512]{2,1,0:T(8,128)(2,1)S(1)} custom-call(s32[16]{0:T(128)S(1)} %get-tuple-element.51.refs_0_, s32[128]{0:T(128)S(1)} %get-tuple-element.52.refs_1_, bf16[48,256,256]{2,1,0:T(8,128)(2,1)S(1)} %bitcast.13, bf16[8,256,512]{2,1,0:T(8,128)(2,1)S(1)} %get-tuple-element.78.refs_3_.refs_2_, ...), custom_call_target="tpu_custom_call" | custom-call | flops 35999997952 | tf_op jit(solution)/shard_map/pallas_call | solution.py:24
  98.0 0.5 collective-permute-start.23
  98.5 4.0 %shard_map.122.refs_0_ = bf16[8,256,512]{2,1,0:T(8,128)(2,1)S(1)} custom-call(s32[16]{0:T(128)S(1)} %get-tuple-element.51.refs_0_, s32[128]{0:T(128)S(1)} %get-tuple-element.52.refs_1_, bf16[48,256,256]{2,1,0:T(8,128)(2,1)S(1)} %bitcast.14, bf16[8,256,512]{2,1,0:T(8,128)(2,1)S(1)} %get-tuple-element.78.refs_3_.refs_2_), custom_call_target="tpu_custom_call" | custom-call | flops 35999997952 | tf_op jit(solution)/shard_map/pallas_call | solution.py:24
  103.0 2.7 %collective-permute-start.34 = (bf16[2,256,512]{2,1,0:T(8,128)(2,1)S(1)}, bf16[2,256,512]{2,1,0:T(8,128)(2,1)S(1)}, u32[]{:S(2)}, u32[]{:S(2)}) collective-permute-start(bf16[2,256,512]{2,1,0:T(8,128)(2,1)S(1)} %get-tuple-element.94.refs_0_), channel_id=1, source_target_pairs={{0,2},{1,3},{6,4},{7,5},{8,10},{9,11},{14,12},{15,13},{16,18},{17,... | collective-permute-start | bytes 1572872 | tf_op jit(solution)/shard_map/ppermute | solution.py:529
  105.9 2.3 %collective-permute-start.25 = (bf16[128,512]{1,0:T(8,128)(2,1)S(1)}, bf16[128,512]{1,0:T(8,128)(2,1)S(1)}, u32[]{:S(2)}, u32[]{:S(2)}) collective-permute-start(bf16[128,512]{1,0:T(8,128)(2,1)S(1)} %get-tuple-element.87), channel_id=1, source_target_pairs={{0,8},{8,0},{16,24},{24,16},{1,9},{9,1},{17,25},{25,17},{2,10},{10... | collective-permute-start | bytes 393224 | tf_op jit(solution)/shard_map/ppermute | solution.py:540
  108.1 2.1 %collective-permute-start.26 = (bf16[128,512]{1,0:T(8,128)(2,1)S(1)}, bf16[128,512]{1,0:T(8,128)(2,1)S(1)}, u32[]{:S(2)}, u32[]{:S(2)}) collective-permute-start(bf16[128,512]{1,0:T(8,128)(2,1)S(1)} %get-tuple-element.88), channel_id=1, source_target_pairs={{0,16},{8,24},{16,0},{24,8},{1,17},{9,25},{17,1},{25,9},{2,18},{10... | collective-permute-start | bytes 393224 | tf_op jit(solution)/shard_map/ppermute | solution.py:540
  110.4 1.4 collective-permute-done.25.refs_1_
  111.9 3.7 %collective-permute-done.26.refs_2_ = bf16[128,512]{1,0:T(8,128)(2,1)S(1)} collective-permute-done((bf16[128,512]{1,0:T(8,128)(2,1)S(1)}, bf16[128,512]{1,0:T(8,128)(2,1)S(1)}, u32[]{:S(2)}, u32[]{:S(2)}) %collective-permute-start.26) | collective-permute-done | bytes 131104 | tf_op jit(solution)/shard_map/ppermute | solution.py:540
  115.6 1.5 collective-permute-done.27.refs_3_
  117.3 1.8 %collective-permute-start.29 = (bf16[32,512]{1,0:T(8,128)(2,1)S(1)}, bf16[32,512]{1,0:T(8,128)(2,1)S(1)}, u32[]{:S(2)}, u32[]{:S(2)}) collective-permute-start(bf16[32,512]{1,0:T(8,128)(2,1)S(1)} %get-tuple-element.92), channel_id=1, source_target_pairs={{0,4},{1,5},{2,6},{3,7},{4,0},{5,1},{6,2},{7,3},{8,12},{9,13},{10,... | collective-permute-start | bytes 98312 | tf_op jit(solution)/shard_map/ppermute | solution.py:529
  119.1 2.6 %collective-permute-start.30 = (bf16[32,512]{1,0:T(8,128)(2,1)S(1)}, bf16[32,512]{1,0:T(8,128)(2,1)S(1)}, u32[]{:S(2)}, u32[]{:S(2)}) collective-permute-start(bf16[32,512]{1,0:T(8,128)(2,1)S(1)} %get-tuple-element.93), channel_id=1, source_target_pairs={{0,6},{1,7},{2,4},{3,5},{4,2},{5,3},{6,0},{7,1},{8,14},{9,15},{10,... | collective-permute-start | bytes 98312 | tf_op jit(solution)/shard_map/ppermute | solution.py:529
  121.7 1.1 collective-permute-done.29.refs_2_
  122.8 2.1 %collective-permute-done.30.refs_3_ = bf16[32,512]{1,0:T(8,128)(2,1)S(1)} collective-permute-done((bf16[32,512]{1,0:T(8,128)(2,1)S(1)}, bf16[32,512]{1,0:T(8,128)(2,1)S(1)}, u32[]{:S(2)}, u32[]{:S(2)}) %collective-permute-start.30) | collective-permute-done | bytes 32800 | tf_op jit(solution)/shard_map/ppermute | solution.py:529
  124.9 2.6 %collective-permute-start.33 = (bf16[32,512]{1,0:T(8,128)(2,1)S(1)}, bf16[32,512]{1,0:T(8,128)(2,1)S(1)}, u32[]{:S(2)}, u32[]{:S(2)}) collective-permute-start(bf16[32,512]{1,0:T(8,128)(2,1)S(1)} %shard_map.128.refs_0_), channel_id=1, source_target_pairs={{0,6},{1,7},{2,4},{3,5},{4,2},{5,3},{6,0},{7,1},{8,14},{9,15},{10,... | collective-permute-start | bytes 98312 | tf_op jit(solution)/shard_map/ppermute | solution.py:529
  127.5 1.8 %collective-permute-start.31 = (bf16[32,512]{1,0:T(8,128)(2,1)S(1)}, bf16[32,512]{1,0:T(8,128)(2,1)S(1)}, u32[]{:S(2)}, u32[]{:S(2)}) collective-permute-start(bf16[32,512]{1,0:T(8,128)(2,1)S(1)} %shard_map.128.refs_0_), channel_id=1, source_target_pairs={{0,2},{1,3},{2,0},{3,1},{4,6},{5,7},{6,4},{7,5},{8,10},{9,11},{10,... | collective-permute-start | bytes 98312 | tf_op jit(solution)/shard_map/ppermute | solution.py:529
  129.3 1.3 collective-permute-done.33.refs_3_
  130.6 1.6 %collective-permute-done.32.refs_2_ = bf16[32,512]{1,0:T(8,128)(2,1)S(1)} collective-permute-done((bf16[32,512]{1,0:T(8,128)(2,1)S(1)}, bf16[32,512]{1,0:T(8,128)(2,1)S(1)}, u32[]{:S(2)}, u32[]{:S(2)}) %collective-permute-start.32) | collective-permute-done | bytes 32800 | tf_op jit(solution)/shard_map/ppermute | solution.py:529
  132.4 2.9 %collective-permute-start.37 = (bf16[2,256,512]{2,1,0:T(8,128)(2,1)S(1)}, bf16[2,256,512]{2,1,0:T(8,128)(2,1)S(1)}, u32[]{:S(2)}, u32[]{:S(2)}) collective-permute-start(bf16[2,256,512]{2,1,0:T(8,128)(2,1)S(1)} %shard_map.130.refs_0_), channel_id=1, source_target_pairs={{0,2},{1,3},{6,4},{7,5},{8,10},{9,11},{14,12},{15,13},{16,18},{17,... | collective-permute-start | bytes 1572872 | tf_op jit(solution)/shard_map/ppermute | solution.py:529
  135.4 0.7 collective-permute-start.35
  136.1 1.8 %collective-permute-start.40 = (bf16[128,512]{1,0:T(8,128)(2,1)S(1)}, bf16[128,512]{1,0:T(8,128)(2,1)S(1)}, u32[]{:S(2)}, u32[]{:S(2)}) collective-permute-start(bf16[128,512]{1,0:T(8,128)(2,1)S(1)} %shard_map.129.refs_1_.refs_0_), channel_id=1, source_target_pairs={{0,24},{8,16},{16,8},{24,0},{1,25},{9,17},{17,9},{25,1},{2,26},{10... | collective-permute-start | bytes 393224 | tf_op jit(solution)/shard_map/ppermute | solution.py:540
  138.3 1.3 collective-permute-start.38
  139.6 2.4 %collective-permute-done.40.refs_3_ = bf16[128,512]{1,0:T(8,128)(2,1)S(1)} collective-permute-done((bf16[128,512]{1,0:T(8,128)(2,1)S(1)}, bf16[128,512]{1,0:T(8,128)(2,1)S(1)}, u32[]{:S(2)}, u32[]{:S(2)}) %collective-permute-start.40) | collective-permute-done | bytes 131104 | tf_op jit(solution)/shard_map/ppermute | solution.py:540
  142.1 1.3 collective-permute-done.39.refs_2_
  143.7 0.7 collective-permute-start.41
  144.5 4.7 %collective-permute-start.36 = (bf16[2,256,512]{2,1,0:T(8,128)(2,1)S(1)}, bf16[2,256,512]{2,1,0:T(8,128)(2,1)S(1)}, u32[]{:S(2)}, u32[]{:S(2)}) collective-permute-start(bf16[2,256,512]{2,1,0:T(8,128)(2,1)S(1)} %shard_map.132), channel_id=1, source_target_pairs={{0,2},{1,3},{2,0},{3,1},{4,6},{5,7},{6,4},{7,5},{8,10},{9,11},{10,... | collective-permute-start | bytes 1572872 | tf_op jit(solution)/shard_map/ppermute | solution.py:529
  149.2 1.5 shard_map.135
  150.7 10.0 %collective-permute-done.36.refs_1_ = bf16[2,256,512]{2,1,0:T(8,128)(2,1)S(1)} collective-permute-done((bf16[2,256,512]{2,1,0:T(8,128)(2,1)S(1)}, bf16[2,256,512]{2,1,0:T(8,128)(2,1)S(1)}, u32[]{:S(2)}, u32[]{:S(2)}) %collective-permute-start.36) | collective-permute-done | bytes 524320 | tf_op jit(solution)/shard_map/ppermute | solution.py:529
  160.7 1.2 copy-done.2
  161.9 1.3 shard_map.136
  (74 shorter events, 5.4 us)
Async XLA Ops:
  1.3 1.0 copy-start.3
  2.4 8.1 %copy-start.1 = (bf16[4,1,512,512]{3,2,1,0:T(8,128)(2,1)S(1)}, bf16[4,1,512,512]{3,2,1,0:T(8,128)(2,1)}, u32[]{:S(2)}) copy-start(bf16[4,1,512,512]{3,2,1,0:T(8,128)(2,1)} %param.8) | copy-start | bytes 6291460
  2.4 8.1 %copy-start.5 = (s32[1,1,48]{2,1,0:T(1,128)S(1)}, s32[1,1,48]{2,1,0:T(1,128)}, u32[]{:S(2)}) copy-start(s32[1,1,48]{2,1,0:T(1,128)} %param.11) | copy-start | bytes 580
  2.4 10.6 %slice-start = ((s8[6291456]{0:T(1024)(128)(4,1)}), s8[4194304]{0:T(1024)(128)(4,1)S(1)}, s32[]{:S(2)}) async-start(s8[6291456]{0:T(1024)(128)(4,1)} %bitcast.8), calls=%async_computation | async-start | bytes 8388608
  2.9 19.9 %collective-permute-start.7 = (bf16[2,512,256]{2,1,0:T(8,128)(2,1)S(1)}, bf16[2,512,256]{2,1,0:T(8,128)(2,1)S(1)}, u32[]{:S(2)}, u32[]{:S(2)}) collective-permute-start(bf16[2,512,256]{2,1,0:T(8,128)(2,1)S(1)} %get-tuple-element.60.refs_3_), channel_id=1, source_target_pairs={{2,4},{3,5},{4,2},{5,3},{10,12},{11,13},{12,10},{13,11},{18,20},{1... | collective-permute-start | bytes 1572872 | tf_op jit(solution)/shard_map/ppermute | solution.py:529
  3.8 19.1 %collective-permute-start.6 = (bf16[2,512,256]{2,1,0:T(8,128)(2,1)S(1)}, bf16[2,512,256]{2,1,0:T(8,128)(2,1)S(1)}, u32[]{:S(2)}, u32[]{:S(2)}) collective-permute-start(bf16[2,512,256]{2,1,0:T(8,128)(2,1)S(1)} %get-tuple-element.60.refs_3_), channel_id=1, source_target_pairs={{0,2},{1,3},{2,0},{3,1},{4,6},{5,7},{6,4},{7,5},{8,10},{9,11},{10,... | collective-permute-start | bytes 1572872 | tf_op jit(solution)/shard_map/ppermute | solution.py:529
  10.4 2.5 %slice-start.1 = ((s8[6291456]{0:T(1024)(128)(4,1)}), s8[2097152]{0:T(1024)(128)(4,1)S(1)}, s32[]{:S(2)}) async-start(s8[6291456]{0:T(1024)(128)(4,1)} %bitcast.8), calls=%async_computation.1 | async-start | bytes 4194304
  16.4 4.2 %collective-permute-start = (bf16[8,256,512]{2,1,0:T(8,128)(2,1)S(1)}, bf16[8,256,512]{2,1,0:T(8,128)(2,1)S(1)}, u32[]{:S(2)}, u32[]{:S(2)}) collective-permute-start(bf16[8,256,512]{2,1,0:T(8,128)(2,1)S(1)} %shard_map.106.refs_2_), channel_id=1, source_target_pairs={{0,1},{1,0},{2,3},{3,2},{4,5},{5,4},{6,7},{7,6},{8,9},{9,8},{10,11... | collective-permute-start | bytes 6291464 | tf_op jit(solution)/shard_map/ppermute | solution.py:537
  21.1 13.9 %collective-permute-start.1 = (bf16[2,256,512]{2,1,0:T(8,128)(2,1)S(1)}, bf16[2,256,512]{2,1,0:T(8,128)(2,1)S(1)}, u32[]{:S(2)}, u32[]{:S(2)}) collective-permute-start(bf16[2,256,512]{2,1,0:T(8,128)(2,1)S(1)} %get-tuple-element.57.refs_0_), channel_id=1, source_target_pairs={{0,2},{1,3},{6,4},{7,5},{8,10},{9,11},{14,12},{15,13},{16,18},{17,... | collective-permute-start | bytes 1572872 | tf_op jit(solution)/shard_map/ppermute | solution.py:529
  22.9 12.9 %collective-permute-start.8 = (bf16[2,512,256]{2,1,0:T(8,128)(2,1)S(1)}, bf16[2,512,256]{2,1,0:T(8,128)(2,1)S(1)}, u32[]{:S(2)}, u32[]{:S(2)}) collective-permute-start(bf16[2,512,256]{2,1,0:T(8,128)(2,1)S(1)} %get-tuple-element.61.refs_4_), channel_id=1, source_target_pairs={{2,4},{3,5},{4,2},{5,3},{10,12},{11,13},{12,10},{13,11},{18,20},{1... | collective-permute-start | bytes 1572872 | tf_op jit(solution)/shard_map/ppermute | solution.py:529
  23.6 22.2 %collective-permute-start.4 = (bf16[2,256,512]{2,1,0:T(8,128)(2,1)S(1)}, bf16[2,256,512]{2,1,0:T(8,128)(2,1)S(1)}, u32[]{:S(2)}, u32[]{:S(2)}) collective-permute-start(bf16[2,256,512]{2,1,0:T(8,128)(2,1)S(1)} %get-tuple-element.56.refs_0_), channel_id=1, source_target_pairs={{0,2},{1,3},{6,4},{7,5},{8,10},{9,11},{14,12},{15,13},{16,18},{17,... | collective-permute-start | bytes 1572872 | tf_op jit(solution)/shard_map/ppermute | solution.py:529
  27.6 18.6 %collective-permute-start.9 = (bf16[2,512,256]{2,1,0:T(8,128)(2,1)S(1)}, bf16[2,512,256]{2,1,0:T(8,128)(2,1)S(1)}, u32[]{:S(2)}, u32[]{:S(2)}) collective-permute-start(bf16[2,512,256]{2,1,0:T(8,128)(2,1)S(1)} %get-tuple-element.62.refs_1_), channel_id=1, source_target_pairs={{2,0},{3,1},{4,6},{5,7},{10,8},{11,9},{12,14},{13,15},{18,16},{19,... | collective-permute-start | bytes 1572872 | tf_op jit(solution)/shard_map/ppermute | solution.py:529
  35.1 10.8 %collective-permute-start.2 = (bf16[2,256,512]{2,1,0:T(8,128)(2,1)S(1)}, bf16[2,256,512]{2,1,0:T(8,128)(2,1)S(1)}, u32[]{:S(2)}, u32[]{:S(2)}) collective-permute-start(bf16[2,256,512]{2,1,0:T(8,128)(2,1)S(1)} %shard_map.108.refs_2_), channel_id=1, source_target_pairs={{2,4},{3,5},{4,2},{5,3},{10,12},{11,13},{12,10},{13,11},{18,20},{1... | collective-permute-start | bytes 1572872 | tf_op jit(solution)/shard_map/ppermute | solution.py:529
  35.9 18.0 %collective-permute-start.10 = (bf16[2,512,256]{2,1,0:T(8,128)(2,1)S(1)}, bf16[2,512,256]{2,1,0:T(8,128)(2,1)S(1)}, u32[]{:S(2)}, u32[]{:S(2)}) collective-permute-start(bf16[2,512,256]{2,1,0:T(8,128)(2,1)S(1)} %shard_map.112.refs_0_), channel_id=1, source_target_pairs={{2,0},{3,1},{4,6},{5,7},{10,8},{11,9},{12,14},{13,15},{18,16},{19,... | collective-permute-start | bytes 1572872 | tf_op jit(solution)/shard_map/ppermute | solution.py:529
  37.2 19.4 %collective-permute-start.11 = (bf16[2,512,256]{2,1,0:T(8,128)(2,1)S(1)}, bf16[2,512,256]{2,1,0:T(8,128)(2,1)S(1)}, u32[]{:S(2)}, u32[]{:S(2)}) collective-permute-start(bf16[2,512,256]{2,1,0:T(8,128)(2,1)S(1)} %get-tuple-element.60.refs_3_), channel_id=1, source_target_pairs={{0,1},{1,0},{2,3},{3,2},{4,5},{5,4},{6,7},{7,6},{8,9},{9,8},{10,11... | collective-permute-start | bytes 1572872 | tf_op jit(solution)/shard_map/ppermute | solution.py:537
  45.8 10.8 %collective-permute-start.12 = (bf16[2,512,256]{2,1,0:T(8,128)(2,1)S(1)}, bf16[2,512,256]{2,1,0:T(8,128)(2,1)S(1)}, u32[]{:S(2)}, u32[]{:S(2)}) collective-permute-start(bf16[2,512,256]{2,1,0:T(8,128)(2,1)S(1)} %get-tuple-element.61.refs_4_), channel_id=1, source_target_pairs={{0,1},{1,0},{2,3},{3,2},{4,5},{5,4},{6,7},{7,6},{8,9},{9,8},{10,11... | collective-permute-start | bytes 1572872 | tf_op jit(solution)/shard_map/ppermute | solution.py:537
  54.0 3.1 %collective-permute-start.13 = (bf16[1,512,256]{2,1,0:T(8,128)(2,1)S(1)}, bf16[1,512,256]{2,1,0:T(8,128)(2,1)S(1)}, u32[]{:S(2)}, u32[]{:S(2)}) collective-permute-start(bf16[1,512,256]{2,1,0:T(8,128)(2,1)S(1)} %get-tuple-element.63.refs_5_), channel_id=1, source_target_pairs={{0,1},{1,0},{2,3},{3,2},{4,5},{5,4},{6,7},{7,6},{8,9},{9,8},{10,11... | collective-permute-start | bytes 786440 | tf_op jit(solution)/shard_map/ppermute | solution.py:537
  54.1 10.9 %collective-permute-start.5 = (bf16[2,256,512]{2,1,0:T(8,128)(2,1)S(1)}, bf16[2,256,512]{2,1,0:T(8,128)(2,1)S(1)}, u32[]{:S(2)}, u32[]{:S(2)}) collective-permute-start(bf16[2,256,512]{2,1,0:T(8,128)(2,1)S(1)} %shard_map.110.refs_4_), channel_id=1, source_target_pairs={{2,4},{3,5},{4,2},{5,3},{10,12},{11,13},{12,10},{13,11},{18,20},{1... | collective-permute-start | bytes 1572872 | tf_op jit(solution)/shard_map/ppermute | solution.py:529
  55.0 14.4 %collective-permute-start.3 = (bf16[2,256,512]{2,1,0:T(8,128)(2,1)S(1)}, bf16[2,256,512]{2,1,0:T(8,128)(2,1)S(1)}, u32[]{:S(2)}, u32[]{:S(2)}) collective-permute-start(bf16[2,256,512]{2,1,0:T(8,128)(2,1)S(1)} %shard_map.109.refs_5_), channel_id=1, source_target_pairs={{0,2},{1,3},{2,0},{3,1},{4,6},{5,7},{6,4},{7,5},{8,10},{9,11},{10,... | collective-permute-start | bytes 1572872 | tf_op jit(solution)/shard_map/ppermute | solution.py:529
  56.6 1.5 collective-permute-start.14
  56.6 1.9 %collective-permute-start.15 = (bf16[1,512,256]{2,1,0:T(8,128)(2,1)S(1)}, bf16[1,512,256]{2,1,0:T(8,128)(2,1)S(1)}, u32[]{:S(2)}, u32[]{:S(2)}) collective-permute-start(bf16[1,512,256]{2,1,0:T(8,128)(2,1)S(1)} %get-tuple-element.65.refs_7_), channel_id=1, source_target_pairs={{0,1},{1,0},{2,3},{3,2},{4,5},{5,4},{6,7},{7,6},{8,9},{9,8},{10,11... | collective-permute-start | bytes 786440 | tf_op jit(solution)/shard_map/ppermute | solution.py:537
  57.1 1.8 %collective-permute-start.16 = (bf16[1,512,256]{2,1,0:T(8,128)(2,1)S(1)}, bf16[1,512,256]{2,1,0:T(8,128)(2,1)S(1)}, u32[]{:S(2)}, u32[]{:S(2)}) collective-permute-start(bf16[1,512,256]{2,1,0:T(8,128)(2,1)S(1)} %get-tuple-element.66.refs_8_), channel_id=1, source_target_pairs={{0,1},{1,0},{2,3},{3,2},{4,5},{5,4},{6,7},{7,6},{8,9},{9,8},{10,11... | collective-permute-start | bytes 786440 | tf_op jit(solution)/shard_map/ppermute | solution.py:537
  65.0 7.4 %copy-start = (bf16[512,512]{1,0:T(8,128)(2,1)S(1)}, bf16[512,512]{1,0:T(8,128)(2,1)}, u32[]{:S(2)}) copy-start(bf16[512,512]{1,0:T(8,128)(2,1)} %refs_4_.6) | copy-start | bytes 1572868
  69.6 5.5 %copy-start.4 = (bf16[512,512]{1,0:T(8,128)(2,1)S(1)}, bf16[512,512]{1,0:T(8,128)(2,1)}, u32[]{:S(2)}) copy-start(bf16[512,512]{1,0:T(8,128)(2,1)} %refs_4_.7) | copy-start | bytes 1572868
  69.6 9.3 %collective-permute-start.17 = (bf16[256,512]{1,0:T(8,128)(2,1)S(1)}, bf16[256,512]{1,0:T(8,128)(2,1)S(1)}, u32[]{:S(2)}, u32[]{:S(2)}) collective-permute-start(bf16[256,512]{1,0:T(8,128)(2,1)S(1)} %get-tuple-element.67.refs_0_), channel_id=1, source_target_pairs={{0,8},{8,0},{16,24},{24,16},{1,9},{9,1},{17,25},{25,17},{2,10},{10... | collective-permute-start | bytes 786440 | tf_op jit(solution)/shard_map/ppermute | solution.py:540
  70.8 10.8 %collective-permute-start.19 = (bf16[256,512]{1,0:T(8,128)(2,1)S(1)}, bf16[256,512]{1,0:T(8,128)(2,1)S(1)}, u32[]{:S(2)}, u32[]{:S(2)}) collective-permute-start(bf16[256,512]{1,0:T(8,128)(2,1)S(1)} %get-tuple-element.68.refs_1_), channel_id=1, source_target_pairs={{0,16},{8,24},{16,0},{24,8},{1,17},{9,25},{17,1},{25,9},{2,18},{10... | collective-permute-start | bytes 786440 | tf_op jit(solution)/shard_map/ppermute | solution.py:540
  73.1 11.4 %collective-permute-start.21 = (bf16[256,512]{1,0:T(8,128)(2,1)S(1)}, bf16[256,512]{1,0:T(8,128)(2,1)S(1)}, u32[]{:S(2)}, u32[]{:S(2)}) collective-permute-start(bf16[256,512]{1,0:T(8,128)(2,1)S(1)} %get-tuple-element.70), channel_id=1, source_target_pairs={{0,8},{8,0},{16,24},{24,16},{1,9},{9,1},{17,25},{25,17},{2,10},{10... | collective-permute-start | bytes 786440 | tf_op jit(solution)/shard_map/ppermute | solution.py:540
  75.1 10.5 %collective-permute-start.22 = (bf16[256,512]{1,0:T(8,128)(2,1)S(1)}, bf16[256,512]{1,0:T(8,128)(2,1)S(1)}, u32[]{:S(2)}, u32[]{:S(2)}) collective-permute-start(bf16[256,512]{1,0:T(8,128)(2,1)S(1)} %get-tuple-element.71), channel_id=1, source_target_pairs={{0,16},{8,24},{16,0},{24,8},{1,17},{9,25},{17,1},{25,9},{2,18},{10... | collective-permute-start | bytes 786440 | tf_op jit(solution)/shard_map/ppermute | solution.py:540
  78.9 12.2 %collective-permute-start.18 = (bf16[256,512]{1,0:T(8,128)(2,1)S(1)}, bf16[256,512]{1,0:T(8,128)(2,1)S(1)}, u32[]{:S(2)}, u32[]{:S(2)}) collective-permute-start(bf16[256,512]{1,0:T(8,128)(2,1)S(1)} %collective-permute-done.17.refs_0_), channel_id=1, source_target_pairs={{0,16},{8,24},{16,0},{24,8},{1,17},{9,25},{17,1},{25,9},{2,18},{10... | collective-permute-start | bytes 786440 | tf_op jit(solution)/shard_map/ppermute | solution.py:540
  81.6 9.5 %collective-permute-start.20 = (bf16[256,512]{1,0:T(8,128)(2,1)S(1)}, bf16[256,512]{1,0:T(8,128)(2,1)S(1)}, u32[]{:S(2)}, u32[]{:S(2)}) collective-permute-start(bf16[256,512]{1,0:T(8,128)(2,1)S(1)} %collective-permute-done.19.refs_3_), channel_id=1, source_target_pairs={{0,8},{8,0},{16,24},{24,16},{1,9},{9,1},{17,25},{25,17},{2,10},{10... | collective-permute-start | bytes 786440 | tf_op jit(solution)/shard_map/ppermute | solution.py:540
  94.4 11.3 %collective-permute-start.24 = (bf16[512,512]{1,0:T(8,128)(2,1)S(1)}, bf16[512,512]{1,0:T(8,128)(2,1)S(1)}, u32[]{:S(2)}, u32[]{:S(2)}) collective-permute-start(bf16[512,512]{1,0:T(8,128)(2,1)S(1)} %get-tuple-element.85), channel_id=1, source_target_pairs={{0,1},{1,0},{2,3},{3,2},{4,5},{5,4},{6,7},{7,6},{8,9},{9,8},{10,11... | collective-permute-start | bytes 1572872 | tf_op jit(solution)/shard_map/ppermute | solution.py:537
  98.0 4.6 %collective-permute-start.23 = (bf16[8,256,512]{2,1,0:T(8,128)(2,1)S(1)}, bf16[8,256,512]{2,1,0:T(8,128)(2,1)S(1)}, u32[]{:S(2)}, u32[]{:S(2)}) collective-permute-start(bf16[8,256,512]{2,1,0:T(8,128)(2,1)S(1)} %shard_map.124), channel_id=1, source_target_pairs={{0,1},{1,0},{2,3},{3,2},{4,5},{5,4},{6,7},{7,6},{8,9},{9,8},{10,11... | collective-permute-start | bytes 6291464 | tf_op jit(solution)/shard_map/ppermute | solution.py:537
  103.0 32.2 %collective-permute-start.34 = (bf16[2,256,512]{2,1,0:T(8,128)(2,1)S(1)}, bf16[2,256,512]{2,1,0:T(8,128)(2,1)S(1)}, u32[]{:S(2)}, u32[]{:S(2)}) collective-permute-start(bf16[2,256,512]{2,1,0:T(8,128)(2,1)S(1)} %get-tuple-element.94.refs_0_), channel_id=1, source_target_pairs={{0,2},{1,3},{6,4},{7,5},{8,10},{9,11},{14,12},{15,13},{16,18},{17,... | collective-permute-start | bytes 1572872 | tf_op jit(solution)/shard_map/ppermute | solution.py:529
  105.9 6.0 %collective-permute-start.25 = (bf16[128,512]{1,0:T(8,128)(2,1)S(1)}, bf16[128,512]{1,0:T(8,128)(2,1)S(1)}, u32[]{:S(2)}, u32[]{:S(2)}) collective-permute-start(bf16[128,512]{1,0:T(8,128)(2,1)S(1)} %get-tuple-element.87), channel_id=1, source_target_pairs={{0,8},{8,0},{16,24},{24,16},{1,9},{9,1},{17,25},{25,17},{2,10},{10... | collective-permute-start | bytes 393224 | tf_op jit(solution)/shard_map/ppermute | solution.py:540
  108.1 7.5 %collective-permute-start.26 = (bf16[128,512]{1,0:T(8,128)(2,1)S(1)}, bf16[128,512]{1,0:T(8,128)(2,1)S(1)}, u32[]{:S(2)}, u32[]{:S(2)}) collective-permute-start(bf16[128,512]{1,0:T(8,128)(2,1)S(1)} %get-tuple-element.88), channel_id=1, source_target_pairs={{0,16},{8,24},{16,0},{24,8},{1,17},{9,25},{17,1},{25,9},{2,18},{10... | collective-permute-start | bytes 393224 | tf_op jit(solution)/shard_map/ppermute | solution.py:540
  110.2 7.0 %collective-permute-start.27 = (bf16[128,512]{1,0:T(8,128)(2,1)S(1)}, bf16[128,512]{1,0:T(8,128)(2,1)S(1)}, u32[]{:S(2)}, u32[]{:S(2)}) collective-permute-start(bf16[128,512]{1,0:T(8,128)(2,1)S(1)} %get-tuple-element.89), channel_id=1, source_target_pairs={{0,24},{8,16},{16,8},{24,0},{1,25},{9,17},{17,9},{25,1},{2,26},{10... | collective-permute-start | bytes 393224 | tf_op jit(solution)/shard_map/ppermute | solution.py:540
  117.2 4.5 %collective-permute-start.28 = (bf16[32,512]{1,0:T(8,128)(2,1)S(1)}, bf16[32,512]{1,0:T(8,128)(2,1)S(1)}, u32[]{:S(2)}, u32[]{:S(2)}) collective-permute-start(bf16[32,512]{1,0:T(8,128)(2,1)S(1)} %get-tuple-element.91), channel_id=1, source_target_pairs={{0,2},{1,3},{2,0},{3,1},{4,6},{5,7},{6,4},{7,5},{8,10},{9,11},{10,... | collective-permute-start | bytes 98312 | tf_op jit(solution)/shard_map/ppermute | solution.py:529
  117.3 5.5 %collective-permute-start.29 = (bf16[32,512]{1,0:T(8,128)(2,1)S(1)}, bf16[32,512]{1,0:T(8,128)(2,1)S(1)}, u32[]{:S(2)}, u32[]{:S(2)}) collective-permute-start(bf16[32,512]{1,0:T(8,128)(2,1)S(1)} %get-tuple-element.92), channel_id=1, source_target_pairs={{0,4},{1,5},{2,6},{3,7},{4,0},{5,1},{6,2},{7,3},{8,12},{9,13},{10,... | collective-permute-start | bytes 98312 | tf_op jit(solution)/shard_map/ppermute | solution.py:529
  119.1 5.7 %collective-permute-start.30 = (bf16[32,512]{1,0:T(8,128)(2,1)S(1)}, bf16[32,512]{1,0:T(8,128)(2,1)S(1)}, u32[]{:S(2)}, u32[]{:S(2)}) collective-permute-start(bf16[32,512]{1,0:T(8,128)(2,1)S(1)} %get-tuple-element.93), channel_id=1, source_target_pairs={{0,6},{1,7},{2,4},{3,5},{4,2},{5,3},{6,0},{7,1},{8,14},{9,15},{10,... | collective-permute-start | bytes 98312 | tf_op jit(solution)/shard_map/ppermute | solution.py:529
  124.9 5.8 %collective-permute-start.33 = (bf16[32,512]{1,0:T(8,128)(2,1)S(1)}, bf16[32,512]{1,0:T(8,128)(2,1)S(1)}, u32[]{:S(2)}, u32[]{:S(2)}) collective-permute-start(bf16[32,512]{1,0:T(8,128)(2,1)S(1)} %shard_map.128.refs_0_), channel_id=1, source_target_pairs={{0,6},{1,7},{2,4},{3,5},{4,2},{5,3},{6,0},{7,1},{8,14},{9,15},{10,... | collective-permute-start | bytes 98312 | tf_op jit(solution)/shard_map/ppermute | solution.py:529
  127.5 4.8 %collective-permute-start.32 = (bf16[32,512]{1,0:T(8,128)(2,1)S(1)}, bf16[32,512]{1,0:T(8,128)(2,1)S(1)}, u32[]{:S(2)}, u32[]{:S(2)}) collective-permute-start(bf16[32,512]{1,0:T(8,128)(2,1)S(1)} %shard_map.128.refs_0_), channel_id=1, source_target_pairs={{0,4},{1,5},{2,6},{3,7},{4,0},{5,1},{6,2},{7,3},{8,12},{9,13},{10,... | collective-permute-start | bytes 98312 | tf_op jit(solution)/shard_map/ppermute | solution.py:529
  127.5 4.8 %collective-permute-start.31 = (bf16[32,512]{1,0:T(8,128)(2,1)S(1)}, bf16[32,512]{1,0:T(8,128)(2,1)S(1)}, u32[]{:S(2)}, u32[]{:S(2)}) collective-permute-start(bf16[32,512]{1,0:T(8,128)(2,1)S(1)} %shard_map.128.refs_0_), channel_id=1, source_target_pairs={{0,2},{1,3},{2,0},{3,1},{4,6},{5,7},{6,4},{7,5},{8,10},{9,11},{10,... | collective-permute-start | bytes 98312 | tf_op jit(solution)/shard_map/ppermute | solution.py:529
  132.4 11.2 %collective-permute-start.37 = (bf16[2,256,512]{2,1,0:T(8,128)(2,1)S(1)}, bf16[2,256,512]{2,1,0:T(8,128)(2,1)S(1)}, u32[]{:S(2)}, u32[]{:S(2)}) collective-permute-start(bf16[2,256,512]{2,1,0:T(8,128)(2,1)S(1)} %shard_map.130.refs_0_), channel_id=1, source_target_pairs={{0,2},{1,3},{6,4},{7,5},{8,10},{9,11},{14,12},{15,13},{16,18},{17,... | collective-permute-start | bytes 1572872 | tf_op jit(solution)/shard_map/ppermute | solution.py:529
  135.4 9.0 %collective-permute-start.35 = (bf16[2,256,512]{2,1,0:T(8,128)(2,1)S(1)}, bf16[2,256,512]{2,1,0:T(8,128)(2,1)S(1)}, u32[]{:S(2)}, u32[]{:S(2)}) collective-permute-start(bf16[2,256,512]{2,1,0:T(8,128)(2,1)S(1)} %shard_map.131.refs_2_), channel_id=1, source_target_pairs={{2,4},{3,5},{4,2},{5,3},{10,12},{11,13},{12,10},{13,11},{18,20},{1... | collective-permute-start | bytes 1572872 | tf_op jit(solution)/shard_map/ppermute | solution.py:529
  136.1 6.0 %collective-permute-start.40 = (bf16[128,512]{1,0:T(8,128)(2,1)S(1)}, bf16[128,512]{1,0:T(8,128)(2,1)S(1)}, u32[]{:S(2)}, u32[]{:S(2)}) collective-permute-start(bf16[128,512]{1,0:T(8,128)(2,1)S(1)} %shard_map.129.refs_1_.refs_0_), channel_id=1, source_target_pairs={{0,24},{8,16},{16,8},{24,0},{1,25},{9,17},{17,9},{25,1},{2,26},{10... | collective-permute-start | bytes 393224 | tf_op jit(solution)/shard_map/ppermute | solution.py:540
  137.9 5.5 %collective-permute-start.39 = (bf16[128,512]{1,0:T(8,128)(2,1)S(1)}, bf16[128,512]{1,0:T(8,128)(2,1)S(1)}, u32[]{:S(2)}, u32[]{:S(2)}) collective-permute-start(bf16[128,512]{1,0:T(8,128)(2,1)S(1)} %shard_map.129.refs_1_.refs_0_), channel_id=1, source_target_pairs={{0,16},{8,24},{16,0},{24,8},{1,17},{9,25},{17,1},{25,9},{2,18},{10... | collective-permute-start | bytes 393224 | tf_op jit(solution)/shard_map/ppermute | solution.py:540
  138.3 5.1 %collective-permute-start.38 = (bf16[128,512]{1,0:T(8,128)(2,1)S(1)}, bf16[128,512]{1,0:T(8,128)(2,1)S(1)}, u32[]{:S(2)}, u32[]{:S(2)}) collective-permute-start(bf16[128,512]{1,0:T(8,128)(2,1)S(1)} %shard_map.129.refs_1_.refs_0_), channel_id=1, source_target_pairs={{0,8},{8,0},{16,24},{24,16},{1,9},{9,1},{17,25},{25,17},{2,10},{10... | collective-permute-start | bytes 393224 | tf_op jit(solution)/shard_map/ppermute | solution.py:540
  143.5 5.8 %collective-permute-start.42 = (bf16[512,512]{1,0:T(8,128)(2,1)S(1)}, bf16[512,512]{1,0:T(8,128)(2,1)S(1)}, u32[]{:S(2)}, u32[]{:S(2)}) collective-permute-start(bf16[512,512]{1,0:T(8,128)(2,1)S(1)} %shard_map.133.refs_3_.refs_0_), channel_id=1, source_target_pairs={{0,1},{1,0},{2,3},{3,2},{4,5},{5,4},{6,7},{7,6},{8,9},{9,8},{10,11... | collective-permute-start | bytes 1572872 | tf_op jit(solution)/shard_map/ppermute | solution.py:537
  143.7 7.0 %collective-permute-start.41 = (bf16[2,256,512]{2,1,0:T(8,128)(2,1)S(1)}, bf16[2,256,512]{2,1,0:T(8,128)(2,1)S(1)}, u32[]{:S(2)}, u32[]{:S(2)}) collective-permute-start(bf16[2,256,512]{2,1,0:T(8,128)(2,1)S(1)} %shard_map.134), channel_id=1, source_target_pairs={{2,4},{3,5},{4,2},{5,3},{10,12},{11,13},{12,10},{13,11},{18,20},{1... | collective-permute-start | bytes 1572872 | tf_op jit(solution)/shard_map/ppermute | solution.py:529
  144.5 16.2 %collective-permute-start.36 = (bf16[2,256,512]{2,1,0:T(8,128)(2,1)S(1)}, bf16[2,256,512]{2,1,0:T(8,128)(2,1)S(1)}, u32[]{:S(2)}, u32[]{:S(2)}) collective-permute-start(bf16[2,256,512]{2,1,0:T(8,128)(2,1)S(1)} %shard_map.132), channel_id=1, source_target_pairs={{0,2},{1,3},{2,0},{3,1},{4,6},{5,7},{6,4},{7,5},{8,10},{9,11},{10,... | collective-permute-start | bytes 1572872 | tf_op jit(solution)/shard_map/ppermute | solution.py:529
  160.7 1.2 copy-start.2

commit v12 on v10

--- a/solution.py
+++ b/solution.py
@@ -118,6 +118,35 @@
     )
 
 
+def sum_large_group(g, number_ref, list_ref, total, product, store):
+    cap = list_ref.shape[0] // number_ref.shape[0]
+    n = number_ref[g]
+    rest = jnp.where(n == 0, 0, ((n - 1) & 3) + 1)
+
+    def take(start, width):
+        entries = [list_ref[g * cap + start + j] for j in range(width)]
+        return product([(lax.shift_right_logical(x, 10), x & 1023) for x in entries])
+
+    @pl.when(n == 0)
+    def _():
+        total[...] = jnp.zeros_like(total)
+
+    def exact(width):
+        @pl.when(rest == width)
+        def _():
+            total[...] = take(0, width)
+
+    for width in range(1, 5):
+        exact(width)
+
+    def four(m, _):
+        total[...] += take(rest + 4 * m, 4)
+        return 0
+
+    lax.fori_loop(0, lax.shift_right_logical(n - rest, 2), four, 0)
+    store(total[...])
+
+
 def sum_group(g, number_ref, list_ref, total, product, store):
     cap = list_ref.shape[0] // number_ref.shape[0]
     n = number_ref[g]
@@ -196,7 +225,7 @@
         [pltpu.VMEM((edge, width), F32)],
         mib=16,
         after=after,
-        cost=36 if parts == (0,) else 20,
+        cost=36,
     )[0]
 
 
@@ -219,7 +248,7 @@
         def store(value):
             out[i] = value.astype(BF16)
 
-        sum_group(i ^ mask, number_ref, list_ref, total, product, store)
+        sum_large_group(i ^ mask, number_ref, list_ref, total, product, store)
         return 0
 
     lax.fori_loop(0, out.shape[0], block, 0)
@@ -241,19 +270,19 @@
 
 
 def pair_sum_body(start, n, keep, come, *outs):
-    for j in range(n):
+    for j, out in enumerate(outs):
         for half in range(2):
-            i = half * n + j
-            outs[j][half] = (keep[i].astype(F32) + come[start + i].astype(F32)).astype(BF16)
+            i = (j // n * 2 + half) * n + j % n
+            out[half] = (keep[i].astype(F32) + come[start + i].astype(F32)).astype(BF16)
 
 
 def pair_sum(keep, come, start):
-    n = keep.shape[0] // 2
+    n = come.shape[0] // 4
     return run(
         functools.partial(pair_sum_body, start, n),
         (keep, come),
         [VMEM] * 2,
-        [shape((2, *keep.shape[1:]))] * n,
+        [shape((2, *keep.shape[1:]))] * (keep.shape[0] // 2),
         mib=12,
     )
 
@@ -343,10 +372,11 @@
 
 
 def second_body(*refs):
-    scale, weight, out = refs[-3:]
+    scale, weight, out, mark = refs[-4:]
     edge = refs[0].shape[1]
+    mark[...] = jnp.zeros_like(mark)
     for half in range(2):
-        summed = tree([x[half].astype(F32) for x in refs[:-3]])
+        summed = tree([x[half].astype(F32) for x in refs[:-4]])
         wide = repeat_lanes(scale[lax.axis_index("row") * 2 + half], summed.shape[1])
         agg = (summed * wide).astype(BF16)
         value = jnp.dot(agg, weight[...], preferred_element_type=F32)
@@ -359,8 +389,8 @@
         second_body,
         (*parts, scale, weight),
         [VMEM] * (2 + len(parts)),
-        [shape((halves * edge, width))],
-    )[0]
+        [shape((halves * edge, width)), shape((8, 128), F32)],
+    )
 
 
 def grad_body(start, last, hidden_ref, aggs, outs, scale, w_first, w_second, *refs):
@@ -537,8 +567,8 @@
         return [line_flip(own, 1), col_send(own, [(1, 2), (2, 1)])]
 
     def gather_far(own, near, middle, after, late):
-        (across,) = relay([col_send(near, [(1, 2), (2, 1)])], after)
         out_two = col_send(middle, [(1, 0), (2, 3)])
+        (across,) = relay([col_send(near, [(1, 2), (2, 1)])], (*after, out_two))
         out_three = col_send(across, [(1, 0), (2, 3)])
         return [own, near, *choose(line - 1, across, middle, out_two, out_three, late)]
 
@@ -550,22 +580,24 @@
         count, slots, values, scale, 2 * n_col
     )
 
-    def run_pass(source, first, after):
+    def run_pass(source, first, cuts, after):
         sums = {}
-        come = core_flip(forward(number, entries, tiles, source, first, 1, (1, 0), after))
-        for place, part in enumerate((1, 0)):
-            keep = forward(number, entries, tiles, source, first, 0, (part,), after)
-            sums[part] = pair_sum(keep, come, place * line)
-            after = sums[part][:1]
-        return sums[0], sums[1]
-
-    own_near, own_far = run_pass(first_in, True, ())
-    own = (*own_near, *own_far)
+        give = forward(number, entries, tiles, source, first, 1, (1, 0), after)
+        come = core_flip(give)
+        for cut in cuts:
+            keep = forward(number, entries, tiles, source, first, 0, cut, after)
+            pieces = pair_sum(keep, come, 0 if 1 in cut else line)
+            for place, part in enumerate(cut):
+                sums[part] = pieces[place * line // 2 : (place + 1) * line // 2]
+            after = pieces[:1]
+        return give, (*sums[0], *sums[1])
+
+    give, own = run_pass(first_in, True, ((1, 0),), ())
     if early:
-        early = relay(early, own_near[:1])
-    parts, late = scatter_line(own, relay(own[2:3], own_near[:1])[0])
+        early = relay(early, (give,))
+    parts, late = scatter_line(own, own[2])
     if early:
-        gathered = gather_far(scaled, *early, own_far[:1], late)
+        gathered = gather_far(scaled, *early, own[:1], late)
     else:
         gathered = [scaled] + [line_flip(scaled, j) for j in range(1, line)]
     ranged = gathered + [core_flip(g) for g in gathered]
@@ -580,9 +612,8 @@
         sums = weight_grads(start, hidden, *stacked, scale, w_first, w_second, sums)
 
     grad_give, grad_keep = sums
-    own_near, own_far = run_pass(stacked[1], False, (grad_keep,))
-    own = (*own_near, *own_far)
-    split = split_sum([grad_keep, core_flip(grad_give)], n_row, "row", own_near[:1])
+    _, own = run_pass(stacked[1], False, ((1,), (0,)), (grad_keep,))
+    split = split_sum([grad_keep, core_flip(grad_give)], n_row, "row", own[:1])
     moment = [split[0]] + [row_flip(split[j], j) for j in range(1, n_row)]
     if split[0].shape[0] % (16 * line) == 0:
         split = split_sum(moment, line, "line")
@@ -597,8 +628,8 @@
     parts, _ = scatter_line(own, behind, (moment,))
     moment = [moment] + [row_flip(moment, j) for j in range(1, n_row)]
     mine = join(moment, "row")
-    logits = second_layer(parts, scale, w_second)
-    return logits, *select(mine, core_flip(mine), (logits,))
+    logits, mark = second_layer(parts, scale, w_second)
+    return logits, *select(mine, core_flip(mine), (mark,))
 
 
 def solution(mesh):

time: 174 us -> 160 us (0.920)
  waiting for transfers between devices: 69.4 us -> 58.5 us
  Pallas kernels: 45.8 us -> 43.3 us
  starting transfers between devices: 52.9 us -> 55.4 us
  local copies, waits for them, and re-layouts: 3.83 us -> 1.77 us
    ppermute x21, waiting for transfers between devices: 49 us -> 39.1 us  [col_send(): lax.ppermute(value, 'col', [(2 * a + k, 2 * b + k) for a, b in pairs for...]
    ppermute x12, starting transfers between devices: 13.4 us -> 16.4 us  [row_flip(): return lax.ppermute(value, 'row', [(a, a ^ j) for a in range(n_row)])]
    pallas_call x39 -> x36, Pallas kernels: 45.8 us -> 43.3 us  [run(): pl.pallas_call(whole, out_shape=outs, in_specs=specs + [ANY] * extra, out...]
    unnamed x17 -> x15, local copies, waits for them, and re-layouts: 3.83 us -> 1.77 us
  transfers between devices with their start and end apart: 43 -> 43, of which waited for: 24 -> 22; matrix products, arithmetic and copies ran while one was open for 0% -> 0% of each run, Pallas kernels for 18% -> 23%
where the time goes in v12:
time: 160 us; the launch traced here: 161 us
  waiting for transfers between devices  58.5 us (37%)
  starting transfers between devices  55.4 us (35%)
  Pallas kernels  43.3 us (27%)
  between operations  1.84 us (1%)
  local copies, waits for them, and re-layouts  1.77 us (1%)
    pallas_call x36, Pallas kernels, run(): pl.pallas_call(whole, out_shape=outs, in_specs=specs + [ANY] * extra, out...  43.3 us
    ppermute x21, waiting for transfers between devices, col_send(): lax.ppermute(value, 'col', [(2 * a + k, 2 * b + k) for a, b in pairs for...  39.1 us
    ppermute x21, starting transfers between devices, col_send(): lax.ppermute(value, 'col', [(2 * a + k, 2 * b + k) for a, b in pairs for...  37.5 us
    ppermute x12, starting transfers between devices, row_flip(): return lax.ppermute(value, 'row', [(a, a ^ j) for a in range(n_row)])  16.4 us
    ppermute x12, waiting for transfers between devices, row_flip(): return lax.ppermute(value, 'row', [(a, a ^ j) for a in range(n_row)])  15.9 us
    ppermute x10, waiting for transfers between devices, core_flip(): return lax.ppermute(value, 'col', [(a, a ^ 1) for a in range(n_col)])  3.54 us
  transfers between devices with their start and end apart: 43, of which 22 were waited for; matrix products, arithmetic and copies ran while one was open for 0% of the time, Pallas kernels for 23%

profile of v12, /device:TPU:0, one launch (start us, length us, event | category | flops | bytes accessed | tf_op | source)
XLA Modules:
  0.0 160.8 jit_solution(12844942008472187521)
XLA Ops:
  0.6 0.7 copy.13
  1.3 1.0 copy-done.2
  2.9 0.8 collective-permute-start.7
  3.8 6.0 %collective-permute-start.6 = (bf16[2,512,256]{2,1,0:T(8,128)(2,1)S(1)}, bf16[2,512,256]{2,1,0:T(8,128)(2,1)S(1)}, u32[]{:S(2)}, u32[]{:S(2)}) collective-permute-start(bf16[2,512,256]{2,1,0:T(8,128)(2,1)S(1)} %get-tuple-element.62.refs_3_), channel_id=1, source_target_pairs={{0,2},{1,3},{2,0},{3,1},{4,6},{5,7},{6,4},{7,5},{8,10},{9,11},{10,... | collective-permute-start | bytes 1572872 | tf_op jit(solution)/shard_map/ppermute | solution.py:531
  10.5 2.6 %shard_map.104 = (bf16[8,256,512]{2,1,0:T(8,128)(2,1)S(1)}, s32[16]{0:T(128)S(1)}, s32[128]{0:T(128)S(1)}, s32[8]{0:T(128)S(1)}, s32[128]{0:T(128)S(1)}) custom-call(s32[1]{0:T(128)} %bitcast.7.refs_0_, s32[48]{0:T(128)S(1)} %bitcast.18, bf16[8,256,512]{2,1,0:T(8,128)(2,1)S(1)} %bitcast.17, f32[8,256,128]{2,1,0:T(8,128)S(1)} %get-tuple-element.52.refs_3_.refs_2_.refs_4_), custom_call_target="tpu_custom_call" | custom-call | flops 35999997952 | tf_op jit(solution)/shard_map/pallas_call | solution.py:25
  13.1 3.7 %shard_map.106.refs_2_ = bf16[8,256,512]{2,1,0:T(8,128)(2,1)S(1)} custom-call(s32[16]{0:T(128)S(1)} %get-tuple-element.53.refs_0_, s32[128]{0:T(128)S(1)} %get-tuple-element.54.refs_1_, bf16[48,256,256]{2,1,0:T(8,128)(2,1)S(1)} %bitcast.10, bf16[8,256,512]{2,1,0:T(8,128)(2,1)S(1)} %get-tuple-element.55.refs_3_), custom_call_target="tpu_custom_call" | custom-call | flops 35999997952 | tf_op jit(solution)/shard_map/pallas_call | solution.py:25
  16.9 4.1 %shard_map.105.refs_0_ = bf16[8,256,512]{2,1,0:T(8,128)(2,1)S(1)} custom-call(s32[16]{0:T(128)S(1)} %get-tuple-element.53.refs_0_, s32[128]{0:T(128)S(1)} %get-tuple-element.54.refs_1_, bf16[48,256,256]{2,1,0:T(8,128)(2,1)S(1)} %bitcast.11, bf16[8,256,512]{2,1,0:T(8,128)(2,1)S(1)} %get-tuple-element.55.refs_3_), custom_call_target="tpu_custom_call" | custom-call | flops 35999997952 | tf_op jit(solution)/shard_map/pallas_call | solution.py:25
  21.5 1.6 %collective-permute-start.1 = (bf16[2,256,512]{2,1,0:T(8,128)(2,1)S(1)}, bf16[2,256,512]{2,1,0:T(8,128)(2,1)S(1)}, u32[]{:S(2)}, u32[]{:S(2)}) collective-permute-start(bf16[2,256,512]{2,1,0:T(8,128)(2,1)S(1)} %get-tuple-element.59.refs_0_), channel_id=1, source_target_pairs={{0,2},{1,3},{6,4},{7,5},{8,10},{9,11},{14,12},{15,13},{16,18},{17,... | collective-permute-start | bytes 1572872 | tf_op jit(solution)/shard_map/ppermute | solution.py:531
  23.3 1.3 collective-permute-start.9
  24.6 0.7 collective-permute-start.8
  25.3 5.9 %collective-permute-start.4 = (bf16[2,256,512]{2,1,0:T(8,128)(2,1)S(1)}, bf16[2,256,512]{2,1,0:T(8,128)(2,1)S(1)}, u32[]{:S(2)}, u32[]{:S(2)}) collective-permute-start(bf16[2,256,512]{2,1,0:T(8,128)(2,1)S(1)} %get-tuple-element.58.refs_0_), channel_id=1, source_target_pairs={{0,2},{1,3},{6,4},{7,5},{8,10},{9,11},{14,12},{15,13},{16,18},{17,... | collective-permute-start | bytes 1572872 | tf_op jit(solution)/shard_map/ppermute | solution.py:531
  31.2 4.2 %collective-permute-done.1.refs_1_ = bf16[2,256,512]{2,1,0:T(8,128)(2,1)S(1)} collective-permute-done((bf16[2,256,512]{2,1,0:T(8,128)(2,1)S(1)}, bf16[2,256,512]{2,1,0:T(8,128)(2,1)S(1)}, u32[]{:S(2)}, u32[]{:S(2)}) %collective-permute-start.1) | collective-permute-done | bytes 524320 | tf_op jit(solution)/shard_map/ppermute | solution.py:531
  35.5 0.7 collective-permute-start.2
  36.2 2.6 %collective-permute-done.9.refs_2_ = bf16[2,512,256]{2,1,0:T(8,128)(2,1)S(1)} collective-permute-done((bf16[2,512,256]{2,1,0:T(8,128)(2,1)S(1)}, bf16[2,512,256]{2,1,0:T(8,128)(2,1)S(1)}, u32[]{:S(2)}, u32[]{:S(2)}) %collective-permute-start.9) | collective-permute-done | bytes 524320 | tf_op jit(solution)/shard_map/ppermute | solution.py:531
  38.9 1.3 collective-permute-start.10
  40.8 5.1 %collective-permute-done.4.refs_1_ = bf16[2,256,512]{2,1,0:T(8,128)(2,1)S(1)} collective-permute-done((bf16[2,256,512]{2,1,0:T(8,128)(2,1)S(1)}, bf16[2,256,512]{2,1,0:T(8,128)(2,1)S(1)}, u32[]{:S(2)}, u32[]{:S(2)}) %collective-permute-start.4) | collective-permute-done | bytes 524320 | tf_op jit(solution)/shard_map/ppermute | solution.py:531
  46.1 8.5 %collective-permute-done.10.refs_3_ = bf16[2,512,256]{2,1,0:T(8,128)(2,1)S(1)} collective-permute-done((bf16[2,512,256]{2,1,0:T(8,128)(2,1)S(1)}, bf16[2,512,256]{2,1,0:T(8,128)(2,1)S(1)}, u32[]{:S(2)}, u32[]{:S(2)}) %collective-permute-start.10) | collective-permute-done | bytes 524320 | tf_op jit(solution)/shard_map/ppermute | solution.py:531
  54.8 0.9 collective-permute-start.5
  55.7 1.5 collective-permute-start.3
  57.8 0.9 collective-permute-done.14.refs_12_
  59.5 7.0 %shard_map.114.refs_4_.refs_0_ = bf16[8,512,256]{2,1,0:T(8,128)(2,1)S(1)} custom-call(s32[8]{0:T(128)S(1)} %get-tuple-element.60.refs_0_, s32[128]{0:T(128)S(1)} %get-tuple-element.61.refs_1_, bf16[48,256,256]{2,1,0:T(8,128)(2,1)S(1)} %bitcast.12, bf16[2,512,256]{2,1,0:T(8,128)(2,1)S(1)} %get-tuple-element.62.refs_3_, ...), custom_call_target="tpu_custom_call" | custom-call | tf_op jit(solution)/shard_map/pallas_call | solution.py:25
  66.4 3.6 %collective-permute-done.3.refs_1_ = bf16[2,256,512]{2,1,0:T(8,128)(2,1)S(1)} collective-permute-done((bf16[2,256,512]{2,1,0:T(8,128)(2,1)S(1)}, bf16[2,256,512]{2,1,0:T(8,128)(2,1)S(1)}, u32[]{:S(2)}, u32[]{:S(2)}) %collective-permute-start.3) | collective-permute-done | bytes 524320 | tf_op jit(solution)/shard_map/ppermute | solution.py:531
  70.3 2.5 %collective-permute-start.17 = (bf16[256,512]{1,0:T(8,128)(2,1)S(1)}, bf16[256,512]{1,0:T(8,128)(2,1)S(1)}, u32[]{:S(2)}, u32[]{:S(2)}) collective-permute-start(bf16[256,512]{1,0:T(8,128)(2,1)S(1)} %get-tuple-element.69.refs_0_), channel_id=1, source_target_pairs={{0,8},{8,0},{16,24},{24,16},{1,9},{9,1},{17,25},{25,17},{2,10},{10... | collective-permute-start | bytes 786440 | tf_op jit(solution)/shard_map/ppermute | solution.py:542
  72.8 2.3 %collective-permute-start.19 = (bf16[256,512]{1,0:T(8,128)(2,1)S(1)}, bf16[256,512]{1,0:T(8,128)(2,1)S(1)}, u32[]{:S(2)}, u32[]{:S(2)}) collective-permute-start(bf16[256,512]{1,0:T(8,128)(2,1)S(1)} %get-tuple-element.70.refs_1_), channel_id=1, source_target_pairs={{0,16},{8,24},{16,0},{24,8},{1,17},{9,25},{17,1},{25,9},{2,18},{10... | collective-permute-start | bytes 786440 | tf_op jit(solution)/shard_map/ppermute | solution.py:542
  75.1 0.6 shard_map.116
  75.9 2.2 %shard_map.118 = (f32[512,512]{1,0:T(8,128)S(1)}, f32[512,512]{1,0:T(8,128)S(1)}) custom-call(bf16[8,512,256]{2,1,0:T(8,128)(2,1)S(1)} %shard_map.114.refs_4_.refs_0_, bf16[2,256,512]{2,1,0:T(8,128)(2,1)S(1)} %get-tuple-element.71.refs_2_.refs_1_.refs_6_, bf16[2,256,512]{2,1,0:T(8,128)(2,1)S(1)} %get-tuple-element.74.refs_2_.refs_7_, ...), custom_call_target="tpu_custom_call" | custom-call | flops 35999997952 | tf_op jit(solution)/shard_map/pallas_call | solution.py:25
  78.2 1.8 %collective-permute-done.17.refs_0_ = bf16[256,512]{1,0:T(8,128)(2,1)S(1)} collective-permute-done((bf16[256,512]{1,0:T(8,128)(2,1)S(1)}, bf16[256,512]{1,0:T(8,128)(2,1)S(1)}, u32[]{:S(2)}, u32[]{:S(2)}) %collective-permute-start.17) | collective-permute-done | bytes 262176 | tf_op jit(solution)/shard_map/ppermute | solution.py:542
  80.0 2.3 %collective-permute-start.18 = (bf16[256,512]{1,0:T(8,128)(2,1)S(1)}, bf16[256,512]{1,0:T(8,128)(2,1)S(1)}, u32[]{:S(2)}, u32[]{:S(2)}) collective-permute-start(bf16[256,512]{1,0:T(8,128)(2,1)S(1)} %collective-permute-done.17.refs_0_), channel_id=1, source_target_pairs={{0,16},{8,24},{16,0},{24,8},{1,17},{9,25},{17,1},{25,9},{2,18},{10... | collective-permute-start | bytes 786440 | tf_op jit(solution)/shard_map/ppermute | solution.py:542
  82.3 2.0 %collective-permute-start.20 = (bf16[256,512]{1,0:T(8,128)(2,1)S(1)}, bf16[256,512]{1,0:T(8,128)(2,1)S(1)}, u32[]{:S(2)}, u32[]{:S(2)}) collective-permute-start(bf16[256,512]{1,0:T(8,128)(2,1)S(1)} %collective-permute-done.19.refs_3_), channel_id=1, source_target_pairs={{0,8},{8,0},{16,24},{24,16},{1,9},{9,1},{17,25},{25,17},{2,10},{10... | collective-permute-start | bytes 786440 | tf_op jit(solution)/shard_map/ppermute | solution.py:542
  84.3 1.3 collective-permute-done.21.refs_1_
  85.6 2.3 %collective-permute-done.22.refs_2_ = bf16[256,512]{1,0:T(8,128)(2,1)S(1)} collective-permute-done((bf16[256,512]{1,0:T(8,128)(2,1)S(1)}, bf16[256,512]{1,0:T(8,128)(2,1)S(1)}, u32[]{:S(2)}, u32[]{:S(2)}) %collective-permute-start.22) | collective-permute-done | bytes 262176 | tf_op jit(solution)/shard_map/ppermute | solution.py:542
  87.9 1.1 shard_map.119
  89.0 4.3 %shard_map.120 = (f32[512,512]{1,0:T(8,128)S(1)}, f32[512,512]{1,0:T(8,128)S(1)}) custom-call(bf16[8,512,256]{2,1,0:T(8,128)(2,1)S(1)} %shard_map.114.refs_4_.refs_0_, bf16[6,256,512]{2,1,0:T(8,128)(2,1)S(1)} %get-tuple-element.76.refs_1_.refs_4_, bf16[6,256,512]{2,1,0:T(8,128)(2,1)S(1)} %get-tuple-element.77.refs_2_.refs_5_, ...), custom_call_target="tpu_custom_call" | custom-call | flops 35999997952 | tf_op jit(solution)/shard_map/pallas_call | solution.py:25
  93.3 0.9 shard_map.121
  94.2 2.4 %shard_map.122 = (bf16[512,512]{1,0:T(8,128)(2,1)S(1)}, bf16[512,512]{1,0:T(8,128)(2,1)S(1)}) custom-call(bf16[8,512,256]{2,1,0:T(8,128)(2,1)S(1)} %shard_map.114.refs_4_.refs_0_, bf16[8,256,512]{2,1,0:T(8,128)(2,1)S(1)} %get-tuple-element.81.refs_1_, bf16[8,256,512]{2,1,0:T(8,128)(2,1)S(1)} %get-tuple-element.80.refs_2_.refs_3_, ...), custom_call_target="tpu_custom_call" | custom-call | flops 35999997952 | tf_op jit(solution)/shard_map/pallas_call | solution.py:25
  96.7 3.9 %shard_map.124 = bf16[8,256,512]{2,1,0:T(8,128)(2,1)S(1)} custom-call(s32[16]{0:T(128)S(1)} %get-tuple-element.53.refs_0_, s32[128]{0:T(128)S(1)} %get-tuple-element.54.refs_1_, bf16[48,256,256]{2,1,0:T(8,128)(2,1)S(1)} %bitcast.13, bf16[8,256,512]{2,1,0:T(8,128)(2,1)S(1)} %get-tuple-element.80.refs_2_.refs_3_, ...), custom_call_target="tpu_custom_call" | custom-call | flops 35999997952 | tf_op jit(solution)/shard_map/pallas_call | solution.py:25
  100.7 2.3 %shard_map.123.refs_0_ = bf16[4,256,512]{2,1,0:T(8,128)(2,1)S(1)} custom-call(s32[16]{0:T(128)S(1)} %get-tuple-element.53.refs_0_, s32[128]{0:T(128)S(1)} %get-tuple-element.54.refs_1_, bf16[48,256,256]{2,1,0:T(8,128)(2,1)S(1)} %bitcast.14, bf16[8,256,512]{2,1,0:T(8,128)(2,1)S(1)} %get-tuple-element.80.refs_2_.refs_3_, ...), custom_call_target="tpu_custom_call" | custom-call | flops 35999997952 | tf_op jit(solution)/shard_map/pallas_call | solution.py:25
  103.0 1.8 %collective-permute-done.23.refs_1_ = bf16[8,256,512]{2,1,0:T(8,128)(2,1)S(1)} collective-permute-done((bf16[8,256,512]{2,1,0:T(8,128)(2,1)S(1)}, bf16[8,256,512]{2,1,0:T(8,128)(2,1)S(1)}, u32[]{:S(2)}, u32[]{:S(2)}) %collective-permute-start.23) | collective-permute-done | bytes 2097184 | tf_op jit(solution)/shard_map/ppermute | solution.py:539
  105.1 3.0 %collective-permute-start.31 = (bf16[2,256,512]{2,1,0:T(8,128)(2,1)S(1)}, bf16[2,256,512]{2,1,0:T(8,128)(2,1)S(1)}, u32[]{:S(2)}, u32[]{:S(2)}) collective-permute-start(bf16[2,256,512]{2,1,0:T(8,128)(2,1)S(1)} %get-tuple-element.96.refs_0_), channel_id=1, source_target_pairs={{0,2},{1,3},{6,4},{7,5},{8,10},{9,11},{14,12},{15,13},{16,18},{17,... | collective-permute-start | bytes 1572872 | tf_op jit(solution)/shard_map/ppermute | solution.py:531
  108.1 2.4 %shard_map.126.refs_0_ = bf16[4,256,512]{2,1,0:T(8,128)(2,1)S(1)} custom-call(s32[16]{0:T(128)S(1)} %get-tuple-element.53.refs_0_, s32[128]{0:T(128)S(1)} %get-tuple-element.54.refs_1_, bf16[48,256,256]{2,1,0:T(8,128)(2,1)S(1)} %bitcast.15, bf16[8,256,512]{2,1,0:T(8,128)(2,1)S(1)} %get-tuple-element.80.refs_2_.refs_3_, ...), custom_call_target="tpu_custom_call" | custom-call | flops 35999997952 | tf_op jit(solution)/shard_map/pallas_call | solution.py:25
  111.4 2.2 %collective-permute-start.26 = (bf16[128,512]{1,0:T(8,128)(2,1)S(1)}, bf16[128,512]{1,0:T(8,128)(2,1)S(1)}, u32[]{:S(2)}, u32[]{:S(2)}) collective-permute-start(bf16[128,512]{1,0:T(8,128)(2,1)S(1)} %get-tuple-element.90), channel_id=1, source_target_pairs={{0,16},{8,24},{16,0},{24,8},{1,17},{9,25},{17,1},{25,9},{2,18},{10... | collective-permute-start | bytes 393224 | tf_op jit(solution)/shard_map/ppermute | solution.py:542
  113.6 1.1 collective-permute-start.27
  114.6 1.4 collective-permute-done.25.refs_1_
  116.0 3.4 %collective-permute-done.26.refs_2_ = bf16[128,512]{1,0:T(8,128)(2,1)S(1)} collective-permute-done((bf16[128,512]{1,0:T(8,128)(2,1)S(1)}, bf16[128,512]{1,0:T(8,128)(2,1)S(1)}, u32[]{:S(2)}, u32[]{:S(2)}) %collective-permute-start.26) | collective-permute-done | bytes 131104 | tf_op jit(solution)/shard_map/ppermute | solution.py:542
  119.4 1.9 %collective-permute-done.27.refs_3_ = bf16[128,512]{1,0:T(8,128)(2,1)S(1)} collective-permute-done((bf16[128,512]{1,0:T(8,128)(2,1)S(1)}, bf16[128,512]{1,0:T(8,128)(2,1)S(1)}, u32[]{:S(2)}, u32[]{:S(2)}) %collective-permute-start.27) | collective-permute-done | bytes 131104 | tf_op jit(solution)/shard_map/ppermute | solution.py:542
  121.4 2.4 %collective-permute-start.29 = (bf16[32,512]{1,0:T(8,128)(2,1)S(1)}, bf16[32,512]{1,0:T(8,128)(2,1)S(1)}, u32[]{:S(2)}, u32[]{:S(2)}) collective-permute-start(bf16[32,512]{1,0:T(8,128)(2,1)S(1)} %get-tuple-element.94), channel_id=1, source_target_pairs={{0,4},{1,5},{2,6},{3,7},{4,0},{5,1},{6,2},{7,3},{8,12},{9,13},{10,... | collective-permute-start | bytes 98312 | tf_op jit(solution)/shard_map/ppermute | solution.py:531
  123.8 2.0 %collective-permute-start.30 = (bf16[32,512]{1,0:T(8,128)(2,1)S(1)}, bf16[32,512]{1,0:T(8,128)(2,1)S(1)}, u32[]{:S(2)}, u32[]{:S(2)}) collective-permute-start(bf16[32,512]{1,0:T(8,128)(2,1)S(1)} %get-tuple-element.95), channel_id=1, source_target_pairs={{0,6},{1,7},{2,4},{3,5},{4,2},{5,3},{6,0},{7,1},{8,14},{9,15},{10,... | collective-permute-start | bytes 98312 | tf_op jit(solution)/shard_map/ppermute | solution.py:531
  125.8 1.0 collective-permute-done.29.refs_2_
  126.8 2.7 %collective-permute-done.30.refs_3_ = bf16[32,512]{1,0:T(8,128)(2,1)S(1)} collective-permute-done((bf16[32,512]{1,0:T(8,128)(2,1)S(1)}, bf16[32,512]{1,0:T(8,128)(2,1)S(1)}, u32[]{:S(2)}, u32[]{:S(2)}) %collective-permute-start.30) | collective-permute-done | bytes 32800 | tf_op jit(solution)/shard_map/ppermute | solution.py:531
  129.5 1.3 collective-permute-start.34
  131.0 0.7 collective-permute-start.32
  131.7 2.1 %collective-permute-start.37 = (bf16[32,512]{1,0:T(8,128)(2,1)S(1)}, bf16[32,512]{1,0:T(8,128)(2,1)S(1)}, u32[]{:S(2)}, u32[]{:S(2)}) collective-permute-start(bf16[32,512]{1,0:T(8,128)(2,1)S(1)} %shard_map.130.refs_1_.refs_0_), channel_id=1, source_target_pairs={{0,6},{1,7},{2,4},{3,5},{4,2},{5,3},{6,0},{7,1},{8,14},{9,15},{10,... | collective-permute-start | bytes 98312 | tf_op jit(solution)/shard_map/ppermute | solution.py:531
  134.4 1.8 %collective-permute-start.35 = (bf16[32,512]{1,0:T(8,128)(2,1)S(1)}, bf16[32,512]{1,0:T(8,128)(2,1)S(1)}, u32[]{:S(2)}, u32[]{:S(2)}) collective-permute-start(bf16[32,512]{1,0:T(8,128)(2,1)S(1)} %shard_map.130.refs_1_.refs_0_), channel_id=1, source_target_pairs={{0,2},{1,3},{2,0},{3,1},{4,6},{5,7},{6,4},{7,5},{8,10},{9,11},{10,... | collective-permute-start | bytes 98312 | tf_op jit(solution)/shard_map/ppermute | solution.py:531
  136.2 8.5 %collective-permute-done.37.refs_3_ = bf16[32,512]{1,0:T(8,128)(2,1)S(1)} collective-permute-done((bf16[32,512]{1,0:T(8,128)(2,1)S(1)}, bf16[32,512]{1,0:T(8,128)(2,1)S(1)}, u32[]{:S(2)}, u32[]{:S(2)}) %collective-permute-start.37) | collective-permute-done | bytes 32800 | tf_op jit(solution)/shard_map/ppermute | solution.py:531
  144.7 1.3 collective-permute-done.36.refs_2_
  146.1 0.7 collective-permute-start.38
  146.9 2.2 %collective-permute-start.33 = (bf16[2,256,512]{2,1,0:T(8,128)(2,1)S(1)}, bf16[2,256,512]{2,1,0:T(8,128)(2,1)S(1)}, u32[]{:S(2)}, u32[]{:S(2)}) collective-permute-start(bf16[2,256,512]{2,1,0:T(8,128)(2,1)S(1)} %shard_map.133), channel_id=1, source_target_pairs={{0,2},{1,3},{2,0},{3,1},{4,6},{5,7},{6,4},{7,5},{8,10},{9,11},{10,... | collective-permute-start | bytes 1572872 | tf_op jit(solution)/shard_map/ppermute | solution.py:531
  149.1 1.7 %collective-permute-start.41 = (bf16[128,512]{1,0:T(8,128)(2,1)S(1)}, bf16[128,512]{1,0:T(8,128)(2,1)S(1)}, u32[]{:S(2)}, u32[]{:S(2)}) collective-permute-start(bf16[128,512]{1,0:T(8,128)(2,1)S(1)} %shard_map.134.refs_3_.refs_0_), channel_id=1, source_target_pairs={{0,24},{8,16},{16,8},{24,0},{1,25},{9,17},{17,9},{25,1},{2,26},{10... | collective-permute-start | bytes 393224 | tf_op jit(solution)/shard_map/ppermute | solution.py:542
  150.9 1.7 %collective-permute-start.39 = (bf16[128,512]{1,0:T(8,128)(2,1)S(1)}, bf16[128,512]{1,0:T(8,128)(2,1)S(1)}, u32[]{:S(2)}, u32[]{:S(2)}) collective-permute-start(bf16[128,512]{1,0:T(8,128)(2,1)S(1)} %shard_map.134.refs_3_.refs_0_), channel_id=1, source_target_pairs={{0,8},{8,0},{16,24},{24,16},{1,9},{9,1},{17,25},{25,17},{2,10},{10... | collective-permute-start | bytes 393224 | tf_op jit(solution)/shard_map/ppermute | solution.py:542
  152.6 2.4 %collective-permute-done.41.refs_3_ = bf16[128,512]{1,0:T(8,128)(2,1)S(1)} collective-permute-done((bf16[128,512]{1,0:T(8,128)(2,1)S(1)}, bf16[128,512]{1,0:T(8,128)(2,1)S(1)}, u32[]{:S(2)}, u32[]{:S(2)}) %collective-permute-start.41) | collective-permute-done | bytes 131104 | tf_op jit(solution)/shard_map/ppermute | solution.py:542
  155.0 1.3 collective-permute-done.40.refs_2_
  156.5 1.6 collective-permute-done.33.refs_1_
  158.1 1.3 shard_map.136
  159.3 1.5 shard_map.138
  (74 shorter events, 6.7 us)
Async XLA Ops:
  1.3 1.0 copy-start.2
  2.4 8.1 %copy-start.1 = (bf16[4,1,512,512]{3,2,1,0:T(8,128)(2,1)S(1)}, bf16[4,1,512,512]{3,2,1,0:T(8,128)(2,1)}, u32[]{:S(2)}) copy-start(bf16[4,1,512,512]{3,2,1,0:T(8,128)(2,1)} %param.8) | copy-start | bytes 6291460
  2.4 8.1 %copy-start.4 = (s32[1,1,48]{2,1,0:T(1,128)S(1)}, s32[1,1,48]{2,1,0:T(1,128)}, u32[]{:S(2)}) copy-start(s32[1,1,48]{2,1,0:T(1,128)} %param.11) | copy-start | bytes 580
  2.4 10.7 %slice-start = ((s8[6291456]{0:T(1024)(128)(4,1)}), s8[4194304]{0:T(1024)(128)(4,1)S(1)}, s32[]{:S(2)}) async-start(s8[6291456]{0:T(1024)(128)(4,1)} %bitcast.8), calls=%async_computation | async-start | bytes 8388608
  2.9 20.2 %collective-permute-start.7 = (bf16[2,512,256]{2,1,0:T(8,128)(2,1)S(1)}, bf16[2,512,256]{2,1,0:T(8,128)(2,1)S(1)}, u32[]{:S(2)}, u32[]{:S(2)}) collective-permute-start(bf16[2,512,256]{2,1,0:T(8,128)(2,1)S(1)} %get-tuple-element.62.refs_3_), channel_id=1, source_target_pairs={{2,4},{3,5},{4,2},{5,3},{10,12},{11,13},{12,10},{13,11},{18,20},{1... | collective-permute-start | bytes 1572872 | tf_op jit(solution)/shard_map/ppermute | solution.py:531
  3.8 19.4 %collective-permute-start.6 = (bf16[2,512,256]{2,1,0:T(8,128)(2,1)S(1)}, bf16[2,512,256]{2,1,0:T(8,128)(2,1)S(1)}, u32[]{:S(2)}, u32[]{:S(2)}) collective-permute-start(bf16[2,512,256]{2,1,0:T(8,128)(2,1)S(1)} %get-tuple-element.62.refs_3_), channel_id=1, source_target_pairs={{0,2},{1,3},{2,0},{3,1},{4,6},{5,7},{6,4},{7,5},{8,10},{9,11},{10,... | collective-permute-start | bytes 1572872 | tf_op jit(solution)/shard_map/ppermute | solution.py:531
  10.4 2.6 %slice-start.1 = ((s8[6291456]{0:T(1024)(128)(4,1)}), s8[2097152]{0:T(1024)(128)(4,1)S(1)}, s32[]{:S(2)}) async-start(s8[6291456]{0:T(1024)(128)(4,1)} %bitcast.8), calls=%async_computation.1 | async-start | bytes 4194304
  16.8 4.2 %collective-permute-start = (bf16[8,256,512]{2,1,0:T(8,128)(2,1)S(1)}, bf16[8,256,512]{2,1,0:T(8,128)(2,1)S(1)}, u32[]{:S(2)}, u32[]{:S(2)}) collective-permute-start(bf16[8,256,512]{2,1,0:T(8,128)(2,1)S(1)} %shard_map.106.refs_2_), channel_id=1, source_target_pairs={{0,1},{1,0},{2,3},{3,2},{4,5},{5,4},{6,7},{7,6},{8,9},{9,8},{10,11... | collective-permute-start | bytes 6291464 | tf_op jit(solution)/shard_map/ppermute | solution.py:539
  21.5 13.9 %collective-permute-start.1 = (bf16[2,256,512]{2,1,0:T(8,128)(2,1)S(1)}, bf16[2,256,512]{2,1,0:T(8,128)(2,1)S(1)}, u32[]{:S(2)}, u32[]{:S(2)}) collective-permute-start(bf16[2,256,512]{2,1,0:T(8,128)(2,1)S(1)} %get-tuple-element.59.refs_0_), channel_id=1, source_target_pairs={{0,2},{1,3},{6,4},{7,5},{8,10},{9,11},{14,12},{15,13},{16,18},{17,... | collective-permute-start | bytes 1572872 | tf_op jit(solution)/shard_map/ppermute | solution.py:531
  23.3 15.6 %collective-permute-start.9 = (bf16[2,512,256]{2,1,0:T(8,128)(2,1)S(1)}, bf16[2,512,256]{2,1,0:T(8,128)(2,1)S(1)}, u32[]{:S(2)}, u32[]{:S(2)}) collective-permute-start(bf16[2,512,256]{2,1,0:T(8,128)(2,1)S(1)} %get-tuple-element.64.refs_1_), channel_id=1, source_target_pairs={{2,0},{3,1},{4,6},{5,7},{10,8},{11,9},{12,14},{13,15},{18,16},{19,... | collective-permute-start | bytes 1572872 | tf_op jit(solution)/shard_map/ppermute | solution.py:531
  24.6 14.3 %collective-permute-start.8 = (bf16[2,512,256]{2,1,0:T(8,128)(2,1)S(1)}, bf16[2,512,256]{2,1,0:T(8,128)(2,1)S(1)}, u32[]{:S(2)}, u32[]{:S(2)}) collective-permute-start(bf16[2,512,256]{2,1,0:T(8,128)(2,1)S(1)} %get-tuple-element.63.refs_4_), channel_id=1, source_target_pairs={{2,4},{3,5},{4,2},{5,3},{10,12},{11,13},{12,10},{13,11},{18,20},{1... | collective-permute-start | bytes 1572872 | tf_op jit(solution)/shard_map/ppermute | solution.py:531
  25.3 20.6 %collective-permute-start.4 = (bf16[2,256,512]{2,1,0:T(8,128)(2,1)S(1)}, bf16[2,256,512]{2,1,0:T(8,128)(2,1)S(1)}, u32[]{:S(2)}, u32[]{:S(2)}) collective-permute-start(bf16[2,256,512]{2,1,0:T(8,128)(2,1)S(1)} %get-tuple-element.58.refs_0_), channel_id=1, source_target_pairs={{0,2},{1,3},{6,4},{7,5},{8,10},{9,11},{14,12},{15,13},{16,18},{17,... | collective-permute-start | bytes 1572872 | tf_op jit(solution)/shard_map/ppermute | solution.py:531
  35.5 10.4 %collective-permute-start.2 = (bf16[2,256,512]{2,1,0:T(8,128)(2,1)S(1)}, bf16[2,256,512]{2,1,0:T(8,128)(2,1)S(1)}, u32[]{:S(2)}, u32[]{:S(2)}) collective-permute-start(bf16[2,256,512]{2,1,0:T(8,128)(2,1)S(1)} %shard_map.108.refs_2_), channel_id=1, source_target_pairs={{2,4},{3,5},{4,2},{5,3},{10,12},{11,13},{12,10},{13,11},{18,20},{1... | collective-permute-start | bytes 1572872 | tf_op jit(solution)/shard_map/ppermute | solution.py:531
  38.9 15.7 %collective-permute-start.10 = (bf16[2,512,256]{2,1,0:T(8,128)(2,1)S(1)}, bf16[2,512,256]{2,1,0:T(8,128)(2,1)S(1)}, u32[]{:S(2)}, u32[]{:S(2)}) collective-permute-start(bf16[2,512,256]{2,1,0:T(8,128)(2,1)S(1)} %shard_map.112.refs_0_), channel_id=1, source_target_pairs={{2,0},{3,1},{4,6},{5,7},{10,8},{11,9},{12,14},{13,15},{18,16},{19,... | collective-permute-start | bytes 1572872 | tf_op jit(solution)/shard_map/ppermute | solution.py:531
  40.2 17.0 %collective-permute-start.11 = (bf16[2,512,256]{2,1,0:T(8,128)(2,1)S(1)}, bf16[2,512,256]{2,1,0:T(8,128)(2,1)S(1)}, u32[]{:S(2)}, u32[]{:S(2)}) collective-permute-start(bf16[2,512,256]{2,1,0:T(8,128)(2,1)S(1)} %get-tuple-element.62.refs_3_), channel_id=1, source_target_pairs={{0,1},{1,0},{2,3},{3,2},{4,5},{5,4},{6,7},{7,6},{8,9},{9,8},{10,11... | collective-permute-start | bytes 1572872 | tf_op jit(solution)/shard_map/ppermute | solution.py:539
  40.3 16.9 %collective-permute-start.12 = (bf16[2,512,256]{2,1,0:T(8,128)(2,1)S(1)}, bf16[2,512,256]{2,1,0:T(8,128)(2,1)S(1)}, u32[]{:S(2)}, u32[]{:S(2)}) collective-permute-start(bf16[2,512,256]{2,1,0:T(8,128)(2,1)S(1)} %get-tuple-element.63.refs_4_), channel_id=1, source_target_pairs={{0,1},{1,0},{2,3},{3,2},{4,5},{5,4},{6,7},{7,6},{8,9},{9,8},{10,11... | collective-permute-start | bytes 1572872 | tf_op jit(solution)/shard_map/ppermute | solution.py:539
  54.7 3.0 %collective-permute-start.13 = (bf16[1,512,256]{2,1,0:T(8,128)(2,1)S(1)}, bf16[1,512,256]{2,1,0:T(8,128)(2,1)S(1)}, u32[]{:S(2)}, u32[]{:S(2)}) collective-permute-start(bf16[1,512,256]{2,1,0:T(8,128)(2,1)S(1)} %get-tuple-element.65.refs_5_), channel_id=1, source_target_pairs={{0,1},{1,0},{2,3},{3,2},{4,5},{5,4},{6,7},{7,6},{8,9},{9,8},{10,11... | collective-permute-start | bytes 786440 | tf_op jit(solution)/shard_map/ppermute | solution.py:539
  54.8 11.7 %collective-permute-start.5 = (bf16[2,256,512]{2,1,0:T(8,128)(2,1)S(1)}, bf16[2,256,512]{2,1,0:T(8,128)(2,1)S(1)}, u32[]{:S(2)}, u32[]{:S(2)}) collective-permute-start(bf16[2,256,512]{2,1,0:T(8,128)(2,1)S(1)} %shard_map.110.refs_4_), channel_id=1, source_target_pairs={{2,4},{3,5},{4,2},{5,3},{10,12},{11,13},{12,10},{13,11},{18,20},{1... | collective-permute-start | bytes 1572872 | tf_op jit(solution)/shard_map/ppermute | solution.py:531
  55.7 14.4 %collective-permute-start.3 = (bf16[2,256,512]{2,1,0:T(8,128)(2,1)S(1)}, bf16[2,256,512]{2,1,0:T(8,128)(2,1)S(1)}, u32[]{:S(2)}, u32[]{:S(2)}) collective-permute-start(bf16[2,256,512]{2,1,0:T(8,128)(2,1)S(1)} %shard_map.109.refs_5_), channel_id=1, source_target_pairs={{0,2},{1,3},{2,0},{3,1},{4,6},{5,7},{6,4},{7,5},{8,10},{9,11},{10,... | collective-permute-start | bytes 1572872 | tf_op jit(solution)/shard_map/ppermute | solution.py:531
  57.2 1.5 collective-permute-start.14
  57.2 1.9 %collective-permute-start.15 = (bf16[1,512,256]{2,1,0:T(8,128)(2,1)S(1)}, bf16[1,512,256]{2,1,0:T(8,128)(2,1)S(1)}, u32[]{:S(2)}, u32[]{:S(2)}) collective-permute-start(bf16[1,512,256]{2,1,0:T(8,128)(2,1)S(1)} %get-tuple-element.67.refs_7_), channel_id=1, source_target_pairs={{0,1},{1,0},{2,3},{3,2},{4,5},{5,4},{6,7},{7,6},{8,9},{9,8},{10,11... | collective-permute-start | bytes 786440 | tf_op jit(solution)/shard_map/ppermute | solution.py:539
  57.7 1.8 %collective-permute-start.16 = (bf16[1,512,256]{2,1,0:T(8,128)(2,1)S(1)}, bf16[1,512,256]{2,1,0:T(8,128)(2,1)S(1)}, u32[]{:S(2)}, u32[]{:S(2)}) collective-permute-start(bf16[1,512,256]{2,1,0:T(8,128)(2,1)S(1)} %get-tuple-element.68.refs_8_), channel_id=1, source_target_pairs={{0,1},{1,0},{2,3},{3,2},{4,5},{5,4},{6,7},{7,6},{8,9},{9,8},{10,11... | collective-permute-start | bytes 786440 | tf_op jit(solution)/shard_map/ppermute | solution.py:539
  66.4 8.7 %copy-start = (bf16[512,512]{1,0:T(8,128)(2,1)S(1)}, bf16[512,512]{1,0:T(8,128)(2,1)}, u32[]{:S(2)}) copy-start(bf16[512,512]{1,0:T(8,128)(2,1)} %refs_4_.6) | copy-start | bytes 1572868
  70.3 5.6 %copy-start.3 = (bf16[512,512]{1,0:T(8,128)(2,1)S(1)}, bf16[512,512]{1,0:T(8,128)(2,1)}, u32[]{:S(2)}) copy-start(bf16[512,512]{1,0:T(8,128)(2,1)} %refs_4_.7) | copy-start | bytes 1572868
  70.3 9.7 %collective-permute-start.17 = (bf16[256,512]{1,0:T(8,128)(2,1)S(1)}, bf16[256,512]{1,0:T(8,128)(2,1)S(1)}, u32[]{:S(2)}, u32[]{:S(2)}) collective-permute-start(bf16[256,512]{1,0:T(8,128)(2,1)S(1)} %get-tuple-element.69.refs_0_), channel_id=1, source_target_pairs={{0,8},{8,0},{16,24},{24,16},{1,9},{9,1},{17,25},{25,17},{2,10},{10... | collective-permute-start | bytes 786440 | tf_op jit(solution)/shard_map/ppermute | solution.py:542
  72.8 9.4 %collective-permute-start.19 = (bf16[256,512]{1,0:T(8,128)(2,1)S(1)}, bf16[256,512]{1,0:T(8,128)(2,1)S(1)}, u32[]{:S(2)}, u32[]{:S(2)}) collective-permute-start(bf16[256,512]{1,0:T(8,128)(2,1)S(1)} %get-tuple-element.70.refs_1_), channel_id=1, source_target_pairs={{0,16},{8,24},{16,0},{24,8},{1,17},{9,25},{17,1},{25,9},{2,18},{10... | collective-permute-start | bytes 786440 | tf_op jit(solution)/shard_map/ppermute | solution.py:542
  75.7 9.8 %collective-permute-start.21 = (bf16[256,512]{1,0:T(8,128)(2,1)S(1)}, bf16[256,512]{1,0:T(8,128)(2,1)S(1)}, u32[]{:S(2)}, u32[]{:S(2)}) collective-permute-start(bf16[256,512]{1,0:T(8,128)(2,1)S(1)} %get-tuple-element.72), channel_id=1, source_target_pairs={{0,8},{8,0},{16,24},{24,16},{1,9},{9,1},{17,25},{25,17},{2,10},{10... | collective-permute-start | bytes 786440 | tf_op jit(solution)/shard_map/ppermute | solution.py:542
  75.9 12.0 %collective-permute-start.22 = (bf16[256,512]{1,0:T(8,128)(2,1)S(1)}, bf16[256,512]{1,0:T(8,128)(2,1)S(1)}, u32[]{:S(2)}, u32[]{:S(2)}) collective-permute-start(bf16[256,512]{1,0:T(8,128)(2,1)S(1)} %get-tuple-element.73), channel_id=1, source_target_pairs={{0,16},{8,24},{16,0},{24,8},{1,17},{9,25},{17,1},{25,9},{2,18},{10... | collective-permute-start | bytes 786440 | tf_op jit(solution)/shard_map/ppermute | solution.py:542
  80.0 13.3 %collective-permute-start.18 = (bf16[256,512]{1,0:T(8,128)(2,1)S(1)}, bf16[256,512]{1,0:T(8,128)(2,1)S(1)}, u32[]{:S(2)}, u32[]{:S(2)}) collective-permute-start(bf16[256,512]{1,0:T(8,128)(2,1)S(1)} %collective-permute-done.17.refs_0_), channel_id=1, source_target_pairs={{0,16},{8,24},{16,0},{24,8},{1,17},{9,25},{17,1},{25,9},{2,18},{10... | collective-permute-start | bytes 786440 | tf_op jit(solution)/shard_map/ppermute | solution.py:542
  82.3 11.1 %collective-permute-start.20 = (bf16[256,512]{1,0:T(8,128)(2,1)S(1)}, bf16[256,512]{1,0:T(8,128)(2,1)S(1)}, u32[]{:S(2)}, u32[]{:S(2)}) collective-permute-start(bf16[256,512]{1,0:T(8,128)(2,1)S(1)} %collective-permute-done.19.refs_3_), channel_id=1, source_target_pairs={{0,8},{8,0},{16,24},{24,16},{1,9},{9,1},{17,25},{25,17},{2,10},{10... | collective-permute-start | bytes 786440 | tf_op jit(solution)/shard_map/ppermute | solution.py:542
  96.7 14.1 %collective-permute-start.24 = (bf16[512,512]{1,0:T(8,128)(2,1)S(1)}, bf16[512,512]{1,0:T(8,128)(2,1)S(1)}, u32[]{:S(2)}, u32[]{:S(2)}) collective-permute-start(bf16[512,512]{1,0:T(8,128)(2,1)S(1)} %get-tuple-element.87), channel_id=1, source_target_pairs={{0,1},{1,0},{2,3},{3,2},{4,5},{5,4},{6,7},{7,6},{8,9},{9,8},{10,11... | collective-permute-start | bytes 1572872 | tf_op jit(solution)/shard_map/ppermute | solution.py:539
  100.6 4.2 %collective-permute-start.23 = (bf16[8,256,512]{2,1,0:T(8,128)(2,1)S(1)}, bf16[8,256,512]{2,1,0:T(8,128)(2,1)S(1)}, u32[]{:S(2)}, u32[]{:S(2)}) collective-permute-start(bf16[8,256,512]{2,1,0:T(8,128)(2,1)S(1)} %shard_map.124), channel_id=1, source_target_pairs={{0,1},{1,0},{2,3},{3,2},{4,5},{5,4},{6,7},{7,6},{8,9},{9,8},{10,11... | collective-permute-start | bytes 6291464 | tf_op jit(solution)/shard_map/ppermute | solution.py:539
  105.1 25.8 %collective-permute-start.31 = (bf16[2,256,512]{2,1,0:T(8,128)(2,1)S(1)}, bf16[2,256,512]{2,1,0:T(8,128)(2,1)S(1)}, u32[]{:S(2)}, u32[]{:S(2)}) collective-permute-start(bf16[2,256,512]{2,1,0:T(8,128)(2,1)S(1)} %get-tuple-element.96.refs_0_), channel_id=1, source_target_pairs={{0,2},{1,3},{6,4},{7,5},{8,10},{9,11},{14,12},{15,13},{16,18},{17,... | collective-permute-start | bytes 1572872 | tf_op jit(solution)/shard_map/ppermute | solution.py:531
  110.9 5.1 %collective-permute-start.25 = (bf16[128,512]{1,0:T(8,128)(2,1)S(1)}, bf16[128,512]{1,0:T(8,128)(2,1)S(1)}, u32[]{:S(2)}, u32[]{:S(2)}) collective-permute-start(bf16[128,512]{1,0:T(8,128)(2,1)S(1)} %get-tuple-element.89), channel_id=1, source_target_pairs={{0,8},{8,0},{16,24},{24,16},{1,9},{9,1},{17,25},{25,17},{2,10},{10... | collective-permute-start | bytes 393224 | tf_op jit(solution)/shard_map/ppermute | solution.py:542
  111.4 8.0 %collective-permute-start.26 = (bf16[128,512]{1,0:T(8,128)(2,1)S(1)}, bf16[128,512]{1,0:T(8,128)(2,1)S(1)}, u32[]{:S(2)}, u32[]{:S(2)}) collective-permute-start(bf16[128,512]{1,0:T(8,128)(2,1)S(1)} %get-tuple-element.90), channel_id=1, source_target_pairs={{0,16},{8,24},{16,0},{24,8},{1,17},{9,25},{17,1},{25,9},{2,18},{10... | collective-permute-start | bytes 393224 | tf_op jit(solution)/shard_map/ppermute | solution.py:542
  113.6 7.7 %collective-permute-start.27 = (bf16[128,512]{1,0:T(8,128)(2,1)S(1)}, bf16[128,512]{1,0:T(8,128)(2,1)S(1)}, u32[]{:S(2)}, u32[]{:S(2)}) collective-permute-start(bf16[128,512]{1,0:T(8,128)(2,1)S(1)} %get-tuple-element.91), channel_id=1, source_target_pairs={{0,24},{8,16},{16,8},{24,0},{1,25},{9,17},{17,9},{25,1},{2,26},{10... | collective-permute-start | bytes 393224 | tf_op jit(solution)/shard_map/ppermute | solution.py:542
  121.3 4.5 %collective-permute-start.28 = (bf16[32,512]{1,0:T(8,128)(2,1)S(1)}, bf16[32,512]{1,0:T(8,128)(2,1)S(1)}, u32[]{:S(2)}, u32[]{:S(2)}) collective-permute-start(bf16[32,512]{1,0:T(8,128)(2,1)S(1)} %get-tuple-element.93), channel_id=1, source_target_pairs={{0,2},{1,3},{2,0},{3,1},{4,6},{5,7},{6,4},{7,5},{8,10},{9,11},{10,... | collective-permute-start | bytes 98312 | tf_op jit(solution)/shard_map/ppermute | solution.py:531
  121.4 5.4 %collective-permute-start.29 = (bf16[32,512]{1,0:T(8,128)(2,1)S(1)}, bf16[32,512]{1,0:T(8,128)(2,1)S(1)}, u32[]{:S(2)}, u32[]{:S(2)}) collective-permute-start(bf16[32,512]{1,0:T(8,128)(2,1)S(1)} %get-tuple-element.94), channel_id=1, source_target_pairs={{0,4},{1,5},{2,6},{3,7},{4,0},{5,1},{6,2},{7,3},{8,12},{9,13},{10,... | collective-permute-start | bytes 98312 | tf_op jit(solution)/shard_map/ppermute | solution.py:531
  123.8 5.7 %collective-permute-start.30 = (bf16[32,512]{1,0:T(8,128)(2,1)S(1)}, bf16[32,512]{1,0:T(8,128)(2,1)S(1)}, u32[]{:S(2)}, u32[]{:S(2)}) collective-permute-start(bf16[32,512]{1,0:T(8,128)(2,1)S(1)} %get-tuple-element.95), channel_id=1, source_target_pairs={{0,6},{1,7},{2,4},{3,5},{4,2},{5,3},{6,0},{7,1},{8,14},{9,15},{10,... | collective-permute-start | bytes 98312 | tf_op jit(solution)/shard_map/ppermute | solution.py:531
  129.5 16.4 %collective-permute-start.34 = (bf16[2,256,512]{2,1,0:T(8,128)(2,1)S(1)}, bf16[2,256,512]{2,1,0:T(8,128)(2,1)S(1)}, u32[]{:S(2)}, u32[]{:S(2)}) collective-permute-start(bf16[2,256,512]{2,1,0:T(8,128)(2,1)S(1)} %shard_map.131.refs_0_), channel_id=1, source_target_pairs={{0,2},{1,3},{6,4},{7,5},{8,10},{9,11},{14,12},{15,13},{16,18},{17,... | collective-permute-start | bytes 1572872 | tf_op jit(solution)/shard_map/ppermute | solution.py:531
  131.0 15.8 %collective-permute-start.32 = (bf16[2,256,512]{2,1,0:T(8,128)(2,1)S(1)}, bf16[2,256,512]{2,1,0:T(8,128)(2,1)S(1)}, u32[]{:S(2)}, u32[]{:S(2)}) collective-permute-start(bf16[2,256,512]{2,1,0:T(8,128)(2,1)S(1)} %shard_map.132.refs_2_), channel_id=1, source_target_pairs={{2,4},{3,5},{4,2},{5,3},{10,12},{11,13},{12,10},{13,11},{18,20},{1... | collective-permute-start | bytes 1572872 | tf_op jit(solution)/shard_map/ppermute | solution.py:531
  131.7 12.9 %collective-permute-start.37 = (bf16[32,512]{1,0:T(8,128)(2,1)S(1)}, bf16[32,512]{1,0:T(8,128)(2,1)S(1)}, u32[]{:S(2)}, u32[]{:S(2)}) collective-permute-start(bf16[32,512]{1,0:T(8,128)(2,1)S(1)} %shard_map.130.refs_1_.refs_0_), channel_id=1, source_target_pairs={{0,6},{1,7},{2,4},{3,5},{4,2},{5,3},{6,0},{7,1},{8,14},{9,15},{10,... | collective-permute-start | bytes 98312 | tf_op jit(solution)/shard_map/ppermute | solution.py:531
  133.8 12.2 %collective-permute-start.36 = (bf16[32,512]{1,0:T(8,128)(2,1)S(1)}, bf16[32,512]{1,0:T(8,128)(2,1)S(1)}, u32[]{:S(2)}, u32[]{:S(2)}) collective-permute-start(bf16[32,512]{1,0:T(8,128)(2,1)S(1)} %shard_map.130.refs_1_.refs_0_), channel_id=1, source_target_pairs={{0,4},{1,5},{2,6},{3,7},{4,0},{5,1},{6,2},{7,3},{8,12},{9,13},{10,... | collective-permute-start | bytes 98312 | tf_op jit(solution)/shard_map/ppermute | solution.py:531
  134.4 11.6 %collective-permute-start.35 = (bf16[32,512]{1,0:T(8,128)(2,1)S(1)}, bf16[32,512]{1,0:T(8,128)(2,1)S(1)}, u32[]{:S(2)}, u32[]{:S(2)}) collective-permute-start(bf16[32,512]{1,0:T(8,128)(2,1)S(1)} %shard_map.130.refs_1_.refs_0_), channel_id=1, source_target_pairs={{0,2},{1,3},{2,0},{3,1},{4,6},{5,7},{6,4},{7,5},{8,10},{9,11},{10,... | collective-permute-start | bytes 98312 | tf_op jit(solution)/shard_map/ppermute | solution.py:531
  146.1 10.4 %collective-permute-start.38 = (bf16[2,256,512]{2,1,0:T(8,128)(2,1)S(1)}, bf16[2,256,512]{2,1,0:T(8,128)(2,1)S(1)}, u32[]{:S(2)}, u32[]{:S(2)}) collective-permute-start(bf16[2,256,512]{2,1,0:T(8,128)(2,1)S(1)} %shard_map.135), channel_id=1, source_target_pairs={{2,4},{3,5},{4,2},{5,3},{10,12},{11,13},{12,10},{13,11},{18,20},{1... | collective-permute-start | bytes 1572872 | tf_op jit(solution)/shard_map/ppermute | solution.py:531
  146.9 11.1 %collective-permute-start.33 = (bf16[2,256,512]{2,1,0:T(8,128)(2,1)S(1)}, bf16[2,256,512]{2,1,0:T(8,128)(2,1)S(1)}, u32[]{:S(2)}, u32[]{:S(2)}) collective-permute-start(bf16[2,256,512]{2,1,0:T(8,128)(2,1)S(1)} %shard_map.133), channel_id=1, source_target_pairs={{0,2},{1,3},{2,0},{3,1},{4,6},{5,7},{6,4},{7,5},{8,10},{9,11},{10,... | collective-permute-start | bytes 1572872 | tf_op jit(solution)/shard_map/ppermute | solution.py:531
  149.1 5.9 %collective-permute-start.41 = (bf16[128,512]{1,0:T(8,128)(2,1)S(1)}, bf16[128,512]{1,0:T(8,128)(2,1)S(1)}, u32[]{:S(2)}, u32[]{:S(2)}) collective-permute-start(bf16[128,512]{1,0:T(8,128)(2,1)S(1)} %shard_map.134.refs_3_.refs_0_), channel_id=1, source_target_pairs={{0,24},{8,16},{16,8},{24,0},{1,25},{9,17},{17,9},{25,1},{2,26},{10... | collective-permute-start | bytes 393224 | tf_op jit(solution)/shard_map/ppermute | solution.py:542
  150.8 5.5 %collective-permute-start.40 = (bf16[128,512]{1,0:T(8,128)(2,1)S(1)}, bf16[128,512]{1,0:T(8,128)(2,1)S(1)}, u32[]{:S(2)}, u32[]{:S(2)}) collective-permute-start(bf16[128,512]{1,0:T(8,128)(2,1)S(1)} %shard_map.134.refs_3_.refs_0_), channel_id=1, source_target_pairs={{0,16},{8,24},{16,0},{24,8},{1,17},{9,25},{17,1},{25,9},{2,18},{10... | collective-permute-start | bytes 393224 | tf_op jit(solution)/shard_map/ppermute | solution.py:542
  150.9 5.5 %collective-permute-start.39 = (bf16[128,512]{1,0:T(8,128)(2,1)S(1)}, bf16[128,512]{1,0:T(8,128)(2,1)S(1)}, u32[]{:S(2)}, u32[]{:S(2)}) collective-permute-start(bf16[128,512]{1,0:T(8,128)(2,1)S(1)} %shard_map.134.refs_3_.refs_0_), channel_id=1, source_target_pairs={{0,8},{8,0},{16,24},{24,16},{1,9},{9,1},{17,25},{25,17},{2,10},{10... | collective-permute-start | bytes 393224 | tf_op jit(solution)/shard_map/ppermute | solution.py:542
  156.4 2.9 %collective-permute-start.42 = (bf16[512,512]{1,0:T(8,128)(2,1)S(1)}, bf16[512,512]{1,0:T(8,128)(2,1)S(1)}, u32[]{:S(2)}, u32[]{:S(2)}) collective-permute-start(bf16[512,512]{1,0:T(8,128)(2,1)S(1)} %shard_map.137.refs_0_), channel_id=1, source_target_pairs={{0,1},{1,0},{2,3},{3,2},{4,5},{5,4},{6,7},{7,6},{8,9},{9,8},{10,11... | collective-permute-start | bytes 1572872 | tf_op jit(solution)/shard_map/ppermute | solution.py:539

commit v13 on v12

--- a/solution.py
+++ b/solution.py
@@ -613,7 +613,7 @@
 
     grad_give, grad_keep = sums
     _, own = run_pass(stacked[1], False, ((1,), (0,)), (grad_keep,))
-    split = split_sum([grad_keep, core_flip(grad_give)], n_row, "row", own[:1])
+    split = split_sum([grad_keep, core_flip(grad_give)], n_row, "row", own[2:3])
     moment = [split[0]] + [row_flip(split[j], j) for j in range(1, n_row)]
     if split[0].shape[0] % (16 * line) == 0:
         split = split_sum(moment, line, "line")

time: 160 us -> 159 us (level)
  Pallas kernels: 43.3 us -> 36.1 us
  waiting for transfers between devices: 58.5 us -> 61.6 us
  starting transfers between devices: 55.4 us -> 57.7 us
    pallas_call x36, Pallas kernels: 43.3 us -> 36.1 us  [run(): pl.pallas_call(whole, out_shape=outs, in_specs=specs + [ANY] * extra, out...]
    ppermute x21, waiting for transfers between devices: 39.1 us -> 42.7 us  [col_send(): lax.ppermute(value, 'col', [(2 * a + k, 2 * b + k) for a, b in pairs for...]
    ppermute x12, waiting for transfers between devices: 15.9 us -> 14.1 us  [row_flip(): return lax.ppermute(value, 'row', [(a, a ^ j) for a in range(n_row)])]
  transfers between devices with their start and end apart: 43 -> 43, of which waited for: 22 -> 23; matrix products, arithmetic and copies ran while one was open for 0% -> 0% of each run, Pallas kernels for 23% -> 19%
where the time goes in v13:
time: 159 us
  waiting for transfers between devices  61.6 us (39%)
  starting transfers between devices  57.7 us (36%)
  Pallas kernels  36.1 us (23%)
  between operations  1.83 us (1%)
  local copies, waits for them, and re-layouts  1.77 us (1%)
    ppermute x21, waiting for transfers between devices, col_send(): lax.ppermute(value, 'col', [(2 * a + k, 2 * b + k) for a, b in pairs for...  42.7 us
    ppermute x21, starting transfers between devices, col_send(): lax.ppermute(value, 'col', [(2 * a + k, 2 * b + k) for a, b in pairs for...  39 us
    pallas_call x36, Pallas kernels, run(): pl.pallas_call(whole, out_shape=outs, in_specs=specs + [ANY] * extra, out...  36.1 us
    ppermute x12, starting transfers between devices, row_flip(): return lax.ppermute(value, 'row', [(a, a ^ j) for a in range(n_row)])  16.4 us
    ppermute x12, waiting for transfers between devices, row_flip(): return lax.ppermute(value, 'row', [(a, a ^ j) for a in range(n_row)])  14.1 us
    ppermute x10, waiting for transfers between devices, core_flip(): return lax.ppermute(value, 'col', [(a, a ^ 1) for a in range(n_col)])  4.9 us
  transfers between devices with their start and end apart: 43, of which 23 were waited for; matrix products, arithmetic and copies ran while one was open for 0% of the time, Pallas kernels for 19%

profile of v13, /device:TPU:0, one launch (start us, length us, event | category | flops | bytes accessed | tf_op | source)
XLA Modules:
  0.0 159.1 jit_solution(10920046150584804562)
XLA Ops:
  0.6 0.7 copy.13
  1.3 1.0 copy-done.2
  2.9 0.8 collective-permute-start.7
  3.8 6.0 %collective-permute-start.6 = (bf16[2,512,256]{2,1,0:T(8,128)(2,1)S(1)}, bf16[2,512,256]{2,1,0:T(8,128)(2,1)S(1)}, u32[]{:S(2)}, u32[]{:S(2)}) collective-permute-start(bf16[2,512,256]{2,1,0:T(8,128)(2,1)S(1)} %get-tuple-element.62.refs_3_), channel_id=1, source_target_pairs={{0,2},{1,3},{2,0},{3,1},{4,6},{5,7},{6,4},{7,5},{8,10},{9,11},{10,... | collective-permute-start | bytes 1572872 | tf_op jit(solution)/shard_map/ppermute | solution.py:531
  10.5 2.2 %shard_map.104 = (bf16[8,256,512]{2,1,0:T(8,128)(2,1)S(1)}, s32[16]{0:T(128)S(1)}, s32[128]{0:T(128)S(1)}, s32[8]{0:T(128)S(1)}, s32[128]{0:T(128)S(1)}) custom-call(s32[1]{0:T(128)} %bitcast.7.refs_0_, s32[48]{0:T(128)S(1)} %bitcast.18, bf16[8,256,512]{2,1,0:T(8,128)(2,1)S(1)} %bitcast.17, f32[8,256,128]{2,1,0:T(8,128)S(1)} %get-tuple-element.52.refs_3_.refs_2_.refs_4_), custom_call_target="tpu_custom_call" | custom-call | flops 35999997952 | tf_op jit(solution)/shard_map/pallas_call | solution.py:25
  12.7 2.8 %shard_map.106.refs_2_ = bf16[8,256,512]{2,1,0:T(8,128)(2,1)S(1)} custom-call(s32[16]{0:T(128)S(1)} %get-tuple-element.53.refs_0_, s32[128]{0:T(128)S(1)} %get-tuple-element.54.refs_1_, bf16[48,256,256]{2,1,0:T(8,128)(2,1)S(1)} %bitcast.10, bf16[8,256,512]{2,1,0:T(8,128)(2,1)S(1)} %get-tuple-element.55.refs_3_), custom_call_target="tpu_custom_call" | custom-call | flops 35999997952 | tf_op jit(solution)/shard_map/pallas_call | solution.py:25
  15.6 2.8 %shard_map.105.refs_0_ = bf16[8,256,512]{2,1,0:T(8,128)(2,1)S(1)} custom-call(s32[16]{0:T(128)S(1)} %get-tuple-element.53.refs_0_, s32[128]{0:T(128)S(1)} %get-tuple-element.54.refs_1_, bf16[48,256,256]{2,1,0:T(8,128)(2,1)S(1)} %bitcast.11, bf16[8,256,512]{2,1,0:T(8,128)(2,1)S(1)} %get-tuple-element.55.refs_3_), custom_call_target="tpu_custom_call" | custom-call | flops 35999997952 | tf_op jit(solution)/shard_map/pallas_call | solution.py:25
  18.4 1.3 collective-permute-done.refs_1_
  20.2 3.1 %collective-permute-start.1 = (bf16[2,256,512]{2,1,0:T(8,128)(2,1)S(1)}, bf16[2,256,512]{2,1,0:T(8,128)(2,1)S(1)}, u32[]{:S(2)}, u32[]{:S(2)}) collective-permute-start(bf16[2,256,512]{2,1,0:T(8,128)(2,1)S(1)} %get-tuple-element.59.refs_0_), channel_id=1, source_target_pairs={{0,2},{1,3},{6,4},{7,5},{8,10},{9,11},{14,12},{15,13},{16,18},{17,... | collective-permute-start | bytes 1572872 | tf_op jit(solution)/shard_map/ppermute | solution.py:531
  23.4 1.3 collective-permute-start.9
  24.7 0.7 collective-permute-start.8
  25.4 6.5 %collective-permute-start.4 = (bf16[2,256,512]{2,1,0:T(8,128)(2,1)S(1)}, bf16[2,256,512]{2,1,0:T(8,128)(2,1)S(1)}, u32[]{:S(2)}, u32[]{:S(2)}) collective-permute-start(bf16[2,256,512]{2,1,0:T(8,128)(2,1)S(1)} %get-tuple-element.58.refs_0_), channel_id=1, source_target_pairs={{0,2},{1,3},{6,4},{7,5},{8,10},{9,11},{14,12},{15,13},{16,18},{17,... | collective-permute-start | bytes 1572872 | tf_op jit(solution)/shard_map/ppermute | solution.py:531
  31.9 3.7 %collective-permute-done.1.refs_1_ = bf16[2,256,512]{2,1,0:T(8,128)(2,1)S(1)} collective-permute-done((bf16[2,256,512]{2,1,0:T(8,128)(2,1)S(1)}, bf16[2,256,512]{2,1,0:T(8,128)(2,1)S(1)}, u32[]{:S(2)}, u32[]{:S(2)}) %collective-permute-start.1) | collective-permute-done | bytes 524320 | tf_op jit(solution)/shard_map/ppermute | solution.py:531
  35.7 0.7 collective-permute-start.2
  36.4 2.6 %collective-permute-done.9.refs_2_ = bf16[2,512,256]{2,1,0:T(8,128)(2,1)S(1)} collective-permute-done((bf16[2,512,256]{2,1,0:T(8,128)(2,1)S(1)}, bf16[2,512,256]{2,1,0:T(8,128)(2,1)S(1)}, u32[]{:S(2)}, u32[]{:S(2)}) %collective-permute-start.9) | collective-permute-done | bytes 524320 | tf_op jit(solution)/shard_map/ppermute | solution.py:531
  39.1 1.3 collective-permute-start.10
  40.9 5.1 %collective-permute-done.4.refs_1_ = bf16[2,256,512]{2,1,0:T(8,128)(2,1)S(1)} collective-permute-done((bf16[2,256,512]{2,1,0:T(8,128)(2,1)S(1)}, bf16[2,256,512]{2,1,0:T(8,128)(2,1)S(1)}, u32[]{:S(2)}, u32[]{:S(2)}) %collective-permute-start.4) | collective-permute-done | bytes 524320 | tf_op jit(solution)/shard_map/ppermute | solution.py:531
  46.3 8.5 %collective-permute-done.10.refs_3_ = bf16[2,512,256]{2,1,0:T(8,128)(2,1)S(1)} collective-permute-done((bf16[2,512,256]{2,1,0:T(8,128)(2,1)S(1)}, bf16[2,512,256]{2,1,0:T(8,128)(2,1)S(1)}, u32[]{:S(2)}, u32[]{:S(2)}) %collective-permute-start.10) | collective-permute-done | bytes 524320 | tf_op jit(solution)/shard_map/ppermute | solution.py:531
  55.0 0.9 collective-permute-start.5
  55.8 1.6 %collective-permute-start.3 = (bf16[2,256,512]{2,1,0:T(8,128)(2,1)S(1)}, bf16[2,256,512]{2,1,0:T(8,128)(2,1)S(1)}, u32[]{:S(2)}, u32[]{:S(2)}) collective-permute-start(bf16[2,256,512]{2,1,0:T(8,128)(2,1)S(1)} %shard_map.109.refs_5_), channel_id=1, source_target_pairs={{0,2},{1,3},{2,0},{3,1},{4,6},{5,7},{6,4},{7,5},{8,10},{9,11},{10,... | collective-permute-start | bytes 1572872 | tf_op jit(solution)/shard_map/ppermute | solution.py:531
  58.0 0.9 collective-permute-done.14.refs_12_
  59.7 4.6 %shard_map.114.refs_4_.refs_0_ = bf16[8,512,256]{2,1,0:T(8,128)(2,1)S(1)} custom-call(s32[8]{0:T(128)S(1)} %get-tuple-element.60.refs_0_, s32[128]{0:T(128)S(1)} %get-tuple-element.61.refs_1_, bf16[48,256,256]{2,1,0:T(8,128)(2,1)S(1)} %bitcast.12, bf16[2,512,256]{2,1,0:T(8,128)(2,1)S(1)} %get-tuple-element.62.refs_3_, ...), custom_call_target="tpu_custom_call" | custom-call | tf_op jit(solution)/shard_map/pallas_call | solution.py:25
  64.3 5.9 %collective-permute-done.3.refs_1_ = bf16[2,256,512]{2,1,0:T(8,128)(2,1)S(1)} collective-permute-done((bf16[2,256,512]{2,1,0:T(8,128)(2,1)S(1)}, bf16[2,256,512]{2,1,0:T(8,128)(2,1)S(1)}, u32[]{:S(2)}, u32[]{:S(2)}) %collective-permute-start.3) | collective-permute-done | bytes 524320 | tf_op jit(solution)/shard_map/ppermute | solution.py:531
  70.5 1.4 collective-permute-start.17
  71.8 2.3 %collective-permute-start.19 = (bf16[256,512]{1,0:T(8,128)(2,1)S(1)}, bf16[256,512]{1,0:T(8,128)(2,1)S(1)}, u32[]{:S(2)}, u32[]{:S(2)}) collective-permute-start(bf16[256,512]{1,0:T(8,128)(2,1)S(1)} %get-tuple-element.70.refs_1_), channel_id=1, source_target_pairs={{0,16},{8,24},{16,0},{24,8},{1,17},{9,25},{17,1},{25,9},{2,18},{10... | collective-permute-start | bytes 786440 | tf_op jit(solution)/shard_map/ppermute | solution.py:542
  75.3 2.2 %shard_map.118 = (f32[512,512]{1,0:T(8,128)S(1)}, f32[512,512]{1,0:T(8,128)S(1)}) custom-call(bf16[8,512,256]{2,1,0:T(8,128)(2,1)S(1)} %shard_map.114.refs_4_.refs_0_, bf16[2,256,512]{2,1,0:T(8,128)(2,1)S(1)} %get-tuple-element.71.refs_2_.refs_1_.refs_6_, bf16[2,256,512]{2,1,0:T(8,128)(2,1)S(1)} %get-tuple-element.74.refs_2_.refs_7_, ...), custom_call_target="tpu_custom_call" | custom-call | flops 35999997952 | tf_op jit(solution)/shard_map/pallas_call | solution.py:25
  77.5 2.2 %collective-permute-done.17.refs_0_ = bf16[256,512]{1,0:T(8,128)(2,1)S(1)} collective-permute-done((bf16[256,512]{1,0:T(8,128)(2,1)S(1)}, bf16[256,512]{1,0:T(8,128)(2,1)S(1)}, u32[]{:S(2)}, u32[]{:S(2)}) %collective-permute-start.17) | collective-permute-done | bytes 262176 | tf_op jit(solution)/shard_map/ppermute | solution.py:542
  79.7 1.7 %collective-permute-start.18 = (bf16[256,512]{1,0:T(8,128)(2,1)S(1)}, bf16[256,512]{1,0:T(8,128)(2,1)S(1)}, u32[]{:S(2)}, u32[]{:S(2)}) collective-permute-start(bf16[256,512]{1,0:T(8,128)(2,1)S(1)} %collective-permute-done.17.refs_0_), channel_id=1, source_target_pairs={{0,16},{8,24},{16,0},{24,8},{1,17},{9,25},{17,1},{25,9},{2,18},{10... | collective-permute-start | bytes 786440 | tf_op jit(solution)/shard_map/ppermute | solution.py:542
  81.4 1.9 %collective-permute-start.20 = (bf16[256,512]{1,0:T(8,128)(2,1)S(1)}, bf16[256,512]{1,0:T(8,128)(2,1)S(1)}, u32[]{:S(2)}, u32[]{:S(2)}) collective-permute-start(bf16[256,512]{1,0:T(8,128)(2,1)S(1)} %collective-permute-done.19.refs_3_), channel_id=1, source_target_pairs={{0,8},{8,0},{16,24},{24,16},{1,9},{9,1},{17,25},{25,17},{2,10},{10... | collective-permute-start | bytes 786440 | tf_op jit(solution)/shard_map/ppermute | solution.py:542
  83.3 2.0 %collective-permute-done.21.refs_1_ = bf16[256,512]{1,0:T(8,128)(2,1)S(1)} collective-permute-done((bf16[256,512]{1,0:T(8,128)(2,1)S(1)}, bf16[256,512]{1,0:T(8,128)(2,1)S(1)}, u32[]{:S(2)}, u32[]{:S(2)}) %collective-permute-start.21) | collective-permute-done | bytes 262176 | tf_op jit(solution)/shard_map/ppermute | solution.py:542
  85.4 1.6 collective-permute-done.22.refs_2_
  86.9 1.1 shard_map.119
  88.0 4.3 %shard_map.120 = (f32[512,512]{1,0:T(8,128)S(1)}, f32[512,512]{1,0:T(8,128)S(1)}) custom-call(bf16[8,512,256]{2,1,0:T(8,128)(2,1)S(1)} %shard_map.114.refs_4_.refs_0_, bf16[6,256,512]{2,1,0:T(8,128)(2,1)S(1)} %get-tuple-element.76.refs_1_.refs_4_, bf16[6,256,512]{2,1,0:T(8,128)(2,1)S(1)} %get-tuple-element.77.refs_2_.refs_5_, ...), custom_call_target="tpu_custom_call" | custom-call | flops 35999997952 | tf_op jit(solution)/shard_map/pallas_call | solution.py:25
  92.4 0.9 shard_map.121
  93.3 2.4 %shard_map.122 = (bf16[512,512]{1,0:T(8,128)(2,1)S(1)}, bf16[512,512]{1,0:T(8,128)(2,1)S(1)}) custom-call(bf16[8,512,256]{2,1,0:T(8,128)(2,1)S(1)} %shard_map.114.refs_4_.refs_0_, bf16[8,256,512]{2,1,0:T(8,128)(2,1)S(1)} %get-tuple-element.81.refs_1_, bf16[8,256,512]{2,1,0:T(8,128)(2,1)S(1)} %get-tuple-element.80.refs_2_.refs_3_, ...), custom_call_target="tpu_custom_call" | custom-call | flops 35999997952 | tf_op jit(solution)/shard_map/pallas_call | solution.py:25
  95.7 3.0 %shard_map.124 = bf16[8,256,512]{2,1,0:T(8,128)(2,1)S(1)} custom-call(s32[16]{0:T(128)S(1)} %get-tuple-element.53.refs_0_, s32[128]{0:T(128)S(1)} %get-tuple-element.54.refs_1_, bf16[48,256,256]{2,1,0:T(8,128)(2,1)S(1)} %bitcast.13, bf16[8,256,512]{2,1,0:T(8,128)(2,1)S(1)} %get-tuple-element.80.refs_2_.refs_3_, ...), custom_call_target="tpu_custom_call" | custom-call | flops 35999997952 | tf_op jit(solution)/shard_map/pallas_call | solution.py:25
  98.8 0.8 collective-permute-start.23
  99.6 1.9 %shard_map.123.refs_0_ = bf16[4,256,512]{2,1,0:T(8,128)(2,1)S(1)} custom-call(s32[16]{0:T(128)S(1)} %get-tuple-element.53.refs_0_, s32[128]{0:T(128)S(1)} %get-tuple-element.54.refs_1_, bf16[48,256,256]{2,1,0:T(8,128)(2,1)S(1)} %bitcast.14, bf16[8,256,512]{2,1,0:T(8,128)(2,1)S(1)} %get-tuple-element.80.refs_2_.refs_3_, ...), custom_call_target="tpu_custom_call" | custom-call | flops 35999997952 | tf_op jit(solution)/shard_map/pallas_call | solution.py:25
  101.5 1.9 %collective-permute-done.23.refs_1_ = bf16[8,256,512]{2,1,0:T(8,128)(2,1)S(1)} collective-permute-done((bf16[8,256,512]{2,1,0:T(8,128)(2,1)S(1)}, bf16[8,256,512]{2,1,0:T(8,128)(2,1)S(1)}, u32[]{:S(2)}, u32[]{:S(2)}) %collective-permute-start.23) | collective-permute-done | bytes 2097184 | tf_op jit(solution)/shard_map/ppermute | solution.py:539
  103.8 1.8 %collective-permute-start.25 = (bf16[128,512]{1,0:T(8,128)(2,1)S(1)}, bf16[128,512]{1,0:T(8,128)(2,1)S(1)}, u32[]{:S(2)}, u32[]{:S(2)}) collective-permute-start(bf16[128,512]{1,0:T(8,128)(2,1)S(1)} %get-tuple-element.89), channel_id=1, source_target_pairs={{0,8},{8,0},{16,24},{24,16},{1,9},{9,1},{17,25},{25,17},{2,10},{10... | collective-permute-start | bytes 393224 | tf_op jit(solution)/shard_map/ppermute | solution.py:542
  105.5 2.0 %collective-permute-start.26 = (bf16[128,512]{1,0:T(8,128)(2,1)S(1)}, bf16[128,512]{1,0:T(8,128)(2,1)S(1)}, u32[]{:S(2)}, u32[]{:S(2)}) collective-permute-start(bf16[128,512]{1,0:T(8,128)(2,1)S(1)} %get-tuple-element.90), channel_id=1, source_target_pairs={{0,16},{8,24},{16,0},{24,8},{1,17},{9,25},{17,1},{25,9},{2,18},{10... | collective-permute-start | bytes 393224 | tf_op jit(solution)/shard_map/ppermute | solution.py:542
  107.5 1.4 collective-permute-start.27
  108.9 2.0 %collective-permute-start.31 = (bf16[2,256,512]{2,1,0:T(8,128)(2,1)S(1)}, bf16[2,256,512]{2,1,0:T(8,128)(2,1)S(1)}, u32[]{:S(2)}, u32[]{:S(2)}) collective-permute-start(bf16[2,256,512]{2,1,0:T(8,128)(2,1)S(1)} %get-tuple-element.96.refs_0_), channel_id=1, source_target_pairs={{0,2},{1,3},{6,4},{7,5},{8,10},{9,11},{14,12},{15,13},{16,18},{17,... | collective-permute-start | bytes 1572872 | tf_op jit(solution)/shard_map/ppermute | solution.py:531
  111.0 2.7 %collective-permute-done.26.refs_2_ = bf16[128,512]{1,0:T(8,128)(2,1)S(1)} collective-permute-done((bf16[128,512]{1,0:T(8,128)(2,1)S(1)}, bf16[128,512]{1,0:T(8,128)(2,1)S(1)}, u32[]{:S(2)}, u32[]{:S(2)}) %collective-permute-start.26) | collective-permute-done | bytes 131104 | tf_op jit(solution)/shard_map/ppermute | solution.py:542
  113.6 1.8 %collective-permute-done.27.refs_3_ = bf16[128,512]{1,0:T(8,128)(2,1)S(1)} collective-permute-done((bf16[128,512]{1,0:T(8,128)(2,1)S(1)}, bf16[128,512]{1,0:T(8,128)(2,1)S(1)}, u32[]{:S(2)}, u32[]{:S(2)}) %collective-permute-start.27) | collective-permute-done | bytes 131104 | tf_op jit(solution)/shard_map/ppermute | solution.py:542
  115.6 1.1 collective-permute-start.29
  116.8 3.2 %collective-permute-start.30 = (bf16[32,512]{1,0:T(8,128)(2,1)S(1)}, bf16[32,512]{1,0:T(8,128)(2,1)S(1)}, u32[]{:S(2)}, u32[]{:S(2)}) collective-permute-start(bf16[32,512]{1,0:T(8,128)(2,1)S(1)} %get-tuple-element.95), channel_id=1, source_target_pairs={{0,6},{1,7},{2,4},{3,5},{4,2},{5,3},{6,0},{7,1},{8,14},{9,15},{10,... | collective-permute-start | bytes 98312 | tf_op jit(solution)/shard_map/ppermute | solution.py:531
  120.0 1.5 shard_map.126.refs_0_
  121.7 1.5 collective-permute-done.28.refs_1_
  123.6 3.9 %collective-permute-done.30.refs_3_ = bf16[32,512]{1,0:T(8,128)(2,1)S(1)} collective-permute-done((bf16[32,512]{1,0:T(8,128)(2,1)S(1)}, bf16[32,512]{1,0:T(8,128)(2,1)S(1)}, u32[]{:S(2)}, u32[]{:S(2)}) %collective-permute-start.30) | collective-permute-done | bytes 32800 | tf_op jit(solution)/shard_map/ppermute | solution.py:531
  127.5 2.2 %collective-permute-start.34 = (bf16[2,256,512]{2,1,0:T(8,128)(2,1)S(1)}, bf16[2,256,512]{2,1,0:T(8,128)(2,1)S(1)}, u32[]{:S(2)}, u32[]{:S(2)}) collective-permute-start(bf16[2,256,512]{2,1,0:T(8,128)(2,1)S(1)} %shard_map.131.refs_0_), channel_id=1, source_target_pairs={{0,2},{1,3},{6,4},{7,5},{8,10},{9,11},{14,12},{15,13},{16,18},{17,... | collective-permute-start | bytes 1572872 | tf_op jit(solution)/shard_map/ppermute | solution.py:531
  130.5 1.2 collective-permute-start.37
  131.7 1.1 collective-permute-start.36
  132.8 2.1 %collective-permute-start.35 = (bf16[32,512]{1,0:T(8,128)(2,1)S(1)}, bf16[32,512]{1,0:T(8,128)(2,1)S(1)}, u32[]{:S(2)}, u32[]{:S(2)}) collective-permute-start(bf16[32,512]{1,0:T(8,128)(2,1)S(1)} %shard_map.130.refs_1_.refs_0_), channel_id=1, source_target_pairs={{0,2},{1,3},{2,0},{3,1},{4,6},{5,7},{6,4},{7,5},{8,10},{9,11},{10,... | collective-permute-start | bytes 98312 | tf_op jit(solution)/shard_map/ppermute | solution.py:531
  135.0 7.0 %collective-permute-done.37.refs_3_ = bf16[32,512]{1,0:T(8,128)(2,1)S(1)} collective-permute-done((bf16[32,512]{1,0:T(8,128)(2,1)S(1)}, bf16[32,512]{1,0:T(8,128)(2,1)S(1)}, u32[]{:S(2)}, u32[]{:S(2)}) %collective-permute-start.37) | collective-permute-done | bytes 32800 | tf_op jit(solution)/shard_map/ppermute | solution.py:531
  141.9 3.2 %collective-permute-done.36.refs_2_ = bf16[32,512]{1,0:T(8,128)(2,1)S(1)} collective-permute-done((bf16[32,512]{1,0:T(8,128)(2,1)S(1)}, bf16[32,512]{1,0:T(8,128)(2,1)S(1)}, u32[]{:S(2)}, u32[]{:S(2)}) %collective-permute-start.36) | collective-permute-done | bytes 32800 | tf_op jit(solution)/shard_map/ppermute | solution.py:531
  146.1 1.8 %collective-permute-start.33 = (bf16[2,256,512]{2,1,0:T(8,128)(2,1)S(1)}, bf16[2,256,512]{2,1,0:T(8,128)(2,1)S(1)}, u32[]{:S(2)}, u32[]{:S(2)}) collective-permute-start(bf16[2,256,512]{2,1,0:T(8,128)(2,1)S(1)} %shard_map.133), channel_id=1, source_target_pairs={{0,2},{1,3},{2,0},{3,1},{4,6},{5,7},{6,4},{7,5},{8,10},{9,11},{10,... | collective-permute-start | bytes 1572872 | tf_op jit(solution)/shard_map/ppermute | solution.py:531
  147.9 1.4 collective-permute-start.41
  150.0 1.4 collective-permute-start.39
  151.4 2.5 %collective-permute-done.41.refs_3_ = bf16[128,512]{1,0:T(8,128)(2,1)S(1)} collective-permute-done((bf16[128,512]{1,0:T(8,128)(2,1)S(1)}, bf16[128,512]{1,0:T(8,128)(2,1)S(1)}, u32[]{:S(2)}, u32[]{:S(2)}) %collective-permute-start.41) | collective-permute-done | bytes 131104 | tf_op jit(solution)/shard_map/ppermute | solution.py:542
  153.9 1.3 collective-permute-done.40.refs_2_
  155.3 1.0 collective-permute-done.33.refs_1_
  156.3 1.3 shard_map.136
  157.6 1.5 shard_map.138
  (74 shorter events, 8.9 us)
Async XLA Ops:
  1.3 1.0 copy-start.2
  2.4 8.1 %copy-start.1 = (bf16[4,1,512,512]{3,2,1,0:T(8,128)(2,1)S(1)}, bf16[4,1,512,512]{3,2,1,0:T(8,128)(2,1)}, u32[]{:S(2)}) copy-start(bf16[4,1,512,512]{3,2,1,0:T(8,128)(2,1)} %param.8) | copy-start | bytes 6291460
  2.4 8.1 %copy-start.4 = (s32[1,1,48]{2,1,0:T(1,128)S(1)}, s32[1,1,48]{2,1,0:T(1,128)}, u32[]{:S(2)}) copy-start(s32[1,1,48]{2,1,0:T(1,128)} %param.11) | copy-start | bytes 580
  2.4 10.3 %slice-start = ((s8[6291456]{0:T(1024)(128)(4,1)}), s8[4194304]{0:T(1024)(128)(4,1)S(1)}, s32[]{:S(2)}) async-start(s8[6291456]{0:T(1024)(128)(4,1)} %bitcast.8), calls=%async_computation | async-start | bytes 8388608
  2.9 20.4 %collective-permute-start.7 = (bf16[2,512,256]{2,1,0:T(8,128)(2,1)S(1)}, bf16[2,512,256]{2,1,0:T(8,128)(2,1)S(1)}, u32[]{:S(2)}, u32[]{:S(2)}) collective-permute-start(bf16[2,512,256]{2,1,0:T(8,128)(2,1)S(1)} %get-tuple-element.62.refs_3_), channel_id=1, source_target_pairs={{2,4},{3,5},{4,2},{5,3},{10,12},{11,13},{12,10},{13,11},{18,20},{1... | collective-permute-start | bytes 1572872 | tf_op jit(solution)/shard_map/ppermute | solution.py:531
  3.8 19.6 %collective-permute-start.6 = (bf16[2,512,256]{2,1,0:T(8,128)(2,1)S(1)}, bf16[2,512,256]{2,1,0:T(8,128)(2,1)S(1)}, u32[]{:S(2)}, u32[]{:S(2)}) collective-permute-start(bf16[2,512,256]{2,1,0:T(8,128)(2,1)S(1)} %get-tuple-element.62.refs_3_), channel_id=1, source_target_pairs={{0,2},{1,3},{2,0},{3,1},{4,6},{5,7},{6,4},{7,5},{8,10},{9,11},{10,... | collective-permute-start | bytes 1572872 | tf_op jit(solution)/shard_map/ppermute | solution.py:531
  10.4 2.3 %slice-start.1 = ((s8[6291456]{0:T(1024)(128)(4,1)}), s8[2097152]{0:T(1024)(128)(4,1)S(1)}, s32[]{:S(2)}) async-start(s8[6291456]{0:T(1024)(128)(4,1)} %bitcast.8), calls=%async_computation.1 | async-start | bytes 4194304
  15.5 4.2 %collective-permute-start = (bf16[8,256,512]{2,1,0:T(8,128)(2,1)S(1)}, bf16[8,256,512]{2,1,0:T(8,128)(2,1)S(1)}, u32[]{:S(2)}, u32[]{:S(2)}) collective-permute-start(bf16[8,256,512]{2,1,0:T(8,128)(2,1)S(1)} %shard_map.106.refs_2_), channel_id=1, source_target_pairs={{0,1},{1,0},{2,3},{3,2},{4,5},{5,4},{6,7},{7,6},{8,9},{9,8},{10,11... | collective-permute-start | bytes 6291464 | tf_op jit(solution)/shard_map/ppermute | solution.py:539
  20.2 15.3 %collective-permute-start.1 = (bf16[2,256,512]{2,1,0:T(8,128)(2,1)S(1)}, bf16[2,256,512]{2,1,0:T(8,128)(2,1)S(1)}, u32[]{:S(2)}, u32[]{:S(2)}) collective-permute-start(bf16[2,256,512]{2,1,0:T(8,128)(2,1)S(1)} %get-tuple-element.59.refs_0_), channel_id=1, source_target_pairs={{0,2},{1,3},{6,4},{7,5},{8,10},{9,11},{14,12},{15,13},{16,18},{17,... | collective-permute-start | bytes 1572872 | tf_op jit(solution)/shard_map/ppermute | solution.py:531
  23.4 15.6 %collective-permute-start.9 = (bf16[2,512,256]{2,1,0:T(8,128)(2,1)S(1)}, bf16[2,512,256]{2,1,0:T(8,128)(2,1)S(1)}, u32[]{:S(2)}, u32[]{:S(2)}) collective-permute-start(bf16[2,512,256]{2,1,0:T(8,128)(2,1)S(1)} %get-tuple-element.64.refs_1_), channel_id=1, source_target_pairs={{2,0},{3,1},{4,6},{5,7},{10,8},{11,9},{12,14},{13,15},{18,16},{19,... | collective-permute-start | bytes 1572872 | tf_op jit(solution)/shard_map/ppermute | solution.py:531
  24.7 14.3 %collective-permute-start.8 = (bf16[2,512,256]{2,1,0:T(8,128)(2,1)S(1)}, bf16[2,512,256]{2,1,0:T(8,128)(2,1)S(1)}, u32[]{:S(2)}, u32[]{:S(2)}) collective-permute-start(bf16[2,512,256]{2,1,0:T(8,128)(2,1)S(1)} %get-tuple-element.63.refs_4_), channel_id=1, source_target_pairs={{2,4},{3,5},{4,2},{5,3},{10,12},{11,13},{12,10},{13,11},{18,20},{1... | collective-permute-start | bytes 1572872 | tf_op jit(solution)/shard_map/ppermute | solution.py:531
  25.4 20.6 %collective-permute-start.4 = (bf16[2,256,512]{2,1,0:T(8,128)(2,1)S(1)}, bf16[2,256,512]{2,1,0:T(8,128)(2,1)S(1)}, u32[]{:S(2)}, u32[]{:S(2)}) collective-permute-start(bf16[2,256,512]{2,1,0:T(8,128)(2,1)S(1)} %get-tuple-element.58.refs_0_), channel_id=1, source_target_pairs={{0,2},{1,3},{6,4},{7,5},{8,10},{9,11},{14,12},{15,13},{16,18},{17,... | collective-permute-start | bytes 1572872 | tf_op jit(solution)/shard_map/ppermute | solution.py:531
  35.7 10.4 %collective-permute-start.2 = (bf16[2,256,512]{2,1,0:T(8,128)(2,1)S(1)}, bf16[2,256,512]{2,1,0:T(8,128)(2,1)S(1)}, u32[]{:S(2)}, u32[]{:S(2)}) collective-permute-start(bf16[2,256,512]{2,1,0:T(8,128)(2,1)S(1)} %shard_map.108.refs_2_), channel_id=1, source_target_pairs={{2,4},{3,5},{4,2},{5,3},{10,12},{11,13},{12,10},{13,11},{18,20},{1... | collective-permute-start | bytes 1572872 | tf_op jit(solution)/shard_map/ppermute | solution.py:531
  39.1 15.7 %collective-permute-start.10 = (bf16[2,512,256]{2,1,0:T(8,128)(2,1)S(1)}, bf16[2,512,256]{2,1,0:T(8,128)(2,1)S(1)}, u32[]{:S(2)}, u32[]{:S(2)}) collective-permute-start(bf16[2,512,256]{2,1,0:T(8,128)(2,1)S(1)} %shard_map.112.refs_0_), channel_id=1, source_target_pairs={{2,0},{3,1},{4,6},{5,7},{10,8},{11,9},{12,14},{13,15},{18,16},{19,... | collective-permute-start | bytes 1572872 | tf_op jit(solution)/shard_map/ppermute | solution.py:531
  40.4 17.1 %collective-permute-start.11 = (bf16[2,512,256]{2,1,0:T(8,128)(2,1)S(1)}, bf16[2,512,256]{2,1,0:T(8,128)(2,1)S(1)}, u32[]{:S(2)}, u32[]{:S(2)}) collective-permute-start(bf16[2,512,256]{2,1,0:T(8,128)(2,1)S(1)} %get-tuple-element.62.refs_3_), channel_id=1, source_target_pairs={{0,1},{1,0},{2,3},{3,2},{4,5},{5,4},{6,7},{7,6},{8,9},{9,8},{10,11... | collective-permute-start | bytes 1572872 | tf_op jit(solution)/shard_map/ppermute | solution.py:539
  40.4 17.0 %collective-permute-start.12 = (bf16[2,512,256]{2,1,0:T(8,128)(2,1)S(1)}, bf16[2,512,256]{2,1,0:T(8,128)(2,1)S(1)}, u32[]{:S(2)}, u32[]{:S(2)}) collective-permute-start(bf16[2,512,256]{2,1,0:T(8,128)(2,1)S(1)} %get-tuple-element.63.refs_4_), channel_id=1, source_target_pairs={{0,1},{1,0},{2,3},{3,2},{4,5},{5,4},{6,7},{7,6},{8,9},{9,8},{10,11... | collective-permute-start | bytes 1572872 | tf_op jit(solution)/shard_map/ppermute | solution.py:539
  54.9 3.1 %collective-permute-start.13 = (bf16[1,512,256]{2,1,0:T(8,128)(2,1)S(1)}, bf16[1,512,256]{2,1,0:T(8,128)(2,1)S(1)}, u32[]{:S(2)}, u32[]{:S(2)}) collective-permute-start(bf16[1,512,256]{2,1,0:T(8,128)(2,1)S(1)} %get-tuple-element.65.refs_5_), channel_id=1, source_target_pairs={{0,1},{1,0},{2,3},{3,2},{4,5},{5,4},{6,7},{7,6},{8,9},{9,8},{10,11... | collective-permute-start | bytes 786440 | tf_op jit(solution)/shard_map/ppermute | solution.py:539
  55.0 9.4 %collective-permute-start.5 = (bf16[2,256,512]{2,1,0:T(8,128)(2,1)S(1)}, bf16[2,256,512]{2,1,0:T(8,128)(2,1)S(1)}, u32[]{:S(2)}, u32[]{:S(2)}) collective-permute-start(bf16[2,256,512]{2,1,0:T(8,128)(2,1)S(1)} %shard_map.110.refs_4_), channel_id=1, source_target_pairs={{2,4},{3,5},{4,2},{5,3},{10,12},{11,13},{12,10},{13,11},{18,20},{1... | collective-permute-start | bytes 1572872 | tf_op jit(solution)/shard_map/ppermute | solution.py:531
  55.8 14.4 %collective-permute-start.3 = (bf16[2,256,512]{2,1,0:T(8,128)(2,1)S(1)}, bf16[2,256,512]{2,1,0:T(8,128)(2,1)S(1)}, u32[]{:S(2)}, u32[]{:S(2)}) collective-permute-start(bf16[2,256,512]{2,1,0:T(8,128)(2,1)S(1)} %shard_map.109.refs_5_), channel_id=1, source_target_pairs={{0,2},{1,3},{2,0},{3,1},{4,6},{5,7},{6,4},{7,5},{8,10},{9,11},{10,... | collective-permute-start | bytes 1572872 | tf_op jit(solution)/shard_map/ppermute | solution.py:531
  57.4 1.5 collective-permute-start.14
  57.5 1.9 %collective-permute-start.15 = (bf16[1,512,256]{2,1,0:T(8,128)(2,1)S(1)}, bf16[1,512,256]{2,1,0:T(8,128)(2,1)S(1)}, u32[]{:S(2)}, u32[]{:S(2)}) collective-permute-start(bf16[1,512,256]{2,1,0:T(8,128)(2,1)S(1)} %get-tuple-element.67.refs_7_), channel_id=1, source_target_pairs={{0,1},{1,0},{2,3},{3,2},{4,5},{5,4},{6,7},{7,6},{8,9},{9,8},{10,11... | collective-permute-start | bytes 786440 | tf_op jit(solution)/shard_map/ppermute | solution.py:539
  58.0 1.8 %collective-permute-start.16 = (bf16[1,512,256]{2,1,0:T(8,128)(2,1)S(1)}, bf16[1,512,256]{2,1,0:T(8,128)(2,1)S(1)}, u32[]{:S(2)}, u32[]{:S(2)}) collective-permute-start(bf16[1,512,256]{2,1,0:T(8,128)(2,1)S(1)} %get-tuple-element.68.refs_8_), channel_id=1, source_target_pairs={{0,1},{1,0},{2,3},{3,2},{4,5},{5,4},{6,7},{7,6},{8,9},{9,8},{10,11... | collective-permute-start | bytes 786440 | tf_op jit(solution)/shard_map/ppermute | solution.py:539
  64.3 9.8 %copy-start = (bf16[512,512]{1,0:T(8,128)(2,1)S(1)}, bf16[512,512]{1,0:T(8,128)(2,1)}, u32[]{:S(2)}) copy-start(bf16[512,512]{1,0:T(8,128)(2,1)} %refs_4_.6) | copy-start | bytes 1572868
  70.4 4.9 %copy-start.3 = (bf16[512,512]{1,0:T(8,128)(2,1)S(1)}, bf16[512,512]{1,0:T(8,128)(2,1)}, u32[]{:S(2)}) copy-start(bf16[512,512]{1,0:T(8,128)(2,1)} %refs_4_.7) | copy-start | bytes 1572868
  70.5 9.3 %collective-permute-start.17 = (bf16[256,512]{1,0:T(8,128)(2,1)S(1)}, bf16[256,512]{1,0:T(8,128)(2,1)S(1)}, u32[]{:S(2)}, u32[]{:S(2)}) collective-permute-start(bf16[256,512]{1,0:T(8,128)(2,1)S(1)} %get-tuple-element.69.refs_0_), channel_id=1, source_target_pairs={{0,8},{8,0},{16,24},{24,16},{1,9},{9,1},{17,25},{25,17},{2,10},{10... | collective-permute-start | bytes 786440 | tf_op jit(solution)/shard_map/ppermute | solution.py:542
  71.8 9.6 %collective-permute-start.19 = (bf16[256,512]{1,0:T(8,128)(2,1)S(1)}, bf16[256,512]{1,0:T(8,128)(2,1)S(1)}, u32[]{:S(2)}, u32[]{:S(2)}) collective-permute-start(bf16[256,512]{1,0:T(8,128)(2,1)S(1)} %get-tuple-element.70.refs_1_), channel_id=1, source_target_pairs={{0,16},{8,24},{16,0},{24,8},{1,17},{9,25},{17,1},{25,9},{2,18},{10... | collective-permute-start | bytes 786440 | tf_op jit(solution)/shard_map/ppermute | solution.py:542
  74.8 10.6 %collective-permute-start.21 = (bf16[256,512]{1,0:T(8,128)(2,1)S(1)}, bf16[256,512]{1,0:T(8,128)(2,1)S(1)}, u32[]{:S(2)}, u32[]{:S(2)}) collective-permute-start(bf16[256,512]{1,0:T(8,128)(2,1)S(1)} %get-tuple-element.72), channel_id=1, source_target_pairs={{0,8},{8,0},{16,24},{24,16},{1,9},{9,1},{17,25},{25,17},{2,10},{10... | collective-permute-start | bytes 786440 | tf_op jit(solution)/shard_map/ppermute | solution.py:542
  75.0 11.9 %collective-permute-start.22 = (bf16[256,512]{1,0:T(8,128)(2,1)S(1)}, bf16[256,512]{1,0:T(8,128)(2,1)S(1)}, u32[]{:S(2)}, u32[]{:S(2)}) collective-permute-start(bf16[256,512]{1,0:T(8,128)(2,1)S(1)} %get-tuple-element.73), channel_id=1, source_target_pairs={{0,16},{8,24},{16,0},{24,8},{1,17},{9,25},{17,1},{25,9},{2,18},{10... | collective-permute-start | bytes 786440 | tf_op jit(solution)/shard_map/ppermute | solution.py:542
  79.7 12.6 %collective-permute-start.18 = (bf16[256,512]{1,0:T(8,128)(2,1)S(1)}, bf16[256,512]{1,0:T(8,128)(2,1)S(1)}, u32[]{:S(2)}, u32[]{:S(2)}) collective-permute-start(bf16[256,512]{1,0:T(8,128)(2,1)S(1)} %collective-permute-done.17.refs_0_), channel_id=1, source_target_pairs={{0,16},{8,24},{16,0},{24,8},{1,17},{9,25},{17,1},{25,9},{2,18},{10... | collective-permute-start | bytes 786440 | tf_op jit(solution)/shard_map/ppermute | solution.py:542
  81.4 10.9 %collective-permute-start.20 = (bf16[256,512]{1,0:T(8,128)(2,1)S(1)}, bf16[256,512]{1,0:T(8,128)(2,1)S(1)}, u32[]{:S(2)}, u32[]{:S(2)}) collective-permute-start(bf16[256,512]{1,0:T(8,128)(2,1)S(1)} %collective-permute-done.19.refs_3_), channel_id=1, source_target_pairs={{0,8},{8,0},{16,24},{24,16},{1,9},{9,1},{17,25},{25,17},{2,10},{10... | collective-permute-start | bytes 786440 | tf_op jit(solution)/shard_map/ppermute | solution.py:542
  95.7 7.9 %collective-permute-start.24 = (bf16[512,512]{1,0:T(8,128)(2,1)S(1)}, bf16[512,512]{1,0:T(8,128)(2,1)S(1)}, u32[]{:S(2)}, u32[]{:S(2)}) collective-permute-start(bf16[512,512]{1,0:T(8,128)(2,1)S(1)} %get-tuple-element.87), channel_id=1, source_target_pairs={{0,1},{1,0},{2,3},{3,2},{4,5},{5,4},{6,7},{7,6},{8,9},{9,8},{10,11... | collective-permute-start | bytes 1572872 | tf_op jit(solution)/shard_map/ppermute | solution.py:539
  98.8 4.6 %collective-permute-start.23 = (bf16[8,256,512]{2,1,0:T(8,128)(2,1)S(1)}, bf16[8,256,512]{2,1,0:T(8,128)(2,1)S(1)}, u32[]{:S(2)}, u32[]{:S(2)}) collective-permute-start(bf16[8,256,512]{2,1,0:T(8,128)(2,1)S(1)} %shard_map.124), channel_id=1, source_target_pairs={{0,1},{1,0},{2,3},{3,2},{4,5},{5,4},{6,7},{7,6},{8,9},{9,8},{10,11... | collective-permute-start | bytes 6291464 | tf_op jit(solution)/shard_map/ppermute | solution.py:539
  103.8 7.2 %collective-permute-start.25 = (bf16[128,512]{1,0:T(8,128)(2,1)S(1)}, bf16[128,512]{1,0:T(8,128)(2,1)S(1)}, u32[]{:S(2)}, u32[]{:S(2)}) collective-permute-start(bf16[128,512]{1,0:T(8,128)(2,1)S(1)} %get-tuple-element.89), channel_id=1, source_target_pairs={{0,8},{8,0},{16,24},{24,16},{1,9},{9,1},{17,25},{25,17},{2,10},{10... | collective-permute-start | bytes 393224 | tf_op jit(solution)/shard_map/ppermute | solution.py:542
  105.5 8.1 %collective-permute-start.26 = (bf16[128,512]{1,0:T(8,128)(2,1)S(1)}, bf16[128,512]{1,0:T(8,128)(2,1)S(1)}, u32[]{:S(2)}, u32[]{:S(2)}) collective-permute-start(bf16[128,512]{1,0:T(8,128)(2,1)S(1)} %get-tuple-element.90), channel_id=1, source_target_pairs={{0,16},{8,24},{16,0},{24,8},{1,17},{9,25},{17,1},{25,9},{2,18},{10... | collective-permute-start | bytes 393224 | tf_op jit(solution)/shard_map/ppermute | solution.py:542
  107.5 7.9 %collective-permute-start.27 = (bf16[128,512]{1,0:T(8,128)(2,1)S(1)}, bf16[128,512]{1,0:T(8,128)(2,1)S(1)}, u32[]{:S(2)}, u32[]{:S(2)}) collective-permute-start(bf16[128,512]{1,0:T(8,128)(2,1)S(1)} %get-tuple-element.91), channel_id=1, source_target_pairs={{0,24},{8,16},{16,8},{24,0},{1,25},{9,17},{17,9},{25,1},{2,26},{10... | collective-permute-start | bytes 393224 | tf_op jit(solution)/shard_map/ppermute | solution.py:542
  108.9 20.7 %collective-permute-start.31 = (bf16[2,256,512]{2,1,0:T(8,128)(2,1)S(1)}, bf16[2,256,512]{2,1,0:T(8,128)(2,1)S(1)}, u32[]{:S(2)}, u32[]{:S(2)}) collective-permute-start(bf16[2,256,512]{2,1,0:T(8,128)(2,1)S(1)} %get-tuple-element.96.refs_0_), channel_id=1, source_target_pairs={{0,2},{1,3},{6,4},{7,5},{8,10},{9,11},{14,12},{15,13},{16,18},{17,... | collective-permute-start | bytes 1572872 | tf_op jit(solution)/shard_map/ppermute | solution.py:531
  115.5 7.7 %collective-permute-start.28 = (bf16[32,512]{1,0:T(8,128)(2,1)S(1)}, bf16[32,512]{1,0:T(8,128)(2,1)S(1)}, u32[]{:S(2)}, u32[]{:S(2)}) collective-permute-start(bf16[32,512]{1,0:T(8,128)(2,1)S(1)} %get-tuple-element.93), channel_id=1, source_target_pairs={{0,2},{1,3},{2,0},{3,1},{4,6},{5,7},{6,4},{7,5},{8,10},{9,11},{10,... | collective-permute-start | bytes 98312 | tf_op jit(solution)/shard_map/ppermute | solution.py:531
  115.6 8.0 %collective-permute-start.29 = (bf16[32,512]{1,0:T(8,128)(2,1)S(1)}, bf16[32,512]{1,0:T(8,128)(2,1)S(1)}, u32[]{:S(2)}, u32[]{:S(2)}) collective-permute-start(bf16[32,512]{1,0:T(8,128)(2,1)S(1)} %get-tuple-element.94), channel_id=1, source_target_pairs={{0,4},{1,5},{2,6},{3,7},{4,0},{5,1},{6,2},{7,3},{8,12},{9,13},{10,... | collective-permute-start | bytes 98312 | tf_op jit(solution)/shard_map/ppermute | solution.py:531
  116.8 10.7 %collective-permute-start.30 = (bf16[32,512]{1,0:T(8,128)(2,1)S(1)}, bf16[32,512]{1,0:T(8,128)(2,1)S(1)}, u32[]{:S(2)}, u32[]{:S(2)}) collective-permute-start(bf16[32,512]{1,0:T(8,128)(2,1)S(1)} %get-tuple-element.95), channel_id=1, source_target_pairs={{0,6},{1,7},{2,4},{3,5},{4,2},{5,3},{6,0},{7,1},{8,14},{9,15},{10,... | collective-permute-start | bytes 98312 | tf_op jit(solution)/shard_map/ppermute | solution.py:531
  127.5 17.6 %collective-permute-start.34 = (bf16[2,256,512]{2,1,0:T(8,128)(2,1)S(1)}, bf16[2,256,512]{2,1,0:T(8,128)(2,1)S(1)}, u32[]{:S(2)}, u32[]{:S(2)}) collective-permute-start(bf16[2,256,512]{2,1,0:T(8,128)(2,1)S(1)} %shard_map.131.refs_0_), channel_id=1, source_target_pairs={{0,2},{1,3},{6,4},{7,5},{8,10},{9,11},{14,12},{15,13},{16,18},{17,... | collective-permute-start | bytes 1572872 | tf_op jit(solution)/shard_map/ppermute | solution.py:531
  129.8 16.2 %collective-permute-start.32 = (bf16[2,256,512]{2,1,0:T(8,128)(2,1)S(1)}, bf16[2,256,512]{2,1,0:T(8,128)(2,1)S(1)}, u32[]{:S(2)}, u32[]{:S(2)}) collective-permute-start(bf16[2,256,512]{2,1,0:T(8,128)(2,1)S(1)} %shard_map.132.refs_2_), channel_id=1, source_target_pairs={{2,4},{3,5},{4,2},{5,3},{10,12},{11,13},{12,10},{13,11},{18,20},{1... | collective-permute-start | bytes 1572872 | tf_op jit(solution)/shard_map/ppermute | solution.py:531
  130.5 11.4 %collective-permute-start.37 = (bf16[32,512]{1,0:T(8,128)(2,1)S(1)}, bf16[32,512]{1,0:T(8,128)(2,1)S(1)}, u32[]{:S(2)}, u32[]{:S(2)}) collective-permute-start(bf16[32,512]{1,0:T(8,128)(2,1)S(1)} %shard_map.130.refs_1_.refs_0_), channel_id=1, source_target_pairs={{0,6},{1,7},{2,4},{3,5},{4,2},{5,3},{6,0},{7,1},{8,14},{9,15},{10,... | collective-permute-start | bytes 98312 | tf_op jit(solution)/shard_map/ppermute | solution.py:531
  131.7 13.4 %collective-permute-start.36 = (bf16[32,512]{1,0:T(8,128)(2,1)S(1)}, bf16[32,512]{1,0:T(8,128)(2,1)S(1)}, u32[]{:S(2)}, u32[]{:S(2)}) collective-permute-start(bf16[32,512]{1,0:T(8,128)(2,1)S(1)} %shard_map.130.refs_1_.refs_0_), channel_id=1, source_target_pairs={{0,4},{1,5},{2,6},{3,7},{4,0},{5,1},{6,2},{7,3},{8,12},{9,13},{10,... | collective-permute-start | bytes 98312 | tf_op jit(solution)/shard_map/ppermute | solution.py:531
  132.8 12.3 %collective-permute-start.35 = (bf16[32,512]{1,0:T(8,128)(2,1)S(1)}, bf16[32,512]{1,0:T(8,128)(2,1)S(1)}, u32[]{:S(2)}, u32[]{:S(2)}) collective-permute-start(bf16[32,512]{1,0:T(8,128)(2,1)S(1)} %shard_map.130.refs_1_.refs_0_), channel_id=1, source_target_pairs={{0,2},{1,3},{2,0},{3,1},{4,6},{5,7},{6,4},{7,5},{8,10},{9,11},{10,... | collective-permute-start | bytes 98312 | tf_op jit(solution)/shard_map/ppermute | solution.py:531
  145.3 10.0 %collective-permute-start.38 = (bf16[2,256,512]{2,1,0:T(8,128)(2,1)S(1)}, bf16[2,256,512]{2,1,0:T(8,128)(2,1)S(1)}, u32[]{:S(2)}, u32[]{:S(2)}) collective-permute-start(bf16[2,256,512]{2,1,0:T(8,128)(2,1)S(1)} %shard_map.135), channel_id=1, source_target_pairs={{2,4},{3,5},{4,2},{5,3},{10,12},{11,13},{12,10},{13,11},{18,20},{1... | collective-permute-start | bytes 1572872 | tf_op jit(solution)/shard_map/ppermute | solution.py:531
  146.1 10.2 %collective-permute-start.33 = (bf16[2,256,512]{2,1,0:T(8,128)(2,1)S(1)}, bf16[2,256,512]{2,1,0:T(8,128)(2,1)S(1)}, u32[]{:S(2)}, u32[]{:S(2)}) collective-permute-start(bf16[2,256,512]{2,1,0:T(8,128)(2,1)S(1)} %shard_map.133), channel_id=1, source_target_pairs={{0,2},{1,3},{2,0},{3,1},{4,6},{5,7},{6,4},{7,5},{8,10},{9,11},{10,... | collective-permute-start | bytes 1572872 | tf_op jit(solution)/shard_map/ppermute | solution.py:531
  147.9 6.0 %collective-permute-start.41 = (bf16[128,512]{1,0:T(8,128)(2,1)S(1)}, bf16[128,512]{1,0:T(8,128)(2,1)S(1)}, u32[]{:S(2)}, u32[]{:S(2)}) collective-permute-start(bf16[128,512]{1,0:T(8,128)(2,1)S(1)} %shard_map.134.refs_3_.refs_0_), channel_id=1, source_target_pairs={{0,24},{8,16},{16,8},{24,0},{1,25},{9,17},{17,9},{25,1},{2,26},{10... | collective-permute-start | bytes 393224 | tf_op jit(solution)/shard_map/ppermute | solution.py:542
  149.3 5.9 %collective-permute-start.40 = (bf16[128,512]{1,0:T(8,128)(2,1)S(1)}, bf16[128,512]{1,0:T(8,128)(2,1)S(1)}, u32[]{:S(2)}, u32[]{:S(2)}) collective-permute-start(bf16[128,512]{1,0:T(8,128)(2,1)S(1)} %shard_map.134.refs_3_.refs_0_), channel_id=1, source_target_pairs={{0,16},{8,24},{16,0},{24,8},{1,17},{9,25},{17,1},{25,9},{2,18},{10... | collective-permute-start | bytes 393224 | tf_op jit(solution)/shard_map/ppermute | solution.py:542
  150.0 5.2 %collective-permute-start.39 = (bf16[128,512]{1,0:T(8,128)(2,1)S(1)}, bf16[128,512]{1,0:T(8,128)(2,1)S(1)}, u32[]{:S(2)}, u32[]{:S(2)}) collective-permute-start(bf16[128,512]{1,0:T(8,128)(2,1)S(1)} %shard_map.134.refs_3_.refs_0_), channel_id=1, source_target_pairs={{0,8},{8,0},{16,24},{24,16},{1,9},{9,1},{17,25},{25,17},{2,10},{10... | collective-permute-start | bytes 393224 | tf_op jit(solution)/shard_map/ppermute | solution.py:542
  155.2 2.4 %collective-permute-start.42 = (bf16[512,512]{1,0:T(8,128)(2,1)S(1)}, bf16[512,512]{1,0:T(8,128)(2,1)S(1)}, u32[]{:S(2)}, u32[]{:S(2)}) collective-permute-start(bf16[512,512]{1,0:T(8,128)(2,1)S(1)} %shard_map.137.refs_0_), channel_id=1, source_target_pairs={{0,1},{1,0},{2,3},{3,2},{4,5},{5,4},{6,7},{7,6},{8,9},{9,8},{10,11... | collective-permute-start | bytes 1572872 | tf_op jit(solution)/shard_map/ppermute | solution.py:539
